TPU v7x, 32 devices: a whole 2x2x4 slice. The times are simulated.
32 devices in a mesh: section: 16 (over z, y, core), head: 2 (over x).
Axes of the slice: x: 2, y: 2, z: 4, core: 2. Of those that a mesh axis runs over, the one named last changes fastest.
Arguments:
- hidden: bfloat16 [2048, 3072], P('section', 'head'), may hold values from -6 to 6
- text_hidden: bfloat16 [256, 3072], P(None, 'head'), may hold values from -6 to 6
- text_mask: int32 [256], replicated, may hold values 0 or 1
- stale_cache: bfloat16 [2, 2048, 1536], P(None, 'section', 'head'), may hold values from -2.5 to 2.5
- qkv_weight: bfloat16 [3072, 4608], P('head'), may hold values from -0.109375 to 0.109375
- out_weight: bfloat16 [1536, 3072], P(None, 'head'), may hold values from -0.15625 to 0.15625
- query_gain: float32 [128], replicated, may hold values from 1 to 2
- key_gain: float32 [128], replicated, may hold values from 1 to 2
- norm_shift: float32 [3072], P('head'), may hold values from -3 to 3
- norm_scale: float32 [3072], P('head'), may hold values from -0.5 to 0.5
- branch_gate: float32 [3072], P('head'), may hold values from 0.5 to 2
Outputs:
- mixed: bfloat16 [2048, 3072], P('section', 'head')
- new_cache: bfloat16 [2, 2048, 1536], P(None, 'section', 'head')
All inputs are finite; a program needn't handle non-finite values.
Results may differ from a plain program's by a relative error of at most 0.0066.
Values may be sent and summed in bfloat16 or wider, within the bound.
No kernel may reach another device: no remote copies, remote signals or barrier semaphores. Data moves between devices by JAX's collectives and lax.ppermute only.
A program may use at most 192 MiB of HBM per device.

v0:
```python
import math

import jax
import jax.numpy as jnp
from jax import lax
from jax.sharding import PartitionSpec as P

D = 3072
HEADS = 12
HEAD_DIM = 128


def head_norm(part_rows, gain_vec):
    return (
        part_rows
        * lax.rsqrt(jnp.mean(part_rows * part_rows, axis=-1, keepdims=True) + 1e-06)
        * gain_vec
    )


def context_terms(query_rows, key_rows, value_rows, keep_rows):
    row_count = key_rows.shape[0]
    head_count = key_rows.shape[1]
    head_depth = key_rows.shape[2]
    block_rows = 1024 if row_count > 1024 and row_count % 1024 == 0 else row_count
    block_count = row_count // block_rows
    factor = 1.0 / math.sqrt(head_depth)

    def absorb_block(carried, block_items):
        key_block, value_block, keep_block = block_items
        scores = (
            jnp.einsum("qhc,khc->hqk", query_rows, key_block, preferred_element_type=jnp.float32)
            * factor
        )
        weights = jnp.exp(scores) * keep_block[None, None, :]
        weighted = jnp.einsum(
            "hqk,khc->qhc",
            weights.astype(jnp.bfloat16),
            value_block,
            preferred_element_type=jnp.float32,
        )
        return ((carried[0] + weighted, carried[1] + jnp.sum(weights, axis=-1).T), None)

    initial = (
        jnp.zeros((query_rows.shape[0], head_count, head_depth), jnp.float32),
        jnp.zeros((query_rows.shape[0], head_count), jnp.float32),
    )
    blocked = (
        key_rows.reshape(block_count, block_rows, head_count, head_depth),
        value_rows.reshape(block_count, block_rows, head_count, head_depth),
        keep_rows.reshape(block_count, block_rows),
    )
    result, unused = lax.scan(absorb_block, initial, blocked)
    return result


def per_device(
    hidden,
    text_hidden,
    text_mask,
    stale_cache,
    qkv_weight,
    out_weight,
    query_gain,
    key_gain,
    norm_shift,
    norm_scale,
    branch_gate,
):
    local_rows = hidden.shape[0]
    head_devices = lax.axis_size("head")
    section_index = lax.axis_index("section")
    local_heads = HEADS // head_devices
    inputs_all = jnp.concatenate([hidden, text_hidden], 0).astype(jnp.float32)
    row_sum, row_square = lax.psum(
        (jnp.sum(inputs_all, axis=1), jnp.sum(inputs_all * inputs_all, axis=1)), "head"
    )
    row_mean = row_sum / D
    row_var = row_square / D - row_mean * row_mean
    normed = (
        (inputs_all - row_mean[:, None]) * lax.rsqrt(row_var + 1e-06)[:, None] * (1.0 + norm_scale)
        + norm_shift
    ).astype(jnp.bfloat16)
    triple = 3 * HEAD_DIM
    columns = qkv_weight
    columns = columns.reshape(columns.shape[0], local_heads * lax.axis_size("head"), triple)
    projected = lax.psum_scatter(
        jnp.einsum("rd,dhc->hrc", normed, columns, preferred_element_type=jnp.float32),
        "head",
        scatter_dimension=0,
        tiled=True,
    )
    projected = jnp.transpose(projected, (1, 0, 2))
    queries_all = head_norm(projected[..., :HEAD_DIM], query_gain).astype(jnp.bfloat16)
    keys_all = head_norm(projected[..., HEAD_DIM : 2 * HEAD_DIM], key_gain).astype(jnp.bfloat16)
    values_all = projected[..., 2 * HEAD_DIM :].astype(jnp.bfloat16)
    own_queries = queries_all[:local_rows]
    own_keys = keys_all[:local_rows]
    own_values = values_all[:local_rows]
    text_keys = keys_all[local_rows:]
    text_values = values_all[local_rows:]
    new_cache = jnp.stack(
        [
            own_keys.reshape(local_rows, local_heads * HEAD_DIM),
            own_values.reshape(local_rows, local_heads * HEAD_DIM),
        ]
    )
    fresh_num, fresh_den = context_terms(
        own_queries, own_keys, own_values, jnp.ones((local_rows,), jnp.float32)
    )
    text_num, text_den = context_terms(
        own_queries, text_keys, text_values, text_mask.astype(jnp.float32)
    )
    base_num = fresh_num + text_num
    base_den = fresh_den + text_den
    own_start = section_index * local_rows
    segment = lax.all_gather(stale_cache, "section", axis=1, tiled=True)
    segment_rows = segment.shape[1]
    positions = jnp.arange(segment_rows, dtype=jnp.int32)
    keep_rows = ((positions < own_start) | (positions >= own_start + local_rows)).astype(
        jnp.float32
    )
    segment_keys = segment[0].reshape(segment_rows, local_heads, HEAD_DIM)
    segment_values = segment[1].reshape(segment_rows, local_heads, HEAD_DIM)
    added_num, added_den = context_terms(own_queries, segment_keys, segment_values, keep_rows)
    total_num = base_num + added_num
    total_den = base_den + added_den
    attended = (
        (total_num / total_den[..., None])
        .astype(jnp.bfloat16)
        .reshape(local_rows, local_heads * HEAD_DIM)
    )
    projection_out = jnp.dot(
        lax.all_gather(attended, "head", axis=1, tiled=True),
        out_weight,
        preferred_element_type=jnp.float32,
    )
    mixed = (hidden.astype(jnp.float32) + branch_gate * projection_out).astype(jnp.bfloat16)
    return (mixed, new_cache)


def solution(mesh):
    in_specs = (
        P("section", "head"),
        P(None, "head"),
        P(),
        P(None, "section", "head"),
        P("head", None),
        P(None, "head"),
        P(),
        P(),
        P("head"),
        P("head"),
        P("head"),
    )
    out_specs = (P("section", "head"), P(None, "section", "head"))
    return jax.shard_map(
        per_device, mesh=mesh, in_specs=in_specs, out_specs=out_specs, check_vma=False
    )
```

profile of v0, /device:TPU:0, one launch (start us, length us, event | category | flops | bytes accessed | tf_op | source)
XLA Modules:
  0.0 173.8 jit_solution(12719828770132805347)
XLA Ops:
  8.8 18.7 %copy.19 = bf16[1536,4608]{0,1:T(8,128)(2,1)} copy(bf16[1536,4608]{1,0:T(8,128)(2,1)} %param.17) | data formatting | bytes 28311552 | tf_op args[4]
  27.9 5.9 %all-reduce = (f32[384]{0:T(512)S(1)}, f32[384]{0:T(512)S(1)}) all-reduce(f32[384]{0:T(512)S(1)} %get-tuple-element.117, f32[384]{0:T(512)S(1)} %get-tuple-element.116), channel_id=1, replica_groups=mesh['section'=16,'head'=2] {'head'}, use_global_device_ids=true, to_apply=%region_3.0 | all-reduce | flops 768 | bytes 6144 | tf_op jit(solution)/shard_map/psum | solution.py:75
  33.9 11.0 %convolution_bitcast_fusion = f32[12,384,384]{2,1,0:T(8,128)} fusion(bf16[1536,12,384]{0,2,1:T(8,128)(2,1)} %bitcast.74, f32[1536]{0:T(1024)S(1)} %copy-done.12, f32[1536]{0:T(1024)S(1)} %broadcast_add_fusion, f32[384]{0:T(512)S(1)} %get-tuple-element.141, f32[384]{0:T(512)S(1)} %get-tuple-element.140, bf16[256,1536]{1,0:T(8,128)(2,1)S(1)} %copy-done.3, ...), kind=kOutput, calls=%fused_computation.21 | convolution fusion | flops 5441126400 | bytes 22428672 | tf_op jit(solution)/shard_map/rd,dhc->hrc/dot_general | solution.py:88
  46.1 29.7 %all-gather.2.cloned.1.call-done = bf16[2,2048,768]{2,1,0:T(8,128)(2,1)} async-done(((bf16[2,128,768]{2,1,0:T(8,128)(2,1)}), bf16[2,2048,768]{2,1,0:T(8,128)(2,1)}) %all-gather.2.cloned.1.call-update) | async-done | bytes 6291472 | tf_op jit(solution)/shard_map/all_gather | solution.py:117
  75.8 5.1 %fusion.47 = (bf16[1,2048,768]{2,1,0:T(8,128)(2,1)S(1)}, bf16[1,2048,768]{2,1,0:T(8,128)(2,1)}) fusion(bf16[2,2048,768]{2,1,0:T(8,128)(2,1)} %all-gather.2.cloned.1.call-done), kind=kLoop, calls=%fused_computation.69 | loop fusion | bytes 12582912 | tf_op jit(solution)/shard_map/slice | solution.py:123
  80.9 7.7 %reshape.61 = bf16[2,1024,6,128]{3,2,1,0:T(8,128)(2,1)} reshape(bf16[1,2048,768]{2,1,0:T(8,128)(2,1)} %get-tuple-element.137) | data formatting | bytes 6291456 | tf_op jit(solution)/shard_map/reshape;reshape;squeeze | solution.py:50
  88.6 6.4 %copy.26 = bf16[2,1024,6,128]{1,3,2,0:T(8,128)(2,1)} copy(bf16[2,1024,6,128]{3,2,1,0:T(8,128)(2,1)} %reshape.61) | data formatting | bytes 6291456
  95.0 4.6 %reshape.62 = bf16[2,1024,6,128]{3,2,1,0:T(8,128)(2,1)} reshape(bf16[1,2048,768]{2,1,0:T(8,128)(2,1)S(1)} %get-tuple-element.136) | data formatting | bytes 6291456 | tf_op jit(solution)/shard_map/reshape;reshape;squeeze | solution.py:49
  99.7 4.4 %copy.27 = bf16[2,1024,6,128]{3,1,2,0:T(8,128)(2,1)} copy(bf16[2,1024,6,128]{3,2,1,0:T(8,128)(2,1)} %reshape.62) | data formatting | bytes 6291456
  104.1 28.2 %reduce-scatter.2.cloned.1.call-done = f32[6,384,384]{2,1,0:T(8,128)} async-done(((f32[12,384,384]{2,1,0:T(8,128)}), f32[6,384,384]{2,1,0:T(8,128)}) %reduce-scatter.2.cloned.1.call-update) | async-done | bytes 3538960 | tf_op jit(solution)/shard_map/reduce_scatter | solution.py:87
  132.3 2.3 %multiply_reduce_fusion = (f32[384,6]{0,1:T(8,128)S(1)}, f32[384,6]{0,1:T(8,128)S(1)}) fusion(f32[384,6,384]{2,0,1:T(8,128)} %bitcast.72), kind=kLoop, calls=%fused_computation.42 | loop fusion | flops 1175040 | bytes 2377728 | tf_op jit(solution)/shard_map/reduce_sum | solution.py:16
  134.7 2.0 %multiply_convert_fusion = (bf16[384,6,128]{2,0,1:T(8,128)(2,1)S(1)}, f32[384,6,128]{2,0,1:T(8,128)S(1)}) fusion(f32[384,6,384]{2,0,1:T(8,128)} %bitcast.73, f32[128]{0:T(128)S(1)} %copy-done.10, f32[384,6]{0,1:T(8,128)S(1)} %get-tuple-element.146), kind=kLoop, calls=%fused_computation.41 | loop fusion | flops 884736 | bytes 4138496 | tf_op jit(solution)/shard_map/convert_element_type | solution.py:95
  137.6 0.9 fusion.48
  138.5 1.6 fusion.49
  140.2 10.7 %while.3 = (s32[]{:T(128)}, f32[128,6,128]{0,2,1:T(8,128)S(1)}, f32[128,6]{0,1:T(8,128)S(1)}, bf16[2,1024,6,128]{1,3,2,0:T(8,128)(2,1)}, bf16[2,1024,6,128]{3,1,...) while((s32[]{:T(128)}, f32[128,6,128]{0,2,1:T(8,128)S(1)}, ...), condition=%wide.region_9.10_spmd.clone, body=%wide.region_7.9_spmd.clone.sunk | while | flops 407569152 | bytes 10450028 | solution.py:53
  140.9 2.1 %bitcast_reduce_fusion.2 = (f32[6,128]{1,0:T(8,128)S(1)}, f32[6,1024,128]{2,1,0:T(8,128)S(1)}) fusion(f32[1024]{0:T(1024)S(1)} %bitcast.75, bf16[128,6,128]{2,0,1:T(8,128)(2,1)} %get-tuple-element.222, bf16[2,1024,6,128]{3,1,2,0:T(8,128)(2,1)} %get-tuple-element.221, s32[]{:T(128)} %get-tuple-element.208), kind=kOutput, calls=%fused_computation.clone.1 | convolution fusion | flops 203685120 | bytes 4922880 | tf_op jit(solution)/shard_map/while/body/eval_jaxpr/qhc,khc->hqk/dot_general | solution.py:32
  143.0 2.4 %fusion.63 = f32[128,6,128]{0,2,1:T(8,128)S(1)} fusion(f32[6,1024,128]{2,1,0:T(8,128)S(1)} %get-tuple-element.197, f32[1024]{0:T(1024)S(1)} %bitcast.76, bf16[2,1024,6,128]{1,3,2,0:T(8,128)(2,1)} %get-tuple-element.220, s32[]{:T(128)} %get-tuple-element.208, f32[128,6,128]{0,2,1:T(8,128)S(1)} %get-tuple-element.209, pred[]{:T(512)S(6)} %compare.3), kind=kOutput, calls=%fused_computation.12.clone.1 | convolution fusion | flops 203882496 | bytes 5509633 | tf_op jit(solution)/shard_map/while/body/eval_jaxpr/hqk,khc->qhc/dot_general | solution.py:36
  145.5 0.7 constant_dynamic-slice_fusion.2
  146.2 2.2 %bitcast_reduce_fusion.2 = (f32[6,128]{1,0:T(8,128)S(1)}, f32[6,1024,128]{2,1,0:T(8,128)S(1)}) fusion(f32[1024]{0:T(1024)S(1)} %bitcast.75, bf16[128,6,128]{2,0,1:T(8,128)(2,1)} %get-tuple-element.222, bf16[2,1024,6,128]{3,1,2,0:T(8,128)(2,1)} %get-tuple-element.221, s32[]{:T(128)} %get-tuple-element.208), kind=kOutput, calls=%fused_computation.clone.1 | convolution fusion | flops 203685120 | bytes 4922880 | tf_op jit(solution)/shard_map/while/body/eval_jaxpr/qhc,khc->hqk/dot_general | solution.py:32
  148.4 2.4 %fusion.63 = f32[128,6,128]{0,2,1:T(8,128)S(1)} fusion(f32[6,1024,128]{2,1,0:T(8,128)S(1)} %get-tuple-element.197, f32[1024]{0:T(1024)S(1)} %bitcast.76, bf16[2,1024,6,128]{1,3,2,0:T(8,128)(2,1)} %get-tuple-element.220, s32[]{:T(128)} %get-tuple-element.208, f32[128,6,128]{0,2,1:T(8,128)S(1)} %get-tuple-element.209, pred[]{:T(512)S(6)} %compare.3), kind=kOutput, calls=%fused_computation.12.clone.1 | convolution fusion | flops 203882496 | bytes 5509633 | tf_op jit(solution)/shard_map/while/body/eval_jaxpr/hqk,khc->qhc/dot_general | solution.py:36
  150.9 2.3 %bitcast_convert_fusion.6 = bf16[384,6,384]{2,0,1:T(8,128)(2,1)S(1)} fusion(f32[6,384,384]{2,1,0:T(8,128)} %reduce-scatter.2.cloned.1.call-done), kind=kLoop, calls=%fused_computation.66 | loop fusion | flops 884736 | bytes 5308416 | tf_op jit(solution)/shard_map/convert
  153.9 7.2 %all_gather.7 = bf16[128,1536]{0,1:T(8,128)(2,1)S(1)} all-gather(bf16[128,768]{0,1:T(8,128)(2,1)S(1)} %bitcast.79), channel_id=1, replica_groups=mesh['section'=16,'head'=2] {'head'}, dimensions={1}, use_global_device_ids=true | all-gather | bytes 589824 | tf_op jit(solution)/shard_map/all_gather | solution.py:134
  161.5 0.9 copy.30
  162.4 3.9 %fusion.18 = bf16[128,1536]{1,0:T(8,128)(2,1)} fusion(bf16[128,1536]{0,1:T(8,128)(2,1)S(1)} %all_gather.7, bf16[1536,1536]{1,0:T(8,128)(2,1)} %param.18, bf16[128,1536]{1,0:T(8,128)(2,1)S(1)} %copy-done.2, f32[1536]{0:T(1024)S(1)} %copy-done.6), kind=kOutput, calls=%fused_computation.24 | convolution fusion | flops 604766208 | bytes 5904384 | tf_op jit(solution)/shard_map/dot_general | solution.py:133
  (53 shorter events, 5.1 us)
Async XLA Ops:
  8.0 67.8 %all-gather.2.cloned.1.call-start = ((), (), s32[]{:S(2)}) async-start(), calls=%async_computation.2 | async-start | bytes 6684672 | tf_op jit(solution)/shard_map/all_gather | solution.py:117
  8.7 18.8 %copy-start.1 = (bf16[128,1536]{1,0:T(8,128)(2,1)S(1)}, bf16[128,1536]{1,0:T(8,128)(2,1)}, u32[]{:S(2)}) copy-start(bf16[128,1536]{1,0:T(8,128)(2,1)} %param.13) | copy-start | bytes 1179652
  8.7 18.8 %copy-start.3 = (bf16[256,1536]{1,0:T(8,128)(2,1)S(1)}, bf16[256,1536]{1,0:T(8,128)(2,1)}, u32[]{:S(2)}) copy-start(bf16[256,1536]{1,0:T(8,128)(2,1)} %param.14) | copy-start | bytes 2359300
  8.8 25.1 %copy-start.7 = (f32[1536]{0:T(1024)S(1)}, f32[1536]{0:T(1024)}, u32[]{:S(2)}) copy-start(f32[1536]{0:T(1024)} %param.22) | copy-start | bytes 18436
  8.8 25.1 %copy-start.12 = (f32[1536]{0:T(1024)S(1)}, f32[1536]{0:T(1024)}, u32[]{:S(2)}) copy-start(f32[1536]{0:T(1024)} %param.21) | copy-start | bytes 18436
  8.8 123.5 %reduce-scatter.2.cloned.1.call-start = ((), (), s32[]{:S(2)}) async-start(), calls=%async_computation.1 | async-start | bytes 10616832 | tf_op jit(solution)/shard_map/reduce_scatter | solution.py:87
  44.8 0.7 copy-start.9
  104.1 30.6 %copy-start.10 = (f32[128]{0:T(128)S(1)}, f32[128]{0:T(128)}, u32[]{:S(2)}) copy-start(f32[128]{0:T(128)} %param.20) | copy-start | bytes 1540
  134.6 2.8 %copy-start.11 = (f32[128]{0:T(128)S(1)}, f32[128]{0:T(128)}, u32[]{:S(2)}) copy-start(f32[128]{0:T(128)} %param.19) | copy-start | bytes 1540
  137.6 2.6 %copy-start = (bf16[128,6,128]{2,0,1:T(8,128)(2,1)}, bf16[128,6,128]{2,0,1:T(8,128)(2,1)S(1)}, u32[]{:S(2)}) copy-start(bf16[128,6,128]{2,0,1:T(8,128)(2,1)S(1)} %fusion.41) | copy-start | bytes 589828
  150.8 2.4 %copy-start.5 = (bf16[6,128,256]{2,1,0:T(8,128)(2,1)S(1)}, bf16[6,128,256]{2,1,0:T(8,128)(2,1)}, u32[]{:S(2)}) copy-start(bf16[6,128,256]{2,1,0:T(8,128)(2,1)} %get-tuple-element.145) | copy-start | bytes 1179652
  150.9 2.7 %copy-start.8 = (f32[6,128]{1,0:T(8,128)S(1)}, f32[6,128]{1,0:T(8,128)}, u32[]{:S(2)}) copy-start(f32[6,128]{1,0:T(8,128)} %get-tuple-element.144) | copy-start | bytes 9220
  150.9 2.7 %copy-start.13 = (bf16[6,128,128]{1,2,0:T(8,128)(2,1)S(1)}, bf16[6,128,128]{1,2,0:T(8,128)(2,1)}, u32[]{:S(2)}) copy-start(bf16[6,128,128]{1,2,0:T(8,128)(2,1)} %get-tuple-element.143) | copy-start | bytes 589828
  153.1 7.9 %copy-start.4 = (bf16[128,6,128]{2,0,1:T(8,128)(2,1)S(1)}, bf16[128,6,128]{2,0,1:T(8,128)(2,1)}, u32[]{:S(2)}) copy-start(bf16[128,6,128]{2,0,1:T(8,128)(2,1)} %slice.45) | copy-start | bytes 589828
  153.6 8.9 %copy-start.2 = (bf16[128,1536]{1,0:T(8,128)(2,1)S(1)}, bf16[128,1536]{1,0:T(8,128)(2,1)}, u32[]{:S(2)}) copy-start(bf16[128,1536]{1,0:T(8,128)(2,1)} %param.13) | copy-start | bytes 1179652
  153.6 8.8 %copy-start.6 = (f32[1536]{0:T(1024)S(1)}, f32[1536]{0:T(1024)}, u32[]{:S(2)}) copy-start(f32[1536]{0:T(1024)} %param.23) | copy-start | bytes 18436
Sparse Core Ops, SparseCore 0:
  11.1 64.6 all-gather.1
Sparse Core Ops, SparseCore 1:
  45.0 87.3 reduce-scatter.1
where the time goes:
time: 175 us; the launch traced here: 174 us
  waiting for transfers between devices  58.6 us (33%)
  local copies, waits for them, and re-layouts  51.1 us (29%)
  matrix products  27.2 us (16%)
  between operations  15.7 us (9%)
  blocking collectives  13.1 us (7%)
  other arithmetic  7.92 us (5%)
    unnamed x32, local copies, waits for them, and re-layouts  31.1 us
    all_gather x1, waiting for transfers between devices, per_device(): segment = lax.all_gather(stale_cache, 'section', axis=1, tiled=True)  29.7 us
    reduce_scatter x1, waiting for transfers between devices, per_device(): lax.psum_scatter(jnp.einsum('rd,dhc->hrc', normed, columns, preferred_ele...  28.2 us
    dot_general x1, matrix products, per_device(): jnp.einsum('rd,dhc->hrc', normed, columns, preferred_element_type=jnp.flo...  11 us
    another operation x1, local copies, waits for them, and re-layouts, context_terms(): value_rows.reshape(block_count, block_rows, head_count, head_depth)  7.75 us
    all_gather x1, blocking collectives, per_device(): lax.all_gather(attended, 'head', axis=1, tiled=True)  7.21 us
    dot_general x4, matrix products, absorb_block(): jnp.einsum('qhc,khc->hqk', query_rows, key_block, preferred_element_type=...  6.88 us
    psum x1, blocking collectives, per_device(): lax.psum((jnp.sum(inputs_all, axis=1), jnp.sum(inputs_all * inputs_all, a...  5.89 us
  transfers between devices with their start and end apart: 2, of which 2 were waited for; matrix products, arithmetic and copies ran while one was open for 34% of the time, Pallas kernels for 0%

commit v1 on v0

v1 whole, which is shorter than its diff:
```python
import functools
import math

import jax
import jax.numpy as jnp
from jax import lax
from jax.experimental import pallas as pl
from jax.experimental.pallas import tpu as pltpu
from jax.sharding import PartitionSpec as P

HEAD_DIM = 128
TRIPLE = 3 * HEAD_DIM
EPS = 1e-06
F32 = jnp.float32
BF16 = jnp.bfloat16


def round_up(value, step):
    return -(-value // step) * step


def split_bf16(value, parts):
    pieces = []
    rest = value
    for _ in range(parts):
        piece = rest.astype(BF16)
        pieces.append(piece)
        rest = rest - piece.astype(F32)
    return pieces


def send_kernel(group_ref, x_ref, t_ref, scale_ref, shift_ref, w_ref, a_ref, msg_ref, stat_ref):
    step = pl.program_id(0)
    video, features = x_ref.shape
    text = t_ref.shape[0]
    columns = w_ref.shape[1]
    width = msg_ref.shape[1] - HEAD_DIM

    @pl.when(step == 0)
    def _():
        gain = 1.0 + scale_ref[...]

        def place(rows_ref, start):
            rows = rows_ref[...].astype(F32)
            count = rows.shape[0]
            mean = jnp.sum(rows, axis=1, keepdims=True) * (1.0 / features)
            centered = rows - mean
            second = jnp.sum(centered * centered, axis=1, keepdims=True)
            a_ref[start : start + count, :] = (centered * gain).astype(BF16)
            pieces = split_bf16(mean, 3) + split_bf16(second, 3)
            lane = lax.broadcasted_iota(jnp.int32, (count, HEAD_DIM), 1)
            packed = jnp.zeros((count, HEAD_DIM), F32)
            for index, piece in enumerate(pieces):
                packed = jnp.where(lane == index, piece.astype(F32), packed)
            msg_ref[start : start + count, width:] = packed.astype(BF16)
            own = jnp.where(lane == 0, mean, jnp.where(lane == 1, second, 0.0))
            stat_ref[start : start + count, :] = own

        place(x_ref, 0)
        place(t_ref, video)
        tail = a_ref.shape[0] - video - text
        pieces = split_bf16(gain, 2) + split_bf16(shift_ref[...], 2)
        row = lax.broadcasted_iota(jnp.int32, (tail, features), 0)
        extra = jnp.zeros((tail, features), F32)
        for index, piece in enumerate(pieces):
            extra = jnp.where(row == index, piece.astype(F32), extra)
        a_ref[video + text :, :] = extra.astype(BF16)
        msg_ref[video + text :, width:] = jnp.zeros((tail, HEAD_DIM), BF16)

    product = jnp.dot(a_ref[...], w_ref[...], preferred_element_type=F32)
    msg_ref[:, pl.ds(pl.multiple_of(step * columns, columns), columns)] = product.astype(BF16)


def own_kernel(group_ref, a_ref, w_ref, out_ref):
    out_ref[...] = jnp.dot(a_ref[...], w_ref[...], preferred_element_type=F32)


def norm_kernel(
    video, text, total_features, own_ref, msg_ref, stat_ref, mstat_ref, qg_ref, kg_ref,
    q_ref, cache_ref, text_ref,
):
    rows = video + text
    half = total_features // 2
    mean_own = stat_ref[:rows, 0:1]
    second_own = stat_ref[:rows, 1:2]
    received = mstat_ref[:rows, :].astype(F32)
    mean_other = received[:, 0:1] + received[:, 1:2] + received[:, 2:3]
    second_other = received[:, 3:4] + received[:, 4:5] + received[:, 5:6]
    gap = 0.5 * (mean_own - mean_other)
    var = (second_own + second_other) * (1.0 / total_features) + gap * gap
    inverse = lax.rsqrt(var + EPS)

    own = own_ref[...]
    other = msg_ref[...].astype(F32)
    scale_own = own[rows : rows + 1] + own[rows + 1 : rows + 2]
    scale_other = other[rows : rows + 1] + other[rows + 1 : rows + 2]
    shift = (own[rows + 2 : rows + 3] + own[rows + 3 : rows + 4]) + (
        other[rows + 2 : rows + 3] + other[rows + 3 : rows + 4]
    )
    total = (own[:rows] + other[:rows] + gap * (scale_own - scale_other)) * inverse + shift

    def head_norm(part, gain):
        square = jnp.sum(part * part, axis=1, keepdims=True) * (1.0 / HEAD_DIM)
        return part * lax.rsqrt(square + EPS) * gain

    q_ref[...] = head_norm(total[:video, :HEAD_DIM], qg_ref[...]).astype(BF16)
    keys = head_norm(total[:, HEAD_DIM : 2 * HEAD_DIM], kg_ref[...]).astype(BF16)
    values = total[:, 2 * HEAD_DIM :].astype(BF16)
    cache_ref[0] = keys[:video]
    cache_ref[1] = values[:video]
    text_ref[0] = keys[video:]
    text_ref[1] = values[video:]


def attention_kernel(
    chip_ref, qo_ref, qp_ref, stale_ref, cache_ref, text_ref, mask_ref, own_ref, msg_ref, own_den_ref,
):
    head = pl.program_id(0)
    blocks, _, video, depth = stale_ref.shape
    factor = math.log2(math.e) / math.sqrt(depth)
    contract = (((1,), (1,)), ((), ()))
    chip = chip_ref[0]

    queries = jnp.concatenate([qo_ref[...], qp_ref[...]], axis=0)
    lane = lax.broadcasted_iota(jnp.int32, (video, HEAD_DIM), 1)

    def weigh(rows, keys):
        scores = lax.dot_general(rows, keys, contract, preferred_element_type=F32)
        return jnp.exp2(scores * factor)

    def lanes(weights):
        total = weights[:, :HEAD_DIM]
        for start in range(HEAD_DIM, weights.shape[1], HEAD_DIM):
            total = total + weights[:, start : start + HEAD_DIM]
        return total

    def times(weights, values):
        return jnp.dot(weights.astype(BF16), values, preferred_element_type=F32)

    fresh = weigh(queries[:video], cache_ref[0])
    num_own = times(fresh, cache_ref[1])
    den_own = lanes(fresh)

    text_k = text_ref[:, 0].reshape(-1, depth)
    text_v = text_ref[:, 1].reshape(-1, depth)
    weights = weigh(queries, text_k) * mask_ref[...]
    num = times(weights, text_v)
    den = lanes(weights)

    keep_rows = lax.broadcasted_iota(jnp.int32, (2 * video, 1), 0) >= video
    for block in range(blocks):
        weights = weigh(queries, stale_ref[block, 0])
        keep = jnp.where(keep_rows | (chip != block), 1.0, 0.0)
        weights = weights * keep
        num = num + times(weights, stale_ref[block, 1])
        den = den + lanes(weights)

    den_own = jnp.sum(den_own + den[:video], axis=1, keepdims=True)
    den_other = jnp.sum(den[video:], axis=1, keepdims=True)
    columns = pl.ds(pl.multiple_of(head * depth, depth), depth)
    width = msg_ref.shape[1] - HEAD_DIM
    own_ref[:, columns] = num_own + num[:video]
    msg_ref[:, columns] = num[video:]

    @pl.when(head == 0)
    def _():
        own_den_ref[...] = jnp.zeros_like(own_den_ref)
        msg_ref[:, width:] = jnp.zeros((video, HEAD_DIM), F32)

    own_den_ref[...] = jnp.where(lane == head, den_own, own_den_ref[...])
    msg_ref[:, width:] = jnp.where(lane == head, den_other, msg_ref[:, width:])


def merge_kernel(group_ref, own_ref, den_ref, msg_ref, w_ref, att_ref, out_ref):
    width = att_ref.shape[1]
    for head in range(width // HEAD_DIM):
        columns = slice(head * HEAD_DIM, (head + 1) * HEAD_DIM)
        num = own_ref[:, columns] + msg_ref[:, columns]
        den = den_ref[:, head : head + 1] + msg_ref[:, width + head : width + head + 1]
        att_ref[:, columns] = (num / den).astype(BF16)
    out_ref[...] = jnp.dot(att_ref[...], w_ref[...], preferred_element_type=F32)


def final_kernel(group_ref, part_ref, att_ref, w_ref, hidden_ref, gate_ref, out_ref):
    total = part_ref[...] + jnp.dot(att_ref[...], w_ref[...], preferred_element_type=F32)
    out_ref[...] = (hidden_ref[...].astype(F32) + gate_ref[...] * total).astype(BF16)


def params(megabytes=48):
    return pltpu.CompilerParams(vmem_limit_bytes=megabytes * 1024 * 1024)


def cost(flops, nbytes, transcendentals=0):
    return pl.CostEstimate(flops=flops, bytes_accessed=nbytes, transcendentals=transcendentals)


def per_device(
    sections, hidden, text_hidden, text_mask, stale_cache, qkv_weight, out_weight, query_gain,
    key_gain, norm_shift, norm_scale, branch_gate,
):
    video, features = hidden.shape
    text_rows = text_hidden.shape[0]
    text = text_rows // sections
    text_pad = round_up(text, 16)
    width = stale_cache.shape[2]
    heads = width // HEAD_DIM
    group_columns = heads * TRIPLE
    chips = sections // 2
    out_features = out_weight.shape[1]
    rows = video + text_pad
    padded = rows + 16

    section = lax.axis_index("section")
    group = lax.axis_index("head").astype(jnp.int32).reshape(1)
    core = section % 2
    chip = (section // 2).astype(jnp.int32).reshape(1)
    same_core = [list(range(c, sections, 2)) for c in range(2)]
    swap_core = [(s, s ^ 1) for s in range(sections)]
    swap_head = [(0, 1), (1, 0)]

    stale = lax.all_gather(
        stale_cache.reshape(2 * video, width), "section", axis=0, tiled=True,
        axis_index_groups=same_core,
    ).reshape(chips, 2, video, width)

    own_text = lax.dynamic_slice_in_dim(text_hidden, section * text, text, 0)
    mask = lax.dynamic_index_in_dim(text_mask.reshape(chips, 2, text), core, 1, keepdims=False)
    if text_pad != text:
        own_text = jnp.pad(own_text, ((0, text_pad - text), (0, 0)))
        mask = jnp.pad(mask, ((0, 0), (0, text_pad - text)))
    mask = mask.astype(F32).reshape(1, chips * text_pad)

    vmem_full = lambda *shape: pl.BlockSpec(shape, lambda h, *_: (0,) * len(shape))
    weight_bytes = features * group_columns * 2
    project_flops = 2 * padded * features * group_columns
    a_rows, message, stats = pl.pallas_call(
        send_kernel,
        grid_spec=pltpu.PrefetchScalarGridSpec(
            num_scalar_prefetch=1,
            grid=(heads,),
            in_specs=[
                vmem_full(video, features),
                vmem_full(text_pad, features),
                vmem_full(1, features),
                vmem_full(1, features),
                pl.BlockSpec((features, TRIPLE), lambda h, g: (0, (1 - g[0]) * heads + h)),
            ],
            out_specs=[
                vmem_full(padded, features),
                vmem_full(padded, group_columns + HEAD_DIM),
                vmem_full(rows, HEAD_DIM),
            ],
        ),
        out_shape=[
            jax.ShapeDtypeStruct((padded, features), BF16),
            jax.ShapeDtypeStruct((padded, group_columns + HEAD_DIM), BF16),
            jax.ShapeDtypeStruct((rows, HEAD_DIM), F32),
        ],
        compiler_params=params(),
        cost_estimate=cost(project_flops, weight_bytes),
        name="project_send",
    )(group, hidden, own_text, norm_scale.reshape(1, -1), norm_shift.reshape(1, -1), qkv_weight)

    received = lax.ppermute(message, "head", swap_head)

    own = pl.pallas_call(
        own_kernel,
        grid_spec=pltpu.PrefetchScalarGridSpec(
            num_scalar_prefetch=1,
            grid=(heads,),
            in_specs=[
                vmem_full(padded, features),
                pl.BlockSpec((features, TRIPLE), lambda h, g: (0, g[0] * heads + h)),
            ],
            out_specs=pl.BlockSpec((padded, TRIPLE), lambda h, g: (0, h)),
        ),
        out_shape=jax.ShapeDtypeStruct((padded, group_columns), F32),
        compiler_params=params(),
        cost_estimate=cost(project_flops, weight_bytes),
        name="project_own",
    )(group, a_rows, qkv_weight)

    queries, new_cache, text_kv = pl.pallas_call(
        functools.partial(norm_kernel, video, text_pad, features * 2),
        grid=(heads,),
        in_specs=[
            pl.BlockSpec((padded, TRIPLE), lambda h: (0, h)),
            pl.BlockSpec((padded, TRIPLE), lambda h: (0, h)),
            vmem_full(rows, HEAD_DIM),
            pl.BlockSpec((padded, HEAD_DIM), lambda h: (0, 3 * heads)),
            vmem_full(1, HEAD_DIM),
            vmem_full(1, HEAD_DIM),
        ],
        out_specs=[
            pl.BlockSpec((video, HEAD_DIM), lambda h: (0, h)),
            pl.BlockSpec((2, video, HEAD_DIM), lambda h: (0, 0, h)),
            pl.BlockSpec((2, text_pad, HEAD_DIM), lambda h: (0, 0, h)),
        ],
        out_shape=[
            jax.ShapeDtypeStruct((video, width), BF16),
            jax.ShapeDtypeStruct((2, video, width), BF16),
            jax.ShapeDtypeStruct((2, text_pad, width), BF16),
        ],
        compiler_params=params(),
        cost_estimate=cost(20 * rows * group_columns, 6 * padded * group_columns),
        name="norm_heads",
    )(own, received, stats, received, query_gain.reshape(1, -1), key_gain.reshape(1, -1))

    other_queries = lax.ppermute(queries, "section", swap_core)
    text_all = lax.all_gather(
        text_kv.reshape(2 * text_pad, width), "section", axis=0, tiled=True,
        axis_index_groups=same_core,
    ).reshape(chips, 2, text_pad, width)

    context = chips * (video + text_pad) + video
    num_own, num_message, den_own = pl.pallas_call(
        attention_kernel,
        grid_spec=pltpu.PrefetchScalarGridSpec(
            num_scalar_prefetch=1,
            grid=(heads,),
            in_specs=[
                pl.BlockSpec((video, HEAD_DIM), lambda h, c: (0, h)),
                pl.BlockSpec((video, HEAD_DIM), lambda h, c: (0, h)),
                pl.BlockSpec((chips, 2, video, HEAD_DIM), lambda h, c: (0, 0, 0, h)),
                pl.BlockSpec((2, video, HEAD_DIM), lambda h, c: (0, 0, h)),
                pl.BlockSpec((chips, 2, text_pad, HEAD_DIM), lambda h, c: (0, 0, 0, h)),
                vmem_full(1, chips * text_pad),
            ],
            out_specs=[
                vmem_full(video, width),
                vmem_full(video, width + HEAD_DIM),
                vmem_full(video, HEAD_DIM),
            ],
        ),
        out_shape=[
            jax.ShapeDtypeStruct((video, width), F32),
            jax.ShapeDtypeStruct((video, width + HEAD_DIM), F32),
            jax.ShapeDtypeStruct((video, HEAD_DIM), F32),
        ],
        compiler_params=params(),
        cost_estimate=cost(8 * video * context * width, 4 * context * width, 2 * video * context * heads),
        name="attend",
    )(chip, queries, other_queries, stale, new_cache, text_all, mask)

    num_received = lax.ppermute(num_message, "section", swap_core)

    attended, part = pl.pallas_call(
        merge_kernel,
        grid_spec=pltpu.PrefetchScalarGridSpec(
            num_scalar_prefetch=1,
            grid=(1,),
            in_specs=[
                vmem_full(video, width),
                vmem_full(video, HEAD_DIM),
                vmem_full(video, width + HEAD_DIM),
                pl.BlockSpec((width, out_features), lambda h, g: (g[0], 0)),
            ],
            out_specs=[vmem_full(video, width), vmem_full(video, out_features)],
        ),
        out_shape=[
            jax.ShapeDtypeStruct((video, width), BF16),
            jax.ShapeDtypeStruct((video, out_features), F32),
        ],
        compiler_params=params(),
        cost_estimate=cost(2 * video * width * out_features, 2 * width * out_features),
        name="merge_out",
    )(group, num_own, den_own, num_received, out_weight)

    other_attended = lax.ppermute(attended, "head", swap_head)

    mixed = pl.pallas_call(
        final_kernel,
        grid_spec=pltpu.PrefetchScalarGridSpec(
            num_scalar_prefetch=1,
            grid=(1,),
            in_specs=[
                vmem_full(video, out_features),
                vmem_full(video, width),
                pl.BlockSpec((width, out_features), lambda h, g: (1 - g[0], 0)),
                vmem_full(video, features),
                vmem_full(1, features),
            ],
            out_specs=vmem_full(video, out_features),
        ),
        out_shape=jax.ShapeDtypeStruct((video, out_features), BF16),
        compiler_params=params(),
        cost_estimate=cost(2 * video * width * out_features, 2 * width * out_features),
        name="final_out",
    )(group, part, other_attended, out_weight, hidden, branch_gate.reshape(1, -1))
    return (mixed, new_cache)


def solution(mesh):
    in_specs = (
        P("section", "head"),
        P(None, "head"),
        P(),
        P(None, "section", "head"),
        P("head", None),
        P(None, "head"),
        P(),
        P(),
        P("head"),
        P("head"),
        P("head"),
    )
    out_specs = (P("section", "head"), P(None, "section", "head"))
    return jax.shard_map(
        functools.partial(per_device, mesh.shape["section"]),
        mesh=mesh, in_specs=in_specs, out_specs=out_specs, check_vma=False,
    )
```

time: 175 us -> 112 us (0.64)
  local copies, waits for them, and re-layouts: 51.1 us -> 7.82 us
  waiting for transfers between devices: 58.6 us -> 27.2 us
  matrix products: 27.2 us -> 0 us
  Pallas kernels: 0 us -> 24.8 us
  blocking collectives: 13.1 us -> 32.5 us
  other arithmetic: 7.92 us -> 0.02 us
  starting transfers between devices: 0.08 us -> 4.61 us
    reduce_scatter x1 -> x0, waiting for transfers between devices: 28.2 us -> none  [per_device(): lax.psum_scatter(jnp.einsum('rd,dhc->hrc', normed, columns, preferred_ele...]
    dot_general x10 -> x0, matrix products: 27.2 us -> none  [the longest x1 11 us: per_device(): jnp.einsum('rd,dhc->hrc', normed, columns, preferred_element_type=jnp.flo...]
    all_gather x1, blocking collectives: 7.21 us -> 32.5 us  [per_device(): lax.all_gather(text_kv.reshape(2 * text_pad, width), 'section', axis=0, t...]
    unnamed x32 -> x20, local copies, waits for them, and re-layouts: 31.1 us -> 6.24 us
    pallas_call x0 -> x6, Pallas kernels: none -> 24.8 us  [the longest x1 6.09 us: per_device(): pl.pallas_call(send_kernel, grid_spec=pltpu.PrefetchScalarGridSpec(num_sc...]
    all_gather x1, waiting for transfers between devices: 29.7 us -> 7.75 us  [per_device(): lax.all_gather(stale_cache.reshape(2 * video, width), 'section', axis=0,...]
    ppermute x0 -> x4, waiting for transfers between devices: none -> 18.8 us  [the longest x1 11.5 us: per_device(): received = lax.ppermute(message, 'head', swap_head)]
    another operation x2 -> x0, local copies, waits for them, and re-layouts: 12.4 us -> none  [the longest x1 7.75 us: context_terms(): value_rows.reshape(block_count, block_rows, head_count, head_depth)]
  transfers between devices with their start and end apart: 2 -> 5, of which waited for: 2 -> 4; matrix products, arithmetic and copies ran while one was open for 34% -> 1% of each run, Pallas kernels for 0% -> 14%
where the time goes in v1:
time: 112 us; the launch traced here: 111 us
  blocking collectives  32.5 us (29%)
  waiting for transfers between devices  27.2 us (24%)
  Pallas kernels  24.8 us (22%)
  between operations  14.1 us (13%)
  local copies, waits for them, and re-layouts  7.82 us (7%)
  starting transfers between devices  4.61 us (4%)
    all_gather x1, blocking collectives, per_device(): lax.all_gather(text_kv.reshape(2 * text_pad, width), 'section', axis=0, t...  32.5 us
    ppermute x1, waiting for transfers between devices, per_device(): received = lax.ppermute(message, 'head', swap_head)  11.5 us
    all_gather x1, waiting for transfers between devices, per_device(): lax.all_gather(stale_cache.reshape(2 * video, width), 'section', axis=0,...  7.75 us
    unnamed x20, local copies, waits for them, and re-layouts  6.24 us
    pallas_call x1, Pallas kernels, per_device(): pl.pallas_call(send_kernel, grid_spec=pltpu.PrefetchScalarGridSpec(num_sc...  6.09 us
    pallas_call x1, Pallas kernels, per_device(): pl.pallas_call(own_kernel, grid_spec=pltpu.PrefetchScalarGridSpec(num_sca...  5.89 us
    pallas_call x1, Pallas kernels, per_device(): pl.pallas_call(attention_kernel, grid_spec=pltpu.PrefetchScalarGridSpec(n...  5.62 us
    ppermute x1, waiting for transfers between devices, per_device(): other_attended = lax.ppermute(attended, 'head', swap_head)  5.5 us
  transfers between devices with their start and end apart: 5, of which 4 were waited for; matrix products, arithmetic and copies ran while one was open for 1% of the time, Pallas kernels for 14%

profile of v1, /device:TPU:0, one launch (start us, length us, event | category | flops | bytes accessed | tf_op | source)
XLA Modules:
  0.0 111.0 jit_solution(14979912218445532207)
XLA Ops:
  7.2 0.0 all-gather.2.cloned.1.call-start
  7.2 0.7 all-gather.2.cloned.1.call-update
  7.9 0.7 reshape.54.scale_ref
  8.6 0.7 reshape.55.shift_ref
  9.3 1.0 copy-done.3
  10.3 6.1 %project_send.1 = (bf16[160,1536]{1,0:T(8,128)(2,1)S(1)}, bf16[160,2432]{1,0:T(8,128)(2,1)S(1)}, f32[144,128]{1,0:T(8,128)S(1)}) custom-call(s32[1]{0:T(128)} %bitcast.group_ref, bf16[128,1536]{1,0:T(8,128)(2,1)S(1)} %copy-done.3, bf16[16,1536]{1,0:T(8,128)(2,1)S(1)} %constant_dynamic-slice_fusion.t_ref, f32[1,1536]{1,0:T(1,128)S(1)} %reshape.54.scale_ref, ...), custom_call_target="tpu_custom_call" | custom-call | flops 1132462080 | bytes 7077888 | tf_op jit(solution)/shard_map/project_send/pallas_call | solution.py:236
  16.4 3.0 %collective-permute-start = (bf16[160,2432]{1,0:T(8,128)(2,1)S(1)}, bf16[160,2432]{1,0:T(8,128)(2,1)S(1)}, u32[]{:S(2)}, u32[]{:S(2)}) collective-permute-start(bf16[160,2432]{1,0:T(8,128)(2,1)S(1)} %get-tuple-element.14), channel_id=1, source_target_pairs={{0,1},{1,0},{2,3},{3,2},{4,5},{5,4},{6,7},{7,6},{8,9},{9,8},{10,11... | collective-permute-start | bytes 2334728 | tf_op jit(solution)/shard_map/ppermute | solution.py:264
  19.4 5.9 %project_own.1.own_ref = f32[160,2304]{1,0:T(8,128)S(1)} custom-call(s32[1]{0:T(128)} %bitcast.group_ref, bf16[160,1536]{1,0:T(8,128)(2,1)S(1)} %get-tuple-element.13.a_ref, bf16[1536,4608]{1,0:T(8,128)(2,1)} %w_ref.5), custom_call_target="tpu_custom_call" | custom-call | flops 1132462080 | bytes 7077888 | tf_op jit(solution)/shard_map/project_own/pallas_call | solution.py:266
  25.3 11.5 %collective-permute-done.msg_ref.mstat_ref = bf16[160,2432]{1,0:T(8,128)(2,1)S(1)} collective-permute-done((bf16[160,2432]{1,0:T(8,128)(2,1)S(1)}, bf16[160,2432]{1,0:T(8,128)(2,1)S(1)}, u32[]{:S(2)}, u32[]{:S(2)}) %collective-permute-start) | collective-permute-done | bytes 778272 | tf_op jit(solution)/shard_map/ppermute | solution.py:264
  36.8 3.7 %norm_heads.1 = (bf16[128,768]{1,0:T(8,128)(2,1)S(1)}, bf16[2,128,768]{2,1,0:T(8,128)(2,1)}, bf16[2,16,768]{2,1,0:T(8,128)(2,1)S(1)}) custom-call(f32[160,2304]{1,0:T(8,128)S(1)} %project_own.1.own_ref, bf16[160,2432]{1,0:T(8,128)(2,1)S(1)} %collective-permute-done.msg_ref.mstat_ref, f32[144,128]{1,0:T(8,128)S(1)} %get-tuple-element.15.stat_ref, ...), custom_call_target="tpu_custom_call" | custom-call | flops 6635520 | bytes 2211840 | tf_op jit(solution)/shard_map/norm_heads/pallas_call | solution.py:283
  40.5 0.1 reshape.62
  40.6 0.1 convert_element_type.14.mask_ref
  40.7 32.5 %all_gather.7 = bf16[256,768]{1,0:T(8,128)(2,1)S(1)} all-gather(bf16[32,768]{1,0:T(8,128)(2,1)S(1)} %bitcast.10), channel_id=1, replica_groups={{0,4,8,12,16,20,24,28},{2,6,10,14,18,22,26,30},{1,5,9,13,17,21,25,29},{..., dimensions={0}, use_global_device_ids=true | all-gather | bytes 442368 | tf_op jit(solution)/shard_map/all_gather | solution.py:310
  73.2 7.8 %all-gather.2.cloned.1.call-done = bf16[2048,768]{1,0:T(8,128)(2,1)} async-done(((bf16[256,768]{1,0:T(8,128)(2,1)}), bf16[2048,768]{1,0:T(8,128)(2,1)}) %all-gather.2.cloned.1.call-update) | async-done | bytes 3145744 | tf_op jit(solution)/shard_map/all_gather | solution.py:221
  80.9 1.9 %copy-done.2 = bf16[2048,768]{1,0:T(8,128)(2,1)S(1)} copy-done((bf16[2048,768]{1,0:T(8,128)(2,1)S(1)}, bf16[2048,768]{1,0:T(8,128)(2,1)}, u32[]{:S(2)}) %copy-start.2) | copy-done | bytes 3145752
  82.8 1.0 copy-done.5
  83.8 5.6 %attend.1 = (f32[128,768]{1,0:T(8,128)S(1)}, f32[128,896]{1,0:T(8,128)S(1)}, f32[128,128]{1,0:T(8,128)S(1)}) custom-call(s32[1]{0:T(128)} %bitcast.1.chip_ref, bf16[128,768]{1,0:T(8,128)(2,1)S(1)} %get-tuple-element.16.qo_ref, bf16[128,768]{1,0:T(8,128)(2,1)S(1)} %collective-permute-done.1.qp_ref, bf16[8,2,128,768]{3,2,1,0:T(8,128)(2,1)S(1)} %bitcast.8, ...), custom_call_target="tpu_custom_call" | custom-call | flops 1006632960 | bytes 3932160 | tf_op jit(solution)/shard_map/attend/pallas_call | solution.py:316
  89.4 0.1 collective-permute-start.2
  89.5 1.8 %collective-permute-done.2.msg_ref = f32[128,896]{1,0:T(8,128)S(1)} collective-permute-done((f32[128,896]{1,0:T(8,128)S(1)}, f32[128,896]{1,0:T(8,128)S(1)}, u32[]{:S(2)}, u32[]{:S(2)}) %collective-permute-start.2) | collective-permute-done | bytes 458784 | tf_op jit(solution)/shard_map/ppermute | solution.py:345
  91.3 2.3 %merge_out.1 = (bf16[128,768]{1,0:T(8,128)(2,1)S(1)}, f32[128,1536]{1,0:T(8,128)S(1)}) custom-call(s32[1]{0:T(128)} %bitcast.group_ref, f32[128,768]{1,0:T(8,128)S(1)} %get-tuple-element.19.own_ref, f32[128,128]{1,0:T(8,128)S(1)} %get-tuple-element.20.den_ref, f32[128,896]{1,0:T(8,128)S(1)} %collective-permute-done.2.msg_ref, bf16[1536,1536]{1,0:T(8,128)(2,1)} %w_ref.7), custom_call_target="tpu_custom_call" | custom-call | flops 301989888 | bytes 2359296 | tf_op jit(solution)/shard_map/merge_out/pallas_call | solution.py:347
  93.6 1.5 %collective-permute-start.3 = (bf16[128,768]{1,0:T(8,128)(2,1)S(1)}, bf16[128,768]{1,0:T(8,128)(2,1)S(1)}, u32[]{:S(2)}, u32[]{:S(2)}) collective-permute-start(bf16[128,768]{1,0:T(8,128)(2,1)S(1)} %get-tuple-element.23), channel_id=1, source_target_pairs={{0,1},{1,0},{2,3},{3,2},{4,5},{5,4},{6,7},{7,6},{8,9},{9,8},{10,11... | collective-permute-start | bytes 589832 | tf_op jit(solution)/shard_map/ppermute | solution.py:369
  95.1 5.5 %collective-permute-done.3.att_ref = bf16[128,768]{1,0:T(8,128)(2,1)S(1)} collective-permute-done((bf16[128,768]{1,0:T(8,128)(2,1)S(1)}, bf16[128,768]{1,0:T(8,128)(2,1)S(1)}, u32[]{:S(2)}, u32[]{:S(2)}) %collective-permute-start.3) | collective-permute-done | bytes 196640 | tf_op jit(solution)/shard_map/ppermute | solution.py:369
  100.6 2.3 %copy-done.1 = bf16[1536,1536]{1,0:T(8,128)(2,1)S(1)} copy-done((bf16[1536,1536]{1,0:T(8,128)(2,1)S(1)}, bf16[1536,1536]{1,0:T(8,128)(2,1)}, u32[]{:S(2)}) %copy-start.1) | copy-done | bytes 4718616
  103.0 1.2 %final_out.1 = bf16[128,1536]{1,0:T(8,128)(2,1)} custom-call(s32[1]{0:T(128)} %bitcast.group_ref, f32[128,1536]{1,0:T(8,128)S(1)} %get-tuple-element.22.part_ref, bf16[128,768]{1,0:T(8,128)(2,1)S(1)} %collective-permute-done.3.att_ref, bf16[1536,1536]{1,0:T(8,128)(2,1)S(1)} %copy-done.1, bf16[128,1536]{1,0:T(8,128)(2,1)S(1)} %copy-done.4, ...), custom_call_target="tpu_custom_call" | custom-call | flops 301989888 | bytes 2359296 | tf_op jit(solution)/shard_map/final_out/pallas_call | solution.py:371
  (21 shorter events, 0.1 us)
Async XLA Ops:
  7.2 2.2 %copy-start = (bf16[256,1536]{1,0:T(8,128)(2,1)S(1)}, bf16[256,1536]{1,0:T(8,128)(2,1)}, u32[]{:S(2)}) copy-start(bf16[256,1536]{1,0:T(8,128)(2,1)} %param.12) | copy-start | bytes 2359300
  7.2 73.7 %all-gather.2.cloned.1.call-start = ((), (), s32[]{:S(2)}) async-start(), calls=%async_computation | async-start | bytes 3538944 | tf_op jit(solution)/shard_map/all_gather | solution.py:221
  9.3 1.0 copy-start.3
  16.4 20.4 %collective-permute-start = (bf16[160,2432]{1,0:T(8,128)(2,1)S(1)}, bf16[160,2432]{1,0:T(8,128)(2,1)S(1)}, u32[]{:S(2)}, u32[]{:S(2)}) collective-permute-start(bf16[160,2432]{1,0:T(8,128)(2,1)S(1)} %get-tuple-element.14), channel_id=1, source_target_pairs={{0,1},{1,0},{2,3},{3,2},{4,5},{5,4},{6,7},{7,6},{8,9},{9,8},{10,11... | collective-permute-start | bytes 2334728 | tf_op jit(solution)/shard_map/ppermute | solution.py:264
  19.4 17.4 %copy-start.6 = (f32[128]{0:T(128)S(1)}, f32[128]{0:T(128)}, u32[]{:S(2)}) copy-start(f32[128]{0:T(128)} %param.17) | copy-start | bytes 1540
  19.4 17.4 %copy-start.7 = (f32[128]{0:T(128)S(1)}, f32[128]{0:T(128)}, u32[]{:S(2)}) copy-start(f32[128]{0:T(128)} %param.18) | copy-start | bytes 1540
  19.4 21.1 %copy-start.9 = (s32[256]{0:T(256)S(1)}, s32[256]{0:T(256)}, u32[]{:S(2)}) copy-start(s32[256]{0:T(256)} %param.13) | copy-start | bytes 3076
  40.5 32.7 %collective-permute-start.1 = (bf16[128,768]{1,0:T(8,128)(2,1)S(1)}, bf16[128,768]{1,0:T(8,128)(2,1)S(1)}, u32[]{:S(2)}, u32[]{:S(2)}) collective-permute-start(bf16[128,768]{1,0:T(8,128)(2,1)S(1)} %get-tuple-element.16.qo_ref), channel_id=1, source_target_pairs={{0,2},{2,0},{4,6},{6,4},{8,10},{10,8},{12,14},{14,12},{16,18},{18,... | collective-permute-start | bytes 589832 | tf_op jit(solution)/shard_map/ppermute | solution.py:309
  80.9 1.9 %copy-start.2 = (bf16[2048,768]{1,0:T(8,128)(2,1)S(1)}, bf16[2048,768]{1,0:T(8,128)(2,1)}, u32[]{:S(2)}) copy-start(bf16[2048,768]{1,0:T(8,128)(2,1)} %all-gather.2.cloned.1.call-done) | copy-start | bytes 9437188
  82.8 1.0 copy-start.5
  83.8 11.3 %copy-start.8 = (f32[1536]{0:T(1024)S(1)}, f32[1536]{0:T(1024)}, u32[]{:S(2)}) copy-start(f32[1536]{0:T(1024)} %param.21) | copy-start | bytes 18436
  83.8 16.8 %copy-start.4 = (bf16[128,1536]{1,0:T(8,128)(2,1)S(1)}, bf16[128,1536]{1,0:T(8,128)(2,1)}, u32[]{:S(2)}) copy-start(bf16[128,1536]{1,0:T(8,128)(2,1)} %hidden_ref.1) | copy-start | bytes 1179652
  89.4 1.9 %collective-permute-start.2 = (f32[128,896]{1,0:T(8,128)S(1)}, f32[128,896]{1,0:T(8,128)S(1)}, u32[]{:S(2)}, u32[]{:S(2)}) collective-permute-start(f32[128,896]{1,0:T(8,128)S(1)} %get-tuple-element.21), channel_id=1, source_target_pairs={{0,2},{2,0},{4,6},{6,4},{8,10},{10,8},{12,14},{14,12},{16,18},{18,... | collective-permute-start | bytes 1376264 | tf_op jit(solution)/shard_map/ppermute | solution.py:345
  93.6 7.0 %collective-permute-start.3 = (bf16[128,768]{1,0:T(8,128)(2,1)S(1)}, bf16[128,768]{1,0:T(8,128)(2,1)S(1)}, u32[]{:S(2)}, u32[]{:S(2)}) collective-permute-start(bf16[128,768]{1,0:T(8,128)(2,1)S(1)} %get-tuple-element.23), channel_id=1, source_target_pairs={{0,1},{1,0},{2,3},{3,2},{4,5},{5,4},{6,7},{7,6},{8,9},{9,8},{10,11... | collective-permute-start | bytes 589832 | tf_op jit(solution)/shard_map/ppermute | solution.py:369
  100.6 2.3 %copy-start.1 = (bf16[1536,1536]{1,0:T(8,128)(2,1)S(1)}, bf16[1536,1536]{1,0:T(8,128)(2,1)}, u32[]{:S(2)}) copy-start(bf16[1536,1536]{1,0:T(8,128)(2,1)} %w_ref.7) | copy-start | bytes 14155780
Sparse Core Ops, SparseCore 0:
  10.2 70.6 all-gather.1

commit v2 on v0

v2 whole, which is shorter than its diff:
```python
import functools
import math

import jax
import jax.numpy as jnp
from jax import lax
from jax.experimental import pallas as pl
from jax.experimental.pallas import tpu as pltpu
from jax.sharding import PartitionSpec as P

HEAD_DIM = 128
TRIPLE = 3 * HEAD_DIM
EXTRA = 16
EPS = 1e-06
F32 = jnp.float32
BF16 = jnp.bfloat16


def split_bf16(value, parts):
    pieces = []
    rest = value
    for _ in range(parts):
        piece = rest.astype(BF16)
        pieces.append(piece)
        rest = rest - piece.astype(F32)
    return pieces


def send_kernel(
    place_ref, x_ref, t_ref, scale_ref, shift_ref, w_ref, a_ref, msg_ref, tmsg_ref, stat_ref,
):
    step = pl.program_id(0)
    video, features = x_ref.shape
    text = t_ref.shape[0]
    top = video + EXTRA
    columns = w_ref.shape[1]
    width = msg_ref.shape[1] - HEAD_DIM
    twidth = tmsg_ref.shape[1] - HEAD_DIM

    @pl.when(step == 0)
    def _():
        gain = 1.0 + scale_ref[...]

        def place(rows_ref, start):
            rows = rows_ref[...].astype(F32)
            count = rows.shape[0]
            mean = jnp.sum(rows, axis=1, keepdims=True) * (1.0 / features)
            centered = rows - mean
            second = jnp.sum(centered * centered, axis=1, keepdims=True)
            a_ref[start : start + count, :] = (centered * gain).astype(BF16)
            pieces = split_bf16(mean, 3) + split_bf16(second, 3)
            lane = lax.broadcasted_iota(jnp.int32, (count, HEAD_DIM), 1)
            packed = jnp.zeros((count, HEAD_DIM), F32)
            for index, piece in enumerate(pieces):
                packed = jnp.where(lane == index, piece.astype(F32), packed)
            stat_ref[start : start + count, :] = jnp.where(
                lane == 0, mean, jnp.where(lane == 1, second, 0.0)
            )
            return packed.astype(BF16)

        msg_ref[:video, width:] = place(x_ref, 0)
        tmsg_ref[:, twidth:] = place(t_ref, top)
        pieces = split_bf16(gain, 2) + split_bf16(shift_ref[...], 2)
        row = lax.broadcasted_iota(jnp.int32, (EXTRA, features), 0)
        extra = jnp.zeros((EXTRA, features), F32)
        for index, piece in enumerate(pieces):
            extra = jnp.where(row == index, piece.astype(F32), extra)
        a_ref[video:top, :] = extra.astype(BF16)
        msg_ref[video:, width:] = jnp.zeros((EXTRA, HEAD_DIM), BF16)
        stat_ref[video:top, :] = jnp.zeros((EXTRA, HEAD_DIM), F32)

    product = jnp.dot(a_ref[...], w_ref[...], preferred_element_type=F32)
    msg_ref[:, pl.ds(pl.multiple_of(step * columns, columns), columns)] = product[:top].astype(BF16)
    heads = columns // TRIPLE
    for index in range(heads):
        start = pl.multiple_of((step * heads + index) * 2 * HEAD_DIM, 2 * HEAD_DIM)
        tmsg_ref[:, pl.ds(start, 2 * HEAD_DIM)] = product[
            top:, index * TRIPLE + HEAD_DIM : (index + 1) * TRIPLE
        ].astype(BF16)


def own_kernel(place_ref, a_ref, w_ref, out_ref, text_ref):
    top = out_ref.shape[0]
    product = jnp.dot(a_ref[...], w_ref[...], preferred_element_type=F32)
    out_ref[...] = product[:top]
    for index in range(w_ref.shape[1] // TRIPLE):
        text_ref[:, index * 2 * HEAD_DIM : (index + 1) * 2 * HEAD_DIM] = product[
            top:, index * TRIPLE + HEAD_DIM : (index + 1) * TRIPLE
        ]


def row_stats(total_features, own, received):
    received = received.astype(F32)
    mean_other = received[:, 0:1] + received[:, 1:2] + received[:, 2:3]
    second_other = received[:, 3:4] + received[:, 4:5] + received[:, 5:6]
    gap = 0.5 * (own[:, 0:1] - mean_other)
    var = (own[:, 1:2] + second_other) * (1.0 / total_features) + gap * gap
    return gap, lax.rsqrt(var + EPS)


def column_terms(own, other):
    other = other.astype(F32)
    scale = (own[0:1] + own[1:2]) - (other[0:1] + other[1:2])
    shift = (own[2:3] + own[3:4]) + (other[2:3] + other[3:4])
    return scale, shift


def head_norm(part, gain):
    square = jnp.sum(part * part, axis=1, keepdims=True) * (1.0 / HEAD_DIM)
    return part * lax.rsqrt(square + EPS) * gain


def norm_kernel(
    total_features, own_ref, msg_ref, stat_ref, qg_ref, kg_ref, q_ref, cache_ref, kv_ref,
):
    video = q_ref.shape[0]
    heads = q_ref.shape[1] // HEAD_DIM
    gap, inverse = row_stats(
        total_features, stat_ref[:video, :], msg_ref[:video, heads * TRIPLE :]
    )
    for head in range(heads):
        part = slice(head * TRIPLE, (head + 1) * TRIPLE)
        columns = slice(head * HEAD_DIM, (head + 1) * HEAD_DIM)
        scale, shift = column_terms(own_ref[video:, part], msg_ref[video:, part])
        total = own_ref[:video, part] + msg_ref[:video, part].astype(F32)
        total = (total + gap * scale) * inverse + shift
        q_ref[:, columns] = head_norm(total[:, :HEAD_DIM], qg_ref[...]).astype(BF16)
        keys = head_norm(total[:, HEAD_DIM : 2 * HEAD_DIM], kg_ref[...]).astype(BF16)
        values = total[:, 2 * HEAD_DIM :].astype(BF16)
        cache_ref[0, :, columns] = keys
        cache_ref[1, :, columns] = values
        kv_ref[0, :, columns] = keys
        kv_ref[1, :, columns] = values


def text_kernel(
    total_features, own_ref, msg_ref, stat_ref, top_ref, tmsg_ref, kg_ref, kv_ref,
):
    heads = kv_ref.shape[2] // HEAD_DIM
    top = top_ref.shape[0]
    video = top - EXTRA
    gap, inverse = row_stats(
        total_features, stat_ref[top:, :], tmsg_ref[:, heads * 2 * HEAD_DIM :]
    )
    for head in range(heads):
        part = slice(head * TRIPLE + HEAD_DIM, (head + 1) * TRIPLE)
        pair = slice(head * 2 * HEAD_DIM, (head + 1) * 2 * HEAD_DIM)
        columns = slice(head * HEAD_DIM, (head + 1) * HEAD_DIM)
        scale, shift = column_terms(top_ref[video:, part], msg_ref[video:, part])
        total = own_ref[:, pair] + tmsg_ref[:, pair].astype(F32)
        total = (total + gap * scale) * inverse + shift
        kv_ref[0, :, columns] = head_norm(total[:, :HEAD_DIM], kg_ref[...]).astype(BF16)
        kv_ref[1, :, columns] = total[:, HEAD_DIM:].astype(BF16)


FACTOR = math.log2(math.e) / math.sqrt(HEAD_DIM)


def weigh(rows, keys):
    scores = lax.dot_general(rows, keys, (((1,), (1,)), ((), ())), preferred_element_type=F32)
    return jnp.exp2(scores * FACTOR)


def lanes(weights):
    total = weights[:, :HEAD_DIM]
    for start in range(HEAD_DIM, weights.shape[1], HEAD_DIM):
        total = total + weights[:, start : start + HEAD_DIM]
    return total


def times(weights, values):
    return jnp.dot(weights.astype(BF16), values, preferred_element_type=F32)


def absorb(queries, blocks, num, den, columns):
    for first in range(0, len(blocks), 2):
        pair = blocks[first : first + 2]
        keys = jnp.concatenate([k(columns) for k, _ in pair], axis=0)
        values = jnp.concatenate([v(columns) for _, v in pair], axis=0)
        weights = weigh(queries, keys)
        num = num + times(weights, values)
        den = den + lanes(weights)
    return num, den


def loaders(ref):
    return (lambda columns: ref[0, :, columns]), (lambda columns: ref[1, :, columns])


def first_kernel(
    count, group_ref, weight_ref, qo_ref, qp_ref, fresh_ref, stale_ref, text_ref, mask_ref, *refs
):
    ring = refs[:count]
    num_ref, den_ref, w_own_ref, w_other_ref, sems = refs[count:]
    depth = w_own_ref.shape[0]
    group = group_ref[0]
    copies = []
    for index, (half, target) in enumerate(((group, w_own_ref), (1 - group, w_other_ref))):
        source = weight_ref.at[pl.ds(pl.multiple_of(half * depth, depth), depth)]
        copies.append(pltpu.make_async_copy(source, target, sems.at[index]))
    for copy in copies:
        copy.start()
    video, width = qo_ref.shape
    lane = lax.broadcasted_iota(jnp.int32, (2 * video, HEAD_DIM), 1)
    packed = jnp.zeros((2 * video, HEAD_DIM), F32)
    for head in range(width // HEAD_DIM):
        columns = slice(head * HEAD_DIM, (head + 1) * HEAD_DIM)
        own, other = qo_ref[:, columns], qp_ref[:, columns]
        queries = jnp.concatenate([own, other], axis=0)
        fresh = weigh(own, fresh_ref[0, :, columns])
        stale = weigh(other, stale_ref[0, :, columns])
        num = jnp.concatenate(
            [times(fresh, fresh_ref[1, :, columns]), times(stale, stale_ref[1, :, columns])], axis=0
        )
        den = jnp.concatenate([fresh, stale], axis=0)
        weights = weigh(queries, text_ref[0, :, columns]) * mask_ref[...]
        num = num + times(weights, text_ref[1, :, columns])
        den = den + lanes(weights)
        num, den = absorb(queries, [loaders(ref) for ref in ring], num, den, columns)
        num_ref[:, columns] = num
        packed = jnp.where(lane == head, jnp.sum(den, axis=1, keepdims=True), packed)
    den_ref[...] = packed
    for copy in copies:
        copy.wait()


def last_kernel(qo_ref, qp_ref, num_ref, den_ref, k_ref, v_ref, own_ref, own_den_ref, msg_ref):
    video, width = qo_ref.shape
    lane = lax.broadcasted_iota(jnp.int32, (2 * video, HEAD_DIM), 1)
    packed = den_ref[...]
    for head in range(width // HEAD_DIM):
        columns = slice(head * HEAD_DIM, (head + 1) * HEAD_DIM)
        queries = jnp.concatenate([qo_ref[:, columns], qp_ref[:, columns]], axis=0)
        weights = weigh(queries, k_ref[:, columns])
        num = num_ref[:, columns] + times(weights, v_ref[:, columns])
        own_ref[:, columns] = num[:video]
        msg_ref[:, columns] = num[video:]
        total = jnp.sum(lanes(weights), axis=1, keepdims=True)
        packed = packed + jnp.where(lane == head, total, 0.0)
    own_den_ref[...] = packed[:video]
    msg_ref[:, width:] = packed[video:]


def merge_kernel(own_ref, den_ref, msg_ref, att_ref):
    width = att_ref.shape[1]
    for head in range(width // HEAD_DIM):
        columns = slice(head * HEAD_DIM, (head + 1) * HEAD_DIM)
        num = own_ref[:, columns] + msg_ref[:, columns]
        den = den_ref[:, head : head + 1] + msg_ref[:, width + head : width + head + 1]
        att_ref[:, columns] = (num / den).astype(BF16)


def part_kernel(att_ref, w_ref, out_ref):
    out_ref[...] = jnp.dot(att_ref[...], w_ref[...], preferred_element_type=F32)


def final_kernel(part_ref, att_ref, w_ref, hidden_ref, gate_ref, out_ref):
    total = part_ref[...] + jnp.dot(att_ref[...], w_ref[...], preferred_element_type=F32)
    out_ref[...] = (hidden_ref[...].astype(F32) + gate_ref[...] * total).astype(BF16)


def params(megabytes):
    return pltpu.CompilerParams(vmem_limit_bytes=megabytes * 1024 * 1024)


def cost(flops, nbytes, transcendentals=0):
    return pl.CostEstimate(
        flops=int(flops), bytes_accessed=int(nbytes), transcendentals=int(transcendentals)
    )


def full(*shape):
    return pl.BlockSpec(shape, lambda *_: (0,) * len(shape))


def plain_call(kernel, outs, name, estimate, *operands):
    return pl.pallas_call(
        kernel,
        in_specs=[pl.BlockSpec(memory_space=pltpu.VMEM)] * len(operands),
        out_specs=[pl.BlockSpec(memory_space=pltpu.VMEM)] * len(outs),
        out_shape=[jax.ShapeDtypeStruct(shape, dtype) for shape, dtype in outs],
        compiler_params=params(24),
        cost_estimate=estimate,
        name=name,
    )(*operands)


def ring_moves(sections):
    chips = sections // 2
    order = list(range(0, chips, 2)) + list(range(chips - 1, 0, -2))
    onward = []
    for here, there in zip(order, order[1:] + order[:1]):
        onward += [(2 * here + core, 2 * there + core) for core in range(2)]
    return sorted(onward), sorted((there, here) for here, there in onward)


def per_device(
    sections, hidden, text_hidden, text_mask, stale_cache, qkv_weight, out_weight, query_gain,
    key_gain, norm_shift, norm_scale, branch_gate,
):
    video, features = hidden.shape
    text = text_hidden.shape[0] // 2
    width = stale_cache.shape[2]
    heads = width // HEAD_DIM
    group_columns = heads * TRIPLE
    chips = sections // 2
    out_features = out_weight.shape[1]
    top = video + EXTRA
    rows = top + text

    group = lax.axis_index("head")
    core = lax.axis_index("section") % 2
    place = jnp.stack([group, core]).astype(jnp.int32)
    swap_core = [(s, s ^ 1) for s in range(sections)]
    swap_head = [(0, 1), (1, 0)]
    onward, back = ring_moves(sections)
    half_way = chips // 2

    mask = lax.dynamic_slice_in_dim(text_mask, core * text, text, 0).astype(F32).reshape(1, text)
    query_gain, key_gain = query_gain.reshape(1, -1), key_gain.reshape(1, -1)

    def ring_step(up, down, *after):
        up, down = lax.optimization_barrier((up, down) + after)[:2]
        return lax.ppermute(up, "section", onward), lax.ppermute(down, "section", back)

    ring = [ring_step(stale_cache, stale_cache)]

    step_heads = 2 if heads % 2 == 0 else 1
    columns = step_heads * TRIPLE
    steps = heads // step_heads
    weight_bytes = features * group_columns * 2
    project_flops = 2 * rows * features * group_columns
    a_rows, message, text_message, stats = pl.pallas_call(
        send_kernel,
        grid_spec=pltpu.PrefetchScalarGridSpec(
            num_scalar_prefetch=1,
            grid=(steps,),
            in_specs=[
                full(video, features),
                pl.BlockSpec((text, features), lambda h, p: (p[1], 0)),
                full(1, features),
                full(1, features),
                pl.BlockSpec((features, columns), lambda h, p: (0, (1 - p[0]) * steps + h)),
            ],
            out_specs=[
                full(rows, features),
                full(top, group_columns + HEAD_DIM),
                full(text, 2 * width + HEAD_DIM),
                full(rows, HEAD_DIM),
            ],
        ),
        out_shape=[
            jax.ShapeDtypeStruct((rows, features), BF16),
            jax.ShapeDtypeStruct((top, group_columns + HEAD_DIM), BF16),
            jax.ShapeDtypeStruct((text, 2 * width + HEAD_DIM), BF16),
            jax.ShapeDtypeStruct((rows, HEAD_DIM), F32),
        ],
        compiler_params=params(50),
        cost_estimate=cost(project_flops, weight_bytes),
        name="project_send",
    )(place, hidden, text_hidden, norm_scale.reshape(1, -1), norm_shift.reshape(1, -1), qkv_weight)

    received = lax.ppermute(message, "head", swap_head)
    text_received = lax.ppermute(text_message, "head", swap_head)
    ring.append(ring_step(*ring[-1], message, text_message))

    own, own_text = pl.pallas_call(
        own_kernel,
        grid_spec=pltpu.PrefetchScalarGridSpec(
            num_scalar_prefetch=1,
            grid=(steps,),
            in_specs=[
                full(rows, features),
                pl.BlockSpec((features, columns), lambda h, p: (0, p[0] * steps + h)),
            ],
            out_specs=[
                pl.BlockSpec((top, columns), lambda h, p: (0, h)),
                pl.BlockSpec((text, step_heads * 2 * HEAD_DIM), lambda h, p: (0, h)),
            ],
        ),
        out_shape=[
            jax.ShapeDtypeStruct((top, group_columns), F32),
            jax.ShapeDtypeStruct((text, 2 * width), F32),
        ],
        compiler_params=params(50),
        cost_estimate=cost(project_flops, weight_bytes),
        name="project_own",
    )(place, a_rows, qkv_weight)

    for _ in range(half_way - 3):
        ring.append(ring_step(*ring[-1], own))
    arrived = [block for step in ring for block in step]
    far_keys = lax.ppermute(ring[-1][0][0], "section", onward)
    far_values = lax.ppermute(ring[-1][1][1], "section", back)

    queries, new_cache, fresh = plain_call(
        functools.partial(norm_kernel, features * 2),
        [((video, width), BF16), ((2, video, width), BF16), ((2, video, width), BF16)],
        "norm_video",
        cost(20 * top * group_columns, 8 * top * group_columns),
        own, received, stats, query_gain, key_gain,
    )
    other_queries = lax.ppermute(queries, "section", swap_core)
    (text_kv,) = plain_call(
        functools.partial(text_kernel, features * 2),
        [((2, text, width), BF16)],
        "norm_text",
        cost(20 * text * group_columns, 8 * text * group_columns),
        own_text, received, stats, own, text_received, key_gain,
    )

    context = (len(arrived) + 1) * video + text
    vmem = pl.BlockSpec(memory_space=pltpu.VMEM)
    num, den, w_own, w_other = pl.pallas_call(
        functools.partial(first_kernel, len(arrived)),
        in_specs=[pl.BlockSpec(memory_space=pltpu.SMEM), pl.BlockSpec(memory_space=pl.ANY)]
        + [vmem] * (6 + len(arrived)),
        out_specs=[vmem] * 4,
        out_shape=[
            jax.ShapeDtypeStruct((2 * video, width), F32),
            jax.ShapeDtypeStruct((2 * video, HEAD_DIM), F32),
            jax.ShapeDtypeStruct((width, out_features), BF16),
            jax.ShapeDtypeStruct((width, out_features), BF16),
        ],
        scratch_shapes=[pltpu.SemaphoreType.DMA((2,))],
        compiler_params=params(24),
        cost_estimate=cost(
            8 * video * context * width, 4 * context * width, 2 * video * context * heads
        ),
        name="attend_first",
    )(
        place[:1], out_weight, queries, other_queries, fresh, stale_cache, text_kv, mask, *arrived
    )
    num_own, den_own, num_message = plain_call(
        last_kernel,
        [((video, width), F32), ((video, HEAD_DIM), F32), ((video, width + HEAD_DIM), F32)],
        "attend_last",
        cost(8 * video * video * width, 12 * video * width, 2 * video * video * heads),
        queries, other_queries, num, den, far_keys, far_values,
    )

    num_received = lax.ppermute(num_message, "section", swap_core)
    (attended,) = plain_call(
        merge_kernel,
        [((video, width), BF16)],
        "merge",
        cost(4 * video * width, 10 * video * width),
        num_own, den_own, num_received,
    )
    other_attended = lax.ppermute(attended, "head", swap_head)

    out_cost = cost(2 * video * width * out_features, 2 * width * out_features)
    (part,) = plain_call(
        part_kernel, [((video, out_features), F32)], "part_out", out_cost, attended, w_own
    )
    (mixed,) = plain_call(
        final_kernel, [((video, out_features), BF16)], "final_out", out_cost,
        part, other_attended, w_other, hidden, branch_gate.reshape(1, -1),
    )
    return (mixed, new_cache)


def solution(mesh):
    in_specs = (
        P("section", "head"),
        P(None, "head"),
        P(),
        P(None, "section", "head"),
        P("head", None),
        P(None, "head"),
        P(),
        P(),
        P("head"),
        P("head"),
        P("head"),
    )
    out_specs = (P("section", "head"), P(None, "section", "head"))
    return jax.shard_map(
        functools.partial(per_device, mesh.shape["section"]),
        mesh=mesh, in_specs=in_specs, out_specs=out_specs, check_vma=False,
    )
```

time: 175 us -> 63.5 us (0.36)
  local copies, waits for them, and re-layouts: 51.1 us -> 8.51 us
  waiting for transfers between devices: 58.6 us -> 16.6 us
  matrix products: 27.2 us -> 0 us
  Pallas kernels: 0 us -> 22.7 us
  between operations: 15.7 us -> 0.86 us
  starting transfers between devices: 0.08 us -> 14.2 us
  blocking collectives: 13.1 us -> 0 us
  other arithmetic: 7.92 us -> 0.15 us
    all_gather x1 -> x0, waiting for transfers between devices: 29.7 us -> none  [per_device(): segment = lax.all_gather(stale_cache, 'section', axis=1, tiled=True)]
    reduce_scatter x1 -> x0, waiting for transfers between devices: 28.2 us -> none  [per_device(): lax.psum_scatter(jnp.einsum('rd,dhc->hrc', normed, columns, preferred_ele...]
    dot_general x10 -> x0, matrix products: 27.2 us -> none  [the longest x1 11 us: per_device(): jnp.einsum('rd,dhc->hrc', normed, columns, preferred_element_type=jnp.flo...]
    unnamed x32 -> x42, local copies, waits for them, and re-layouts: 31.1 us -> 5.67 us
    pallas_call x0 -> x9, Pallas kernels: none -> 22.7 us  [the longest x1 6.88 us: per_device(): pl.pallas_call(send_kernel, grid_spec=pltpu.PrefetchScalarGridSpec(num_sc...]
    ppermute x0 -> x13, waiting for transfers between devices: none -> 16.6 us  [the longest x1 5.33 us: per_device(): received = lax.ppermute(message, 'head', swap_head)]
    ppermute x0 -> x13, starting transfers between devices: none -> 14.2 us  [the longest x3 6.61 us: ring_step(): lax.ppermute(up, 'section', onward)]
    another operation x2 -> x0, local copies, waits for them, and re-layouts: 12.4 us -> none  [the longest x1 7.75 us: context_terms(): value_rows.reshape(block_count, block_rows, head_count, head_depth)]
  transfers between devices with their start and end apart: 2 -> 13, of which waited for: 2 -> 7; matrix products, arithmetic and copies ran while one was open for 34% -> 5% of each run, Pallas kernels for 0% -> 31%
where the time goes in v2:
time: 63.5 us; the launch traced here: 63.1 us
  Pallas kernels  22.7 us (36%)
  waiting for transfers between devices  16.6 us (26%)
  starting transfers between devices  14.2 us (22%)
  local copies, waits for them, and re-layouts  8.51 us (13%)
  between operations  0.86 us (1%)
    pallas_call x1, Pallas kernels, per_device(): pl.pallas_call(send_kernel, grid_spec=pltpu.PrefetchScalarGridSpec(num_sc...  6.88 us
    ppermute x3, starting transfers between devices, ring_step(): lax.ppermute(up, 'section', onward)  6.61 us
    pallas_call x6, Pallas kernels, plain_call(): pl.pallas_call(kernel, in_specs=[pl.BlockSpec(memory_space=pltpu.VMEM)] *...  6.41 us
    unnamed x42, local copies, waits for them, and re-layouts  5.67 us
    pallas_call x1, Pallas kernels, per_device(): pl.pallas_call(own_kernel, grid_spec=pltpu.PrefetchScalarGridSpec(num_sca...  5.6 us
    ppermute x1, waiting for transfers between devices, per_device(): received = lax.ppermute(message, 'head', swap_head)  5.33 us
    ppermute x1, waiting for transfers between devices, per_device(): other_attended = lax.ppermute(attended, 'head', swap_head)  4.8 us
    pallas_call x1, Pallas kernels, per_device(): pl.pallas_call(functools.partial(first_kernel, len(arrived)), in_specs=[p...  3.82 us
  transfers between devices with their start and end apart: 13, of which 7 were waited for; matrix products, arithmetic and copies ran while one was open for 5% of the time, Pallas kernels for 31%

profile of v2, /device:TPU:0, one launch (start us, length us, event | category | flops | bytes accessed | tf_op | source)
XLA Modules:
  0.0 63.1 jit_solution(2720642412579943596)
XLA Ops:
  0.6 3.1 %collective-permute-start.3 = (bf16[2,128,768]{2,1,0:T(8,128)(2,1)}, bf16[2,128,768]{2,1,0:T(8,128)(2,1)S(1)}, u32[]{:S(2)}, u32[]{:S(2)}) collective-permute-start(bf16[2,128,768]{2,1,0:T(8,128)(2,1)} %stale_ref.1), channel_id=1, source_target_pairs={{0,8},{2,10},{4,0},{6,2},{8,16},{10,18},{12,4},{14,6},{16,24},{18,... | collective-permute-start | bytes 1179656 | tf_op jit(solution)/shard_map/ppermute | solution.py:324
  5.2 1.0 %copy-done.1 = bf16[128,1536]{1,0:T(8,128)(2,1)S(1)} copy-done((bf16[128,1536]{1,0:T(8,128)(2,1)S(1)}, bf16[128,1536]{1,0:T(8,128)(2,1)}, u32[]{:S(2)}) %copy-start.1) | copy-done | bytes 393240
  6.2 1.1 %copy-done.3 = bf16[256,1536]{1,0:T(8,128)(2,1)S(1)} copy-done((bf16[256,1536]{1,0:T(8,128)(2,1)S(1)}, bf16[256,1536]{1,0:T(8,128)(2,1)}, u32[]{:S(2)}) %copy-start.3) | copy-done | bytes 786456
  7.3 6.9 %project_send.1 = (bf16[272,1536]{1,0:T(8,128)(2,1)S(1)}, bf16[144,2432]{1,0:T(8,128)(2,1)S(1)}, bf16[128,1664]{1,0:T(8,128)(2,1)}, f32[272,128]{1,0:T(8,128)S(1)}) custom-call(s32[2]{0:T(128)S(1)} %pad_add_fusion.place_ref, bf16[128,1536]{1,0:T(8,128)(2,1)S(1)} %copy-done.1, bf16[256,1536]{1,0:T(8,128)(2,1)S(1)} %copy-done.3, ...), custom_call_target="tpu_custom_call" | custom-call | flops 1925185536 | bytes 7077888 | tf_op jit(solution)/shard_map/project_send/pallas_call | solution.py:333
  14.5 1.8 %collective-permute-start.5 = (bf16[2,128,768]{2,1,0:T(8,128)(2,1)S(1)}, bf16[2,128,768]{2,1,0:T(8,128)(2,1)S(1)}, u32[]{:S(2)}, u32[]{:S(2)}) collective-permute-start(bf16[2,128,768]{2,1,0:T(8,128)(2,1)S(1)} %collective-permute-done.3.refs_0_), channel_id=1, source_target_pairs={{0,8},{2,10},{4,0},{6,2},{8,16},{10,18},{12,4},{14,6},{16,24},{18,... | collective-permute-start | bytes 1179656 | tf_op jit(solution)/shard_map/ppermute | solution.py:324
  16.5 1.7 %collective-permute-start = (bf16[144,2432]{1,0:T(8,128)(2,1)S(1)}, bf16[144,2432]{1,0:T(8,128)(2,1)S(1)}, u32[]{:S(2)}, u32[]{:S(2)}) collective-permute-start(bf16[144,2432]{1,0:T(8,128)(2,1)S(1)} %get-tuple-element.26), channel_id=1, source_target_pairs={{0,1},{1,0},{2,3},{3,2},{4,5},{5,4},{6,7},{7,6},{8,9},{9,8},{10,11... | collective-permute-start | bytes 2101256 | tf_op jit(solution)/shard_map/ppermute | solution.py:363
  18.2 5.6 %project_own.1 = (f32[144,2304]{1,0:T(8,128)S(1)}, f32[128,1536]{1,0:T(8,128)S(1)}) custom-call(s32[2]{0:T(128)S(1)} %pad_add_fusion.place_ref, bf16[272,1536]{1,0:T(8,128)(2,1)S(1)} %get-tuple-element.24.a_ref, bf16[1536,4608]{1,0:T(8,128)(2,1)} %w_ref.3), custom_call_target="tpu_custom_call" | custom-call | flops 1925185536 | bytes 7077888 | tf_op jit(solution)/shard_map/project_own/pallas_call | solution.py:367
  23.9 1.0 %collective-permute-done.5.refs_2_ = bf16[2,128,768]{2,1,0:T(8,128)(2,1)S(1)} collective-permute-done((bf16[2,128,768]{2,1,0:T(8,128)(2,1)S(1)}, bf16[2,128,768]{2,1,0:T(8,128)(2,1)S(1)}, u32[]{:S(2)}, u32[]{:S(2)}) %collective-permute-start.5) | collective-permute-done | bytes 393248 | tf_op jit(solution)/shard_map/ppermute | solution.py:324
  24.9 1.5 %collective-permute-done.6.refs_3_ = bf16[2,128,768]{2,1,0:T(8,128)(2,1)S(1)} collective-permute-done((bf16[2,128,768]{2,1,0:T(8,128)(2,1)S(1)}, bf16[2,128,768]{2,1,0:T(8,128)(2,1)S(1)}, u32[]{:S(2)}, u32[]{:S(2)}) %collective-permute-start.6) | collective-permute-done | bytes 393248 | tf_op jit(solution)/shard_map/ppermute | solution.py:324
  26.6 1.7 %collective-permute-start.7 = (bf16[2,128,768]{2,1,0:T(8,128)(2,1)S(1)}, bf16[2,128,768]{2,1,0:T(8,128)(2,1)S(1)}, u32[]{:S(2)}, u32[]{:S(2)}) collective-permute-start(bf16[2,128,768]{2,1,0:T(8,128)(2,1)S(1)} %collective-permute-done.5.refs_2_), channel_id=1, source_target_pairs={{0,8},{2,10},{4,0},{6,2},{8,16},{10,18},{12,4},{14,6},{16,24},{18,... | collective-permute-start | bytes 1179656 | tf_op jit(solution)/shard_map/ppermute | solution.py:324
  28.3 1.5 %collective-permute-start.2 = (bf16[128,1664]{1,0:T(8,128)(2,1)}, bf16[128,1664]{1,0:T(8,128)(2,1)}, u32[]{:S(2)}, u32[]{:S(2)}) collective-permute-start(bf16[128,1664]{1,0:T(8,128)(2,1)} %get-tuple-element.31), channel_id=1, source_target_pairs={{0,1},{1,0},{2,3},{3,2},{4,5},{5,4},{6,7},{7,6},{8,9},{9,8},{10,11... | collective-permute-start | bytes 1277960 | tf_op jit(solution)/shard_map/ppermute | solution.py:364
  29.8 5.3 %collective-permute-done.msg_ref = bf16[144,2432]{1,0:T(8,128)(2,1)S(1)} collective-permute-done((bf16[144,2432]{1,0:T(8,128)(2,1)S(1)}, bf16[144,2432]{1,0:T(8,128)(2,1)S(1)}, u32[]{:S(2)}, u32[]{:S(2)}) %collective-permute-start) | collective-permute-done | bytes 700448 | tf_op jit(solution)/shard_map/ppermute | solution.py:363
  35.2 1.4 %norm_video.1 = (bf16[128,768]{1,0:T(8,128)(2,1)S(1)}, bf16[2,128,768]{2,1,0:T(8,128)(2,1)}, bf16[2,128,768]{2,1,0:T(8,128)(2,1)S(1)}) custom-call(f32[144,2304]{1,0:T(8,128)S(1)} %get-tuple-element.25.own_ref.top_ref, bf16[144,2432]{1,0:T(8,128)(2,1)S(1)} %collective-permute-done.msg_ref, f32[272,128]{1,0:T(8,128)S(1)} %get-tuple-element.27.stat_ref, ...), custom_call_target="tpu_custom_call" | custom-call | flops 6635520 | bytes 2654208 | tf_op jit(solution)/shard_map/norm_video/pallas_call | solution.py:277
  37.3 1.7 %collective-permute-start.10 = (bf16[128,768]{1,0:T(8,128)(2,1)}, bf16[128,768]{1,0:T(8,128)(2,1)S(1)}, u32[]{:S(2)}, u32[]{:S(2)}) collective-permute-start(bf16[128,768]{1,0:T(8,128)(2,1)} %slice_bitcast_fusion), channel_id=1, source_target_pairs={{0,4},{2,6},{4,12},{6,14},{8,0},{10,2},{12,20},{14,22},{16,8},{18,... | collective-permute-start | bytes 589832 | tf_op jit(solution)/shard_map/ppermute | solution.py:394
  40.1 2.0 %collective-permute-done.2.tmsg_ref = bf16[128,1664]{1,0:T(8,128)(2,1)} collective-permute-done((bf16[128,1664]{1,0:T(8,128)(2,1)}, bf16[128,1664]{1,0:T(8,128)(2,1)}, u32[]{:S(2)}, u32[]{:S(2)}) %collective-permute-start.2) | collective-permute-done | bytes 426016 | tf_op jit(solution)/shard_map/ppermute | solution.py:364
  42.1 1.1 %copy-done.5 = f32[128,1536]{1,0:T(8,128)S(1)} copy-done((f32[128,1536]{1,0:T(8,128)S(1)}, f32[128,1536]{1,0:T(8,128)}, u32[]{:S(2)}) %copy-start.5) | copy-done | bytes 786456
  43.3 1.6 %norm_text.1.text_ref = bf16[2,128,768]{2,1,0:T(8,128)(2,1)S(1)} custom-call(f32[128,1536]{1,0:T(8,128)S(1)} %copy-done.5, bf16[144,2432]{1,0:T(8,128)(2,1)S(1)} %collective-permute-done.msg_ref, f32[272,128]{1,0:T(8,128)S(1)} %get-tuple-element.27.stat_ref, f32[144,2304]{1,0:T(8,128)S(1)} %get-tuple-element.25.own_ref.top_ref, ...), custom_call_target="tpu_custom_call" | custom-call | flops 5898240 | bytes 2359296 | tf_op jit(solution)/shard_map/norm_text/pallas_call | solution.py:277
  45.0 2.3 %copy-done = bf16[1536,1536]{1,0:T(8,128)(2,1)S(1)} copy-done((bf16[1536,1536]{1,0:T(8,128)(2,1)S(1)}, bf16[1536,1536]{1,0:T(8,128)(2,1)}, u32[]{:S(2)}) %copy-start) | copy-done | bytes 4718616
  47.3 3.8 %attend_first.1 = (f32[256,768]{1,0:T(8,128)S(1)}, f32[256,128]{1,0:T(8,128)S(1)}, bf16[768,1536]{1,0:T(8,128)(2,1)S(1)}, bf16[768,1536]{1,0:T(8,128)(2,1)S(1)}) custom-call(s32[1]{0:T(128)} %bitcast.group_ref, bf16[1536,1536]{1,0:T(8,128)(2,1)S(1)} %copy-done, bf16[128,768]{1,0:T(8,128)(2,1)S(1)} %get-tuple-element.28.qo_ref, ...), custom_call_target="tpu_custom_call" | custom-call | flops 805306368 | bytes 3145728 | tf_op jit(solution)/shard_map/attend_first/pallas_call | solution.py:414
  51.2 1.5 %attend_last.1 = (f32[128,768]{1,0:T(8,128)S(1)}, f32[128,128]{1,0:T(8,128)S(1)}, f32[128,896]{1,0:T(8,128)S(1)}) custom-call(bf16[128,768]{1,0:T(8,128)(2,1)S(1)} %get-tuple-element.28.qo_ref, bf16[128,768]{1,0:T(8,128)(2,1)S(1)} %collective-permute-done.1.qp_ref, f32[256,768]{1,0:T(8,128)S(1)} %get-tuple-element.38.num_ref, ...), custom_call_target="tpu_custom_call" | custom-call | flops 100663296 | bytes 1179648 | tf_op jit(solution)/shard_map/attend_last/pallas_call | solution.py:277
  52.8 1.8 %collective-permute-done.11.msg_ref = f32[128,896]{1,0:T(8,128)S(1)} collective-permute-done((f32[128,896]{1,0:T(8,128)S(1)}, f32[128,896]{1,0:T(8,128)S(1)}, u32[]{:S(2)}, u32[]{:S(2)}) %collective-permute-start.11) | collective-permute-done | bytes 458784 | tf_op jit(solution)/shard_map/ppermute | solution.py:442
  54.8 1.7 %collective-permute-start.12 = (bf16[128,768]{1,0:T(8,128)(2,1)S(1)}, bf16[128,768]{1,0:T(8,128)(2,1)S(1)}, u32[]{:S(2)}, u32[]{:S(2)}) collective-permute-start(bf16[128,768]{1,0:T(8,128)(2,1)S(1)} %merge.1.att_ref), channel_id=1, source_target_pairs={{0,1},{1,0},{2,3},{3,2},{4,5},{5,4},{6,7},{7,6},{8,9},{9,8},{10,11... | collective-permute-start | bytes 589832 | tf_op jit(solution)/shard_map/ppermute | solution.py:450
  57.0 4.8 %collective-permute-done.12.att_ref = bf16[128,768]{1,0:T(8,128)(2,1)S(1)} collective-permute-done((bf16[128,768]{1,0:T(8,128)(2,1)S(1)}, bf16[128,768]{1,0:T(8,128)(2,1)S(1)}, u32[]{:S(2)}, u32[]{:S(2)}) %collective-permute-start.12) | collective-permute-done | bytes 196640 | tf_op jit(solution)/shard_map/ppermute | solution.py:450
  61.8 1.2 %final_out.1 = bf16[128,1536]{1,0:T(8,128)(2,1)} custom-call(f32[128,1536]{1,0:T(8,128)S(1)} %part_out.1.part_ref, bf16[128,768]{1,0:T(8,128)(2,1)S(1)} %collective-permute-done.12.att_ref, bf16[768,1536]{1,0:T(8,128)(2,1)S(1)} %get-tuple-element.44.w_ref, bf16[128,1536]{1,0:T(8,128)(2,1)S(1)} %copy-done.2, f32[1,1536]{1,0:T(1,128)S(1)} %reshape.27.gate_ref), custom_call_target="tpu_custom_call" | custom-call | flops 301989888 | bytes 2359296 | tf_op jit(solution)/shard_map/final_out/pallas_call | solution.py:277
  (60 shorter events, 5.0 us)
Async XLA Ops:
  0.6 13.6 %collective-permute-start.3 = (bf16[2,128,768]{2,1,0:T(8,128)(2,1)}, bf16[2,128,768]{2,1,0:T(8,128)(2,1)S(1)}, u32[]{:S(2)}, u32[]{:S(2)}) collective-permute-start(bf16[2,128,768]{2,1,0:T(8,128)(2,1)} %stale_ref.1), channel_id=1, source_target_pairs={{0,8},{2,10},{4,0},{6,2},{8,16},{10,18},{12,4},{14,6},{16,24},{18,... | collective-permute-start | bytes 1179656 | tf_op jit(solution)/shard_map/ppermute | solution.py:324
  3.7 10.8 %collective-permute-start.4 = (bf16[2,128,768]{2,1,0:T(8,128)(2,1)}, bf16[2,128,768]{2,1,0:T(8,128)(2,1)S(1)}, u32[]{:S(2)}, u32[]{:S(2)}) collective-permute-start(bf16[2,128,768]{2,1,0:T(8,128)(2,1)} %stale_ref.1), channel_id=1, source_target_pairs={{0,4},{2,6},{4,12},{6,14},{8,0},{10,2},{12,20},{14,22},{16,8},{18,... | collective-permute-start | bytes 1179656 | tf_op jit(solution)/shard_map/ppermute | solution.py:324
  14.2 9.6 %copy-start.7 = (bf16[2,128,768]{2,1,0:T(8,128)(2,1)}, bf16[2,128,768]{2,1,0:T(8,128)(2,1)S(1)}, u32[]{:S(2)}) copy-start(bf16[2,128,768]{2,1,0:T(8,128)(2,1)S(1)} %collective-permute-done.3.refs_0_) | copy-start | bytes 1179652
  14.5 9.4 %copy-start.9 = (bf16[2,128,768]{2,1,0:T(8,128)(2,1)}, bf16[2,128,768]{2,1,0:T(8,128)(2,1)S(1)}, u32[]{:S(2)}) copy-start(bf16[2,128,768]{2,1,0:T(8,128)(2,1)S(1)} %collective-permute-done.4.refs_1_) | copy-start | bytes 1179652
  14.5 10.4 %collective-permute-start.5 = (bf16[2,128,768]{2,1,0:T(8,128)(2,1)S(1)}, bf16[2,128,768]{2,1,0:T(8,128)(2,1)S(1)}, u32[]{:S(2)}, u32[]{:S(2)}) collective-permute-start(bf16[2,128,768]{2,1,0:T(8,128)(2,1)S(1)} %collective-permute-done.3.refs_0_), channel_id=1, source_target_pairs={{0,8},{2,10},{4,0},{6,2},{8,16},{10,18},{12,4},{14,6},{16,24},{18,... | collective-permute-start | bytes 1179656 | tf_op jit(solution)/shard_map/ppermute | solution.py:324
  16.3 10.0 %collective-permute-start.6 = (bf16[2,128,768]{2,1,0:T(8,128)(2,1)S(1)}, bf16[2,128,768]{2,1,0:T(8,128)(2,1)S(1)}, u32[]{:S(2)}, u32[]{:S(2)}) collective-permute-start(bf16[2,128,768]{2,1,0:T(8,128)(2,1)S(1)} %collective-permute-done.4.refs_1_), channel_id=1, source_target_pairs={{0,4},{2,6},{4,12},{6,14},{8,0},{10,2},{12,20},{14,22},{16,8},{18,... | collective-permute-start | bytes 1179656 | tf_op jit(solution)/shard_map/ppermute | solution.py:324
  16.5 18.6 %collective-permute-start = (bf16[144,2432]{1,0:T(8,128)(2,1)S(1)}, bf16[144,2432]{1,0:T(8,128)(2,1)S(1)}, u32[]{:S(2)}, u32[]{:S(2)}) collective-permute-start(bf16[144,2432]{1,0:T(8,128)(2,1)S(1)} %get-tuple-element.26), channel_id=1, source_target_pairs={{0,1},{1,0},{2,3},{3,2},{4,5},{5,4},{6,7},{7,6},{8,9},{9,8},{10,11... | collective-permute-start | bytes 2101256 | tf_op jit(solution)/shard_map/ppermute | solution.py:363
  18.2 16.9 %copy-start.17 = (f32[128]{0:T(128)S(1)}, f32[128]{0:T(128)}, u32[]{:S(2)}) copy-start(f32[128]{0:T(128)} %param.18) | copy-start | bytes 1540
  18.2 16.9 %copy-start.18 = (f32[128]{0:T(128)S(1)}, f32[128]{0:T(128)}, u32[]{:S(2)}) copy-start(f32[128]{0:T(128)} %param.17) | copy-start | bytes 1540
  23.9 15.2 %copy-start.4 = (f32[128,1536]{1,0:T(8,128)}, f32[128,1536]{1,0:T(8,128)S(1)}, u32[]{:S(2)}) copy-start(f32[128,1536]{1,0:T(8,128)S(1)} %get-tuple-element.30.own_ref) | copy-start | bytes 2359300
  23.9 16.2 %copy-start.20 = (s32[256]{0:T(256)S(1)}, s32[256]{0:T(256)}, u32[]{:S(2)}) copy-start(s32[256]{0:T(256)} %param.13) | copy-start | bytes 3076
  24.8 14.9 %copy-start.11 = (bf16[2,128,768]{2,1,0:T(8,128)(2,1)}, bf16[2,128,768]{2,1,0:T(8,128)(2,1)S(1)}, u32[]{:S(2)}) copy-start(bf16[2,128,768]{2,1,0:T(8,128)(2,1)S(1)} %collective-permute-done.5.refs_2_) | copy-start | bytes 1179652
  26.3 13.4 %copy-start.13 = (bf16[2,128,768]{2,1,0:T(8,128)(2,1)}, bf16[2,128,768]{2,1,0:T(8,128)(2,1)S(1)}, u32[]{:S(2)}) copy-start(bf16[2,128,768]{2,1,0:T(8,128)(2,1)S(1)} %collective-permute-done.6.refs_3_) | copy-start | bytes 1179652
  26.3 10.2 %collective-permute-start.8 = (bf16[2,128,768]{2,1,0:T(8,128)(2,1)S(1)}, bf16[2,128,768]{2,1,0:T(8,128)(2,1)S(1)}, u32[]{:S(2)}, u32[]{:S(2)}) collective-permute-start(bf16[2,128,768]{2,1,0:T(8,128)(2,1)S(1)} %collective-permute-done.6.refs_3_), channel_id=1, source_target_pairs={{0,4},{2,6},{4,12},{6,14},{8,0},{10,2},{12,20},{14,22},{16,8},{18,... | collective-permute-start | bytes 1179656 | tf_op jit(solution)/shard_map/ppermute | solution.py:324
  26.6 12.4 %collective-permute-start.7 = (bf16[2,128,768]{2,1,0:T(8,128)(2,1)S(1)}, bf16[2,128,768]{2,1,0:T(8,128)(2,1)S(1)}, u32[]{:S(2)}, u32[]{:S(2)}) collective-permute-start(bf16[2,128,768]{2,1,0:T(8,128)(2,1)S(1)} %collective-permute-done.5.refs_2_), channel_id=1, source_target_pairs={{0,8},{2,10},{4,0},{6,2},{8,16},{10,18},{12,4},{14,6},{16,24},{18,... | collective-permute-start | bytes 1179656 | tf_op jit(solution)/shard_map/ppermute | solution.py:324
  28.3 13.8 %collective-permute-start.2 = (bf16[128,1664]{1,0:T(8,128)(2,1)}, bf16[128,1664]{1,0:T(8,128)(2,1)}, u32[]{:S(2)}, u32[]{:S(2)}) collective-permute-start(bf16[128,1664]{1,0:T(8,128)(2,1)} %get-tuple-element.31), channel_id=1, source_target_pairs={{0,1},{1,0},{2,3},{3,2},{4,5},{5,4},{6,7},{7,6},{8,9},{9,8},{10,11... | collective-permute-start | bytes 1277960 | tf_op jit(solution)/shard_map/ppermute | solution.py:364
  36.5 3.2 %copy-start.15 = (bf16[2,128,768]{2,1,0:T(8,128)(2,1)}, bf16[2,128,768]{2,1,0:T(8,128)(2,1)S(1)}, u32[]{:S(2)}) copy-start(bf16[2,128,768]{2,1,0:T(8,128)(2,1)S(1)} %get-tuple-element.29.fresh_ref) | copy-start | bytes 1179652
  36.5 8.4 %collective-permute-start.1 = (bf16[128,768]{1,0:T(8,128)(2,1)S(1)}, bf16[128,768]{1,0:T(8,128)(2,1)S(1)}, u32[]{:S(2)}, u32[]{:S(2)}) collective-permute-start(bf16[128,768]{1,0:T(8,128)(2,1)S(1)} %get-tuple-element.28.qo_ref), channel_id=1, source_target_pairs={{0,2},{2,0},{4,6},{6,4},{8,10},{10,8},{12,14},{14,12},{16,18},{18,... | collective-permute-start | bytes 589832 | tf_op jit(solution)/shard_map/ppermute | solution.py:403
  37.3 13.9 %collective-permute-start.10 = (bf16[128,768]{1,0:T(8,128)(2,1)}, bf16[128,768]{1,0:T(8,128)(2,1)S(1)}, u32[]{:S(2)}, u32[]{:S(2)}) collective-permute-start(bf16[128,768]{1,0:T(8,128)(2,1)} %slice_bitcast_fusion), channel_id=1, source_target_pairs={{0,4},{2,6},{4,12},{6,14},{8,0},{10,2},{12,20},{14,22},{16,8},{18,... | collective-permute-start | bytes 589832 | tf_op jit(solution)/shard_map/ppermute | solution.py:394
  39.7 11.5 %collective-permute-start.9 = (bf16[128,768]{1,0:T(8,128)(2,1)}, bf16[128,768]{1,0:T(8,128)(2,1)}, u32[]{:S(2)}, u32[]{:S(2)}) collective-permute-start(bf16[128,768]{1,0:T(8,128)(2,1)} %slice_bitcast_fusion.1), channel_id=1, source_target_pairs={{0,8},{2,10},{4,0},{6,2},{8,16},{10,18},{12,4},{14,6},{16,24},{18,... | collective-permute-start | bytes 589832 | tf_op jit(solution)/shard_map/ppermute | solution.py:393
  51.2 5.4 %copy-start.19 = (f32[1536]{0:T(1024)S(1)}, f32[1536]{0:T(1024)}, u32[]{:S(2)}) copy-start(f32[1536]{0:T(1024)} %param.21) | copy-start | bytes 18436
  52.7 9.1 %copy-start.2 = (bf16[128,1536]{1,0:T(8,128)(2,1)S(1)}, bf16[128,1536]{1,0:T(8,128)(2,1)}, u32[]{:S(2)}) copy-start(bf16[128,1536]{1,0:T(8,128)(2,1)} %hidden_ref.1) | copy-start | bytes 1179652
  52.8 1.9 %collective-permute-start.11 = (f32[128,896]{1,0:T(8,128)S(1)}, f32[128,896]{1,0:T(8,128)S(1)}, u32[]{:S(2)}, u32[]{:S(2)}) collective-permute-start(f32[128,896]{1,0:T(8,128)S(1)} %get-tuple-element.42), channel_id=1, source_target_pairs={{0,2},{2,0},{4,6},{6,4},{8,10},{10,8},{12,14},{14,12},{16,18},{18,... | collective-permute-start | bytes 1376264 | tf_op jit(solution)/shard_map/ppermute | solution.py:442
  54.8 7.0 %collective-permute-start.12 = (bf16[128,768]{1,0:T(8,128)(2,1)S(1)}, bf16[128,768]{1,0:T(8,128)(2,1)S(1)}, u32[]{:S(2)}, u32[]{:S(2)}) collective-permute-start(bf16[128,768]{1,0:T(8,128)(2,1)S(1)} %merge.1.att_ref), channel_id=1, source_target_pairs={{0,1},{1,0},{2,3},{3,2},{4,5},{5,4},{6,7},{7,6},{8,9},{9,8},{10,11... | collective-permute-start | bytes 589832 | tf_op jit(solution)/shard_map/ppermute | solution.py:450
  (10 other events, 15.8 us)

commit v3 on v2

v3 whole, which is shorter than its diff:
```python
import functools
import math

import jax
import jax.numpy as jnp
from jax import lax
from jax.experimental import pallas as pl
from jax.experimental.pallas import tpu as pltpu
from jax.sharding import PartitionSpec as P

HEAD_DIM = 128
TRIPLE = 3 * HEAD_DIM
EXTRA = 16
STAT_ROW = 8
EPS = 1e-06
F32 = jnp.float32
BF16 = jnp.bfloat16


def split_bf16(value, parts):
    pieces = []
    rest = value
    for _ in range(parts):
        piece = rest.astype(BF16)
        pieces.append(piece)
        rest = rest - piece.astype(F32)
    return pieces


def start_weights(w_ref, buffer_ref, sems, first):
    count, _, columns = buffer_ref.shape
    copies = []
    for index in range(count):
        start = pl.multiple_of(first + index * columns, HEAD_DIM)
        copy = pltpu.make_async_copy(
            w_ref.at[:, pl.ds(start, columns)], buffer_ref.at[index], sems.at[index]
        )
        copy.start()
        copies.append(copy)
    return copies


def send_kernel(
    place_ref, x_ref, t_ref, scale_ref, shift_ref, w_ref,
    a_ref, msg_ref, stat_ref, x_buffer, t_buffer, w_buffer, in_sems, w_sems,
):
    video, features = x_buffer.shape
    text = t_buffer.shape[0]
    top = video + EXTRA
    blocks, _, columns = w_buffer.shape
    width = blocks * columns
    x_copy = pltpu.make_async_copy(x_ref, x_buffer, in_sems.at[0])
    t_copy = pltpu.make_async_copy(
        t_ref.at[pl.ds(pl.multiple_of(place_ref[1] * text, text), text)], t_buffer, in_sems.at[1]
    )
    x_copy.start()
    t_copy.start()
    w_copies = start_weights(w_ref, w_buffer, w_sems, (1 - place_ref[0]) * width)

    gain = 1.0 + scale_ref[...].reshape(1, features)
    pieces = split_bf16(gain, 2) + split_bf16(shift_ref[...].reshape(1, features), 2)
    row = lax.broadcasted_iota(jnp.int32, (EXTRA, features), 0)
    extra = jnp.zeros((EXTRA, features), F32)
    for index, piece in enumerate(pieces):
        extra = jnp.where(row == index, piece.astype(F32), extra)
    a_ref[video:top, :] = extra.astype(BF16)

    def prepare(rows_ref, start):
        rows = rows_ref[...].astype(F32)
        count = rows.shape[0]
        mean = jnp.sum(rows, axis=1, keepdims=True) * (1.0 / features)
        centered = rows - mean
        second = jnp.sum(centered * centered, axis=1, keepdims=True)
        a_ref[start : start + count, :] = (centered * gain).astype(BF16)
        lane = lax.broadcasted_iota(jnp.int32, (count, HEAD_DIM), 1)
        packed = jnp.zeros((count, HEAD_DIM), F32)
        for index, piece in enumerate(split_bf16(mean, 3) + split_bf16(second, 3)):
            packed = jnp.where(lane == STAT_ROW + index, piece.astype(F32), packed)
        stat_ref[start : start + count, :] = jnp.where(
            lane == 0, mean, jnp.where(lane == 1, second, 0.0)
        )
        return jnp.transpose(packed)[:EXTRA]

    x_copy.wait()
    video_stats = prepare(x_buffer, 0)
    t_copy.wait()
    text_stats = prepare(t_buffer, top)
    stat_ref[video:top, :] = jnp.zeros((EXTRA, HEAD_DIM), F32)

    heads = columns // TRIPLE
    for block in range(blocks):
        w_copies[block].wait()
        product = jnp.dot(a_ref[...], w_buffer[block], preferred_element_type=F32)
        start = block * columns
        msg_ref[:top, start : start + columns] = product[:top].astype(BF16)
        if block == 0:
            msg_ref[video:top, : video + text] = (
                product[video:top, : video + text]
                + jnp.concatenate([video_stats, text_stats], axis=1)
            ).astype(BF16)
        for head in range(heads):
            pair = product[top:, head * TRIPLE + HEAD_DIM : (head + 1) * TRIPLE].astype(BF16)
            for quarter in range(4):
                rows, cells = text_slot(text, width, block * heads + head, quarter)
                msg_ref[top + rows.start : top + rows.stop, cells] = pair[
                    quarter * text // 4 : (quarter + 1) * text // 4
                ]


def text_slot(text, width, head, quarter):
    slots = width // (2 * HEAD_DIM)
    band, slot = divmod(head * 4 + quarter, slots)
    depth = text // 4
    return (
        slice(band * depth, (band + 1) * depth),
        slice(slot * 2 * HEAD_DIM, (slot + 1) * 2 * HEAD_DIM),
    )


def own_kernel(place_ref, a_ref, w_ref, out_ref, text_ref, w_buffer, w_sems):
    top = out_ref.shape[0]
    blocks, _, columns = w_buffer.shape
    heads = columns // TRIPLE
    w_copies = start_weights(w_ref, w_buffer, w_sems, place_ref[0] * blocks * columns)
    for block in range(blocks):
        w_copies[block].wait()
        product = jnp.dot(a_ref[...], w_buffer[block], preferred_element_type=F32)
        out_ref[:, block * columns : (block + 1) * columns] = product[:top]
        for index in range(heads):
            start = (block * heads + index) * 2 * HEAD_DIM
            text_ref[:, start : start + 2 * HEAD_DIM] = product[
                top:, index * TRIPLE + HEAD_DIM : (index + 1) * TRIPLE
            ]


def row_stats(total_features, own, received):
    count = own.shape[0]
    received = received.astype(F32)
    padding = jnp.zeros((HEAD_DIM - received.shape[0], count), F32)
    received = jnp.transpose(jnp.concatenate([received, padding], axis=0))
    parts = [received[:, STAT_ROW + index : STAT_ROW + index + 1] for index in range(6)]
    gap = 0.5 * (own[:, 0:1] - (parts[0] + parts[1] + parts[2]))
    second = own[:, 1:2] + (parts[3] + parts[4] + parts[5])
    var = second * (1.0 / total_features) + gap * gap
    return gap, lax.rsqrt(var + EPS)


def column_terms(own, other):
    other = other.astype(F32)
    scale = (own[0:1] + own[1:2]) - (other[0:1] + other[1:2])
    shift = (own[2:3] + own[3:4]) + (other[2:3] + other[3:4])
    return scale, shift


def head_norm(part, gain):
    square = jnp.sum(part * part, axis=1, keepdims=True) * (1.0 / HEAD_DIM)
    return part * lax.rsqrt(square + EPS) * gain


def norm_kernel(
    total_features, own_ref, msg_ref, stat_ref, qg_ref, kg_ref, q_ref, cache_ref, kv_ref,
):
    video = q_ref.shape[0]
    top = video + EXTRA
    heads = q_ref.shape[1] // HEAD_DIM
    gap, inverse = row_stats(total_features, stat_ref[:video, :], msg_ref[video:top, :video])
    for head in range(heads):
        part = slice(head * TRIPLE, (head + 1) * TRIPLE)
        columns = slice(head * HEAD_DIM, (head + 1) * HEAD_DIM)
        scale, shift = column_terms(own_ref[video:, part], msg_ref[video:top, part])
        total = own_ref[:video, part] + msg_ref[:video, part].astype(F32)
        total = (total + gap * scale) * inverse + shift
        q_ref[:, columns] = head_norm(total[:, :HEAD_DIM], qg_ref[...]).astype(BF16)
        keys = head_norm(total[:, HEAD_DIM : 2 * HEAD_DIM], kg_ref[...]).astype(BF16)
        values = total[:, 2 * HEAD_DIM :].astype(BF16)
        cache_ref[0, :, columns] = keys
        cache_ref[1, :, columns] = values
        kv_ref[0, :, columns] = keys
        kv_ref[1, :, columns] = values


def text_kernel(total_features, own_ref, msg_ref, stat_ref, top_ref, kg_ref, kv_ref):
    text = kv_ref.shape[1]
    heads = kv_ref.shape[2] // HEAD_DIM
    top, width = top_ref.shape
    video = top - EXTRA
    gap, inverse = row_stats(
        total_features, stat_ref[top:, :], msg_ref[video:top, video : video + text]
    )
    for head in range(heads):
        part = slice(head * TRIPLE + HEAD_DIM, (head + 1) * TRIPLE)
        pair = slice(head * 2 * HEAD_DIM, (head + 1) * 2 * HEAD_DIM)
        columns = slice(head * HEAD_DIM, (head + 1) * HEAD_DIM)
        scale, shift = column_terms(top_ref[video:, part], msg_ref[video:top, part])
        other = []
        for quarter in range(4):
            rows, cells = text_slot(text, width, head, quarter)
            other.append(msg_ref[top + rows.start : top + rows.stop, cells])
        total = own_ref[:, pair] + jnp.concatenate(other, axis=0).astype(F32)
        total = (total + gap * scale) * inverse + shift
        kv_ref[0, :, columns] = head_norm(total[:, :HEAD_DIM], kg_ref[...]).astype(BF16)
        kv_ref[1, :, columns] = total[:, HEAD_DIM:].astype(BF16)


FACTOR = math.log2(math.e) / math.sqrt(HEAD_DIM)


def weigh(rows, keys):
    scores = lax.dot_general(rows, keys, (((1,), (1,)), ((), ())), preferred_element_type=F32)
    return jnp.exp2(scores * FACTOR)


def lanes(weights):
    total = weights[:, :HEAD_DIM]
    for start in range(HEAD_DIM, weights.shape[1], HEAD_DIM):
        total = total + weights[:, start : start + HEAD_DIM]
    return total


def times(weights, values):
    return jnp.dot(weights.astype(BF16), values, preferred_element_type=F32)


def absorb(queries, blocks, num, den, columns):
    for first in range(0, len(blocks), 2):
        pair = blocks[first : first + 2]
        keys = jnp.concatenate([k(columns) for k, _ in pair], axis=0)
        values = jnp.concatenate([v(columns) for _, v in pair], axis=0)
        weights = weigh(queries, keys)
        num = num + times(weights, values)
        den = den + lanes(weights)
    return num, den


def loaders(ref):
    return (lambda columns: ref[0, :, columns]), (lambda columns: ref[1, :, columns])


def first_kernel(
    count, group_ref, weight_ref, qo_ref, qp_ref, fresh_ref, stale_ref, text_ref, mask_ref, *refs
):
    ring = refs[:count]
    num_ref, den_ref, w_own_ref, w_other_ref, stale_buffer, sems = refs[count:]
    depth = w_own_ref.shape[0]
    group = group_ref[0]
    stale_copy = pltpu.make_async_copy(stale_ref, stale_buffer, sems.at[2])
    stale_copy.start()
    copies = []
    for index, (half, target) in enumerate(((group, w_own_ref), (1 - group, w_other_ref))):
        source = weight_ref.at[pl.ds(pl.multiple_of(half * depth, depth), depth)]
        copies.append(pltpu.make_async_copy(source, target, sems.at[index]))
    for copy in copies:
        copy.start()
    video, width = qo_ref.shape
    lane = lax.broadcasted_iota(jnp.int32, (2 * video, HEAD_DIM), 1)
    packed = jnp.zeros((2 * video, HEAD_DIM), F32)
    stale_copy.wait()
    for head in range(width // HEAD_DIM):
        columns = slice(head * HEAD_DIM, (head + 1) * HEAD_DIM)
        own, other = qo_ref[:, columns], qp_ref[:, columns]
        queries = jnp.concatenate([own, other], axis=0)
        fresh = weigh(own, fresh_ref[0, :, columns])
        stale = weigh(other, stale_buffer[0, :, columns])
        num = jnp.concatenate(
            [times(fresh, fresh_ref[1, :, columns]), times(stale, stale_buffer[1, :, columns])], axis=0
        )
        den = jnp.concatenate([fresh, stale], axis=0)
        weights = weigh(queries, text_ref[0, :, columns]) * mask_ref[...]
        num = num + times(weights, text_ref[1, :, columns])
        den = den + lanes(weights)
        num, den = absorb(queries, [loaders(ref) for ref in ring], num, den, columns)
        num_ref[:, columns] = num
        packed = jnp.where(lane == head, jnp.sum(den, axis=1, keepdims=True), packed)
    den_ref[...] = packed
    for copy in copies:
        copy.wait()


def last_kernel(qo_ref, qp_ref, num_ref, den_ref, kv_ref, own_ref, own_den_ref, msg_ref):
    video, width = qo_ref.shape
    lane = lax.broadcasted_iota(jnp.int32, (2 * video, HEAD_DIM), 1)
    packed = den_ref[...]
    for head in range(width // HEAD_DIM):
        columns = slice(head * HEAD_DIM, (head + 1) * HEAD_DIM)
        queries = jnp.concatenate([qo_ref[:, columns], qp_ref[:, columns]], axis=0)
        weights = weigh(queries, kv_ref[0, :, columns])
        num = num_ref[:, columns] + times(weights, kv_ref[1, :, columns])
        own_ref[:, columns] = num[:video]
        msg_ref[:, columns] = num[video:]
        total = jnp.sum(lanes(weights), axis=1, keepdims=True)
        packed = packed + jnp.where(lane == head, total, 0.0)
    own_den_ref[...] = packed[:video]
    msg_ref[:, width:] = packed[video:]


def merge_kernel(own_ref, den_ref, msg_ref, att_ref):
    width = att_ref.shape[1]
    for head in range(width // HEAD_DIM):
        columns = slice(head * HEAD_DIM, (head + 1) * HEAD_DIM)
        num = own_ref[:, columns] + msg_ref[:, columns]
        den = den_ref[:, head : head + 1] + msg_ref[:, width + head : width + head + 1]
        att_ref[:, columns] = (num / den).astype(BF16)


def part_kernel(att_ref, w_ref, out_ref):
    out_ref[...] = jnp.dot(att_ref[...], w_ref[...], preferred_element_type=F32)


def final_kernel(part_ref, att_ref, w_ref, hidden_ref, gate_ref, out_ref):
    total = part_ref[...] + jnp.dot(att_ref[...], w_ref[...], preferred_element_type=F32)
    out_ref[...] = (hidden_ref[...].astype(F32) + gate_ref[...] * total).astype(BF16)


def params(megabytes):
    return pltpu.CompilerParams(vmem_limit_bytes=megabytes * 1024 * 1024)


def cost(flops, nbytes, transcendentals=0):
    return pl.CostEstimate(
        flops=int(flops), bytes_accessed=int(nbytes), transcendentals=int(transcendentals)
    )


def plain_call(kernel, outs, name, estimate, *operands):
    return pl.pallas_call(
        kernel,
        in_specs=[pl.BlockSpec(memory_space=pltpu.VMEM)] * len(operands),
        out_specs=[pl.BlockSpec(memory_space=pltpu.VMEM)] * len(outs),
        out_shape=[jax.ShapeDtypeStruct(shape, dtype) for shape, dtype in outs],
        compiler_params=params(24),
        cost_estimate=estimate,
        name=name,
    )(*operands)


def ring_moves(sections):
    chips = sections // 2
    order = list(range(0, chips, 2)) + list(range(chips - 1, 0, -2))
    moves = [], []
    for here, there in zip(order, order[1:] + order[:1]):
        for core in range(2):
            moves[core].append((2 * here + core, 2 * there + core))
            moves[1 - core].append((2 * there + core, 2 * here + core))
    return sorted(moves[0]), sorted(moves[1])


def per_device(
    sections, hidden, text_hidden, text_mask, stale_cache, qkv_weight, out_weight, query_gain,
    key_gain, norm_shift, norm_scale, branch_gate,
):
    video, features = hidden.shape
    text = text_hidden.shape[0] // 2
    width = stale_cache.shape[2]
    heads = width // HEAD_DIM
    group_columns = heads * TRIPLE
    chips = sections // 2
    out_features = out_weight.shape[1]
    top = video + EXTRA
    rows = top + text

    group = lax.axis_index("head")
    core = lax.axis_index("section") % 2
    place = jnp.stack([group, core]).astype(jnp.int32)
    swap_core = [(s, s ^ 1) for s in range(sections)]
    swap_head = [(0, 1), (1, 0)]
    first_way, second_way = ring_moves(sections)
    half_way = chips // 2

    mask = lax.dynamic_slice_in_dim(text_mask, core * text, text, 0).astype(F32).reshape(1, text)
    query_gain, key_gain = query_gain.reshape(1, -1), key_gain.reshape(1, -1)

    def ring_step(up, down, *after):
        up, down = lax.optimization_barrier((up, down) + after)[:2]
        return lax.ppermute(up, "section", first_way), lax.ppermute(down, "section", second_way)

    ring = [ring_step(stale_cache, stale_cache)]

    block_heads = 2 if heads % 2 == 0 else 1
    columns = block_heads * TRIPLE
    blocks = heads // block_heads
    bands = -(-heads * 4 // (group_columns // (2 * HEAD_DIM)))
    message_rows = top + bands * text // 4
    project_cost = cost(2 * rows * features * group_columns, 2 * features * group_columns)
    vmem = pl.BlockSpec(memory_space=pltpu.VMEM)
    hbm = pl.BlockSpec(memory_space=pltpu.HBM)
    smem = pl.BlockSpec(memory_space=pltpu.SMEM)
    weight_scratch = [
        pltpu.VMEM((blocks, features, columns), BF16),
        pltpu.SemaphoreType.DMA((blocks,)),
    ]
    a_rows, message, stats = pl.pallas_call(
        send_kernel,
        in_specs=[smem, hbm, hbm, vmem, vmem, hbm],
        out_specs=[vmem] * 3,
        out_shape=[
            jax.ShapeDtypeStruct((rows, features), BF16),
            jax.ShapeDtypeStruct((message_rows, group_columns), BF16),
            jax.ShapeDtypeStruct((rows, HEAD_DIM), F32),
        ],
        scratch_shapes=[
            pltpu.VMEM((video, features), BF16),
            pltpu.VMEM((text, features), BF16),
            weight_scratch[0],
            pltpu.SemaphoreType.DMA((2,)),
            weight_scratch[1],
        ],
        compiler_params=params(40),
        cost_estimate=project_cost,
        name="project_send",
    )(place, hidden, text_hidden, norm_scale, norm_shift, qkv_weight)

    received = lax.ppermute(message, "head", swap_head)
    ring.append(ring_step(*ring[-1], message))

    own, own_text = pl.pallas_call(
        own_kernel,
        in_specs=[smem, vmem, hbm],
        out_specs=[vmem] * 2,
        out_shape=[
            jax.ShapeDtypeStruct((top, group_columns), F32),
            jax.ShapeDtypeStruct((text, 2 * width), F32),
        ],
        scratch_shapes=weight_scratch,
        compiler_params=params(40),
        cost_estimate=project_cost,
        name="project_own",
    )(place, a_rows, qkv_weight)

    for _ in range(half_way - 3):
        ring.append(ring_step(*ring[-1], own))
    arrived = [block for step in ring for block in step]
    far = lax.ppermute(ring[-1][0], "section", first_way)

    queries, new_cache, fresh = plain_call(
        functools.partial(norm_kernel, features * 2),
        [((video, width), BF16), ((2, video, width), BF16), ((2, video, width), BF16)],
        "norm_video",
        cost(20 * top * group_columns, 8 * top * group_columns),
        own, received, stats, query_gain, key_gain,
    )
    other_queries = lax.ppermute(queries, "section", swap_core)
    (text_kv,) = plain_call(
        functools.partial(text_kernel, features * 2),
        [((2, text, width), BF16)],
        "norm_text",
        cost(20 * text * group_columns, 8 * text * group_columns),
        own_text, received, stats, own, key_gain,
    )

    context = (len(arrived) + 1) * video + text
    num, den, w_own, w_other = pl.pallas_call(
        functools.partial(first_kernel, len(arrived)),
        in_specs=[smem, hbm] + [vmem] * 3 + [hbm] + [vmem] * (2 + len(arrived)),
        out_specs=[vmem] * 4,
        out_shape=[
            jax.ShapeDtypeStruct((2 * video, width), F32),
            jax.ShapeDtypeStruct((2 * video, HEAD_DIM), F32),
            jax.ShapeDtypeStruct((width, out_features), BF16),
            jax.ShapeDtypeStruct((width, out_features), BF16),
        ],
        scratch_shapes=[
            pltpu.VMEM(stale_cache.shape, BF16),
            pltpu.SemaphoreType.DMA((3,)),
        ],
        compiler_params=params(24),
        cost_estimate=cost(
            8 * video * context * width, 4 * context * width, 2 * video * context * heads
        ),
        name="attend_first",
    )(
        place[:1], out_weight, queries, other_queries, fresh, stale_cache, text_kv, mask, *arrived
    )
    num_own, den_own, num_message = plain_call(
        last_kernel,
        [((video, width), F32), ((video, HEAD_DIM), F32), ((video, width + HEAD_DIM), F32)],
        "attend_last",
        cost(8 * video * video * width, 12 * video * width, 2 * video * video * heads),
        queries, other_queries, num, den, far,
    )

    num_received = lax.ppermute(num_message, "section", swap_core)
    (attended,) = plain_call(
        merge_kernel,
        [((video, width), BF16)],
        "merge",
        cost(4 * video * width, 10 * video * width),
        num_own, den_own, num_received,
    )
    other_attended = lax.ppermute(attended, "head", swap_head)

    out_cost = cost(2 * video * width * out_features, 2 * width * out_features)
    (part,) = plain_call(
        part_kernel, [((video, out_features), F32)], "part_out", out_cost, attended, w_own
    )
    (mixed,) = plain_call(
        final_kernel, [((video, out_features), BF16)], "final_out", out_cost,
        part, other_attended, w_other, hidden, branch_gate.reshape(1, -1),
    )
    return (mixed, new_cache)


def solution(mesh):
    in_specs = (
        P("section", "head"),
        P(None, "head"),
        P(),
        P(None, "section", "head"),
        P("head", None),
        P(None, "head"),
        P(),
        P(),
        P("head"),
        P("head"),
        P("head"),
    )
    out_specs = (P("section", "head"), P(None, "section", "head"))
    return jax.shard_map(
        functools.partial(per_device, mesh.shape["section"]),
        mesh=mesh, in_specs=in_specs, out_specs=out_specs, check_vma=False,
    )
```

time: 63.5 us -> 64.2 us (1.011)
  waiting for transfers between devices: 16.6 us -> 21 us
  starting transfers between devices: 14.2 us -> 11.9 us
  local copies, waits for them, and re-layouts: 8.51 us -> 7.29 us
  Pallas kernels: 22.7 us -> 21.8 us
  other arithmetic: 0.15 us -> 0.93 us
    ppermute x9 -> x7, waiting for transfers between devices: 4.7 us -> 14.5 us  [the longest x3 14.5 us: ring_step(): lax.ppermute(up, 'section', first_way)]
    ppermute x1, waiting for transfers between devices: 5.33 us -> 0.14 us  [per_device(): received = lax.ppermute(message, 'head', swap_head)]
    ppermute x9 -> x7, starting transfers between devices: 10.7 us -> 7.3 us  [the longest x3 4.94 us: ring_step(): lax.ppermute(up, 'section', first_way)]
    unnamed x42 -> x30, local copies, waits for them, and re-layouts: 5.67 us -> 7.29 us
    squeeze x2 -> x0, local copies, waits for them, and re-layouts: 1.44 us -> none  [the longest x1 0.75 us: per_device(): far_values = lax.ppermute(ring[-1][1][1], 'section', back)]
    reshape x2 -> x0, local copies, waits for them, and re-layouts: 1.4 us -> none  [the longest x1 0.7 us: per_device(): norm_scale.reshape(1, -1)]
    reshape x1, other arithmetic: 0.07 us -> 0.85 us  [per_device(): lax.dynamic_slice_in_dim(text_mask, core * text, text, 0).astype(F32)]
    pallas_call x6, Pallas kernels: 6.41 us -> 5.7 us  [plain_call(): pl.pallas_call(kernel, in_specs=[pl.BlockSpec(memory_space=pltpu.VMEM)] *...]
  transfers between devices with their start and end apart: 13 -> 11, of which waited for: 7 -> 5; matrix products, arithmetic and copies ran while one was open for 5% -> 1% of each run, Pallas kernels for 31% -> 29%
where the time goes in v3:
time: 64.2 us; the launch traced here: 63.8 us
  Pallas kernels  21.8 us (34%)
  waiting for transfers between devices  21 us (33%)
  starting transfers between devices  11.9 us (19%)
  local copies, waits for them, and re-layouts  7.29 us (11%)
  other arithmetic  0.93 us (1%)
  between operations  0.78 us (1%)
    ppermute x3, waiting for transfers between devices, ring_step(): lax.ppermute(up, 'section', first_way)  14.5 us
    unnamed x30, local copies, waits for them, and re-layouts  7.29 us
    pallas_call x6, Pallas kernels, plain_call(): pl.pallas_call(kernel, in_specs=[pl.BlockSpec(memory_space=pltpu.VMEM)] *...  5.7 us
    pallas_call x1, Pallas kernels, per_device(): pl.pallas_call(functools.partial(first_kernel, len(arrived)), in_specs=[s...  5.53 us
    pallas_call x1, Pallas kernels, per_device(): pl.pallas_call(send_kernel, in_specs=[smem, hbm, hbm, vmem, vmem, hbm], o...  5.51 us
    pallas_call x1, Pallas kernels, per_device(): pl.pallas_call(own_kernel, in_specs=[smem, vmem, hbm], out_specs=[vmem] *...  5.11 us
    ppermute x1, waiting for transfers between devices, per_device(): other_attended = lax.ppermute(attended, 'head', swap_head)  4.94 us
    ppermute x3, starting transfers between devices, ring_step(): lax.ppermute(up, 'section', first_way)  4.94 us
  transfers between devices with their start and end apart: 11, of which 5 were waited for; matrix products, arithmetic and copies ran while one was open for 1% of the time, Pallas kernels for 29%

profile of v3, /device:TPU:0, one launch (start us, length us, event | category | flops | bytes accessed | tf_op | source)
XLA Modules:
  0.0 63.8 jit_solution(1506812274978929294)
XLA Ops:
  0.6 3.1 %collective-permute-start.2 = (bf16[2,128,768]{2,1,0:T(8,128)(2,1)}, bf16[2,128,768]{2,1,0:T(8,128)(2,1)}, u32[]{:S(2)}, u32[]{:S(2)}) collective-permute-start(bf16[2,128,768]{2,1,0:T(8,128)(2,1)} %stale_ref.1), channel_id=1, source_target_pairs={{0,8},{2,6},{4,0},{6,14},{8,16},{10,2},{12,4},{14,22},{16,24},{18,... | collective-permute-start | bytes 1179656 | tf_op jit(solution)/shard_map/ppermute | solution.py:374
  3.8 1.0 %copy-done.1 = bf16[128,1536]{1,0:T(8,128)(2,1)S(1)} copy-done((bf16[128,1536]{1,0:T(8,128)(2,1)S(1)}, bf16[128,1536]{1,0:T(8,128)(2,1)}, u32[]{:S(2)}) %copy-start.1) | copy-done | bytes 393240
  4.8 1.1 %copy-done.3 = bf16[256,1536]{1,0:T(8,128)(2,1)S(1)} copy-done((bf16[256,1536]{1,0:T(8,128)(2,1)S(1)}, bf16[256,1536]{1,0:T(8,128)(2,1)}, u32[]{:S(2)}) %copy-start.3) | copy-done | bytes 786456
  5.9 0.7 %copy-done.9 = f32[1536]{0:T(1024)S(1)} copy-done((f32[1536]{0:T(1024)S(1)}, f32[1536]{0:T(1024)}, u32[]{:S(2)}) %copy-start.9) | copy-done | bytes 6168
  6.6 0.7 %copy-done.10 = f32[1536]{0:T(1024)S(1)} copy-done((f32[1536]{0:T(1024)S(1)}, f32[1536]{0:T(1024)}, u32[]{:S(2)}) %copy-start.10) | copy-done | bytes 6168
  7.3 5.5 %project_send.1 = (bf16[272,1536]{1,0:T(8,128)(2,1)S(1)}, bf16[240,2304]{1,0:T(8,128)(2,1)S(1)}, f32[272,128]{1,0:T(8,128)S(1)}) custom-call(s32[2]{0:T(128)S(1)} %pad_add_fusion.place_ref, bf16[128,1536]{1,0:T(8,128)(2,1)S(1)} %copy-done.1, bf16[256,1536]{1,0:T(8,128)(2,1)S(1)} %copy-done.3, f32[1536]{0:T(1024)S(1)} %copy-done.9, f32[1536]{0:T(1024)S(1)} %copy-done.10, ...), custom_call_target="tpu_custom_call" | custom-call | flops 1925185536 | bytes 7077888 | tf_op jit(solution)/shard_map/project_send/pallas_call | solution.py:391
  12.8 2.0 %collective-permute-start = (bf16[240,2304]{1,0:T(8,128)(2,1)S(1)}, bf16[240,2304]{1,0:T(8,128)(2,1)S(1)}, u32[]{:S(2)}, u32[]{:S(2)}) collective-permute-start(bf16[240,2304]{1,0:T(8,128)(2,1)S(1)} %get-tuple-element.25), channel_id=1, source_target_pairs={{0,1},{1,0},{2,3},{3,2},{4,5},{5,4},{6,7},{7,6},{8,9},{9,8},{10,11... | collective-permute-start | bytes 3317768 | tf_op jit(solution)/shard_map/ppermute | solution.py:412
  14.8 1.6 %collective-permute-start.4 = (bf16[2,128,768]{2,1,0:T(8,128)(2,1)}, bf16[2,128,768]{2,1,0:T(8,128)(2,1)S(1)}, u32[]{:S(2)}, u32[]{:S(2)}) collective-permute-start(bf16[2,128,768]{2,1,0:T(8,128)(2,1)} %collective-permute-done.2.refs_0_), channel_id=1, source_target_pairs={{0,8},{2,6},{4,0},{6,14},{8,16},{10,2},{12,4},{14,22},{16,24},{18,... | collective-permute-start | bytes 1179656 | tf_op jit(solution)/shard_map/ppermute | solution.py:374
  16.9 5.1 %project_own.1 = (f32[144,2304]{1,0:T(8,128)S(1)}, f32[128,1536]{1,0:T(8,128)S(1)}) custom-call(s32[2]{0:T(128)S(1)} %pad_add_fusion.place_ref, bf16[272,1536]{1,0:T(8,128)(2,1)S(1)} %get-tuple-element.23.a_ref, bf16[1536,4608]{1,0:T(8,128)(2,1)} %w_ref.3), custom_call_target="tpu_custom_call" | custom-call | flops 1925185536 | bytes 7077888 | tf_op jit(solution)/shard_map/project_own/pallas_call | solution.py:415
  22.0 4.9 %collective-permute-done.4.refs_2_ = bf16[2,128,768]{2,1,0:T(8,128)(2,1)S(1)} collective-permute-done((bf16[2,128,768]{2,1,0:T(8,128)(2,1)}, bf16[2,128,768]{2,1,0:T(8,128)(2,1)S(1)}, u32[]{:S(2)}, u32[]{:S(2)}) %collective-permute-start.4) | collective-permute-done | bytes 393248 | tf_op jit(solution)/shard_map/ppermute | solution.py:374
  27.1 1.7 %collective-permute-start.7 = (bf16[2,128,768]{2,1,0:T(8,128)(2,1)}, bf16[2,128,768]{2,1,0:T(8,128)(2,1)}, u32[]{:S(2)}, u32[]{:S(2)}) collective-permute-start(bf16[2,128,768]{2,1,0:T(8,128)(2,1)} %collective-permute-done.5.refs_3_), channel_id=1, source_target_pairs={{0,4},{2,10},{4,12},{6,2},{8,0},{10,18},{12,20},{14,6},{16,8},{18,... | collective-permute-start | bytes 1179656 | tf_op jit(solution)/shard_map/ppermute | solution.py:374
  28.9 9.6 %collective-permute-done.6.refs_4_ = bf16[2,128,768]{2,1,0:T(8,128)(2,1)} collective-permute-done((bf16[2,128,768]{2,1,0:T(8,128)(2,1)S(1)}, bf16[2,128,768]{2,1,0:T(8,128)(2,1)}, u32[]{:S(2)}, u32[]{:S(2)}) %collective-permute-start.6) | collective-permute-done | bytes 393248 | tf_op jit(solution)/shard_map/ppermute | solution.py:374
  38.8 1.5 %norm_video.1 = (bf16[128,768]{1,0:T(8,128)(2,1)S(1)}, bf16[2,128,768]{2,1,0:T(8,128)(2,1)}, bf16[2,128,768]{2,1,0:T(8,128)(2,1)S(1)}) custom-call(f32[144,2304]{1,0:T(8,128)S(1)} %get-tuple-element.24.own_ref.top_ref, bf16[240,2304]{1,0:T(8,128)(2,1)S(1)} %collective-permute-done.msg_ref, f32[272,128]{1,0:T(8,128)S(1)} %get-tuple-element.26.stat_ref, ...), custom_call_target="tpu_custom_call" | custom-call | flops 6635520 | bytes 2654208 | tf_op jit(solution)/shard_map/norm_video/pallas_call | solution.py:325
  40.3 0.7 %copy-done.7 = bf16[2,128,768]{2,1,0:T(8,128)(2,1)} copy-done((bf16[2,128,768]{2,1,0:T(8,128)(2,1)}, bf16[2,128,768]{2,1,0:T(8,128)(2,1)S(1)}, u32[]{:S(2)}) %copy-start.7) | copy-done | bytes 393240
  41.1 0.9 %convert_bitcast_fusion.mask_ref = f32[1,128]{1,0:T(1,128)S(1)} fusion(s32[256]{0:T(256)} %param.13, s32[]{:T(128)S(6)} %select_n.11), kind=kLoop, calls=%fused_computation.1 | loop fusion | flops 128 | bytes 1028 | tf_op jit(solution)/shard_map/reshape | solution.py:369
  42.0 0.7 %copy-done.12 = f32[128]{0:T(128)S(1)} copy-done((f32[128]{0:T(128)S(1)}, f32[128]{0:T(128)}, u32[]{:S(2)}) %copy-start.12) | copy-done | bytes 536
  42.6 0.6 norm_text.1.text_ref
  43.3 2.3 %copy-done = bf16[1536,1536]{1,0:T(8,128)(2,1)S(1)} copy-done((bf16[1536,1536]{1,0:T(8,128)(2,1)S(1)}, bf16[1536,1536]{1,0:T(8,128)(2,1)}, u32[]{:S(2)}) %copy-start) | copy-done | bytes 4718616
  45.6 5.5 %attend_first.1 = (f32[256,768]{1,0:T(8,128)S(1)}, f32[256,128]{1,0:T(8,128)S(1)}, bf16[768,1536]{1,0:T(8,128)(2,1)S(1)}, bf16[768,1536]{1,0:T(8,128)(2,1)S(1)}) custom-call(s32[1]{0:T(128)} %bitcast.group_ref, bf16[1536,1536]{1,0:T(8,128)(2,1)S(1)} %copy-done, bf16[128,768]{1,0:T(8,128)(2,1)S(1)} %get-tuple-element.27.qo_ref, ...), custom_call_target="tpu_custom_call" | custom-call | flops 805306368 | bytes 3145728 | tf_op jit(solution)/shard_map/attend_first/pallas_call | solution.py:451
  51.2 1.7 %attend_last.1 = (f32[128,768]{1,0:T(8,128)S(1)}, f32[128,128]{1,0:T(8,128)S(1)}, f32[128,896]{1,0:T(8,128)S(1)}) custom-call(bf16[128,768]{1,0:T(8,128)(2,1)S(1)} %get-tuple-element.27.qo_ref, bf16[128,768]{1,0:T(8,128)(2,1)} %collective-permute-done.1.qp_ref, f32[256,768]{1,0:T(8,128)S(1)} %get-tuple-element.36.num_ref, ...), custom_call_target="tpu_custom_call" | custom-call | flops 100663296 | bytes 1179648 | tf_op jit(solution)/shard_map/attend_last/pallas_call | solution.py:325
  53.4 1.4 %collective-permute-done.9.msg_ref = f32[128,896]{1,0:T(8,128)S(1)} collective-permute-done((f32[128,896]{1,0:T(8,128)S(1)}, f32[128,896]{1,0:T(8,128)S(1)}, u32[]{:S(2)}, u32[]{:S(2)}) %collective-permute-start.9) | collective-permute-done | bytes 458784 | tf_op jit(solution)/shard_map/ppermute | solution.py:481
  55.1 2.1 %collective-permute-start.10 = (bf16[128,768]{1,0:T(8,128)(2,1)S(1)}, bf16[128,768]{1,0:T(8,128)(2,1)S(1)}, u32[]{:S(2)}, u32[]{:S(2)}) collective-permute-start(bf16[128,768]{1,0:T(8,128)(2,1)S(1)} %merge.1.att_ref), channel_id=1, source_target_pairs={{0,1},{1,0},{2,3},{3,2},{4,5},{5,4},{6,7},{7,6},{8,9},{9,8},{10,11... | collective-permute-start | bytes 589832 | tf_op jit(solution)/shard_map/ppermute | solution.py:489
  57.6 4.9 %collective-permute-done.10.att_ref = bf16[128,768]{1,0:T(8,128)(2,1)S(1)} collective-permute-done((bf16[128,768]{1,0:T(8,128)(2,1)S(1)}, bf16[128,768]{1,0:T(8,128)(2,1)S(1)}, u32[]{:S(2)}, u32[]{:S(2)}) %collective-permute-start.10) | collective-permute-done | bytes 196640 | tf_op jit(solution)/shard_map/ppermute | solution.py:489
  62.6 1.2 %final_out.1 = bf16[128,1536]{1,0:T(8,128)(2,1)} custom-call(f32[128,1536]{1,0:T(8,128)S(1)} %part_out.1.part_ref, bf16[128,768]{1,0:T(8,128)(2,1)S(1)} %collective-permute-done.10.att_ref, bf16[768,1536]{1,0:T(8,128)(2,1)S(1)} %get-tuple-element.42.w_ref, bf16[128,1536]{1,0:T(8,128)(2,1)S(1)} %copy-done.2, f32[1,1536]{1,0:T(1,128)S(1)} %reshape.19.gate_ref), custom_call_target="tpu_custom_call" | custom-call | flops 301989888 | bytes 2359296 | tf_op jit(solution)/shard_map/final_out/pallas_call | solution.py:325
  (40 shorter events, 2.4 us)
Async XLA Ops:
  0.6 14.2 %collective-permute-start.2 = (bf16[2,128,768]{2,1,0:T(8,128)(2,1)}, bf16[2,128,768]{2,1,0:T(8,128)(2,1)}, u32[]{:S(2)}, u32[]{:S(2)}) collective-permute-start(bf16[2,128,768]{2,1,0:T(8,128)(2,1)} %stale_ref.1), channel_id=1, source_target_pairs={{0,8},{2,6},{4,0},{6,14},{8,16},{10,2},{12,4},{14,22},{16,24},{18,... | collective-permute-start | bytes 1179656 | tf_op jit(solution)/shard_map/ppermute | solution.py:374
  3.7 11.1 %collective-permute-start.3 = (bf16[2,128,768]{2,1,0:T(8,128)(2,1)}, bf16[2,128,768]{2,1,0:T(8,128)(2,1)}, u32[]{:S(2)}, u32[]{:S(2)}) collective-permute-start(bf16[2,128,768]{2,1,0:T(8,128)(2,1)} %stale_ref.1), channel_id=1, source_target_pairs={{0,4},{2,10},{4,12},{6,2},{8,0},{10,18},{12,20},{14,6},{16,8},{18,... | collective-permute-start | bytes 1179656 | tf_op jit(solution)/shard_map/ppermute | solution.py:374
  3.8 1.0 %copy-start.1 = (bf16[128,1536]{1,0:T(8,128)(2,1)S(1)}, bf16[128,1536]{1,0:T(8,128)(2,1)}, u32[]{:S(2)}) copy-start(bf16[128,1536]{1,0:T(8,128)(2,1)} %hidden_ref.1) | copy-start | bytes 1179652
  4.8 1.1 %copy-start.3 = (bf16[256,1536]{1,0:T(8,128)(2,1)S(1)}, bf16[256,1536]{1,0:T(8,128)(2,1)}, u32[]{:S(2)}) copy-start(bf16[256,1536]{1,0:T(8,128)(2,1)} %t_ref.1) | copy-start | bytes 2359300
  5.9 0.7 %copy-start.9 = (f32[1536]{0:T(1024)S(1)}, f32[1536]{0:T(1024)}, u32[]{:S(2)}) copy-start(f32[1536]{0:T(1024)} %scale_ref.1) | copy-start | bytes 18436
  12.8 26.0 %collective-permute-start = (bf16[240,2304]{1,0:T(8,128)(2,1)S(1)}, bf16[240,2304]{1,0:T(8,128)(2,1)S(1)}, u32[]{:S(2)}, u32[]{:S(2)}) collective-permute-start(bf16[240,2304]{1,0:T(8,128)(2,1)S(1)} %get-tuple-element.25), channel_id=1, source_target_pairs={{0,1},{1,0},{2,3},{3,2},{4,5},{5,4},{6,7},{7,6},{8,9},{9,8},{10,11... | collective-permute-start | bytes 3317768 | tf_op jit(solution)/shard_map/ppermute | solution.py:412
  14.8 12.0 %collective-permute-start.4 = (bf16[2,128,768]{2,1,0:T(8,128)(2,1)}, bf16[2,128,768]{2,1,0:T(8,128)(2,1)S(1)}, u32[]{:S(2)}, u32[]{:S(2)}) collective-permute-start(bf16[2,128,768]{2,1,0:T(8,128)(2,1)} %collective-permute-done.2.refs_0_), channel_id=1, source_target_pairs={{0,8},{2,6},{4,0},{6,14},{8,16},{10,2},{12,4},{14,22},{16,24},{18,... | collective-permute-start | bytes 1179656 | tf_op jit(solution)/shard_map/ppermute | solution.py:374
  16.4 10.4 %collective-permute-start.5 = (bf16[2,128,768]{2,1,0:T(8,128)(2,1)}, bf16[2,128,768]{2,1,0:T(8,128)(2,1)}, u32[]{:S(2)}, u32[]{:S(2)}) collective-permute-start(bf16[2,128,768]{2,1,0:T(8,128)(2,1)} %collective-permute-done.3.refs_1_), channel_id=1, source_target_pairs={{0,4},{2,10},{4,12},{6,2},{8,0},{10,18},{12,20},{14,6},{16,8},{18,... | collective-permute-start | bytes 1179656 | tf_op jit(solution)/shard_map/ppermute | solution.py:374
  16.9 21.9 %copy-start.11 = (f32[128]{0:T(128)S(1)}, f32[128]{0:T(128)}, u32[]{:S(2)}) copy-start(f32[128]{0:T(128)} %param.18) | copy-start | bytes 1540
  16.9 21.9 %copy-start.13 = (f32[128]{0:T(128)S(1)}, f32[128]{0:T(128)}, u32[]{:S(2)}) copy-start(f32[128]{0:T(128)} %param.17) | copy-start | bytes 1540
  26.9 13.5 %copy-start.5 = (bf16[2,128,768]{2,1,0:T(8,128)(2,1)}, bf16[2,128,768]{2,1,0:T(8,128)(2,1)S(1)}, u32[]{:S(2)}) copy-start(bf16[2,128,768]{2,1,0:T(8,128)(2,1)S(1)} %collective-permute-done.4.refs_2_) | copy-start | bytes 1179652
  26.9 11.7 %collective-permute-start.6 = (bf16[2,128,768]{2,1,0:T(8,128)(2,1)S(1)}, bf16[2,128,768]{2,1,0:T(8,128)(2,1)}, u32[]{:S(2)}, u32[]{:S(2)}) collective-permute-start(bf16[2,128,768]{2,1,0:T(8,128)(2,1)S(1)} %collective-permute-done.4.refs_2_), channel_id=1, source_target_pairs={{0,8},{2,6},{4,0},{6,14},{8,16},{10,2},{12,4},{14,22},{16,24},{18,... | collective-permute-start | bytes 1179656 | tf_op jit(solution)/shard_map/ppermute | solution.py:374
  27.1 16.1 %collective-permute-start.7 = (bf16[2,128,768]{2,1,0:T(8,128)(2,1)}, bf16[2,128,768]{2,1,0:T(8,128)(2,1)}, u32[]{:S(2)}, u32[]{:S(2)}) collective-permute-start(bf16[2,128,768]{2,1,0:T(8,128)(2,1)} %collective-permute-done.5.refs_3_), channel_id=1, source_target_pairs={{0,4},{2,10},{4,12},{6,2},{8,0},{10,18},{12,20},{14,6},{16,8},{18,... | collective-permute-start | bytes 1179656 | tf_op jit(solution)/shard_map/ppermute | solution.py:374
  38.5 12.6 %collective-permute-start.8 = (bf16[2,128,768]{2,1,0:T(8,128)(2,1)}, bf16[2,128,768]{2,1,0:T(8,128)(2,1)}, u32[]{:S(2)}, u32[]{:S(2)}) collective-permute-start(bf16[2,128,768]{2,1,0:T(8,128)(2,1)} %collective-permute-done.6.refs_4_), channel_id=1, source_target_pairs={{0,8},{2,6},{4,0},{6,14},{8,16},{10,2},{12,4},{14,22},{16,24},{18,... | collective-permute-start | bytes 1179656 | tf_op jit(solution)/shard_map/ppermute | solution.py:432
  40.3 0.7 %copy-start.7 = (bf16[2,128,768]{2,1,0:T(8,128)(2,1)}, bf16[2,128,768]{2,1,0:T(8,128)(2,1)S(1)}, u32[]{:S(2)}) copy-start(bf16[2,128,768]{2,1,0:T(8,128)(2,1)S(1)} %get-tuple-element.28.fresh_ref) | copy-start | bytes 1179652
  41.1 2.1 %collective-permute-start.1 = (bf16[128,768]{1,0:T(8,128)(2,1)S(1)}, bf16[128,768]{1,0:T(8,128)(2,1)}, u32[]{:S(2)}, u32[]{:S(2)}) collective-permute-start(bf16[128,768]{1,0:T(8,128)(2,1)S(1)} %get-tuple-element.27.qo_ref), channel_id=1, source_target_pairs={{0,2},{2,0},{4,6},{6,4},{8,10},{10,8},{12,14},{14,12},{16,18},{18,... | collective-permute-start | bytes 589832 | tf_op jit(solution)/shard_map/ppermute | solution.py:441
  41.1 2.1 %copy-start.4 = (bf16[2,128,768]{2,1,0:T(8,128)(2,1)S(1)}, bf16[2,128,768]{2,1,0:T(8,128)(2,1)}, u32[]{:S(2)}) copy-start(bf16[2,128,768]{2,1,0:T(8,128)(2,1)} %stale_ref.1) | copy-start | bytes 1179652
  41.1 2.1 %copy-start.6 = (bf16[2,128,768]{2,1,0:T(8,128)(2,1)S(1)}, bf16[2,128,768]{2,1,0:T(8,128)(2,1)}, u32[]{:S(2)}) copy-start(bf16[2,128,768]{2,1,0:T(8,128)(2,1)} %copy-done.5) | copy-start | bytes 1179652
  41.1 2.2 %copy-start.8 = (bf16[2,128,768]{2,1,0:T(8,128)(2,1)S(1)}, bf16[2,128,768]{2,1,0:T(8,128)(2,1)}, u32[]{:S(2)}) copy-start(bf16[2,128,768]{2,1,0:T(8,128)(2,1)} %copy-done.7) | copy-start | bytes 1179652
  43.2 2.3 %copy-start = (bf16[1536,1536]{1,0:T(8,128)(2,1)S(1)}, bf16[1536,1536]{1,0:T(8,128)(2,1)}, u32[]{:S(2)}) copy-start(bf16[1536,1536]{1,0:T(8,128)(2,1)} %weight_ref.1) | copy-start | bytes 14155780
  51.1 6.0 %copy-start.14 = (f32[1536]{0:T(1024)S(1)}, f32[1536]{0:T(1024)}, u32[]{:S(2)}) copy-start(f32[1536]{0:T(1024)} %param.21) | copy-start | bytes 18436
  52.9 9.7 %copy-start.2 = (bf16[128,1536]{1,0:T(8,128)(2,1)S(1)}, bf16[128,1536]{1,0:T(8,128)(2,1)}, u32[]{:S(2)}) copy-start(bf16[128,1536]{1,0:T(8,128)(2,1)} %hidden_ref.1) | copy-start | bytes 1179652
  52.9 2.0 %collective-permute-start.9 = (f32[128,896]{1,0:T(8,128)S(1)}, f32[128,896]{1,0:T(8,128)S(1)}, u32[]{:S(2)}, u32[]{:S(2)}) collective-permute-start(f32[128,896]{1,0:T(8,128)S(1)} %get-tuple-element.40), channel_id=1, source_target_pairs={{0,2},{2,0},{4,6},{6,4},{8,10},{10,8},{12,14},{14,12},{16,18},{18,... | collective-permute-start | bytes 1376264 | tf_op jit(solution)/shard_map/ppermute | solution.py:481
  55.1 7.5 %collective-permute-start.10 = (bf16[128,768]{1,0:T(8,128)(2,1)S(1)}, bf16[128,768]{1,0:T(8,128)(2,1)S(1)}, u32[]{:S(2)}, u32[]{:S(2)}) collective-permute-start(bf16[128,768]{1,0:T(8,128)(2,1)S(1)} %merge.1.att_ref), channel_id=1, source_target_pairs={{0,1},{1,0},{2,3},{3,2},{4,5},{5,4},{6,7},{7,6},{8,9},{9,8},{10,11... | collective-permute-start | bytes 589832 | tf_op jit(solution)/shard_map/ppermute | solution.py:489
  (2 other events, 1.4 us)

commit v4 on v3

--- a/solution.py
+++ b/solution.py
@@ -42,7 +42,8 @@
 
 def send_kernel(
     place_ref, x_ref, t_ref, scale_ref, shift_ref, w_ref,
-    a_ref, msg_ref, stat_ref, x_buffer, t_buffer, w_buffer, in_sems, w_sems,
+    a_ref, msg_ref, stat_ref, x_buffer, t_buffer, scale_buffer, shift_buffer, w_buffer,
+    in_sems, w_sems,
 ):
     video, features = x_buffer.shape
     text = t_buffer.shape[0]
@@ -53,12 +54,16 @@
     t_copy = pltpu.make_async_copy(
         t_ref.at[pl.ds(pl.multiple_of(place_ref[1] * text, text), text)], t_buffer, in_sems.at[1]
     )
-    x_copy.start()
-    t_copy.start()
+    scale_copy = pltpu.make_async_copy(scale_ref, scale_buffer, in_sems.at[2])
+    shift_copy = pltpu.make_async_copy(shift_ref, shift_buffer, in_sems.at[3])
+    for copy in (scale_copy, shift_copy, x_copy, t_copy):
+        copy.start()
     w_copies = start_weights(w_ref, w_buffer, w_sems, (1 - place_ref[0]) * width)
 
-    gain = 1.0 + scale_ref[...].reshape(1, features)
-    pieces = split_bf16(gain, 2) + split_bf16(shift_ref[...].reshape(1, features), 2)
+    scale_copy.wait()
+    shift_copy.wait()
+    gain = 1.0 + scale_buffer[...].reshape(1, features)
+    pieces = split_bf16(gain, 2) + split_bf16(shift_buffer[...].reshape(1, features), 2)
     row = lax.broadcasted_iota(jnp.int32, (EXTRA, features), 0)
     extra = jnp.zeros((EXTRA, features), F32)
     for index, piece in enumerate(pieces):
@@ -117,11 +122,18 @@
     )
 
 
-def own_kernel(place_ref, a_ref, w_ref, out_ref, text_ref, w_buffer, w_sems):
+def own_kernel(place_ref, a_ref, w_ref, *refs):
+    small = (len(refs) - 5) // 2
+    out_ref, text_ref = refs[small : small + 2]
+    w_buffer, w_sems, sems = refs[-3:]
     top = out_ref.shape[0]
     blocks, _, columns = w_buffer.shape
     heads = columns // TRIPLE
     w_copies = start_weights(w_ref, w_buffer, w_sems, place_ref[0] * blocks * columns)
+    copies = []
+    for index, (source, target) in enumerate(zip(refs[:small], refs[small + 2 : -3])):
+        copies.append(pltpu.make_async_copy(source, target, sems.at[index]))
+        copies[-1].start()
     for block in range(blocks):
         w_copies[block].wait()
         product = jnp.dot(a_ref[...], w_buffer[block], preferred_element_type=F32)
@@ -131,6 +143,8 @@
             text_ref[:, start : start + 2 * HEAD_DIM] = product[
                 top:, index * TRIPLE + HEAD_DIM : (index + 1) * TRIPLE
             ]
+    for copy in copies:
+        copy.wait()
 
 
 def row_stats(total_features, own, received):
@@ -162,6 +176,8 @@
 ):
     video = q_ref.shape[0]
     top = video + EXTRA
+    query_gain = qg_ref[...].reshape(1, HEAD_DIM)
+    key_gain = kg_ref[...].reshape(1, HEAD_DIM)
     heads = q_ref.shape[1] // HEAD_DIM
     gap, inverse = row_stats(total_features, stat_ref[:video, :], msg_ref[video:top, :video])
     for head in range(heads):
@@ -170,8 +186,8 @@
         scale, shift = column_terms(own_ref[video:, part], msg_ref[video:top, part])
         total = own_ref[:video, part] + msg_ref[:video, part].astype(F32)
         total = (total + gap * scale) * inverse + shift
-        q_ref[:, columns] = head_norm(total[:, :HEAD_DIM], qg_ref[...]).astype(BF16)
-        keys = head_norm(total[:, HEAD_DIM : 2 * HEAD_DIM], kg_ref[...]).astype(BF16)
+        q_ref[:, columns] = head_norm(total[:, :HEAD_DIM], query_gain).astype(BF16)
+        keys = head_norm(total[:, HEAD_DIM : 2 * HEAD_DIM], key_gain).astype(BF16)
         values = total[:, 2 * HEAD_DIM :].astype(BF16)
         cache_ref[0, :, columns] = keys
         cache_ref[1, :, columns] = values
@@ -184,6 +200,7 @@
     heads = kv_ref.shape[2] // HEAD_DIM
     top, width = top_ref.shape
     video = top - EXTRA
+    key_gain = kg_ref[...].reshape(1, HEAD_DIM)
     gap, inverse = row_stats(
         total_features, stat_ref[top:, :], msg_ref[video:top, video : video + text]
     )
@@ -198,7 +215,7 @@
             other.append(msg_ref[top + rows.start : top + rows.stop, cells])
         total = own_ref[:, pair] + jnp.concatenate(other, axis=0).astype(F32)
         total = (total + gap * scale) * inverse + shift
-        kv_ref[0, :, columns] = head_norm(total[:, :HEAD_DIM], kg_ref[...]).astype(BF16)
+        kv_ref[0, :, columns] = head_norm(total[:, :HEAD_DIM], key_gain).astype(BF16)
         kv_ref[1, :, columns] = total[:, HEAD_DIM:].astype(BF16)
 
 
@@ -237,12 +254,12 @@
 
 
 def first_kernel(
-    count, group_ref, weight_ref, qo_ref, qp_ref, fresh_ref, stale_ref, text_ref, mask_ref, *refs
+    count, place_ref, weight_ref, qo_ref, qp_ref, fresh_ref, stale_ref, text_ref, mask_ref, *refs
 ):
     ring = refs[:count]
     num_ref, den_ref, w_own_ref, w_other_ref, stale_buffer, sems = refs[count:]
     depth = w_own_ref.shape[0]
-    group = group_ref[0]
+    group = place_ref[0]
     stale_copy = pltpu.make_async_copy(stale_ref, stale_buffer, sems.at[2])
     stale_copy.start()
     copies = []
@@ -254,23 +271,34 @@
     video, width = qo_ref.shape
     lane = lax.broadcasted_iota(jnp.int32, (2 * video, HEAD_DIM), 1)
     packed = jnp.zeros((2 * video, HEAD_DIM), F32)
+    text = text_ref.shape[1]
+    mask = mask_ref[...].reshape(1, 2 * text).astype(F32)
+    mask = jnp.where(place_ref[1] == 0, mask[:, :text], mask[:, text:])
+    for head in range(width // HEAD_DIM):
+        columns = slice(head * HEAD_DIM, (head + 1) * HEAD_DIM)
+        own = qo_ref[:, columns]
+        queries = jnp.concatenate([own, qp_ref[:, columns]], axis=0)
+        weights = weigh(queries, text_ref[0, :, columns]) * mask
+        num = times(weights, text_ref[1, :, columns])
+        den = lanes(weights)
+        num, den = absorb(queries, [loaders(ref) for ref in ring], num, den, columns)
+        fresh = weigh(own, fresh_ref[0, :, columns])
+        num_ref[:video, columns] = num[:video] + times(fresh, fresh_ref[1, :, columns])
+        num_ref[video:, columns] = num[video:]
+        packed = jnp.where(
+            lane == head,
+            jnp.sum(jnp.concatenate([den[:video] + fresh, den[video:]], axis=0), axis=1, keepdims=True),
+            packed,
+        )
     stale_copy.wait()
     for head in range(width // HEAD_DIM):
         columns = slice(head * HEAD_DIM, (head + 1) * HEAD_DIM)
-        own, other = qo_ref[:, columns], qp_ref[:, columns]
-        queries = jnp.concatenate([own, other], axis=0)
-        fresh = weigh(own, fresh_ref[0, :, columns])
-        stale = weigh(other, stale_buffer[0, :, columns])
-        num = jnp.concatenate(
-            [times(fresh, fresh_ref[1, :, columns]), times(stale, stale_buffer[1, :, columns])], axis=0
+        stale = weigh(qp_ref[:, columns], stale_buffer[0, :, columns])
+        num_ref[video:, columns] += times(stale, stale_buffer[1, :, columns])
+        total = jnp.concatenate(
+            [jnp.zeros((video, 1), F32), jnp.sum(stale, axis=1, keepdims=True)], axis=0
         )
-        den = jnp.concatenate([fresh, stale], axis=0)
-        weights = weigh(queries, text_ref[0, :, columns]) * mask_ref[...]
-        num = num + times(weights, text_ref[1, :, columns])
-        den = den + lanes(weights)
-        num, den = absorb(queries, [loaders(ref) for ref in ring], num, den, columns)
-        num_ref[:, columns] = num
-        packed = jnp.where(lane == head, jnp.sum(den, axis=1, keepdims=True), packed)
+        packed = packed + jnp.where(lane == head, total, 0.0)
     den_ref[...] = packed
     for copy in copies:
         copy.wait()
@@ -308,11 +336,16 @@
 
 def final_kernel(part_ref, att_ref, w_ref, hidden_ref, gate_ref, out_ref):
     total = part_ref[...] + jnp.dot(att_ref[...], w_ref[...], preferred_element_type=F32)
-    out_ref[...] = (hidden_ref[...].astype(F32) + gate_ref[...] * total).astype(BF16)
+    gate = gate_ref[...].reshape(1, total.shape[1])
+    out_ref[...] = (hidden_ref[...].astype(F32) + gate * total).astype(BF16)
 
 
 def params(megabytes):
     return pltpu.CompilerParams(vmem_limit_bytes=megabytes * 1024 * 1024)
+
+
+def in_hbm(array):
+    return pltpu.with_memory_space_constraint(array, pltpu.HBM)
 
 
 def cost(flops, nbytes, transcendentals=0):
@@ -366,8 +399,6 @@
     first_way, second_way = ring_moves(sections)
     half_way = chips // 2
 
-    mask = lax.dynamic_slice_in_dim(text_mask, core * text, text, 0).astype(F32).reshape(1, text)
-    query_gain, key_gain = query_gain.reshape(1, -1), key_gain.reshape(1, -1)
 
     def ring_step(up, down, *after):
         up, down = lax.optimization_barrier((up, down) + after)[:2]
@@ -390,7 +421,7 @@
     ]
     a_rows, message, stats = pl.pallas_call(
         send_kernel,
-        in_specs=[smem, hbm, hbm, vmem, vmem, hbm],
+        in_specs=[smem] + [hbm] * 5,
         out_specs=[vmem] * 3,
         out_shape=[
             jax.ShapeDtypeStruct((rows, features), BF16),
@@ -400,31 +431,35 @@
         scratch_shapes=[
             pltpu.VMEM((video, features), BF16),
             pltpu.VMEM((text, features), BF16),
+            pltpu.VMEM((features,), F32),
+            pltpu.VMEM((features,), F32),
             weight_scratch[0],
-            pltpu.SemaphoreType.DMA((2,)),
+            pltpu.SemaphoreType.DMA((4,)),
             weight_scratch[1],
         ],
         compiler_params=params(40),
         cost_estimate=project_cost,
         name="project_send",
-    )(place, hidden, text_hidden, norm_scale, norm_shift, qkv_weight)
+    )(place, *map(in_hbm, (hidden, text_hidden, norm_scale, norm_shift, qkv_weight)))
 
     received = lax.ppermute(message, "head", swap_head)
     ring.append(ring_step(*ring[-1], message))
 
-    own, own_text = pl.pallas_call(
+    small = (query_gain, key_gain, text_mask, branch_gate, hidden)
+    own, own_text, query_gain, key_gain, text_mask, branch_gate, hidden = pl.pallas_call(
         own_kernel,
-        in_specs=[smem, vmem, hbm],
-        out_specs=[vmem] * 2,
+        in_specs=[smem, vmem, hbm] + [hbm] * len(small),
+        out_specs=[vmem] * (2 + len(small)),
         out_shape=[
             jax.ShapeDtypeStruct((top, group_columns), F32),
             jax.ShapeDtypeStruct((text, 2 * width), F32),
-        ],
-        scratch_shapes=weight_scratch,
+        ]
+        + [jax.ShapeDtypeStruct(array.shape, array.dtype) for array in small],
+        scratch_shapes=weight_scratch + [pltpu.SemaphoreType.DMA((len(small),))],
         compiler_params=params(40),
         cost_estimate=project_cost,
         name="project_own",
-    )(place, a_rows, qkv_weight)
+    )(place, a_rows, *map(in_hbm, (qkv_weight,) + small))
 
     for _ in range(half_way - 3):
         ring.append(ring_step(*ring[-1], own))
@@ -468,7 +503,8 @@
         ),
         name="attend_first",
     )(
-        place[:1], out_weight, queries, other_queries, fresh, stale_cache, text_kv, mask, *arrived
+        place, in_hbm(out_weight), queries, other_queries, fresh, in_hbm(stale_cache), text_kv,
+        text_mask, *arrived,
     )
     num_own, den_own, num_message = plain_call(
         last_kernel,
@@ -494,7 +530,7 @@
     )
     (mixed,) = plain_call(
         final_kernel, [((video, out_features), BF16)], "final_out", out_cost,
-        part, other_attended, w_other, hidden, branch_gate.reshape(1, -1),
+        part, other_attended, w_other, hidden, branch_gate,
     )
     return (mixed, new_cache)
 

time: 64.2 us -> 58.9 us (0.917)
  local copies, waits for them, and re-layouts: 7.29 us -> 0 us
  starting transfers between devices: 11.9 us -> 13.9 us
  other arithmetic: 0.93 us -> 0.07 us
  waiting for transfers between devices: 21 us -> 21.8 us
    unnamed x30 -> x0, local copies, waits for them, and re-layouts: 7.29 us -> none
    ppermute x1, starting transfers between devices: 0.16 us -> 2.48 us  [per_device(): far = lax.ppermute(ring[-1][0], 'section', first_way)]
    ppermute x3, starting transfers between devices: 4.94 us -> 6.67 us  [ring_step(): lax.ppermute(up, 'section', first_way)]
    pallas_call x6, Pallas kernels: 5.7 us -> 4.6 us  [plain_call(): pl.pallas_call(kernel, in_specs=[pl.BlockSpec(memory_space=pltpu.VMEM)] *...]
    pallas_call x2, Pallas kernels: 10.6 us -> 11.6 us  [the longest x1 6.43 us: per_device(): pl.pallas_call(send_kernel, in_specs=[smem] + [hbm] * 5, out_specs=[vmem]...]
    ppermute x1, starting transfers between devices: 2.08 us -> 1.16 us  [per_device(): other_attended = lax.ppermute(attended, 'head', swap_head)]
    reshape x1 -> x0, other arithmetic: 0.85 us -> none  [per_device(): lax.dynamic_slice_in_dim(text_mask, core * text, text, 0).astype(F32)]
    ppermute x3, starting transfers between devices: 2.2 us -> 1.36 us  [ring_step(): lax.ppermute(down, 'section', second_way)]
  transfers between devices with their start and end apart: 11 -> 11, of which waited for: 5 -> 6; matrix products, arithmetic and copies ran while one was open for 1% -> 0% of each run, Pallas kernels for 29% -> 34%
where the time goes in v4:
time: 58.9 us; the launch traced here: 58.7 us
  Pallas kernels  22.2 us (38%)
  waiting for transfers between devices  21.8 us (37%)
  starting transfers between devices  13.9 us (24%)
  between operations  0.7 us (1%)
    ppermute x3, waiting for transfers between devices, ring_step(): lax.ppermute(up, 'section', first_way)  13.9 us
    ppermute x3, starting transfers between devices, ring_step(): lax.ppermute(up, 'section', first_way)  6.67 us
    pallas_call x1, Pallas kernels, per_device(): pl.pallas_call(send_kernel, in_specs=[smem] + [hbm] * 5, out_specs=[vmem]...  6.43 us
    pallas_call x1, Pallas kernels, per_device(): pl.pallas_call(functools.partial(first_kernel, len(arrived)), in_specs=[s...  5.99 us
    ppermute x1, waiting for transfers between devices, per_device(): other_attended = lax.ppermute(attended, 'head', swap_head)  5.37 us
    pallas_call x1, Pallas kernels, per_device(): pl.pallas_call(own_kernel, in_specs=[smem, vmem, hbm] + [hbm] * len(small...  5.22 us
    pallas_call x6, Pallas kernels, plain_call(): pl.pallas_call(kernel, in_specs=[pl.BlockSpec(memory_space=pltpu.VMEM)] *...  4.6 us
    ppermute x1, starting transfers between devices, per_device(): far = lax.ppermute(ring[-1][0], 'section', first_way)  2.48 us
  transfers between devices with their start and end apart: 11, of which 6 were waited for; matrix products, arithmetic and copies ran while one was open for 0% of the time, Pallas kernels for 34%

profile of v4, /device:TPU:0, one launch (start us, length us, event | category | flops | bytes accessed | tf_op | source)
XLA Modules:
  0.0 58.7 jit_solution(8668131325692608009)
XLA Ops:
  0.6 3.1 %collective-permute-start.2 = (bf16[2,128,768]{2,1,0:T(8,128)(2,1)}, bf16[2,128,768]{2,1,0:T(8,128)(2,1)S(1)}, u32[]{:S(2)}, u32[]{:S(2)}) collective-permute-start(bf16[2,128,768]{2,1,0:T(8,128)(2,1)} %stale_ref.1), channel_id=1, source_target_pairs={{0,8},{2,6},{4,0},{6,14},{8,16},{10,2},{12,4},{14,22},{16,24},{18,... | collective-permute-start | bytes 1179656 | tf_op jit(solution)/shard_map/ppermute | solution.py:405
  3.8 6.4 %project_send.1 = (bf16[272,1536]{1,0:T(8,128)(2,1)S(1)}, bf16[240,2304]{1,0:T(8,128)(2,1)S(1)}, f32[272,128]{1,0:T(8,128)S(1)}) custom-call(s32[2]{0:T(128)S(1)} %pad_add_fusion.place_ref, bf16[128,1536]{1,0:T(8,128)(2,1)} %refs_4_.1, bf16[256,1536]{1,0:T(8,128)(2,1)} %t_ref.1, f32[1536]{0:T(1024)} %scale_ref.1, f32[1536]{0:T(1024)} %shift_ref.1, ...), custom_call_target="tpu_custom_call" | custom-call | flops 1925185536 | bytes 7077888 | tf_op jit(solution)/shard_map/project_send/pallas_call | solution.py:422
  10.2 2.0 %collective-permute-start = (bf16[240,2304]{1,0:T(8,128)(2,1)S(1)}, bf16[240,2304]{1,0:T(8,128)(2,1)S(1)}, u32[]{:S(2)}, u32[]{:S(2)}) collective-permute-start(bf16[240,2304]{1,0:T(8,128)(2,1)S(1)} %get-tuple-element.30), channel_id=1, source_target_pairs={{0,1},{1,0},{2,3},{3,2},{4,5},{5,4},{6,7},{7,6},{8,9},{9,8},{10,11... | collective-permute-start | bytes 3317768 | tf_op jit(solution)/shard_map/ppermute | solution.py:445
  12.2 1.1 %collective-permute-done.2.refs_0_ = bf16[2,128,768]{2,1,0:T(8,128)(2,1)S(1)} collective-permute-done((bf16[2,128,768]{2,1,0:T(8,128)(2,1)}, bf16[2,128,768]{2,1,0:T(8,128)(2,1)S(1)}, u32[]{:S(2)}, u32[]{:S(2)}) %collective-permute-start.2) | collective-permute-done | bytes 393248 | tf_op jit(solution)/shard_map/ppermute | solution.py:405
  13.3 1.6 %collective-permute-start.4 = (bf16[2,128,768]{2,1,0:T(8,128)(2,1)S(1)}, bf16[2,128,768]{2,1,0:T(8,128)(2,1)S(1)}, u32[]{:S(2)}, u32[]{:S(2)}) collective-permute-start(bf16[2,128,768]{2,1,0:T(8,128)(2,1)S(1)} %collective-permute-done.2.refs_0_), channel_id=1, source_target_pairs={{0,8},{2,6},{4,0},{6,14},{8,16},{10,2},{12,4},{14,22},{16,24},{18,... | collective-permute-start | bytes 1179656 | tf_op jit(solution)/shard_map/ppermute | solution.py:405
  14.8 0.8 %collective-permute-start.5 = (bf16[2,128,768]{2,1,0:T(8,128)(2,1)S(1)}, bf16[2,128,768]{2,1,0:T(8,128)(2,1)S(1)}, u32[]{:S(2)}, u32[]{:S(2)}) collective-permute-start(bf16[2,128,768]{2,1,0:T(8,128)(2,1)S(1)} %collective-permute-done.3.refs_1_), channel_id=1, source_target_pairs={{0,4},{2,10},{4,12},{6,2},{8,0},{10,18},{12,20},{14,6},{16,8},{18,... | collective-permute-start | bytes 1179656 | tf_op jit(solution)/shard_map/ppermute | solution.py:405
  15.7 5.2 %project_own.1 = (f32[144,2304]{1,0:T(8,128)S(1)}, f32[128,1536]{1,0:T(8,128)S(1)}, f32[128]{0:T(128)S(1)}, f32[128]{0:T(128)S(1)}, s32[256]{0:T(256)S(1)}, /*in...) custom-call(s32[2]{0:T(128)S(1)} %pad_add_fusion.place_ref, bf16[272,1536]{1,0:T(8,128)(2,1)S(1)} %get-tuple-element.28.a_ref, ...), custom_call_target="tpu_custom_call" | custom-call | flops 1925185536 | bytes 7077888 | tf_op jit(solution)/shard_map/project_own/pallas_call | solution.py:449
  20.9 3.9 %collective-permute-done.4.refs_2_ = bf16[2,128,768]{2,1,0:T(8,128)(2,1)S(1)} collective-permute-done((bf16[2,128,768]{2,1,0:T(8,128)(2,1)S(1)}, bf16[2,128,768]{2,1,0:T(8,128)(2,1)S(1)}, u32[]{:S(2)}, u32[]{:S(2)}) %collective-permute-start.4) | collective-permute-done | bytes 393248 | tf_op jit(solution)/shard_map/ppermute | solution.py:405
  24.8 2.0 %collective-permute-start.6 = (bf16[2,128,768]{2,1,0:T(8,128)(2,1)S(1)}, bf16[2,128,768]{2,1,0:T(8,128)(2,1)S(1)}, u32[]{:S(2)}, u32[]{:S(2)}) collective-permute-start(bf16[2,128,768]{2,1,0:T(8,128)(2,1)S(1)} %collective-permute-done.4.refs_2_), channel_id=1, source_target_pairs={{0,8},{2,6},{4,0},{6,14},{8,16},{10,2},{12,4},{14,22},{16,24},{18,... | collective-permute-start | bytes 1179656 | tf_op jit(solution)/shard_map/ppermute | solution.py:405
  26.8 0.5 collective-permute-start.7
  27.3 9.0 %collective-permute-done.6.refs_4_ = bf16[2,128,768]{2,1,0:T(8,128)(2,1)S(1)} collective-permute-done((bf16[2,128,768]{2,1,0:T(8,128)(2,1)S(1)}, bf16[2,128,768]{2,1,0:T(8,128)(2,1)S(1)}, u32[]{:S(2)}, u32[]{:S(2)}) %collective-permute-start.6) | collective-permute-done | bytes 393248 | tf_op jit(solution)/shard_map/ppermute | solution.py:405
  36.3 2.5 %collective-permute-start.8 = (bf16[2,128,768]{2,1,0:T(8,128)(2,1)S(1)}, bf16[2,128,768]{2,1,0:T(8,128)(2,1)S(1)}, u32[]{:S(2)}, u32[]{:S(2)}) collective-permute-start(bf16[2,128,768]{2,1,0:T(8,128)(2,1)S(1)} %collective-permute-done.6.refs_4_), channel_id=1, source_target_pairs={{0,8},{2,6},{4,0},{6,14},{8,16},{10,2},{12,4},{14,22},{16,24},{18,... | collective-permute-start | bytes 1179656 | tf_op jit(solution)/shard_map/ppermute | solution.py:467
  38.8 1.5 %norm_video.1 = (bf16[128,768]{1,0:T(8,128)(2,1)S(1)}, bf16[2,128,768]{2,1,0:T(8,128)(2,1)}, bf16[2,128,768]{2,1,0:T(8,128)(2,1)S(1)}) custom-call(f32[144,2304]{1,0:T(8,128)S(1)} %get-tuple-element.29.own_ref.top_ref, bf16[240,2304]{1,0:T(8,128)(2,1)S(1)} %collective-permute-done.msg_ref, f32[272,128]{1,0:T(8,128)S(1)} %get-tuple-element.31.stat_ref, ...), custom_call_target="tpu_custom_call" | custom-call | flops 6635520 | bytes 2654208 | tf_op jit(solution)/shard_map/norm_video/pallas_call | solution.py:358
  40.3 0.6 norm_text.1.text_ref
  40.9 0.8 %collective-permute-done.1.qp_ref = bf16[128,768]{1,0:T(8,128)(2,1)S(1)} collective-permute-done((bf16[128,768]{1,0:T(8,128)(2,1)S(1)}, bf16[128,768]{1,0:T(8,128)(2,1)S(1)}, u32[]{:S(2)}, u32[]{:S(2)}) %collective-permute-start.1) | collective-permute-done | bytes 196640 | tf_op jit(solution)/shard_map/ppermute | solution.py:476
  41.8 6.0 %attend_first.1 = (f32[256,768]{1,0:T(8,128)S(1)}, f32[256,128]{1,0:T(8,128)S(1)}, bf16[768,1536]{1,0:T(8,128)(2,1)S(1)}, bf16[768,1536]{1,0:T(8,128)(2,1)S(1)}) custom-call(s32[2]{0:T(128)S(1)} %pad_add_fusion.place_ref, bf16[1536,1536]{1,0:T(8,128)(2,1)} %weight_ref.1, bf16[128,768]{1,0:T(8,128)(2,1)S(1)} %get-tuple-element.34.qo_ref, ...), custom_call_target="tpu_custom_call" | custom-call | flops 805306368 | bytes 3145728 | tf_op jit(solution)/shard_map/attend_first/pallas_call | solution.py:486
  47.8 0.6 %attend_last.1 = (f32[128,768]{1,0:T(8,128)S(1)}, f32[128,128]{1,0:T(8,128)S(1)}, f32[128,896]{1,0:T(8,128)S(1)}) custom-call(bf16[128,768]{1,0:T(8,128)(2,1)S(1)} %get-tuple-element.34.qo_ref, bf16[128,768]{1,0:T(8,128)(2,1)S(1)} %collective-permute-done.1.qp_ref, f32[256,768]{1,0:T(8,128)S(1)} %get-tuple-element.44.num_ref, ...), custom_call_target="tpu_custom_call" | custom-call | flops 100663296 | bytes 1179648 | tf_op jit(solution)/shard_map/attend_last/pallas_call | solution.py:358
  48.4 0.2 collective-permute-start.9
  48.6 1.7 %collective-permute-done.9.msg_ref = f32[128,896]{1,0:T(8,128)S(1)} collective-permute-done((f32[128,896]{1,0:T(8,128)S(1)}, f32[128,896]{1,0:T(8,128)S(1)}, u32[]{:S(2)}, u32[]{:S(2)}) %collective-permute-start.9) | collective-permute-done | bytes 458784 | tf_op jit(solution)/shard_map/ppermute | solution.py:517
  50.3 0.2 merge.1.att_ref
  50.5 1.2 %collective-permute-start.10 = (bf16[128,768]{1,0:T(8,128)(2,1)S(1)}, bf16[128,768]{1,0:T(8,128)(2,1)S(1)}, u32[]{:S(2)}, u32[]{:S(2)}) collective-permute-start(bf16[128,768]{1,0:T(8,128)(2,1)S(1)} %merge.1.att_ref), channel_id=1, source_target_pairs={{0,1},{1,0},{2,3},{3,2},{4,5},{5,4},{6,7},{7,6},{8,9},{9,8},{10,11... | collective-permute-start | bytes 589832 | tf_op jit(solution)/shard_map/ppermute | solution.py:525
  51.6 0.5 part_out.1.part_ref
  52.1 5.4 %collective-permute-done.10.att_ref = bf16[128,768]{1,0:T(8,128)(2,1)S(1)} collective-permute-done((bf16[128,768]{1,0:T(8,128)(2,1)S(1)}, bf16[128,768]{1,0:T(8,128)(2,1)S(1)}, u32[]{:S(2)}, u32[]{:S(2)}) %collective-permute-start.10) | collective-permute-done | bytes 196640 | tf_op jit(solution)/shard_map/ppermute | solution.py:525
  57.5 1.2 %final_out.1 = bf16[128,1536]{1,0:T(8,128)(2,1)} custom-call(f32[128,1536]{1,0:T(8,128)S(1)} %part_out.1.part_ref, bf16[128,768]{1,0:T(8,128)(2,1)S(1)} %collective-permute-done.10.att_ref, bf16[768,1536]{1,0:T(8,128)(2,1)S(1)} %get-tuple-element.50.w_ref, bf16[128,1536]{1,0:T(8,128)(2,1)S(1)} %get-tuple-element.51.hidden_ref, ...), custom_call_target="tpu_custom_call" | custom-call | flops 301989888 | bytes 2359296 | tf_op jit(solution)/shard_map/final_out/pallas_call | solution.py:358
  (8 shorter events, 0.1 us)
Async XLA Ops:
  0.6 12.7 %collective-permute-start.2 = (bf16[2,128,768]{2,1,0:T(8,128)(2,1)}, bf16[2,128,768]{2,1,0:T(8,128)(2,1)S(1)}, u32[]{:S(2)}, u32[]{:S(2)}) collective-permute-start(bf16[2,128,768]{2,1,0:T(8,128)(2,1)} %stale_ref.1), channel_id=1, source_target_pairs={{0,8},{2,6},{4,0},{6,14},{8,16},{10,2},{12,4},{14,22},{16,24},{18,... | collective-permute-start | bytes 1179656 | tf_op jit(solution)/shard_map/ppermute | solution.py:405
  3.7 9.6 %collective-permute-start.3 = (bf16[2,128,768]{2,1,0:T(8,128)(2,1)}, bf16[2,128,768]{2,1,0:T(8,128)(2,1)S(1)}, u32[]{:S(2)}, u32[]{:S(2)}) collective-permute-start(bf16[2,128,768]{2,1,0:T(8,128)(2,1)} %stale_ref.1), channel_id=1, source_target_pairs={{0,4},{2,10},{4,12},{6,2},{8,0},{10,18},{12,20},{14,6},{16,8},{18,... | collective-permute-start | bytes 1179656 | tf_op jit(solution)/shard_map/ppermute | solution.py:405
  10.2 28.6 %collective-permute-start = (bf16[240,2304]{1,0:T(8,128)(2,1)S(1)}, bf16[240,2304]{1,0:T(8,128)(2,1)S(1)}, u32[]{:S(2)}, u32[]{:S(2)}) collective-permute-start(bf16[240,2304]{1,0:T(8,128)(2,1)S(1)} %get-tuple-element.30), channel_id=1, source_target_pairs={{0,1},{1,0},{2,3},{3,2},{4,5},{5,4},{6,7},{7,6},{8,9},{9,8},{10,11... | collective-permute-start | bytes 3317768 | tf_op jit(solution)/shard_map/ppermute | solution.py:445
  13.3 11.5 %collective-permute-start.4 = (bf16[2,128,768]{2,1,0:T(8,128)(2,1)S(1)}, bf16[2,128,768]{2,1,0:T(8,128)(2,1)S(1)}, u32[]{:S(2)}, u32[]{:S(2)}) collective-permute-start(bf16[2,128,768]{2,1,0:T(8,128)(2,1)S(1)} %collective-permute-done.2.refs_0_), channel_id=1, source_target_pairs={{0,8},{2,6},{4,0},{6,14},{8,16},{10,2},{12,4},{14,22},{16,24},{18,... | collective-permute-start | bytes 1179656 | tf_op jit(solution)/shard_map/ppermute | solution.py:405
  14.8 9.9 %collective-permute-start.5 = (bf16[2,128,768]{2,1,0:T(8,128)(2,1)S(1)}, bf16[2,128,768]{2,1,0:T(8,128)(2,1)S(1)}, u32[]{:S(2)}, u32[]{:S(2)}) collective-permute-start(bf16[2,128,768]{2,1,0:T(8,128)(2,1)S(1)} %collective-permute-done.3.refs_1_), channel_id=1, source_target_pairs={{0,4},{2,10},{4,12},{6,2},{8,0},{10,18},{12,20},{14,6},{16,8},{18,... | collective-permute-start | bytes 1179656 | tf_op jit(solution)/shard_map/ppermute | solution.py:405
  24.8 11.5 %collective-permute-start.6 = (bf16[2,128,768]{2,1,0:T(8,128)(2,1)S(1)}, bf16[2,128,768]{2,1,0:T(8,128)(2,1)S(1)}, u32[]{:S(2)}, u32[]{:S(2)}) collective-permute-start(bf16[2,128,768]{2,1,0:T(8,128)(2,1)S(1)} %collective-permute-done.4.refs_2_), channel_id=1, source_target_pairs={{0,8},{2,6},{4,0},{6,14},{8,16},{10,2},{12,4},{14,22},{16,24},{18,... | collective-permute-start | bytes 1179656 | tf_op jit(solution)/shard_map/ppermute | solution.py:405
  26.8 14.1 %collective-permute-start.7 = (bf16[2,128,768]{2,1,0:T(8,128)(2,1)S(1)}, bf16[2,128,768]{2,1,0:T(8,128)(2,1)S(1)}, u32[]{:S(2)}, u32[]{:S(2)}) collective-permute-start(bf16[2,128,768]{2,1,0:T(8,128)(2,1)S(1)} %collective-permute-done.5.refs_3_), channel_id=1, source_target_pairs={{0,4},{2,10},{4,12},{6,2},{8,0},{10,18},{12,20},{14,6},{16,8},{18,... | collective-permute-start | bytes 1179656 | tf_op jit(solution)/shard_map/ppermute | solution.py:405
  36.3 11.5 %collective-permute-start.8 = (bf16[2,128,768]{2,1,0:T(8,128)(2,1)S(1)}, bf16[2,128,768]{2,1,0:T(8,128)(2,1)S(1)}, u32[]{:S(2)}, u32[]{:S(2)}) collective-permute-start(bf16[2,128,768]{2,1,0:T(8,128)(2,1)S(1)} %collective-permute-done.6.refs_4_), channel_id=1, source_target_pairs={{0,8},{2,6},{4,0},{6,14},{8,16},{10,2},{12,4},{14,22},{16,24},{18,... | collective-permute-start | bytes 1179656 | tf_op jit(solution)/shard_map/ppermute | solution.py:467
  40.3 1.4 %collective-permute-start.1 = (bf16[128,768]{1,0:T(8,128)(2,1)S(1)}, bf16[128,768]{1,0:T(8,128)(2,1)S(1)}, u32[]{:S(2)}, u32[]{:S(2)}) collective-permute-start(bf16[128,768]{1,0:T(8,128)(2,1)S(1)} %get-tuple-element.34.qo_ref), channel_id=1, source_target_pairs={{0,2},{2,0},{4,6},{6,4},{8,10},{10,8},{12,14},{14,12},{16,18},{18,... | collective-permute-start | bytes 589832 | tf_op jit(solution)/shard_map/ppermute | solution.py:476
  48.4 1.9 %collective-permute-start.9 = (f32[128,896]{1,0:T(8,128)S(1)}, f32[128,896]{1,0:T(8,128)S(1)}, u32[]{:S(2)}, u32[]{:S(2)}) collective-permute-start(f32[128,896]{1,0:T(8,128)S(1)} %get-tuple-element.48), channel_id=1, source_target_pairs={{0,2},{2,0},{4,6},{6,4},{8,10},{10,8},{12,14},{14,12},{16,18},{18,... | collective-permute-start | bytes 1376264 | tf_op jit(solution)/shard_map/ppermute | solution.py:517
  50.5 7.0 %collective-permute-start.10 = (bf16[128,768]{1,0:T(8,128)(2,1)S(1)}, bf16[128,768]{1,0:T(8,128)(2,1)S(1)}, u32[]{:S(2)}, u32[]{:S(2)}) collective-permute-start(bf16[128,768]{1,0:T(8,128)(2,1)S(1)} %merge.1.att_ref), channel_id=1, source_target_pairs={{0,1},{1,0},{2,3},{3,2},{4,5},{5,4},{6,7},{7,6},{8,9},{9,8},{10,11... | collective-permute-start | bytes 589832 | tf_op jit(solution)/shard_map/ppermute | solution.py:525

commit v5 on v3

v5 whole, which is shorter than its diff:
```python
import functools
import math

import jax
import jax.numpy as jnp
from jax import lax
from jax.experimental import pallas as pl
from jax.experimental.pallas import tpu as pltpu
from jax.sharding import PartitionSpec as P

HEAD_DIM = 128
TRIPLE = 3 * HEAD_DIM
EXTRA = 16
STAT_ROW = 8
EPS = 1e-06
F32 = jnp.float32
BF16 = jnp.bfloat16


def split_bf16(value, parts):
    pieces = []
    rest = value
    for _ in range(parts):
        piece = rest.astype(BF16)
        pieces.append(piece)
        rest = rest - piece.astype(F32)
    return pieces


def start_weights(w_ref, buffer_ref, sems, first):
    count, _, columns = buffer_ref.shape
    copies = []
    for index in range(count):
        start = pl.multiple_of(first + index * columns, HEAD_DIM)
        copy = pltpu.make_async_copy(
            w_ref.at[:, pl.ds(start, columns)], buffer_ref.at[index], sems.at[index]
        )
        copy.start()
        copies.append(copy)
    return copies


def send_kernel(
    place_ref, x_ref, t_ref, scale_ref, shift_ref, w_ref,
    a_ref, msg_ref, tmsg_ref, stat_ref, w_own_ref,
    x_buffer, t_buffer, scale_buffer, shift_buffer, w_buffer, in_sems, w_sems, own_sems,
):
    video, features = x_buffer.shape
    text = t_buffer.shape[0]
    top = video + EXTRA
    blocks, _, columns = w_buffer.shape
    width = blocks * columns
    copies = [
        pltpu.make_async_copy(scale_ref, scale_buffer, in_sems.at[0]),
        pltpu.make_async_copy(shift_ref, shift_buffer, in_sems.at[1]),
        pltpu.make_async_copy(x_ref, x_buffer, in_sems.at[2]),
        pltpu.make_async_copy(
            t_ref.at[pl.ds(pl.multiple_of(place_ref[1] * text, text), text)], t_buffer, in_sems.at[3]
        ),
    ]
    for copy in copies:
        copy.start()
    w_copies = start_weights(w_ref, w_buffer, w_sems, (1 - place_ref[0]) * width)
    own_copies = start_weights(w_ref, w_own_ref, own_sems, place_ref[0] * width)

    copies[0].wait()
    copies[1].wait()
    gain = 1.0 + scale_buffer[...].reshape(1, features)
    pieces = split_bf16(gain, 2) + split_bf16(shift_buffer[...].reshape(1, features), 2)
    row = lax.broadcasted_iota(jnp.int32, (EXTRA, features), 0)
    extra = jnp.zeros((EXTRA, features), F32)
    for index, piece in enumerate(pieces):
        extra = jnp.where(row == index, piece.astype(F32), extra)
    a_ref[video:top, :] = extra.astype(BF16)

    def prepare(rows_ref, start):
        rows = rows_ref[...].astype(F32)
        count = rows.shape[0]
        mean = jnp.sum(rows, axis=1, keepdims=True) * (1.0 / features)
        centered = rows - mean
        second = jnp.sum(centered * centered, axis=1, keepdims=True)
        a_ref[start : start + count, :] = (centered * gain).astype(BF16)
        lane = lax.broadcasted_iota(jnp.int32, (count, HEAD_DIM), 1)
        packed = jnp.zeros((count, HEAD_DIM), F32)
        for index, piece in enumerate(split_bf16(mean, 3) + split_bf16(second, 3)):
            packed = jnp.where(lane == STAT_ROW + index, piece.astype(F32), packed)
        stat_ref[start : start + count, :] = jnp.where(
            lane == 0, mean, jnp.where(lane == 1, second, 0.0)
        )
        return jnp.transpose(packed)[:EXTRA]

    copies[2].wait()
    video_stats = prepare(x_buffer, 0)
    copies[3].wait()
    text_stats = prepare(t_buffer, top)
    stat_ref[video:top, :] = jnp.zeros((EXTRA, HEAD_DIM), F32)

    def write(start, product):
        cells = slice(start, start + product.shape[1])
        msg_ref[:, cells] = product[:top].astype(BF16)
        if start == 0:
            stats = jnp.concatenate([video_stats, text_stats], axis=1)
            msg_ref[video:, : video + text] = (product[video:top] + stats).astype(BF16)
        for source, target in text_columns(start, product.shape[1]):
            tmsg_ref[:, target] = product[top:, source].astype(BF16)

    for block in range(blocks):
        w_copies[block].wait()
        multiply(a_ref, w_buffer.at[block], block * columns, write)
    for copy in own_copies:
        copy.wait()


PIECE = 2 * HEAD_DIM


def multiply(a_ref, w_ref, first, write):
    for start in range(0, w_ref.shape[1], PIECE):
        piece = jnp.dot(
            a_ref[...], w_ref[:, start : start + PIECE], preferred_element_type=F32
        )
        write(first + start, piece)


def text_columns(first, count):
    for start in range(0, count, HEAD_DIM):
        head, kind = divmod((first + start) // HEAD_DIM, 3)
        if kind:
            target = (2 * head + kind - 1) * HEAD_DIM
            yield slice(start, start + HEAD_DIM), slice(target, target + HEAD_DIM)


def own_kernel(place_ref, a_ref, w_ref, out_weight_ref, *refs):
    small = (len(refs) - 5) // 2
    out_ref, text_ref, w_own_ref, w_other_ref = refs[small : small + 4]
    sems = refs[-1]
    top = out_ref.shape[0]
    depth = w_own_ref.shape[0]
    group = place_ref[0]
    pairs = list(zip(refs[:small], refs[small + 4 : -1]))
    for half, target in ((group, w_own_ref), (1 - group, w_other_ref)):
        rows = pl.ds(pl.multiple_of(half * depth, depth), depth)
        pairs.append((out_weight_ref.at[rows], target))
    copies = []
    for index, (source, target) in enumerate(pairs):
        copies.append(pltpu.make_async_copy(source, target, sems.at[index]))
        copies[-1].start()

    def write(start, product):
        out_ref[:, start : start + product.shape[1]] = product[:top]
        for source, target in text_columns(start, product.shape[1]):
            text_ref[:, target] = product[top:, source]

    blocks, _, columns = w_ref.shape
    for block in range(blocks):
        multiply(a_ref, w_ref.at[block], block * columns, write)
    for copy in copies:
        copy.wait()


def split_kernel(block_ref, first_ref, second_ref, sems):
    width = first_ref.shape[2]
    copies = [
        pltpu.make_async_copy(
            block_ref.at[:, :, pl.ds(index * width, width)], target, sems.at[index]
        )
        for index, target in enumerate((first_ref, second_ref))
    ]
    for copy in copies:
        copy.start()
    for copy in copies:
        copy.wait()


def row_stats(total_features, own, received):
    count = own.shape[0]
    received = received.astype(F32)
    padding = jnp.zeros((HEAD_DIM - received.shape[0], count), F32)
    received = jnp.transpose(jnp.concatenate([received, padding], axis=0))
    parts = [received[:, STAT_ROW + index : STAT_ROW + index + 1] for index in range(6)]
    gap = 0.5 * (own[:, 0:1] - (parts[0] + parts[1] + parts[2]))
    second = own[:, 1:2] + (parts[3] + parts[4] + parts[5])
    var = second * (1.0 / total_features) + gap * gap
    return gap, lax.rsqrt(var + EPS)


def column_terms(own, other):
    other = other.astype(F32)
    scale = (own[0:1] + own[1:2]) - (other[0:1] + other[1:2])
    shift = (own[2:3] + own[3:4]) + (other[2:3] + other[3:4])
    return scale, shift


def head_norm(part, gain):
    square = jnp.sum(part * part, axis=1, keepdims=True) * (1.0 / HEAD_DIM)
    return part * lax.rsqrt(square + EPS) * gain


def norm_kernel(
    total_features, own_ref, msg_ref, stat_ref, qg_ref, kg_ref, q_ref, cache_ref, kv_ref,
):
    video = q_ref.shape[0]
    top = video + EXTRA
    query_gain = qg_ref[...].reshape(1, HEAD_DIM)
    key_gain = kg_ref[...].reshape(1, HEAD_DIM)
    heads = q_ref.shape[1] // HEAD_DIM
    gap, inverse = row_stats(total_features, stat_ref[:video, :], msg_ref[video:top, :video])
    for head in range(heads):
        part = slice(head * TRIPLE, (head + 1) * TRIPLE)
        columns = slice(head * HEAD_DIM, (head + 1) * HEAD_DIM)
        scale, shift = column_terms(own_ref[video:, part], msg_ref[video:top, part])
        total = own_ref[:video, part] + msg_ref[:video, part].astype(F32)
        total = (total + gap * scale) * inverse + shift
        q_ref[:, columns] = head_norm(total[:, :HEAD_DIM], query_gain).astype(BF16)
        keys = head_norm(total[:, HEAD_DIM : 2 * HEAD_DIM], key_gain).astype(BF16)
        values = total[:, 2 * HEAD_DIM :].astype(BF16)
        cache_ref[0, :, columns] = keys
        cache_ref[1, :, columns] = values
        kv_ref[0, :, columns] = keys
        kv_ref[1, :, columns] = values


def text_kernel(total_features, own_ref, tmsg_ref, stat_ref, top_ref, msg_ref, kg_ref, kv_ref):
    text = kv_ref.shape[1]
    heads = kv_ref.shape[2] // HEAD_DIM
    top = top_ref.shape[0]
    video = top - EXTRA
    key_gain = kg_ref[...].reshape(1, HEAD_DIM)
    gap, inverse = row_stats(
        total_features, stat_ref[top:, :], msg_ref[video:top, video : video + text]
    )
    for head in range(heads):
        part = slice(head * TRIPLE + HEAD_DIM, (head + 1) * TRIPLE)
        pair = slice(head * 2 * HEAD_DIM, (head + 1) * 2 * HEAD_DIM)
        columns = slice(head * HEAD_DIM, (head + 1) * HEAD_DIM)
        scale, shift = column_terms(top_ref[video:, part], msg_ref[video:top, part])
        total = own_ref[:, pair] + tmsg_ref[:, pair].astype(F32)
        total = (total + gap * scale) * inverse + shift
        kv_ref[0, :, columns] = head_norm(total[:, :HEAD_DIM], key_gain).astype(BF16)
        kv_ref[1, :, columns] = total[:, HEAD_DIM:].astype(BF16)


FACTOR = math.log2(math.e) / math.sqrt(HEAD_DIM)


def weigh(rows, keys):
    scores = lax.dot_general(rows, keys, (((1,), (1,)), ((), ())), preferred_element_type=F32)
    return jnp.exp2(scores * FACTOR)


def lanes(weights):
    total = weights[:, :HEAD_DIM]
    for start in range(HEAD_DIM, weights.shape[1], HEAD_DIM):
        total = total + weights[:, start : start + HEAD_DIM]
    return total


def times(weights, values):
    return jnp.dot(weights.astype(BF16), values, preferred_element_type=F32)


def absorb(queries, blocks, num, den):
    for first in range(0, len(blocks), 2):
        pair = blocks[first : first + 2]
        keys = jnp.concatenate([ref[0, :, columns] for ref, columns in pair], axis=0)
        values = jnp.concatenate([ref[1, :, columns] for ref, columns in pair], axis=0)
        weights = weigh(queries, keys)
        num = num + times(weights, values)
        den = den + lanes(weights)
    return num, den


def first_kernel(qo_ref, qp_ref, fresh_ref, *refs):
    num_ref, den_ref = refs[-2:]
    stales, halves = refs[:2], refs[2:-2]
    video, width = qo_ref.shape
    lane = lax.broadcasted_iota(jnp.int32, (2 * video, HEAD_DIM), 1)
    packed = jnp.zeros((2 * video, HEAD_DIM), F32)
    for head in range(width // HEAD_DIM):
        columns = slice(head * HEAD_DIM, (head + 1) * HEAD_DIM)
        second, start = divmod(head * HEAD_DIM, width // 2)
        cells = slice(start, start + HEAD_DIM)
        own, other = qo_ref[:, columns], qp_ref[:, columns]
        queries = jnp.concatenate([own, other], axis=0)
        fresh = weigh(own, fresh_ref[0, :, columns])
        stale_ref = stales[second]
        stale = weigh(other, stale_ref[0, :, cells])
        num = jnp.concatenate(
            [times(fresh, fresh_ref[1, :, columns]), times(stale, stale_ref[1, :, cells])], axis=0
        )
        den = jnp.concatenate([fresh, stale], axis=0)
        num, den = absorb(queries, [(ref, cells) for ref in halves[second::2]], num, den)
        num_ref[:, columns] = num
        packed = jnp.where(lane == head, jnp.sum(den, axis=1, keepdims=True), packed)
    den_ref[...] = packed


def last_kernel(
    first, place_ref, qo_ref, qp_ref, num_ref, den_ref, text_ref, mask_ref, far_ref,
    own_ref, own_den_ref, msg_ref,
):
    video = qo_ref.shape[0]
    text, width = text_ref.shape[1], far_ref.shape[2]
    lane = lax.broadcasted_iota(jnp.int32, (2 * video, HEAD_DIM), 1)
    mask = mask_ref[...].reshape(1, 2 * text).astype(F32)
    mask = jnp.where(place_ref[1] == 0, mask[:, :text], mask[:, text:])
    keep = jnp.concatenate([mask, jnp.ones((1, video), F32)], axis=1)
    packed = den_ref[...]
    for head in range(width // HEAD_DIM):
        cells = slice(head * HEAD_DIM, (head + 1) * HEAD_DIM)
        columns = slice((first + head) * HEAD_DIM, (first + head + 1) * HEAD_DIM)
        queries = jnp.concatenate([qo_ref[:, columns], qp_ref[:, columns]], axis=0)
        keys = jnp.concatenate([text_ref[0, :, columns], far_ref[0, :, cells]], axis=0)
        values = jnp.concatenate([text_ref[1, :, columns], far_ref[1, :, cells]], axis=0)
        weights = weigh(queries, keys) * keep
        num = num_ref[:, columns] + times(weights, values)
        own_ref[:, cells] = num[:video]
        msg_ref[:, cells] = num[video:]
        total = jnp.sum(lanes(weights), axis=1, keepdims=True)
        packed = packed + jnp.where(lane == first + head, total, 0.0)
    own_den_ref[...] = packed[:video]
    msg_ref[:, width:] = packed[video:]


def merge_kernel(first, own_ref, den_ref, msg_ref, att_ref):
    width = att_ref.shape[1]
    for head in range(width // HEAD_DIM):
        columns = slice(head * HEAD_DIM, (head + 1) * HEAD_DIM)
        lane = first + head
        num = own_ref[:, columns] + msg_ref[:, columns]
        den = den_ref[:, lane : lane + 1] + msg_ref[:, width + lane : width + lane + 1]
        att_ref[:, columns] = (num / den).astype(BF16)


def project_out(first_ref, second_ref, w_ref):
    half = first_ref.shape[1]
    return jnp.dot(first_ref[...], w_ref[:half, :], preferred_element_type=F32) + jnp.dot(
        second_ref[...], w_ref[half:, :], preferred_element_type=F32
    )


def part_kernel(first_ref, second_ref, w_ref, out_ref):
    out_ref[...] = project_out(first_ref, second_ref, w_ref)


def final_kernel(part_ref, first_ref, second_ref, w_ref, hidden_ref, gate_ref, out_ref):
    total = part_ref[...] + project_out(first_ref, second_ref, w_ref)
    gate = gate_ref[...].reshape(1, total.shape[1])
    out_ref[...] = (hidden_ref[...].astype(F32) + gate * total).astype(BF16)


def params(megabytes):
    return pltpu.CompilerParams(vmem_limit_bytes=megabytes * 1024 * 1024)


def in_hbm(array):
    return pltpu.with_memory_space_constraint(array, pltpu.HBM)


def cost(flops, nbytes, transcendentals=0):
    return pl.CostEstimate(
        flops=int(flops), bytes_accessed=int(nbytes), transcendentals=int(transcendentals)
    )


def plain_call(kernel, outs, name, estimate, *operands):
    return pl.pallas_call(
        kernel,
        in_specs=[pl.BlockSpec(memory_space=pltpu.VMEM)] * len(operands),
        out_specs=[pl.BlockSpec(memory_space=pltpu.VMEM)] * len(outs),
        out_shape=[jax.ShapeDtypeStruct(shape, dtype) for shape, dtype in outs],
        compiler_params=params(24),
        cost_estimate=estimate,
        name=name,
    )(*operands)


def ring_moves(sections):
    chips = sections // 2
    order = list(range(0, chips, 2)) + list(range(chips - 1, 0, -2))
    moves = [], []
    for here, there in zip(order, order[1:] + order[:1]):
        for core in range(2):
            moves[core].append((2 * here + core, 2 * there + core))
            moves[1 - core].append((2 * there + core, 2 * here + core))
    return sorted(moves[0]), sorted(moves[1])


def per_device(
    sections, hidden, text_hidden, text_mask, stale_cache, qkv_weight, out_weight, query_gain,
    key_gain, norm_shift, norm_scale, branch_gate,
):
    video, features = hidden.shape
    text = text_hidden.shape[0] // 2
    width = stale_cache.shape[2]
    heads = width // HEAD_DIM
    group_columns = heads * TRIPLE
    chips = sections // 2
    out_features = out_weight.shape[1]
    top = video + EXTRA
    rows = top + text

    group = lax.axis_index("head")
    core = lax.axis_index("section") % 2
    place = jnp.stack([group, core]).astype(jnp.int32)
    swap_core = [(s, s ^ 1) for s in range(sections)]
    swap_head = [(0, 1), (1, 0)]
    ways = ring_moves(sections)
    half_way = chips // 2

    def ring_step(blocks):
        return [lax.ppermute(block, "section", way) for block, way in zip(blocks, ways)]

    vmem = pl.BlockSpec(memory_space=pltpu.VMEM)
    hbm = pl.BlockSpec(memory_space=pltpu.HBM)
    smem = pl.BlockSpec(memory_space=pltpu.SMEM)
    half_block = jax.ShapeDtypeStruct((2, video, width // 2), BF16)
    stale = pl.pallas_call(
        split_kernel,
        in_specs=[hbm],
        out_specs=[vmem] * 2,
        out_shape=[half_block] * 2,
        scratch_shapes=[pltpu.SemaphoreType.DMA((2,))],
        compiler_params=params(16),
        cost_estimate=cost(0, 8 * video * width),
        name="split_heads",
    )(in_hbm(stale_cache))
    place = lax.optimization_barrier((place, *stale))[0]
    chains = [[ring_step((half, half))] for half in stale]

    block_heads = 2 if heads % 2 == 0 else 1
    columns = block_heads * TRIPLE
    blocks = heads // block_heads
    project_cost = cost(8 * rows * features * group_columns, 2 * features * group_columns)
    a_rows, message, text_message, stats, w_columns = pl.pallas_call(
        send_kernel,
        in_specs=[smem] + [hbm] * 5,
        out_specs=[vmem] * 5,
        out_shape=[
            jax.ShapeDtypeStruct((rows, features), BF16),
            jax.ShapeDtypeStruct((top, group_columns), BF16),
            jax.ShapeDtypeStruct((text, 2 * width), BF16),
            jax.ShapeDtypeStruct((rows, HEAD_DIM), F32),
            jax.ShapeDtypeStruct((blocks, features, columns), BF16),
        ],
        scratch_shapes=[
            pltpu.VMEM((video, features), BF16),
            pltpu.VMEM((text, features), BF16),
            pltpu.VMEM((features,), F32),
            pltpu.VMEM((features,), F32),
            pltpu.VMEM((blocks, features, columns), BF16),
            pltpu.SemaphoreType.DMA((4,)),
            pltpu.SemaphoreType.DMA((blocks,)),
            pltpu.SemaphoreType.DMA((blocks,)),
        ],
        compiler_params=params(28),
        cost_estimate=project_cost,
        name="project_send",
    )(
        place,
        *map(in_hbm, (hidden, text_hidden, norm_scale, norm_shift, qkv_weight)),
    )

    received = lax.ppermute(message, "head", swap_head)

    for chain in chains:
        chain.append(ring_step(lax.optimization_barrier((*chain[-1], message))[:2]))

    small = (query_gain, key_gain, text_mask, branch_gate, hidden)
    outs = pl.pallas_call(
        own_kernel,
        in_specs=[smem, vmem, vmem, hbm] + [hbm] * len(small),
        out_specs=[vmem] * (4 + len(small)),
        out_shape=[
            jax.ShapeDtypeStruct((top, group_columns), F32),
            jax.ShapeDtypeStruct((text, 2 * width), F32),
            jax.ShapeDtypeStruct((width, out_features), BF16),
            jax.ShapeDtypeStruct((width, out_features), BF16),
        ]
        + [jax.ShapeDtypeStruct(array.shape, array.dtype) for array in small],
        scratch_shapes=[pltpu.SemaphoreType.DMA((len(small) + 2,))],
        compiler_params=params(24),
        cost_estimate=project_cost,
        name="project_own",
    )(place, a_rows, w_columns, *map(in_hbm, (out_weight,) + small))
    own, own_text, w_own, w_other = outs[:4]
    query_gain, key_gain, text_mask, branch_gate, hidden = outs[4:]

    for step in range(half_way - 3):
        for chain in chains:
            last = chain[-1]
            if step == 0:
                last = lax.optimization_barrier((*last, own))[:2]
            chain.append(ring_step(last))

    received = lax.optimization_barrier((received, *chains[1][1]))[0]
    text_message = lax.optimization_barrier((text_message, received))[0]
    text_received = lax.ppermute(text_message, "head", swap_head)

    queries, new_cache, fresh = plain_call(
        functools.partial(norm_kernel, features * 2),
        [((video, width), BF16), ((2, video, width), BF16), ((2, video, width), BF16)],
        "norm_video",
        cost(20 * top * group_columns, 8 * top * group_columns),
        own, received, stats, query_gain, key_gain,
    )
    other_queries = lax.ppermute(queries, "section", swap_core)
    far = [
        lax.ppermute(lax.optimization_barrier((chain[-1][0], queries))[0], "section", ways[0])
        for chain in chains
    ]

    halves = [
        block
        for steps in zip(*chains)
        for way in range(2)
        for block in (steps[0][way], steps[1][way])
    ]
    context = (len(halves) // 2 + 1) * video
    num, den = plain_call(
        first_kernel,
        [((2 * video, width), F32), ((2 * video, HEAD_DIM), F32)],
        "attend_first",
        cost(8 * video * context * width, 4 * context * width, 2 * video * context * heads),
        queries, other_queries, fresh, *stale, *halves,
    )
    (text_kv,) = plain_call(
        functools.partial(text_kernel, features * 2),
        [((2, text, width), BF16)],
        "norm_text",
        cost(20 * text * group_columns, 8 * text * group_columns),
        own_text, text_received, stats, own, received, key_gain,
    )

    last_context = video + text
    attended, other_attended = [], []
    for index, block in enumerate(far):
        first = index * heads // 2
        num_own, den_own, num_message = pl.pallas_call(
            functools.partial(last_kernel, first),
            in_specs=[smem] + [vmem] * 7,
            out_specs=[vmem] * 3,
            out_shape=[
                jax.ShapeDtypeStruct((video, width // 2), F32),
                jax.ShapeDtypeStruct((video, HEAD_DIM), F32),
                jax.ShapeDtypeStruct((video, width // 2 + HEAD_DIM), F32),
            ],
            compiler_params=params(24),
            cost_estimate=cost(
                4 * video * last_context * width, 6 * video * width, video * last_context * heads
            ),
            name="attend_last",
        )(place, queries, other_queries, num, den, text_kv, text_mask, block)
        num_received = lax.ppermute(num_message, "section", swap_core)
        attended += plain_call(
            functools.partial(merge_kernel, first),
            [((video, width // 2), BF16)],
            "merge",
            cost(2 * video * width, 5 * video * width),
            num_own, den_own, num_received,
        )
        other_attended.append(lax.ppermute(attended[-1], "head", swap_head))

    out_cost = cost(2 * video * width * out_features, 2 * width * out_features)
    (part,) = plain_call(
        part_kernel, [((video, out_features), F32)], "part_out", out_cost, *attended, w_own
    )
    (mixed,) = plain_call(
        final_kernel, [((video, out_features), BF16)], "final_out", out_cost,
        part, *other_attended, w_other, hidden, branch_gate,
    )
    return (mixed, new_cache)


def solution(mesh):
    in_specs = (
        P("section", "head"),
        P(None, "head"),
        P(),
        P(None, "section", "head"),
        P("head", None),
        P(None, "head"),
        P(),
        P(),
        P("head"),
        P("head"),
        P("head"),
    )
    out_specs = (P("section", "head"), P(None, "section", "head"))
    return jax.shard_map(
        functools.partial(per_device, mesh.shape["section"]),
        mesh=mesh, in_specs=in_specs, out_specs=out_specs, check_vma=False,
    )
```

time: 64.2 us -> 58.8 us (0.916)
  starting transfers between devices: 11.9 us -> 22 us
  waiting for transfers between devices: 21 us -> 13.2 us
  local copies, waits for them, and re-layouts: 7.29 us -> 0 us
  other arithmetic: 0.93 us -> 0.07 us
  Pallas kernels: 21.8 us -> 22.6 us
    ppermute x8 -> x17, waiting for transfers between devices: 19.4 us -> 7.91 us  [the longest x2 4.02 us: per_device(): other_attended.append(lax.ppermute(attended[-1], 'head', swap_head))]
    ppermute x8 -> x17, starting transfers between devices: 9.38 us -> 19.4 us  [the longest x12 14 us: ring_step(): lax.ppermute(block, 'section', way)]
    unnamed x30 -> x0, local copies, waits for them, and re-layouts: 7.29 us -> none
    ppermute x1, waiting for transfers between devices: 0.14 us -> 4.82 us  [per_device(): received = lax.ppermute(message, 'head', swap_head)]
    pallas_call x6 -> x7, Pallas kernels: 5.7 us -> 7.55 us  [plain_call(): pl.pallas_call(kernel, in_specs=[pl.BlockSpec(memory_space=pltpu.VMEM)] *...]
    pallas_call x3 -> x5, Pallas kernels: 16.1 us -> 15 us  [the longest x1 8.5 us: per_device(): pl.pallas_call(send_kernel, in_specs=[smem] + [hbm] * 5, out_specs=[vmem]...]
    ppermute x1 -> x2, waiting for transfers between devices: 1.44 us -> 0.43 us  [per_device(): num_received = lax.ppermute(num_message, 'section', swap_core)]
    reshape x1 -> x0, other arithmetic: 0.85 us -> none  [per_device(): lax.dynamic_slice_in_dim(text_mask, core * text, text, 0).astype(F32)]
  transfers between devices with their start and end apart: 11 -> 21, of which waited for: 5 -> 7; matrix products, arithmetic and copies ran while one was open for 1% -> 0% of each run, Pallas kernels for 29% -> 34%
where the time goes in v5:
time: 58.8 us; the launch traced here: 58.6 us
  Pallas kernels  22.6 us (38%)
  starting transfers between devices  22 us (37%)
  waiting for transfers between devices  13.2 us (22%)
  between operations  0.75 us (1%)
    ppermute x12, starting transfers between devices, ring_step(): lax.ppermute(block, 'section', way)  14 us
    pallas_call x1, Pallas kernels, per_device(): pl.pallas_call(send_kernel, in_specs=[smem] + [hbm] * 5, out_specs=[vmem]...  8.5 us
    pallas_call x7, Pallas kernels, plain_call(): pl.pallas_call(kernel, in_specs=[pl.BlockSpec(memory_space=pltpu.VMEM)] *...  7.55 us
    ppermute x1, waiting for transfers between devices, per_device(): received = lax.ppermute(message, 'head', swap_head)  4.82 us
    ppermute x2, waiting for transfers between devices, per_device(): other_attended.append(lax.ppermute(attended[-1], 'head', swap_head))  4.02 us
    ppermute x12, waiting for transfers between devices, ring_step(): lax.ppermute(block, 'section', way)  3.88 us
    pallas_call x1, Pallas kernels, per_device(): pl.pallas_call(own_kernel, in_specs=[smem, vmem, vmem, hbm] + [hbm] * len...  3.18 us
    pallas_call x2, Pallas kernels, per_device(): pl.pallas_call(functools.partial(last_kernel, first), in_specs=[smem] + [...  2.31 us
  transfers between devices with their start and end apart: 21, of which 7 were waited for; matrix products, arithmetic and copies ran while one was open for 0% of the time, Pallas kernels for 34%

profile of v5, /device:TPU:0, one launch (start us, length us, event | category | flops | bytes accessed | tf_op | source)
XLA Modules:
  0.0 58.6 jit_solution(3606963031470165521)
XLA Ops:
  0.6 1.0 %split_heads.1 = (bf16[2,128,384]{2,1,0:T(8,128)(2,1)S(1)}, bf16[2,128,384]{2,1,0:T(8,128)(2,1)S(1)}) custom-call(bf16[2,128,768]{2,1,0:T(8,128)(2,1)} %block_ref.1), custom_call_target="tpu_custom_call" | custom-call | bytes 786432 | tf_op jit(solution)/shard_map/split_heads/pallas_call | solution.py:418
  1.7 3.1 %collective-permute-start.1 = (bf16[2,128,384]{2,1,0:T(8,128)(2,1)S(1)}, bf16[2,128,384]{2,1,0:T(8,128)(2,1)S(1)}, u32[]{:S(2)}, u32[]{:S(2)}) collective-permute-start(bf16[2,128,384]{2,1,0:T(8,128)(2,1)S(1)} %get-tuple-element.43.refs_1_), channel_id=1, source_target_pairs={{0,8},{2,6},{4,0},{6,14},{8,16},{10,2},{12,4},{14,22},{16,24},{18,... | collective-permute-start | bytes 589832 | tf_op jit(solution)/shard_map/ppermute | solution.py:412
  4.8 2.0 %collective-permute-start.6 = (bf16[2,128,384]{2,1,0:T(8,128)(2,1)S(1)}, bf16[2,128,384]{2,1,0:T(8,128)(2,1)S(1)}, u32[]{:S(2)}, u32[]{:S(2)}) collective-permute-start(bf16[2,128,384]{2,1,0:T(8,128)(2,1)S(1)} %get-tuple-element.42.refs_0_), channel_id=1, source_target_pairs={{0,8},{2,6},{4,0},{6,14},{8,16},{10,2},{12,4},{14,22},{16,24},{18,... | collective-permute-start | bytes 589832 | tf_op jit(solution)/shard_map/ppermute | solution.py:412
  6.9 8.5 %project_send.1 = (bf16[272,1536]{1,0:T(8,128)(2,1)S(1)}, bf16[144,2304]{1,0:T(8,128)(2,1)S(1)}, bf16[128,1536]{1,0:T(8,128)(2,1)S(1)}, f32[272,128]{1,0:T(8,128)S(1)}, bf16[3,1536,768]{2,1,0:T(8,128)(2,1)S(1)}) custom-call(s32[2]{0:T(128)S(1)} %pad_add_fusion.place_ref, bf16[128,1536]{1,0:T(8,128)(2,1)} %refs_4_.1, bf16[256,1536]{1,0:T(8,128)(2,1)} %t_ref.1, ...), custom_call_target="tpu_custom_call" | custom-call | flops 7700742144 | bytes 7077888 | tf_op jit(solution)/shard_map/project_send/pallas_call | solution.py:435
  15.4 2.0 %collective-permute-start = (bf16[144,2304]{1,0:T(8,128)(2,1)S(1)}, bf16[144,2304]{1,0:T(8,128)(2,1)S(1)}, u32[]{:S(2)}, u32[]{:S(2)}) collective-permute-start(bf16[144,2304]{1,0:T(8,128)(2,1)S(1)} %get-tuple-element.48), channel_id=1, source_target_pairs={{0,1},{1,0},{2,3},{3,2},{4,5},{5,4},{6,7},{7,6},{8,9},{9,8},{10,11... | collective-permute-start | bytes 1990664 | tf_op jit(solution)/shard_map/ppermute | solution.py:464
  17.4 1.6 %collective-permute-start.3 = (bf16[2,128,384]{2,1,0:T(8,128)(2,1)S(1)}, bf16[2,128,384]{2,1,0:T(8,128)(2,1)S(1)}, u32[]{:S(2)}, u32[]{:S(2)}) collective-permute-start(bf16[2,128,384]{2,1,0:T(8,128)(2,1)S(1)} %collective-permute-done.1.refs_3_), channel_id=1, source_target_pairs={{0,8},{2,6},{4,0},{6,14},{8,16},{10,2},{12,4},{14,22},{16,24},{18,... | collective-permute-start | bytes 589832 | tf_op jit(solution)/shard_map/ppermute | solution.py:412
  19.4 1.6 %collective-permute-start.8 = (bf16[2,128,384]{2,1,0:T(8,128)(2,1)S(1)}, bf16[2,128,384]{2,1,0:T(8,128)(2,1)S(1)}, u32[]{:S(2)}, u32[]{:S(2)}) collective-permute-start(bf16[2,128,384]{2,1,0:T(8,128)(2,1)S(1)} %collective-permute-done.6.refs_2_), channel_id=1, source_target_pairs={{0,8},{2,6},{4,0},{6,14},{8,16},{10,2},{12,4},{14,22},{16,24},{18,... | collective-permute-start | bytes 589832 | tf_op jit(solution)/shard_map/ppermute | solution.py:412
  21.4 3.2 %project_own.1 = (f32[144,2304]{1,0:T(8,128)S(1)}, f32[128,1536]{1,0:T(8,128)S(1)}, bf16[768,1536]{1,0:T(8,128)(2,1)S(1)}, bf16[768,1536]{1,0:T(8,128)(2,1)S(1)}...) custom-call(s32[2]{0:T(128)S(1)} %pad_add_fusion.place_ref, ...), custom_call_target="tpu_custom_call" | custom-call | flops 7700742144 | bytes 7077888 | tf_op jit(solution)/shard_map/project_own/pallas_call | solution.py:470
  25.2 1.3 %collective-permute-start.11 = (bf16[2,128,384]{2,1,0:T(8,128)(2,1)S(1)}, bf16[2,128,384]{2,1,0:T(8,128)(2,1)S(1)}, u32[]{:S(2)}, u32[]{:S(2)}) collective-permute-start(bf16[2,128,384]{2,1,0:T(8,128)(2,1)S(1)} %collective-permute-done.3.refs_7_), channel_id=1, source_target_pairs={{0,8},{2,6},{4,0},{6,14},{8,16},{10,2},{12,4},{14,22},{16,24},{18,... | collective-permute-start | bytes 589832 | tf_op jit(solution)/shard_map/ppermute | solution.py:412
  26.5 4.8 %collective-permute-done.msg_ref = bf16[144,2304]{1,0:T(8,128)(2,1)S(1)} collective-permute-done((bf16[144,2304]{1,0:T(8,128)(2,1)S(1)}, bf16[144,2304]{1,0:T(8,128)(2,1)S(1)}, u32[]{:S(2)}, u32[]{:S(2)}) %collective-permute-start) | collective-permute-done | bytes 663584 | tf_op jit(solution)/shard_map/ppermute | solution.py:464
  31.3 1.6 %collective-permute-start.14 = (bf16[128,1536]{1,0:T(8,128)(2,1)S(1)}, bf16[128,1536]{1,0:T(8,128)(2,1)S(1)}, u32[]{:S(2)}, u32[]{:S(2)}) collective-permute-start(bf16[128,1536]{1,0:T(8,128)(2,1)S(1)} %get-tuple-element.67), channel_id=1, source_target_pairs={{0,1},{1,0},{2,3},{3,2},{4,5},{5,4},{6,7},{7,6},{8,9},{9,8},{10,11... | collective-permute-start | bytes 1179656 | tf_op jit(solution)/shard_map/ppermute | solution.py:498
  32.9 1.6 %collective-permute-start.10 = (bf16[2,128,384]{2,1,0:T(8,128)(2,1)S(1)}, bf16[2,128,384]{2,1,0:T(8,128)(2,1)S(1)}, u32[]{:S(2)}, u32[]{:S(2)}) collective-permute-start(bf16[2,128,384]{2,1,0:T(8,128)(2,1)S(1)} %collective-permute-done.8.refs_6_), channel_id=1, source_target_pairs={{0,8},{2,6},{4,0},{6,14},{8,16},{10,2},{12,4},{14,22},{16,24},{18,... | collective-permute-start | bytes 589832 | tf_op jit(solution)/shard_map/ppermute | solution.py:412
  34.9 1.5 %collective-permute-start.12 = (bf16[2,128,384]{2,1,0:T(8,128)(2,1)S(1)}, bf16[2,128,384]{2,1,0:T(8,128)(2,1)S(1)}, u32[]{:S(2)}, u32[]{:S(2)}) collective-permute-start(bf16[2,128,384]{2,1,0:T(8,128)(2,1)S(1)} %collective-permute-done.9.refs_8_), channel_id=1, source_target_pairs={{0,4},{2,10},{4,12},{6,2},{8,0},{10,18},{12,20},{14,6},{16,8},{18,... | collective-permute-start | bytes 589832 | tf_op jit(solution)/shard_map/ppermute | solution.py:412
  36.5 1.5 %norm_video.1 = (bf16[128,768]{1,0:T(8,128)(2,1)S(1)}, bf16[2,128,768]{2,1,0:T(8,128)(2,1)}, bf16[2,128,768]{2,1,0:T(8,128)(2,1)S(1)}) custom-call(f32[144,2304]{1,0:T(8,128)S(1)} %get-tuple-element.47.own_ref.top_ref, bf16[144,2304]{1,0:T(8,128)(2,1)S(1)} %collective-permute-done.msg_ref, f32[272,128]{1,0:T(8,128)S(1)} %get-tuple-element.52.stat_ref, ...), custom_call_target="tpu_custom_call" | custom-call | flops 6635520 | bytes 2654208 | tf_op jit(solution)/shard_map/norm_video/pallas_call | solution.py:367
  38.0 2.6 %collective-permute-done.10.refs_10_ = bf16[2,128,384]{2,1,0:T(8,128)(2,1)S(1)} collective-permute-done((bf16[2,128,384]{2,1,0:T(8,128)(2,1)S(1)}, bf16[2,128,384]{2,1,0:T(8,128)(2,1)S(1)}, u32[]{:S(2)}, u32[]{:S(2)}) %collective-permute-start.10) | collective-permute-done | bytes 196640 | tf_op jit(solution)/shard_map/ppermute | solution.py:412
  41.1 1.6 %collective-permute-start.15 = (bf16[2,128,384]{2,1,0:T(8,128)(2,1)S(1)}, bf16[2,128,384]{2,1,0:T(8,128)(2,1)S(1)}, u32[]{:S(2)}, u32[]{:S(2)}) collective-permute-start(bf16[2,128,384]{2,1,0:T(8,128)(2,1)S(1)} %collective-permute-done.10.refs_10_), channel_id=1, source_target_pairs={{0,8},{2,6},{4,0},{6,14},{8,16},{10,2},{12,4},{14,22},{16,24},{18,... | collective-permute-start | bytes 589832 | tf_op jit(solution)/shard_map/ppermute | solution.py:509
  42.7 0.7 %collective-permute-done.12.refs_12_ = bf16[2,128,384]{2,1,0:T(8,128)(2,1)S(1)} collective-permute-done((bf16[2,128,384]{2,1,0:T(8,128)(2,1)S(1)}, bf16[2,128,384]{2,1,0:T(8,128)(2,1)S(1)}, u32[]{:S(2)}, u32[]{:S(2)}) %collective-permute-start.12) | collective-permute-done | bytes 196640 | tf_op jit(solution)/shard_map/ppermute | solution.py:412
  43.4 3.3 %attend_first.1 = (f32[256,768]{1,0:T(8,128)S(1)}, f32[256,128]{1,0:T(8,128)S(1)}) custom-call(bf16[128,768]{1,0:T(8,128)(2,1)S(1)} %get-tuple-element.55.qo_ref, bf16[128,768]{1,0:T(8,128)(2,1)S(1)} %collective-permute-done.5.qp_ref, bf16[2,128,768]{2,1,0:T(8,128)(2,1)S(1)} %get-tuple-element.56.fresh_ref, ...), custom_call_target="tpu_custom_call" | custom-call | flops 704643072 | bytes 2752512 | tf_op jit(solution)/shard_map/attend_first/pallas_call | solution.py:367
  47.2 1.2 %attend_last.3 = (f32[128,384]{1,0:T(8,128)S(1)}, f32[128,128]{1,0:T(8,128)S(1)}, f32[128,512]{1,0:T(8,128)S(1)}) custom-call(s32[2]{0:T(128)S(1)} %pad_add_fusion.place_ref, bf16[128,768]{1,0:T(8,128)(2,1)S(1)} %get-tuple-element.55.qo_ref, bf16[128,768]{1,0:T(8,128)(2,1)S(1)} %collective-permute-done.5.qp_ref, f32[256,768]{1,0:T(8,128)S(1)} %get-tuple-element.63.num_ref, ...), custom_call_target="tpu_custom_call" | custom-call | flops 100663296 | bytes 589824 | tf_op jit(solution)/shard_map/attend_last/pallas_call | solution.py:539
  48.5 1.2 %attend_last.2 = (f32[128,384]{1,0:T(8,128)S(1)}, f32[128,128]{1,0:T(8,128)S(1)}, f32[128,512]{1,0:T(8,128)S(1)}) custom-call(s32[2]{0:T(128)S(1)} %pad_add_fusion.place_ref, bf16[128,768]{1,0:T(8,128)(2,1)S(1)} %get-tuple-element.55.qo_ref, bf16[128,768]{1,0:T(8,128)(2,1)S(1)} %collective-permute-done.5.qp_ref, f32[256,768]{1,0:T(8,128)S(1)} %get-tuple-element.63.num_ref, ...), custom_call_target="tpu_custom_call" | custom-call | flops 100663296 | bytes 589824 | tf_op jit(solution)/shard_map/attend_last/pallas_call | solution.py:539
  51.5 1.1 %collective-permute-start.19 = (bf16[128,384]{1,0:T(8,128)(2,1)S(1)}, bf16[128,384]{1,0:T(8,128)(2,1)S(1)}, u32[]{:S(2)}, u32[]{:S(2)}) collective-permute-start(bf16[128,384]{1,0:T(8,128)(2,1)S(1)} %merge.2.first_ref), channel_id=1, source_target_pairs={{0,1},{1,0},{2,3},{3,2},{4,5},{5,4},{6,7},{7,6},{8,9},{9,8},{10,11... | collective-permute-start | bytes 294920 | tf_op jit(solution)/shard_map/ppermute | solution.py:562
  53.2 2.6 %collective-permute-done.20.second_ref = bf16[128,384]{1,0:T(8,128)(2,1)S(1)} collective-permute-done((bf16[128,384]{1,0:T(8,128)(2,1)S(1)}, bf16[128,384]{1,0:T(8,128)(2,1)S(1)}, u32[]{:S(2)}, u32[]{:S(2)}) %collective-permute-start.20) | collective-permute-done | bytes 98336 | tf_op jit(solution)/shard_map/ppermute | solution.py:562
  55.8 1.5 %collective-permute-done.19.first_ref = bf16[128,384]{1,0:T(8,128)(2,1)S(1)} collective-permute-done((bf16[128,384]{1,0:T(8,128)(2,1)S(1)}, bf16[128,384]{1,0:T(8,128)(2,1)S(1)}, u32[]{:S(2)}, u32[]{:S(2)}) %collective-permute-start.19) | collective-permute-done | bytes 98336 | tf_op jit(solution)/shard_map/ppermute | solution.py:562
  57.2 1.4 %final_out.1 = bf16[128,1536]{1,0:T(8,128)(2,1)} custom-call(f32[128,1536]{1,0:T(8,128)S(1)} %part_out.1.part_ref, bf16[128,384]{1,0:T(8,128)(2,1)S(1)} %collective-permute-done.19.first_ref, bf16[128,384]{1,0:T(8,128)(2,1)S(1)} %collective-permute-done.20.second_ref, bf16[768,1536]{1,0:T(8,128)(2,1)S(1)} %get-tuple-element.78.w_ref, ...), custom_call_target="tpu_custom_call" | custom-call | flops 301989888 | bytes 2359296 | tf_op jit(solution)/shard_map/final_out/pallas_call | solution.py:367
  (31 shorter events, 5.6 us)
Async XLA Ops:
  1.7 15.7 %collective-permute-start.1 = (bf16[2,128,384]{2,1,0:T(8,128)(2,1)S(1)}, bf16[2,128,384]{2,1,0:T(8,128)(2,1)S(1)}, u32[]{:S(2)}, u32[]{:S(2)}) collective-permute-start(bf16[2,128,384]{2,1,0:T(8,128)(2,1)S(1)} %get-tuple-element.43.refs_1_), channel_id=1, source_target_pairs={{0,8},{2,6},{4,0},{6,14},{8,16},{10,2},{12,4},{14,22},{16,24},{18,... | collective-permute-start | bytes 589832 | tf_op jit(solution)/shard_map/ppermute | solution.py:412
  4.8 12.6 %collective-permute-start.2 = (bf16[2,128,384]{2,1,0:T(8,128)(2,1)S(1)}, bf16[2,128,384]{2,1,0:T(8,128)(2,1)S(1)}, u32[]{:S(2)}, u32[]{:S(2)}) collective-permute-start(bf16[2,128,384]{2,1,0:T(8,128)(2,1)S(1)} %get-tuple-element.43.refs_1_), channel_id=1, source_target_pairs={{0,4},{2,10},{4,12},{6,2},{8,0},{10,18},{12,20},{14,6},{16,8},{18,... | collective-permute-start | bytes 589832 | tf_op jit(solution)/shard_map/ppermute | solution.py:412
  4.8 14.6 %collective-permute-start.6 = (bf16[2,128,384]{2,1,0:T(8,128)(2,1)S(1)}, bf16[2,128,384]{2,1,0:T(8,128)(2,1)S(1)}, u32[]{:S(2)}, u32[]{:S(2)}) collective-permute-start(bf16[2,128,384]{2,1,0:T(8,128)(2,1)S(1)} %get-tuple-element.42.refs_0_), channel_id=1, source_target_pairs={{0,8},{2,6},{4,0},{6,14},{8,16},{10,2},{12,4},{14,22},{16,24},{18,... | collective-permute-start | bytes 589832 | tf_op jit(solution)/shard_map/ppermute | solution.py:412
  6.8 12.6 %collective-permute-start.7 = (bf16[2,128,384]{2,1,0:T(8,128)(2,1)S(1)}, bf16[2,128,384]{2,1,0:T(8,128)(2,1)S(1)}, u32[]{:S(2)}, u32[]{:S(2)}) collective-permute-start(bf16[2,128,384]{2,1,0:T(8,128)(2,1)S(1)} %get-tuple-element.42.refs_0_), channel_id=1, source_target_pairs={{0,4},{2,10},{4,12},{6,2},{8,0},{10,18},{12,20},{14,6},{16,8},{18,... | collective-permute-start | bytes 589832 | tf_op jit(solution)/shard_map/ppermute | solution.py:412
  15.4 15.9 %collective-permute-start = (bf16[144,2304]{1,0:T(8,128)(2,1)S(1)}, bf16[144,2304]{1,0:T(8,128)(2,1)S(1)}, u32[]{:S(2)}, u32[]{:S(2)}) collective-permute-start(bf16[144,2304]{1,0:T(8,128)(2,1)S(1)} %get-tuple-element.48), channel_id=1, source_target_pairs={{0,1},{1,0},{2,3},{3,2},{4,5},{5,4},{6,7},{7,6},{8,9},{9,8},{10,11... | collective-permute-start | bytes 1990664 | tf_op jit(solution)/shard_map/ppermute | solution.py:464
  17.4 7.8 %collective-permute-start.3 = (bf16[2,128,384]{2,1,0:T(8,128)(2,1)S(1)}, bf16[2,128,384]{2,1,0:T(8,128)(2,1)S(1)}, u32[]{:S(2)}, u32[]{:S(2)}) collective-permute-start(bf16[2,128,384]{2,1,0:T(8,128)(2,1)S(1)} %collective-permute-done.1.refs_3_), channel_id=1, source_target_pairs={{0,8},{2,6},{4,0},{6,14},{8,16},{10,2},{12,4},{14,22},{16,24},{18,... | collective-permute-start | bytes 589832 | tf_op jit(solution)/shard_map/ppermute | solution.py:412
  19.0 6.2 %collective-permute-start.4 = (bf16[2,128,384]{2,1,0:T(8,128)(2,1)S(1)}, bf16[2,128,384]{2,1,0:T(8,128)(2,1)S(1)}, u32[]{:S(2)}, u32[]{:S(2)}) collective-permute-start(bf16[2,128,384]{2,1,0:T(8,128)(2,1)S(1)} %collective-permute-done.2.refs_5_), channel_id=1, source_target_pairs={{0,4},{2,10},{4,12},{6,2},{8,0},{10,18},{12,20},{14,6},{16,8},{18,... | collective-permute-start | bytes 589832 | tf_op jit(solution)/shard_map/ppermute | solution.py:412
  19.4 13.5 %collective-permute-start.8 = (bf16[2,128,384]{2,1,0:T(8,128)(2,1)S(1)}, bf16[2,128,384]{2,1,0:T(8,128)(2,1)S(1)}, u32[]{:S(2)}, u32[]{:S(2)}) collective-permute-start(bf16[2,128,384]{2,1,0:T(8,128)(2,1)S(1)} %collective-permute-done.6.refs_2_), channel_id=1, source_target_pairs={{0,8},{2,6},{4,0},{6,14},{8,16},{10,2},{12,4},{14,22},{16,24},{18,... | collective-permute-start | bytes 589832 | tf_op jit(solution)/shard_map/ppermute | solution.py:412
  21.0 11.9 %collective-permute-start.9 = (bf16[2,128,384]{2,1,0:T(8,128)(2,1)S(1)}, bf16[2,128,384]{2,1,0:T(8,128)(2,1)S(1)}, u32[]{:S(2)}, u32[]{:S(2)}) collective-permute-start(bf16[2,128,384]{2,1,0:T(8,128)(2,1)S(1)} %collective-permute-done.7.refs_4_), channel_id=1, source_target_pairs={{0,4},{2,10},{4,12},{6,2},{8,0},{10,18},{12,20},{14,6},{16,8},{18,... | collective-permute-start | bytes 589832 | tf_op jit(solution)/shard_map/ppermute | solution.py:412
  25.2 12.8 %collective-permute-start.11 = (bf16[2,128,384]{2,1,0:T(8,128)(2,1)S(1)}, bf16[2,128,384]{2,1,0:T(8,128)(2,1)S(1)}, u32[]{:S(2)}, u32[]{:S(2)}) collective-permute-start(bf16[2,128,384]{2,1,0:T(8,128)(2,1)S(1)} %collective-permute-done.3.refs_7_), channel_id=1, source_target_pairs={{0,8},{2,6},{4,0},{6,14},{8,16},{10,2},{12,4},{14,22},{16,24},{18,... | collective-permute-start | bytes 589832 | tf_op jit(solution)/shard_map/ppermute | solution.py:412
  31.3 15.3 %collective-permute-start.14 = (bf16[128,1536]{1,0:T(8,128)(2,1)S(1)}, bf16[128,1536]{1,0:T(8,128)(2,1)S(1)}, u32[]{:S(2)}, u32[]{:S(2)}) collective-permute-start(bf16[128,1536]{1,0:T(8,128)(2,1)S(1)} %get-tuple-element.67), channel_id=1, source_target_pairs={{0,1},{1,0},{2,3},{3,2},{4,5},{5,4},{6,7},{7,6},{8,9},{9,8},{10,11... | collective-permute-start | bytes 1179656 | tf_op jit(solution)/shard_map/ppermute | solution.py:498
  32.9 7.7 %collective-permute-start.10 = (bf16[2,128,384]{2,1,0:T(8,128)(2,1)S(1)}, bf16[2,128,384]{2,1,0:T(8,128)(2,1)S(1)}, u32[]{:S(2)}, u32[]{:S(2)}) collective-permute-start(bf16[2,128,384]{2,1,0:T(8,128)(2,1)S(1)} %collective-permute-done.8.refs_6_), channel_id=1, source_target_pairs={{0,8},{2,6},{4,0},{6,14},{8,16},{10,2},{12,4},{14,22},{16,24},{18,... | collective-permute-start | bytes 589832 | tf_op jit(solution)/shard_map/ppermute | solution.py:412
  34.5 6.6 %collective-permute-start.13 = (bf16[2,128,384]{2,1,0:T(8,128)(2,1)S(1)}, bf16[2,128,384]{2,1,0:T(8,128)(2,1)S(1)}, u32[]{:S(2)}, u32[]{:S(2)}) collective-permute-start(bf16[2,128,384]{2,1,0:T(8,128)(2,1)S(1)} %collective-permute-done.4.refs_9_), channel_id=1, source_target_pairs={{0,4},{2,10},{4,12},{6,2},{8,0},{10,18},{12,20},{14,6},{16,8},{18,... | collective-permute-start | bytes 589832 | tf_op jit(solution)/shard_map/ppermute | solution.py:412
  34.9 8.4 %collective-permute-start.12 = (bf16[2,128,384]{2,1,0:T(8,128)(2,1)S(1)}, bf16[2,128,384]{2,1,0:T(8,128)(2,1)S(1)}, u32[]{:S(2)}, u32[]{:S(2)}) collective-permute-start(bf16[2,128,384]{2,1,0:T(8,128)(2,1)S(1)} %collective-permute-done.9.refs_8_), channel_id=1, source_target_pairs={{0,4},{2,10},{4,12},{6,2},{8,0},{10,18},{12,20},{14,6},{16,8},{18,... | collective-permute-start | bytes 589832 | tf_op jit(solution)/shard_map/ppermute | solution.py:412
  38.0 5.4 %collective-permute-start.5 = (bf16[128,768]{1,0:T(8,128)(2,1)S(1)}, bf16[128,768]{1,0:T(8,128)(2,1)S(1)}, u32[]{:S(2)}, u32[]{:S(2)}) collective-permute-start(bf16[128,768]{1,0:T(8,128)(2,1)S(1)} %get-tuple-element.55.qo_ref), channel_id=1, source_target_pairs={{0,2},{2,0},{4,6},{6,4},{8,10},{10,8},{12,14},{14,12},{16,18},{18,... | collective-permute-start | bytes 589832 | tf_op jit(solution)/shard_map/ppermute | solution.py:507
  40.6 6.7 %collective-permute-start.17 = (bf16[2,128,384]{2,1,0:T(8,128)(2,1)S(1)}, bf16[2,128,384]{2,1,0:T(8,128)(2,1)S(1)}, u32[]{:S(2)}, u32[]{:S(2)}) collective-permute-start(bf16[2,128,384]{2,1,0:T(8,128)(2,1)S(1)} %collective-permute-done.11.refs_11_), channel_id=1, source_target_pairs={{0,8},{2,6},{4,0},{6,14},{8,16},{10,2},{12,4},{14,22},{16,24},{18,... | collective-permute-start | bytes 589832 | tf_op jit(solution)/shard_map/ppermute | solution.py:509
  41.1 7.4 %collective-permute-start.15 = (bf16[2,128,384]{2,1,0:T(8,128)(2,1)S(1)}, bf16[2,128,384]{2,1,0:T(8,128)(2,1)S(1)}, u32[]{:S(2)}, u32[]{:S(2)}) collective-permute-start(bf16[2,128,384]{2,1,0:T(8,128)(2,1)S(1)} %collective-permute-done.10.refs_10_), channel_id=1, source_target_pairs={{0,8},{2,6},{4,0},{6,14},{8,16},{10,2},{12,4},{14,22},{16,24},{18,... | collective-permute-start | bytes 589832 | tf_op jit(solution)/shard_map/ppermute | solution.py:509
  48.4 1.8 %collective-permute-start.18 = (f32[128,512]{1,0:T(8,128)S(1)}, f32[128,512]{1,0:T(8,128)S(1)}, u32[]{:S(2)}, u32[]{:S(2)}) collective-permute-start(f32[128,512]{1,0:T(8,128)S(1)} %get-tuple-element.76), channel_id=1, source_target_pairs={{0,2},{2,0},{4,6},{6,4},{8,10},{10,8},{12,14},{14,12},{16,18},{18,... | collective-permute-start | bytes 786440 | tf_op jit(solution)/shard_map/ppermute | solution.py:554
  49.6 1.7 %collective-permute-start.16 = (f32[128,512]{1,0:T(8,128)S(1)}, f32[128,512]{1,0:T(8,128)S(1)}, u32[]{:S(2)}, u32[]{:S(2)}) collective-permute-start(f32[128,512]{1,0:T(8,128)S(1)} %get-tuple-element.72), channel_id=1, source_target_pairs={{0,2},{2,0},{4,6},{6,4},{8,10},{10,8},{12,14},{14,12},{16,18},{18,... | collective-permute-start | bytes 786440 | tf_op jit(solution)/shard_map/ppermute | solution.py:554
  50.3 5.4 %collective-permute-start.20 = (bf16[128,384]{1,0:T(8,128)(2,1)S(1)}, bf16[128,384]{1,0:T(8,128)(2,1)S(1)}, u32[]{:S(2)}, u32[]{:S(2)}) collective-permute-start(bf16[128,384]{1,0:T(8,128)(2,1)S(1)} %merge.3.second_ref), channel_id=1, source_target_pairs={{0,1},{1,0},{2,3},{3,2},{4,5},{5,4},{6,7},{7,6},{8,9},{9,8},{10,11... | collective-permute-start | bytes 294920 | tf_op jit(solution)/shard_map/ppermute | solution.py:562
  51.5 5.7 %collective-permute-start.19 = (bf16[128,384]{1,0:T(8,128)(2,1)S(1)}, bf16[128,384]{1,0:T(8,128)(2,1)S(1)}, u32[]{:S(2)}, u32[]{:S(2)}) collective-permute-start(bf16[128,384]{1,0:T(8,128)(2,1)S(1)} %merge.2.first_ref), channel_id=1, source_target_pairs={{0,1},{1,0},{2,3},{3,2},{4,5},{5,4},{6,7},{7,6},{8,9},{9,8},{10,11... | collective-permute-start | bytes 294920 | tf_op jit(solution)/shard_map/ppermute | solution.py:562

commit v6 on v5

--- a/solution.py
+++ b/solution.py
@@ -12,6 +12,8 @@
 TRIPLE = 3 * HEAD_DIM
 EXTRA = 16
 STAT_ROW = 8
+PIECE = 2 * HEAD_DIM
+IN_FLIGHT = 6
 EPS = 1e-06
 F32 = jnp.float32
 BF16 = jnp.bfloat16
@@ -27,29 +29,26 @@
     return pieces
 
 
-def start_weights(w_ref, buffer_ref, sems, first):
-    count, _, columns = buffer_ref.shape
+def chunk_copies(w_ref, first, targets, sems, base):
     copies = []
-    for index in range(count):
-        start = pl.multiple_of(first + index * columns, HEAD_DIM)
-        copy = pltpu.make_async_copy(
-            w_ref.at[:, pl.ds(start, columns)], buffer_ref.at[index], sems.at[index]
+    for index, target in enumerate(targets):
+        start = pl.multiple_of(first + index * PIECE, HEAD_DIM)
+        copies.append(
+            pltpu.make_async_copy(w_ref.at[:, pl.ds(start, PIECE)], target, sems.at[base + index])
         )
-        copy.start()
-        copies.append(copy)
     return copies
 
 
 def send_kernel(
     place_ref, x_ref, t_ref, scale_ref, shift_ref, w_ref,
-    a_ref, msg_ref, tmsg_ref, stat_ref, w_own_ref,
-    x_buffer, t_buffer, scale_buffer, shift_buffer, w_buffer, in_sems, w_sems, own_sems,
+    a_ref, msg_ref, stat_ref, ahead_ref,
+    x_buffer, t_buffer, scale_buffer, shift_buffer, w_buffer, in_sems, w_sems,
 ):
     video, features = x_buffer.shape
     text = t_buffer.shape[0]
     top = video + EXTRA
-    blocks, _, columns = w_buffer.shape
-    width = blocks * columns
+    chunks = w_buffer.shape[0]
+    width = chunks * PIECE
     copies = [
         pltpu.make_async_copy(scale_ref, scale_buffer, in_sems.at[0]),
         pltpu.make_async_copy(shift_ref, shift_buffer, in_sems.at[1]),
@@ -58,10 +57,14 @@
             t_ref.at[pl.ds(pl.multiple_of(place_ref[1] * text, text), text)], t_buffer, in_sems.at[3]
         ),
     ]
-    for copy in copies:
+    w_copies = chunk_copies(
+        w_ref, (1 - place_ref[0]) * width, [w_buffer.at[i] for i in range(chunks)], w_sems, 0
+    ) + chunk_copies(
+        w_ref, place_ref[0] * width, [ahead_ref.at[i] for i in range(ahead_ref.shape[0])],
+        w_sems, chunks,
+    )
+    for copy in copies + w_copies[:IN_FLIGHT]:
         copy.start()
-    w_copies = start_weights(w_ref, w_buffer, w_sems, (1 - place_ref[0]) * width)
-    own_copies = start_weights(w_ref, w_own_ref, own_sems, place_ref[0] * width)
 
     copies[0].wait()
     copies[1].wait()
@@ -95,79 +98,75 @@
     text_stats = prepare(t_buffer, top)
     stat_ref[video:top, :] = jnp.zeros((EXTRA, HEAD_DIM), F32)
 
-    def write(start, product):
-        cells = slice(start, start + product.shape[1])
-        msg_ref[:, cells] = product[:top].astype(BF16)
-        if start == 0:
+    for index, copy in enumerate(w_copies):
+        copy.wait()
+        if index + IN_FLIGHT < len(w_copies):
+            w_copies[index + IN_FLIGHT].start()
+        if index >= chunks:
+            continue
+        start = index * PIECE
+        product = jnp.dot(a_ref[...], w_buffer[index], preferred_element_type=F32)
+        msg_ref[:top, start : start + PIECE] = product[:top].astype(BF16)
+        if index == 0:
             stats = jnp.concatenate([video_stats, text_stats], axis=1)
-            msg_ref[video:, : video + text] = (product[video:top] + stats).astype(BF16)
-        for source, target in text_columns(start, product.shape[1]):
-            tmsg_ref[:, target] = product[top:, source].astype(BF16)
-
-    for block in range(blocks):
-        w_copies[block].wait()
-        multiply(a_ref, w_buffer.at[block], block * columns, write)
-    for copy in own_copies:
-        copy.wait()
-
-
-PIECE = 2 * HEAD_DIM
-
-
-def multiply(a_ref, w_ref, first, write):
-    for start in range(0, w_ref.shape[1], PIECE):
-        piece = jnp.dot(
-            a_ref[...], w_ref[:, start : start + PIECE], preferred_element_type=F32
-        )
-        write(first + start, piece)
-
-
-def text_columns(first, count):
-    for start in range(0, count, HEAD_DIM):
+            msg_ref[video:top, : video + text] = (product[video:top] + stats).astype(BF16)
+        for source, target in text_columns(start):
+            part = product[top:, source].astype(BF16)
+            for quarter in range(4):
+                rows, cells = text_slot(text, width, target, quarter)
+                msg_ref[top + rows.start : top + rows.stop, cells] = part[
+                    quarter * text // 4 : (quarter + 1) * text // 4
+                ]
+
+
+def text_slot(text, width, column, quarter):
+    slots = width // PIECE
+    band, slot = divmod(column // PIECE * 4 + quarter, slots)
+    depth = text // 4
+    start = slot * PIECE + column % PIECE
+    return slice(band * depth, (band + 1) * depth), slice(start, start + HEAD_DIM)
+
+
+def text_columns(first):
+    for start in range(0, PIECE, HEAD_DIM):
         head, kind = divmod((first + start) // HEAD_DIM, 3)
         if kind:
-            target = (2 * head + kind - 1) * HEAD_DIM
-            yield slice(start, start + HEAD_DIM), slice(target, target + HEAD_DIM)
-
-
-def own_kernel(place_ref, a_ref, w_ref, out_weight_ref, *refs):
-    small = (len(refs) - 5) // 2
+            yield slice(start, start + HEAD_DIM), (2 * head + kind - 1) * HEAD_DIM
+
+
+def own_kernel(place_ref, a_ref, ahead_ref, w_ref, out_weight_ref, *refs):
+    small = (len(refs) - 7) // 2
     out_ref, text_ref, w_own_ref, w_other_ref = refs[small : small + 4]
-    sems = refs[-1]
+    w_buffer, w_sems, sems = refs[-3:]
     top = out_ref.shape[0]
     depth = w_own_ref.shape[0]
     group = place_ref[0]
-    pairs = list(zip(refs[:small], refs[small + 4 : -1]))
+    ahead, later = ahead_ref.shape[0], w_buffer.shape[0]
+    w_copies = chunk_copies(
+        w_ref, (group * (ahead + later) + ahead) * PIECE, [w_buffer.at[i] for i in range(later)],
+        w_sems, 0,
+    )
+    pairs = list(zip(refs[:small], refs[small + 4 : -3]))
     for half, target in ((group, w_own_ref), (1 - group, w_other_ref)):
         rows = pl.ds(pl.multiple_of(half * depth, depth), depth)
         pairs.append((out_weight_ref.at[rows], target))
-    copies = []
-    for index, (source, target) in enumerate(pairs):
-        copies.append(pltpu.make_async_copy(source, target, sems.at[index]))
-        copies[-1].start()
-
-    def write(start, product):
-        out_ref[:, start : start + product.shape[1]] = product[:top]
-        for source, target in text_columns(start, product.shape[1]):
-            text_ref[:, target] = product[top:, source]
-
-    blocks, _, columns = w_ref.shape
-    for block in range(blocks):
-        multiply(a_ref, w_ref.at[block], block * columns, write)
-    for copy in copies:
-        copy.wait()
-
-
-def split_kernel(block_ref, first_ref, second_ref, sems):
-    width = first_ref.shape[2]
     copies = [
-        pltpu.make_async_copy(
-            block_ref.at[:, :, pl.ds(index * width, width)], target, sems.at[index]
-        )
-        for index, target in enumerate((first_ref, second_ref))
+        pltpu.make_async_copy(source, target, sems.at[index])
+        for index, (source, target) in enumerate(pairs)
     ]
-    for copy in copies:
+    for copy in w_copies + copies:
         copy.start()
+
+    for index in range(ahead + later):
+        if index < ahead:
+            columns = ahead_ref[index]
+        else:
+            w_copies[index - ahead].wait()
+            columns = w_buffer[index - ahead]
+        product = jnp.dot(a_ref[...], columns, preferred_element_type=F32)
+        out_ref[:, index * PIECE : (index + 1) * PIECE] = product[:top]
+        for source, target in text_columns(index * PIECE):
+            text_ref[:, target : target + HEAD_DIM] = product[top:, source]
     for copy in copies:
         copy.wait()
 
@@ -220,10 +219,10 @@
         kv_ref[1, :, columns] = values
 
 
-def text_kernel(total_features, own_ref, tmsg_ref, stat_ref, top_ref, msg_ref, kg_ref, kv_ref):
+def text_kernel(total_features, own_ref, msg_ref, stat_ref, top_ref, kg_ref, kv_ref):
     text = kv_ref.shape[1]
     heads = kv_ref.shape[2] // HEAD_DIM
-    top = top_ref.shape[0]
+    top, width = top_ref.shape
     video = top - EXTRA
     key_gain = kg_ref[...].reshape(1, HEAD_DIM)
     gap, inverse = row_stats(
@@ -231,10 +230,15 @@
     )
     for head in range(heads):
         part = slice(head * TRIPLE + HEAD_DIM, (head + 1) * TRIPLE)
-        pair = slice(head * 2 * HEAD_DIM, (head + 1) * 2 * HEAD_DIM)
+        pair = slice(head * PIECE, (head + 1) * PIECE)
         columns = slice(head * HEAD_DIM, (head + 1) * HEAD_DIM)
         scale, shift = column_terms(top_ref[video:, part], msg_ref[video:top, part])
-        total = own_ref[:, pair] + tmsg_ref[:, pair].astype(F32)
+        other = []
+        for quarter in range(4):
+            rows, cells = text_slot(text, width, head * PIECE, quarter)
+            cells = slice(cells.start, cells.start + PIECE)
+            other.append(msg_ref[top + rows.start : top + rows.stop, cells])
+        total = own_ref[:, pair] + jnp.concatenate(other, axis=0).astype(F32)
         total = (total + gap * scale) * inverse + shift
         kv_ref[0, :, columns] = head_norm(total[:, :HEAD_DIM], key_gain).astype(BF16)
         kv_ref[1, :, columns] = total[:, HEAD_DIM:].astype(BF16)
@@ -270,50 +274,44 @@
     return num, den
 
 
-def first_kernel(qo_ref, qp_ref, fresh_ref, *refs):
+def first_kernel(place_ref, qo_ref, qp_ref, fresh_ref, stale_ref, text_ref, mask_ref, *refs):
     num_ref, den_ref = refs[-2:]
-    stales, halves = refs[:2], refs[2:-2]
     video, width = qo_ref.shape
+    text = text_ref.shape[1]
     lane = lax.broadcasted_iota(jnp.int32, (2 * video, HEAD_DIM), 1)
+    mask = mask_ref[...].reshape(1, 2 * text).astype(F32)
+    mask = jnp.where(place_ref[1] == 0, mask[:, :text], mask[:, text:])
     packed = jnp.zeros((2 * video, HEAD_DIM), F32)
     for head in range(width // HEAD_DIM):
         columns = slice(head * HEAD_DIM, (head + 1) * HEAD_DIM)
-        second, start = divmod(head * HEAD_DIM, width // 2)
-        cells = slice(start, start + HEAD_DIM)
         own, other = qo_ref[:, columns], qp_ref[:, columns]
         queries = jnp.concatenate([own, other], axis=0)
         fresh = weigh(own, fresh_ref[0, :, columns])
-        stale_ref = stales[second]
-        stale = weigh(other, stale_ref[0, :, cells])
+        stale = weigh(other, stale_ref[0, :, columns])
         num = jnp.concatenate(
-            [times(fresh, fresh_ref[1, :, columns]), times(stale, stale_ref[1, :, cells])], axis=0
+            [times(fresh, fresh_ref[1, :, columns]), times(stale, stale_ref[1, :, columns])], axis=0
         )
         den = jnp.concatenate([fresh, stale], axis=0)
-        num, den = absorb(queries, [(ref, cells) for ref in halves[second::2]], num, den)
+        weights = weigh(queries, text_ref[0, :, columns]) * mask
+        num = num + times(weights, text_ref[1, :, columns])
+        den = den + lanes(weights)
+        num, den = absorb(queries, [(ref, columns) for ref in refs[:-2]], num, den)
         num_ref[:, columns] = num
         packed = jnp.where(lane == head, jnp.sum(den, axis=1, keepdims=True), packed)
     den_ref[...] = packed
 
 
-def last_kernel(
-    first, place_ref, qo_ref, qp_ref, num_ref, den_ref, text_ref, mask_ref, far_ref,
-    own_ref, own_den_ref, msg_ref,
-):
+def last_kernel(first, qo_ref, qp_ref, num_ref, den_ref, far_ref, own_ref, own_den_ref, msg_ref):
     video = qo_ref.shape[0]
-    text, width = text_ref.shape[1], far_ref.shape[2]
+    width = own_ref.shape[1]
     lane = lax.broadcasted_iota(jnp.int32, (2 * video, HEAD_DIM), 1)
-    mask = mask_ref[...].reshape(1, 2 * text).astype(F32)
-    mask = jnp.where(place_ref[1] == 0, mask[:, :text], mask[:, text:])
-    keep = jnp.concatenate([mask, jnp.ones((1, video), F32)], axis=1)
     packed = den_ref[...]
     for head in range(width // HEAD_DIM):
         cells = slice(head * HEAD_DIM, (head + 1) * HEAD_DIM)
         columns = slice((first + head) * HEAD_DIM, (first + head + 1) * HEAD_DIM)
         queries = jnp.concatenate([qo_ref[:, columns], qp_ref[:, columns]], axis=0)
-        keys = jnp.concatenate([text_ref[0, :, columns], far_ref[0, :, cells]], axis=0)
-        values = jnp.concatenate([text_ref[1, :, columns], far_ref[1, :, cells]], axis=0)
-        weights = weigh(queries, keys) * keep
-        num = num_ref[:, columns] + times(weights, values)
+        weights = weigh(queries, far_ref[0, :, columns])
+        num = num_ref[:, columns] + times(weights, far_ref[1, :, columns])
         own_ref[:, cells] = num[:video]
         msg_ref[:, cells] = num[video:]
         total = jnp.sum(lanes(weights), axis=1, keepdims=True)
@@ -414,62 +412,44 @@
     vmem = pl.BlockSpec(memory_space=pltpu.VMEM)
     hbm = pl.BlockSpec(memory_space=pltpu.HBM)
     smem = pl.BlockSpec(memory_space=pltpu.SMEM)
-    half_block = jax.ShapeDtypeStruct((2, video, width // 2), BF16)
-    stale = pl.pallas_call(
-        split_kernel,
-        in_specs=[hbm],
-        out_specs=[vmem] * 2,
-        out_shape=[half_block] * 2,
-        scratch_shapes=[pltpu.SemaphoreType.DMA((2,))],
-        compiler_params=params(16),
-        cost_estimate=cost(0, 8 * video * width),
-        name="split_heads",
-    )(in_hbm(stale_cache))
-    place = lax.optimization_barrier((place, *stale))[0]
-    chains = [[ring_step((half, half))] for half in stale]
-
-    block_heads = 2 if heads % 2 == 0 else 1
-    columns = block_heads * TRIPLE
-    blocks = heads // block_heads
+    ring = [ring_step((stale_cache, stale_cache))]
+
+    chunks = group_columns // PIECE
+    ahead = chunks * 2 // 3
+    bands = -(-heads * 4 // chunks)
+    message_rows = top + bands * text // 4
     project_cost = cost(8 * rows * features * group_columns, 2 * features * group_columns)
-    a_rows, message, text_message, stats, w_columns = pl.pallas_call(
+    a_rows, message, stats, w_ahead = pl.pallas_call(
         send_kernel,
         in_specs=[smem] + [hbm] * 5,
-        out_specs=[vmem] * 5,
+        out_specs=[vmem] * 4,
         out_shape=[
             jax.ShapeDtypeStruct((rows, features), BF16),
-            jax.ShapeDtypeStruct((top, group_columns), BF16),
-            jax.ShapeDtypeStruct((text, 2 * width), BF16),
+            jax.ShapeDtypeStruct((message_rows, group_columns), BF16),
             jax.ShapeDtypeStruct((rows, HEAD_DIM), F32),
-            jax.ShapeDtypeStruct((blocks, features, columns), BF16),
+            jax.ShapeDtypeStruct((ahead, features, PIECE), BF16),
         ],
         scratch_shapes=[
             pltpu.VMEM((video, features), BF16),
             pltpu.VMEM((text, features), BF16),
             pltpu.VMEM((features,), F32),
             pltpu.VMEM((features,), F32),
-            pltpu.VMEM((blocks, features, columns), BF16),
+            pltpu.VMEM((chunks, features, PIECE), BF16),
             pltpu.SemaphoreType.DMA((4,)),
-            pltpu.SemaphoreType.DMA((blocks,)),
-            pltpu.SemaphoreType.DMA((blocks,)),
+            pltpu.SemaphoreType.DMA((chunks + ahead,)),
         ],
-        compiler_params=params(28),
+        compiler_params=params(40),
         cost_estimate=project_cost,
         name="project_send",
-    )(
-        place,
-        *map(in_hbm, (hidden, text_hidden, norm_scale, norm_shift, qkv_weight)),
-    )
+    )(place, *map(in_hbm, (hidden, text_hidden, norm_scale, norm_shift, qkv_weight)))
 
     received = lax.ppermute(message, "head", swap_head)
-
-    for chain in chains:
-        chain.append(ring_step(lax.optimization_barrier((*chain[-1], message))[:2]))
-
-    small = (query_gain, key_gain, text_mask, branch_gate, hidden)
+    ring.append(ring_step(lax.optimization_barrier((*ring[-1], message))[:2]))
+
+    small = (query_gain, key_gain, text_mask, branch_gate, hidden, stale_cache)
     outs = pl.pallas_call(
         own_kernel,
-        in_specs=[smem, vmem, vmem, hbm] + [hbm] * len(small),
+        in_specs=[smem, vmem, vmem, hbm, hbm] + [hbm] * len(small),
         out_specs=[vmem] * (4 + len(small)),
         out_shape=[
             jax.ShapeDtypeStruct((top, group_columns), F32),
@@ -478,79 +458,68 @@
             jax.ShapeDtypeStruct((width, out_features), BF16),
         ]
         + [jax.ShapeDtypeStruct(array.shape, array.dtype) for array in small],
-        scratch_shapes=[pltpu.SemaphoreType.DMA((len(small) + 2,))],
-        compiler_params=params(24),
+        scratch_shapes=[
+            pltpu.VMEM((chunks - ahead, features, PIECE), BF16),
+            pltpu.SemaphoreType.DMA((chunks - ahead,)),
+            pltpu.SemaphoreType.DMA((len(small) + 2,)),
+        ],
+        compiler_params=params(36),
         cost_estimate=project_cost,
         name="project_own",
-    )(place, a_rows, w_columns, *map(in_hbm, (out_weight,) + small))
+    )(place, a_rows, w_ahead, *map(in_hbm, (qkv_weight, out_weight) + small))
     own, own_text, w_own, w_other = outs[:4]
-    query_gain, key_gain, text_mask, branch_gate, hidden = outs[4:]
-
-    for step in range(half_way - 3):
-        for chain in chains:
-            last = chain[-1]
-            if step == 0:
-                last = lax.optimization_barrier((*last, own))[:2]
-            chain.append(ring_step(last))
-
-    received = lax.optimization_barrier((received, *chains[1][1]))[0]
-    text_message = lax.optimization_barrier((text_message, received))[0]
-    text_received = lax.ppermute(text_message, "head", swap_head)
+    query_gain, key_gain, text_mask, branch_gate, hidden, stale = outs[4:]
+
+    for _ in range(half_way - 3):
+        ring.append(ring_step(lax.optimization_barrier((*ring[-1], own))[:2]))
+    far = lax.ppermute(ring[-1][0], "section", ways[0])
 
     queries, new_cache, fresh = plain_call(
         functools.partial(norm_kernel, features * 2),
         [((video, width), BF16), ((2, video, width), BF16), ((2, video, width), BF16)],
         "norm_video",
-        cost(20 * top * group_columns, 8 * top * group_columns),
+        cost(1000 * top * group_columns, 8 * top * group_columns),
         own, received, stats, query_gain, key_gain,
     )
     other_queries = lax.ppermute(queries, "section", swap_core)
-    far = [
-        lax.ppermute(lax.optimization_barrier((chain[-1][0], queries))[0], "section", ways[0])
-        for chain in chains
-    ]
-
-    halves = [
-        block
-        for steps in zip(*chains)
-        for way in range(2)
-        for block in (steps[0][way], steps[1][way])
-    ]
-    context = (len(halves) // 2 + 1) * video
-    num, den = plain_call(
-        first_kernel,
-        [((2 * video, width), F32), ((2 * video, HEAD_DIM), F32)],
-        "attend_first",
-        cost(8 * video * context * width, 4 * context * width, 2 * video * context * heads),
-        queries, other_queries, fresh, *stale, *halves,
-    )
     (text_kv,) = plain_call(
         functools.partial(text_kernel, features * 2),
         [((2, text, width), BF16)],
         "norm_text",
-        cost(20 * text * group_columns, 8 * text * group_columns),
-        own_text, text_received, stats, own, received, key_gain,
-    )
-
-    last_context = video + text
+        cost(1000 * text * group_columns, 8 * text * group_columns),
+        own_text, received, stats, own, key_gain,
+    )
+
+    blocks = [block for step in ring for block in step]
+    context = (len(blocks) + 1) * video + text
+    num, den = pl.pallas_call(
+        first_kernel,
+        in_specs=[smem] + [vmem] * (6 + len(blocks)),
+        out_specs=[vmem] * 2,
+        out_shape=[
+            jax.ShapeDtypeStruct((2 * video, width), F32),
+            jax.ShapeDtypeStruct((2 * video, HEAD_DIM), F32),
+        ],
+        compiler_params=params(24),
+        cost_estimate=cost(
+            32 * video * context * width, 4 * context * width, 2 * video * context * heads
+        ),
+        name="attend_first",
+    )(place, queries, other_queries, fresh, stale, text_kv, text_mask, *blocks)
+
     attended, other_attended = [], []
-    for index, block in enumerate(far):
-        first = index * heads // 2
-        num_own, den_own, num_message = pl.pallas_call(
+    for first in (0, heads // 2):
+        num_own, den_own, num_message = plain_call(
             functools.partial(last_kernel, first),
-            in_specs=[smem] + [vmem] * 7,
-            out_specs=[vmem] * 3,
-            out_shape=[
-                jax.ShapeDtypeStruct((video, width // 2), F32),
-                jax.ShapeDtypeStruct((video, HEAD_DIM), F32),
-                jax.ShapeDtypeStruct((video, width // 2 + HEAD_DIM), F32),
+            [
+                ((video, width // 2), F32),
+                ((video, HEAD_DIM), F32),
+                ((video, width // 2 + HEAD_DIM), F32),
             ],
-            compiler_params=params(24),
-            cost_estimate=cost(
-                4 * video * last_context * width, 6 * video * width, video * last_context * heads
-            ),
-            name="attend_last",
-        )(place, queries, other_queries, num, den, text_kv, text_mask, block)
+            "attend_last",
+            cost(16 * video * video * width, 6 * video * width, video * video * heads),
+            queries, other_queries, num, den, far,
+        )
         num_received = lax.ppermute(num_message, "section", swap_core)
         attended += plain_call(
             functools.partial(merge_kernel, first),
@@ -561,7 +530,7 @@
         )
         other_attended.append(lax.ppermute(attended[-1], "head", swap_head))
 
-    out_cost = cost(2 * video * width * out_features, 2 * width * out_features)
+    out_cost = cost(4 * video * width * out_features, 2 * width * out_features)
     (part,) = plain_call(
         part_kernel, [((video, out_features), F32)], "part_out", out_cost, *attended, w_own
     )

time: 58.8 us -> 59.2 us (level)
  starting transfers between devices: 22 us -> 13.7 us
  waiting for transfers between devices: 13.2 us -> 20.7 us
  Pallas kernels: 22.6 us -> 23.9 us
    ppermute x12 -> x6, starting transfers between devices: 14 us -> 7.14 us  [ring_step(): lax.ppermute(block, 'section', way)]
    ppermute x1, waiting for transfers between devices: 4.82 us -> 10.6 us  [per_device(): received = lax.ppermute(message, 'head', swap_head)]
    pallas_call x4 -> x2, Pallas kernels: 6.53 us -> 9.2 us  [the longest x1 5.17 us: per_device(): pl.pallas_call(own_kernel, in_specs=[smem, vmem, vmem, hbm, hbm] + [hbm]...]
    pallas_call x7 -> x8, Pallas kernels: 7.55 us -> 5.28 us  [plain_call(): pl.pallas_call(kernel, in_specs=[pl.BlockSpec(memory_space=pltpu.VMEM)] *...]
    ppermute x3 -> x1, starting transfers between devices: 3.67 us -> 1.68 us  [per_device(): far = lax.ppermute(ring[-1][0], 'section', ways[0])]
    ppermute x3 -> x1, waiting for transfers between devices: 0.01 us -> 1.45 us  [per_device(): far = lax.ppermute(ring[-1][0], 'section', ways[0])]
    pallas_call x1, Pallas kernels: 8.5 us -> 9.37 us  [per_device(): pl.pallas_call(send_kernel, in_specs=[smem] + [hbm] * 5, out_specs=[vmem]...]
    ppermute x12 -> x6, waiting for transfers between devices: 3.88 us -> 4.17 us  [ring_step(): lax.ppermute(block, 'section', way)]
  transfers between devices with their start and end apart: 21 -> 13, of which waited for: 7 -> 6; matrix products, arithmetic and copies ran while one was open for 0% -> 0% of each run, Pallas kernels for 34% -> 37%
where the time goes in v6:
time: 59.2 us; the launch traced here: 59 us
  Pallas kernels  23.9 us (40%)
  waiting for transfers between devices  20.7 us (35%)
  starting transfers between devices  13.7 us (23%)
  between operations  0.73 us (1%)
    ppermute x1, waiting for transfers between devices, per_device(): received = lax.ppermute(message, 'head', swap_head)  10.6 us
    pallas_call x1, Pallas kernels, per_device(): pl.pallas_call(send_kernel, in_specs=[smem] + [hbm] * 5, out_specs=[vmem]...  9.37 us
    ppermute x6, starting transfers between devices, ring_step(): lax.ppermute(block, 'section', way)  7.14 us
    pallas_call x8, Pallas kernels, plain_call(): pl.pallas_call(kernel, in_specs=[pl.BlockSpec(memory_space=pltpu.VMEM)] *...  5.28 us
    pallas_call x1, Pallas kernels, per_device(): pl.pallas_call(own_kernel, in_specs=[smem, vmem, vmem, hbm, hbm] + [hbm]...  5.17 us
    ppermute x6, waiting for transfers between devices, ring_step(): lax.ppermute(block, 'section', way)  4.17 us
    ppermute x2, waiting for transfers between devices, per_device(): other_attended.append(lax.ppermute(attended[-1], 'head', swap_head))  4.04 us
    pallas_call x1, Pallas kernels, per_device(): pl.pallas_call(first_kernel, in_specs=[smem] + [vmem] * (6 + len(blocks))...  4.03 us
  transfers between devices with their start and end apart: 13, of which 6 were waited for; matrix products, arithmetic and copies ran while one was open for 0% of the time, Pallas kernels for 37%

profile of v6, /device:TPU:0, one launch (start us, length us, event | category | flops | bytes accessed | tf_op | source)
XLA Modules:
  0.0 59.0 jit_solution(9087650618191798054)
XLA Ops:
  0.6 3.1 %collective-permute-start.2 = (bf16[2,128,768]{2,1,0:T(8,128)(2,1)}, bf16[2,128,768]{2,1,0:T(8,128)(2,1)S(1)}, u32[]{:S(2)}, u32[]{:S(2)}) collective-permute-start(bf16[2,128,768]{2,1,0:T(8,128)(2,1)} %refs_5_.1), channel_id=1, source_target_pairs={{0,8},{2,6},{4,0},{6,14},{8,16},{10,2},{12,4},{14,22},{16,24},{18,... | collective-permute-start | bytes 1179656 | tf_op jit(solution)/shard_map/ppermute | solution.py:410
  3.8 9.4 %project_send.1 = (bf16[272,1536]{1,0:T(8,128)(2,1)S(1)}, bf16[240,2304]{1,0:T(8,128)(2,1)S(1)}, f32[272,128]{1,0:T(8,128)S(1)}, bf16[6,1536,256]{2,1,0:T(8,128)(2,1)S(1)}) custom-call(s32[2]{0:T(128)S(1)} %pad_add_fusion.place_ref, bf16[128,1536]{1,0:T(8,128)(2,1)} %refs_4_.1, bf16[256,1536]{1,0:T(8,128)(2,1)} %t_ref.1, f32[1536]{0:T(1024)} %scale_ref.1, ...), custom_call_target="tpu_custom_call" | custom-call | flops 7700742144 | bytes 7077888 | tf_op jit(solution)/shard_map/project_send/pallas_call | solution.py:422
  13.2 2.0 %collective-permute-start = (bf16[240,2304]{1,0:T(8,128)(2,1)S(1)}, bf16[240,2304]{1,0:T(8,128)(2,1)S(1)}, u32[]{:S(2)}, u32[]{:S(2)}) collective-permute-start(bf16[240,2304]{1,0:T(8,128)(2,1)S(1)} %get-tuple-element.34), channel_id=1, source_target_pairs={{0,1},{1,0},{2,3},{3,2},{4,5},{5,4},{6,7},{7,6},{8,9},{9,8},{10,11... | collective-permute-start | bytes 3317768 | tf_op jit(solution)/shard_map/ppermute | solution.py:446
  15.2 1.6 %collective-permute-start.4 = (bf16[2,128,768]{2,1,0:T(8,128)(2,1)S(1)}, bf16[2,128,768]{2,1,0:T(8,128)(2,1)S(1)}, u32[]{:S(2)}, u32[]{:S(2)}) collective-permute-start(bf16[2,128,768]{2,1,0:T(8,128)(2,1)S(1)} %collective-permute-done.2.refs_0_), channel_id=1, source_target_pairs={{0,8},{2,6},{4,0},{6,14},{8,16},{10,2},{12,4},{14,22},{16,24},{18,... | collective-permute-start | bytes 1179656 | tf_op jit(solution)/shard_map/ppermute | solution.py:410
  16.8 0.4 collective-permute-start.5
  17.2 5.2 %project_own.1 = (f32[144,2304]{1,0:T(8,128)S(1)}, f32[128,1536]{1,0:T(8,128)S(1)}, bf16[768,1536]{1,0:T(8,128)(2,1)S(1)}, bf16[768,1536]{1,0:T(8,128)(2,1)S(1)}...) custom-call(s32[2]{0:T(128)S(1)} %pad_add_fusion.place_ref, ...), custom_call_target="tpu_custom_call" | custom-call | flops 7700742144 | bytes 7077888 | tf_op jit(solution)/shard_map/project_own/pallas_call | solution.py:450
  22.4 4.2 %collective-permute-done.4.refs_2_ = bf16[2,128,768]{2,1,0:T(8,128)(2,1)S(1)} collective-permute-done((bf16[2,128,768]{2,1,0:T(8,128)(2,1)S(1)}, bf16[2,128,768]{2,1,0:T(8,128)(2,1)S(1)}, u32[]{:S(2)}, u32[]{:S(2)}) %collective-permute-start.4) | collective-permute-done | bytes 393248 | tf_op jit(solution)/shard_map/ppermute | solution.py:410
  26.9 1.6 %collective-permute-start.7 = (bf16[2,128,768]{2,1,0:T(8,128)(2,1)S(1)}, bf16[2,128,768]{2,1,0:T(8,128)(2,1)S(1)}, u32[]{:S(2)}, u32[]{:S(2)}) collective-permute-start(bf16[2,128,768]{2,1,0:T(8,128)(2,1)S(1)} %collective-permute-done.5.refs_3_), channel_id=1, source_target_pairs={{0,4},{2,10},{4,12},{6,2},{8,0},{10,18},{12,20},{14,6},{16,8},{18,... | collective-permute-start | bytes 1179656 | tf_op jit(solution)/shard_map/ppermute | solution.py:410
  28.6 10.6 %collective-permute-done.msg_ref = bf16[240,2304]{1,0:T(8,128)(2,1)S(1)} collective-permute-done((bf16[240,2304]{1,0:T(8,128)(2,1)S(1)}, bf16[240,2304]{1,0:T(8,128)(2,1)S(1)}, u32[]{:S(2)}, u32[]{:S(2)}) %collective-permute-start) | collective-permute-done | bytes 1105952 | tf_op jit(solution)/shard_map/ppermute | solution.py:446
  39.1 1.5 %norm_video.1 = (bf16[128,768]{1,0:T(8,128)(2,1)S(1)}, bf16[2,128,768]{2,1,0:T(8,128)(2,1)}, bf16[2,128,768]{2,1,0:T(8,128)(2,1)S(1)}) custom-call(f32[144,2304]{1,0:T(8,128)S(1)} %get-tuple-element.33.own_ref.top_ref, bf16[240,2304]{1,0:T(8,128)(2,1)S(1)} %collective-permute-done.msg_ref, f32[272,128]{1,0:T(8,128)S(1)} %get-tuple-element.35.stat_ref, ...), custom_call_target="tpu_custom_call" | custom-call | flops 331776000 | bytes 2654208 | tf_op jit(solution)/shard_map/norm_video/pallas_call | solution.py:365
  40.7 1.7 %collective-permute-start.8 = (bf16[2,128,768]{2,1,0:T(8,128)(2,1)S(1)}, bf16[2,128,768]{2,1,0:T(8,128)(2,1)S(1)}, u32[]{:S(2)}, u32[]{:S(2)}) collective-permute-start(bf16[2,128,768]{2,1,0:T(8,128)(2,1)S(1)} %collective-permute-done.6.refs_4_), channel_id=1, source_target_pairs={{0,8},{2,6},{4,0},{6,14},{8,16},{10,2},{12,4},{14,22},{16,24},{18,... | collective-permute-start | bytes 1179656 | tf_op jit(solution)/shard_map/ppermute | solution.py:475
  42.4 0.6 norm_text.1.text_ref
  43.0 4.0 %attend_first.1 = (f32[256,768]{1,0:T(8,128)S(1)}, f32[256,128]{1,0:T(8,128)S(1)}) custom-call(s32[2]{0:T(128)S(1)} %pad_add_fusion.place_ref, bf16[128,768]{1,0:T(8,128)(2,1)S(1)} %get-tuple-element.38.qo_ref, bf16[128,768]{1,0:T(8,128)(2,1)S(1)} %collective-permute-done.1.qp_ref, bf16[2,128,768]{2,1,0:T(8,128)(2,1)S(1)} %get-tuple-element.39.fresh_ref, ...), custom_call_target="tpu_custom_call" | custom-call | flops 3221225472 | bytes 3145728 | tf_op jit(solution)/shard_map/attend_first/pallas_call | solution.py:495
  47.0 1.4 %collective-permute-done.8.far_ref = bf16[2,128,768]{2,1,0:T(8,128)(2,1)S(1)} collective-permute-done((bf16[2,128,768]{2,1,0:T(8,128)(2,1)S(1)}, bf16[2,128,768]{2,1,0:T(8,128)(2,1)S(1)}, u32[]{:S(2)}, u32[]{:S(2)}) %collective-permute-start.8) | collective-permute-done | bytes 393248 | tf_op jit(solution)/shard_map/ppermute | solution.py:475
  48.5 0.5 attend_last.3
  49.0 0.5 attend_last.2
  49.5 0.6 collective-permute-start.9
  50.1 0.5 collective-permute-done.10.msg_ref
  50.7 1.7 %collective-permute-start.12 = (bf16[128,384]{1,0:T(8,128)(2,1)S(1)}, bf16[128,384]{1,0:T(8,128)(2,1)S(1)}, u32[]{:S(2)}, u32[]{:S(2)}) collective-permute-start(bf16[128,384]{1,0:T(8,128)(2,1)S(1)} %merge.3.second_ref), channel_id=1, source_target_pairs={{0,1},{1,0},{2,3},{3,2},{4,5},{5,4},{6,7},{7,6},{8,9},{9,8},{10,11... | collective-permute-start | bytes 294920 | tf_op jit(solution)/shard_map/ppermute | solution.py:531
  52.5 0.6 collective-permute-start.11
  53.1 0.6 part_out.1.part_ref
  53.7 2.6 %collective-permute-done.12.second_ref = bf16[128,384]{1,0:T(8,128)(2,1)S(1)} collective-permute-done((bf16[128,384]{1,0:T(8,128)(2,1)S(1)}, bf16[128,384]{1,0:T(8,128)(2,1)S(1)}, u32[]{:S(2)}, u32[]{:S(2)}) %collective-permute-start.12) | collective-permute-done | bytes 98336 | tf_op jit(solution)/shard_map/ppermute | solution.py:531
  56.2 1.5 %collective-permute-done.11.first_ref = bf16[128,384]{1,0:T(8,128)(2,1)S(1)} collective-permute-done((bf16[128,384]{1,0:T(8,128)(2,1)S(1)}, bf16[128,384]{1,0:T(8,128)(2,1)S(1)}, u32[]{:S(2)}, u32[]{:S(2)}) %collective-permute-start.11) | collective-permute-done | bytes 98336 | tf_op jit(solution)/shard_map/ppermute | solution.py:531
  57.7 1.3 %final_out.1 = bf16[128,1536]{1,0:T(8,128)(2,1)} custom-call(f32[128,1536]{1,0:T(8,128)S(1)} %part_out.1.part_ref, bf16[128,384]{1,0:T(8,128)(2,1)S(1)} %collective-permute-done.11.first_ref, bf16[128,384]{1,0:T(8,128)(2,1)S(1)} %collective-permute-done.12.second_ref, bf16[768,1536]{1,0:T(8,128)(2,1)S(1)} %get-tuple-element.56.w_ref, ...), custom_call_target="tpu_custom_call" | custom-call | flops 603979776 | bytes 2359296 | tf_op jit(solution)/shard_map/final_out/pallas_call | solution.py:365
  (14 shorter events, 0.8 us)
Async XLA Ops:
  0.6 14.5 %collective-permute-start.2 = (bf16[2,128,768]{2,1,0:T(8,128)(2,1)}, bf16[2,128,768]{2,1,0:T(8,128)(2,1)S(1)}, u32[]{:S(2)}, u32[]{:S(2)}) collective-permute-start(bf16[2,128,768]{2,1,0:T(8,128)(2,1)} %refs_5_.1), channel_id=1, source_target_pairs={{0,8},{2,6},{4,0},{6,14},{8,16},{10,2},{12,4},{14,22},{16,24},{18,... | collective-permute-start | bytes 1179656 | tf_op jit(solution)/shard_map/ppermute | solution.py:410
  3.7 11.5 %collective-permute-start.3 = (bf16[2,128,768]{2,1,0:T(8,128)(2,1)}, bf16[2,128,768]{2,1,0:T(8,128)(2,1)S(1)}, u32[]{:S(2)}, u32[]{:S(2)}) collective-permute-start(bf16[2,128,768]{2,1,0:T(8,128)(2,1)} %refs_5_.1), channel_id=1, source_target_pairs={{0,4},{2,10},{4,12},{6,2},{8,0},{10,18},{12,20},{14,6},{16,8},{18,... | collective-permute-start | bytes 1179656 | tf_op jit(solution)/shard_map/ppermute | solution.py:410
  13.2 26.0 %collective-permute-start = (bf16[240,2304]{1,0:T(8,128)(2,1)S(1)}, bf16[240,2304]{1,0:T(8,128)(2,1)S(1)}, u32[]{:S(2)}, u32[]{:S(2)}) collective-permute-start(bf16[240,2304]{1,0:T(8,128)(2,1)S(1)} %get-tuple-element.34), channel_id=1, source_target_pairs={{0,1},{1,0},{2,3},{3,2},{4,5},{5,4},{6,7},{7,6},{8,9},{9,8},{10,11... | collective-permute-start | bytes 3317768 | tf_op jit(solution)/shard_map/ppermute | solution.py:446
  15.2 11.4 %collective-permute-start.4 = (bf16[2,128,768]{2,1,0:T(8,128)(2,1)S(1)}, bf16[2,128,768]{2,1,0:T(8,128)(2,1)S(1)}, u32[]{:S(2)}, u32[]{:S(2)}) collective-permute-start(bf16[2,128,768]{2,1,0:T(8,128)(2,1)S(1)} %collective-permute-done.2.refs_0_), channel_id=1, source_target_pairs={{0,8},{2,6},{4,0},{6,14},{8,16},{10,2},{12,4},{14,22},{16,24},{18,... | collective-permute-start | bytes 1179656 | tf_op jit(solution)/shard_map/ppermute | solution.py:410
  16.8 9.8 %collective-permute-start.5 = (bf16[2,128,768]{2,1,0:T(8,128)(2,1)S(1)}, bf16[2,128,768]{2,1,0:T(8,128)(2,1)S(1)}, u32[]{:S(2)}, u32[]{:S(2)}) collective-permute-start(bf16[2,128,768]{2,1,0:T(8,128)(2,1)S(1)} %collective-permute-done.3.refs_1_), channel_id=1, source_target_pairs={{0,4},{2,10},{4,12},{6,2},{8,0},{10,18},{12,20},{14,6},{16,8},{18,... | collective-permute-start | bytes 1179656 | tf_op jit(solution)/shard_map/ppermute | solution.py:410
  26.5 14.1 %collective-permute-start.6 = (bf16[2,128,768]{2,1,0:T(8,128)(2,1)S(1)}, bf16[2,128,768]{2,1,0:T(8,128)(2,1)S(1)}, u32[]{:S(2)}, u32[]{:S(2)}) collective-permute-start(bf16[2,128,768]{2,1,0:T(8,128)(2,1)S(1)} %collective-permute-done.4.refs_2_), channel_id=1, source_target_pairs={{0,8},{2,6},{4,0},{6,14},{8,16},{10,2},{12,4},{14,22},{16,24},{18,... | collective-permute-start | bytes 1179656 | tf_op jit(solution)/shard_map/ppermute | solution.py:410
  26.9 16.0 %collective-permute-start.7 = (bf16[2,128,768]{2,1,0:T(8,128)(2,1)S(1)}, bf16[2,128,768]{2,1,0:T(8,128)(2,1)S(1)}, u32[]{:S(2)}, u32[]{:S(2)}) collective-permute-start(bf16[2,128,768]{2,1,0:T(8,128)(2,1)S(1)} %collective-permute-done.5.refs_3_), channel_id=1, source_target_pairs={{0,4},{2,10},{4,12},{6,2},{8,0},{10,18},{12,20},{14,6},{16,8},{18,... | collective-permute-start | bytes 1179656 | tf_op jit(solution)/shard_map/ppermute | solution.py:410
  40.7 2.3 %collective-permute-start.1 = (bf16[128,768]{1,0:T(8,128)(2,1)S(1)}, bf16[128,768]{1,0:T(8,128)(2,1)S(1)}, u32[]{:S(2)}, u32[]{:S(2)}) collective-permute-start(bf16[128,768]{1,0:T(8,128)(2,1)S(1)} %get-tuple-element.38.qo_ref), channel_id=1, source_target_pairs={{0,2},{2,0},{4,6},{6,4},{8,10},{10,8},{12,14},{14,12},{16,18},{18,... | collective-permute-start | bytes 589832 | tf_op jit(solution)/shard_map/ppermute | solution.py:484
  40.7 7.8 %collective-permute-start.8 = (bf16[2,128,768]{2,1,0:T(8,128)(2,1)S(1)}, bf16[2,128,768]{2,1,0:T(8,128)(2,1)S(1)}, u32[]{:S(2)}, u32[]{:S(2)}) collective-permute-start(bf16[2,128,768]{2,1,0:T(8,128)(2,1)S(1)} %collective-permute-done.6.refs_4_), channel_id=1, source_target_pairs={{0,8},{2,6},{4,0},{6,14},{8,16},{10,2},{12,4},{14,22},{16,24},{18,... | collective-permute-start | bytes 1179656 | tf_op jit(solution)/shard_map/ppermute | solution.py:475
  49.0 1.6 %collective-permute-start.10 = (f32[128,512]{1,0:T(8,128)S(1)}, f32[128,512]{1,0:T(8,128)S(1)}, u32[]{:S(2)}, u32[]{:S(2)}) collective-permute-start(f32[128,512]{1,0:T(8,128)S(1)} %get-tuple-element.54), channel_id=1, source_target_pairs={{0,2},{2,0},{4,6},{6,4},{8,10},{10,8},{12,14},{14,12},{16,18},{18,... | collective-permute-start | bytes 786440 | tf_op jit(solution)/shard_map/ppermute | solution.py:523
  49.5 2.8 %collective-permute-start.9 = (f32[128,512]{1,0:T(8,128)S(1)}, f32[128,512]{1,0:T(8,128)S(1)}, u32[]{:S(2)}, u32[]{:S(2)}) collective-permute-start(f32[128,512]{1,0:T(8,128)S(1)} %get-tuple-element.51), channel_id=1, source_target_pairs={{0,2},{2,0},{4,6},{6,4},{8,10},{10,8},{12,14},{14,12},{16,18},{18,... | collective-permute-start | bytes 786440 | tf_op jit(solution)/shard_map/ppermute | solution.py:523
  50.7 5.5 %collective-permute-start.12 = (bf16[128,384]{1,0:T(8,128)(2,1)S(1)}, bf16[128,384]{1,0:T(8,128)(2,1)S(1)}, u32[]{:S(2)}, u32[]{:S(2)}) collective-permute-start(bf16[128,384]{1,0:T(8,128)(2,1)S(1)} %merge.3.second_ref), channel_id=1, source_target_pairs={{0,1},{1,0},{2,3},{3,2},{4,5},{5,4},{6,7},{7,6},{8,9},{9,8},{10,11... | collective-permute-start | bytes 294920 | tf_op jit(solution)/shard_map/ppermute | solution.py:531
  52.5 5.2 %collective-permute-start.11 = (bf16[128,384]{1,0:T(8,128)(2,1)S(1)}, bf16[128,384]{1,0:T(8,128)(2,1)S(1)}, u32[]{:S(2)}, u32[]{:S(2)}) collective-permute-start(bf16[128,384]{1,0:T(8,128)(2,1)S(1)} %merge.2.first_ref), channel_id=1, source_target_pairs={{0,1},{1,0},{2,3},{3,2},{4,5},{5,4},{6,7},{7,6},{8,9},{9,8},{10,11... | collective-permute-start | bytes 294920 | tf_op jit(solution)/shard_map/ppermute | solution.py:531

commit v7 on v6

--- a/solution.py
+++ b/solution.py
@@ -13,7 +13,6 @@
 EXTRA = 16
 STAT_ROW = 8
 PIECE = 2 * HEAD_DIM
-IN_FLIGHT = 6
 EPS = 1e-06
 F32 = jnp.float32
 BF16 = jnp.bfloat16
@@ -29,12 +28,13 @@
     return pieces
 
 
-def chunk_copies(w_ref, first, targets, sems, base):
+def block_copies(w_ref, first, targets, sems, base):
     copies = []
     for index, target in enumerate(targets):
-        start = pl.multiple_of(first + index * PIECE, HEAD_DIM)
+        columns = target.shape[1]
+        start = pl.multiple_of(first + index * columns, HEAD_DIM)
         copies.append(
-            pltpu.make_async_copy(w_ref.at[:, pl.ds(start, PIECE)], target, sems.at[base + index])
+            pltpu.make_async_copy(w_ref.at[:, pl.ds(start, columns)], target, sems.at[base + index])
         )
     return copies
 
@@ -47,8 +47,8 @@
     video, features = x_buffer.shape
     text = t_buffer.shape[0]
     top = video + EXTRA
-    chunks = w_buffer.shape[0]
-    width = chunks * PIECE
+    blocks, _, columns = w_buffer.shape
+    width = blocks * columns
     copies = [
         pltpu.make_async_copy(scale_ref, scale_buffer, in_sems.at[0]),
         pltpu.make_async_copy(shift_ref, shift_buffer, in_sems.at[1]),
@@ -57,13 +57,13 @@
             t_ref.at[pl.ds(pl.multiple_of(place_ref[1] * text, text), text)], t_buffer, in_sems.at[3]
         ),
     ]
-    w_copies = chunk_copies(
-        w_ref, (1 - place_ref[0]) * width, [w_buffer.at[i] for i in range(chunks)], w_sems, 0
-    ) + chunk_copies(
+    w_copies = block_copies(
+        w_ref, (1 - place_ref[0]) * width, [w_buffer.at[i] for i in range(blocks)], w_sems, 0
+    ) + block_copies(
         w_ref, place_ref[0] * width, [ahead_ref.at[i] for i in range(ahead_ref.shape[0])],
-        w_sems, chunks,
-    )
-    for copy in copies + w_copies[:IN_FLIGHT]:
+        w_sems, blocks,
+    )
+    for copy in copies + w_copies[:1]:
         copy.start()
 
     copies[0].wait()
@@ -93,30 +93,36 @@
         return jnp.transpose(packed)[:EXTRA]
 
     copies[2].wait()
+    w_copies[1].start()
     video_stats = prepare(x_buffer, 0)
     copies[3].wait()
+    w_copies[2].start()
     text_stats = prepare(t_buffer, top)
     stat_ref[video:top, :] = jnp.zeros((EXTRA, HEAD_DIM), F32)
 
-    for index, copy in enumerate(w_copies):
+    for block in range(blocks):
+        w_copies[block].wait()
+        if block + 3 < len(w_copies):
+            w_copies[block + 3].start()
+        for piece in range(columns // PIECE):
+            start = block * columns + piece * PIECE
+            product = jnp.dot(
+                a_ref[...], w_buffer[block, :, piece * PIECE : (piece + 1) * PIECE],
+                preferred_element_type=F32,
+            )
+            msg_ref[:top, start : start + PIECE] = product[:top].astype(BF16)
+            if start == 0:
+                stats = jnp.concatenate([video_stats, text_stats], axis=1)
+                msg_ref[video:top, : video + text] = (product[video:top] + stats).astype(BF16)
+            for source, target in text_columns(start):
+                part = product[top:, source].astype(BF16)
+                for quarter in range(4):
+                    rows, cells = text_slot(text, width, target, quarter)
+                    msg_ref[top + rows.start : top + rows.stop, cells] = part[
+                        quarter * text // 4 : (quarter + 1) * text // 4
+                    ]
+    for copy in w_copies[blocks:]:
         copy.wait()
-        if index + IN_FLIGHT < len(w_copies):
-            w_copies[index + IN_FLIGHT].start()
-        if index >= chunks:
-            continue
-        start = index * PIECE
-        product = jnp.dot(a_ref[...], w_buffer[index], preferred_element_type=F32)
-        msg_ref[:top, start : start + PIECE] = product[:top].astype(BF16)
-        if index == 0:
-            stats = jnp.concatenate([video_stats, text_stats], axis=1)
-            msg_ref[video:top, : video + text] = (product[video:top] + stats).astype(BF16)
-        for source, target in text_columns(start):
-            part = product[top:, source].astype(BF16)
-            for quarter in range(4):
-                rows, cells = text_slot(text, width, target, quarter)
-                msg_ref[top + rows.start : top + rows.stop, cells] = part[
-                    quarter * text // 4 : (quarter + 1) * text // 4
-                ]
 
 
 def text_slot(text, width, column, quarter):
@@ -141,9 +147,10 @@
     top = out_ref.shape[0]
     depth = w_own_ref.shape[0]
     group = place_ref[0]
-    ahead, later = ahead_ref.shape[0], w_buffer.shape[0]
-    w_copies = chunk_copies(
-        w_ref, (group * (ahead + later) + ahead) * PIECE, [w_buffer.at[i] for i in range(later)],
+    ahead, _, columns = ahead_ref.shape
+    later = w_buffer.shape[0]
+    w_copies = block_copies(
+        w_ref, (group * (ahead + later) + ahead) * columns, [w_buffer.at[i] for i in range(later)],
         w_sems, 0,
     )
     pairs = list(zip(refs[:small], refs[small + 4 : -3]))
@@ -154,19 +161,28 @@
         pltpu.make_async_copy(source, target, sems.at[index])
         for index, (source, target) in enumerate(pairs)
     ]
-    for copy in w_copies + copies:
+    for copy in w_copies:
         copy.start()
 
-    for index in range(ahead + later):
-        if index < ahead:
-            columns = ahead_ref[index]
-        else:
-            w_copies[index - ahead].wait()
-            columns = w_buffer[index - ahead]
-        product = jnp.dot(a_ref[...], columns, preferred_element_type=F32)
-        out_ref[:, index * PIECE : (index + 1) * PIECE] = product[:top]
-        for source, target in text_columns(index * PIECE):
+    def write(start, product):
+        out_ref[:, start : start + PIECE] = product[:top]
+        for source, target in text_columns(start):
             text_ref[:, target : target + HEAD_DIM] = product[top:, source]
+
+    for block in range(ahead + later):
+        if block == ahead:
+            for copy in w_copies:
+                copy.wait()
+        if block == min(1, ahead):
+            for copy in copies:
+                copy.start()
+        for piece in range(columns // PIECE):
+            cells = slice(piece * PIECE, (piece + 1) * PIECE)
+            part = ahead_ref[block, :, cells] if block < ahead else w_buffer[block - ahead, :, cells]
+            write(
+                block * columns + piece * PIECE,
+                jnp.dot(a_ref[...], part, preferred_element_type=F32),
+            )
     for copy in copies:
         copy.wait()
 
@@ -330,19 +346,23 @@
         att_ref[:, columns] = (num / den).astype(BF16)
 
 
-def project_out(first_ref, second_ref, w_ref):
+def part_kernel(first_ref, second_ref, w_ref, out_ref):
     half = first_ref.shape[1]
-    return jnp.dot(first_ref[...], w_ref[:half, :], preferred_element_type=F32) + jnp.dot(
-        second_ref[...], w_ref[half:, :], preferred_element_type=F32
-    )
-
-
-def part_kernel(first_ref, second_ref, w_ref, out_ref):
-    out_ref[...] = project_out(first_ref, second_ref, w_ref)
-
-
-def final_kernel(part_ref, first_ref, second_ref, w_ref, hidden_ref, gate_ref, out_ref):
-    total = part_ref[...] + project_out(first_ref, second_ref, w_ref)
+    out_ref[...] = jnp.dot(
+        first_ref[...], w_ref[:half, :], preferred_element_type=F32
+    ) + jnp.dot(second_ref[...], w_ref[half:, :], preferred_element_type=F32)
+
+
+def more_kernel(part_ref, att_ref, w_ref, out_ref):
+    half = att_ref.shape[1]
+    out_ref[...] = part_ref[...] + jnp.dot(
+        att_ref[...], w_ref[:half, :], preferred_element_type=F32
+    )
+
+
+def final_kernel(part_ref, att_ref, w_ref, hidden_ref, gate_ref, out_ref):
+    half = att_ref.shape[1]
+    total = part_ref[...] + jnp.dot(att_ref[...], w_ref[half:, :], preferred_element_type=F32)
     gate = gate_ref[...].reshape(1, total.shape[1])
     out_ref[...] = (hidden_ref[...].astype(F32) + gate * total).astype(BF16)
 
@@ -414,9 +434,10 @@
     smem = pl.BlockSpec(memory_space=pltpu.SMEM)
     ring = [ring_step((stale_cache, stale_cache))]
 
-    chunks = group_columns // PIECE
-    ahead = chunks * 2 // 3
-    bands = -(-heads * 4 // chunks)
+    columns = 2 * TRIPLE
+    blocks = group_columns // columns
+    ahead = blocks - 1
+    bands = -(-heads * 4 // (group_columns // PIECE))
     message_rows = top + bands * text // 4
     project_cost = cost(8 * rows * features * group_columns, 2 * features * group_columns)
     a_rows, message, stats, w_ahead = pl.pallas_call(
@@ -427,16 +448,16 @@
             jax.ShapeDtypeStruct((rows, features), BF16),
             jax.ShapeDtypeStruct((message_rows, group_columns), BF16),
             jax.ShapeDtypeStruct((rows, HEAD_DIM), F32),
-            jax.ShapeDtypeStruct((ahead, features, PIECE), BF16),
+            jax.ShapeDtypeStruct((ahead, features, columns), BF16),
         ],
         scratch_shapes=[
             pltpu.VMEM((video, features), BF16),
             pltpu.VMEM((text, features), BF16),
             pltpu.VMEM((features,), F32),
             pltpu.VMEM((features,), F32),
-            pltpu.VMEM((chunks, features, PIECE), BF16),
+            pltpu.VMEM((blocks, features, columns), BF16),
             pltpu.SemaphoreType.DMA((4,)),
-            pltpu.SemaphoreType.DMA((chunks + ahead,)),
+            pltpu.SemaphoreType.DMA((blocks + ahead,)),
         ],
         compiler_params=params(40),
         cost_estimate=project_cost,
@@ -459,8 +480,8 @@
         ]
         + [jax.ShapeDtypeStruct(array.shape, array.dtype) for array in small],
         scratch_shapes=[
-            pltpu.VMEM((chunks - ahead, features, PIECE), BF16),
-            pltpu.SemaphoreType.DMA((chunks - ahead,)),
+            pltpu.VMEM((blocks - ahead, features, columns), BF16),
+            pltpu.SemaphoreType.DMA((blocks - ahead,)),
             pltpu.SemaphoreType.DMA((len(small) + 2,)),
         ],
         compiler_params=params(36),
@@ -490,11 +511,11 @@
         own_text, received, stats, own, key_gain,
     )
 
-    blocks = [block for step in ring for block in step]
-    context = (len(blocks) + 1) * video + text
+    arrived = [block for step in ring for block in step]
+    context = (len(arrived) + 1) * video + text
     num, den = pl.pallas_call(
         first_kernel,
-        in_specs=[smem] + [vmem] * (6 + len(blocks)),
+        in_specs=[smem] + [vmem] * (6 + len(arrived)),
         out_specs=[vmem] * 2,
         out_shape=[
             jax.ShapeDtypeStruct((2 * video, width), F32),
@@ -505,10 +526,12 @@
             32 * video * context * width, 4 * context * width, 2 * video * context * heads
         ),
         name="attend_first",
-    )(place, queries, other_queries, fresh, stale, text_kv, text_mask, *blocks)
+    )(place, queries, other_queries, fresh, stale, text_kv, text_mask, *arrived)
 
     attended, other_attended = [], []
     for first in (0, heads // 2):
+        if attended:
+            num = lax.optimization_barrier((num, num_own))[0]
         num_own, den_own, num_message = plain_call(
             functools.partial(last_kernel, first),
             [
@@ -534,9 +557,13 @@
     (part,) = plain_call(
         part_kernel, [((video, out_features), F32)], "part_out", out_cost, *attended, w_own
     )
+    (part,) = plain_call(
+        more_kernel, [((video, out_features), F32)], "more_out", out_cost,
+        part, other_attended[0], w_other,
+    )
     (mixed,) = plain_call(
         final_kernel, [((video, out_features), BF16)], "final_out", out_cost,
-        part, *other_attended, w_other, hidden, branch_gate,
+        part, other_attended[1], w_other, hidden, branch_gate,
     )
     return (mixed, new_cache)
 

time: 59.2 us -> 55.3 us (0.934)
  Pallas kernels: 23.9 us -> 20.2 us
  waiting for transfers between devices: 20.7 us -> 19.9 us
    pallas_call x1, Pallas kernels: 9.37 us -> 5.64 us  [per_device(): pl.pallas_call(send_kernel, in_specs=[smem] + [hbm] * 5, out_specs=[vmem]...]
    ppermute x1, waiting for transfers between devices: 10.6 us -> 8.26 us  [per_device(): received = lax.ppermute(message, 'head', swap_head)]
    ppermute x6, waiting for transfers between devices: 4.17 us -> 6.08 us  [ring_step(): lax.ppermute(block, 'section', way)]
    pallas_call x8 -> x9, Pallas kernels: 5.28 us -> 5.44 us  [plain_call(): pl.pallas_call(kernel, in_specs=[pl.BlockSpec(memory_space=pltpu.VMEM)] *...]
  transfers between devices with their start and end apart: 13 -> 13, of which waited for: 6 -> 8; matrix products, arithmetic and copies ran while one was open for 0% -> 0% of each run, Pallas kernels for 37% -> 34%
where the time goes in v7:
time: 55.3 us; the launch traced here: 55.1 us
  Pallas kernels  20.2 us (37%)
  waiting for transfers between devices  19.9 us (36%)
  starting transfers between devices  14.2 us (26%)
  between operations  0.73 us (1%)
    ppermute x1, waiting for transfers between devices, per_device(): received = lax.ppermute(message, 'head', swap_head)  8.26 us
    ppermute x6, starting transfers between devices, ring_step(): lax.ppermute(block, 'section', way)  7.66 us
    ppermute x6, waiting for transfers between devices, ring_step(): lax.ppermute(block, 'section', way)  6.08 us
    pallas_call x1, Pallas kernels, per_device(): pl.pallas_call(send_kernel, in_specs=[smem] + [hbm] * 5, out_specs=[vmem]...  5.64 us
    pallas_call x9, Pallas kernels, plain_call(): pl.pallas_call(kernel, in_specs=[pl.BlockSpec(memory_space=pltpu.VMEM)] *...  5.44 us
    pallas_call x1, Pallas kernels, per_device(): pl.pallas_call(own_kernel, in_specs=[smem, vmem, vmem, hbm, hbm] + [hbm]...  5.05 us
    pallas_call x1, Pallas kernels, per_device(): pl.pallas_call(first_kernel, in_specs=[smem] + [vmem] * (6 + len(arrived)...  4.03 us
    ppermute x2, waiting for transfers between devices, per_device(): other_attended.append(lax.ppermute(attended[-1], 'head', swap_head))  3.63 us
  transfers between devices with their start and end apart: 13, of which 8 were waited for; matrix products, arithmetic and copies ran while one was open for 0% of the time, Pallas kernels for 34%

profile of v7, /device:TPU:0, one launch (start us, length us, event | category | flops | bytes accessed | tf_op | source)
XLA Modules:
  0.0 55.1 jit_solution(12953093700120275813)
XLA Ops:
  0.6 3.1 %collective-permute-start.2 = (bf16[2,128,768]{2,1,0:T(8,128)(2,1)}, bf16[2,128,768]{2,1,0:T(8,128)(2,1)S(1)}, u32[]{:S(2)}, u32[]{:S(2)}) collective-permute-start(bf16[2,128,768]{2,1,0:T(8,128)(2,1)} %refs_5_.1), channel_id=1, source_target_pairs={{0,8},{2,6},{4,0},{6,14},{8,16},{10,2},{12,4},{14,22},{16,24},{18,... | collective-permute-start | bytes 1179656 | tf_op jit(solution)/shard_map/ppermute | solution.py:430
  3.8 5.6 %project_send.1 = (bf16[272,1536]{1,0:T(8,128)(2,1)S(1)}, bf16[240,2304]{1,0:T(8,128)(2,1)S(1)}, f32[272,128]{1,0:T(8,128)S(1)}, bf16[2,1536,768]{2,1,0:T(8,128)(2,1)S(1)}) custom-call(s32[2]{0:T(128)S(1)} %pad_add_fusion.place_ref, bf16[128,1536]{1,0:T(8,128)(2,1)} %refs_4_.1, bf16[256,1536]{1,0:T(8,128)(2,1)} %t_ref.1, f32[1536]{0:T(1024)} %scale_ref.1, ...), custom_call_target="tpu_custom_call" | custom-call | flops 7700742144 | bytes 7077888 | tf_op jit(solution)/shard_map/project_send/pallas_call | solution.py:443
  9.4 2.0 %collective-permute-start = (bf16[240,2304]{1,0:T(8,128)(2,1)S(1)}, bf16[240,2304]{1,0:T(8,128)(2,1)S(1)}, u32[]{:S(2)}, u32[]{:S(2)}) collective-permute-start(bf16[240,2304]{1,0:T(8,128)(2,1)S(1)} %get-tuple-element.35), channel_id=1, source_target_pairs={{0,1},{1,0},{2,3},{3,2},{4,5},{5,4},{6,7},{7,6},{8,9},{9,8},{10,11... | collective-permute-start | bytes 3317768 | tf_op jit(solution)/shard_map/ppermute | solution.py:467
  11.4 1.9 %collective-permute-done.2.refs_0_ = bf16[2,128,768]{2,1,0:T(8,128)(2,1)S(1)} collective-permute-done((bf16[2,128,768]{2,1,0:T(8,128)(2,1)}, bf16[2,128,768]{2,1,0:T(8,128)(2,1)S(1)}, u32[]{:S(2)}, u32[]{:S(2)}) %collective-permute-start.2) | collective-permute-done | bytes 393248 | tf_op jit(solution)/shard_map/ppermute | solution.py:430
  13.3 1.6 %collective-permute-start.4 = (bf16[2,128,768]{2,1,0:T(8,128)(2,1)S(1)}, bf16[2,128,768]{2,1,0:T(8,128)(2,1)S(1)}, u32[]{:S(2)}, u32[]{:S(2)}) collective-permute-start(bf16[2,128,768]{2,1,0:T(8,128)(2,1)S(1)} %collective-permute-done.2.refs_0_), channel_id=1, source_target_pairs={{0,8},{2,6},{4,0},{6,14},{8,16},{10,2},{12,4},{14,22},{16,24},{18,... | collective-permute-start | bytes 1179656 | tf_op jit(solution)/shard_map/ppermute | solution.py:430
  14.8 0.8 %collective-permute-start.5 = (bf16[2,128,768]{2,1,0:T(8,128)(2,1)S(1)}, bf16[2,128,768]{2,1,0:T(8,128)(2,1)S(1)}, u32[]{:S(2)}, u32[]{:S(2)}) collective-permute-start(bf16[2,128,768]{2,1,0:T(8,128)(2,1)S(1)} %collective-permute-done.3.refs_1_), channel_id=1, source_target_pairs={{0,4},{2,10},{4,12},{6,2},{8,0},{10,18},{12,20},{14,6},{16,8},{18,... | collective-permute-start | bytes 1179656 | tf_op jit(solution)/shard_map/ppermute | solution.py:430
  15.7 5.0 %project_own.1 = (f32[144,2304]{1,0:T(8,128)S(1)}, f32[128,1536]{1,0:T(8,128)S(1)}, bf16[768,1536]{1,0:T(8,128)(2,1)S(1)}, bf16[768,1536]{1,0:T(8,128)(2,1)S(1)}...) custom-call(s32[2]{0:T(128)S(1)} %pad_add_fusion.place_ref, ...), custom_call_target="tpu_custom_call" | custom-call | flops 7700742144 | bytes 7077888 | tf_op jit(solution)/shard_map/project_own/pallas_call | solution.py:471
  20.7 3.9 %collective-permute-done.4.refs_2_ = bf16[2,128,768]{2,1,0:T(8,128)(2,1)S(1)} collective-permute-done((bf16[2,128,768]{2,1,0:T(8,128)(2,1)S(1)}, bf16[2,128,768]{2,1,0:T(8,128)(2,1)S(1)}, u32[]{:S(2)}, u32[]{:S(2)}) %collective-permute-start.4) | collective-permute-done | bytes 393248 | tf_op jit(solution)/shard_map/ppermute | solution.py:430
  25.0 1.7 %collective-permute-start.6 = (bf16[2,128,768]{2,1,0:T(8,128)(2,1)S(1)}, bf16[2,128,768]{2,1,0:T(8,128)(2,1)S(1)}, u32[]{:S(2)}, u32[]{:S(2)}) collective-permute-start(bf16[2,128,768]{2,1,0:T(8,128)(2,1)S(1)} %collective-permute-done.4.refs_2_), channel_id=1, source_target_pairs={{0,8},{2,6},{4,0},{6,14},{8,16},{10,2},{12,4},{14,22},{16,24},{18,... | collective-permute-start | bytes 1179656 | tf_op jit(solution)/shard_map/ppermute | solution.py:430
  27.1 8.3 %collective-permute-done.msg_ref = bf16[240,2304]{1,0:T(8,128)(2,1)S(1)} collective-permute-done((bf16[240,2304]{1,0:T(8,128)(2,1)S(1)}, bf16[240,2304]{1,0:T(8,128)(2,1)S(1)}, u32[]{:S(2)}, u32[]{:S(2)}) %collective-permute-start) | collective-permute-done | bytes 1105952 | tf_op jit(solution)/shard_map/ppermute | solution.py:467
  35.4 1.5 %norm_video.1 = (bf16[128,768]{1,0:T(8,128)(2,1)S(1)}, bf16[2,128,768]{2,1,0:T(8,128)(2,1)}, bf16[2,128,768]{2,1,0:T(8,128)(2,1)S(1)}) custom-call(f32[144,2304]{1,0:T(8,128)S(1)} %get-tuple-element.34.own_ref.top_ref, bf16[240,2304]{1,0:T(8,128)(2,1)S(1)} %collective-permute-done.msg_ref, f32[272,128]{1,0:T(8,128)S(1)} %get-tuple-element.36.stat_ref, ...), custom_call_target="tpu_custom_call" | custom-call | flops 331776000 | bytes 2654208 | tf_op jit(solution)/shard_map/norm_video/pallas_call | solution.py:385
  36.9 1.7 %collective-permute-start.8 = (bf16[2,128,768]{2,1,0:T(8,128)(2,1)S(1)}, bf16[2,128,768]{2,1,0:T(8,128)(2,1)S(1)}, u32[]{:S(2)}, u32[]{:S(2)}) collective-permute-start(bf16[2,128,768]{2,1,0:T(8,128)(2,1)S(1)} %collective-permute-done.6.refs_4_), channel_id=1, source_target_pairs={{0,8},{2,6},{4,0},{6,14},{8,16},{10,2},{12,4},{14,22},{16,24},{18,... | collective-permute-start | bytes 1179656 | tf_op jit(solution)/shard_map/ppermute | solution.py:496
  38.6 0.6 %norm_text.1.text_ref = bf16[2,128,768]{2,1,0:T(8,128)(2,1)S(1)} custom-call(f32[128,1536]{1,0:T(8,128)S(1)} %get-tuple-element.42.own_ref, bf16[240,2304]{1,0:T(8,128)(2,1)S(1)} %collective-permute-done.msg_ref, f32[272,128]{1,0:T(8,128)S(1)} %get-tuple-element.36.stat_ref, f32[144,2304]{1,0:T(8,128)S(1)} %get-tuple-element.34.own_ref.top_ref, ...), custom_call_target="tpu_custom_call" | custom-call | flops 294912000 | bytes 2359296 | tf_op jit(solution)/shard_map/norm_text/pallas_call | solution.py:385
  39.2 4.0 %attend_first.1 = (f32[256,768]{1,0:T(8,128)S(1)}, f32[256,128]{1,0:T(8,128)S(1)}) custom-call(s32[2]{0:T(128)S(1)} %pad_add_fusion.place_ref, bf16[128,768]{1,0:T(8,128)(2,1)S(1)} %get-tuple-element.39.qo_ref, bf16[128,768]{1,0:T(8,128)(2,1)S(1)} %collective-permute-done.1.qp_ref, bf16[2,128,768]{2,1,0:T(8,128)(2,1)S(1)} %get-tuple-element.40.fresh_ref, ...), custom_call_target="tpu_custom_call" | custom-call | flops 3221225472 | bytes 3145728 | tf_op jit(solution)/shard_map/attend_first/pallas_call | solution.py:516
  43.3 1.5 %collective-permute-done.8.far_ref = bf16[2,128,768]{2,1,0:T(8,128)(2,1)S(1)} collective-permute-done((bf16[2,128,768]{2,1,0:T(8,128)(2,1)S(1)}, bf16[2,128,768]{2,1,0:T(8,128)(2,1)S(1)}, u32[]{:S(2)}, u32[]{:S(2)}) %collective-permute-start.8) | collective-permute-done | bytes 393248 | tf_op jit(solution)/shard_map/ppermute | solution.py:496
  44.7 0.5 attend_last.2
  45.3 0.5 attend_last.3
  45.8 0.6 %collective-permute-start.10 = (f32[128,512]{1,0:T(8,128)S(1)}, f32[128,512]{1,0:T(8,128)S(1)}, u32[]{:S(2)}, u32[]{:S(2)}) collective-permute-start(f32[128,512]{1,0:T(8,128)S(1)} %get-tuple-element.56), channel_id=1, source_target_pairs={{0,2},{2,0},{4,6},{6,4},{8,10},{10,8},{12,14},{14,12},{16,18},{18,... | collective-permute-start | bytes 786440 | tf_op jit(solution)/shard_map/ppermute | solution.py:546
  47.0 1.7 %collective-permute-start.11 = (bf16[128,384]{1,0:T(8,128)(2,1)S(1)}, bf16[128,384]{1,0:T(8,128)(2,1)S(1)}, u32[]{:S(2)}, u32[]{:S(2)}) collective-permute-start(bf16[128,384]{1,0:T(8,128)(2,1)S(1)} %merge.2.first_ref), channel_id=1, source_target_pairs={{0,1},{1,0},{2,3},{3,2},{4,5},{5,4},{6,7},{7,6},{8,9},{9,8},{10,11... | collective-permute-start | bytes 294920 | tf_op jit(solution)/shard_map/ppermute | solution.py:554
  48.8 0.6 %collective-permute-start.12 = (bf16[128,384]{1,0:T(8,128)(2,1)S(1)}, bf16[128,384]{1,0:T(8,128)(2,1)S(1)}, u32[]{:S(2)}, u32[]{:S(2)}) collective-permute-start(bf16[128,384]{1,0:T(8,128)(2,1)S(1)} %merge.3.second_ref), channel_id=1, source_target_pairs={{0,1},{1,0},{2,3},{3,2},{4,5},{5,4},{6,7},{7,6},{8,9},{9,8},{10,11... | collective-permute-start | bytes 294920 | tf_op jit(solution)/shard_map/ppermute | solution.py:554
  49.4 0.6 %part_out.1.part_ref = f32[128,1536]{1,0:T(8,128)S(1)} custom-call(bf16[128,384]{1,0:T(8,128)(2,1)S(1)} %merge.2.first_ref, bf16[128,384]{1,0:T(8,128)(2,1)S(1)} %merge.3.second_ref, bf16[768,1536]{1,0:T(8,128)(2,1)S(1)} %get-tuple-element.57.w_ref), custom_call_target="tpu_custom_call" | custom-call | flops 603979776 | bytes 2359296 | tf_op jit(solution)/shard_map/part_out/pallas_call | solution.py:385
  49.9 2.5 %collective-permute-done.11.att_ref = bf16[128,384]{1,0:T(8,128)(2,1)S(1)} collective-permute-done((bf16[128,384]{1,0:T(8,128)(2,1)S(1)}, bf16[128,384]{1,0:T(8,128)(2,1)S(1)}, u32[]{:S(2)}, u32[]{:S(2)}) %collective-permute-start.11) | collective-permute-done | bytes 98336 | tf_op jit(solution)/shard_map/ppermute | solution.py:554
  52.8 1.1 %collective-permute-done.12.att_ref = bf16[128,384]{1,0:T(8,128)(2,1)S(1)} collective-permute-done((bf16[128,384]{1,0:T(8,128)(2,1)S(1)}, bf16[128,384]{1,0:T(8,128)(2,1)S(1)}, u32[]{:S(2)}, u32[]{:S(2)}) %collective-permute-start.12) | collective-permute-done | bytes 98336 | tf_op jit(solution)/shard_map/ppermute | solution.py:554
  54.0 1.1 %final_out.1 = bf16[128,1536]{1,0:T(8,128)(2,1)} custom-call(f32[128,1536]{1,0:T(8,128)S(1)} %more_out.1.part_ref, bf16[128,384]{1,0:T(8,128)(2,1)S(1)} %collective-permute-done.12.att_ref, bf16[768,1536]{1,0:T(8,128)(2,1)S(1)} %get-tuple-element.58.w_ref, bf16[128,1536]{1,0:T(8,128)(2,1)S(1)} %get-tuple-element.59.hidden_ref, ...), custom_call_target="tpu_custom_call" | custom-call | flops 603979776 | bytes 2359296 | tf_op jit(solution)/shard_map/final_out/pallas_call | solution.py:385
  (15 shorter events, 2.1 us)
Async XLA Ops:
  0.6 12.7 %collective-permute-start.2 = (bf16[2,128,768]{2,1,0:T(8,128)(2,1)}, bf16[2,128,768]{2,1,0:T(8,128)(2,1)S(1)}, u32[]{:S(2)}, u32[]{:S(2)}) collective-permute-start(bf16[2,128,768]{2,1,0:T(8,128)(2,1)} %refs_5_.1), channel_id=1, source_target_pairs={{0,8},{2,6},{4,0},{6,14},{8,16},{10,2},{12,4},{14,22},{16,24},{18,... | collective-permute-start | bytes 1179656 | tf_op jit(solution)/shard_map/ppermute | solution.py:430
  3.7 9.6 %collective-permute-start.3 = (bf16[2,128,768]{2,1,0:T(8,128)(2,1)}, bf16[2,128,768]{2,1,0:T(8,128)(2,1)S(1)}, u32[]{:S(2)}, u32[]{:S(2)}) collective-permute-start(bf16[2,128,768]{2,1,0:T(8,128)(2,1)} %refs_5_.1), channel_id=1, source_target_pairs={{0,4},{2,10},{4,12},{6,2},{8,0},{10,18},{12,20},{14,6},{16,8},{18,... | collective-permute-start | bytes 1179656 | tf_op jit(solution)/shard_map/ppermute | solution.py:430
  9.4 26.0 %collective-permute-start = (bf16[240,2304]{1,0:T(8,128)(2,1)S(1)}, bf16[240,2304]{1,0:T(8,128)(2,1)S(1)}, u32[]{:S(2)}, u32[]{:S(2)}) collective-permute-start(bf16[240,2304]{1,0:T(8,128)(2,1)S(1)} %get-tuple-element.35), channel_id=1, source_target_pairs={{0,1},{1,0},{2,3},{3,2},{4,5},{5,4},{6,7},{7,6},{8,9},{9,8},{10,11... | collective-permute-start | bytes 3317768 | tf_op jit(solution)/shard_map/ppermute | solution.py:467
  13.3 11.3 %collective-permute-start.4 = (bf16[2,128,768]{2,1,0:T(8,128)(2,1)S(1)}, bf16[2,128,768]{2,1,0:T(8,128)(2,1)S(1)}, u32[]{:S(2)}, u32[]{:S(2)}) collective-permute-start(bf16[2,128,768]{2,1,0:T(8,128)(2,1)S(1)} %collective-permute-done.2.refs_0_), channel_id=1, source_target_pairs={{0,8},{2,6},{4,0},{6,14},{8,16},{10,2},{12,4},{14,22},{16,24},{18,... | collective-permute-start | bytes 1179656 | tf_op jit(solution)/shard_map/ppermute | solution.py:430
  14.8 10.1 %collective-permute-start.5 = (bf16[2,128,768]{2,1,0:T(8,128)(2,1)S(1)}, bf16[2,128,768]{2,1,0:T(8,128)(2,1)S(1)}, u32[]{:S(2)}, u32[]{:S(2)}) collective-permute-start(bf16[2,128,768]{2,1,0:T(8,128)(2,1)S(1)} %collective-permute-done.3.refs_1_), channel_id=1, source_target_pairs={{0,4},{2,10},{4,12},{6,2},{8,0},{10,18},{12,20},{14,6},{16,8},{18,... | collective-permute-start | bytes 1179656 | tf_op jit(solution)/shard_map/ppermute | solution.py:430
  25.0 12.0 %collective-permute-start.6 = (bf16[2,128,768]{2,1,0:T(8,128)(2,1)S(1)}, bf16[2,128,768]{2,1,0:T(8,128)(2,1)S(1)}, u32[]{:S(2)}, u32[]{:S(2)}) collective-permute-start(bf16[2,128,768]{2,1,0:T(8,128)(2,1)S(1)} %collective-permute-done.4.refs_2_), channel_id=1, source_target_pairs={{0,8},{2,6},{4,0},{6,14},{8,16},{10,2},{12,4},{14,22},{16,24},{18,... | collective-permute-start | bytes 1179656 | tf_op jit(solution)/shard_map/ppermute | solution.py:430
  26.7 12.5 %collective-permute-start.7 = (bf16[2,128,768]{2,1,0:T(8,128)(2,1)S(1)}, bf16[2,128,768]{2,1,0:T(8,128)(2,1)S(1)}, u32[]{:S(2)}, u32[]{:S(2)}) collective-permute-start(bf16[2,128,768]{2,1,0:T(8,128)(2,1)S(1)} %collective-permute-done.5.refs_3_), channel_id=1, source_target_pairs={{0,4},{2,10},{4,12},{6,2},{8,0},{10,18},{12,20},{14,6},{16,8},{18,... | collective-permute-start | bytes 1179656 | tf_op jit(solution)/shard_map/ppermute | solution.py:430
  36.9 2.3 %collective-permute-start.1 = (bf16[128,768]{1,0:T(8,128)(2,1)S(1)}, bf16[128,768]{1,0:T(8,128)(2,1)S(1)}, u32[]{:S(2)}, u32[]{:S(2)}) collective-permute-start(bf16[128,768]{1,0:T(8,128)(2,1)S(1)} %get-tuple-element.39.qo_ref), channel_id=1, source_target_pairs={{0,2},{2,0},{4,6},{6,4},{8,10},{10,8},{12,14},{14,12},{16,18},{18,... | collective-permute-start | bytes 589832 | tf_op jit(solution)/shard_map/ppermute | solution.py:505
  36.9 7.8 %collective-permute-start.8 = (bf16[2,128,768]{2,1,0:T(8,128)(2,1)S(1)}, bf16[2,128,768]{2,1,0:T(8,128)(2,1)S(1)}, u32[]{:S(2)}, u32[]{:S(2)}) collective-permute-start(bf16[2,128,768]{2,1,0:T(8,128)(2,1)S(1)} %collective-permute-done.6.refs_4_), channel_id=1, source_target_pairs={{0,8},{2,6},{4,0},{6,14},{8,16},{10,2},{12,4},{14,22},{16,24},{18,... | collective-permute-start | bytes 1179656 | tf_op jit(solution)/shard_map/ppermute | solution.py:496
  45.2 1.6 %collective-permute-start.9 = (f32[128,512]{1,0:T(8,128)S(1)}, f32[128,512]{1,0:T(8,128)S(1)}, u32[]{:S(2)}, u32[]{:S(2)}) collective-permute-start(f32[128,512]{1,0:T(8,128)S(1)} %get-tuple-element.52), channel_id=1, source_target_pairs={{0,2},{2,0},{4,6},{6,4},{8,10},{10,8},{12,14},{14,12},{16,18},{18,... | collective-permute-start | bytes 786440 | tf_op jit(solution)/shard_map/ppermute | solution.py:546
  45.8 2.8 %collective-permute-start.10 = (f32[128,512]{1,0:T(8,128)S(1)}, f32[128,512]{1,0:T(8,128)S(1)}, u32[]{:S(2)}, u32[]{:S(2)}) collective-permute-start(f32[128,512]{1,0:T(8,128)S(1)} %get-tuple-element.56), channel_id=1, source_target_pairs={{0,2},{2,0},{4,6},{6,4},{8,10},{10,8},{12,14},{14,12},{16,18},{18,... | collective-permute-start | bytes 786440 | tf_op jit(solution)/shard_map/ppermute | solution.py:546
  47.0 5.5 %collective-permute-start.11 = (bf16[128,384]{1,0:T(8,128)(2,1)S(1)}, bf16[128,384]{1,0:T(8,128)(2,1)S(1)}, u32[]{:S(2)}, u32[]{:S(2)}) collective-permute-start(bf16[128,384]{1,0:T(8,128)(2,1)S(1)} %merge.2.first_ref), channel_id=1, source_target_pairs={{0,1},{1,0},{2,3},{3,2},{4,5},{5,4},{6,7},{7,6},{8,9},{9,8},{10,11... | collective-permute-start | bytes 294920 | tf_op jit(solution)/shard_map/ppermute | solution.py:554
  48.8 5.2 %collective-permute-start.12 = (bf16[128,384]{1,0:T(8,128)(2,1)S(1)}, bf16[128,384]{1,0:T(8,128)(2,1)S(1)}, u32[]{:S(2)}, u32[]{:S(2)}) collective-permute-start(bf16[128,384]{1,0:T(8,128)(2,1)S(1)} %merge.3.second_ref), channel_id=1, source_target_pairs={{0,1},{1,0},{2,3},{3,2},{4,5},{5,4},{6,7},{7,6},{8,9},{9,8},{10,11... | collective-permute-start | bytes 294920 | tf_op jit(solution)/shard_map/ppermute | solution.py:554

commit v8 on v7

--- a/solution.py
+++ b/solution.py
@@ -41,7 +41,7 @@
 
 def send_kernel(
     place_ref, x_ref, t_ref, scale_ref, shift_ref, w_ref,
-    a_ref, msg_ref, stat_ref, ahead_ref,
+    a_ref, msg_ref, tmsg_ref, stat_ref, ahead_ref,
     x_buffer, t_buffer, scale_buffer, shift_buffer, w_buffer, in_sems, w_sems,
 ):
     video, features = x_buffer.shape
@@ -110,27 +110,14 @@
                 a_ref[...], w_buffer[block, :, piece * PIECE : (piece + 1) * PIECE],
                 preferred_element_type=F32,
             )
-            msg_ref[:top, start : start + PIECE] = product[:top].astype(BF16)
+            msg_ref[:, start : start + PIECE] = product[:top].astype(BF16)
             if start == 0:
                 stats = jnp.concatenate([video_stats, text_stats], axis=1)
-                msg_ref[video:top, : video + text] = (product[video:top] + stats).astype(BF16)
+                msg_ref[video:, : video + text] = (product[video:top] + stats).astype(BF16)
             for source, target in text_columns(start):
-                part = product[top:, source].astype(BF16)
-                for quarter in range(4):
-                    rows, cells = text_slot(text, width, target, quarter)
-                    msg_ref[top + rows.start : top + rows.stop, cells] = part[
-                        quarter * text // 4 : (quarter + 1) * text // 4
-                    ]
+                tmsg_ref[:, target : target + HEAD_DIM] = product[top:, source].astype(BF16)
     for copy in w_copies[blocks:]:
         copy.wait()
-
-
-def text_slot(text, width, column, quarter):
-    slots = width // PIECE
-    band, slot = divmod(column // PIECE * 4 + quarter, slots)
-    depth = text // 4
-    start = slot * PIECE + column % PIECE
-    return slice(band * depth, (band + 1) * depth), slice(start, start + HEAD_DIM)
 
 
 def text_columns(first):
@@ -235,10 +222,10 @@
         kv_ref[1, :, columns] = values
 
 
-def text_kernel(total_features, own_ref, msg_ref, stat_ref, top_ref, kg_ref, kv_ref):
+def text_kernel(total_features, own_ref, tmsg_ref, stat_ref, top_ref, msg_ref, kg_ref, kv_ref):
     text = kv_ref.shape[1]
     heads = kv_ref.shape[2] // HEAD_DIM
-    top, width = top_ref.shape
+    top = top_ref.shape[0]
     video = top - EXTRA
     key_gain = kg_ref[...].reshape(1, HEAD_DIM)
     gap, inverse = row_stats(
@@ -249,12 +236,7 @@
         pair = slice(head * PIECE, (head + 1) * PIECE)
         columns = slice(head * HEAD_DIM, (head + 1) * HEAD_DIM)
         scale, shift = column_terms(top_ref[video:, part], msg_ref[video:top, part])
-        other = []
-        for quarter in range(4):
-            rows, cells = text_slot(text, width, head * PIECE, quarter)
-            cells = slice(cells.start, cells.start + PIECE)
-            other.append(msg_ref[top + rows.start : top + rows.stop, cells])
-        total = own_ref[:, pair] + jnp.concatenate(other, axis=0).astype(F32)
+        total = own_ref[:, pair] + tmsg_ref[:, pair].astype(F32)
         total = (total + gap * scale) * inverse + shift
         kv_ref[0, :, columns] = head_norm(total[:, :HEAD_DIM], key_gain).astype(BF16)
         kv_ref[1, :, columns] = total[:, HEAD_DIM:].astype(BF16)
@@ -290,16 +272,24 @@
     return num, den
 
 
-def first_kernel(place_ref, qo_ref, qp_ref, fresh_ref, stale_ref, text_ref, mask_ref, *refs):
+def split_kernel(*refs):
+    count = len(refs) // 3
+    for index in range(count):
+        half = refs[index].shape[2] // 2
+        refs[count + 2 * index][...] = refs[index][:, :, :half]
+        refs[count + 2 * index + 1][...] = refs[index][:, :, half:]
+
+
+def first_kernel(count, qo_ref, qp_ref, fresh_ref, stale_ref, *refs):
     num_ref, den_ref = refs[-2:]
+    whole, halves = refs[:count], refs[count:-2]
     video, width = qo_ref.shape
-    text = text_ref.shape[1]
     lane = lax.broadcasted_iota(jnp.int32, (2 * video, HEAD_DIM), 1)
-    mask = mask_ref[...].reshape(1, 2 * text).astype(F32)
-    mask = jnp.where(place_ref[1] == 0, mask[:, :text], mask[:, text:])
     packed = jnp.zeros((2 * video, HEAD_DIM), F32)
     for head in range(width // HEAD_DIM):
         columns = slice(head * HEAD_DIM, (head + 1) * HEAD_DIM)
+        second, start = divmod(head * HEAD_DIM, width // 2)
+        cells = slice(start, start + HEAD_DIM)
         own, other = qo_ref[:, columns], qp_ref[:, columns]
         queries = jnp.concatenate([own, other], axis=0)
         fresh = weigh(own, fresh_ref[0, :, columns])
@@ -308,26 +298,32 @@
             [times(fresh, fresh_ref[1, :, columns]), times(stale, stale_ref[1, :, columns])], axis=0
         )
         den = jnp.concatenate([fresh, stale], axis=0)
-        weights = weigh(queries, text_ref[0, :, columns]) * mask
-        num = num + times(weights, text_ref[1, :, columns])
-        den = den + lanes(weights)
-        num, den = absorb(queries, [(ref, columns) for ref in refs[:-2]], num, den)
+        blocks = [(ref, columns) for ref in whole] + [(ref, cells) for ref in halves[second::2]]
+        num, den = absorb(queries, blocks, num, den)
         num_ref[:, columns] = num
         packed = jnp.where(lane == head, jnp.sum(den, axis=1, keepdims=True), packed)
     den_ref[...] = packed
 
 
-def last_kernel(first, qo_ref, qp_ref, num_ref, den_ref, far_ref, own_ref, own_den_ref, msg_ref):
+def last_kernel(
+    first, place_ref, qo_ref, qp_ref, num_ref, den_ref, text_ref, mask_ref, far_ref,
+    own_ref, own_den_ref, msg_ref,
+):
     video = qo_ref.shape[0]
-    width = own_ref.shape[1]
+    text, width = text_ref.shape[1], far_ref.shape[2]
     lane = lax.broadcasted_iota(jnp.int32, (2 * video, HEAD_DIM), 1)
+    mask = mask_ref[...].reshape(1, 2 * text).astype(F32)
+    mask = jnp.where(place_ref[1] == 0, mask[:, :text], mask[:, text:])
+    keep = jnp.concatenate([mask, jnp.ones((1, video), F32)], axis=1)
     packed = den_ref[...]
     for head in range(width // HEAD_DIM):
         cells = slice(head * HEAD_DIM, (head + 1) * HEAD_DIM)
         columns = slice((first + head) * HEAD_DIM, (first + head + 1) * HEAD_DIM)
         queries = jnp.concatenate([qo_ref[:, columns], qp_ref[:, columns]], axis=0)
-        weights = weigh(queries, far_ref[0, :, columns])
-        num = num_ref[:, columns] + times(weights, far_ref[1, :, columns])
+        keys = jnp.concatenate([text_ref[0, :, columns], far_ref[0, :, cells]], axis=0)
+        values = jnp.concatenate([text_ref[1, :, columns], far_ref[1, :, cells]], axis=0)
+        weights = weigh(queries, keys) * keep
+        num = num_ref[:, columns] + times(weights, values)
         own_ref[:, cells] = num[:video]
         msg_ref[:, cells] = num[video:]
         total = jnp.sum(lanes(weights), axis=1, keepdims=True)
@@ -432,21 +428,20 @@
     vmem = pl.BlockSpec(memory_space=pltpu.VMEM)
     hbm = pl.BlockSpec(memory_space=pltpu.HBM)
     smem = pl.BlockSpec(memory_space=pltpu.SMEM)
-    ring = [ring_step((stale_cache, stale_cache))]
+    whole = ring_step((stale_cache, stale_cache))
 
     columns = 2 * TRIPLE
     blocks = group_columns // columns
     ahead = blocks - 1
-    bands = -(-heads * 4 // (group_columns // PIECE))
-    message_rows = top + bands * text // 4
     project_cost = cost(8 * rows * features * group_columns, 2 * features * group_columns)
-    a_rows, message, stats, w_ahead = pl.pallas_call(
+    a_rows, message, text_message, stats, w_ahead = pl.pallas_call(
         send_kernel,
         in_specs=[smem] + [hbm] * 5,
-        out_specs=[vmem] * 4,
+        out_specs=[vmem] * 5,
         out_shape=[
             jax.ShapeDtypeStruct((rows, features), BF16),
-            jax.ShapeDtypeStruct((message_rows, group_columns), BF16),
+            jax.ShapeDtypeStruct((top, group_columns), BF16),
+            jax.ShapeDtypeStruct((text, 2 * width), BF16),
             jax.ShapeDtypeStruct((rows, HEAD_DIM), F32),
             jax.ShapeDtypeStruct((ahead, features, columns), BF16),
         ],
@@ -465,7 +460,11 @@
     )(place, *map(in_hbm, (hidden, text_hidden, norm_scale, norm_shift, qkv_weight)))
 
     received = lax.ppermute(message, "head", swap_head)
-    ring.append(ring_step(lax.optimization_barrier((*ring[-1], message))[:2]))
+    split = plain_call(
+        split_kernel, [((2, video, width // 2), BF16)] * 4, "split_heads", cost(0, 8 * video * width),
+        *lax.optimization_barrier((*whole, message))[:2],
+    )
+    chains = [[ring_step((split[0], split[2]))], [ring_step((split[1], split[3]))]]
 
     small = (query_gain, key_gain, text_mask, branch_gate, hidden, stale_cache)
     outs = pl.pallas_call(
@@ -492,9 +491,11 @@
     query_gain, key_gain, text_mask, branch_gate, hidden, stale = outs[4:]
 
     for _ in range(half_way - 3):
-        ring.append(ring_step(lax.optimization_barrier((*ring[-1], own))[:2]))
-    far = lax.ppermute(ring[-1][0], "section", ways[0])
-
+        for chain in chains:
+            chain.append(ring_step(lax.optimization_barrier((*chain[-1], own))[:2]))
+    far = [lax.ppermute(chain[-1][0], "section", ways[0]) for chain in chains]
+
+    received = lax.optimization_barrier((received, *chains[0][0], *chains[1][0]))[0]
     queries, new_cache, fresh = plain_call(
         functools.partial(norm_kernel, features * 2),
         [((video, width), BF16), ((2, video, width), BF16), ((2, video, width), BF16)],
@@ -503,46 +504,53 @@
         own, received, stats, query_gain, key_gain,
     )
     other_queries = lax.ppermute(queries, "section", swap_core)
+    text_received = lax.ppermute(
+        lax.optimization_barrier((text_message, queries))[0], "head", swap_head
+    )
+
+    halves = [
+        block
+        for steps in zip(*chains)
+        for way in range(2)
+        for block in (steps[0][way], steps[1][way])
+    ]
+    context = (len(halves) // 2 + 3) * video
+    num, den = plain_call(
+        functools.partial(first_kernel, 2),
+        [((2 * video, width), F32), ((2 * video, HEAD_DIM), F32)],
+        "attend_first",
+        cost(32 * video * context * width, 4 * context * width, 2 * video * context * heads),
+        queries, other_queries, fresh, stale, *whole, *halves,
+    )
     (text_kv,) = plain_call(
         functools.partial(text_kernel, features * 2),
         [((2, text, width), BF16)],
         "norm_text",
         cost(1000 * text * group_columns, 8 * text * group_columns),
-        own_text, received, stats, own, key_gain,
-    )
-
-    arrived = [block for step in ring for block in step]
-    context = (len(arrived) + 1) * video + text
-    num, den = pl.pallas_call(
-        first_kernel,
-        in_specs=[smem] + [vmem] * (6 + len(arrived)),
-        out_specs=[vmem] * 2,
-        out_shape=[
-            jax.ShapeDtypeStruct((2 * video, width), F32),
-            jax.ShapeDtypeStruct((2 * video, HEAD_DIM), F32),
-        ],
-        compiler_params=params(24),
-        cost_estimate=cost(
-            32 * video * context * width, 4 * context * width, 2 * video * context * heads
-        ),
-        name="attend_first",
-    )(place, queries, other_queries, fresh, stale, text_kv, text_mask, *arrived)
-
+        own_text, text_received, stats, own, received, key_gain,
+    )
+
+    last_context = video + text
     attended, other_attended = [], []
-    for first in (0, heads // 2):
+    for index, block in enumerate(far):
+        first = index * heads // 2
         if attended:
             num = lax.optimization_barrier((num, num_own))[0]
-        num_own, den_own, num_message = plain_call(
+        num_own, den_own, num_message = pl.pallas_call(
             functools.partial(last_kernel, first),
-            [
-                ((video, width // 2), F32),
-                ((video, HEAD_DIM), F32),
-                ((video, width // 2 + HEAD_DIM), F32),
+            in_specs=[smem] + [vmem] * 7,
+            out_specs=[vmem] * 3,
+            out_shape=[
+                jax.ShapeDtypeStruct((video, width // 2), F32),
+                jax.ShapeDtypeStruct((video, HEAD_DIM), F32),
+                jax.ShapeDtypeStruct((video, width // 2 + HEAD_DIM), F32),
             ],
-            "attend_last",
-            cost(16 * video * video * width, 6 * video * width, video * video * heads),
-            queries, other_queries, num, den, far,
-        )
+            compiler_params=params(24),
+            cost_estimate=cost(
+                16 * video * last_context * width, 6 * video * width, video * last_context * heads
+            ),
+            name="attend_last",
+        )(place, queries, other_queries, num, den, text_kv, text_mask, block)
         num_received = lax.ppermute(num_message, "section", swap_core)
         attended += plain_call(
             functools.partial(merge_kernel, first),

time: 55.3 us -> 54.3 us (0.982)
  waiting for transfers between devices: 19.9 us -> 8.94 us
  starting transfers between devices: 14.2 us -> 23.6 us
    ppermute x1, waiting for transfers between devices: 8.26 us -> 0.01 us  [per_device(): received = lax.ppermute(message, 'head', swap_head)]
    ppermute x6 -> x10, starting transfers between devices: 7.66 us -> 13 us  [ring_step(): lax.ppermute(block, 'section', way)]
    ppermute x1 -> x3, starting transfers between devices: 1.68 us -> 5.35 us  [the longest x2 3.85 us: per_device(): far = [lax.ppermute(chain[-1][0], 'section', ways[0]) for chain in chains]]
    ppermute x6 -> x10, waiting for transfers between devices: 6.08 us -> 2.82 us  [ring_step(): lax.ppermute(block, 'section', way)]
    pallas_call x9, Pallas kernels: 5.44 us -> 7.77 us  [plain_call(): pl.pallas_call(kernel, in_specs=[pl.BlockSpec(memory_space=pltpu.VMEM)] *...]
    pallas_call x1 -> x2, Pallas kernels: 4.03 us -> 2.29 us  [per_device(): pl.pallas_call(functools.partial(last_kernel, first), in_specs=[smem] + [...]
    ppermute x1 -> x3, waiting for transfers between devices: 1.45 us -> 2.91 us  [the longest x1 2.91 us: per_device(): lax.ppermute(lax.optimization_barrier((text_message, queries))[0], 'head'...]
  transfers between devices with their start and end apart: 13 -> 19, of which waited for: 8 -> 6; matrix products, arithmetic and copies ran while one was open for 0% -> 0% of each run, Pallas kernels for 34% -> 36%
where the time goes in v8:
time: 54.3 us; the launch traced here: 54.1 us
  starting transfers between devices  23.6 us (43%)
  Pallas kernels  20.7 us (38%)
  waiting for transfers between devices  8.94 us (16%)
  between operations  0.76 us (1%)
    ppermute x10, starting transfers between devices, ring_step(): lax.ppermute(block, 'section', way)  13 us
    pallas_call x9, Pallas kernels, plain_call(): pl.pallas_call(kernel, in_specs=[pl.BlockSpec(memory_space=pltpu.VMEM)] *...  7.77 us
    pallas_call x1, Pallas kernels, per_device(): pl.pallas_call(send_kernel, in_specs=[smem] + [hbm] * 5, out_specs=[vmem]...  5.64 us
    pallas_call x1, Pallas kernels, per_device(): pl.pallas_call(own_kernel, in_specs=[smem, vmem, vmem, hbm, hbm] + [hbm]...  5.05 us
    ppermute x2, starting transfers between devices, per_device(): far = [lax.ppermute(chain[-1][0], 'section', ways[0]) for chain in chains]  3.85 us
    ppermute x2, waiting for transfers between devices, per_device(): other_attended.append(lax.ppermute(attended[-1], 'head', swap_head))  3.2 us
    ppermute x1, waiting for transfers between devices, per_device(): lax.ppermute(lax.optimization_barrier((text_message, queries))[0], 'head'...  2.91 us
    ppermute x10, waiting for transfers between devices, ring_step(): lax.ppermute(block, 'section', way)  2.82 us
  transfers between devices with their start and end apart: 19, of which 6 were waited for; matrix products, arithmetic and copies ran while one was open for 0% of the time, Pallas kernels for 36%

profile of v8, /device:TPU:0, one launch (start us, length us, event | category | flops | bytes accessed | tf_op | source)
XLA Modules:
  0.0 54.1 jit_solution(7938680720882773115)
XLA Ops:
  0.6 3.1 %collective-permute-start.1 = (bf16[2,128,768]{2,1,0:T(8,128)(2,1)}, bf16[2,128,768]{2,1,0:T(8,128)(2,1)S(1)}, u32[]{:S(2)}, u32[]{:S(2)}) collective-permute-start(bf16[2,128,768]{2,1,0:T(8,128)(2,1)} %refs_5_.1), channel_id=1, source_target_pairs={{0,8},{2,6},{4,0},{6,14},{8,16},{10,2},{12,4},{14,22},{16,24},{18,... | collective-permute-start | bytes 1179656 | tf_op jit(solution)/shard_map/ppermute | solution.py:426
  3.8 5.6 %project_send.1 = (bf16[272,1536]{1,0:T(8,128)(2,1)S(1)}, bf16[144,2304]{1,0:T(8,128)(2,1)S(1)}, bf16[128,1536]{1,0:T(8,128)(2,1)S(1)}, f32[272,128]{1,0:T(8,128)S(1)}, bf16[2,1536,768]{2,1,0:T(8,128)(2,1)S(1)}) custom-call(s32[2]{0:T(128)S(1)} %pad_add_fusion.place_ref, bf16[128,1536]{1,0:T(8,128)(2,1)} %refs_4_.1, bf16[256,1536]{1,0:T(8,128)(2,1)} %t_ref.1, ...), custom_call_target="tpu_custom_call" | custom-call | flops 7700742144 | bytes 7077888 | tf_op jit(solution)/shard_map/project_send/pallas_call | solution.py:437
  9.4 2.0 %collective-permute-start = (bf16[144,2304]{1,0:T(8,128)(2,1)S(1)}, bf16[144,2304]{1,0:T(8,128)(2,1)S(1)}, u32[]{:S(2)}, u32[]{:S(2)}) collective-permute-start(bf16[144,2304]{1,0:T(8,128)(2,1)S(1)} %get-tuple-element.44), channel_id=1, source_target_pairs={{0,1},{1,0},{2,3},{3,2},{4,5},{5,4},{6,7},{7,6},{8,9},{9,8},{10,11... | collective-permute-start | bytes 1990664 | tf_op jit(solution)/shard_map/ppermute | solution.py:462
  11.4 1.9 %collective-permute-done.1.refs_0_ = bf16[2,128,768]{2,1,0:T(8,128)(2,1)S(1)} collective-permute-done((bf16[2,128,768]{2,1,0:T(8,128)(2,1)}, bf16[2,128,768]{2,1,0:T(8,128)(2,1)S(1)}, u32[]{:S(2)}, u32[]{:S(2)}) %collective-permute-start.1) | collective-permute-done | bytes 393248 | tf_op jit(solution)/shard_map/ppermute | solution.py:426
  13.4 1.6 %collective-permute-start.3 = (bf16[2,128,384]{2,1,0:T(8,128)(2,1)S(1)}, bf16[2,128,384]{2,1,0:T(8,128)(2,1)S(1)}, u32[]{:S(2)}, u32[]{:S(2)}) collective-permute-start(bf16[2,128,384]{2,1,0:T(8,128)(2,1)S(1)} %get-tuple-element.47), channel_id=1, source_target_pairs={{0,8},{2,6},{4,0},{6,14},{8,16},{10,2},{12,4},{14,22},{16,24},{18,... | collective-permute-start | bytes 589832 | tf_op jit(solution)/shard_map/ppermute | solution.py:426
  15.0 0.9 %collective-permute-start.4 = (bf16[2,128,384]{2,1,0:T(8,128)(2,1)S(1)}, bf16[2,128,384]{2,1,0:T(8,128)(2,1)S(1)}, u32[]{:S(2)}, u32[]{:S(2)}) collective-permute-start(bf16[2,128,384]{2,1,0:T(8,128)(2,1)S(1)} %get-tuple-element.48), channel_id=1, source_target_pairs={{0,4},{2,10},{4,12},{6,2},{8,0},{10,18},{12,20},{14,6},{16,8},{18,... | collective-permute-start | bytes 589832 | tf_op jit(solution)/shard_map/ppermute | solution.py:426
  15.9 1.1 %collective-permute-start.5 = (bf16[2,128,384]{2,1,0:T(8,128)(2,1)S(1)}, bf16[2,128,384]{2,1,0:T(8,128)(2,1)S(1)}, u32[]{:S(2)}, u32[]{:S(2)}) collective-permute-start(bf16[2,128,384]{2,1,0:T(8,128)(2,1)S(1)} %get-tuple-element.49), channel_id=1, source_target_pairs={{0,8},{2,6},{4,0},{6,14},{8,16},{10,2},{12,4},{14,22},{16,24},{18,... | collective-permute-start | bytes 589832 | tf_op jit(solution)/shard_map/ppermute | solution.py:426
  17.9 5.0 %project_own.1 = (f32[144,2304]{1,0:T(8,128)S(1)}, f32[128,1536]{1,0:T(8,128)S(1)}, bf16[768,1536]{1,0:T(8,128)(2,1)S(1)}, bf16[768,1536]{1,0:T(8,128)(2,1)S(1)}...) custom-call(s32[2]{0:T(128)S(1)} %pad_add_fusion.place_ref, ...), custom_call_target="tpu_custom_call" | custom-call | flops 7700742144 | bytes 7077888 | tf_op jit(solution)/shard_map/project_own/pallas_call | solution.py:470
  23.0 1.2 %collective-permute-start.8 = (bf16[2,128,384]{2,1,0:T(8,128)(2,1)S(1)}, bf16[2,128,384]{2,1,0:T(8,128)(2,1)S(1)}, u32[]{:S(2)}, u32[]{:S(2)}) collective-permute-start(bf16[2,128,384]{2,1,0:T(8,128)(2,1)S(1)} %collective-permute-done.3.refs_2_), channel_id=1, source_target_pairs={{0,8},{2,6},{4,0},{6,14},{8,16},{10,2},{12,4},{14,22},{16,24},{18,... | collective-permute-start | bytes 589832 | tf_op jit(solution)/shard_map/ppermute | solution.py:426
  25.1 1.7 %collective-permute-start.9 = (bf16[2,128,384]{2,1,0:T(8,128)(2,1)S(1)}, bf16[2,128,384]{2,1,0:T(8,128)(2,1)S(1)}, u32[]{:S(2)}, u32[]{:S(2)}) collective-permute-start(bf16[2,128,384]{2,1,0:T(8,128)(2,1)S(1)} %collective-permute-done.5.refs_3_), channel_id=1, source_target_pairs={{0,8},{2,6},{4,0},{6,14},{8,16},{10,2},{12,4},{14,22},{16,24},{18,... | collective-permute-start | bytes 589832 | tf_op jit(solution)/shard_map/ppermute | solution.py:426
  27.3 2.0 %collective-permute-start.11 = (bf16[2,128,384]{2,1,0:T(8,128)(2,1)S(1)}, bf16[2,128,384]{2,1,0:T(8,128)(2,1)S(1)}, u32[]{:S(2)}, u32[]{:S(2)}) collective-permute-start(bf16[2,128,384]{2,1,0:T(8,128)(2,1)S(1)} %collective-permute-done.6.refs_5_), channel_id=1, source_target_pairs={{0,4},{2,10},{4,12},{6,2},{8,0},{10,18},{12,20},{14,6},{16,8},{18,... | collective-permute-start | bytes 589832 | tf_op jit(solution)/shard_map/ppermute | solution.py:426
  29.3 1.5 %norm_video.1 = (bf16[128,768]{1,0:T(8,128)(2,1)S(1)}, bf16[2,128,768]{2,1,0:T(8,128)(2,1)}, bf16[2,128,768]{2,1,0:T(8,128)(2,1)S(1)}) custom-call(f32[144,2304]{1,0:T(8,128)S(1)} %get-tuple-element.43.own_ref.top_ref, bf16[144,2304]{1,0:T(8,128)(2,1)S(1)} %collective-permute-done.msg_ref, f32[272,128]{1,0:T(8,128)S(1)} %get-tuple-element.52.stat_ref, ...), custom_call_target="tpu_custom_call" | custom-call | flops 331776000 | bytes 2654208 | tf_op jit(solution)/shard_map/norm_video/pallas_call | solution.py:381
  30.9 1.5 %collective-permute-start.12 = (bf16[128,1536]{1,0:T(8,128)(2,1)S(1)}, bf16[128,1536]{1,0:T(8,128)(2,1)S(1)}, u32[]{:S(2)}, u32[]{:S(2)}) collective-permute-start(bf16[128,1536]{1,0:T(8,128)(2,1)S(1)} %get-tuple-element.66), channel_id=1, source_target_pairs={{0,1},{1,0},{2,3},{3,2},{4,5},{5,4},{6,7},{7,6},{8,9},{9,8},{10,11... | collective-permute-start | bytes 1179656 | tf_op jit(solution)/shard_map/ppermute | solution.py:507
  32.4 2.2 %collective-permute-start.13 = (bf16[2,128,384]{2,1,0:T(8,128)(2,1)S(1)}, bf16[2,128,384]{2,1,0:T(8,128)(2,1)S(1)}, u32[]{:S(2)}, u32[]{:S(2)}) collective-permute-start(bf16[2,128,384]{2,1,0:T(8,128)(2,1)S(1)} %collective-permute-done.8.refs_6_), channel_id=1, source_target_pairs={{0,8},{2,6},{4,0},{6,14},{8,16},{10,2},{12,4},{14,22},{16,24},{18,... | collective-permute-start | bytes 589832 | tf_op jit(solution)/shard_map/ppermute | solution.py:496
  34.6 1.6 %collective-permute-start.15 = (bf16[2,128,384]{2,1,0:T(8,128)(2,1)S(1)}, bf16[2,128,384]{2,1,0:T(8,128)(2,1)S(1)}, u32[]{:S(2)}, u32[]{:S(2)}) collective-permute-start(bf16[2,128,384]{2,1,0:T(8,128)(2,1)S(1)} %collective-permute-done.9.refs_7_), channel_id=1, source_target_pairs={{0,8},{2,6},{4,0},{6,14},{8,16},{10,2},{12,4},{14,22},{16,24},{18,... | collective-permute-start | bytes 589832 | tf_op jit(solution)/shard_map/ppermute | solution.py:496
  36.2 3.3 %attend_first.1 = (f32[256,768]{1,0:T(8,128)S(1)}, f32[256,128]{1,0:T(8,128)S(1)}) custom-call(bf16[128,768]{1,0:T(8,128)(2,1)S(1)} %get-tuple-element.55.qo_ref, bf16[128,768]{1,0:T(8,128)(2,1)S(1)} %collective-permute-done.7.qp_ref, bf16[2,128,768]{2,1,0:T(8,128)(2,1)S(1)} %get-tuple-element.56.fresh_ref, ...), custom_call_target="tpu_custom_call" | custom-call | flops 2818572288 | bytes 2752512 | tf_op jit(solution)/shard_map/attend_first/pallas_call | solution.py:381
  39.5 2.9 %collective-permute-done.12.tmsg_ref = bf16[128,1536]{1,0:T(8,128)(2,1)S(1)} collective-permute-done((bf16[128,1536]{1,0:T(8,128)(2,1)S(1)}, bf16[128,1536]{1,0:T(8,128)(2,1)S(1)}, u32[]{:S(2)}, u32[]{:S(2)}) %collective-permute-start.12) | collective-permute-done | bytes 393248 | tf_op jit(solution)/shard_map/ppermute | solution.py:507
  43.0 1.1 %attend_last.2 = (f32[128,384]{1,0:T(8,128)S(1)}, f32[128,128]{1,0:T(8,128)S(1)}, f32[128,512]{1,0:T(8,128)S(1)}) custom-call(s32[2]{0:T(128)S(1)} %pad_add_fusion.place_ref, bf16[128,768]{1,0:T(8,128)(2,1)S(1)} %get-tuple-element.55.qo_ref, bf16[128,768]{1,0:T(8,128)(2,1)S(1)} %collective-permute-done.7.qp_ref, f32[256,768]{1,0:T(8,128)S(1)} %get-tuple-element.71.num_ref, ...), custom_call_target="tpu_custom_call" | custom-call | flops 402653184 | bytes 589824 | tf_op jit(solution)/shard_map/attend_last/pallas_call | solution.py:539
  44.2 1.1 %attend_last.3 = (f32[128,384]{1,0:T(8,128)S(1)}, f32[128,128]{1,0:T(8,128)S(1)}, f32[128,512]{1,0:T(8,128)S(1)}) custom-call(s32[2]{0:T(128)S(1)} %pad_add_fusion.place_ref, bf16[128,768]{1,0:T(8,128)(2,1)S(1)} %get-tuple-element.55.qo_ref, bf16[128,768]{1,0:T(8,128)(2,1)S(1)} %collective-permute-done.7.qp_ref, f32[256,768]{1,0:T(8,128)S(1)} %get-tuple-element.71.num_ref, ...), custom_call_target="tpu_custom_call" | custom-call | flops 402653184 | bytes 589824 | tf_op jit(solution)/shard_map/attend_last/pallas_call | solution.py:539
  46.1 1.6 %collective-permute-start.17 = (bf16[128,384]{1,0:T(8,128)(2,1)S(1)}, bf16[128,384]{1,0:T(8,128)(2,1)S(1)}, u32[]{:S(2)}, u32[]{:S(2)}) collective-permute-start(bf16[128,384]{1,0:T(8,128)(2,1)S(1)} %merge.2.first_ref), channel_id=1, source_target_pairs={{0,1},{1,0},{2,3},{3,2},{4,5},{5,4},{6,7},{7,6},{8,9},{9,8},{10,11... | collective-permute-start | bytes 294920 | tf_op jit(solution)/shard_map/ppermute | solution.py:562
  47.8 1.0 %collective-permute-start.18 = (bf16[128,384]{1,0:T(8,128)(2,1)S(1)}, bf16[128,384]{1,0:T(8,128)(2,1)S(1)}, u32[]{:S(2)}, u32[]{:S(2)}) collective-permute-start(bf16[128,384]{1,0:T(8,128)(2,1)S(1)} %merge.3.second_ref), channel_id=1, source_target_pairs={{0,1},{1,0},{2,3},{3,2},{4,5},{5,4},{6,7},{7,6},{8,9},{9,8},{10,11... | collective-permute-start | bytes 294920 | tf_op jit(solution)/shard_map/ppermute | solution.py:562
  49.4 2.1 %collective-permute-done.17.att_ref = bf16[128,384]{1,0:T(8,128)(2,1)S(1)} collective-permute-done((bf16[128,384]{1,0:T(8,128)(2,1)S(1)}, bf16[128,384]{1,0:T(8,128)(2,1)S(1)}, u32[]{:S(2)}, u32[]{:S(2)}) %collective-permute-start.17) | collective-permute-done | bytes 98336 | tf_op jit(solution)/shard_map/ppermute | solution.py:562
  51.9 1.1 %collective-permute-done.18.att_ref = bf16[128,384]{1,0:T(8,128)(2,1)S(1)} collective-permute-done((bf16[128,384]{1,0:T(8,128)(2,1)S(1)}, bf16[128,384]{1,0:T(8,128)(2,1)S(1)}, u32[]{:S(2)}, u32[]{:S(2)}) %collective-permute-start.18) | collective-permute-done | bytes 98336 | tf_op jit(solution)/shard_map/ppermute | solution.py:562
  53.0 1.1 %final_out.1 = bf16[128,1536]{1,0:T(8,128)(2,1)} custom-call(f32[128,1536]{1,0:T(8,128)S(1)} %more_out.1.part_ref, bf16[128,384]{1,0:T(8,128)(2,1)S(1)} %collective-permute-done.18.att_ref, bf16[768,1536]{1,0:T(8,128)(2,1)S(1)} %get-tuple-element.76.w_ref, bf16[128,1536]{1,0:T(8,128)(2,1)S(1)} %get-tuple-element.77.hidden_ref, ...), custom_call_target="tpu_custom_call" | custom-call | flops 603979776 | bytes 2359296 | tf_op jit(solution)/shard_map/final_out/pallas_call | solution.py:381
  (28 shorter events, 5.0 us)
Async XLA Ops:
  0.6 12.7 %collective-permute-start.1 = (bf16[2,128,768]{2,1,0:T(8,128)(2,1)}, bf16[2,128,768]{2,1,0:T(8,128)(2,1)S(1)}, u32[]{:S(2)}, u32[]{:S(2)}) collective-permute-start(bf16[2,128,768]{2,1,0:T(8,128)(2,1)} %refs_5_.1), channel_id=1, source_target_pairs={{0,8},{2,6},{4,0},{6,14},{8,16},{10,2},{12,4},{14,22},{16,24},{18,... | collective-permute-start | bytes 1179656 | tf_op jit(solution)/shard_map/ppermute | solution.py:426
  3.7 9.6 %collective-permute-start.2 = (bf16[2,128,768]{2,1,0:T(8,128)(2,1)}, bf16[2,128,768]{2,1,0:T(8,128)(2,1)S(1)}, u32[]{:S(2)}, u32[]{:S(2)}) collective-permute-start(bf16[2,128,768]{2,1,0:T(8,128)(2,1)} %refs_5_.1), channel_id=1, source_target_pairs={{0,4},{2,10},{4,12},{6,2},{8,0},{10,18},{12,20},{14,6},{16,8},{18,... | collective-permute-start | bytes 1179656 | tf_op jit(solution)/shard_map/ppermute | solution.py:426
  9.4 19.9 %collective-permute-start = (bf16[144,2304]{1,0:T(8,128)(2,1)S(1)}, bf16[144,2304]{1,0:T(8,128)(2,1)S(1)}, u32[]{:S(2)}, u32[]{:S(2)}) collective-permute-start(bf16[144,2304]{1,0:T(8,128)(2,1)S(1)} %get-tuple-element.44), channel_id=1, source_target_pairs={{0,1},{1,0},{2,3},{3,2},{4,5},{5,4},{6,7},{7,6},{8,9},{9,8},{10,11... | collective-permute-start | bytes 1990664 | tf_op jit(solution)/shard_map/ppermute | solution.py:462
  13.4 9.6 %collective-permute-start.3 = (bf16[2,128,384]{2,1,0:T(8,128)(2,1)S(1)}, bf16[2,128,384]{2,1,0:T(8,128)(2,1)S(1)}, u32[]{:S(2)}, u32[]{:S(2)}) collective-permute-start(bf16[2,128,384]{2,1,0:T(8,128)(2,1)S(1)} %get-tuple-element.47), channel_id=1, source_target_pairs={{0,8},{2,6},{4,0},{6,14},{8,16},{10,2},{12,4},{14,22},{16,24},{18,... | collective-permute-start | bytes 589832 | tf_op jit(solution)/shard_map/ppermute | solution.py:426
  15.0 8.0 %collective-permute-start.4 = (bf16[2,128,384]{2,1,0:T(8,128)(2,1)S(1)}, bf16[2,128,384]{2,1,0:T(8,128)(2,1)S(1)}, u32[]{:S(2)}, u32[]{:S(2)}) collective-permute-start(bf16[2,128,384]{2,1,0:T(8,128)(2,1)S(1)} %get-tuple-element.48), channel_id=1, source_target_pairs={{0,4},{2,10},{4,12},{6,2},{8,0},{10,18},{12,20},{14,6},{16,8},{18,... | collective-permute-start | bytes 589832 | tf_op jit(solution)/shard_map/ppermute | solution.py:426
  15.9 8.9 %collective-permute-start.5 = (bf16[2,128,384]{2,1,0:T(8,128)(2,1)S(1)}, bf16[2,128,384]{2,1,0:T(8,128)(2,1)S(1)}, u32[]{:S(2)}, u32[]{:S(2)}) collective-permute-start(bf16[2,128,384]{2,1,0:T(8,128)(2,1)S(1)} %get-tuple-element.49), channel_id=1, source_target_pairs={{0,8},{2,6},{4,0},{6,14},{8,16},{10,2},{12,4},{14,22},{16,24},{18,... | collective-permute-start | bytes 589832 | tf_op jit(solution)/shard_map/ppermute | solution.py:426
  17.0 8.1 %collective-permute-start.6 = (bf16[2,128,384]{2,1,0:T(8,128)(2,1)S(1)}, bf16[2,128,384]{2,1,0:T(8,128)(2,1)S(1)}, u32[]{:S(2)}, u32[]{:S(2)}) collective-permute-start(bf16[2,128,384]{2,1,0:T(8,128)(2,1)S(1)} %get-tuple-element.50), channel_id=1, source_target_pairs={{0,4},{2,10},{4,12},{6,2},{8,0},{10,18},{12,20},{14,6},{16,8},{18,... | collective-permute-start | bytes 589832 | tf_op jit(solution)/shard_map/ppermute | solution.py:426
  23.0 7.9 %collective-permute-start.8 = (bf16[2,128,384]{2,1,0:T(8,128)(2,1)S(1)}, bf16[2,128,384]{2,1,0:T(8,128)(2,1)S(1)}, u32[]{:S(2)}, u32[]{:S(2)}) collective-permute-start(bf16[2,128,384]{2,1,0:T(8,128)(2,1)S(1)} %collective-permute-done.3.refs_2_), channel_id=1, source_target_pairs={{0,8},{2,6},{4,0},{6,14},{8,16},{10,2},{12,4},{14,22},{16,24},{18,... | collective-permute-start | bytes 589832 | tf_op jit(solution)/shard_map/ppermute | solution.py:426
  25.1 7.3 %collective-permute-start.9 = (bf16[2,128,384]{2,1,0:T(8,128)(2,1)S(1)}, bf16[2,128,384]{2,1,0:T(8,128)(2,1)S(1)}, u32[]{:S(2)}, u32[]{:S(2)}) collective-permute-start(bf16[2,128,384]{2,1,0:T(8,128)(2,1)S(1)} %collective-permute-done.5.refs_3_), channel_id=1, source_target_pairs={{0,8},{2,6},{4,0},{6,14},{8,16},{10,2},{12,4},{14,22},{16,24},{18,... | collective-permute-start | bytes 589832 | tf_op jit(solution)/shard_map/ppermute | solution.py:426
  26.8 7.8 %collective-permute-start.10 = (bf16[2,128,384]{2,1,0:T(8,128)(2,1)S(1)}, bf16[2,128,384]{2,1,0:T(8,128)(2,1)S(1)}, u32[]{:S(2)}, u32[]{:S(2)}) collective-permute-start(bf16[2,128,384]{2,1,0:T(8,128)(2,1)S(1)} %collective-permute-done.4.refs_4_), channel_id=1, source_target_pairs={{0,4},{2,10},{4,12},{6,2},{8,0},{10,18},{12,20},{14,6},{16,8},{18,... | collective-permute-start | bytes 589832 | tf_op jit(solution)/shard_map/ppermute | solution.py:426
  27.3 8.9 %collective-permute-start.11 = (bf16[2,128,384]{2,1,0:T(8,128)(2,1)S(1)}, bf16[2,128,384]{2,1,0:T(8,128)(2,1)S(1)}, u32[]{:S(2)}, u32[]{:S(2)}) collective-permute-start(bf16[2,128,384]{2,1,0:T(8,128)(2,1)S(1)} %collective-permute-done.6.refs_5_), channel_id=1, source_target_pairs={{0,4},{2,10},{4,12},{6,2},{8,0},{10,18},{12,20},{14,6},{16,8},{18,... | collective-permute-start | bytes 589832 | tf_op jit(solution)/shard_map/ppermute | solution.py:426
  30.9 5.4 %collective-permute-start.7 = (bf16[128,768]{1,0:T(8,128)(2,1)S(1)}, bf16[128,768]{1,0:T(8,128)(2,1)S(1)}, u32[]{:S(2)}, u32[]{:S(2)}) collective-permute-start(bf16[128,768]{1,0:T(8,128)(2,1)S(1)} %get-tuple-element.55.qo_ref), channel_id=1, source_target_pairs={{0,2},{2,0},{4,6},{6,4},{8,10},{10,8},{12,14},{14,12},{16,18},{18,... | collective-permute-start | bytes 589832 | tf_op jit(solution)/shard_map/ppermute | solution.py:506
  30.9 11.5 %collective-permute-start.12 = (bf16[128,1536]{1,0:T(8,128)(2,1)S(1)}, bf16[128,1536]{1,0:T(8,128)(2,1)S(1)}, u32[]{:S(2)}, u32[]{:S(2)}) collective-permute-start(bf16[128,1536]{1,0:T(8,128)(2,1)S(1)} %get-tuple-element.66), channel_id=1, source_target_pairs={{0,1},{1,0},{2,3},{3,2},{4,5},{5,4},{6,7},{7,6},{8,9},{9,8},{10,11... | collective-permute-start | bytes 1179656 | tf_op jit(solution)/shard_map/ppermute | solution.py:507
  32.4 10.6 %collective-permute-start.13 = (bf16[2,128,384]{2,1,0:T(8,128)(2,1)S(1)}, bf16[2,128,384]{2,1,0:T(8,128)(2,1)S(1)}, u32[]{:S(2)}, u32[]{:S(2)}) collective-permute-start(bf16[2,128,384]{2,1,0:T(8,128)(2,1)S(1)} %collective-permute-done.8.refs_6_), channel_id=1, source_target_pairs={{0,8},{2,6},{4,0},{6,14},{8,16},{10,2},{12,4},{14,22},{16,24},{18,... | collective-permute-start | bytes 589832 | tf_op jit(solution)/shard_map/ppermute | solution.py:496
  34.6 9.6 %collective-permute-start.15 = (bf16[2,128,384]{2,1,0:T(8,128)(2,1)S(1)}, bf16[2,128,384]{2,1,0:T(8,128)(2,1)S(1)}, u32[]{:S(2)}, u32[]{:S(2)}) collective-permute-start(bf16[2,128,384]{2,1,0:T(8,128)(2,1)S(1)} %collective-permute-done.9.refs_7_), channel_id=1, source_target_pairs={{0,8},{2,6},{4,0},{6,14},{8,16},{10,2},{12,4},{14,22},{16,24},{18,... | collective-permute-start | bytes 589832 | tf_op jit(solution)/shard_map/ppermute | solution.py:496
  44.1 1.8 %collective-permute-start.14 = (f32[128,512]{1,0:T(8,128)S(1)}, f32[128,512]{1,0:T(8,128)S(1)}, u32[]{:S(2)}, u32[]{:S(2)}) collective-permute-start(f32[128,512]{1,0:T(8,128)S(1)} %get-tuple-element.70), channel_id=1, source_target_pairs={{0,2},{2,0},{4,6},{6,4},{8,10},{10,8},{12,14},{14,12},{16,18},{18,... | collective-permute-start | bytes 786440 | tf_op jit(solution)/shard_map/ppermute | solution.py:554
  45.4 2.3 %collective-permute-start.16 = (f32[128,512]{1,0:T(8,128)S(1)}, f32[128,512]{1,0:T(8,128)S(1)}, u32[]{:S(2)}, u32[]{:S(2)}) collective-permute-start(f32[128,512]{1,0:T(8,128)S(1)} %get-tuple-element.74), channel_id=1, source_target_pairs={{0,2},{2,0},{4,6},{6,4},{8,10},{10,8},{12,14},{14,12},{16,18},{18,... | collective-permute-start | bytes 786440 | tf_op jit(solution)/shard_map/ppermute | solution.py:554
  46.1 5.4 %collective-permute-start.17 = (bf16[128,384]{1,0:T(8,128)(2,1)S(1)}, bf16[128,384]{1,0:T(8,128)(2,1)S(1)}, u32[]{:S(2)}, u32[]{:S(2)}) collective-permute-start(bf16[128,384]{1,0:T(8,128)(2,1)S(1)} %merge.2.first_ref), channel_id=1, source_target_pairs={{0,1},{1,0},{2,3},{3,2},{4,5},{5,4},{6,7},{7,6},{8,9},{9,8},{10,11... | collective-permute-start | bytes 294920 | tf_op jit(solution)/shard_map/ppermute | solution.py:562
  47.8 5.2 %collective-permute-start.18 = (bf16[128,384]{1,0:T(8,128)(2,1)S(1)}, bf16[128,384]{1,0:T(8,128)(2,1)S(1)}, u32[]{:S(2)}, u32[]{:S(2)}) collective-permute-start(bf16[128,384]{1,0:T(8,128)(2,1)S(1)} %merge.3.second_ref), channel_id=1, source_target_pairs={{0,1},{1,0},{2,3},{3,2},{4,5},{5,4},{6,7},{7,6},{8,9},{9,8},{10,11... | collective-permute-start | bytes 294920 | tf_op jit(solution)/shard_map/ppermute | solution.py:562

commit v9 on v8

--- a/solution.py
+++ b/solution.py
@@ -41,7 +41,7 @@
 
 def send_kernel(
     place_ref, x_ref, t_ref, scale_ref, shift_ref, w_ref,
-    a_ref, msg_ref, tmsg_ref, stat_ref, ahead_ref,
+    a_ref, msg_ref, stat_ref, ahead_ref,
     x_buffer, t_buffer, scale_buffer, shift_buffer, w_buffer, in_sems, w_sems,
 ):
     video, features = x_buffer.shape
@@ -73,7 +73,7 @@
     row = lax.broadcasted_iota(jnp.int32, (EXTRA, features), 0)
     extra = jnp.zeros((EXTRA, features), F32)
     for index, piece in enumerate(pieces):
-        extra = jnp.where(row == index, piece.astype(F32), extra)
+        extra = jnp.where(row % 4 == index, piece.astype(F32), extra)
     a_ref[video:top, :] = extra.astype(BF16)
 
     def prepare(rows_ref, start):
@@ -100,24 +100,57 @@
     text_stats = prepare(t_buffer, top)
     stat_ref[video:top, :] = jnp.zeros((EXTRA, HEAD_DIM), F32)
 
+    band = lax.broadcasted_iota(jnp.int32, (EXTRA, PIECE), 0) // 4
+    spare = heads_of(width) * 4
     for block in range(blocks):
         w_copies[block].wait()
         if block + 3 < len(w_copies):
             w_copies[block + 3].start()
-        for piece in range(columns // PIECE):
-            start = block * columns + piece * PIECE
+        for piece in range(block * columns // PIECE, (block + 1) * columns // PIECE):
+            start = piece * PIECE
+            local = start - block * columns
             product = jnp.dot(
-                a_ref[...], w_buffer[block, :, piece * PIECE : (piece + 1) * PIECE],
-                preferred_element_type=F32,
+                a_ref[...], w_buffer[block, :, local : local + PIECE], preferred_element_type=F32
             )
-            msg_ref[:, start : start + PIECE] = product[:top].astype(BF16)
-            if start == 0:
-                stats = jnp.concatenate([video_stats, text_stats], axis=1)
-                msg_ref[video:, : video + text] = (product[video:top] + stats).astype(BF16)
+            msg_ref[:video, start : start + PIECE] = product[:video].astype(BF16)
+            group, member = divmod(piece, 4)
+            if member == 0:
+                terms = product[video:top]
+            else:
+                terms = jnp.where(band == member, product[video:top], terms)
+            if member == 3 or start + PIECE == width:
+                rows, cells = slot(text, width, spare, group)
+                msg_ref[video + rows.start : video + rows.stop, cells] = terms.astype(BF16)
             for source, target in text_columns(start):
-                tmsg_ref[:, target : target + HEAD_DIM] = product[top:, source].astype(BF16)
+                part = product[top:, source].astype(BF16)
+                for quarter in range(4):
+                    rows, cells = slot(text, width, target // PIECE * 4 + quarter)
+                    first = cells.start + target % PIECE
+                    msg_ref[
+                        video + rows.start : video + rows.stop, first : first + HEAD_DIM
+                    ] = part[quarter * text // 4 : (quarter + 1) * text // 4]
+    rows, cells = slot(text, width, spare, -(-width // PIECE // 4))
+    msg_ref[video + rows.start : video + rows.stop, cells] = jnp.concatenate(
+        [video_stats, text_stats], axis=1
+    ).astype(BF16)
     for copy in w_copies[blocks:]:
         copy.wait()
+
+
+def heads_of(width):
+    return width // TRIPLE
+
+
+def slot(text, width, index, part=None):
+    depth = text // 4
+    if part is not None:
+        index += part // (depth // EXTRA)
+    band, place = divmod(index, width // PIECE)
+    rows = slice(band * depth, (band + 1) * depth)
+    if part is not None:
+        first = rows.start + part % (depth // EXTRA) * EXTRA
+        rows = slice(first, first + EXTRA)
+    return rows, slice(place * PIECE, (place + 1) * PIECE)
 
 
 def text_columns(first):
@@ -186,8 +219,21 @@
     return gap, lax.rsqrt(var + EPS)
 
 
-def column_terms(own, other):
-    other = other.astype(F32)
+def received_stats(msg_ref, video, text):
+    width = msg_ref.shape[1]
+    rows, cells = slot(text, width, heads_of(width) * 4, -(-width // PIECE // 4))
+    return msg_ref[video + rows.start : video + rows.stop, cells]
+
+
+def column_terms(own_ref, msg_ref, video, text, part):
+    width = msg_ref.shape[1]
+    piece, half = divmod(part, 2)
+    group, member = divmod(piece, 4)
+    rows, cells = slot(text, width, heads_of(width) * 4, group)
+    first = cells.start + half * HEAD_DIM
+    other = msg_ref[video + rows.start : video + rows.stop, first : first + HEAD_DIM].astype(F32)
+    other = other[4 * member : 4 * member + 4]
+    own = own_ref[video : video + 8, part * HEAD_DIM : (part + 1) * HEAD_DIM]
     scale = (own[0:1] + own[1:2]) - (other[0:1] + other[1:2])
     shift = (own[2:3] + own[3:4]) + (other[2:3] + other[3:4])
     return scale, shift
@@ -199,47 +245,56 @@
 
 
 def norm_kernel(
-    total_features, own_ref, msg_ref, stat_ref, qg_ref, kg_ref, q_ref, cache_ref, kv_ref,
+    total_features, text, own_ref, msg_ref, stat_ref, qg_ref, kg_ref, q_ref, cache_ref, kv_ref,
 ):
     video = q_ref.shape[0]
-    top = video + EXTRA
+    heads = q_ref.shape[1] // HEAD_DIM
     query_gain = qg_ref[...].reshape(1, HEAD_DIM)
     key_gain = kg_ref[...].reshape(1, HEAD_DIM)
-    heads = q_ref.shape[1] // HEAD_DIM
-    gap, inverse = row_stats(total_features, stat_ref[:video, :], msg_ref[video:top, :video])
+    stats = received_stats(msg_ref, video, text)[:, :video]
+    gap, inverse = row_stats(total_features, stat_ref[:video, :], stats)
+
+    def total(part):
+        cells = slice(part * HEAD_DIM, (part + 1) * HEAD_DIM)
+        scale, shift = column_terms(own_ref, msg_ref, video, text, part)
+        both = own_ref[:video, cells] + msg_ref[:video, cells].astype(F32)
+        return (both + gap * scale) * inverse + shift
+
     for head in range(heads):
-        part = slice(head * TRIPLE, (head + 1) * TRIPLE)
         columns = slice(head * HEAD_DIM, (head + 1) * HEAD_DIM)
-        scale, shift = column_terms(own_ref[video:, part], msg_ref[video:top, part])
-        total = own_ref[:video, part] + msg_ref[:video, part].astype(F32)
-        total = (total + gap * scale) * inverse + shift
-        q_ref[:, columns] = head_norm(total[:, :HEAD_DIM], query_gain).astype(BF16)
-        keys = head_norm(total[:, HEAD_DIM : 2 * HEAD_DIM], key_gain).astype(BF16)
-        values = total[:, 2 * HEAD_DIM :].astype(BF16)
+        q_ref[:, columns] = head_norm(total(3 * head), query_gain).astype(BF16)
+        keys = head_norm(total(3 * head + 1), key_gain).astype(BF16)
+        values = total(3 * head + 2).astype(BF16)
         cache_ref[0, :, columns] = keys
         cache_ref[1, :, columns] = values
         kv_ref[0, :, columns] = keys
         kv_ref[1, :, columns] = values
 
 
-def text_kernel(total_features, own_ref, tmsg_ref, stat_ref, top_ref, msg_ref, kg_ref, kv_ref):
+def text_kernel(total_features, own_ref, msg_ref, stat_ref, top_ref, kg_ref, kv_ref):
     text = kv_ref.shape[1]
     heads = kv_ref.shape[2] // HEAD_DIM
-    top = top_ref.shape[0]
+    top, width = top_ref.shape
     video = top - EXTRA
     key_gain = kg_ref[...].reshape(1, HEAD_DIM)
-    gap, inverse = row_stats(
-        total_features, stat_ref[top:, :], msg_ref[video:top, video : video + text]
-    )
+    stats = received_stats(msg_ref, video, text)[:, video : video + text]
+    gap, inverse = row_stats(total_features, stat_ref[top:, :], stats)
     for head in range(heads):
-        part = slice(head * TRIPLE + HEAD_DIM, (head + 1) * TRIPLE)
-        pair = slice(head * PIECE, (head + 1) * PIECE)
         columns = slice(head * HEAD_DIM, (head + 1) * HEAD_DIM)
-        scale, shift = column_terms(top_ref[video:, part], msg_ref[video:top, part])
-        total = own_ref[:, pair] + tmsg_ref[:, pair].astype(F32)
-        total = (total + gap * scale) * inverse + shift
-        kv_ref[0, :, columns] = head_norm(total[:, :HEAD_DIM], key_gain).astype(BF16)
-        kv_ref[1, :, columns] = total[:, HEAD_DIM:].astype(BF16)
+        other = []
+        for quarter in range(4):
+            rows, cells = slot(text, width, head * 4 + quarter)
+            other.append(msg_ref[video + rows.start : video + rows.stop, cells])
+        total = own_ref[:, head * PIECE : (head + 1) * PIECE]
+        total = total + jnp.concatenate(other, axis=0).astype(F32)
+
+        def finish(part):
+            scale, shift = column_terms(top_ref, msg_ref, video, text, 3 * head + 1 + part)
+            both = total[:, part * HEAD_DIM : (part + 1) * HEAD_DIM]
+            return (both + gap * scale) * inverse + shift
+
+        kv_ref[0, :, columns] = head_norm(finish(0), key_gain).astype(BF16)
+        kv_ref[1, :, columns] = finish(1).astype(BF16)
 
 
 FACTOR = math.log2(math.e) / math.sqrt(HEAD_DIM)
@@ -259,17 +314,6 @@
 
 def times(weights, values):
     return jnp.dot(weights.astype(BF16), values, preferred_element_type=F32)
-
-
-def absorb(queries, blocks, num, den):
-    for first in range(0, len(blocks), 2):
-        pair = blocks[first : first + 2]
-        keys = jnp.concatenate([ref[0, :, columns] for ref, columns in pair], axis=0)
-        values = jnp.concatenate([ref[1, :, columns] for ref, columns in pair], axis=0)
-        weights = weigh(queries, keys)
-        num = num + times(weights, values)
-        den = den + lanes(weights)
-    return num, den
 
 
 def split_kernel(*refs):
@@ -280,16 +324,20 @@
         refs[count + 2 * index + 1][...] = refs[index][:, :, half:]
 
 
-def first_kernel(count, qo_ref, qp_ref, fresh_ref, stale_ref, *refs):
-    num_ref, den_ref = refs[-2:]
-    whole, halves = refs[:count], refs[count:-2]
-    video, width = qo_ref.shape
+def attend_kernel(
+    first, count, place_ref, qo_ref, qp_ref, fresh_ref, stale_ref, text_ref, mask_ref, *refs
+):
+    own_ref, own_den_ref, msg_ref = refs[-3:]
+    video, width = own_ref.shape
+    text = text_ref.shape[1]
     lane = lax.broadcasted_iota(jnp.int32, (2 * video, HEAD_DIM), 1)
+    mask = mask_ref[...].reshape(1, 2 * text).astype(F32)
+    mask = jnp.where(place_ref[1] == 0, mask[:, :text], mask[:, text:])
+    keep = jnp.concatenate([jnp.ones((1, video), F32), mask], axis=1)
     packed = jnp.zeros((2 * video, HEAD_DIM), F32)
     for head in range(width // HEAD_DIM):
-        columns = slice(head * HEAD_DIM, (head + 1) * HEAD_DIM)
-        second, start = divmod(head * HEAD_DIM, width // 2)
-        cells = slice(start, start + HEAD_DIM)
+        cells = slice(head * HEAD_DIM, (head + 1) * HEAD_DIM)
+        columns = slice((first + head) * HEAD_DIM, (first + head + 1) * HEAD_DIM)
         own, other = qo_ref[:, columns], qp_ref[:, columns]
         queries = jnp.concatenate([own, other], axis=0)
         fresh = weigh(own, fresh_ref[0, :, columns])
@@ -298,36 +346,25 @@
             [times(fresh, fresh_ref[1, :, columns]), times(stale, stale_ref[1, :, columns])], axis=0
         )
         den = jnp.concatenate([fresh, stale], axis=0)
-        blocks = [(ref, columns) for ref in whole] + [(ref, cells) for ref in halves[second::2]]
-        num, den = absorb(queries, blocks, num, den)
-        num_ref[:, columns] = num
-        packed = jnp.where(lane == head, jnp.sum(den, axis=1, keepdims=True), packed)
-    den_ref[...] = packed
-
-
-def last_kernel(
-    first, place_ref, qo_ref, qp_ref, num_ref, den_ref, text_ref, mask_ref, far_ref,
-    own_ref, own_den_ref, msg_ref,
-):
-    video = qo_ref.shape[0]
-    text, width = text_ref.shape[1], far_ref.shape[2]
-    lane = lax.broadcasted_iota(jnp.int32, (2 * video, HEAD_DIM), 1)
-    mask = mask_ref[...].reshape(1, 2 * text).astype(F32)
-    mask = jnp.where(place_ref[1] == 0, mask[:, :text], mask[:, text:])
-    keep = jnp.concatenate([mask, jnp.ones((1, video), F32)], axis=1)
-    packed = den_ref[...]
-    for head in range(width // HEAD_DIM):
-        cells = slice(head * HEAD_DIM, (head + 1) * HEAD_DIM)
-        columns = slice((first + head) * HEAD_DIM, (first + head + 1) * HEAD_DIM)
-        queries = jnp.concatenate([qo_ref[:, columns], qp_ref[:, columns]], axis=0)
-        keys = jnp.concatenate([text_ref[0, :, columns], far_ref[0, :, cells]], axis=0)
-        values = jnp.concatenate([text_ref[1, :, columns], far_ref[1, :, cells]], axis=0)
-        weights = weigh(queries, keys) * keep
-        num = num_ref[:, columns] + times(weights, values)
+        blocks = [(ref, columns) for ref in refs[:count]] + [(ref, cells) for ref in refs[count:-3]]
+        blocks.append((text_ref, columns))
+        for start in range(len(blocks) % 2, len(blocks), 2):
+            pair = blocks[start : start + 2]
+            keys = jnp.concatenate([ref[0, :, part] for ref, part in pair], axis=0)
+            values = jnp.concatenate([ref[1, :, part] for ref, part in pair], axis=0)
+            weights = weigh(queries, keys)
+            if start + 2 == len(blocks):
+                weights = weights * keep
+            num = num + times(weights, values)
+            den = den + lanes(weights)
+        if len(blocks) % 2:
+            ref, part = blocks[0]
+            weights = weigh(queries, ref[0, :, part])
+            num = num + times(weights, ref[1, :, part])
+            den = den + weights
         own_ref[:, cells] = num[:video]
         msg_ref[:, cells] = num[video:]
-        total = jnp.sum(lanes(weights), axis=1, keepdims=True)
-        packed = packed + jnp.where(lane == first + head, total, 0.0)
+        packed = jnp.where(lane == first + head, jnp.sum(den, axis=1, keepdims=True), packed)
     own_den_ref[...] = packed[:video]
     msg_ref[:, width:] = packed[video:]
 
@@ -433,15 +470,16 @@
     columns = 2 * TRIPLE
     blocks = group_columns // columns
     ahead = blocks - 1
+    slots = heads * 4 + -(-(-(-group_columns // PIECE // 4) + 1) * 16 // (text // 4))
+    message_rows = video + -(-slots // (group_columns // PIECE)) * text // 4
     project_cost = cost(8 * rows * features * group_columns, 2 * features * group_columns)
-    a_rows, message, text_message, stats, w_ahead = pl.pallas_call(
+    a_rows, message, stats, w_ahead = pl.pallas_call(
         send_kernel,
         in_specs=[smem] + [hbm] * 5,
-        out_specs=[vmem] * 5,
+        out_specs=[vmem] * 4,
         out_shape=[
             jax.ShapeDtypeStruct((rows, features), BF16),
-            jax.ShapeDtypeStruct((top, group_columns), BF16),
-            jax.ShapeDtypeStruct((text, 2 * width), BF16),
+            jax.ShapeDtypeStruct((message_rows, group_columns), BF16),
             jax.ShapeDtypeStruct((rows, HEAD_DIM), F32),
             jax.ShapeDtypeStruct((ahead, features, columns), BF16),
         ],
@@ -494,51 +532,35 @@
         for chain in chains:
             chain.append(ring_step(lax.optimization_barrier((*chain[-1], own))[:2]))
     far = [lax.ppermute(chain[-1][0], "section", ways[0]) for chain in chains]
+    ends = [chain[-1][1] for chain in chains]
 
     received = lax.optimization_barrier((received, *chains[0][0], *chains[1][0]))[0]
     queries, new_cache, fresh = plain_call(
-        functools.partial(norm_kernel, features * 2),
+        functools.partial(norm_kernel, features * 2, text),
         [((video, width), BF16), ((2, video, width), BF16), ((2, video, width), BF16)],
         "norm_video",
         cost(1000 * top * group_columns, 8 * top * group_columns),
         own, received, stats, query_gain, key_gain,
     )
     other_queries = lax.ppermute(queries, "section", swap_core)
-    text_received = lax.ppermute(
-        lax.optimization_barrier((text_message, queries))[0], "head", swap_head
-    )
-
-    halves = [
-        block
-        for steps in zip(*chains)
-        for way in range(2)
-        for block in (steps[0][way], steps[1][way])
-    ]
-    context = (len(halves) // 2 + 3) * video
-    num, den = plain_call(
-        functools.partial(first_kernel, 2),
-        [((2 * video, width), F32), ((2 * video, HEAD_DIM), F32)],
-        "attend_first",
-        cost(32 * video * context * width, 4 * context * width, 2 * video * context * heads),
-        queries, other_queries, fresh, stale, *whole, *halves,
-    )
     (text_kv,) = plain_call(
         functools.partial(text_kernel, features * 2),
         [((2, text, width), BF16)],
         "norm_text",
         cost(1000 * text * group_columns, 8 * text * group_columns),
-        own_text, text_received, stats, own, received, key_gain,
-    )
-
-    last_context = video + text
+        own_text, lax.optimization_barrier((received, *far, *ends))[0], stats, own, key_gain,
+    )
+
+    context = chips * video + video + text
     attended, other_attended = [], []
-    for index, block in enumerate(far):
+    for index, chain in enumerate(chains):
         first = index * heads // 2
+        halves = [block for step in chain for block in step] + [far[index]]
         if attended:
-            num = lax.optimization_barrier((num, num_own))[0]
+            queries = lax.optimization_barrier((queries, num_own))[0]
         num_own, den_own, num_message = pl.pallas_call(
-            functools.partial(last_kernel, first),
-            in_specs=[smem] + [vmem] * 7,
+            functools.partial(attend_kernel, first, len(whole)),
+            in_specs=[smem] + [vmem] * (6 + len(whole) + len(halves)),
             out_specs=[vmem] * 3,
             out_shape=[
                 jax.ShapeDtypeStruct((video, width // 2), F32),
@@ -547,10 +569,10 @@
             ],
             compiler_params=params(24),
             cost_estimate=cost(
-                16 * video * last_context * width, 6 * video * width, video * last_context * heads
+                16 * video * context * width, 2 * context * width, video * context * heads
             ),
-            name="attend_last",
-        )(place, queries, other_queries, num, den, text_kv, text_mask, block)
+            name="attend",
+        )(place, queries, other_queries, fresh, stale, text_kv, text_mask, *whole, *halves)
         num_received = lax.ppermute(num_message, "section", swap_core)
         attended += plain_call(
             functools.partial(merge_kernel, first),

time: 54.3 us -> 54.4 us (level)
  waiting for transfers between devices: 8.94 us -> 11.3 us
  starting transfers between devices: 23.6 us -> 21.8 us
    ppermute x10, waiting for transfers between devices: 2.82 us -> 7.75 us  [ring_step(): lax.ppermute(block, 'section', way)]
    pallas_call x9 -> x8, Pallas kernels: 7.77 us -> 4.51 us  [plain_call(): pl.pallas_call(kernel, in_specs=[pl.BlockSpec(memory_space=pltpu.VMEM)] *...]
    ppermute x1 -> x0, waiting for transfers between devices: 2.91 us -> none  [per_device(): lax.ppermute(lax.optimization_barrier((text_message, queries))[0], 'head'...]
    pallas_call x2, Pallas kernels: 2.29 us -> 5.06 us  [per_device(): pl.pallas_call(functools.partial(attend_kernel, first, len(whole)), in_sp...]
    ppermute x1 -> x0, starting transfers between devices: 1.49 us -> none  [per_device(): lax.ppermute(lax.optimization_barrier((text_message, queries))[0], 'head'...]
    ppermute x2, starting transfers between devices: 3.85 us -> 2.96 us  [per_device(): far = [lax.ppermute(chain[-1][0], 'section', ways[0]) for chain in chains]]
    ppermute x2, starting transfers between devices: 2.59 us -> 3.22 us  [per_device(): other_attended.append(lax.ppermute(attended[-1], 'head', swap_head))]
    ppermute x2, waiting for transfers between devices: 0.01 us -> 0.62 us  [per_device(): far = [lax.ppermute(chain[-1][0], 'section', ways[0]) for chain in chains]]
  transfers between devices with their start and end apart: 19 -> 18, of which waited for: 6 -> 8; matrix products, arithmetic and copies ran while one was open for 0% -> 0% of each run, Pallas kernels for 36% -> 31%
where the time goes in v9:
time: 54.4 us; the launch traced here: 54.2 us
  starting transfers between devices  21.8 us (40%)
  Pallas kernels  20.2 us (37%)
  waiting for transfers between devices  11.3 us (21%)
  between operations  0.74 us (1%)
    ppermute x10, starting transfers between devices, ring_step(): lax.ppermute(block, 'section', way)  13 us
    ppermute x10, waiting for transfers between devices, ring_step(): lax.ppermute(block, 'section', way)  7.75 us
    pallas_call x1, Pallas kernels, per_device(): pl.pallas_call(send_kernel, in_specs=[smem] + [hbm] * 5, out_specs=[vmem]...  5.63 us
    pallas_call x2, Pallas kernels, per_device(): pl.pallas_call(functools.partial(attend_kernel, first, len(whole)), in_sp...  5.06 us
    pallas_call x1, Pallas kernels, per_device(): pl.pallas_call(own_kernel, in_specs=[smem, vmem, vmem, hbm, hbm] + [hbm]...  5.05 us
    pallas_call x8, Pallas kernels, plain_call(): pl.pallas_call(kernel, in_specs=[pl.BlockSpec(memory_space=pltpu.VMEM)] *...  4.51 us
    ppermute x2, starting transfers between devices, per_device(): other_attended.append(lax.ppermute(attended[-1], 'head', swap_head))  3.22 us
    ppermute x2, starting transfers between devices, per_device(): far = [lax.ppermute(chain[-1][0], 'section', ways[0]) for chain in chains]  2.96 us
  transfers between devices with their start and end apart: 18, of which 8 were waited for; matrix products, arithmetic and copies ran while one was open for 0% of the time, Pallas kernels for 31%

profile of v9, /device:TPU:0, one launch (start us, length us, event | category | flops | bytes accessed | tf_op | source)
XLA Modules:
  0.0 54.2 jit_solution(10425315526193311704)
XLA Ops:
  0.6 3.1 %collective-permute-start.1 = (bf16[2,128,768]{2,1,0:T(8,128)(2,1)}, bf16[2,128,768]{2,1,0:T(8,128)(2,1)S(1)}, u32[]{:S(2)}, u32[]{:S(2)}) collective-permute-start(bf16[2,128,768]{2,1,0:T(8,128)(2,1)} %refs_5_.1), channel_id=1, source_target_pairs={{0,8},{2,6},{4,0},{6,14},{8,16},{10,2},{12,4},{14,22},{16,24},{18,... | collective-permute-start | bytes 1179656 | tf_op jit(solution)/shard_map/ppermute | solution.py:463
  3.8 5.6 %project_send.1 = (bf16[272,1536]{1,0:T(8,128)(2,1)S(1)}, bf16[224,2304]{1,0:T(8,128)(2,1)S(1)}, f32[272,128]{1,0:T(8,128)S(1)}, bf16[2,1536,768]{2,1,0:T(8,128)(2,1)S(1)}) custom-call(s32[2]{0:T(128)S(1)} %pad_add_fusion.place_ref, bf16[128,1536]{1,0:T(8,128)(2,1)} %refs_4_.1, bf16[256,1536]{1,0:T(8,128)(2,1)} %t_ref.1, f32[1536]{0:T(1024)} %scale_ref.1, ...), custom_call_target="tpu_custom_call" | custom-call | flops 7700742144 | bytes 7077888 | tf_op jit(solution)/shard_map/project_send/pallas_call | solution.py:476
  9.4 2.0 %collective-permute-start = (bf16[224,2304]{1,0:T(8,128)(2,1)S(1)}, bf16[224,2304]{1,0:T(8,128)(2,1)S(1)}, u32[]{:S(2)}, u32[]{:S(2)}) collective-permute-start(bf16[224,2304]{1,0:T(8,128)(2,1)S(1)} %get-tuple-element.41), channel_id=1, source_target_pairs={{0,1},{1,0},{2,3},{3,2},{4,5},{5,4},{6,7},{7,6},{8,9},{9,8},{10,11... | collective-permute-start | bytes 3096584 | tf_op jit(solution)/shard_map/ppermute | solution.py:500
  11.4 1.9 %collective-permute-done.1.refs_0_ = bf16[2,128,768]{2,1,0:T(8,128)(2,1)S(1)} collective-permute-done((bf16[2,128,768]{2,1,0:T(8,128)(2,1)}, bf16[2,128,768]{2,1,0:T(8,128)(2,1)S(1)}, u32[]{:S(2)}, u32[]{:S(2)}) %collective-permute-start.1) | collective-permute-done | bytes 393248 | tf_op jit(solution)/shard_map/ppermute | solution.py:463
  13.4 1.6 %collective-permute-start.3 = (bf16[2,128,384]{2,1,0:T(8,128)(2,1)S(1)}, bf16[2,128,384]{2,1,0:T(8,128)(2,1)S(1)}, u32[]{:S(2)}, u32[]{:S(2)}) collective-permute-start(bf16[2,128,384]{2,1,0:T(8,128)(2,1)S(1)} %get-tuple-element.44), channel_id=1, source_target_pairs={{0,8},{2,6},{4,0},{6,14},{8,16},{10,2},{12,4},{14,22},{16,24},{18,... | collective-permute-start | bytes 589832 | tf_op jit(solution)/shard_map/ppermute | solution.py:463
  15.0 0.9 %collective-permute-start.4 = (bf16[2,128,384]{2,1,0:T(8,128)(2,1)S(1)}, bf16[2,128,384]{2,1,0:T(8,128)(2,1)S(1)}, u32[]{:S(2)}, u32[]{:S(2)}) collective-permute-start(bf16[2,128,384]{2,1,0:T(8,128)(2,1)S(1)} %get-tuple-element.45), channel_id=1, source_target_pairs={{0,4},{2,10},{4,12},{6,2},{8,0},{10,18},{12,20},{14,6},{16,8},{18,... | collective-permute-start | bytes 589832 | tf_op jit(solution)/shard_map/ppermute | solution.py:463
  15.9 1.1 %collective-permute-start.5 = (bf16[2,128,384]{2,1,0:T(8,128)(2,1)S(1)}, bf16[2,128,384]{2,1,0:T(8,128)(2,1)S(1)}, u32[]{:S(2)}, u32[]{:S(2)}) collective-permute-start(bf16[2,128,384]{2,1,0:T(8,128)(2,1)S(1)} %get-tuple-element.46), channel_id=1, source_target_pairs={{0,8},{2,6},{4,0},{6,14},{8,16},{10,2},{12,4},{14,22},{16,24},{18,... | collective-permute-start | bytes 589832 | tf_op jit(solution)/shard_map/ppermute | solution.py:463
  17.0 0.9 %collective-permute-start.6 = (bf16[2,128,384]{2,1,0:T(8,128)(2,1)S(1)}, bf16[2,128,384]{2,1,0:T(8,128)(2,1)S(1)}, u32[]{:S(2)}, u32[]{:S(2)}) collective-permute-start(bf16[2,128,384]{2,1,0:T(8,128)(2,1)S(1)} %get-tuple-element.47), channel_id=1, source_target_pairs={{0,4},{2,10},{4,12},{6,2},{8,0},{10,18},{12,20},{14,6},{16,8},{18,... | collective-permute-start | bytes 589832 | tf_op jit(solution)/shard_map/ppermute | solution.py:463
  17.9 5.0 %project_own.1 = (f32[144,2304]{1,0:T(8,128)S(1)}, f32[128,1536]{1,0:T(8,128)S(1)}, bf16[768,1536]{1,0:T(8,128)(2,1)S(1)}, bf16[768,1536]{1,0:T(8,128)(2,1)S(1)}...) custom-call(s32[2]{0:T(128)S(1)} %pad_add_fusion.place_ref, ...), custom_call_target="tpu_custom_call" | custom-call | flops 7700742144 | bytes 7077888 | tf_op jit(solution)/shard_map/project_own/pallas_call | solution.py:508
  23.0 1.2 %collective-permute-start.8 = (bf16[2,128,384]{2,1,0:T(8,128)(2,1)S(1)}, bf16[2,128,384]{2,1,0:T(8,128)(2,1)S(1)}, u32[]{:S(2)}, u32[]{:S(2)}) collective-permute-start(bf16[2,128,384]{2,1,0:T(8,128)(2,1)S(1)} %collective-permute-done.3.refs_2_), channel_id=1, source_target_pairs={{0,8},{2,6},{4,0},{6,14},{8,16},{10,2},{12,4},{14,22},{16,24},{18,... | collective-permute-start | bytes 589832 | tf_op jit(solution)/shard_map/ppermute | solution.py:463
  25.1 1.7 %collective-permute-start.10 = (bf16[2,128,384]{2,1,0:T(8,128)(2,1)S(1)}, bf16[2,128,384]{2,1,0:T(8,128)(2,1)S(1)}, u32[]{:S(2)}, u32[]{:S(2)}) collective-permute-start(bf16[2,128,384]{2,1,0:T(8,128)(2,1)S(1)} %collective-permute-done.5.refs_2_), channel_id=1, source_target_pairs={{0,8},{2,6},{4,0},{6,14},{8,16},{10,2},{12,4},{14,22},{16,24},{18,... | collective-permute-start | bytes 589832 | tf_op jit(solution)/shard_map/ppermute | solution.py:463
  27.3 2.0 %collective-permute-start.13 = (bf16[2,128,384]{2,1,0:T(8,128)(2,1)S(1)}, bf16[2,128,384]{2,1,0:T(8,128)(2,1)S(1)}, u32[]{:S(2)}, u32[]{:S(2)}) collective-permute-start(bf16[2,128,384]{2,1,0:T(8,128)(2,1)S(1)} %collective-permute-done.6.refs_3_), channel_id=1, source_target_pairs={{0,4},{2,10},{4,12},{6,2},{8,0},{10,18},{12,20},{14,6},{16,8},{18,... | collective-permute-start | bytes 589832 | tf_op jit(solution)/shard_map/ppermute | solution.py:463
  29.8 2.1 %collective-permute-done.10.refs_4_ = bf16[2,128,384]{2,1,0:T(8,128)(2,1)S(1)} collective-permute-done((bf16[2,128,384]{2,1,0:T(8,128)(2,1)S(1)}, bf16[2,128,384]{2,1,0:T(8,128)(2,1)S(1)}, u32[]{:S(2)}, u32[]{:S(2)}) %collective-permute-start.10) | collective-permute-done | bytes 196640 | tf_op jit(solution)/shard_map/ppermute | solution.py:463
  31.9 2.5 %collective-permute-start.11 = (bf16[2,128,384]{2,1,0:T(8,128)(2,1)S(1)}, bf16[2,128,384]{2,1,0:T(8,128)(2,1)S(1)}, u32[]{:S(2)}, u32[]{:S(2)}) collective-permute-start(bf16[2,128,384]{2,1,0:T(8,128)(2,1)S(1)} %collective-permute-done.10.refs_4_), channel_id=1, source_target_pairs={{0,8},{2,6},{4,0},{6,14},{8,16},{10,2},{12,4},{14,22},{16,24},{18,... | collective-permute-start | bytes 589832 | tf_op jit(solution)/shard_map/ppermute | solution.py:534
  34.4 1.5 %norm_video.1 = (bf16[128,768]{1,0:T(8,128)(2,1)S(1)}, bf16[2,128,768]{2,1,0:T(8,128)(2,1)}, bf16[2,128,768]{2,1,0:T(8,128)(2,1)S(1)}) custom-call(f32[144,2304]{1,0:T(8,128)S(1)} %get-tuple-element.40.own_ref.top_ref, bf16[224,2304]{1,0:T(8,128)(2,1)S(1)} %collective-permute-done.msg_ref, f32[272,128]{1,0:T(8,128)S(1)} %get-tuple-element.49.stat_ref, ...), custom_call_target="tpu_custom_call" | custom-call | flops 331776000 | bytes 2654208 | tf_op jit(solution)/shard_map/norm_video/pallas_call | solution.py:418
  35.9 2.8 %collective-permute-done.13.refs_5_ = bf16[2,128,384]{2,1,0:T(8,128)(2,1)S(1)} collective-permute-done((bf16[2,128,384]{2,1,0:T(8,128)(2,1)S(1)}, bf16[2,128,384]{2,1,0:T(8,128)(2,1)S(1)}, u32[]{:S(2)}, u32[]{:S(2)}) %collective-permute-start.13) | collective-permute-done | bytes 196640 | tf_op jit(solution)/shard_map/ppermute | solution.py:463
  38.8 0.6 %collective-permute-done.11.refs_6_ = bf16[2,128,384]{2,1,0:T(8,128)(2,1)S(1)} collective-permute-done((bf16[2,128,384]{2,1,0:T(8,128)(2,1)S(1)}, bf16[2,128,384]{2,1,0:T(8,128)(2,1)S(1)}, u32[]{:S(2)}, u32[]{:S(2)}) %collective-permute-start.11) | collective-permute-done | bytes 196640 | tf_op jit(solution)/shard_map/ppermute | solution.py:534
  40.0 2.5 %attend.2 = (f32[128,384]{1,0:T(8,128)S(1)}, f32[128,128]{1,0:T(8,128)S(1)}, f32[128,512]{1,0:T(8,128)S(1)}) custom-call(s32[2]{0:T(128)S(1)} %pad_add_fusion.place_ref, bf16[128,768]{1,0:T(8,128)(2,1)S(1)} %get-tuple-element.65.qo_ref, bf16[128,768]{1,0:T(8,128)(2,1)S(1)} %collective-permute-done.7.qp_ref, ...), custom_call_target="tpu_custom_call" | custom-call | flops 2013265920 | bytes 1966080 | tf_op jit(solution)/shard_map/attend/pallas_call | solution.py:561
  42.6 2.5 %attend.3 = (f32[128,384]{1,0:T(8,128)S(1)}, f32[128,128]{1,0:T(8,128)S(1)}, f32[128,512]{1,0:T(8,128)S(1)}) custom-call(s32[2]{0:T(128)S(1)} %pad_add_fusion.place_ref, bf16[128,768]{1,0:T(8,128)(2,1)S(1)} %get-tuple-element.65.qo_ref, bf16[128,768]{1,0:T(8,128)(2,1)S(1)} %collective-permute-done.7.qp_ref, ...), custom_call_target="tpu_custom_call" | custom-call | flops 2013265920 | bytes 1966080 | tf_op jit(solution)/shard_map/attend/pallas_call | solution.py:561
  45.8 2.2 %collective-permute-start.16 = (bf16[128,384]{1,0:T(8,128)(2,1)S(1)}, bf16[128,384]{1,0:T(8,128)(2,1)S(1)}, u32[]{:S(2)}, u32[]{:S(2)}) collective-permute-start(bf16[128,384]{1,0:T(8,128)(2,1)S(1)} %merge.2.first_ref), channel_id=1, source_target_pairs={{0,1},{1,0},{2,3},{3,2},{4,5},{5,4},{6,7},{7,6},{8,9},{9,8},{10,11... | collective-permute-start | bytes 294920 | tf_op jit(solution)/shard_map/ppermute | solution.py:584
  48.2 1.0 %collective-permute-start.17 = (bf16[128,384]{1,0:T(8,128)(2,1)S(1)}, bf16[128,384]{1,0:T(8,128)(2,1)S(1)}, u32[]{:S(2)}, u32[]{:S(2)}) collective-permute-start(bf16[128,384]{1,0:T(8,128)(2,1)S(1)} %merge.3.second_ref), channel_id=1, source_target_pairs={{0,1},{1,0},{2,3},{3,2},{4,5},{5,4},{6,7},{7,6},{8,9},{9,8},{10,11... | collective-permute-start | bytes 294920 | tf_op jit(solution)/shard_map/ppermute | solution.py:584
  49.8 1.7 %collective-permute-done.16.att_ref = bf16[128,384]{1,0:T(8,128)(2,1)S(1)} collective-permute-done((bf16[128,384]{1,0:T(8,128)(2,1)S(1)}, bf16[128,384]{1,0:T(8,128)(2,1)S(1)}, u32[]{:S(2)}, u32[]{:S(2)}) %collective-permute-start.16) | collective-permute-done | bytes 98336 | tf_op jit(solution)/shard_map/ppermute | solution.py:584
  51.8 1.3 %collective-permute-done.17.att_ref = bf16[128,384]{1,0:T(8,128)(2,1)S(1)} collective-permute-done((bf16[128,384]{1,0:T(8,128)(2,1)S(1)}, bf16[128,384]{1,0:T(8,128)(2,1)S(1)}, u32[]{:S(2)}, u32[]{:S(2)}) %collective-permute-start.17) | collective-permute-done | bytes 98336 | tf_op jit(solution)/shard_map/ppermute | solution.py:584
  53.1 1.1 %final_out.1 = bf16[128,1536]{1,0:T(8,128)(2,1)} custom-call(f32[128,1536]{1,0:T(8,128)S(1)} %more_out.1.part_ref, bf16[128,384]{1,0:T(8,128)(2,1)S(1)} %collective-permute-done.17.att_ref, bf16[768,1536]{1,0:T(8,128)(2,1)S(1)} %get-tuple-element.70.w_ref, bf16[128,1536]{1,0:T(8,128)(2,1)S(1)} %get-tuple-element.71.hidden_ref, ...), custom_call_target="tpu_custom_call" | custom-call | flops 603979776 | bytes 2359296 | tf_op jit(solution)/shard_map/final_out/pallas_call | solution.py:418
  (25 shorter events, 4.5 us)
Async XLA Ops:
  0.6 12.7 %collective-permute-start.1 = (bf16[2,128,768]{2,1,0:T(8,128)(2,1)}, bf16[2,128,768]{2,1,0:T(8,128)(2,1)S(1)}, u32[]{:S(2)}, u32[]{:S(2)}) collective-permute-start(bf16[2,128,768]{2,1,0:T(8,128)(2,1)} %refs_5_.1), channel_id=1, source_target_pairs={{0,8},{2,6},{4,0},{6,14},{8,16},{10,2},{12,4},{14,22},{16,24},{18,... | collective-permute-start | bytes 1179656 | tf_op jit(solution)/shard_map/ppermute | solution.py:463
  3.7 9.6 %collective-permute-start.2 = (bf16[2,128,768]{2,1,0:T(8,128)(2,1)}, bf16[2,128,768]{2,1,0:T(8,128)(2,1)S(1)}, u32[]{:S(2)}, u32[]{:S(2)}) collective-permute-start(bf16[2,128,768]{2,1,0:T(8,128)(2,1)} %refs_5_.1), channel_id=1, source_target_pairs={{0,4},{2,10},{4,12},{6,2},{8,0},{10,18},{12,20},{14,6},{16,8},{18,... | collective-permute-start | bytes 1179656 | tf_op jit(solution)/shard_map/ppermute | solution.py:463
  9.4 25.0 %collective-permute-start = (bf16[224,2304]{1,0:T(8,128)(2,1)S(1)}, bf16[224,2304]{1,0:T(8,128)(2,1)S(1)}, u32[]{:S(2)}, u32[]{:S(2)}) collective-permute-start(bf16[224,2304]{1,0:T(8,128)(2,1)S(1)} %get-tuple-element.41), channel_id=1, source_target_pairs={{0,1},{1,0},{2,3},{3,2},{4,5},{5,4},{6,7},{7,6},{8,9},{9,8},{10,11... | collective-permute-start | bytes 3096584 | tf_op jit(solution)/shard_map/ppermute | solution.py:500
  13.4 9.6 %collective-permute-start.3 = (bf16[2,128,384]{2,1,0:T(8,128)(2,1)S(1)}, bf16[2,128,384]{2,1,0:T(8,128)(2,1)S(1)}, u32[]{:S(2)}, u32[]{:S(2)}) collective-permute-start(bf16[2,128,384]{2,1,0:T(8,128)(2,1)S(1)} %get-tuple-element.44), channel_id=1, source_target_pairs={{0,8},{2,6},{4,0},{6,14},{8,16},{10,2},{12,4},{14,22},{16,24},{18,... | collective-permute-start | bytes 589832 | tf_op jit(solution)/shard_map/ppermute | solution.py:463
  15.0 8.0 %collective-permute-start.4 = (bf16[2,128,384]{2,1,0:T(8,128)(2,1)S(1)}, bf16[2,128,384]{2,1,0:T(8,128)(2,1)S(1)}, u32[]{:S(2)}, u32[]{:S(2)}) collective-permute-start(bf16[2,128,384]{2,1,0:T(8,128)(2,1)S(1)} %get-tuple-element.45), channel_id=1, source_target_pairs={{0,4},{2,10},{4,12},{6,2},{8,0},{10,18},{12,20},{14,6},{16,8},{18,... | collective-permute-start | bytes 589832 | tf_op jit(solution)/shard_map/ppermute | solution.py:463
  15.9 8.9 %collective-permute-start.5 = (bf16[2,128,384]{2,1,0:T(8,128)(2,1)S(1)}, bf16[2,128,384]{2,1,0:T(8,128)(2,1)S(1)}, u32[]{:S(2)}, u32[]{:S(2)}) collective-permute-start(bf16[2,128,384]{2,1,0:T(8,128)(2,1)S(1)} %get-tuple-element.46), channel_id=1, source_target_pairs={{0,8},{2,6},{4,0},{6,14},{8,16},{10,2},{12,4},{14,22},{16,24},{18,... | collective-permute-start | bytes 589832 | tf_op jit(solution)/shard_map/ppermute | solution.py:463
  17.0 8.1 %collective-permute-start.6 = (bf16[2,128,384]{2,1,0:T(8,128)(2,1)S(1)}, bf16[2,128,384]{2,1,0:T(8,128)(2,1)S(1)}, u32[]{:S(2)}, u32[]{:S(2)}) collective-permute-start(bf16[2,128,384]{2,1,0:T(8,128)(2,1)S(1)} %get-tuple-element.47), channel_id=1, source_target_pairs={{0,4},{2,10},{4,12},{6,2},{8,0},{10,18},{12,20},{14,6},{16,8},{18,... | collective-permute-start | bytes 589832 | tf_op jit(solution)/shard_map/ppermute | solution.py:463
  23.0 6.4 %collective-permute-start.8 = (bf16[2,128,384]{2,1,0:T(8,128)(2,1)S(1)}, bf16[2,128,384]{2,1,0:T(8,128)(2,1)S(1)}, u32[]{:S(2)}, u32[]{:S(2)}) collective-permute-start(bf16[2,128,384]{2,1,0:T(8,128)(2,1)S(1)} %collective-permute-done.3.refs_2_), channel_id=1, source_target_pairs={{0,8},{2,6},{4,0},{6,14},{8,16},{10,2},{12,4},{14,22},{16,24},{18,... | collective-permute-start | bytes 589832 | tf_op jit(solution)/shard_map/ppermute | solution.py:463
  25.1 6.9 %collective-permute-start.10 = (bf16[2,128,384]{2,1,0:T(8,128)(2,1)S(1)}, bf16[2,128,384]{2,1,0:T(8,128)(2,1)S(1)}, u32[]{:S(2)}, u32[]{:S(2)}) collective-permute-start(bf16[2,128,384]{2,1,0:T(8,128)(2,1)S(1)} %collective-permute-done.5.refs_2_), channel_id=1, source_target_pairs={{0,8},{2,6},{4,0},{6,14},{8,16},{10,2},{12,4},{14,22},{16,24},{18,... | collective-permute-start | bytes 589832 | tf_op jit(solution)/shard_map/ppermute | solution.py:463
  26.8 9.1 %collective-permute-start.12 = (bf16[2,128,384]{2,1,0:T(8,128)(2,1)S(1)}, bf16[2,128,384]{2,1,0:T(8,128)(2,1)S(1)}, u32[]{:S(2)}, u32[]{:S(2)}) collective-permute-start(bf16[2,128,384]{2,1,0:T(8,128)(2,1)S(1)} %collective-permute-done.4.refs_3_), channel_id=1, source_target_pairs={{0,4},{2,10},{4,12},{6,2},{8,0},{10,18},{12,20},{14,6},{16,8},{18,... | collective-permute-start | bytes 589832 | tf_op jit(solution)/shard_map/ppermute | solution.py:463
  27.3 11.4 %collective-permute-start.13 = (bf16[2,128,384]{2,1,0:T(8,128)(2,1)S(1)}, bf16[2,128,384]{2,1,0:T(8,128)(2,1)S(1)}, u32[]{:S(2)}, u32[]{:S(2)}) collective-permute-start(bf16[2,128,384]{2,1,0:T(8,128)(2,1)S(1)} %collective-permute-done.6.refs_3_), channel_id=1, source_target_pairs={{0,4},{2,10},{4,12},{6,2},{8,0},{10,18},{12,20},{14,6},{16,8},{18,... | collective-permute-start | bytes 589832 | tf_op jit(solution)/shard_map/ppermute | solution.py:463
  29.3 9.4 %collective-permute-start.9 = (bf16[2,128,384]{2,1,0:T(8,128)(2,1)S(1)}, bf16[2,128,384]{2,1,0:T(8,128)(2,1)S(1)}, u32[]{:S(2)}, u32[]{:S(2)}) collective-permute-start(bf16[2,128,384]{2,1,0:T(8,128)(2,1)S(1)} %collective-permute-done.8.refs_4_), channel_id=1, source_target_pairs={{0,8},{2,6},{4,0},{6,14},{8,16},{10,2},{12,4},{14,22},{16,24},{18,... | collective-permute-start | bytes 589832 | tf_op jit(solution)/shard_map/ppermute | solution.py:534
  31.9 7.4 %collective-permute-start.11 = (bf16[2,128,384]{2,1,0:T(8,128)(2,1)S(1)}, bf16[2,128,384]{2,1,0:T(8,128)(2,1)S(1)}, u32[]{:S(2)}, u32[]{:S(2)}) collective-permute-start(bf16[2,128,384]{2,1,0:T(8,128)(2,1)S(1)} %collective-permute-done.10.refs_4_), channel_id=1, source_target_pairs={{0,8},{2,6},{4,0},{6,14},{8,16},{10,2},{12,4},{14,22},{16,24},{18,... | collective-permute-start | bytes 589832 | tf_op jit(solution)/shard_map/ppermute | solution.py:534
  35.9 4.0 %collective-permute-start.7 = (bf16[128,768]{1,0:T(8,128)(2,1)S(1)}, bf16[128,768]{1,0:T(8,128)(2,1)S(1)}, u32[]{:S(2)}, u32[]{:S(2)}) collective-permute-start(bf16[128,768]{1,0:T(8,128)(2,1)S(1)} %get-tuple-element.65.qo_ref), channel_id=1, source_target_pairs={{0,2},{2,0},{4,6},{6,4},{8,10},{10,8},{12,14},{14,12},{16,18},{18,... | collective-permute-start | bytes 589832 | tf_op jit(solution)/shard_map/ppermute | solution.py:545
  42.5 3.2 %collective-permute-start.14 = (f32[128,512]{1,0:T(8,128)S(1)}, f32[128,512]{1,0:T(8,128)S(1)}, u32[]{:S(2)}, u32[]{:S(2)}) collective-permute-start(f32[128,512]{1,0:T(8,128)S(1)} %get-tuple-element.64), channel_id=1, source_target_pairs={{0,2},{2,0},{4,6},{6,4},{8,10},{10,8},{12,14},{14,12},{16,18},{18,... | collective-permute-start | bytes 786440 | tf_op jit(solution)/shard_map/ppermute | solution.py:576
  45.1 2.9 %collective-permute-start.15 = (f32[128,512]{1,0:T(8,128)S(1)}, f32[128,512]{1,0:T(8,128)S(1)}, u32[]{:S(2)}, u32[]{:S(2)}) collective-permute-start(f32[128,512]{1,0:T(8,128)S(1)} %get-tuple-element.68), channel_id=1, source_target_pairs={{0,2},{2,0},{4,6},{6,4},{8,10},{10,8},{12,14},{14,12},{16,18},{18,... | collective-permute-start | bytes 786440 | tf_op jit(solution)/shard_map/ppermute | solution.py:576
  45.8 5.6 %collective-permute-start.16 = (bf16[128,384]{1,0:T(8,128)(2,1)S(1)}, bf16[128,384]{1,0:T(8,128)(2,1)S(1)}, u32[]{:S(2)}, u32[]{:S(2)}) collective-permute-start(bf16[128,384]{1,0:T(8,128)(2,1)S(1)} %merge.2.first_ref), channel_id=1, source_target_pairs={{0,1},{1,0},{2,3},{3,2},{4,5},{5,4},{6,7},{7,6},{8,9},{9,8},{10,11... | collective-permute-start | bytes 294920 | tf_op jit(solution)/shard_map/ppermute | solution.py:584
  48.2 4.9 %collective-permute-start.17 = (bf16[128,384]{1,0:T(8,128)(2,1)S(1)}, bf16[128,384]{1,0:T(8,128)(2,1)S(1)}, u32[]{:S(2)}, u32[]{:S(2)}) collective-permute-start(bf16[128,384]{1,0:T(8,128)(2,1)S(1)} %merge.3.second_ref), channel_id=1, source_target_pairs={{0,1},{1,0},{2,3},{3,2},{4,5},{5,4},{6,7},{7,6},{8,9},{9,8},{10,11... | collective-permute-start | bytes 294920 | tf_op jit(solution)/shard_map/ppermute | solution.py:584

commit v10 on v9

--- a/solution.py
+++ b/solution.py
@@ -245,10 +245,10 @@
 
 
 def norm_kernel(
-    total_features, text, own_ref, msg_ref, stat_ref, qg_ref, kg_ref, q_ref, cache_ref, kv_ref,
+    total_features, text, own_ref, msg_ref, stat_ref, qg_ref, kg_ref, qa_ref, qb_ref, cache_ref, kv_ref,
 ):
-    video = q_ref.shape[0]
-    heads = q_ref.shape[1] // HEAD_DIM
+    video = qa_ref.shape[0]
+    half = qa_ref.shape[1] // HEAD_DIM
     query_gain = qg_ref[...].reshape(1, HEAD_DIM)
     key_gain = kg_ref[...].reshape(1, HEAD_DIM)
     stats = received_stats(msg_ref, video, text)[:, :video]
@@ -260,9 +260,11 @@
         both = own_ref[:video, cells] + msg_ref[:video, cells].astype(F32)
         return (both + gap * scale) * inverse + shift
 
-    for head in range(heads):
+    for head in range(2 * half):
         columns = slice(head * HEAD_DIM, (head + 1) * HEAD_DIM)
-        q_ref[:, columns] = head_norm(total(3 * head), query_gain).astype(BF16)
+        cells = slice(head % half * HEAD_DIM, (head % half + 1) * HEAD_DIM)
+        q_ref = qa_ref if head < half else qb_ref
+        q_ref[:, cells] = head_norm(total(3 * head), query_gain).astype(BF16)
         keys = head_norm(total(3 * head + 1), key_gain).astype(BF16)
         values = total(3 * head + 2).astype(BF16)
         cache_ref[0, :, columns] = keys
@@ -338,7 +340,7 @@
     for head in range(width // HEAD_DIM):
         cells = slice(head * HEAD_DIM, (head + 1) * HEAD_DIM)
         columns = slice((first + head) * HEAD_DIM, (first + head + 1) * HEAD_DIM)
-        own, other = qo_ref[:, columns], qp_ref[:, columns]
+        own, other = qo_ref[:, cells], qp_ref[:, cells]
         queries = jnp.concatenate([own, other], axis=0)
         fresh = weigh(own, fresh_ref[0, :, columns])
         stale = weigh(other, stale_ref[0, :, columns])
@@ -535,20 +537,20 @@
     ends = [chain[-1][1] for chain in chains]
 
     received = lax.optimization_barrier((received, *chains[0][0], *chains[1][0]))[0]
-    queries, new_cache, fresh = plain_call(
+    *queries, new_cache, fresh = plain_call(
         functools.partial(norm_kernel, features * 2, text),
-        [((video, width), BF16), ((2, video, width), BF16), ((2, video, width), BF16)],
+        [((video, width // 2), BF16)] * 2 + [((2, video, width), BF16)] * 2,
         "norm_video",
         cost(1000 * top * group_columns, 8 * top * group_columns),
         own, received, stats, query_gain, key_gain,
     )
-    other_queries = lax.ppermute(queries, "section", swap_core)
+    other_queries = [lax.ppermute(half, "section", swap_core) for half in queries]
     (text_kv,) = plain_call(
         functools.partial(text_kernel, features * 2),
         [((2, text, width), BF16)],
         "norm_text",
-        cost(1000 * text * group_columns, 8 * text * group_columns),
-        own_text, lax.optimization_barrier((received, *far, *ends))[0], stats, own, key_gain,
+        cost(text * group_columns, text * group_columns),
+        own_text, lax.optimization_barrier((received, far[0], ends[0]))[0], stats, own, key_gain,
     )
 
     context = chips * video + video + text
@@ -556,8 +558,9 @@
     for index, chain in enumerate(chains):
         first = index * heads // 2
         halves = [block for step in chain for block in step] + [far[index]]
+        own_queries = queries[index]
         if attended:
-            queries = lax.optimization_barrier((queries, num_own))[0]
+            own_queries = lax.optimization_barrier((own_queries, num_own))[0]
         num_own, den_own, num_message = pl.pallas_call(
             functools.partial(attend_kernel, first, len(whole)),
             in_specs=[smem] + [vmem] * (6 + len(whole) + len(halves)),
@@ -569,10 +572,13 @@
             ],
             compiler_params=params(24),
             cost_estimate=cost(
-                16 * video * context * width, 2 * context * width, video * context * heads
+                video * context, context * width, video * heads
             ),
             name="attend",
-        )(place, queries, other_queries, fresh, stale, text_kv, text_mask, *whole, *halves)
+        )(
+            place, own_queries, other_queries[index], fresh, stale, text_kv, text_mask,
+            *whole, *halves,
+        )
         num_received = lax.ppermute(num_message, "section", swap_core)
         attended += plain_call(
             functools.partial(merge_kernel, first),

time: 54.4 us -> 51.6 us (0.949)
  waiting for transfers between devices: 11.3 us -> 8.58 us
    ppermute x10, waiting for transfers between devices: 7.75 us -> 5.41 us  [ring_step(): lax.ppermute(block, 'section', way)]
    ppermute x10, starting transfers between devices: 13 us -> 11.9 us  [ring_step(): lax.ppermute(block, 'section', way)]
    ppermute x2, starting transfers between devices: 2.96 us -> 3.59 us  [per_device(): far = [lax.ppermute(chain[-1][0], 'section', ways[0]) for chain in chains]]
  transfers between devices with their start and end apart: 18 -> 19, of which waited for: 8 -> 9; matrix products, arithmetic and copies ran while one was open for 0% -> 0% of each run, Pallas kernels for 31% -> 37%
where the time goes in v10:
time: 51.6 us; the launch traced here: 51.5 us
  starting transfers between devices  21.8 us (42%)
  Pallas kernels  20.3 us (39%)
  waiting for transfers between devices  8.58 us (17%)
  between operations  0.73 us (1%)
    ppermute x10, starting transfers between devices, ring_step(): lax.ppermute(block, 'section', way)  11.9 us
    pallas_call x1, Pallas kernels, per_device(): pl.pallas_call(send_kernel, in_specs=[smem] + [hbm] * 5, out_specs=[vmem]...  5.63 us
    ppermute x10, waiting for transfers between devices, ring_step(): lax.ppermute(block, 'section', way)  5.41 us
    pallas_call x2, Pallas kernels, per_device(): pl.pallas_call(functools.partial(attend_kernel, first, len(whole)), in_sp...  5.06 us
    pallas_call x1, Pallas kernels, per_device(): pl.pallas_call(own_kernel, in_specs=[smem, vmem, vmem, hbm, hbm] + [hbm]...  5.05 us
    pallas_call x8, Pallas kernels, plain_call(): pl.pallas_call(kernel, in_specs=[pl.BlockSpec(memory_space=pltpu.VMEM)] *...  4.51 us
    ppermute x2, starting transfers between devices, per_device(): far = [lax.ppermute(chain[-1][0], 'section', ways[0]) for chain in chains]  3.59 us
    ppermute x2, starting transfers between devices, per_device(): other_attended.append(lax.ppermute(attended[-1], 'head', swap_head))  3.15 us
  transfers between devices with their start and end apart: 19, of which 9 were waited for; matrix products, arithmetic and copies ran while one was open for 0% of the time, Pallas kernels for 37%

profile of v10, /device:TPU:0, one launch (start us, length us, event | category | flops | bytes accessed | tf_op | source)
XLA Modules:
  0.0 51.5 jit_solution(6819979049449814692)
XLA Ops:
  0.6 3.1 %collective-permute-start.1 = (bf16[2,128,768]{2,1,0:T(8,128)(2,1)}, bf16[2,128,768]{2,1,0:T(8,128)(2,1)S(1)}, u32[]{:S(2)}, u32[]{:S(2)}) collective-permute-start(bf16[2,128,768]{2,1,0:T(8,128)(2,1)} %refs_5_.1), channel_id=1, source_target_pairs={{0,8},{2,6},{4,0},{6,14},{8,16},{10,2},{12,4},{14,22},{16,24},{18,... | collective-permute-start | bytes 1179656 | tf_op jit(solution)/shard_map/ppermute | solution.py:465
  3.8 5.6 %project_send.1 = (bf16[272,1536]{1,0:T(8,128)(2,1)S(1)}, bf16[224,2304]{1,0:T(8,128)(2,1)S(1)}, f32[272,128]{1,0:T(8,128)S(1)}, bf16[2,1536,768]{2,1,0:T(8,128)(2,1)S(1)}) custom-call(s32[2]{0:T(128)S(1)} %pad_add_fusion.place_ref, bf16[128,1536]{1,0:T(8,128)(2,1)} %refs_4_.1, bf16[256,1536]{1,0:T(8,128)(2,1)} %t_ref.1, f32[1536]{0:T(1024)} %scale_ref.1, ...), custom_call_target="tpu_custom_call" | custom-call | flops 7700742144 | bytes 7077888 | tf_op jit(solution)/shard_map/project_send/pallas_call | solution.py:478
  9.4 2.0 %collective-permute-start = (bf16[224,2304]{1,0:T(8,128)(2,1)S(1)}, bf16[224,2304]{1,0:T(8,128)(2,1)S(1)}, u32[]{:S(2)}, u32[]{:S(2)}) collective-permute-start(bf16[224,2304]{1,0:T(8,128)(2,1)S(1)} %get-tuple-element.42), channel_id=1, source_target_pairs={{0,1},{1,0},{2,3},{3,2},{4,5},{5,4},{6,7},{7,6},{8,9},{9,8},{10,11... | collective-permute-start | bytes 3096584 | tf_op jit(solution)/shard_map/ppermute | solution.py:502
  11.4 1.9 %collective-permute-done.1.refs_0_ = bf16[2,128,768]{2,1,0:T(8,128)(2,1)S(1)} collective-permute-done((bf16[2,128,768]{2,1,0:T(8,128)(2,1)}, bf16[2,128,768]{2,1,0:T(8,128)(2,1)S(1)}, u32[]{:S(2)}, u32[]{:S(2)}) %collective-permute-start.1) | collective-permute-done | bytes 393248 | tf_op jit(solution)/shard_map/ppermute | solution.py:465
  13.4 1.6 %collective-permute-start.3 = (bf16[2,128,384]{2,1,0:T(8,128)(2,1)S(1)}, bf16[2,128,384]{2,1,0:T(8,128)(2,1)S(1)}, u32[]{:S(2)}, u32[]{:S(2)}) collective-permute-start(bf16[2,128,384]{2,1,0:T(8,128)(2,1)S(1)} %get-tuple-element.45), channel_id=1, source_target_pairs={{0,8},{2,6},{4,0},{6,14},{8,16},{10,2},{12,4},{14,22},{16,24},{18,... | collective-permute-start | bytes 589832 | tf_op jit(solution)/shard_map/ppermute | solution.py:465
  15.0 0.9 %collective-permute-start.4 = (bf16[2,128,384]{2,1,0:T(8,128)(2,1)S(1)}, bf16[2,128,384]{2,1,0:T(8,128)(2,1)S(1)}, u32[]{:S(2)}, u32[]{:S(2)}) collective-permute-start(bf16[2,128,384]{2,1,0:T(8,128)(2,1)S(1)} %get-tuple-element.46), channel_id=1, source_target_pairs={{0,4},{2,10},{4,12},{6,2},{8,0},{10,18},{12,20},{14,6},{16,8},{18,... | collective-permute-start | bytes 589832 | tf_op jit(solution)/shard_map/ppermute | solution.py:465
  15.9 1.1 %collective-permute-start.5 = (bf16[2,128,384]{2,1,0:T(8,128)(2,1)S(1)}, bf16[2,128,384]{2,1,0:T(8,128)(2,1)S(1)}, u32[]{:S(2)}, u32[]{:S(2)}) collective-permute-start(bf16[2,128,384]{2,1,0:T(8,128)(2,1)S(1)} %get-tuple-element.47), channel_id=1, source_target_pairs={{0,8},{2,6},{4,0},{6,14},{8,16},{10,2},{12,4},{14,22},{16,24},{18,... | collective-permute-start | bytes 589832 | tf_op jit(solution)/shard_map/ppermute | solution.py:465
  17.0 0.9 %collective-permute-start.6 = (bf16[2,128,384]{2,1,0:T(8,128)(2,1)S(1)}, bf16[2,128,384]{2,1,0:T(8,128)(2,1)S(1)}, u32[]{:S(2)}, u32[]{:S(2)}) collective-permute-start(bf16[2,128,384]{2,1,0:T(8,128)(2,1)S(1)} %get-tuple-element.48), channel_id=1, source_target_pairs={{0,4},{2,10},{4,12},{6,2},{8,0},{10,18},{12,20},{14,6},{16,8},{18,... | collective-permute-start | bytes 589832 | tf_op jit(solution)/shard_map/ppermute | solution.py:465
  17.9 5.0 %project_own.1 = (f32[144,2304]{1,0:T(8,128)S(1)}, f32[128,1536]{1,0:T(8,128)S(1)}, bf16[768,1536]{1,0:T(8,128)(2,1)S(1)}, bf16[768,1536]{1,0:T(8,128)(2,1)S(1)}...) custom-call(s32[2]{0:T(128)S(1)} %pad_add_fusion.place_ref, ...), custom_call_target="tpu_custom_call" | custom-call | flops 7700742144 | bytes 7077888 | tf_op jit(solution)/shard_map/project_own/pallas_call | solution.py:510
  23.0 1.2 %collective-permute-start.8 = (bf16[2,128,384]{2,1,0:T(8,128)(2,1)S(1)}, bf16[2,128,384]{2,1,0:T(8,128)(2,1)S(1)}, u32[]{:S(2)}, u32[]{:S(2)}) collective-permute-start(bf16[2,128,384]{2,1,0:T(8,128)(2,1)S(1)} %collective-permute-done.3.refs_2_), channel_id=1, source_target_pairs={{0,8},{2,6},{4,0},{6,14},{8,16},{10,2},{12,4},{14,22},{16,24},{18,... | collective-permute-start | bytes 589832 | tf_op jit(solution)/shard_map/ppermute | solution.py:465
  25.1 1.7 %collective-permute-start.13 = (bf16[2,128,384]{2,1,0:T(8,128)(2,1)S(1)}, bf16[2,128,384]{2,1,0:T(8,128)(2,1)S(1)}, u32[]{:S(2)}, u32[]{:S(2)}) collective-permute-start(bf16[2,128,384]{2,1,0:T(8,128)(2,1)S(1)} %collective-permute-done.5.refs_2_), channel_id=1, source_target_pairs={{0,8},{2,6},{4,0},{6,14},{8,16},{10,2},{12,4},{14,22},{16,24},{18,... | collective-permute-start | bytes 589832 | tf_op jit(solution)/shard_map/ppermute | solution.py:465
  27.3 1.4 %collective-permute-done.8.refs_4_ = bf16[2,128,384]{2,1,0:T(8,128)(2,1)S(1)} collective-permute-done((bf16[2,128,384]{2,1,0:T(8,128)(2,1)S(1)}, bf16[2,128,384]{2,1,0:T(8,128)(2,1)S(1)}, u32[]{:S(2)}, u32[]{:S(2)}) %collective-permute-start.8) | collective-permute-done | bytes 196640 | tf_op jit(solution)/shard_map/ppermute | solution.py:465
  28.7 1.1 %collective-permute-start.9 = (bf16[2,128,384]{2,1,0:T(8,128)(2,1)S(1)}, bf16[2,128,384]{2,1,0:T(8,128)(2,1)S(1)}, u32[]{:S(2)}, u32[]{:S(2)}) collective-permute-start(bf16[2,128,384]{2,1,0:T(8,128)(2,1)S(1)} %collective-permute-done.8.refs_4_), channel_id=1, source_target_pairs={{0,8},{2,6},{4,0},{6,14},{8,16},{10,2},{12,4},{14,22},{16,24},{18,... | collective-permute-start | bytes 589832 | tf_op jit(solution)/shard_map/ppermute | solution.py:536
  29.8 0.9 %collective-permute-start.14 = (bf16[2,128,384]{2,1,0:T(8,128)(2,1)S(1)}, bf16[2,128,384]{2,1,0:T(8,128)(2,1)S(1)}, u32[]{:S(2)}, u32[]{:S(2)}) collective-permute-start(bf16[2,128,384]{2,1,0:T(8,128)(2,1)S(1)} %collective-permute-done.6.refs_3_), channel_id=1, source_target_pairs={{0,4},{2,10},{4,12},{6,2},{8,0},{10,18},{12,20},{14,6},{16,8},{18,... | collective-permute-start | bytes 589832 | tf_op jit(solution)/shard_map/ppermute | solution.py:465
  30.7 1.2 %collective-permute-done.13.refs_4_ = bf16[2,128,384]{2,1,0:T(8,128)(2,1)S(1)} collective-permute-done((bf16[2,128,384]{2,1,0:T(8,128)(2,1)S(1)}, bf16[2,128,384]{2,1,0:T(8,128)(2,1)S(1)}, u32[]{:S(2)}, u32[]{:S(2)}) %collective-permute-start.13) | collective-permute-done | bytes 196640 | tf_op jit(solution)/shard_map/ppermute | solution.py:465
  31.9 2.5 %collective-permute-start.15 = (bf16[2,128,384]{2,1,0:T(8,128)(2,1)S(1)}, bf16[2,128,384]{2,1,0:T(8,128)(2,1)S(1)}, u32[]{:S(2)}, u32[]{:S(2)}) collective-permute-start(bf16[2,128,384]{2,1,0:T(8,128)(2,1)S(1)} %collective-permute-done.13.refs_4_), channel_id=1, source_target_pairs={{0,8},{2,6},{4,0},{6,14},{8,16},{10,2},{12,4},{14,22},{16,24},{18,... | collective-permute-start | bytes 589832 | tf_op jit(solution)/shard_map/ppermute | solution.py:536
  34.4 1.5 %norm_video.1 = (bf16[128,384]{1,0:T(8,128)(2,1)S(1)}, bf16[128,384]{1,0:T(8,128)(2,1)S(1)}, bf16[2,128,768]{2,1,0:T(8,128)(2,1)}, bf16[2,128,768]{2,1,0:T(8,128)(2,1)S(1)}) custom-call(f32[144,2304]{1,0:T(8,128)S(1)} %get-tuple-element.41.own_ref.top_ref, bf16[224,2304]{1,0:T(8,128)(2,1)S(1)} %collective-permute-done.msg_ref, ...), custom_call_target="tpu_custom_call" | custom-call | flops 331776000 | bytes 2654208 | tf_op jit(solution)/shard_map/norm_video/pallas_call | solution.py:420
  37.2 2.5 %attend.2 = (f32[128,384]{1,0:T(8,128)S(1)}, f32[128,128]{1,0:T(8,128)S(1)}, f32[128,512]{1,0:T(8,128)S(1)}) custom-call(s32[2]{0:T(128)S(1)} %pad_add_fusion.place_ref, bf16[128,384]{1,0:T(8,128)(2,1)S(1)} %get-tuple-element.53.qo_ref, bf16[128,384]{1,0:T(8,128)(2,1)S(1)} %collective-permute-done.7.qp_ref, ...), custom_call_target="tpu_custom_call" | custom-call | flops 163840 | bytes 983040 | tf_op jit(solution)/shard_map/attend/pallas_call | solution.py:564
  40.0 2.5 %attend.3 = (f32[128,384]{1,0:T(8,128)S(1)}, f32[128,128]{1,0:T(8,128)S(1)}, f32[128,512]{1,0:T(8,128)S(1)}) custom-call(s32[2]{0:T(128)S(1)} %pad_add_fusion.place_ref, bf16[128,384]{1,0:T(8,128)(2,1)S(1)} %get-tuple-element.65.qo_ref, bf16[128,384]{1,0:T(8,128)(2,1)S(1)} %collective-permute-done.12.qp_ref, ...), custom_call_target="tpu_custom_call" | custom-call | flops 163840 | bytes 983040 | tf_op jit(solution)/shard_map/attend/pallas_call | solution.py:564
  43.1 2.1 %collective-permute-start.17 = (bf16[128,384]{1,0:T(8,128)(2,1)S(1)}, bf16[128,384]{1,0:T(8,128)(2,1)S(1)}, u32[]{:S(2)}, u32[]{:S(2)}) collective-permute-start(bf16[128,384]{1,0:T(8,128)(2,1)S(1)} %merge.2.first_ref), channel_id=1, source_target_pairs={{0,1},{1,0},{2,3},{3,2},{4,5},{5,4},{6,7},{7,6},{8,9},{9,8},{10,11... | collective-permute-start | bytes 294920 | tf_op jit(solution)/shard_map/ppermute | solution.py:590
  45.4 1.0 %collective-permute-start.18 = (bf16[128,384]{1,0:T(8,128)(2,1)S(1)}, bf16[128,384]{1,0:T(8,128)(2,1)S(1)}, u32[]{:S(2)}, u32[]{:S(2)}) collective-permute-start(bf16[128,384]{1,0:T(8,128)(2,1)S(1)} %merge.3.second_ref), channel_id=1, source_target_pairs={{0,1},{1,0},{2,3},{3,2},{4,5},{5,4},{6,7},{7,6},{8,9},{9,8},{10,11... | collective-permute-start | bytes 294920 | tf_op jit(solution)/shard_map/ppermute | solution.py:590
  47.0 1.7 %collective-permute-done.17.att_ref = bf16[128,384]{1,0:T(8,128)(2,1)S(1)} collective-permute-done((bf16[128,384]{1,0:T(8,128)(2,1)S(1)}, bf16[128,384]{1,0:T(8,128)(2,1)S(1)}, u32[]{:S(2)}, u32[]{:S(2)}) %collective-permute-start.17) | collective-permute-done | bytes 98336 | tf_op jit(solution)/shard_map/ppermute | solution.py:590
  49.0 1.3 %collective-permute-done.18.att_ref = bf16[128,384]{1,0:T(8,128)(2,1)S(1)} collective-permute-done((bf16[128,384]{1,0:T(8,128)(2,1)S(1)}, bf16[128,384]{1,0:T(8,128)(2,1)S(1)}, u32[]{:S(2)}, u32[]{:S(2)}) %collective-permute-start.18) | collective-permute-done | bytes 98336 | tf_op jit(solution)/shard_map/ppermute | solution.py:590
  50.3 1.1 %final_out.1 = bf16[128,1536]{1,0:T(8,128)(2,1)} custom-call(f32[128,1536]{1,0:T(8,128)S(1)} %more_out.1.part_ref, bf16[128,384]{1,0:T(8,128)(2,1)S(1)} %collective-permute-done.18.att_ref, bf16[768,1536]{1,0:T(8,128)(2,1)S(1)} %get-tuple-element.72.w_ref, bf16[128,1536]{1,0:T(8,128)(2,1)S(1)} %get-tuple-element.73.hidden_ref, ...), custom_call_target="tpu_custom_call" | custom-call | flops 603979776 | bytes 2359296 | tf_op jit(solution)/shard_map/final_out/pallas_call | solution.py:420
  (27 shorter events, 4.8 us)
Async XLA Ops:
  0.6 12.7 %collective-permute-start.1 = (bf16[2,128,768]{2,1,0:T(8,128)(2,1)}, bf16[2,128,768]{2,1,0:T(8,128)(2,1)S(1)}, u32[]{:S(2)}, u32[]{:S(2)}) collective-permute-start(bf16[2,128,768]{2,1,0:T(8,128)(2,1)} %refs_5_.1), channel_id=1, source_target_pairs={{0,8},{2,6},{4,0},{6,14},{8,16},{10,2},{12,4},{14,22},{16,24},{18,... | collective-permute-start | bytes 1179656 | tf_op jit(solution)/shard_map/ppermute | solution.py:465
  3.7 9.6 %collective-permute-start.2 = (bf16[2,128,768]{2,1,0:T(8,128)(2,1)}, bf16[2,128,768]{2,1,0:T(8,128)(2,1)S(1)}, u32[]{:S(2)}, u32[]{:S(2)}) collective-permute-start(bf16[2,128,768]{2,1,0:T(8,128)(2,1)} %refs_5_.1), channel_id=1, source_target_pairs={{0,4},{2,10},{4,12},{6,2},{8,0},{10,18},{12,20},{14,6},{16,8},{18,... | collective-permute-start | bytes 1179656 | tf_op jit(solution)/shard_map/ppermute | solution.py:465
  9.4 25.0 %collective-permute-start = (bf16[224,2304]{1,0:T(8,128)(2,1)S(1)}, bf16[224,2304]{1,0:T(8,128)(2,1)S(1)}, u32[]{:S(2)}, u32[]{:S(2)}) collective-permute-start(bf16[224,2304]{1,0:T(8,128)(2,1)S(1)} %get-tuple-element.42), channel_id=1, source_target_pairs={{0,1},{1,0},{2,3},{3,2},{4,5},{5,4},{6,7},{7,6},{8,9},{9,8},{10,11... | collective-permute-start | bytes 3096584 | tf_op jit(solution)/shard_map/ppermute | solution.py:502
  13.4 9.6 %collective-permute-start.3 = (bf16[2,128,384]{2,1,0:T(8,128)(2,1)S(1)}, bf16[2,128,384]{2,1,0:T(8,128)(2,1)S(1)}, u32[]{:S(2)}, u32[]{:S(2)}) collective-permute-start(bf16[2,128,384]{2,1,0:T(8,128)(2,1)S(1)} %get-tuple-element.45), channel_id=1, source_target_pairs={{0,8},{2,6},{4,0},{6,14},{8,16},{10,2},{12,4},{14,22},{16,24},{18,... | collective-permute-start | bytes 589832 | tf_op jit(solution)/shard_map/ppermute | solution.py:465
  15.0 8.0 %collective-permute-start.4 = (bf16[2,128,384]{2,1,0:T(8,128)(2,1)S(1)}, bf16[2,128,384]{2,1,0:T(8,128)(2,1)S(1)}, u32[]{:S(2)}, u32[]{:S(2)}) collective-permute-start(bf16[2,128,384]{2,1,0:T(8,128)(2,1)S(1)} %get-tuple-element.46), channel_id=1, source_target_pairs={{0,4},{2,10},{4,12},{6,2},{8,0},{10,18},{12,20},{14,6},{16,8},{18,... | collective-permute-start | bytes 589832 | tf_op jit(solution)/shard_map/ppermute | solution.py:465
  15.9 8.9 %collective-permute-start.5 = (bf16[2,128,384]{2,1,0:T(8,128)(2,1)S(1)}, bf16[2,128,384]{2,1,0:T(8,128)(2,1)S(1)}, u32[]{:S(2)}, u32[]{:S(2)}) collective-permute-start(bf16[2,128,384]{2,1,0:T(8,128)(2,1)S(1)} %get-tuple-element.47), channel_id=1, source_target_pairs={{0,8},{2,6},{4,0},{6,14},{8,16},{10,2},{12,4},{14,22},{16,24},{18,... | collective-permute-start | bytes 589832 | tf_op jit(solution)/shard_map/ppermute | solution.py:465
  17.0 8.1 %collective-permute-start.6 = (bf16[2,128,384]{2,1,0:T(8,128)(2,1)S(1)}, bf16[2,128,384]{2,1,0:T(8,128)(2,1)S(1)}, u32[]{:S(2)}, u32[]{:S(2)}) collective-permute-start(bf16[2,128,384]{2,1,0:T(8,128)(2,1)S(1)} %get-tuple-element.48), channel_id=1, source_target_pairs={{0,4},{2,10},{4,12},{6,2},{8,0},{10,18},{12,20},{14,6},{16,8},{18,... | collective-permute-start | bytes 589832 | tf_op jit(solution)/shard_map/ppermute | solution.py:465
  23.0 5.7 %collective-permute-start.8 = (bf16[2,128,384]{2,1,0:T(8,128)(2,1)S(1)}, bf16[2,128,384]{2,1,0:T(8,128)(2,1)S(1)}, u32[]{:S(2)}, u32[]{:S(2)}) collective-permute-start(bf16[2,128,384]{2,1,0:T(8,128)(2,1)S(1)} %collective-permute-done.3.refs_2_), channel_id=1, source_target_pairs={{0,8},{2,6},{4,0},{6,14},{8,16},{10,2},{12,4},{14,22},{16,24},{18,... | collective-permute-start | bytes 589832 | tf_op jit(solution)/shard_map/ppermute | solution.py:465
  25.1 6.9 %collective-permute-start.13 = (bf16[2,128,384]{2,1,0:T(8,128)(2,1)S(1)}, bf16[2,128,384]{2,1,0:T(8,128)(2,1)S(1)}, u32[]{:S(2)}, u32[]{:S(2)}) collective-permute-start(bf16[2,128,384]{2,1,0:T(8,128)(2,1)S(1)} %collective-permute-done.5.refs_2_), channel_id=1, source_target_pairs={{0,8},{2,6},{4,0},{6,14},{8,16},{10,2},{12,4},{14,22},{16,24},{18,... | collective-permute-start | bytes 589832 | tf_op jit(solution)/shard_map/ppermute | solution.py:465
  26.8 9.1 %collective-permute-start.10 = (bf16[2,128,384]{2,1,0:T(8,128)(2,1)S(1)}, bf16[2,128,384]{2,1,0:T(8,128)(2,1)S(1)}, u32[]{:S(2)}, u32[]{:S(2)}) collective-permute-start(bf16[2,128,384]{2,1,0:T(8,128)(2,1)S(1)} %collective-permute-done.4.refs_3_), channel_id=1, source_target_pairs={{0,4},{2,10},{4,12},{6,2},{8,0},{10,18},{12,20},{14,6},{16,8},{18,... | collective-permute-start | bytes 589832 | tf_op jit(solution)/shard_map/ppermute | solution.py:465
  28.7 7.8 %collective-permute-start.9 = (bf16[2,128,384]{2,1,0:T(8,128)(2,1)S(1)}, bf16[2,128,384]{2,1,0:T(8,128)(2,1)S(1)}, u32[]{:S(2)}, u32[]{:S(2)}) collective-permute-start(bf16[2,128,384]{2,1,0:T(8,128)(2,1)S(1)} %collective-permute-done.8.refs_4_), channel_id=1, source_target_pairs={{0,8},{2,6},{4,0},{6,14},{8,16},{10,2},{12,4},{14,22},{16,24},{18,... | collective-permute-start | bytes 589832 | tf_op jit(solution)/shard_map/ppermute | solution.py:536
  29.8 10.2 %collective-permute-start.14 = (bf16[2,128,384]{2,1,0:T(8,128)(2,1)S(1)}, bf16[2,128,384]{2,1,0:T(8,128)(2,1)S(1)}, u32[]{:S(2)}, u32[]{:S(2)}) collective-permute-start(bf16[2,128,384]{2,1,0:T(8,128)(2,1)S(1)} %collective-permute-done.6.refs_3_), channel_id=1, source_target_pairs={{0,4},{2,10},{4,12},{6,2},{8,0},{10,18},{12,20},{14,6},{16,8},{18,... | collective-permute-start | bytes 589832 | tf_op jit(solution)/shard_map/ppermute | solution.py:465
  31.9 8.0 %collective-permute-start.15 = (bf16[2,128,384]{2,1,0:T(8,128)(2,1)S(1)}, bf16[2,128,384]{2,1,0:T(8,128)(2,1)S(1)}, u32[]{:S(2)}, u32[]{:S(2)}) collective-permute-start(bf16[2,128,384]{2,1,0:T(8,128)(2,1)S(1)} %collective-permute-done.13.refs_4_), channel_id=1, source_target_pairs={{0,8},{2,6},{4,0},{6,14},{8,16},{10,2},{12,4},{14,22},{16,24},{18,... | collective-permute-start | bytes 589832 | tf_op jit(solution)/shard_map/ppermute | solution.py:536
  35.9 1.3 %collective-permute-start.7 = (bf16[128,384]{1,0:T(8,128)(2,1)S(1)}, bf16[128,384]{1,0:T(8,128)(2,1)S(1)}, u32[]{:S(2)}, u32[]{:S(2)}) collective-permute-start(bf16[128,384]{1,0:T(8,128)(2,1)S(1)} %get-tuple-element.53.qo_ref), channel_id=1, source_target_pairs={{0,2},{2,0},{4,6},{6,4},{8,10},{10,8},{12,14},{14,12},{16,18},{18,... | collective-permute-start | bytes 294920 | tf_op jit(solution)/shard_map/ppermute | solution.py:547
  35.9 4.0 %collective-permute-start.12 = (bf16[128,384]{1,0:T(8,128)(2,1)S(1)}, bf16[128,384]{1,0:T(8,128)(2,1)S(1)}, u32[]{:S(2)}, u32[]{:S(2)}) collective-permute-start(bf16[128,384]{1,0:T(8,128)(2,1)S(1)} %get-tuple-element.65.qo_ref), channel_id=1, source_target_pairs={{0,2},{2,0},{4,6},{6,4},{8,10},{10,8},{12,14},{14,12},{16,18},{18,... | collective-permute-start | bytes 294920 | tf_op jit(solution)/shard_map/ppermute | solution.py:547
  39.8 3.2 %collective-permute-start.11 = (f32[128,512]{1,0:T(8,128)S(1)}, f32[128,512]{1,0:T(8,128)S(1)}, u32[]{:S(2)}, u32[]{:S(2)}) collective-permute-start(f32[128,512]{1,0:T(8,128)S(1)} %get-tuple-element.63), channel_id=1, source_target_pairs={{0,2},{2,0},{4,6},{6,4},{8,10},{10,8},{12,14},{14,12},{16,18},{18,... | collective-permute-start | bytes 786440 | tf_op jit(solution)/shard_map/ppermute | solution.py:582
  42.5 2.7 %collective-permute-start.16 = (f32[128,512]{1,0:T(8,128)S(1)}, f32[128,512]{1,0:T(8,128)S(1)}, u32[]{:S(2)}, u32[]{:S(2)}) collective-permute-start(f32[128,512]{1,0:T(8,128)S(1)} %get-tuple-element.70), channel_id=1, source_target_pairs={{0,2},{2,0},{4,6},{6,4},{8,10},{10,8},{12,14},{14,12},{16,18},{18,... | collective-permute-start | bytes 786440 | tf_op jit(solution)/shard_map/ppermute | solution.py:582
  43.1 5.6 %collective-permute-start.17 = (bf16[128,384]{1,0:T(8,128)(2,1)S(1)}, bf16[128,384]{1,0:T(8,128)(2,1)S(1)}, u32[]{:S(2)}, u32[]{:S(2)}) collective-permute-start(bf16[128,384]{1,0:T(8,128)(2,1)S(1)} %merge.2.first_ref), channel_id=1, source_target_pairs={{0,1},{1,0},{2,3},{3,2},{4,5},{5,4},{6,7},{7,6},{8,9},{9,8},{10,11... | collective-permute-start | bytes 294920 | tf_op jit(solution)/shard_map/ppermute | solution.py:590
  45.4 5.0 %collective-permute-start.18 = (bf16[128,384]{1,0:T(8,128)(2,1)S(1)}, bf16[128,384]{1,0:T(8,128)(2,1)S(1)}, u32[]{:S(2)}, u32[]{:S(2)}) collective-permute-start(bf16[128,384]{1,0:T(8,128)(2,1)S(1)} %merge.3.second_ref), channel_id=1, source_target_pairs={{0,1},{1,0},{2,3},{3,2},{4,5},{5,4},{6,7},{7,6},{8,9},{9,8},{10,11... | collective-permute-start | bytes 294920 | tf_op jit(solution)/shard_map/ppermute | solution.py:590

commit v11 on v10

--- a/solution.py
+++ b/solution.py
@@ -245,7 +245,7 @@
 
 
 def norm_kernel(
-    total_features, text, own_ref, msg_ref, stat_ref, qg_ref, kg_ref, qa_ref, qb_ref, cache_ref, kv_ref,
+    total_features, text, own_ref, msg_ref, stat_ref, qg_ref, kg_ref, qa_ref, qb_ref, kv_ref,
 ):
     video = qa_ref.shape[0]
     half = qa_ref.shape[1] // HEAD_DIM
@@ -267,8 +267,6 @@
         q_ref[:, cells] = head_norm(total(3 * head), query_gain).astype(BF16)
         keys = head_norm(total(3 * head + 1), key_gain).astype(BF16)
         values = total(3 * head + 2).astype(BF16)
-        cache_ref[0, :, columns] = keys
-        cache_ref[1, :, columns] = values
         kv_ref[0, :, columns] = keys
         kv_ref[1, :, columns] = values
 
@@ -327,8 +325,13 @@
 
 
 def attend_kernel(
-    first, count, place_ref, qo_ref, qp_ref, fresh_ref, stale_ref, text_ref, mask_ref, *refs
+    first, count, copy_out, place_ref, qo_ref, qp_ref, fresh_ref, stale_ref, text_ref, mask_ref, *refs
 ):
+    if copy_out:
+        cache_ref, sem = refs[-2:]
+        refs = refs[:-2]
+        cache_copy = pltpu.make_async_copy(fresh_ref, cache_ref, sem)
+        cache_copy.start()
     own_ref, own_den_ref, msg_ref = refs[-3:]
     video, width = own_ref.shape
     text = text_ref.shape[1]
@@ -336,18 +339,20 @@
     mask = mask_ref[...].reshape(1, 2 * text).astype(F32)
     mask = jnp.where(place_ref[1] == 0, mask[:, :text], mask[:, text:])
     keep = jnp.concatenate([jnp.ones((1, video), F32), mask], axis=1)
+    same_patch = (
+        (lax.broadcasted_iota(jnp.int32, (2 * video, 2 * video), 0) < video)
+        == (lax.broadcasted_iota(jnp.int32, (2 * video, 2 * video), 1) < video)
+    ).astype(F32)
     packed = jnp.zeros((2 * video, HEAD_DIM), F32)
     for head in range(width // HEAD_DIM):
         cells = slice(head * HEAD_DIM, (head + 1) * HEAD_DIM)
         columns = slice((first + head) * HEAD_DIM, (first + head + 1) * HEAD_DIM)
-        own, other = qo_ref[:, cells], qp_ref[:, cells]
-        queries = jnp.concatenate([own, other], axis=0)
-        fresh = weigh(own, fresh_ref[0, :, columns])
-        stale = weigh(other, stale_ref[0, :, columns])
-        num = jnp.concatenate(
-            [times(fresh, fresh_ref[1, :, columns]), times(stale, stale_ref[1, :, columns])], axis=0
-        )
-        den = jnp.concatenate([fresh, stale], axis=0)
+        queries = jnp.concatenate([qo_ref[:, cells], qp_ref[:, cells]], axis=0)
+        keys = jnp.concatenate([fresh_ref[0, :, columns], stale_ref[0, :, columns]], axis=0)
+        values = jnp.concatenate([fresh_ref[1, :, columns], stale_ref[1, :, columns]], axis=0)
+        weights = weigh(queries, keys) * same_patch
+        num = times(weights, values)
+        den = lanes(weights)
         blocks = [(ref, columns) for ref in refs[:count]] + [(ref, cells) for ref in refs[count:-3]]
         blocks.append((text_ref, columns))
         for start in range(len(blocks) % 2, len(blocks), 2):
@@ -369,6 +374,8 @@
         packed = jnp.where(lane == first + head, jnp.sum(den, axis=1, keepdims=True), packed)
     own_den_ref[...] = packed[:video]
     msg_ref[:, width:] = packed[video:]
+    if copy_out:
+        cache_copy.wait()
 
 
 def merge_kernel(first, own_ref, den_ref, msg_ref, att_ref):
@@ -537,9 +544,9 @@
     ends = [chain[-1][1] for chain in chains]
 
     received = lax.optimization_barrier((received, *chains[0][0], *chains[1][0]))[0]
-    *queries, new_cache, fresh = plain_call(
+    *queries, fresh = plain_call(
         functools.partial(norm_kernel, features * 2, text),
-        [((video, width // 2), BF16)] * 2 + [((2, video, width), BF16)] * 2,
+        [((video, width // 2), BF16)] * 2 + [((2, video, width), BF16)],
         "norm_video",
         cost(1000 * top * group_columns, 8 * top * group_columns),
         own, received, stats, query_gain, key_gain,
@@ -550,7 +557,7 @@
         [((2, text, width), BF16)],
         "norm_text",
         cost(text * group_columns, text * group_columns),
-        own_text, lax.optimization_barrier((received, far[0], ends[0]))[0], stats, own, key_gain,
+        own_text, received, stats, own, key_gain,
     )
 
     context = chips * video + video + text
@@ -561,15 +568,18 @@
         own_queries = queries[index]
         if attended:
             own_queries = lax.optimization_barrier((own_queries, num_own))[0]
-        num_own, den_own, num_message = pl.pallas_call(
-            functools.partial(attend_kernel, first, len(whole)),
+        copy_out = index == 1
+        num_own, den_own, num_message, *copied = pl.pallas_call(
+            functools.partial(attend_kernel, first, len(whole), copy_out),
             in_specs=[smem] + [vmem] * (6 + len(whole) + len(halves)),
-            out_specs=[vmem] * 3,
+            out_specs=[vmem] * 3 + [hbm] * copy_out,
             out_shape=[
                 jax.ShapeDtypeStruct((video, width // 2), F32),
                 jax.ShapeDtypeStruct((video, HEAD_DIM), F32),
                 jax.ShapeDtypeStruct((video, width // 2 + HEAD_DIM), F32),
-            ],
+            ]
+            + [jax.ShapeDtypeStruct(fresh.shape, BF16)] * copy_out,
+            scratch_shapes=[pltpu.SemaphoreType.DMA] * copy_out,
             compiler_params=params(24),
             cost_estimate=cost(
                 video * context, context * width, video * heads
@@ -601,7 +611,7 @@
         final_kernel, [((video, out_features), BF16)], "final_out", out_cost,
         part, other_attended[1], w_other, hidden, branch_gate,
     )
-    return (mixed, new_cache)
+    return (mixed, copied[0])
 
 
 def solution(mesh):

time: 51.6 us -> 51 us (0.988)
  Pallas kernels: 20.3 us -> 19.1 us
    pallas_call x8, Pallas kernels: 4.51 us -> 3.75 us  [plain_call(): pl.pallas_call(kernel, in_specs=[pl.BlockSpec(memory_space=pltpu.VMEM)] *...]
  transfers between devices with their start and end apart: 19 -> 19, of which waited for: 9 -> 9; matrix products, arithmetic and copies ran while one was open for 0% -> 0% of each run, Pallas kernels for 37% -> 35%
where the time goes in v11:
time: 51 us; the launch traced here: 50.8 us
  starting transfers between devices  21.9 us (43%)
  Pallas kernels  19.1 us (37%)
  waiting for transfers between devices  8.98 us (18%)
  between operations  0.75 us (1%)
    ppermute x10, starting transfers between devices, ring_step(): lax.ppermute(block, 'section', way)  11.9 us
    pallas_call x1, Pallas kernels, per_device(): pl.pallas_call(send_kernel, in_specs=[smem] + [hbm] * 5, out_specs=[vmem]...  5.63 us
    ppermute x10, waiting for transfers between devices, ring_step(): lax.ppermute(block, 'section', way)  5.41 us
    pallas_call x1, Pallas kernels, per_device(): pl.pallas_call(own_kernel, in_specs=[smem, vmem, vmem, hbm, hbm] + [hbm]...  5.05 us
    pallas_call x2, Pallas kernels, per_device(): pl.pallas_call(functools.partial(attend_kernel, first, len(whole), copy_o...  4.66 us
    pallas_call x8, Pallas kernels, plain_call(): pl.pallas_call(kernel, in_specs=[pl.BlockSpec(memory_space=pltpu.VMEM)] *...  3.75 us
    ppermute x2, starting transfers between devices, per_device(): far = [lax.ppermute(chain[-1][0], 'section', ways[0]) for chain in chains]  3.59 us
    ppermute x2, starting transfers between devices, per_device(): other_attended.append(lax.ppermute(attended[-1], 'head', swap_head))  3.48 us
  transfers between devices with their start and end apart: 19, of which 9 were waited for; matrix products, arithmetic and copies ran while one was open for 0% of the time, Pallas kernels for 35%

profile of v11, /device:TPU:0, one launch (start us, length us, event | category | flops | bytes accessed | tf_op | source)
XLA Modules:
  0.0 50.8 jit_solution(1922193305836958253)
XLA Ops:
  0.6 3.1 %collective-permute-start.1 = (bf16[2,128,768]{2,1,0:T(8,128)(2,1)}, bf16[2,128,768]{2,1,0:T(8,128)(2,1)S(1)}, u32[]{:S(2)}, u32[]{:S(2)}) collective-permute-start(bf16[2,128,768]{2,1,0:T(8,128)(2,1)} %refs_5_.1), channel_id=1, source_target_pairs={{0,8},{2,6},{4,0},{6,14},{8,16},{10,2},{12,4},{14,22},{16,24},{18,... | collective-permute-start | bytes 1179656 | tf_op jit(solution)/shard_map/ppermute | solution.py:472
  3.8 5.6 %project_send.1 = (bf16[272,1536]{1,0:T(8,128)(2,1)S(1)}, bf16[224,2304]{1,0:T(8,128)(2,1)S(1)}, f32[272,128]{1,0:T(8,128)S(1)}, bf16[2,1536,768]{2,1,0:T(8,128)(2,1)S(1)}) custom-call(s32[2]{0:T(128)S(1)} %pad_add_fusion.place_ref, bf16[128,1536]{1,0:T(8,128)(2,1)} %refs_4_.1, bf16[256,1536]{1,0:T(8,128)(2,1)} %t_ref.1, f32[1536]{0:T(1024)} %scale_ref.1, ...), custom_call_target="tpu_custom_call" | custom-call | flops 7700742144 | bytes 7077888 | tf_op jit(solution)/shard_map/project_send/pallas_call | solution.py:485
  9.4 2.0 %collective-permute-start = (bf16[224,2304]{1,0:T(8,128)(2,1)S(1)}, bf16[224,2304]{1,0:T(8,128)(2,1)S(1)}, u32[]{:S(2)}, u32[]{:S(2)}) collective-permute-start(bf16[224,2304]{1,0:T(8,128)(2,1)S(1)} %get-tuple-element.41), channel_id=1, source_target_pairs={{0,1},{1,0},{2,3},{3,2},{4,5},{5,4},{6,7},{7,6},{8,9},{9,8},{10,11... | collective-permute-start | bytes 3096584 | tf_op jit(solution)/shard_map/ppermute | solution.py:509
  11.4 1.9 %collective-permute-done.1.refs_0_ = bf16[2,128,768]{2,1,0:T(8,128)(2,1)S(1)} collective-permute-done((bf16[2,128,768]{2,1,0:T(8,128)(2,1)}, bf16[2,128,768]{2,1,0:T(8,128)(2,1)S(1)}, u32[]{:S(2)}, u32[]{:S(2)}) %collective-permute-start.1) | collective-permute-done | bytes 393248 | tf_op jit(solution)/shard_map/ppermute | solution.py:472
  13.4 1.6 %collective-permute-start.3 = (bf16[2,128,384]{2,1,0:T(8,128)(2,1)S(1)}, bf16[2,128,384]{2,1,0:T(8,128)(2,1)S(1)}, u32[]{:S(2)}, u32[]{:S(2)}) collective-permute-start(bf16[2,128,384]{2,1,0:T(8,128)(2,1)S(1)} %get-tuple-element.44), channel_id=1, source_target_pairs={{0,8},{2,6},{4,0},{6,14},{8,16},{10,2},{12,4},{14,22},{16,24},{18,... | collective-permute-start | bytes 589832 | tf_op jit(solution)/shard_map/ppermute | solution.py:472
  15.0 0.9 %collective-permute-start.4 = (bf16[2,128,384]{2,1,0:T(8,128)(2,1)S(1)}, bf16[2,128,384]{2,1,0:T(8,128)(2,1)S(1)}, u32[]{:S(2)}, u32[]{:S(2)}) collective-permute-start(bf16[2,128,384]{2,1,0:T(8,128)(2,1)S(1)} %get-tuple-element.45), channel_id=1, source_target_pairs={{0,4},{2,10},{4,12},{6,2},{8,0},{10,18},{12,20},{14,6},{16,8},{18,... | collective-permute-start | bytes 589832 | tf_op jit(solution)/shard_map/ppermute | solution.py:472
  15.9 1.1 %collective-permute-start.5 = (bf16[2,128,384]{2,1,0:T(8,128)(2,1)S(1)}, bf16[2,128,384]{2,1,0:T(8,128)(2,1)S(1)}, u32[]{:S(2)}, u32[]{:S(2)}) collective-permute-start(bf16[2,128,384]{2,1,0:T(8,128)(2,1)S(1)} %get-tuple-element.46), channel_id=1, source_target_pairs={{0,8},{2,6},{4,0},{6,14},{8,16},{10,2},{12,4},{14,22},{16,24},{18,... | collective-permute-start | bytes 589832 | tf_op jit(solution)/shard_map/ppermute | solution.py:472
  17.0 0.9 %collective-permute-start.6 = (bf16[2,128,384]{2,1,0:T(8,128)(2,1)S(1)}, bf16[2,128,384]{2,1,0:T(8,128)(2,1)S(1)}, u32[]{:S(2)}, u32[]{:S(2)}) collective-permute-start(bf16[2,128,384]{2,1,0:T(8,128)(2,1)S(1)} %get-tuple-element.47), channel_id=1, source_target_pairs={{0,4},{2,10},{4,12},{6,2},{8,0},{10,18},{12,20},{14,6},{16,8},{18,... | collective-permute-start | bytes 589832 | tf_op jit(solution)/shard_map/ppermute | solution.py:472
  17.9 5.0 %project_own.1 = (f32[144,2304]{1,0:T(8,128)S(1)}, f32[128,1536]{1,0:T(8,128)S(1)}, bf16[768,1536]{1,0:T(8,128)(2,1)S(1)}, bf16[768,1536]{1,0:T(8,128)(2,1)S(1)}...) custom-call(s32[2]{0:T(128)S(1)} %pad_add_fusion.place_ref, ...), custom_call_target="tpu_custom_call" | custom-call | flops 7700742144 | bytes 7077888 | tf_op jit(solution)/shard_map/project_own/pallas_call | solution.py:517
  23.0 1.2 %collective-permute-start.8 = (bf16[2,128,384]{2,1,0:T(8,128)(2,1)S(1)}, bf16[2,128,384]{2,1,0:T(8,128)(2,1)S(1)}, u32[]{:S(2)}, u32[]{:S(2)}) collective-permute-start(bf16[2,128,384]{2,1,0:T(8,128)(2,1)S(1)} %collective-permute-done.3.refs_2_), channel_id=1, source_target_pairs={{0,8},{2,6},{4,0},{6,14},{8,16},{10,2},{12,4},{14,22},{16,24},{18,... | collective-permute-start | bytes 589832 | tf_op jit(solution)/shard_map/ppermute | solution.py:472
  25.1 1.7 %collective-permute-start.13 = (bf16[2,128,384]{2,1,0:T(8,128)(2,1)S(1)}, bf16[2,128,384]{2,1,0:T(8,128)(2,1)S(1)}, u32[]{:S(2)}, u32[]{:S(2)}) collective-permute-start(bf16[2,128,384]{2,1,0:T(8,128)(2,1)S(1)} %collective-permute-done.5.refs_2_), channel_id=1, source_target_pairs={{0,8},{2,6},{4,0},{6,14},{8,16},{10,2},{12,4},{14,22},{16,24},{18,... | collective-permute-start | bytes 589832 | tf_op jit(solution)/shard_map/ppermute | solution.py:472
  27.3 1.4 %collective-permute-done.8.refs_4_ = bf16[2,128,384]{2,1,0:T(8,128)(2,1)S(1)} collective-permute-done((bf16[2,128,384]{2,1,0:T(8,128)(2,1)S(1)}, bf16[2,128,384]{2,1,0:T(8,128)(2,1)S(1)}, u32[]{:S(2)}, u32[]{:S(2)}) %collective-permute-start.8) | collective-permute-done | bytes 196640 | tf_op jit(solution)/shard_map/ppermute | solution.py:472
  28.7 1.1 %collective-permute-start.10 = (bf16[2,128,384]{2,1,0:T(8,128)(2,1)S(1)}, bf16[2,128,384]{2,1,0:T(8,128)(2,1)S(1)}, u32[]{:S(2)}, u32[]{:S(2)}) collective-permute-start(bf16[2,128,384]{2,1,0:T(8,128)(2,1)S(1)} %collective-permute-done.8.refs_4_), channel_id=1, source_target_pairs={{0,8},{2,6},{4,0},{6,14},{8,16},{10,2},{12,4},{14,22},{16,24},{18,... | collective-permute-start | bytes 589832 | tf_op jit(solution)/shard_map/ppermute | solution.py:543
  29.8 0.9 %collective-permute-start.14 = (bf16[2,128,384]{2,1,0:T(8,128)(2,1)S(1)}, bf16[2,128,384]{2,1,0:T(8,128)(2,1)S(1)}, u32[]{:S(2)}, u32[]{:S(2)}) collective-permute-start(bf16[2,128,384]{2,1,0:T(8,128)(2,1)S(1)} %collective-permute-done.6.refs_3_), channel_id=1, source_target_pairs={{0,4},{2,10},{4,12},{6,2},{8,0},{10,18},{12,20},{14,6},{16,8},{18,... | collective-permute-start | bytes 589832 | tf_op jit(solution)/shard_map/ppermute | solution.py:472
  30.7 1.2 %collective-permute-done.13.refs_4_ = bf16[2,128,384]{2,1,0:T(8,128)(2,1)S(1)} collective-permute-done((bf16[2,128,384]{2,1,0:T(8,128)(2,1)S(1)}, bf16[2,128,384]{2,1,0:T(8,128)(2,1)S(1)}, u32[]{:S(2)}, u32[]{:S(2)}) %collective-permute-start.13) | collective-permute-done | bytes 196640 | tf_op jit(solution)/shard_map/ppermute | solution.py:472
  31.9 2.5 %collective-permute-start.15 = (bf16[2,128,384]{2,1,0:T(8,128)(2,1)S(1)}, bf16[2,128,384]{2,1,0:T(8,128)(2,1)S(1)}, u32[]{:S(2)}, u32[]{:S(2)}) collective-permute-start(bf16[2,128,384]{2,1,0:T(8,128)(2,1)S(1)} %collective-permute-done.13.refs_4_), channel_id=1, source_target_pairs={{0,8},{2,6},{4,0},{6,14},{8,16},{10,2},{12,4},{14,22},{16,24},{18,... | collective-permute-start | bytes 589832 | tf_op jit(solution)/shard_map/ppermute | solution.py:543
  34.4 0.8 %norm_video.1 = (bf16[128,384]{1,0:T(8,128)(2,1)S(1)}, bf16[128,384]{1,0:T(8,128)(2,1)S(1)}, bf16[2,128,768]{2,1,0:T(8,128)(2,1)S(1)}) custom-call(f32[144,2304]{1,0:T(8,128)S(1)} %get-tuple-element.40.own_ref.top_ref, bf16[224,2304]{1,0:T(8,128)(2,1)S(1)} %collective-permute-done.msg_ref, f32[272,128]{1,0:T(8,128)S(1)} %get-tuple-element.49.stat_ref, ...), custom_call_target="tpu_custom_call" | custom-call | flops 331776000 | bytes 2654208 | tf_op jit(solution)/shard_map/norm_video/pallas_call | solution.py:427
  36.6 2.3 %attend.2 = (f32[128,384]{1,0:T(8,128)S(1)}, f32[128,128]{1,0:T(8,128)S(1)}, f32[128,512]{1,0:T(8,128)S(1)}) custom-call(s32[2]{0:T(128)S(1)} %pad_add_fusion.place_ref, bf16[128,384]{1,0:T(8,128)(2,1)S(1)} %get-tuple-element.52.qo_ref, bf16[128,384]{1,0:T(8,128)(2,1)S(1)} %collective-permute-done.7.qp_ref, ...), custom_call_target="tpu_custom_call" | custom-call | flops 163840 | bytes 983040 | tf_op jit(solution)/shard_map/attend/pallas_call | solution.py:572
  39.4 2.3 %attend.3 = (f32[128,384]{1,0:T(8,128)S(1)}, f32[128,128]{1,0:T(8,128)S(1)}, f32[128,512]{1,0:T(8,128)S(1)}, bf16[2,128,768]{2,1,0:T(8,128)(2,1)}) custom-call(s32[2]{0:T(128)S(1)} %pad_add_fusion.place_ref, bf16[128,384]{1,0:T(8,128)(2,1)S(1)} %get-tuple-element.63.qo_ref, bf16[128,384]{1,0:T(8,128)(2,1)S(1)} %collective-permute-done.12.qp_ref, ...), custom_call_target="tpu_custom_call" | custom-call | flops 163840 | bytes 983040 | tf_op jit(solution)/shard_map/attend/pallas_call | solution.py:572
  42.0 2.2 %collective-permute-start.17 = (bf16[128,384]{1,0:T(8,128)(2,1)S(1)}, bf16[128,384]{1,0:T(8,128)(2,1)S(1)}, u32[]{:S(2)}, u32[]{:S(2)}) collective-permute-start(bf16[128,384]{1,0:T(8,128)(2,1)S(1)} %merge.2.first_ref), channel_id=1, source_target_pairs={{0,1},{1,0},{2,3},{3,2},{4,5},{5,4},{6,7},{7,6},{8,9},{9,8},{10,11... | collective-permute-start | bytes 294920 | tf_op jit(solution)/shard_map/ppermute | solution.py:600
  44.4 1.3 %collective-permute-start.18 = (bf16[128,384]{1,0:T(8,128)(2,1)S(1)}, bf16[128,384]{1,0:T(8,128)(2,1)S(1)}, u32[]{:S(2)}, u32[]{:S(2)}) collective-permute-start(bf16[128,384]{1,0:T(8,128)(2,1)S(1)} %merge.3.second_ref), channel_id=1, source_target_pairs={{0,1},{1,0},{2,3},{3,2},{4,5},{5,4},{6,7},{7,6},{8,9},{9,8},{10,11... | collective-permute-start | bytes 294920 | tf_op jit(solution)/shard_map/ppermute | solution.py:600
  46.2 1.6 %collective-permute-done.17.att_ref = bf16[128,384]{1,0:T(8,128)(2,1)S(1)} collective-permute-done((bf16[128,384]{1,0:T(8,128)(2,1)S(1)}, bf16[128,384]{1,0:T(8,128)(2,1)S(1)}, u32[]{:S(2)}, u32[]{:S(2)}) %collective-permute-start.17) | collective-permute-done | bytes 98336 | tf_op jit(solution)/shard_map/ppermute | solution.py:600
  48.3 1.4 %collective-permute-done.18.att_ref = bf16[128,384]{1,0:T(8,128)(2,1)S(1)} collective-permute-done((bf16[128,384]{1,0:T(8,128)(2,1)S(1)}, bf16[128,384]{1,0:T(8,128)(2,1)S(1)}, u32[]{:S(2)}, u32[]{:S(2)}) %collective-permute-start.18) | collective-permute-done | bytes 98336 | tf_op jit(solution)/shard_map/ppermute | solution.py:600
  49.7 1.1 %final_out.1 = bf16[128,1536]{1,0:T(8,128)(2,1)} custom-call(f32[128,1536]{1,0:T(8,128)S(1)} %more_out.1.part_ref, bf16[128,384]{1,0:T(8,128)(2,1)S(1)} %collective-permute-done.18.att_ref, bf16[768,1536]{1,0:T(8,128)(2,1)S(1)} %get-tuple-element.70.w_ref, bf16[128,1536]{1,0:T(8,128)(2,1)S(1)} %get-tuple-element.71.hidden_ref, ...), custom_call_target="tpu_custom_call" | custom-call | flops 603979776 | bytes 2359296 | tf_op jit(solution)/shard_map/final_out/pallas_call | solution.py:427
  (27 shorter events, 4.8 us)
Async XLA Ops:
  0.6 12.7 %collective-permute-start.1 = (bf16[2,128,768]{2,1,0:T(8,128)(2,1)}, bf16[2,128,768]{2,1,0:T(8,128)(2,1)S(1)}, u32[]{:S(2)}, u32[]{:S(2)}) collective-permute-start(bf16[2,128,768]{2,1,0:T(8,128)(2,1)} %refs_5_.1), channel_id=1, source_target_pairs={{0,8},{2,6},{4,0},{6,14},{8,16},{10,2},{12,4},{14,22},{16,24},{18,... | collective-permute-start | bytes 1179656 | tf_op jit(solution)/shard_map/ppermute | solution.py:472
  3.7 9.6 %collective-permute-start.2 = (bf16[2,128,768]{2,1,0:T(8,128)(2,1)}, bf16[2,128,768]{2,1,0:T(8,128)(2,1)S(1)}, u32[]{:S(2)}, u32[]{:S(2)}) collective-permute-start(bf16[2,128,768]{2,1,0:T(8,128)(2,1)} %refs_5_.1), channel_id=1, source_target_pairs={{0,4},{2,10},{4,12},{6,2},{8,0},{10,18},{12,20},{14,6},{16,8},{18,... | collective-permute-start | bytes 1179656 | tf_op jit(solution)/shard_map/ppermute | solution.py:472
  9.4 25.0 %collective-permute-start = (bf16[224,2304]{1,0:T(8,128)(2,1)S(1)}, bf16[224,2304]{1,0:T(8,128)(2,1)S(1)}, u32[]{:S(2)}, u32[]{:S(2)}) collective-permute-start(bf16[224,2304]{1,0:T(8,128)(2,1)S(1)} %get-tuple-element.41), channel_id=1, source_target_pairs={{0,1},{1,0},{2,3},{3,2},{4,5},{5,4},{6,7},{7,6},{8,9},{9,8},{10,11... | collective-permute-start | bytes 3096584 | tf_op jit(solution)/shard_map/ppermute | solution.py:509
  13.4 9.6 %collective-permute-start.3 = (bf16[2,128,384]{2,1,0:T(8,128)(2,1)S(1)}, bf16[2,128,384]{2,1,0:T(8,128)(2,1)S(1)}, u32[]{:S(2)}, u32[]{:S(2)}) collective-permute-start(bf16[2,128,384]{2,1,0:T(8,128)(2,1)S(1)} %get-tuple-element.44), channel_id=1, source_target_pairs={{0,8},{2,6},{4,0},{6,14},{8,16},{10,2},{12,4},{14,22},{16,24},{18,... | collective-permute-start | bytes 589832 | tf_op jit(solution)/shard_map/ppermute | solution.py:472
  15.0 8.0 %collective-permute-start.4 = (bf16[2,128,384]{2,1,0:T(8,128)(2,1)S(1)}, bf16[2,128,384]{2,1,0:T(8,128)(2,1)S(1)}, u32[]{:S(2)}, u32[]{:S(2)}) collective-permute-start(bf16[2,128,384]{2,1,0:T(8,128)(2,1)S(1)} %get-tuple-element.45), channel_id=1, source_target_pairs={{0,4},{2,10},{4,12},{6,2},{8,0},{10,18},{12,20},{14,6},{16,8},{18,... | collective-permute-start | bytes 589832 | tf_op jit(solution)/shard_map/ppermute | solution.py:472
  15.9 8.9 %collective-permute-start.5 = (bf16[2,128,384]{2,1,0:T(8,128)(2,1)S(1)}, bf16[2,128,384]{2,1,0:T(8,128)(2,1)S(1)}, u32[]{:S(2)}, u32[]{:S(2)}) collective-permute-start(bf16[2,128,384]{2,1,0:T(8,128)(2,1)S(1)} %get-tuple-element.46), channel_id=1, source_target_pairs={{0,8},{2,6},{4,0},{6,14},{8,16},{10,2},{12,4},{14,22},{16,24},{18,... | collective-permute-start | bytes 589832 | tf_op jit(solution)/shard_map/ppermute | solution.py:472
  17.0 8.1 %collective-permute-start.6 = (bf16[2,128,384]{2,1,0:T(8,128)(2,1)S(1)}, bf16[2,128,384]{2,1,0:T(8,128)(2,1)S(1)}, u32[]{:S(2)}, u32[]{:S(2)}) collective-permute-start(bf16[2,128,384]{2,1,0:T(8,128)(2,1)S(1)} %get-tuple-element.47), channel_id=1, source_target_pairs={{0,4},{2,10},{4,12},{6,2},{8,0},{10,18},{12,20},{14,6},{16,8},{18,... | collective-permute-start | bytes 589832 | tf_op jit(solution)/shard_map/ppermute | solution.py:472
  23.0 5.7 %collective-permute-start.8 = (bf16[2,128,384]{2,1,0:T(8,128)(2,1)S(1)}, bf16[2,128,384]{2,1,0:T(8,128)(2,1)S(1)}, u32[]{:S(2)}, u32[]{:S(2)}) collective-permute-start(bf16[2,128,384]{2,1,0:T(8,128)(2,1)S(1)} %collective-permute-done.3.refs_2_), channel_id=1, source_target_pairs={{0,8},{2,6},{4,0},{6,14},{8,16},{10,2},{12,4},{14,22},{16,24},{18,... | collective-permute-start | bytes 589832 | tf_op jit(solution)/shard_map/ppermute | solution.py:472
  25.1 6.9 %collective-permute-start.13 = (bf16[2,128,384]{2,1,0:T(8,128)(2,1)S(1)}, bf16[2,128,384]{2,1,0:T(8,128)(2,1)S(1)}, u32[]{:S(2)}, u32[]{:S(2)}) collective-permute-start(bf16[2,128,384]{2,1,0:T(8,128)(2,1)S(1)} %collective-permute-done.5.refs_2_), channel_id=1, source_target_pairs={{0,8},{2,6},{4,0},{6,14},{8,16},{10,2},{12,4},{14,22},{16,24},{18,... | collective-permute-start | bytes 589832 | tf_op jit(solution)/shard_map/ppermute | solution.py:472
  26.8 8.5 %collective-permute-start.9 = (bf16[2,128,384]{2,1,0:T(8,128)(2,1)S(1)}, bf16[2,128,384]{2,1,0:T(8,128)(2,1)S(1)}, u32[]{:S(2)}, u32[]{:S(2)}) collective-permute-start(bf16[2,128,384]{2,1,0:T(8,128)(2,1)S(1)} %collective-permute-done.4.refs_3_), channel_id=1, source_target_pairs={{0,4},{2,10},{4,12},{6,2},{8,0},{10,18},{12,20},{14,6},{16,8},{18,... | collective-permute-start | bytes 589832 | tf_op jit(solution)/shard_map/ppermute | solution.py:472
  28.7 7.8 %collective-permute-start.10 = (bf16[2,128,384]{2,1,0:T(8,128)(2,1)S(1)}, bf16[2,128,384]{2,1,0:T(8,128)(2,1)S(1)}, u32[]{:S(2)}, u32[]{:S(2)}) collective-permute-start(bf16[2,128,384]{2,1,0:T(8,128)(2,1)S(1)} %collective-permute-done.8.refs_4_), channel_id=1, source_target_pairs={{0,8},{2,6},{4,0},{6,14},{8,16},{10,2},{12,4},{14,22},{16,24},{18,... | collective-permute-start | bytes 589832 | tf_op jit(solution)/shard_map/ppermute | solution.py:543
  29.8 9.3 %collective-permute-start.14 = (bf16[2,128,384]{2,1,0:T(8,128)(2,1)S(1)}, bf16[2,128,384]{2,1,0:T(8,128)(2,1)S(1)}, u32[]{:S(2)}, u32[]{:S(2)}) collective-permute-start(bf16[2,128,384]{2,1,0:T(8,128)(2,1)S(1)} %collective-permute-done.6.refs_3_), channel_id=1, source_target_pairs={{0,4},{2,10},{4,12},{6,2},{8,0},{10,18},{12,20},{14,6},{16,8},{18,... | collective-permute-start | bytes 589832 | tf_op jit(solution)/shard_map/ppermute | solution.py:472
  31.9 7.4 %collective-permute-start.15 = (bf16[2,128,384]{2,1,0:T(8,128)(2,1)S(1)}, bf16[2,128,384]{2,1,0:T(8,128)(2,1)S(1)}, u32[]{:S(2)}, u32[]{:S(2)}) collective-permute-start(bf16[2,128,384]{2,1,0:T(8,128)(2,1)S(1)} %collective-permute-done.13.refs_4_), channel_id=1, source_target_pairs={{0,8},{2,6},{4,0},{6,14},{8,16},{10,2},{12,4},{14,22},{16,24},{18,... | collective-permute-start | bytes 589832 | tf_op jit(solution)/shard_map/ppermute | solution.py:543
  35.2 1.4 %collective-permute-start.7 = (bf16[128,384]{1,0:T(8,128)(2,1)S(1)}, bf16[128,384]{1,0:T(8,128)(2,1)S(1)}, u32[]{:S(2)}, u32[]{:S(2)}) collective-permute-start(bf16[128,384]{1,0:T(8,128)(2,1)S(1)} %get-tuple-element.52.qo_ref), channel_id=1, source_target_pairs={{0,2},{2,0},{4,6},{6,4},{8,10},{10,8},{12,14},{14,12},{16,18},{18,... | collective-permute-start | bytes 294920 | tf_op jit(solution)/shard_map/ppermute | solution.py:554
  35.3 4.1 %collective-permute-start.12 = (bf16[128,384]{1,0:T(8,128)(2,1)S(1)}, bf16[128,384]{1,0:T(8,128)(2,1)S(1)}, u32[]{:S(2)}, u32[]{:S(2)}) collective-permute-start(bf16[128,384]{1,0:T(8,128)(2,1)S(1)} %get-tuple-element.63.qo_ref), channel_id=1, source_target_pairs={{0,2},{2,0},{4,6},{6,4},{8,10},{10,8},{12,14},{14,12},{16,18},{18,... | collective-permute-start | bytes 294920 | tf_op jit(solution)/shard_map/ppermute | solution.py:554
  38.9 3.0 %collective-permute-start.11 = (f32[128,512]{1,0:T(8,128)S(1)}, f32[128,512]{1,0:T(8,128)S(1)}, u32[]{:S(2)}, u32[]{:S(2)}) collective-permute-start(f32[128,512]{1,0:T(8,128)S(1)} %get-tuple-element.61), channel_id=1, source_target_pairs={{0,2},{2,0},{4,6},{6,4},{8,10},{10,8},{12,14},{14,12},{16,18},{18,... | collective-permute-start | bytes 786440 | tf_op jit(solution)/shard_map/ppermute | solution.py:592
  41.7 2.5 %collective-permute-start.16 = (f32[128,512]{1,0:T(8,128)S(1)}, f32[128,512]{1,0:T(8,128)S(1)}, u32[]{:S(2)}, u32[]{:S(2)}) collective-permute-start(f32[128,512]{1,0:T(8,128)S(1)} %get-tuple-element.68), channel_id=1, source_target_pairs={{0,2},{2,0},{4,6},{6,4},{8,10},{10,8},{12,14},{14,12},{16,18},{18,... | collective-permute-start | bytes 786440 | tf_op jit(solution)/shard_map/ppermute | solution.py:592
  42.0 5.8 %collective-permute-start.17 = (bf16[128,384]{1,0:T(8,128)(2,1)S(1)}, bf16[128,384]{1,0:T(8,128)(2,1)S(1)}, u32[]{:S(2)}, u32[]{:S(2)}) collective-permute-start(bf16[128,384]{1,0:T(8,128)(2,1)S(1)} %merge.2.first_ref), channel_id=1, source_target_pairs={{0,1},{1,0},{2,3},{3,2},{4,5},{5,4},{6,7},{7,6},{8,9},{9,8},{10,11... | collective-permute-start | bytes 294920 | tf_op jit(solution)/shard_map/ppermute | solution.py:600
  44.4 5.3 %collective-permute-start.18 = (bf16[128,384]{1,0:T(8,128)(2,1)S(1)}, bf16[128,384]{1,0:T(8,128)(2,1)S(1)}, u32[]{:S(2)}, u32[]{:S(2)}) collective-permute-start(bf16[128,384]{1,0:T(8,128)(2,1)S(1)} %merge.3.second_ref), channel_id=1, source_target_pairs={{0,1},{1,0},{2,3},{3,2},{4,5},{5,4},{6,7},{7,6},{8,9},{9,8},{10,11... | collective-permute-start | bytes 294920 | tf_op jit(solution)/shard_map/ppermute | solution.py:600

commit v12 on v11

v12 whole, which is shorter than its diff:
```python
import functools
import math

import jax
import jax.numpy as jnp
from jax import lax
from jax.experimental import pallas as pl
from jax.experimental.pallas import tpu as pltpu
from jax.sharding import PartitionSpec as P

HEAD_DIM = 128
TRIPLE = 3 * HEAD_DIM
EXTRA = 16
PIECE = 2 * HEAD_DIM
EPS = 1e-06
F32 = jnp.float32
BF16 = jnp.bfloat16


def split_bf16(value, parts):
    pieces = []
    rest = value
    for _ in range(parts):
        piece = rest.astype(BF16)
        pieces.append(piece)
        rest = rest - piece.astype(F32)
    return pieces


def head_rows(video, text):
    return 3 * video + 2 * text + EXTRA


def column_copy(w_ref, first, target, sem):
    columns = target.shape[1]
    start = pl.multiple_of(first, HEAD_DIM)
    return pltpu.make_async_copy(w_ref.at[:, pl.ds(start, columns)], target, sem)


def partial_sums(a_ref, w_ref, video, text, msg_ref, first):
    band = lax.broadcasted_iota(jnp.int32, (EXTRA, HEAD_DIM), 0) // 4
    top = video + EXTRA
    terms = None
    for start in range(0, w_ref.shape[1], PIECE):
        stop = min(start + PIECE, w_ref.shape[1])
        product = jnp.dot(a_ref[...], w_ref[:, start:stop], preferred_element_type=F32)
        for local in range(0, stop - start, HEAD_DIM):
            part = product[:, local : local + HEAD_DIM]
            head, kind = divmod((start + local) // HEAD_DIM, 3)
            base = (first + head) * head_rows(video, text)
            msg_ref[base + kind * video : base + (kind + 1) * video, :] = part[:video].astype(BF16)
            terms = part[video:top] if kind == 0 else jnp.where(band == kind, part[video:top], terms)
            base += 3 * video
            if kind:
                rows = slice(base + (kind - 1) * text, base + kind * text)
                msg_ref[rows, :] = part[top:].astype(BF16)
            if kind == 2:
                base += 2 * text
                msg_ref[base : base + EXTRA, :] = terms.astype(BF16)


def send_kernel(
    place_ref, x_ref, t_ref, scale_ref, shift_ref, w_ref,
    a_ref, msg_ref, stat_ref, ahead_ref,
    x_buffer, t_buffer, scale_buffer, shift_buffer, w_buffer, sems,
):
    video, features = x_buffer.shape
    text = t_buffer.shape[0]
    top = video + EXTRA
    columns = w_buffer.shape[1]
    base = (1 - place_ref[0]) * (w_ref.shape[1] // 2)
    copies = [
        pltpu.make_async_copy(scale_ref, scale_buffer, sems.at[0]),
        pltpu.make_async_copy(shift_ref, shift_buffer, sems.at[1]),
        pltpu.make_async_copy(x_ref, x_buffer, sems.at[2]),
        pltpu.make_async_copy(
            t_ref.at[pl.ds(pl.multiple_of(place_ref[1] * text, text), text)], t_buffer, sems.at[3]
        ),
        column_copy(w_ref, base, w_buffer, sems.at[4]),
        column_copy(w_ref, base + columns, ahead_ref, sems.at[5]),
    ]
    for copy in copies[:5]:
        copy.start()

    copies[0].wait()
    copies[1].wait()
    gain = 1.0 + scale_buffer[...].reshape(1, features)
    pieces = split_bf16(gain, 2) + split_bf16(shift_buffer[...].reshape(1, features), 2)
    row = lax.broadcasted_iota(jnp.int32, (EXTRA, features), 0)
    extra = jnp.zeros((EXTRA, features), F32)
    for index, piece in enumerate(pieces):
        extra = jnp.where(row % 4 == index, piece.astype(F32), extra)
    a_ref[video:top, :] = extra.astype(BF16)

    def prepare(rows_ref, start):
        rows = rows_ref[...].astype(F32)
        count = rows.shape[0]
        mean = jnp.sum(rows, axis=1, keepdims=True) * (1.0 / features)
        centered = rows - mean
        second = jnp.sum(centered * centered, axis=1, keepdims=True)
        a_ref[start : start + count, :] = (centered * gain).astype(BF16)
        lane = lax.broadcasted_iota(jnp.int32, (count, HEAD_DIM), 1)
        packed = jnp.zeros((count, HEAD_DIM), F32)
        for index, piece in enumerate(split_bf16(mean, 3) + split_bf16(second, 3)):
            packed = jnp.where(lane == index, piece.astype(F32), packed)
        stat_ref[start : start + count, :] = jnp.where(
            lane == 0, mean, jnp.where(lane == 1, second, 0.0)
        )
        return jnp.transpose(packed)[:EXTRA]

    copies[2].wait()
    copies[5].start()
    stats = [prepare(x_buffer, 0)]
    copies[3].wait()
    stats.append(prepare(t_buffer, top))
    stat_ref[video:top, :] = jnp.zeros((EXTRA, HEAD_DIM), F32)
    start = head_rows(video, text) * columns // TRIPLE
    msg_ref[start : start + 2 * EXTRA, :] = jnp.concatenate(stats, axis=0).astype(BF16)
    copies[4].wait()
    partial_sums(a_ref, w_buffer, video, text, msg_ref, 0)
    copies[5].wait()


def send_more_kernel(
    video, place_ref, a_ref, ahead_ref, w_ref, msg_ref, own_ahead_ref, w_buffer, last_buffer, sems,
):
    text = a_ref.shape[0] - video - EXTRA
    width = w_ref.shape[1] // 2
    other, own = (1 - place_ref[0]) * width, place_ref[0] * width
    first = width - last_buffer.shape[1]
    copies = [
        column_copy(w_ref, other + first - w_buffer.shape[1], w_buffer, sems.at[0]),
        column_copy(w_ref, other + first, last_buffer, sems.at[1]),
        column_copy(w_ref, own, own_ahead_ref, sems.at[2]),
    ]
    copies[0].start()
    copies[1].start()
    partial_sums(a_ref, ahead_ref, video, text, msg_ref, 0)
    copies[0].wait()
    copies[2].start()
    head = ahead_ref.shape[1] // TRIPLE
    partial_sums(a_ref, w_buffer, video, text, msg_ref, head)
    copies[1].wait()
    head += w_buffer.shape[1] // TRIPLE
    partial_sums(a_ref, last_buffer, video, text, msg_ref, head)
    copies[2].wait()


def own_kernel(place_ref, a_ref, ahead_ref, w_ref, *refs):
    small = (len(refs) - 4) // 2
    out_ref, text_ref = refs[small : small + 2]
    w_buffer, sems = refs[-2:]
    top = out_ref.shape[0]
    later, _, columns = w_buffer.shape
    base = place_ref[0] * (w_ref.shape[1] // 2) + columns
    copies = [
        column_copy(w_ref, base + index * columns, w_buffer.at[index], sems.at[index])
        for index in range(later)
    ]
    for source, target in zip(refs[:small], refs[small + 2 : -2]):
        copies.append(pltpu.make_async_copy(source, target, sems.at[len(copies)]))
    for copy in copies:
        copy.start()

    for block in range(later + 1):
        if block:
            copies[block - 1].wait()
        for start in range(0, columns, PIECE):
            cells = slice(start, start + PIECE)
            part = w_buffer[block - 1, :, cells] if block else ahead_ref[:, cells]
            product = jnp.dot(a_ref[...], part, preferred_element_type=F32)
            first = block * columns + start
            out_ref[:, first : first + PIECE] = product[:top]
            for local in range(0, PIECE, HEAD_DIM):
                head, kind = divmod((first + local) // HEAD_DIM, 3)
                if kind:
                    target = (2 * head + kind - 1) * HEAD_DIM
                    text_ref[:, target : target + HEAD_DIM] = product[
                        top:, local : local + HEAD_DIM
                    ]
    for copy in copies[later:]:
        copy.wait()


def row_stats(total_features, own, received):
    count = own.shape[0]
    received = received.astype(F32)
    padding = jnp.zeros((HEAD_DIM - received.shape[0], count), F32)
    received = jnp.transpose(jnp.concatenate([received, padding], axis=0))
    parts = [received[:, index : index + 1] for index in range(6)]
    gap = 0.5 * (own[:, 0:1] - (parts[0] + parts[1] + parts[2]))
    second = own[:, 1:2] + (parts[3] + parts[4] + parts[5])
    var = second * (1.0 / total_features) + gap * gap
    return gap, lax.rsqrt(var + EPS)


def column_terms(own_ref, msg_ref, video, base, part):
    other = msg_ref[base : base + EXTRA, :].astype(F32)
    other = other[4 * (part % 3) : 4 * (part % 3) + 4]
    own = own_ref[video : video + 8, part * HEAD_DIM : (part + 1) * HEAD_DIM]
    scale = (own[0:1] + own[1:2]) - (other[0:1] + other[1:2])
    shift = (own[2:3] + own[3:4]) + (other[2:3] + other[3:4])
    return scale, shift


def head_place(head, rows, first_ref, more_ref):
    early = first_ref.shape[0] // rows
    return (first_ref, head * rows) if head < early else (more_ref, (head - early) * rows)


def head_norm(part, gain):
    square = jnp.sum(part * part, axis=1, keepdims=True) * (1.0 / HEAD_DIM)
    return part * lax.rsqrt(square + EPS) * gain


def norm_kernel(
    total_features, text, own_ref, first_ref, more_ref, stat_ref, qg_ref, kg_ref,
    qa_ref, qb_ref, kv_ref,
):
    video = qa_ref.shape[0]
    half = qa_ref.shape[1] // HEAD_DIM
    rows = head_rows(video, text)
    query_gain = qg_ref[...].reshape(1, HEAD_DIM)
    key_gain = kg_ref[...].reshape(1, HEAD_DIM)
    start = first_ref.shape[0] - 2 * EXTRA
    gap, inverse = row_stats(
        total_features, stat_ref[:video, :], first_ref[start : start + EXTRA, :video]
    )
    for head in range(2 * half):
        msg_ref, base = head_place(head, rows, first_ref, more_ref)

        def total(kind):
            part = 3 * head + kind
            scale, shift = column_terms(own_ref, msg_ref, video, base + rows - EXTRA, part)
            other = msg_ref[base + kind * video : base + (kind + 1) * video, :].astype(F32)
            both = own_ref[:video, part * HEAD_DIM : (part + 1) * HEAD_DIM] + other
            return (both + gap * scale) * inverse + shift

        columns = slice(head * HEAD_DIM, (head + 1) * HEAD_DIM)
        cells = slice(head % half * HEAD_DIM, (head % half + 1) * HEAD_DIM)
        q_ref = qa_ref if head < half else qb_ref
        q_ref[:, cells] = head_norm(total(0), query_gain).astype(BF16)
        kv_ref[0, :, columns] = head_norm(total(1), key_gain).astype(BF16)
        kv_ref[1, :, columns] = total(2).astype(BF16)


def text_kernel(
    total_features, own_ref, first_ref, more_ref, stat_ref, top_ref, kg_ref, kv_ref
):
    text = kv_ref.shape[1]
    heads = kv_ref.shape[2] // HEAD_DIM
    video = top_ref.shape[0] - EXTRA
    rows = head_rows(video, text)
    key_gain = kg_ref[...].reshape(1, HEAD_DIM)
    start = first_ref.shape[0] - EXTRA
    gap, inverse = row_stats(
        total_features, stat_ref[video + EXTRA :, :], first_ref[start : start + EXTRA, :text]
    )
    for head in range(heads):
        msg_ref, base = head_place(head, rows, first_ref, more_ref)

        def total(kind):
            scale, shift = column_terms(
                top_ref, msg_ref, video, base + rows - EXTRA, 3 * head + 1 + kind
            )
            start = base + 3 * video + kind * text
            other = msg_ref[start : start + text, :].astype(F32)
            first = (2 * head + kind) * HEAD_DIM
            return (own_ref[:, first : first + HEAD_DIM] + other + gap * scale) * inverse + shift

        columns = slice(head * HEAD_DIM, (head + 1) * HEAD_DIM)
        kv_ref[0, :, columns] = head_norm(total(0), key_gain).astype(BF16)
        kv_ref[1, :, columns] = total(1).astype(BF16)


FACTOR = math.log2(math.e) / math.sqrt(HEAD_DIM)


def split_kernel(*refs):
    count = len(refs) // 3
    for index in range(count):
        half = refs[index].shape[2] // 2
        refs[count + 2 * index][...] = refs[index][:, :, :half]
        refs[count + 2 * index + 1][...] = refs[index][:, :, half:]


AT_ONCE = 10


def attend_kernel(
    first, count, second, place_ref, weight_ref, qo_ref, qp_ref, fresh_ref, stale_ref, text_ref,
    mask_ref, *refs,
):
    if second:
        *refs, own_ref, own_den_ref, msg_ref, w_ref, cache_ref, sems = refs
    else:
        *refs, own_ref, own_den_ref, msg_ref, w_ref, sems = refs
    depth = w_ref.shape[0]
    half = 1 - place_ref[0] if second else place_ref[0]
    rows = pl.ds(pl.multiple_of(half * depth, depth), depth)
    copies = [pltpu.make_async_copy(weight_ref.at[rows], w_ref, sems.at[0])]
    if second:
        copies.append(pltpu.make_async_copy(fresh_ref, cache_ref, sems.at[1]))
    for copy in copies:
        copy.start()

    video, width = own_ref.shape
    text = text_ref.shape[1]
    lane = lax.broadcasted_iota(jnp.int32, (2 * video, HEAD_DIM), 1)
    mask = mask_ref[...].reshape(1, 2 * text).astype(F32)
    mask = jnp.where(place_ref[1] == 0, mask[:, :text], mask[:, text:])
    own_row = lax.broadcasted_iota(jnp.int32, (2 * video, 1), 0) < video
    packed = jnp.zeros((2 * video, HEAD_DIM), F32)
    for head in range(width // HEAD_DIM):
        cells = slice(head * HEAD_DIM, (head + 1) * HEAD_DIM)
        columns = slice((first + head) * HEAD_DIM, (first + head + 1) * HEAD_DIM)
        queries = jnp.concatenate([qo_ref[:, cells], qp_ref[:, cells]], axis=0)
        keeps = [jnp.where(own_row, 1.0, 0.0), jnp.where(own_row, 0.0, 1.0), mask]
        blocks = [(fresh_ref, columns), (stale_ref, columns), (text_ref, columns)]
        blocks += [(ref, columns) for ref in refs[:count]] + [(ref, cells) for ref in refs[count:]]
        total = None
        for start in range(0, len(blocks), AT_ONCE):
            group = blocks[start : start + AT_ONCE]
            keys = jnp.concatenate([ref[0, :, part] for ref, part in group], axis=0)
            values = jnp.concatenate([ref[1, :, part] for ref, part in group], axis=0)
            scores = lax.dot_general(
                queries, keys, (((1,), (1,)), ((), ())), preferred_element_type=F32
            )
            weights, place = [], 0
            for index, (ref, _) in enumerate(group):
                size = ref.shape[1]
                part = jnp.exp2(scores[:, place : place + size] * FACTOR)
                if start + index < len(keeps):
                    part = part * keeps[start + index]
                weights.append(part.astype(BF16))
                place += size
            values = jnp.concatenate([values, jnp.ones((place, HEAD_DIM), BF16)], axis=1)
            sums = jnp.dot(
                jnp.concatenate(weights, axis=1), values, preferred_element_type=F32
            )
            total = sums if total is None else total + sums
        own_ref[:, cells] = total[:video, :HEAD_DIM]
        msg_ref[:, cells] = total[video:, :HEAD_DIM]
        packed = jnp.where(lane == first + head, total[:, HEAD_DIM:], packed)
    own_den_ref[...] = packed[:video]
    msg_ref[:, width:] = packed[video:]
    for copy in copies:
        copy.wait()


def merge_kernel(first, own_ref, den_ref, msg_ref, att_ref):
    width = att_ref.shape[1]
    for head in range(width // HEAD_DIM):
        columns = slice(head * HEAD_DIM, (head + 1) * HEAD_DIM)
        lane = first + head
        num = own_ref[:, columns] + msg_ref[:, columns]
        den = den_ref[:, lane : lane + 1] + msg_ref[:, width + lane : width + lane + 1]
        att_ref[:, columns] = (num / den).astype(BF16)


def part_kernel(first_ref, second_ref, w_ref, out_ref):
    half = first_ref.shape[1]
    out_ref[...] = jnp.dot(
        first_ref[...], w_ref[:half, :], preferred_element_type=F32
    ) + jnp.dot(second_ref[...], w_ref[half:, :], preferred_element_type=F32)


def more_kernel(part_ref, att_ref, w_ref, out_ref):
    half = att_ref.shape[1]
    out_ref[...] = part_ref[...] + jnp.dot(
        att_ref[...], w_ref[:half, :], preferred_element_type=F32
    )


def final_kernel(part_ref, att_ref, w_ref, hidden_ref, gate_ref, out_ref):
    half = att_ref.shape[1]
    total = part_ref[...] + jnp.dot(att_ref[...], w_ref[half:, :], preferred_element_type=F32)
    gate = gate_ref[...].reshape(1, total.shape[1])
    out_ref[...] = (hidden_ref[...].astype(F32) + gate * total).astype(BF16)


def params(megabytes):
    return pltpu.CompilerParams(vmem_limit_bytes=megabytes * 1024 * 1024)


def in_hbm(array):
    return pltpu.with_memory_space_constraint(array, pltpu.HBM)


def cost(flops, nbytes, transcendentals=0):
    return pl.CostEstimate(
        flops=int(flops), bytes_accessed=int(nbytes), transcendentals=int(transcendentals)
    )


def plain_call(kernel, outs, name, estimate, *operands):
    return pl.pallas_call(
        kernel,
        in_specs=[pl.BlockSpec(memory_space=pltpu.VMEM)] * len(operands),
        out_specs=[pl.BlockSpec(memory_space=pltpu.VMEM)] * len(outs),
        out_shape=[jax.ShapeDtypeStruct(shape, dtype) for shape, dtype in outs],
        compiler_params=params(24),
        cost_estimate=estimate,
        name=name,
    )(*operands)


def ring_moves(sections):
    chips = sections // 2
    order = list(range(0, chips, 2)) + list(range(chips - 1, 0, -2))
    moves = [], []
    for here, there in zip(order, order[1:] + order[:1]):
        for core in range(2):
            moves[core].append((2 * here + core, 2 * there + core))
            moves[1 - core].append((2 * there + core, 2 * here + core))
    return sorted(moves[0]), sorted(moves[1])


def per_device(
    sections, hidden, text_hidden, text_mask, stale_cache, qkv_weight, out_weight, query_gain,
    key_gain, norm_shift, norm_scale, branch_gate,
):
    video, features = hidden.shape
    text = text_hidden.shape[0] // 2
    width = stale_cache.shape[2]
    heads = width // HEAD_DIM
    group_columns = heads * TRIPLE
    chips = sections // 2
    out_features = out_weight.shape[1]
    top = video + EXTRA
    rows = top + text

    group = lax.axis_index("head")
    core = lax.axis_index("section") % 2
    place = jnp.stack([group, core]).astype(jnp.int32)
    swap_core = [(s, s ^ 1) for s in range(sections)]
    swap_head = [(0, 1), (1, 0)]
    ways = ring_moves(sections)
    half_way = chips // 2

    def ring_step(blocks):
        return [lax.ppermute(block, "section", way) for block, way in zip(blocks, ways)]

    vmem = pl.BlockSpec(memory_space=pltpu.VMEM)
    hbm = pl.BlockSpec(memory_space=pltpu.HBM)
    smem = pl.BlockSpec(memory_space=pltpu.SMEM)
    whole = ring_step((stale_cache, stale_cache))

    columns = 2 * TRIPLE
    blocks = group_columns // columns
    per_head = head_rows(video, text)

    def project_cost(share):
        share = 8 * rows * features * group_columns * share
        return cost(share, share // (4 * rows))

    a_rows, message, stats, ahead = pl.pallas_call(
        send_kernel,
        in_specs=[smem] + [hbm] * 5,
        out_specs=[vmem] * 4,
        out_shape=[
            jax.ShapeDtypeStruct((rows, features), BF16),
            jax.ShapeDtypeStruct((per_head + 2 * EXTRA, HEAD_DIM), BF16),
            jax.ShapeDtypeStruct((rows, HEAD_DIM), F32),
            jax.ShapeDtypeStruct((features, columns), BF16),
        ],
        scratch_shapes=[
            pltpu.VMEM((video, features), BF16),
            pltpu.VMEM((text, features), BF16),
            pltpu.VMEM((features,), F32),
            pltpu.VMEM((features,), F32),
            pltpu.VMEM((features, TRIPLE), BF16),
            pltpu.SemaphoreType.DMA((6,)),
        ],
        compiler_params=params(40),
        cost_estimate=project_cost(0.4),
        name="project_send",
    )(place, *map(in_hbm, (hidden, text_hidden, norm_scale, norm_shift, qkv_weight)))
    received = lax.ppermute(message, "head", swap_head)

    message_more, own_ahead = pl.pallas_call(
        functools.partial(send_more_kernel, video),
        in_specs=[smem, vmem, vmem, hbm],
        out_specs=[vmem] * 2,
        out_shape=[
            jax.ShapeDtypeStruct(((heads - 1) * per_head, HEAD_DIM), BF16),
            jax.ShapeDtypeStruct((features, columns), BF16),
        ],
        scratch_shapes=[
            pltpu.VMEM((features, group_columns - columns - 2 * TRIPLE), BF16),
            pltpu.VMEM((features, TRIPLE), BF16),
            pltpu.SemaphoreType.DMA((3,)),
        ],
        compiler_params=params(40),
        cost_estimate=project_cost(0.6),
        name="project_send_more",
    )(place, a_rows, ahead, in_hbm(qkv_weight))
    received_more = lax.ppermute(message_more, "head", swap_head)

    split = plain_call(
        split_kernel, [((2, video, width // 2), BF16)] * 4, "split_heads", cost(0, 8 * video * width),
        *lax.optimization_barrier((*whole, message_more, received))[:2],
    )
    chains = [[ring_step((split[0], split[2]))], [ring_step((split[1], split[3]))]]

    small = (query_gain, key_gain, text_mask, branch_gate, hidden, stale_cache)
    outs = pl.pallas_call(
        own_kernel,
        in_specs=[smem, vmem, vmem, hbm] + [hbm] * len(small),
        out_specs=[vmem] * (2 + len(small)),
        out_shape=[
            jax.ShapeDtypeStruct((top, group_columns), F32),
            jax.ShapeDtypeStruct((text, 2 * width), F32),
        ]
        + [jax.ShapeDtypeStruct(array.shape, array.dtype) for array in small],
        scratch_shapes=[
            pltpu.VMEM((blocks - 1, features, columns), BF16),
            pltpu.SemaphoreType.DMA((blocks - 1 + len(small),)),
        ],
        compiler_params=params(40),
        cost_estimate=project_cost(1),
        name="project_own",
    )(place, a_rows, own_ahead, *map(in_hbm, (qkv_weight,) + small))
    own, own_text = outs[:2]
    query_gain, key_gain, text_mask, branch_gate, hidden, stale = outs[2:]

    for _ in range(half_way - 3):
        for chain in chains:
            chain.append(ring_step(lax.optimization_barrier((*chain[-1], own))[:2]))
    far = [lax.ppermute(chain[-1][0], "section", ways[0]) for chain in chains]
    ends = [chain[-1][1] for chain in chains]

    received_more = lax.optimization_barrier((received_more, *chains[0][0], *chains[1][0]))[0]
    *queries, fresh = plain_call(
        functools.partial(norm_kernel, features * 2, text),
        [((video, width // 2), BF16)] * 2 + [((2, video, width), BF16)],
        "norm_video",
        cost(1000 * top * group_columns, 8 * top * group_columns),
        own, received, received_more, stats, query_gain, key_gain,
    )
    other_queries = [lax.ppermute(half, "section", swap_core) for half in queries]
    (text_kv,) = plain_call(
        functools.partial(text_kernel, features * 2),
        [((2, text, width), BF16)],
        "norm_text",
        cost(text * group_columns, text * group_columns),
        own_text, received, received_more, stats, own, key_gain,
    )

    context = chips * video + video + text
    attended, other_attended, w_halves = [], [], []
    for index, chain in enumerate(chains):
        first = index * heads // 2
        halves = [block for step in chain for block in step] + [far[index]]
        own_queries = queries[index]
        if attended:
            own_queries = lax.optimization_barrier((own_queries, num_own))[0]
        second = index == 1
        num_own, den_own, num_message, w_half, *copied = pl.pallas_call(
            functools.partial(attend_kernel, first, len(whole), second),
            in_specs=[smem, hbm] + [vmem] * (6 + len(whole) + len(halves)),
            out_specs=[vmem] * 4 + [hbm] * second,
            out_shape=[
                jax.ShapeDtypeStruct((video, width // 2), F32),
                jax.ShapeDtypeStruct((video, HEAD_DIM), F32),
                jax.ShapeDtypeStruct((video, width // 2 + HEAD_DIM), F32),
                jax.ShapeDtypeStruct((width, out_features), BF16),
            ]
            + [jax.ShapeDtypeStruct(fresh.shape, BF16)] * second,
            scratch_shapes=[pltpu.SemaphoreType.DMA((2,))],
            compiler_params=params(24),
            cost_estimate=cost(
                video * context, context * width, video * heads
            ),
            name="attend",
        )(
            place, in_hbm(out_weight), own_queries, other_queries[index], fresh, stale, text_kv,
            text_mask, *whole, *halves,
        )
        w_halves.append(w_half)
        num_received = lax.ppermute(num_message, "section", swap_core)
        attended += plain_call(
            functools.partial(merge_kernel, first),
            [((video, width // 2), BF16)],
            "merge",
            cost(2 * video * width, 5 * video * width),
            num_own, den_own, num_received,
        )
        other_attended.append(lax.ppermute(attended[-1], "head", swap_head))

    out_cost = cost(4 * video * width * out_features, 2 * width * out_features)
    (part,) = plain_call(
        part_kernel, [((video, out_features), F32)], "part_out", out_cost, *attended, w_halves[0]
    )
    (part,) = plain_call(
        more_kernel, [((video, out_features), F32)], "more_out", out_cost,
        part, other_attended[0], w_halves[1],
    )
    (mixed,) = plain_call(
        final_kernel, [((video, out_features), BF16)], "final_out", out_cost,
        part, other_attended[1], w_halves[1], hidden, branch_gate,
    )
    return (mixed, copied[0])


def solution(mesh):
    in_specs = (
        P("section", "head"),
        P(None, "head"),
        P(),
        P(None, "section", "head"),
        P("head", None),
        P(None, "head"),
        P(),
        P(),
        P("head"),
        P("head"),
        P("head"),
    )
    out_specs = (P("section", "head"), P(None, "section", "head"))
    return jax.shard_map(
        functools.partial(per_device, mesh.shape["section"]),
        mesh=mesh, in_specs=in_specs, out_specs=out_specs, check_vma=False,
    )
```

time: 51 us -> 53.1 us (1.041)
  Pallas kernels: 19.1 us -> 22.7 us
  waiting for transfers between devices: 8.98 us -> 6.35 us
  starting transfers between devices: 21.9 us -> 22.8 us
    pallas_call x3 -> x4, Pallas kernels: 9.71 us -> 15.7 us  [the longest x2 6.78 us: per_device(): pl.pallas_call(functools.partial(attend_kernel, first, len(whole), second...]
    ppermute x10, waiting for transfers between devices: 5.41 us -> 3.12 us  [ring_step(): lax.ppermute(block, 'section', way)]
    pallas_call x1, Pallas kernels: 5.63 us -> 3.4 us  [per_device(): pl.pallas_call(send_kernel, in_specs=[smem] + [hbm] * 5, out_specs=[vmem]...]
    ppermute x2, starting transfers between devices: 3.59 us -> 4.18 us  [per_device(): far = [lax.ppermute(chain[-1][0], 'section', ways[0]) for chain in chains]]
  transfers between devices with their start and end apart: 19 -> 20, of which waited for: 9 -> 6; matrix products, arithmetic and copies ran while one was open for 0% -> 0% of each run, Pallas kernels for 35% -> 41%
where the time goes in v12:
time: 53.1 us; the launch traced here: 52.8 us
  starting transfers between devices  22.8 us (43%)
  Pallas kernels  22.7 us (43%)
  waiting for transfers between devices  6.35 us (12%)
  between operations  0.77 us (1%)
    ppermute x10, starting transfers between devices, ring_step(): lax.ppermute(block, 'section', way)  12.1 us
    pallas_call x2, Pallas kernels, per_device(): pl.pallas_call(functools.partial(attend_kernel, first, len(whole), second...  6.78 us
    pallas_call x1, Pallas kernels, per_device(): pl.pallas_call(own_kernel, in_specs=[smem, vmem, vmem, hbm] + [hbm] * len...  4.9 us
    ppermute x2, starting transfers between devices, per_device(): far = [lax.ppermute(chain[-1][0], 'section', ways[0]) for chain in chains]  4.18 us
    pallas_call x1, Pallas kernels, per_device(): pl.pallas_call(functools.partial(send_more_kernel, video), in_specs=[smem...  4.01 us
    pallas_call x8, Pallas kernels, plain_call(): pl.pallas_call(kernel, in_specs=[pl.BlockSpec(memory_space=pltpu.VMEM)] *...  3.63 us
    pallas_call x1, Pallas kernels, per_device(): pl.pallas_call(send_kernel, in_specs=[smem] + [hbm] * 5, out_specs=[vmem]...  3.4 us
    ppermute x2, starting transfers between devices, per_device(): other_attended.append(lax.ppermute(attended[-1], 'head', swap_head))  3.18 us
  transfers between devices with their start and end apart: 20, of which 6 were waited for; matrix products, arithmetic and copies ran while one was open for 0% of the time, Pallas kernels for 41%

profile of v12, /device:TPU:0, one launch (start us, length us, event | category | flops | bytes accessed | tf_op | source)
XLA Modules:
  0.0 52.8 jit_solution(18392031735058762201)
XLA Ops:
  0.6 3.1 %collective-permute-start.2 = (bf16[2,128,768]{2,1,0:T(8,128)(2,1)}, bf16[2,128,768]{2,1,0:T(8,128)(2,1)S(1)}, u32[]{:S(2)}, u32[]{:S(2)}) collective-permute-start(bf16[2,128,768]{2,1,0:T(8,128)(2,1)} %refs_5_.1), channel_id=1, source_target_pairs={{0,8},{2,6},{4,0},{6,14},{8,16},{10,2},{12,4},{14,22},{16,24},{18,... | collective-permute-start | bytes 1179656 | tf_op jit(solution)/shard_map/ppermute | solution.py:442
  3.8 3.4 %project_send.1 = (bf16[272,1536]{1,0:T(8,128)(2,1)S(1)}, bf16[688,128]{1,0:T(8,128)(2,1)S(1)}, f32[272,128]{1,0:T(8,128)S(1)}, bf16[1536,768]{1,0:T(8,128)(2,1)S(1)}) custom-call(s32[2]{0:T(128)S(1)} %pad_add_fusion.place_ref, bf16[128,1536]{1,0:T(8,128)(2,1)} %refs_4_.1, bf16[256,1536]{1,0:T(8,128)(2,1)} %t_ref.1, f32[1536]{0:T(1024)} %scale_ref.1, ...), custom_call_target="tpu_custom_call" | custom-call | flops 3080296960 | bytes 2831155 | tf_op jit(solution)/shard_map/project_send/pallas_call | solution.py:457
  7.2 2.0 %collective-permute-start = (bf16[688,128]{1,0:T(8,128)(2,1)S(1)}, bf16[688,128]{1,0:T(8,128)(2,1)S(1)}, u32[]{:S(2)}, u32[]{:S(2)}) collective-permute-start(bf16[688,128]{1,0:T(8,128)(2,1)S(1)} %get-tuple-element.44), channel_id=1, source_target_pairs={{0,1},{1,0},{2,3},{3,2},{4,5},{5,4},{6,7},{7,6},{8,9},{9,8},{10,11... | collective-permute-start | bytes 528392 | tf_op jit(solution)/shard_map/ppermute | solution.py:479
  9.2 4.0 %project_send_more.1 = (bf16[3280,128]{1,0:T(8,128)(2,1)S(1)}, bf16[1536,768]{1,0:T(8,128)(2,1)S(1)}) custom-call(s32[2]{0:T(128)S(1)} %pad_add_fusion.place_ref, bf16[272,1536]{1,0:T(8,128)(2,1)S(1)} %get-tuple-element.40.a_ref, bf16[1536,768]{1,0:T(8,128)(2,1)S(1)} %get-tuple-element.41.ahead_ref, bf16[1536,4608]{1,0:T(8,128)(2,1)} %w_ref.5), custom_call_target="tpu_custom_call" | custom-call | flops 4620445184 | bytes 4246732 | tf_op jit(solution)/shard_map/project_send_more/pallas_call | solution.py:481
  13.5 2.1 %collective-permute-start.4 = (bf16[2,128,384]{2,1,0:T(8,128)(2,1)S(1)}, bf16[2,128,384]{2,1,0:T(8,128)(2,1)S(1)}, u32[]{:S(2)}, u32[]{:S(2)}) collective-permute-start(bf16[2,128,384]{2,1,0:T(8,128)(2,1)S(1)} %get-tuple-element.48), channel_id=1, source_target_pairs={{0,8},{2,6},{4,0},{6,14},{8,16},{10,2},{12,4},{14,22},{16,24},{18,... | collective-permute-start | bytes 589832 | tf_op jit(solution)/shard_map/ppermute | solution.py:442
  15.9 1.7 %collective-permute-start.6 = (bf16[2,128,384]{2,1,0:T(8,128)(2,1)S(1)}, bf16[2,128,384]{2,1,0:T(8,128)(2,1)S(1)}, u32[]{:S(2)}, u32[]{:S(2)}) collective-permute-start(bf16[2,128,384]{2,1,0:T(8,128)(2,1)S(1)} %get-tuple-element.50), channel_id=1, source_target_pairs={{0,8},{2,6},{4,0},{6,14},{8,16},{10,2},{12,4},{14,22},{16,24},{18,... | collective-permute-start | bytes 589832 | tf_op jit(solution)/shard_map/ppermute | solution.py:442
  17.9 4.9 %project_own.1 = (f32[144,2304]{1,0:T(8,128)S(1)}, f32[128,1536]{1,0:T(8,128)S(1)}, f32[128]{0:T(128)S(1)}, f32[128]{0:T(128)S(1)}, s32[256]{0:T(256)S(1)}, /*in...) custom-call(s32[2]{0:T(128)S(1)} %pad_add_fusion.place_ref, ...), custom_call_target="tpu_custom_call" | custom-call | flops 7700742144 | bytes 7077888 | tf_op jit(solution)/shard_map/project_own/pallas_call | solution.py:507
  22.8 1.7 %collective-permute-start.9 = (bf16[2,128,384]{2,1,0:T(8,128)(2,1)S(1)}, bf16[2,128,384]{2,1,0:T(8,128)(2,1)S(1)}, u32[]{:S(2)}, u32[]{:S(2)}) collective-permute-start(bf16[2,128,384]{2,1,0:T(8,128)(2,1)S(1)} %collective-permute-done.4.refs_2_), channel_id=1, source_target_pairs={{0,8},{2,6},{4,0},{6,14},{8,16},{10,2},{12,4},{14,22},{16,24},{18,... | collective-permute-start | bytes 589832 | tf_op jit(solution)/shard_map/ppermute | solution.py:442
  24.9 2.0 %collective-permute-start.14 = (bf16[2,128,384]{2,1,0:T(8,128)(2,1)S(1)}, bf16[2,128,384]{2,1,0:T(8,128)(2,1)S(1)}, u32[]{:S(2)}, u32[]{:S(2)}) collective-permute-start(bf16[2,128,384]{2,1,0:T(8,128)(2,1)S(1)} %collective-permute-done.6.refs_2_), channel_id=1, source_target_pairs={{0,8},{2,6},{4,0},{6,14},{8,16},{10,2},{12,4},{14,22},{16,24},{18,... | collective-permute-start | bytes 589832 | tf_op jit(solution)/shard_map/ppermute | solution.py:442
  27.0 0.5 collective-permute-start.10
  27.5 1.1 %collective-permute-done.9.refs_4_ = bf16[2,128,384]{2,1,0:T(8,128)(2,1)S(1)} collective-permute-done((bf16[2,128,384]{2,1,0:T(8,128)(2,1)S(1)}, bf16[2,128,384]{2,1,0:T(8,128)(2,1)S(1)}, u32[]{:S(2)}, u32[]{:S(2)}) %collective-permute-start.9) | collective-permute-done | bytes 196640 | tf_op jit(solution)/shard_map/ppermute | solution.py:442
  28.6 1.7 %collective-permute-start.11 = (bf16[2,128,384]{2,1,0:T(8,128)(2,1)S(1)}, bf16[2,128,384]{2,1,0:T(8,128)(2,1)S(1)}, u32[]{:S(2)}, u32[]{:S(2)}) collective-permute-start(bf16[2,128,384]{2,1,0:T(8,128)(2,1)S(1)} %collective-permute-done.9.refs_4_), channel_id=1, source_target_pairs={{0,8},{2,6},{4,0},{6,14},{8,16},{10,2},{12,4},{14,22},{16,24},{18,... | collective-permute-start | bytes 589832 | tf_op jit(solution)/shard_map/ppermute | solution.py:530
  30.6 1.7 %collective-permute-done.14.refs_4_ = bf16[2,128,384]{2,1,0:T(8,128)(2,1)S(1)} collective-permute-done((bf16[2,128,384]{2,1,0:T(8,128)(2,1)S(1)}, bf16[2,128,384]{2,1,0:T(8,128)(2,1)S(1)}, u32[]{:S(2)}, u32[]{:S(2)}) %collective-permute-start.14) | collective-permute-done | bytes 196640 | tf_op jit(solution)/shard_map/ppermute | solution.py:442
  32.2 2.5 %collective-permute-start.16 = (bf16[2,128,384]{2,1,0:T(8,128)(2,1)S(1)}, bf16[2,128,384]{2,1,0:T(8,128)(2,1)S(1)}, u32[]{:S(2)}, u32[]{:S(2)}) collective-permute-start(bf16[2,128,384]{2,1,0:T(8,128)(2,1)S(1)} %collective-permute-done.14.refs_4_), channel_id=1, source_target_pairs={{0,8},{2,6},{4,0},{6,14},{8,16},{10,2},{12,4},{14,22},{16,24},{18,... | collective-permute-start | bytes 589832 | tf_op jit(solution)/shard_map/ppermute | solution.py:530
  34.7 0.7 %norm_video.1 = (bf16[128,384]{1,0:T(8,128)(2,1)S(1)}, bf16[128,384]{1,0:T(8,128)(2,1)S(1)}, bf16[2,128,768]{2,1,0:T(8,128)(2,1)S(1)}) custom-call(f32[144,2304]{1,0:T(8,128)S(1)} %get-tuple-element.43.own_ref.top_ref, bf16[688,128]{1,0:T(8,128)(2,1)S(1)} %collective-permute-done.first_ref, bf16[3280,128]{1,0:T(8,128)(2,1)S(1)} %collective-permute-done.1.more_ref, ...), custom_call_target="tpu_custom_call" | custom-call | flops 331776000 | bytes 2654208 | tf_op jit(solution)/shard_map/norm_video/pallas_call | solution.py:397
  36.0 0.5 norm_text.1.text_ref
  36.8 3.3 %attend.2 = (f32[128,384]{1,0:T(8,128)S(1)}, f32[128,128]{1,0:T(8,128)S(1)}, f32[128,512]{1,0:T(8,128)S(1)}, bf16[768,1536]{1,0:T(8,128)(2,1)S(1)}) custom-call(s32[2]{0:T(128)S(1)} %pad_add_fusion.place_ref, bf16[1536,1536]{1,0:T(8,128)(2,1)} %weight_ref.3, bf16[128,384]{1,0:T(8,128)(2,1)S(1)} %get-tuple-element.56.qo_ref, ...), custom_call_target="tpu_custom_call" | custom-call | flops 163840 | bytes 983040 | tf_op jit(solution)/shard_map/attend/pallas_call | solution.py:559
  40.3 3.5 %attend.3 = (f32[128,384]{1,0:T(8,128)S(1)}, f32[128,128]{1,0:T(8,128)S(1)}, f32[128,512]{1,0:T(8,128)S(1)}, bf16[768,1536]{1,0:T(8,128)(2,1)S(1)}, bf16[2,128,768]{2,1,0:T(8,128)(2,1)}) custom-call(s32[2]{0:T(128)S(1)} %pad_add_fusion.place_ref, bf16[1536,1536]{1,0:T(8,128)(2,1)} %weight_ref.3, bf16[128,384]{1,0:T(8,128)(2,1)S(1)} %get-tuple-element.67.qo_ref, ...), custom_call_target="tpu_custom_call" | custom-call | flops 163840 | bytes 983040 | tf_op jit(solution)/shard_map/attend/pallas_call | solution.py:559
  44.4 2.1 %collective-permute-start.18 = (bf16[128,384]{1,0:T(8,128)(2,1)S(1)}, bf16[128,384]{1,0:T(8,128)(2,1)S(1)}, u32[]{:S(2)}, u32[]{:S(2)}) collective-permute-start(bf16[128,384]{1,0:T(8,128)(2,1)S(1)} %merge.2.first_ref), channel_id=1, source_target_pairs={{0,1},{1,0},{2,3},{3,2},{4,5},{5,4},{6,7},{7,6},{8,9},{9,8},{10,11... | collective-permute-start | bytes 294920 | tf_op jit(solution)/shard_map/ppermute | solution.py:589
  46.7 1.0 %collective-permute-start.19 = (bf16[128,384]{1,0:T(8,128)(2,1)S(1)}, bf16[128,384]{1,0:T(8,128)(2,1)S(1)}, u32[]{:S(2)}, u32[]{:S(2)}) collective-permute-start(bf16[128,384]{1,0:T(8,128)(2,1)S(1)} %merge.3.second_ref), channel_id=1, source_target_pairs={{0,1},{1,0},{2,3},{3,2},{4,5},{5,4},{6,7},{7,6},{8,9},{9,8},{10,11... | collective-permute-start | bytes 294920 | tf_op jit(solution)/shard_map/ppermute | solution.py:589
  47.7 0.6 %part_out.1.part_ref = f32[128,1536]{1,0:T(8,128)S(1)} custom-call(bf16[128,384]{1,0:T(8,128)(2,1)S(1)} %merge.2.first_ref, bf16[128,384]{1,0:T(8,128)(2,1)S(1)} %merge.3.second_ref, bf16[768,1536]{1,0:T(8,128)(2,1)S(1)} %get-tuple-element.73.w_ref), custom_call_target="tpu_custom_call" | custom-call | flops 603979776 | bytes 2359296 | tf_op jit(solution)/shard_map/part_out/pallas_call | solution.py:397
  48.3 1.7 %collective-permute-done.18.att_ref = bf16[128,384]{1,0:T(8,128)(2,1)S(1)} collective-permute-done((bf16[128,384]{1,0:T(8,128)(2,1)S(1)}, bf16[128,384]{1,0:T(8,128)(2,1)S(1)}, u32[]{:S(2)}, u32[]{:S(2)}) %collective-permute-start.18) | collective-permute-done | bytes 98336 | tf_op jit(solution)/shard_map/ppermute | solution.py:589
  50.3 1.3 %collective-permute-done.19.att_ref = bf16[128,384]{1,0:T(8,128)(2,1)S(1)} collective-permute-done((bf16[128,384]{1,0:T(8,128)(2,1)S(1)}, bf16[128,384]{1,0:T(8,128)(2,1)S(1)}, u32[]{:S(2)}, u32[]{:S(2)}) %collective-permute-start.19) | collective-permute-done | bytes 98336 | tf_op jit(solution)/shard_map/ppermute | solution.py:589
  51.6 1.1 %final_out.1 = bf16[128,1536]{1,0:T(8,128)(2,1)} custom-call(f32[128,1536]{1,0:T(8,128)S(1)} %more_out.1.part_ref, bf16[128,384]{1,0:T(8,128)(2,1)S(1)} %collective-permute-done.19.att_ref, bf16[768,1536]{1,0:T(8,128)(2,1)S(1)} %get-tuple-element.74.w_ref, bf16[128,1536]{1,0:T(8,128)(2,1)S(1)} %get-tuple-element.75.hidden_ref, ...), custom_call_target="tpu_custom_call" | custom-call | flops 603979776 | bytes 2359296 | tf_op jit(solution)/shard_map/final_out/pallas_call | solution.py:397
  (30 shorter events, 3.8 us)
Async XLA Ops:
  0.6 12.8 %collective-permute-start.2 = (bf16[2,128,768]{2,1,0:T(8,128)(2,1)}, bf16[2,128,768]{2,1,0:T(8,128)(2,1)S(1)}, u32[]{:S(2)}, u32[]{:S(2)}) collective-permute-start(bf16[2,128,768]{2,1,0:T(8,128)(2,1)} %refs_5_.1), channel_id=1, source_target_pairs={{0,8},{2,6},{4,0},{6,14},{8,16},{10,2},{12,4},{14,22},{16,24},{18,... | collective-permute-start | bytes 1179656 | tf_op jit(solution)/shard_map/ppermute | solution.py:442
  3.7 9.7 %collective-permute-start.3 = (bf16[2,128,768]{2,1,0:T(8,128)(2,1)}, bf16[2,128,768]{2,1,0:T(8,128)(2,1)S(1)}, u32[]{:S(2)}, u32[]{:S(2)}) collective-permute-start(bf16[2,128,768]{2,1,0:T(8,128)(2,1)} %refs_5_.1), channel_id=1, source_target_pairs={{0,4},{2,10},{4,12},{6,2},{8,0},{10,18},{12,20},{14,6},{16,8},{18,... | collective-permute-start | bytes 1179656 | tf_op jit(solution)/shard_map/ppermute | solution.py:442
  7.2 6.2 %collective-permute-start = (bf16[688,128]{1,0:T(8,128)(2,1)S(1)}, bf16[688,128]{1,0:T(8,128)(2,1)S(1)}, u32[]{:S(2)}, u32[]{:S(2)}) collective-permute-start(bf16[688,128]{1,0:T(8,128)(2,1)S(1)} %get-tuple-element.44), channel_id=1, source_target_pairs={{0,1},{1,0},{2,3},{3,2},{4,5},{5,4},{6,7},{7,6},{8,9},{9,8},{10,11... | collective-permute-start | bytes 528392 | tf_op jit(solution)/shard_map/ppermute | solution.py:479
  13.2 21.5 %collective-permute-start.1 = (bf16[3280,128]{1,0:T(8,128)(2,1)S(1)}, bf16[3280,128]{1,0:T(8,128)(2,1)S(1)}, u32[]{:S(2)}, u32[]{:S(2)}) collective-permute-start(bf16[3280,128]{1,0:T(8,128)(2,1)S(1)} %get-tuple-element.45), channel_id=1, source_target_pairs={{0,1},{1,0},{2,3},{3,2},{4,5},{5,4},{6,7},{7,6},{8,9},{9,8},{10,11... | collective-permute-start | bytes 2519048 | tf_op jit(solution)/shard_map/ppermute | solution.py:498
  13.5 9.4 %collective-permute-start.4 = (bf16[2,128,384]{2,1,0:T(8,128)(2,1)S(1)}, bf16[2,128,384]{2,1,0:T(8,128)(2,1)S(1)}, u32[]{:S(2)}, u32[]{:S(2)}) collective-permute-start(bf16[2,128,384]{2,1,0:T(8,128)(2,1)S(1)} %get-tuple-element.48), channel_id=1, source_target_pairs={{0,8},{2,6},{4,0},{6,14},{8,16},{10,2},{12,4},{14,22},{16,24},{18,... | collective-permute-start | bytes 589832 | tf_op jit(solution)/shard_map/ppermute | solution.py:442
  15.5 7.3 %collective-permute-start.5 = (bf16[2,128,384]{2,1,0:T(8,128)(2,1)S(1)}, bf16[2,128,384]{2,1,0:T(8,128)(2,1)S(1)}, u32[]{:S(2)}, u32[]{:S(2)}) collective-permute-start(bf16[2,128,384]{2,1,0:T(8,128)(2,1)S(1)} %get-tuple-element.49), channel_id=1, source_target_pairs={{0,4},{2,10},{4,12},{6,2},{8,0},{10,18},{12,20},{14,6},{16,8},{18,... | collective-permute-start | bytes 589832 | tf_op jit(solution)/shard_map/ppermute | solution.py:442
  15.9 9.0 %collective-permute-start.6 = (bf16[2,128,384]{2,1,0:T(8,128)(2,1)S(1)}, bf16[2,128,384]{2,1,0:T(8,128)(2,1)S(1)}, u32[]{:S(2)}, u32[]{:S(2)}) collective-permute-start(bf16[2,128,384]{2,1,0:T(8,128)(2,1)S(1)} %get-tuple-element.50), channel_id=1, source_target_pairs={{0,8},{2,6},{4,0},{6,14},{8,16},{10,2},{12,4},{14,22},{16,24},{18,... | collective-permute-start | bytes 589832 | tf_op jit(solution)/shard_map/ppermute | solution.py:442
  17.6 7.4 %collective-permute-start.7 = (bf16[2,128,384]{2,1,0:T(8,128)(2,1)S(1)}, bf16[2,128,384]{2,1,0:T(8,128)(2,1)S(1)}, u32[]{:S(2)}, u32[]{:S(2)}) collective-permute-start(bf16[2,128,384]{2,1,0:T(8,128)(2,1)S(1)} %get-tuple-element.51), channel_id=1, source_target_pairs={{0,4},{2,10},{4,12},{6,2},{8,0},{10,18},{12,20},{14,6},{16,8},{18,... | collective-permute-start | bytes 589832 | tf_op jit(solution)/shard_map/ppermute | solution.py:442
  22.8 5.7 %collective-permute-start.9 = (bf16[2,128,384]{2,1,0:T(8,128)(2,1)S(1)}, bf16[2,128,384]{2,1,0:T(8,128)(2,1)S(1)}, u32[]{:S(2)}, u32[]{:S(2)}) collective-permute-start(bf16[2,128,384]{2,1,0:T(8,128)(2,1)S(1)} %collective-permute-done.4.refs_2_), channel_id=1, source_target_pairs={{0,8},{2,6},{4,0},{6,14},{8,16},{10,2},{12,4},{14,22},{16,24},{18,... | collective-permute-start | bytes 589832 | tf_op jit(solution)/shard_map/ppermute | solution.py:442
  24.9 7.3 %collective-permute-start.14 = (bf16[2,128,384]{2,1,0:T(8,128)(2,1)S(1)}, bf16[2,128,384]{2,1,0:T(8,128)(2,1)S(1)}, u32[]{:S(2)}, u32[]{:S(2)}) collective-permute-start(bf16[2,128,384]{2,1,0:T(8,128)(2,1)S(1)} %collective-permute-done.6.refs_2_), channel_id=1, source_target_pairs={{0,8},{2,6},{4,0},{6,14},{8,16},{10,2},{12,4},{14,22},{16,24},{18,... | collective-permute-start | bytes 589832 | tf_op jit(solution)/shard_map/ppermute | solution.py:442
  27.0 8.6 %collective-permute-start.10 = (bf16[2,128,384]{2,1,0:T(8,128)(2,1)S(1)}, bf16[2,128,384]{2,1,0:T(8,128)(2,1)S(1)}, u32[]{:S(2)}, u32[]{:S(2)}) collective-permute-start(bf16[2,128,384]{2,1,0:T(8,128)(2,1)S(1)} %collective-permute-done.5.refs_3_), channel_id=1, source_target_pairs={{0,4},{2,10},{4,12},{6,2},{8,0},{10,18},{12,20},{14,6},{16,8},{18,... | collective-permute-start | bytes 589832 | tf_op jit(solution)/shard_map/ppermute | solution.py:442
  28.6 8.2 %collective-permute-start.11 = (bf16[2,128,384]{2,1,0:T(8,128)(2,1)S(1)}, bf16[2,128,384]{2,1,0:T(8,128)(2,1)S(1)}, u32[]{:S(2)}, u32[]{:S(2)}) collective-permute-start(bf16[2,128,384]{2,1,0:T(8,128)(2,1)S(1)} %collective-permute-done.9.refs_4_), channel_id=1, source_target_pairs={{0,8},{2,6},{4,0},{6,14},{8,16},{10,2},{12,4},{14,22},{16,24},{18,... | collective-permute-start | bytes 589832 | tf_op jit(solution)/shard_map/ppermute | solution.py:530
  30.3 10.1 %collective-permute-start.15 = (bf16[2,128,384]{2,1,0:T(8,128)(2,1)S(1)}, bf16[2,128,384]{2,1,0:T(8,128)(2,1)S(1)}, u32[]{:S(2)}, u32[]{:S(2)}) collective-permute-start(bf16[2,128,384]{2,1,0:T(8,128)(2,1)S(1)} %collective-permute-done.7.refs_3_), channel_id=1, source_target_pairs={{0,4},{2,10},{4,12},{6,2},{8,0},{10,18},{12,20},{14,6},{16,8},{18,... | collective-permute-start | bytes 589832 | tf_op jit(solution)/shard_map/ppermute | solution.py:442
  32.2 8.1 %collective-permute-start.16 = (bf16[2,128,384]{2,1,0:T(8,128)(2,1)S(1)}, bf16[2,128,384]{2,1,0:T(8,128)(2,1)S(1)}, u32[]{:S(2)}, u32[]{:S(2)}) collective-permute-start(bf16[2,128,384]{2,1,0:T(8,128)(2,1)S(1)} %collective-permute-done.14.refs_4_), channel_id=1, source_target_pairs={{0,8},{2,6},{4,0},{6,14},{8,16},{10,2},{12,4},{14,22},{16,24},{18,... | collective-permute-start | bytes 589832 | tf_op jit(solution)/shard_map/ppermute | solution.py:530
  35.4 1.4 %collective-permute-start.8 = (bf16[128,384]{1,0:T(8,128)(2,1)S(1)}, bf16[128,384]{1,0:T(8,128)(2,1)S(1)}, u32[]{:S(2)}, u32[]{:S(2)}) collective-permute-start(bf16[128,384]{1,0:T(8,128)(2,1)S(1)} %get-tuple-element.56.qo_ref), channel_id=1, source_target_pairs={{0,2},{2,0},{4,6},{6,4},{8,10},{10,8},{12,14},{14,12},{16,18},{18,... | collective-permute-start | bytes 294920 | tf_op jit(solution)/shard_map/ppermute | solution.py:541
  35.5 4.8 %collective-permute-start.13 = (bf16[128,384]{1,0:T(8,128)(2,1)S(1)}, bf16[128,384]{1,0:T(8,128)(2,1)S(1)}, u32[]{:S(2)}, u32[]{:S(2)}) collective-permute-start(bf16[128,384]{1,0:T(8,128)(2,1)S(1)} %get-tuple-element.67.qo_ref), channel_id=1, source_target_pairs={{0,2},{2,0},{4,6},{6,4},{8,10},{10,8},{12,14},{14,12},{16,18},{18,... | collective-permute-start | bytes 294920 | tf_op jit(solution)/shard_map/ppermute | solution.py:541
  40.1 4.1 %collective-permute-start.12 = (f32[128,512]{1,0:T(8,128)S(1)}, f32[128,512]{1,0:T(8,128)S(1)}, u32[]{:S(2)}, u32[]{:S(2)}) collective-permute-start(f32[128,512]{1,0:T(8,128)S(1)} %get-tuple-element.65), channel_id=1, source_target_pairs={{0,2},{2,0},{4,6},{6,4},{8,10},{10,8},{12,14},{14,12},{16,18},{18,... | collective-permute-start | bytes 786440 | tf_op jit(solution)/shard_map/ppermute | solution.py:581
  43.8 2.7 %collective-permute-start.17 = (f32[128,512]{1,0:T(8,128)S(1)}, f32[128,512]{1,0:T(8,128)S(1)}, u32[]{:S(2)}, u32[]{:S(2)}) collective-permute-start(f32[128,512]{1,0:T(8,128)S(1)} %get-tuple-element.72), channel_id=1, source_target_pairs={{0,2},{2,0},{4,6},{6,4},{8,10},{10,8},{12,14},{14,12},{16,18},{18,... | collective-permute-start | bytes 786440 | tf_op jit(solution)/shard_map/ppermute | solution.py:581
  44.4 5.6 %collective-permute-start.18 = (bf16[128,384]{1,0:T(8,128)(2,1)S(1)}, bf16[128,384]{1,0:T(8,128)(2,1)S(1)}, u32[]{:S(2)}, u32[]{:S(2)}) collective-permute-start(bf16[128,384]{1,0:T(8,128)(2,1)S(1)} %merge.2.first_ref), channel_id=1, source_target_pairs={{0,1},{1,0},{2,3},{3,2},{4,5},{5,4},{6,7},{7,6},{8,9},{9,8},{10,11... | collective-permute-start | bytes 294920 | tf_op jit(solution)/shard_map/ppermute | solution.py:589
  46.7 5.0 %collective-permute-start.19 = (bf16[128,384]{1,0:T(8,128)(2,1)S(1)}, bf16[128,384]{1,0:T(8,128)(2,1)S(1)}, u32[]{:S(2)}, u32[]{:S(2)}) collective-permute-start(bf16[128,384]{1,0:T(8,128)(2,1)S(1)} %merge.3.second_ref), channel_id=1, source_target_pairs={{0,1},{1,0},{2,3},{3,2},{4,5},{5,4},{6,7},{7,6},{8,9},{9,8},{10,11... | collective-permute-start | bytes 294920 | tf_op jit(solution)/shard_map/ppermute | solution.py:589

commit v13 on v12

--- a/solution.py
+++ b/solution.py
@@ -284,68 +284,98 @@
         refs[count + 2 * index + 1][...] = refs[index][:, :, half:]
 
 
-AT_ONCE = 10
+def weigh(rows, keys):
+    scores = lax.dot_general(rows, keys, (((1,), (1,)), ((), ())), preferred_element_type=F32)
+    return jnp.exp2(scores * FACTOR)
+
+
+def lanes(weights):
+    total = weights[:, :HEAD_DIM]
+    for start in range(HEAD_DIM, weights.shape[1], HEAD_DIM):
+        total = total + weights[:, start : start + HEAD_DIM]
+    return total
+
+
+def times(weights, values):
+    return jnp.dot(weights.astype(BF16), values, preferred_element_type=F32)
+
+
+def both(group, index):
+    return jnp.concatenate([ref[index, :, part] for ref, part in group], axis=0)
 
 
 def attend_kernel(
-    first, count, second, place_ref, weight_ref, qo_ref, qp_ref, fresh_ref, stale_ref, text_ref,
-    mask_ref, *refs,
+    first, count, place_ref, qo_ref, qp_ref, fresh_ref, stale_ref, text_ref, mask_ref, *refs,
 ):
-    if second:
-        *refs, own_ref, own_den_ref, msg_ref, w_ref, cache_ref, sems = refs
+    finish = len(refs[-1].shape) == 0
+    if finish:
+        *refs, own_ref, own_den_ref, msg_ref, cache_ref, sem = refs
+        cache_copy = pltpu.make_async_copy(fresh_ref, cache_ref, sem)
+        cache_copy.start()
     else:
-        *refs, own_ref, own_den_ref, msg_ref, w_ref, sems = refs
-    depth = w_ref.shape[0]
-    half = 1 - place_ref[0] if second else place_ref[0]
-    rows = pl.ds(pl.multiple_of(half * depth, depth), depth)
-    copies = [pltpu.make_async_copy(weight_ref.at[rows], w_ref, sems.at[0])]
-    if second:
-        copies.append(pltpu.make_async_copy(fresh_ref, cache_ref, sems.at[1]))
-    for copy in copies:
-        copy.start()
-
-    video, width = own_ref.shape
+        *refs, num_ref, den_ref = refs
+    video, width = qo_ref.shape
     text = text_ref.shape[1]
     lane = lax.broadcasted_iota(jnp.int32, (2 * video, HEAD_DIM), 1)
     mask = mask_ref[...].reshape(1, 2 * text).astype(F32)
     mask = jnp.where(place_ref[1] == 0, mask[:, :text], mask[:, text:])
-    own_row = lax.broadcasted_iota(jnp.int32, (2 * video, 1), 0) < video
+    keep = jnp.concatenate([jnp.ones((1, video), F32), mask], axis=1)
+    same_patch = (
+        (lax.broadcasted_iota(jnp.int32, (2 * video, 2 * video), 0) < video)
+        == (lax.broadcasted_iota(jnp.int32, (2 * video, 2 * video), 1) < video)
+    ).astype(F32)
     packed = jnp.zeros((2 * video, HEAD_DIM), F32)
     for head in range(width // HEAD_DIM):
         cells = slice(head * HEAD_DIM, (head + 1) * HEAD_DIM)
         columns = slice((first + head) * HEAD_DIM, (first + head + 1) * HEAD_DIM)
         queries = jnp.concatenate([qo_ref[:, cells], qp_ref[:, cells]], axis=0)
-        keeps = [jnp.where(own_row, 1.0, 0.0), jnp.where(own_row, 0.0, 1.0), mask]
-        blocks = [(fresh_ref, columns), (stale_ref, columns), (text_ref, columns)]
-        blocks += [(ref, columns) for ref in refs[:count]] + [(ref, cells) for ref in refs[count:]]
-        total = None
-        for start in range(0, len(blocks), AT_ONCE):
-            group = blocks[start : start + AT_ONCE]
-            keys = jnp.concatenate([ref[0, :, part] for ref, part in group], axis=0)
-            values = jnp.concatenate([ref[1, :, part] for ref, part in group], axis=0)
-            scores = lax.dot_general(
-                queries, keys, (((1,), (1,)), ((), ())), preferred_element_type=F32
-            )
-            weights, place = [], 0
-            for index, (ref, _) in enumerate(group):
-                size = ref.shape[1]
-                part = jnp.exp2(scores[:, place : place + size] * FACTOR)
-                if start + index < len(keeps):
-                    part = part * keeps[start + index]
-                weights.append(part.astype(BF16))
-                place += size
-            values = jnp.concatenate([values, jnp.ones((place, HEAD_DIM), BF16)], axis=1)
-            sums = jnp.dot(
-                jnp.concatenate(weights, axis=1), values, preferred_element_type=F32
-            )
-            total = sums if total is None else total + sums
-        own_ref[:, cells] = total[:video, :HEAD_DIM]
-        msg_ref[:, cells] = total[video:, :HEAD_DIM]
-        packed = jnp.where(lane == first + head, total[:, HEAD_DIM:], packed)
+        pair = [(fresh_ref, columns), (stale_ref, columns)]
+        weights = weigh(queries, both(pair, 0)) * same_patch
+        num = times(weights, both(pair, 1))
+        den = lanes(weights)
+        blocks = [(ref, columns) for ref in refs[:count]] + [(ref, cells) for ref in refs[count:]]
+        blocks.append((text_ref, columns))
+        odd = len(blocks) % 2
+        for start in range(odd, len(blocks), 2):
+            pair = blocks[start : start + 2]
+            weights = weigh(queries, both(pair, 0))
+            if start + 2 == len(blocks):
+                weights = weights * keep
+            num = num + times(weights, both(pair, 1))
+            den = den + lanes(weights)
+        if odd:
+            weights = weigh(queries, both(blocks[:1], 0))
+            num = num + times(weights, both(blocks[:1], 1))
+            den = den + weights
+        if finish:
+            own_ref[:, cells] = num[:video]
+            msg_ref[:, cells] = num[video:]
+        else:
+            num_ref[:, cells] = num
+        packed = jnp.where(lane == first + head, jnp.sum(den, axis=1, keepdims=True), packed)
+    if finish:
+        own_den_ref[...] = packed[:video]
+        msg_ref[:, width:] = packed[video:]
+        cache_copy.wait()
+    else:
+        den_ref[...] = packed
+
+
+def last_kernel(first, qo_ref, qp_ref, num_ref, den_ref, far_ref, own_ref, own_den_ref, msg_ref):
+    video, width = qo_ref.shape
+    lane = lax.broadcasted_iota(jnp.int32, (2 * video, HEAD_DIM), 1)
+    packed = den_ref[...]
+    for head in range(width // HEAD_DIM):
+        cells = slice(head * HEAD_DIM, (head + 1) * HEAD_DIM)
+        queries = jnp.concatenate([qo_ref[:, cells], qp_ref[:, cells]], axis=0)
+        weights = weigh(queries, far_ref[0, :, cells])
+        num = num_ref[:, cells] + times(weights, far_ref[1, :, cells])
+        own_ref[:, cells] = num[:video]
+        msg_ref[:, cells] = num[video:]
+        total = jnp.sum(lanes(weights), axis=1, keepdims=True)
+        packed = packed + jnp.where(lane == first + head, total, 0.0)
     own_den_ref[...] = packed[:video]
     msg_ref[:, width:] = packed[video:]
-    for copy in copies:
-        copy.wait()
 
 
 def merge_kernel(first, own_ref, den_ref, msg_ref, att_ref):
@@ -358,11 +388,21 @@
         att_ref[:, columns] = (num / den).astype(BF16)
 
 
-def part_kernel(first_ref, second_ref, w_ref, out_ref):
+def part_kernel(place_ref, weight_ref, first_ref, second_ref, out_ref, w_other_ref, w_ref, sems):
+    depth = w_ref.shape[0]
     half = first_ref.shape[1]
+    copies = []
+    for index, (group, target) in enumerate(
+        ((place_ref[0], w_ref), (1 - place_ref[0], w_other_ref))
+    ):
+        rows = pl.ds(pl.multiple_of(group * depth, depth), depth)
+        copies.append(pltpu.make_async_copy(weight_ref.at[rows], target, sems.at[index]))
+        copies[-1].start()
+    copies[0].wait()
     out_ref[...] = jnp.dot(
         first_ref[...], w_ref[:half, :], preferred_element_type=F32
     ) + jnp.dot(second_ref[...], w_ref[half:, :], preferred_element_type=F32)
+    copies[1].wait()
 
 
 def more_kernel(part_ref, att_ref, w_ref, out_ref):
@@ -527,8 +567,7 @@
     for _ in range(half_way - 3):
         for chain in chains:
             chain.append(ring_step(lax.optimization_barrier((*chain[-1], own))[:2]))
-    far = [lax.ppermute(chain[-1][0], "section", ways[0]) for chain in chains]
-    ends = [chain[-1][1] for chain in chains]
+    far = [lax.ppermute(chains[0][-1][0], "section", ways[0])]
 
     received_more = lax.optimization_barrier((received_more, *chains[0][0], *chains[1][0]))[0]
     *queries, fresh = plain_call(
@@ -547,37 +586,53 @@
         own_text, received, received_more, stats, own, key_gain,
     )
 
+    last = lax.optimization_barrier((chains[1][-1][0], text_kv, queries[0]))[0]
+    far.append(lax.ppermute(last, "section", ways[0]))
     context = chips * video + video + text
-    attended, other_attended, w_halves = [], [], []
+    finished = [
+        jax.ShapeDtypeStruct((video, width // 2), F32),
+        jax.ShapeDtypeStruct((video, HEAD_DIM), F32),
+        jax.ShapeDtypeStruct((video, width // 2 + HEAD_DIM), F32),
+    ]
+    attended, other_attended = [], []
     for index, chain in enumerate(chains):
         first = index * heads // 2
-        halves = [block for step in chain for block in step] + [far[index]]
+        halves = [block for step in chain for block in step]
+        finish = index == 1
         own_queries = queries[index]
-        if attended:
+        if finish:
+            halves.append(far[index])
             own_queries = lax.optimization_barrier((own_queries, num_own))[0]
-        second = index == 1
-        num_own, den_own, num_message, w_half, *copied = pl.pallas_call(
-            functools.partial(attend_kernel, first, len(whole), second),
-            in_specs=[smem, hbm] + [vmem] * (6 + len(whole) + len(halves)),
-            out_specs=[vmem] * 4 + [hbm] * second,
-            out_shape=[
-                jax.ShapeDtypeStruct((video, width // 2), F32),
-                jax.ShapeDtypeStruct((video, HEAD_DIM), F32),
-                jax.ShapeDtypeStruct((video, width // 2 + HEAD_DIM), F32),
-                jax.ShapeDtypeStruct((width, out_features), BF16),
+            outs = finished + [jax.ShapeDtypeStruct(fresh.shape, BF16)]
+        else:
+            outs = [
+                jax.ShapeDtypeStruct((2 * video, width // 2), F32),
+                jax.ShapeDtypeStruct((2 * video, HEAD_DIM), F32),
             ]
-            + [jax.ShapeDtypeStruct(fresh.shape, BF16)] * second,
-            scratch_shapes=[pltpu.SemaphoreType.DMA((2,))],
+        outs = pl.pallas_call(
+            functools.partial(attend_kernel, first, len(whole)),
+            in_specs=[smem] + [vmem] * (6 + len(whole) + len(halves)),
+            out_specs=[vmem] * (len(outs) - finish) + [hbm] * finish,
+            out_shape=outs,
+            scratch_shapes=[pltpu.SemaphoreType.DMA] * finish,
             compiler_params=params(24),
-            cost_estimate=cost(
-                video * context, context * width, video * heads
-            ),
+            cost_estimate=cost(video * context, context * width, video * heads),
             name="attend",
         )(
-            place, in_hbm(out_weight), own_queries, other_queries[index], fresh, stale, text_kv,
-            text_mask, *whole, *halves,
+            place, own_queries, other_queries[index], fresh, stale, text_kv, text_mask,
+            *whole, *halves,
         )
-        w_halves.append(w_half)
+        if finish:
+            *outs, new_cache = outs
+        else:
+            outs = plain_call(
+                functools.partial(last_kernel, first),
+                [(out.shape, out.dtype) for out in finished],
+                "attend_last",
+                cost(video * video, video * width),
+                own_queries, other_queries[index], *outs, far[index],
+            )
+        num_own, den_own, num_message = outs
         num_received = lax.ppermute(num_message, "section", swap_core)
         attended += plain_call(
             functools.partial(merge_kernel, first),
@@ -589,18 +644,31 @@
         other_attended.append(lax.ppermute(attended[-1], "head", swap_head))
 
     out_cost = cost(4 * video * width * out_features, 2 * width * out_features)
-    (part,) = plain_call(
-        part_kernel, [((video, out_features), F32)], "part_out", out_cost, *attended, w_halves[0]
-    )
+    part, w_other = pl.pallas_call(
+        part_kernel,
+        in_specs=[smem, hbm, vmem, vmem],
+        out_specs=[vmem] * 2,
+        out_shape=[
+            jax.ShapeDtypeStruct((video, out_features), F32),
+            jax.ShapeDtypeStruct((width, out_features), BF16),
+        ],
+        scratch_shapes=[
+            pltpu.VMEM((width, out_features), BF16),
+            pltpu.SemaphoreType.DMA((2,)),
+        ],
+        compiler_params=params(24),
+        cost_estimate=out_cost,
+        name="part_out",
+    )(place, in_hbm(out_weight), *attended)
     (part,) = plain_call(
         more_kernel, [((video, out_features), F32)], "more_out", out_cost,
-        part, other_attended[0], w_halves[1],
+        part, other_attended[0], w_other,
     )
     (mixed,) = plain_call(
         final_kernel, [((video, out_features), BF16)], "final_out", out_cost,
-        part, other_attended[1], w_halves[1], hidden, branch_gate,
-    )
-    return (mixed, copied[0])
+        part, other_attended[1], w_other, hidden, branch_gate,
+    )
+    return (mixed, new_cache)
 
 
 def solution(mesh):

time: 53.1 us -> 51.3 us (0.966)
  starting transfers between devices: 22.8 us -> 21.4 us
  waiting for transfers between devices: 6.35 us -> 5.42 us
  Pallas kernels: 22.7 us -> 23.4 us
    ppermute x1, waiting for transfers between devices: 0.01 us -> 2.27 us  [per_device(): received_more = lax.ppermute(message_more, 'head', swap_head)]
    ppermute x2, waiting for transfers between devices: 2.95 us -> 0.87 us  [per_device(): other_attended.append(lax.ppermute(attended[-1], 'head', swap_head))]
    ppermute x10, waiting for transfers between devices: 3.12 us -> 1.47 us  [ring_step(): lax.ppermute(block, 'section', way)]
    ppermute x2, starting transfers between devices: 4.18 us -> 3.33 us  [the longest x1 1.7 us: per_device(): far = [lax.ppermute(chains[0][-1][0], 'section', ways[0])]]
    pallas_call x2 -> x3, Pallas kernels: 6.78 us -> 7.51 us  [the longest x2 4.57 us: per_device(): pl.pallas_call(functools.partial(attend_kernel, first, len(whole)), in_sp...]
  transfers between devices with their start and end apart: 20 -> 20, of which waited for: 6 -> 5; matrix products, arithmetic and copies ran while one was open for 0% -> 0% of each run, Pallas kernels for 41% -> 44%
where the time goes in v13:
time: 51.3 us; the launch traced here: 51.1 us
  Pallas kernels  23.4 us (46%)
  starting transfers between devices  21.4 us (42%)
  waiting for transfers between devices  5.42 us (11%)
  between operations  0.79 us (2%)
    ppermute x10, starting transfers between devices, ring_step(): lax.ppermute(block, 'section', way)  12.1 us
    pallas_call x1, Pallas kernels, per_device(): pl.pallas_call(own_kernel, in_specs=[smem, vmem, vmem, hbm] + [hbm] * len...  4.9 us
    pallas_call x2, Pallas kernels, per_device(): pl.pallas_call(functools.partial(attend_kernel, first, len(whole)), in_sp...  4.57 us
    pallas_call x1, Pallas kernels, per_device(): pl.pallas_call(functools.partial(send_more_kernel, video), in_specs=[smem...  4.01 us
    pallas_call x8, Pallas kernels, plain_call(): pl.pallas_call(kernel, in_specs=[pl.BlockSpec(memory_space=pltpu.VMEM)] *...  3.57 us
    pallas_call x1, Pallas kernels, per_device(): pl.pallas_call(send_kernel, in_specs=[smem] + [hbm] * 5, out_specs=[vmem]...  3.4 us
    pallas_call x1, Pallas kernels, per_device(): pl.pallas_call(part_kernel, in_specs=[smem, hbm, vmem, vmem], out_specs=[...  2.94 us
    ppermute x2, starting transfers between devices, per_device(): other_attended.append(lax.ppermute(attended[-1], 'head', swap_head))  2.67 us
  transfers between devices with their start and end apart: 20, of which 5 were waited for; matrix products, arithmetic and copies ran while one was open for 0% of the time, Pallas kernels for 44%

profile of v13, /device:TPU:0, one launch (start us, length us, event | category | flops | bytes accessed | tf_op | source)
XLA Modules:
  0.0 51.1 jit_solution(10185928430682674251)
XLA Ops:
  0.6 3.1 %collective-permute-start.2 = (bf16[2,128,768]{2,1,0:T(8,128)(2,1)}, bf16[2,128,768]{2,1,0:T(8,128)(2,1)S(1)}, u32[]{:S(2)}, u32[]{:S(2)}) collective-permute-start(bf16[2,128,768]{2,1,0:T(8,128)(2,1)} %refs_5_.1), channel_id=1, source_target_pairs={{0,8},{2,6},{4,0},{6,14},{8,16},{10,2},{12,4},{14,22},{16,24},{18,... | collective-permute-start | bytes 1179656 | tf_op jit(solution)/shard_map/ppermute | solution.py:482
  3.8 3.4 %project_send.1 = (bf16[272,1536]{1,0:T(8,128)(2,1)S(1)}, bf16[688,128]{1,0:T(8,128)(2,1)S(1)}, f32[272,128]{1,0:T(8,128)S(1)}, bf16[1536,768]{1,0:T(8,128)(2,1)S(1)}) custom-call(s32[2]{0:T(128)S(1)} %pad_add_fusion.place_ref, bf16[128,1536]{1,0:T(8,128)(2,1)} %refs_4_.1, bf16[256,1536]{1,0:T(8,128)(2,1)} %t_ref.1, f32[1536]{0:T(1024)} %scale_ref.1, ...), custom_call_target="tpu_custom_call" | custom-call | flops 3080296960 | bytes 2831155 | tf_op jit(solution)/shard_map/project_send/pallas_call | solution.py:497
  7.2 2.0 %collective-permute-start = (bf16[688,128]{1,0:T(8,128)(2,1)S(1)}, bf16[688,128]{1,0:T(8,128)(2,1)S(1)}, u32[]{:S(2)}, u32[]{:S(2)}) collective-permute-start(bf16[688,128]{1,0:T(8,128)(2,1)S(1)} %get-tuple-element.47), channel_id=1, source_target_pairs={{0,1},{1,0},{2,3},{3,2},{4,5},{5,4},{6,7},{7,6},{8,9},{9,8},{10,11... | collective-permute-start | bytes 528392 | tf_op jit(solution)/shard_map/ppermute | solution.py:519
  9.2 4.0 %project_send_more.1 = (bf16[3280,128]{1,0:T(8,128)(2,1)S(1)}, bf16[1536,768]{1,0:T(8,128)(2,1)S(1)}) custom-call(s32[2]{0:T(128)S(1)} %pad_add_fusion.place_ref, bf16[272,1536]{1,0:T(8,128)(2,1)S(1)} %get-tuple-element.43.a_ref, bf16[1536,768]{1,0:T(8,128)(2,1)S(1)} %get-tuple-element.44.ahead_ref, bf16[1536,4608]{1,0:T(8,128)(2,1)} %w_ref.5), custom_call_target="tpu_custom_call" | custom-call | flops 4620445184 | bytes 4246732 | tf_op jit(solution)/shard_map/project_send_more/pallas_call | solution.py:521
  13.5 2.1 %collective-permute-start.4 = (bf16[2,128,384]{2,1,0:T(8,128)(2,1)S(1)}, bf16[2,128,384]{2,1,0:T(8,128)(2,1)S(1)}, u32[]{:S(2)}, u32[]{:S(2)}) collective-permute-start(bf16[2,128,384]{2,1,0:T(8,128)(2,1)S(1)} %get-tuple-element.51), channel_id=1, source_target_pairs={{0,8},{2,6},{4,0},{6,14},{8,16},{10,2},{12,4},{14,22},{16,24},{18,... | collective-permute-start | bytes 589832 | tf_op jit(solution)/shard_map/ppermute | solution.py:482
  15.9 1.7 %collective-permute-start.6 = (bf16[2,128,384]{2,1,0:T(8,128)(2,1)S(1)}, bf16[2,128,384]{2,1,0:T(8,128)(2,1)S(1)}, u32[]{:S(2)}, u32[]{:S(2)}) collective-permute-start(bf16[2,128,384]{2,1,0:T(8,128)(2,1)S(1)} %get-tuple-element.53), channel_id=1, source_target_pairs={{0,8},{2,6},{4,0},{6,14},{8,16},{10,2},{12,4},{14,22},{16,24},{18,... | collective-permute-start | bytes 589832 | tf_op jit(solution)/shard_map/ppermute | solution.py:482
  17.9 4.9 %project_own.1 = (f32[144,2304]{1,0:T(8,128)S(1)}, f32[128,1536]{1,0:T(8,128)S(1)}, f32[128]{0:T(128)S(1)}, f32[128]{0:T(128)S(1)}, s32[256]{0:T(256)S(1)}, /*in...) custom-call(s32[2]{0:T(128)S(1)} %pad_add_fusion.place_ref, ...), custom_call_target="tpu_custom_call" | custom-call | flops 7700742144 | bytes 7077888 | tf_op jit(solution)/shard_map/project_own/pallas_call | solution.py:547
  22.8 1.7 %collective-permute-start.9 = (bf16[2,128,384]{2,1,0:T(8,128)(2,1)S(1)}, bf16[2,128,384]{2,1,0:T(8,128)(2,1)S(1)}, u32[]{:S(2)}, u32[]{:S(2)}) collective-permute-start(bf16[2,128,384]{2,1,0:T(8,128)(2,1)S(1)} %collective-permute-done.4.refs_2_), channel_id=1, source_target_pairs={{0,8},{2,6},{4,0},{6,14},{8,16},{10,2},{12,4},{14,22},{16,24},{18,... | collective-permute-start | bytes 589832 | tf_op jit(solution)/shard_map/ppermute | solution.py:482
  24.9 2.0 %collective-permute-start.14 = (bf16[2,128,384]{2,1,0:T(8,128)(2,1)S(1)}, bf16[2,128,384]{2,1,0:T(8,128)(2,1)S(1)}, u32[]{:S(2)}, u32[]{:S(2)}) collective-permute-start(bf16[2,128,384]{2,1,0:T(8,128)(2,1)S(1)} %collective-permute-done.6.refs_2_), channel_id=1, source_target_pairs={{0,8},{2,6},{4,0},{6,14},{8,16},{10,2},{12,4},{14,22},{16,24},{18,... | collective-permute-start | bytes 589832 | tf_op jit(solution)/shard_map/ppermute | solution.py:482
  27.5 1.1 %collective-permute-done.9.refs_4_ = bf16[2,128,384]{2,1,0:T(8,128)(2,1)S(1)} collective-permute-done((bf16[2,128,384]{2,1,0:T(8,128)(2,1)S(1)}, bf16[2,128,384]{2,1,0:T(8,128)(2,1)S(1)}, u32[]{:S(2)}, u32[]{:S(2)}) %collective-permute-start.9) | collective-permute-done | bytes 196640 | tf_op jit(solution)/shard_map/ppermute | solution.py:482
  28.6 1.7 %collective-permute-start.11 = (bf16[2,128,384]{2,1,0:T(8,128)(2,1)S(1)}, bf16[2,128,384]{2,1,0:T(8,128)(2,1)S(1)}, u32[]{:S(2)}, u32[]{:S(2)}) collective-permute-start(bf16[2,128,384]{2,1,0:T(8,128)(2,1)S(1)} %collective-permute-done.9.refs_4_), channel_id=1, source_target_pairs={{0,8},{2,6},{4,0},{6,14},{8,16},{10,2},{12,4},{14,22},{16,24},{18,... | collective-permute-start | bytes 589832 | tf_op jit(solution)/shard_map/ppermute | solution.py:570
  30.6 2.3 %collective-permute-done.1.more_ref = bf16[3280,128]{1,0:T(8,128)(2,1)S(1)} collective-permute-done((bf16[3280,128]{1,0:T(8,128)(2,1)S(1)}, bf16[3280,128]{1,0:T(8,128)(2,1)S(1)}, u32[]{:S(2)}, u32[]{:S(2)}) %collective-permute-start.1) | collective-permute-done | bytes 839712 | tf_op jit(solution)/shard_map/ppermute | solution.py:538
  32.9 0.5 %norm_text.1.text_ref = bf16[2,128,768]{2,1,0:T(8,128)(2,1)S(1)} custom-call(f32[128,1536]{1,0:T(8,128)S(1)} %get-tuple-element.62.own_ref, bf16[688,128]{1,0:T(8,128)(2,1)S(1)} %collective-permute-done.first_ref, bf16[3280,128]{1,0:T(8,128)(2,1)S(1)} %collective-permute-done.1.more_ref, f32[272,128]{1,0:T(8,128)S(1)} %get-tuple-element.56.stat_ref, ...), custom_call_target="tpu_custom_call" | custom-call | flops 294912 | bytes 294912 | tf_op jit(solution)/shard_map/norm_text/pallas_call | solution.py:437
  33.4 0.7 %norm_video.1 = (bf16[128,384]{1,0:T(8,128)(2,1)S(1)}, bf16[128,384]{1,0:T(8,128)(2,1)S(1)}, bf16[2,128,768]{2,1,0:T(8,128)(2,1)S(1)}) custom-call(f32[144,2304]{1,0:T(8,128)S(1)} %get-tuple-element.46.own_ref.top_ref, bf16[688,128]{1,0:T(8,128)(2,1)S(1)} %collective-permute-done.first_ref, bf16[3280,128]{1,0:T(8,128)(2,1)S(1)} %collective-permute-done.1.more_ref, ...), custom_call_target="tpu_custom_call" | custom-call | flops 331776000 | bytes 2654208 | tf_op jit(solution)/shard_map/norm_video/pallas_call | solution.py:437
  34.1 1.6 %collective-permute-start.16 = (bf16[2,128,384]{2,1,0:T(8,128)(2,1)S(1)}, bf16[2,128,384]{2,1,0:T(8,128)(2,1)S(1)}, u32[]{:S(2)}, u32[]{:S(2)}) collective-permute-start(bf16[2,128,384]{2,1,0:T(8,128)(2,1)S(1)} %collective-permute-done.14.refs_4_), channel_id=1, source_target_pairs={{0,8},{2,6},{4,0},{6,14},{8,16},{10,2},{12,4},{14,22},{16,24},{18,... | collective-permute-start | bytes 589832 | tf_op jit(solution)/shard_map/ppermute | solution.py:590
  35.7 0.5 collective-permute-start.13
  36.3 0.8 %collective-permute-done.8.qp_ref = bf16[128,384]{1,0:T(8,128)(2,1)S(1)} collective-permute-done((bf16[128,384]{1,0:T(8,128)(2,1)S(1)}, bf16[128,384]{1,0:T(8,128)(2,1)S(1)}, u32[]{:S(2)}, u32[]{:S(2)}) %collective-permute-start.8) | collective-permute-done | bytes 98336 | tf_op jit(solution)/shard_map/ppermute | solution.py:580
  37.0 2.2 %attend.2 = (f32[256,384]{1,0:T(8,128)S(1)}, f32[256,128]{1,0:T(8,128)S(1)}) custom-call(s32[2]{0:T(128)S(1)} %pad_add_fusion.place_ref, bf16[128,384]{1,0:T(8,128)(2,1)S(1)} %get-tuple-element.59.qo_ref, bf16[128,384]{1,0:T(8,128)(2,1)S(1)} %collective-permute-done.8.qp_ref, bf16[2,128,768]{2,1,0:T(8,128)(2,1)S(1)} %get-tuple-element.60.fresh_ref, ...), custom_call_target="tpu_custom_call" | custom-call | flops 163840 | bytes 983040 | tf_op jit(solution)/shard_map/attend/pallas_call | solution.py:612
  40.0 2.3 %attend.3 = (f32[128,384]{1,0:T(8,128)S(1)}, f32[128,128]{1,0:T(8,128)S(1)}, f32[128,512]{1,0:T(8,128)S(1)}, bf16[2,128,768]{2,1,0:T(8,128)(2,1)}) custom-call(s32[2]{0:T(128)S(1)} %pad_add_fusion.place_ref, bf16[128,384]{1,0:T(8,128)(2,1)S(1)} %get-tuple-element.72.qo_ref, bf16[128,384]{1,0:T(8,128)(2,1)S(1)} %collective-permute-done.13.qp_ref, ...), custom_call_target="tpu_custom_call" | custom-call | flops 163840 | bytes 983040 | tf_op jit(solution)/shard_map/attend/pallas_call | solution.py:612
  42.9 1.3 %collective-permute-start.18 = (bf16[128,384]{1,0:T(8,128)(2,1)S(1)}, bf16[128,384]{1,0:T(8,128)(2,1)S(1)}, u32[]{:S(2)}, u32[]{:S(2)}) collective-permute-start(bf16[128,384]{1,0:T(8,128)(2,1)S(1)} %merge.2.first_ref), channel_id=1, source_target_pairs={{0,1},{1,0},{2,3},{3,2},{4,5},{5,4},{6,7},{7,6},{8,9},{9,8},{10,11... | collective-permute-start | bytes 294920 | tf_op jit(solution)/shard_map/ppermute | solution.py:644
  44.4 1.4 %collective-permute-start.19 = (bf16[128,384]{1,0:T(8,128)(2,1)S(1)}, bf16[128,384]{1,0:T(8,128)(2,1)S(1)}, u32[]{:S(2)}, u32[]{:S(2)}) collective-permute-start(bf16[128,384]{1,0:T(8,128)(2,1)S(1)} %merge.3.second_ref), channel_id=1, source_target_pairs={{0,1},{1,0},{2,3},{3,2},{4,5},{5,4},{6,7},{7,6},{8,9},{9,8},{10,11... | collective-permute-start | bytes 294920 | tf_op jit(solution)/shard_map/ppermute | solution.py:644
  45.7 2.9 %part_out.1 = (f32[128,1536]{1,0:T(8,128)S(1)}, bf16[768,1536]{1,0:T(8,128)(2,1)S(1)}) custom-call(s32[2]{0:T(128)S(1)} %pad_add_fusion.place_ref, bf16[1536,1536]{1,0:T(8,128)(2,1)} %weight_ref.1, bf16[128,384]{1,0:T(8,128)(2,1)S(1)} %merge.2.first_ref, bf16[128,384]{1,0:T(8,128)(2,1)S(1)} %merge.3.second_ref), custom_call_target="tpu_custom_call" | custom-call | flops 603979776 | bytes 2359296 | tf_op jit(solution)/shard_map/part_out/pallas_call | solution.py:647
  49.1 0.9 %collective-permute-done.19.att_ref = bf16[128,384]{1,0:T(8,128)(2,1)S(1)} collective-permute-done((bf16[128,384]{1,0:T(8,128)(2,1)S(1)}, bf16[128,384]{1,0:T(8,128)(2,1)S(1)}, u32[]{:S(2)}, u32[]{:S(2)}) %collective-permute-start.19) | collective-permute-done | bytes 98336 | tf_op jit(solution)/shard_map/ppermute | solution.py:644
  50.0 1.1 %final_out.1 = bf16[128,1536]{1,0:T(8,128)(2,1)} custom-call(f32[128,1536]{1,0:T(8,128)S(1)} %more_out.1.part_ref, bf16[128,384]{1,0:T(8,128)(2,1)S(1)} %collective-permute-done.19.att_ref, bf16[768,1536]{1,0:T(8,128)(2,1)S(1)} %get-tuple-element.80.w_ref, bf16[128,1536]{1,0:T(8,128)(2,1)S(1)} %get-tuple-element.81.hidden_ref, ...), custom_call_target="tpu_custom_call" | custom-call | flops 603979776 | bytes 2359296 | tf_op jit(solution)/shard_map/final_out/pallas_call | solution.py:437
  (31 shorter events, 4.0 us)
Async XLA Ops:
  0.6 12.8 %collective-permute-start.2 = (bf16[2,128,768]{2,1,0:T(8,128)(2,1)}, bf16[2,128,768]{2,1,0:T(8,128)(2,1)S(1)}, u32[]{:S(2)}, u32[]{:S(2)}) collective-permute-start(bf16[2,128,768]{2,1,0:T(8,128)(2,1)} %refs_5_.1), channel_id=1, source_target_pairs={{0,8},{2,6},{4,0},{6,14},{8,16},{10,2},{12,4},{14,22},{16,24},{18,... | collective-permute-start | bytes 1179656 | tf_op jit(solution)/shard_map/ppermute | solution.py:482
  3.7 9.7 %collective-permute-start.3 = (bf16[2,128,768]{2,1,0:T(8,128)(2,1)}, bf16[2,128,768]{2,1,0:T(8,128)(2,1)S(1)}, u32[]{:S(2)}, u32[]{:S(2)}) collective-permute-start(bf16[2,128,768]{2,1,0:T(8,128)(2,1)} %refs_5_.1), channel_id=1, source_target_pairs={{0,4},{2,10},{4,12},{6,2},{8,0},{10,18},{12,20},{14,6},{16,8},{18,... | collective-permute-start | bytes 1179656 | tf_op jit(solution)/shard_map/ppermute | solution.py:482
  7.2 6.2 %collective-permute-start = (bf16[688,128]{1,0:T(8,128)(2,1)S(1)}, bf16[688,128]{1,0:T(8,128)(2,1)S(1)}, u32[]{:S(2)}, u32[]{:S(2)}) collective-permute-start(bf16[688,128]{1,0:T(8,128)(2,1)S(1)} %get-tuple-element.47), channel_id=1, source_target_pairs={{0,1},{1,0},{2,3},{3,2},{4,5},{5,4},{6,7},{7,6},{8,9},{9,8},{10,11... | collective-permute-start | bytes 528392 | tf_op jit(solution)/shard_map/ppermute | solution.py:519
  13.2 19.6 %collective-permute-start.1 = (bf16[3280,128]{1,0:T(8,128)(2,1)S(1)}, bf16[3280,128]{1,0:T(8,128)(2,1)S(1)}, u32[]{:S(2)}, u32[]{:S(2)}) collective-permute-start(bf16[3280,128]{1,0:T(8,128)(2,1)S(1)} %get-tuple-element.48), channel_id=1, source_target_pairs={{0,1},{1,0},{2,3},{3,2},{4,5},{5,4},{6,7},{7,6},{8,9},{9,8},{10,11... | collective-permute-start | bytes 2519048 | tf_op jit(solution)/shard_map/ppermute | solution.py:538
  13.5 9.4 %collective-permute-start.4 = (bf16[2,128,384]{2,1,0:T(8,128)(2,1)S(1)}, bf16[2,128,384]{2,1,0:T(8,128)(2,1)S(1)}, u32[]{:S(2)}, u32[]{:S(2)}) collective-permute-start(bf16[2,128,384]{2,1,0:T(8,128)(2,1)S(1)} %get-tuple-element.51), channel_id=1, source_target_pairs={{0,8},{2,6},{4,0},{6,14},{8,16},{10,2},{12,4},{14,22},{16,24},{18,... | collective-permute-start | bytes 589832 | tf_op jit(solution)/shard_map/ppermute | solution.py:482
  15.5 7.3 %collective-permute-start.5 = (bf16[2,128,384]{2,1,0:T(8,128)(2,1)S(1)}, bf16[2,128,384]{2,1,0:T(8,128)(2,1)S(1)}, u32[]{:S(2)}, u32[]{:S(2)}) collective-permute-start(bf16[2,128,384]{2,1,0:T(8,128)(2,1)S(1)} %get-tuple-element.52), channel_id=1, source_target_pairs={{0,4},{2,10},{4,12},{6,2},{8,0},{10,18},{12,20},{14,6},{16,8},{18,... | collective-permute-start | bytes 589832 | tf_op jit(solution)/shard_map/ppermute | solution.py:482
  15.9 9.0 %collective-permute-start.6 = (bf16[2,128,384]{2,1,0:T(8,128)(2,1)S(1)}, bf16[2,128,384]{2,1,0:T(8,128)(2,1)S(1)}, u32[]{:S(2)}, u32[]{:S(2)}) collective-permute-start(bf16[2,128,384]{2,1,0:T(8,128)(2,1)S(1)} %get-tuple-element.53), channel_id=1, source_target_pairs={{0,8},{2,6},{4,0},{6,14},{8,16},{10,2},{12,4},{14,22},{16,24},{18,... | collective-permute-start | bytes 589832 | tf_op jit(solution)/shard_map/ppermute | solution.py:482
  17.6 7.4 %collective-permute-start.7 = (bf16[2,128,384]{2,1,0:T(8,128)(2,1)S(1)}, bf16[2,128,384]{2,1,0:T(8,128)(2,1)S(1)}, u32[]{:S(2)}, u32[]{:S(2)}) collective-permute-start(bf16[2,128,384]{2,1,0:T(8,128)(2,1)S(1)} %get-tuple-element.54), channel_id=1, source_target_pairs={{0,4},{2,10},{4,12},{6,2},{8,0},{10,18},{12,20},{14,6},{16,8},{18,... | collective-permute-start | bytes 589832 | tf_op jit(solution)/shard_map/ppermute | solution.py:482
  22.8 5.7 %collective-permute-start.9 = (bf16[2,128,384]{2,1,0:T(8,128)(2,1)S(1)}, bf16[2,128,384]{2,1,0:T(8,128)(2,1)S(1)}, u32[]{:S(2)}, u32[]{:S(2)}) collective-permute-start(bf16[2,128,384]{2,1,0:T(8,128)(2,1)S(1)} %collective-permute-done.4.refs_2_), channel_id=1, source_target_pairs={{0,8},{2,6},{4,0},{6,14},{8,16},{10,2},{12,4},{14,22},{16,24},{18,... | collective-permute-start | bytes 589832 | tf_op jit(solution)/shard_map/ppermute | solution.py:482
  24.9 9.2 %collective-permute-start.14 = (bf16[2,128,384]{2,1,0:T(8,128)(2,1)S(1)}, bf16[2,128,384]{2,1,0:T(8,128)(2,1)S(1)}, u32[]{:S(2)}, u32[]{:S(2)}) collective-permute-start(bf16[2,128,384]{2,1,0:T(8,128)(2,1)S(1)} %collective-permute-done.6.refs_2_), channel_id=1, source_target_pairs={{0,8},{2,6},{4,0},{6,14},{8,16},{10,2},{12,4},{14,22},{16,24},{18,... | collective-permute-start | bytes 589832 | tf_op jit(solution)/shard_map/ppermute | solution.py:482
  27.0 8.8 %collective-permute-start.10 = (bf16[2,128,384]{2,1,0:T(8,128)(2,1)S(1)}, bf16[2,128,384]{2,1,0:T(8,128)(2,1)S(1)}, u32[]{:S(2)}, u32[]{:S(2)}) collective-permute-start(bf16[2,128,384]{2,1,0:T(8,128)(2,1)S(1)} %collective-permute-done.5.refs_3_), channel_id=1, source_target_pairs={{0,4},{2,10},{4,12},{6,2},{8,0},{10,18},{12,20},{14,6},{16,8},{18,... | collective-permute-start | bytes 589832 | tf_op jit(solution)/shard_map/ppermute | solution.py:482
  28.6 10.7 %collective-permute-start.11 = (bf16[2,128,384]{2,1,0:T(8,128)(2,1)S(1)}, bf16[2,128,384]{2,1,0:T(8,128)(2,1)S(1)}, u32[]{:S(2)}, u32[]{:S(2)}) collective-permute-start(bf16[2,128,384]{2,1,0:T(8,128)(2,1)S(1)} %collective-permute-done.9.refs_4_), channel_id=1, source_target_pairs={{0,8},{2,6},{4,0},{6,14},{8,16},{10,2},{12,4},{14,22},{16,24},{18,... | collective-permute-start | bytes 589832 | tf_op jit(solution)/shard_map/ppermute | solution.py:570
  30.3 9.7 %collective-permute-start.15 = (bf16[2,128,384]{2,1,0:T(8,128)(2,1)S(1)}, bf16[2,128,384]{2,1,0:T(8,128)(2,1)S(1)}, u32[]{:S(2)}, u32[]{:S(2)}) collective-permute-start(bf16[2,128,384]{2,1,0:T(8,128)(2,1)S(1)} %collective-permute-done.7.refs_3_), channel_id=1, source_target_pairs={{0,4},{2,10},{4,12},{6,2},{8,0},{10,18},{12,20},{14,6},{16,8},{18,... | collective-permute-start | bytes 589832 | tf_op jit(solution)/shard_map/ppermute | solution.py:482
  34.1 5.9 %collective-permute-start.16 = (bf16[2,128,384]{2,1,0:T(8,128)(2,1)S(1)}, bf16[2,128,384]{2,1,0:T(8,128)(2,1)S(1)}, u32[]{:S(2)}, u32[]{:S(2)}) collective-permute-start(bf16[2,128,384]{2,1,0:T(8,128)(2,1)S(1)} %collective-permute-done.14.refs_4_), channel_id=1, source_target_pairs={{0,8},{2,6},{4,0},{6,14},{8,16},{10,2},{12,4},{14,22},{16,24},{18,... | collective-permute-start | bytes 589832 | tf_op jit(solution)/shard_map/ppermute | solution.py:590
  35.7 1.3 %collective-permute-start.8 = (bf16[128,384]{1,0:T(8,128)(2,1)S(1)}, bf16[128,384]{1,0:T(8,128)(2,1)S(1)}, u32[]{:S(2)}, u32[]{:S(2)}) collective-permute-start(bf16[128,384]{1,0:T(8,128)(2,1)S(1)} %get-tuple-element.59.qo_ref), channel_id=1, source_target_pairs={{0,2},{2,0},{4,6},{6,4},{8,10},{10,8},{12,14},{14,12},{16,18},{18,... | collective-permute-start | bytes 294920 | tf_op jit(solution)/shard_map/ppermute | solution.py:580
  35.7 4.3 %collective-permute-start.13 = (bf16[128,384]{1,0:T(8,128)(2,1)S(1)}, bf16[128,384]{1,0:T(8,128)(2,1)S(1)}, u32[]{:S(2)}, u32[]{:S(2)}) collective-permute-start(bf16[128,384]{1,0:T(8,128)(2,1)S(1)} %get-tuple-element.72.qo_ref), channel_id=1, source_target_pairs={{0,2},{2,0},{4,6},{6,4},{8,10},{10,8},{12,14},{14,12},{16,18},{18,... | collective-permute-start | bytes 294920 | tf_op jit(solution)/shard_map/ppermute | solution.py:580
  39.8 3.0 %collective-permute-start.12 = (f32[128,512]{1,0:T(8,128)S(1)}, f32[128,512]{1,0:T(8,128)S(1)}, u32[]{:S(2)}, u32[]{:S(2)}) collective-permute-start(f32[128,512]{1,0:T(8,128)S(1)} %get-tuple-element.70), channel_id=1, source_target_pairs={{0,2},{2,0},{4,6},{6,4},{8,10},{10,8},{12,14},{14,12},{16,18},{18,... | collective-permute-start | bytes 786440 | tf_op jit(solution)/shard_map/ppermute | solution.py:636
  42.4 1.9 %collective-permute-start.17 = (f32[128,512]{1,0:T(8,128)S(1)}, f32[128,512]{1,0:T(8,128)S(1)}, u32[]{:S(2)}, u32[]{:S(2)}) collective-permute-start(f32[128,512]{1,0:T(8,128)S(1)} %get-tuple-element.78), channel_id=1, source_target_pairs={{0,2},{2,0},{4,6},{6,4},{8,10},{10,8},{12,14},{14,12},{16,18},{18,... | collective-permute-start | bytes 786440 | tf_op jit(solution)/shard_map/ppermute | solution.py:636
  42.9 5.8 %collective-permute-start.18 = (bf16[128,384]{1,0:T(8,128)(2,1)S(1)}, bf16[128,384]{1,0:T(8,128)(2,1)S(1)}, u32[]{:S(2)}, u32[]{:S(2)}) collective-permute-start(bf16[128,384]{1,0:T(8,128)(2,1)S(1)} %merge.2.first_ref), channel_id=1, source_target_pairs={{0,1},{1,0},{2,3},{3,2},{4,5},{5,4},{6,7},{7,6},{8,9},{9,8},{10,11... | collective-permute-start | bytes 294920 | tf_op jit(solution)/shard_map/ppermute | solution.py:644
  44.4 5.6 %collective-permute-start.19 = (bf16[128,384]{1,0:T(8,128)(2,1)S(1)}, bf16[128,384]{1,0:T(8,128)(2,1)S(1)}, u32[]{:S(2)}, u32[]{:S(2)}) collective-permute-start(bf16[128,384]{1,0:T(8,128)(2,1)S(1)} %merge.3.second_ref), channel_id=1, source_target_pairs={{0,1},{1,0},{2,3},{3,2},{4,5},{5,4},{6,7},{7,6},{8,9},{9,8},{10,11... | collective-permute-start | bytes 294920 | tf_op jit(solution)/shard_map/ppermute | solution.py:644

commit v14 on v13

--- a/solution.py
+++ b/solution.py
@@ -122,52 +122,49 @@
 
 
 def send_more_kernel(
-    video, place_ref, a_ref, ahead_ref, w_ref, msg_ref, own_ahead_ref, w_buffer, last_buffer, sems,
+    video, place_ref, a_ref, ahead_ref, w_ref, msg_ref, w_buffer, last_buffer, sems,
 ):
     text = a_ref.shape[0] - video - EXTRA
     width = w_ref.shape[1] // 2
-    other, own = (1 - place_ref[0]) * width, place_ref[0] * width
+    other = (1 - place_ref[0]) * width
     first = width - last_buffer.shape[1]
     copies = [
         column_copy(w_ref, other + first - w_buffer.shape[1], w_buffer, sems.at[0]),
         column_copy(w_ref, other + first, last_buffer, sems.at[1]),
-        column_copy(w_ref, own, own_ahead_ref, sems.at[2]),
     ]
     copies[0].start()
     copies[1].start()
     partial_sums(a_ref, ahead_ref, video, text, msg_ref, 0)
     copies[0].wait()
-    copies[2].start()
     head = ahead_ref.shape[1] // TRIPLE
     partial_sums(a_ref, w_buffer, video, text, msg_ref, head)
     copies[1].wait()
     head += w_buffer.shape[1] // TRIPLE
     partial_sums(a_ref, last_buffer, video, text, msg_ref, head)
-    copies[2].wait()
-
-
-def own_kernel(place_ref, a_ref, ahead_ref, w_ref, *refs):
+
+
+def own_kernel(place_ref, a_ref, w_ref, *refs):
     small = (len(refs) - 4) // 2
     out_ref, text_ref = refs[small : small + 2]
     w_buffer, sems = refs[-2:]
     top = out_ref.shape[0]
-    later, _, columns = w_buffer.shape
-    base = place_ref[0] * (w_ref.shape[1] // 2) + columns
+    blocks, _, columns = w_buffer.shape
+    base = place_ref[0] * (w_ref.shape[1] // 2)
     copies = [
         column_copy(w_ref, base + index * columns, w_buffer.at[index], sems.at[index])
-        for index in range(later)
+        for index in range(blocks)
     ]
     for source, target in zip(refs[:small], refs[small + 2 : -2]):
         copies.append(pltpu.make_async_copy(source, target, sems.at[len(copies)]))
-    for copy in copies:
+    for copy in copies[:2]:
         copy.start()
 
-    for block in range(later + 1):
-        if block:
-            copies[block - 1].wait()
+    for block in range(blocks):
+        copies[block].wait()
+        for copy in copies[2:3] if block == 0 else copies[3:] if block == 1 else ():
+            copy.start()
         for start in range(0, columns, PIECE):
-            cells = slice(start, start + PIECE)
-            part = w_buffer[block - 1, :, cells] if block else ahead_ref[:, cells]
+            part = w_buffer[block, :, start : start + PIECE]
             product = jnp.dot(a_ref[...], part, preferred_element_type=F32)
             first = block * columns + start
             out_ref[:, first : first + PIECE] = product[:top]
@@ -178,7 +175,7 @@
                     text_ref[:, target : target + HEAD_DIM] = product[
                         top:, local : local + HEAD_DIM
                     ]
-    for copy in copies[later:]:
+    for copy in copies[blocks:]:
         copy.wait()
 
 
@@ -518,18 +515,15 @@
     )(place, *map(in_hbm, (hidden, text_hidden, norm_scale, norm_shift, qkv_weight)))
     received = lax.ppermute(message, "head", swap_head)
 
-    message_more, own_ahead = pl.pallas_call(
+    message_more = pl.pallas_call(
         functools.partial(send_more_kernel, video),
         in_specs=[smem, vmem, vmem, hbm],
-        out_specs=[vmem] * 2,
-        out_shape=[
-            jax.ShapeDtypeStruct(((heads - 1) * per_head, HEAD_DIM), BF16),
-            jax.ShapeDtypeStruct((features, columns), BF16),
-        ],
+        out_specs=vmem,
+        out_shape=jax.ShapeDtypeStruct(((heads - 1) * per_head, HEAD_DIM), BF16),
         scratch_shapes=[
             pltpu.VMEM((features, group_columns - columns - 2 * TRIPLE), BF16),
             pltpu.VMEM((features, TRIPLE), BF16),
-            pltpu.SemaphoreType.DMA((3,)),
+            pltpu.SemaphoreType.DMA((2,)),
         ],
         compiler_params=params(40),
         cost_estimate=project_cost(0.6),
@@ -546,7 +540,7 @@
     small = (query_gain, key_gain, text_mask, branch_gate, hidden, stale_cache)
     outs = pl.pallas_call(
         own_kernel,
-        in_specs=[smem, vmem, vmem, hbm] + [hbm] * len(small),
+        in_specs=[smem, vmem, hbm] + [hbm] * len(small),
         out_specs=[vmem] * (2 + len(small)),
         out_shape=[
             jax.ShapeDtypeStruct((top, group_columns), F32),
@@ -554,13 +548,13 @@
         ]
         + [jax.ShapeDtypeStruct(array.shape, array.dtype) for array in small],
         scratch_shapes=[
-            pltpu.VMEM((blocks - 1, features, columns), BF16),
-            pltpu.SemaphoreType.DMA((blocks - 1 + len(small),)),
+            pltpu.VMEM((blocks, features, columns), BF16),
+            pltpu.SemaphoreType.DMA((blocks + len(small),)),
         ],
         compiler_params=params(40),
         cost_estimate=project_cost(1),
         name="project_own",
-    )(place, a_rows, own_ahead, *map(in_hbm, (qkv_weight,) + small))
+    )(place, a_rows, *map(in_hbm, (qkv_weight,) + small))
     own, own_text = outs[:2]
     query_gain, key_gain, text_mask, branch_gate, hidden, stale = outs[2:]
 
@@ -583,7 +577,8 @@
         [((2, text, width), BF16)],
         "norm_text",
         cost(text * group_columns, text * group_columns),
-        own_text, received, received_more, stats, own, key_gain,
+        lax.optimization_barrier((own_text, queries[0]))[0], received, received_more, stats, own,
+        key_gain,
     )
 
     last = lax.optimization_barrier((chains[1][-1][0], text_kv, queries[0]))[0]

time: 51.3 us -> 53.6 us (1.045)
  waiting for transfers between devices: 5.42 us -> 7.22 us
  Pallas kernels: 23.4 us -> 24.2 us
    ppermute x10, waiting for transfers between devices: 1.47 us -> 4.8 us  [ring_step(): lax.ppermute(block, 'section', way)]
    ppermute x1, waiting for transfers between devices: 2.27 us -> 0.01 us  [per_device(): received_more = lax.ppermute(message_more, 'head', swap_head)]
    ppermute x1, waiting for transfers between devices: 0.01 us -> 0.91 us  [per_device(): far.append(lax.ppermute(last, 'section', ways[0]))]
    ppermute x1, starting transfers between devices: 1.63 us -> 0.89 us  [per_device(): far.append(lax.ppermute(last, 'section', ways[0]))]
    pallas_call x1, Pallas kernels: 4.01 us -> 4.6 us  [per_device(): pl.pallas_call(functools.partial(send_more_kernel, video), in_specs=[smem...]
    ppermute x2, starting transfers between devices: 2.67 us -> 3.21 us  [per_device(): other_attended.append(lax.ppermute(attended[-1], 'head', swap_head))]
  transfers between devices with their start and end apart: 20 -> 20, of which waited for: 5 -> 5; matrix products, arithmetic and copies ran while one was open for 0% -> 0% of each run, Pallas kernels for 44% -> 43%
where the time goes in v14:
time: 53.6 us; the launch traced here: 53.4 us
  Pallas kernels  24.2 us (45%)
  starting transfers between devices  21.1 us (39%)
  waiting for transfers between devices  7.22 us (13%)
  between operations  0.78 us (1%)
    ppermute x10, starting transfers between devices, ring_step(): lax.ppermute(block, 'section', way)  12.7 us
    pallas_call x1, Pallas kernels, per_device(): pl.pallas_call(own_kernel, in_specs=[smem, vmem, hbm] + [hbm] * len(small...  5.17 us
    ppermute x10, waiting for transfers between devices, ring_step(): lax.ppermute(block, 'section', way)  4.8 us
    pallas_call x1, Pallas kernels, per_device(): pl.pallas_call(functools.partial(send_more_kernel, video), in_specs=[smem...  4.6 us
    pallas_call x2, Pallas kernels, per_device(): pl.pallas_call(functools.partial(attend_kernel, first, len(whole)), in_sp...  4.56 us
    pallas_call x8, Pallas kernels, plain_call(): pl.pallas_call(kernel, in_specs=[pl.BlockSpec(memory_space=pltpu.VMEM)] *...  3.58 us
    pallas_call x1, Pallas kernels, per_device(): pl.pallas_call(send_kernel, in_specs=[smem] + [hbm] * 5, out_specs=[vmem]...  3.4 us
    ppermute x2, starting transfers between devices, per_device(): other_attended.append(lax.ppermute(attended[-1], 'head', swap_head))  3.21 us
  transfers between devices with their start and end apart: 20, of which 5 were waited for; matrix products, arithmetic and copies ran while one was open for 0% of the time, Pallas kernels for 43%

profile of v14, /device:TPU:0, one launch (start us, length us, event | category | flops | bytes accessed | tf_op | source)
XLA Modules:
  0.0 53.4 jit_solution(7674247633175602806)
XLA Ops:
  0.6 3.1 %collective-permute-start.2 = (bf16[2,128,768]{2,1,0:T(8,128)(2,1)}, bf16[2,128,768]{2,1,0:T(8,128)(2,1)S(1)}, u32[]{:S(2)}, u32[]{:S(2)}) collective-permute-start(bf16[2,128,768]{2,1,0:T(8,128)(2,1)} %refs_5_.1), channel_id=1, source_target_pairs={{0,8},{2,6},{4,0},{6,14},{8,16},{10,2},{12,4},{14,22},{16,24},{18,... | collective-permute-start | bytes 1179656 | tf_op jit(solution)/shard_map/ppermute | solution.py:479
  3.8 3.4 %project_send.1 = (bf16[272,1536]{1,0:T(8,128)(2,1)S(1)}, bf16[688,128]{1,0:T(8,128)(2,1)S(1)}, f32[272,128]{1,0:T(8,128)S(1)}, bf16[1536,768]{1,0:T(8,128)(2,1)S(1)}) custom-call(s32[2]{0:T(128)S(1)} %pad_add_fusion.place_ref, bf16[128,1536]{1,0:T(8,128)(2,1)} %refs_4_.1, bf16[256,1536]{1,0:T(8,128)(2,1)} %t_ref.1, f32[1536]{0:T(1024)} %scale_ref.1, ...), custom_call_target="tpu_custom_call" | custom-call | flops 3080296960 | bytes 2831155 | tf_op jit(solution)/shard_map/project_send/pallas_call | solution.py:494
  7.2 2.0 %collective-permute-start = (bf16[688,128]{1,0:T(8,128)(2,1)S(1)}, bf16[688,128]{1,0:T(8,128)(2,1)S(1)}, u32[]{:S(2)}, u32[]{:S(2)}) collective-permute-start(bf16[688,128]{1,0:T(8,128)(2,1)S(1)} %get-tuple-element.44), channel_id=1, source_target_pairs={{0,1},{1,0},{2,3},{3,2},{4,5},{5,4},{6,7},{7,6},{8,9},{9,8},{10,11... | collective-permute-start | bytes 528392 | tf_op jit(solution)/shard_map/ppermute | solution.py:516
  9.2 4.6 %project_send_more.1 = bf16[3280,128]{1,0:T(8,128)(2,1)S(1)} custom-call(s32[2]{0:T(128)S(1)} %pad_add_fusion.place_ref, bf16[272,1536]{1,0:T(8,128)(2,1)S(1)} %get-tuple-element.42.a_ref, bf16[1536,768]{1,0:T(8,128)(2,1)S(1)} %get-tuple-element.45.ahead_ref, bf16[1536,4608]{1,0:T(8,128)(2,1)} %w_ref.5), custom_call_target="tpu_custom_call" | custom-call | flops 4620445184 | bytes 4246732 | tf_op jit(solution)/shard_map/project_send_more/pallas_call | solution.py:518
  14.1 2.1 %collective-permute-start.6 = (bf16[2,128,384]{2,1,0:T(8,128)(2,1)S(1)}, bf16[2,128,384]{2,1,0:T(8,128)(2,1)S(1)}, u32[]{:S(2)}, u32[]{:S(2)}) collective-permute-start(bf16[2,128,384]{2,1,0:T(8,128)(2,1)S(1)} %get-tuple-element.50), channel_id=1, source_target_pairs={{0,8},{2,6},{4,0},{6,14},{8,16},{10,2},{12,4},{14,22},{16,24},{18,... | collective-permute-start | bytes 589832 | tf_op jit(solution)/shard_map/ppermute | solution.py:479
  16.1 2.0 %collective-permute-start.4 = (bf16[2,128,384]{2,1,0:T(8,128)(2,1)S(1)}, bf16[2,128,384]{2,1,0:T(8,128)(2,1)S(1)}, u32[]{:S(2)}, u32[]{:S(2)}) collective-permute-start(bf16[2,128,384]{2,1,0:T(8,128)(2,1)S(1)} %get-tuple-element.48), channel_id=1, source_target_pairs={{0,8},{2,6},{4,0},{6,14},{8,16},{10,2},{12,4},{14,22},{16,24},{18,... | collective-permute-start | bytes 589832 | tf_op jit(solution)/shard_map/ppermute | solution.py:479
  18.2 5.2 %project_own.1 = (f32[144,2304]{1,0:T(8,128)S(1)}, f32[128,1536]{1,0:T(8,128)S(1)}, f32[128]{0:T(128)S(1)}, f32[128]{0:T(128)S(1)}, s32[256]{0:T(256)S(1)}, /*in...) custom-call(s32[2]{0:T(128)S(1)} %pad_add_fusion.place_ref, ...), custom_call_target="tpu_custom_call" | custom-call | flops 7700742144 | bytes 7077888 | tf_op jit(solution)/shard_map/project_own/pallas_call | solution.py:541
  23.3 2.2 %collective-permute-done.4.refs_2_ = bf16[2,128,384]{2,1,0:T(8,128)(2,1)S(1)} collective-permute-done((bf16[2,128,384]{2,1,0:T(8,128)(2,1)S(1)}, bf16[2,128,384]{2,1,0:T(8,128)(2,1)S(1)}, u32[]{:S(2)}, u32[]{:S(2)}) %collective-permute-start.4) | collective-permute-done | bytes 196640 | tf_op jit(solution)/shard_map/ppermute | solution.py:479
  25.6 1.4 %collective-permute-start.9 = (bf16[2,128,384]{2,1,0:T(8,128)(2,1)S(1)}, bf16[2,128,384]{2,1,0:T(8,128)(2,1)S(1)}, u32[]{:S(2)}, u32[]{:S(2)}) collective-permute-start(bf16[2,128,384]{2,1,0:T(8,128)(2,1)S(1)} %collective-permute-done.4.refs_2_), channel_id=1, source_target_pairs={{0,8},{2,6},{4,0},{6,14},{8,16},{10,2},{12,4},{14,22},{16,24},{18,... | collective-permute-start | bytes 589832 | tf_op jit(solution)/shard_map/ppermute | solution.py:479
  27.6 1.4 %collective-permute-start.10 = (bf16[2,128,384]{2,1,0:T(8,128)(2,1)S(1)}, bf16[2,128,384]{2,1,0:T(8,128)(2,1)S(1)}, u32[]{:S(2)}, u32[]{:S(2)}) collective-permute-start(bf16[2,128,384]{2,1,0:T(8,128)(2,1)S(1)} %collective-permute-done.5.refs_3_), channel_id=1, source_target_pairs={{0,4},{2,10},{4,12},{6,2},{8,0},{10,18},{12,20},{14,6},{16,8},{18,... | collective-permute-start | bytes 589832 | tf_op jit(solution)/shard_map/ppermute | solution.py:479
  29.0 2.5 %collective-permute-done.9.refs_4_ = bf16[2,128,384]{2,1,0:T(8,128)(2,1)S(1)} collective-permute-done((bf16[2,128,384]{2,1,0:T(8,128)(2,1)S(1)}, bf16[2,128,384]{2,1,0:T(8,128)(2,1)S(1)}, u32[]{:S(2)}, u32[]{:S(2)}) %collective-permute-start.9) | collective-permute-done | bytes 196640 | tf_op jit(solution)/shard_map/ppermute | solution.py:479
  31.5 1.4 %collective-permute-start.11 = (bf16[2,128,384]{2,1,0:T(8,128)(2,1)S(1)}, bf16[2,128,384]{2,1,0:T(8,128)(2,1)S(1)}, u32[]{:S(2)}, u32[]{:S(2)}) collective-permute-start(bf16[2,128,384]{2,1,0:T(8,128)(2,1)S(1)} %collective-permute-done.9.refs_4_), channel_id=1, source_target_pairs={{0,8},{2,6},{4,0},{6,14},{8,16},{10,2},{12,4},{14,22},{16,24},{18,... | collective-permute-start | bytes 589832 | tf_op jit(solution)/shard_map/ppermute | solution.py:564
  32.9 2.1 %collective-permute-start.15 = (bf16[2,128,384]{2,1,0:T(8,128)(2,1)S(1)}, bf16[2,128,384]{2,1,0:T(8,128)(2,1)S(1)}, u32[]{:S(2)}, u32[]{:S(2)}) collective-permute-start(bf16[2,128,384]{2,1,0:T(8,128)(2,1)S(1)} %collective-permute-done.7.refs_3_), channel_id=1, source_target_pairs={{0,4},{2,10},{4,12},{6,2},{8,0},{10,18},{12,20},{14,6},{16,8},{18,... | collective-permute-start | bytes 589832 | tf_op jit(solution)/shard_map/ppermute | solution.py:479
  35.0 0.7 %norm_video.1 = (bf16[128,384]{1,0:T(8,128)(2,1)S(1)}, bf16[128,384]{1,0:T(8,128)(2,1)S(1)}, bf16[2,128,768]{2,1,0:T(8,128)(2,1)S(1)}) custom-call(f32[144,2304]{1,0:T(8,128)S(1)} %get-tuple-element.43.own_ref.top_ref, bf16[688,128]{1,0:T(8,128)(2,1)S(1)} %collective-permute-done.first_ref, bf16[3280,128]{1,0:T(8,128)(2,1)S(1)} %collective-permute-done.1.more_ref, ...), custom_call_target="tpu_custom_call" | custom-call | flops 331776000 | bytes 2654208 | tf_op jit(solution)/shard_map/norm_video/pallas_call | solution.py:434
  36.3 0.9 %collective-permute-start.16 = (bf16[2,128,384]{2,1,0:T(8,128)(2,1)S(1)}, bf16[2,128,384]{2,1,0:T(8,128)(2,1)S(1)}, u32[]{:S(2)}, u32[]{:S(2)}) collective-permute-start(bf16[2,128,384]{2,1,0:T(8,128)(2,1)S(1)} %collective-permute-done.14.refs_4_), channel_id=1, source_target_pairs={{0,8},{2,6},{4,0},{6,14},{8,16},{10,2},{12,4},{14,22},{16,24},{18,... | collective-permute-start | bytes 589832 | tf_op jit(solution)/shard_map/ppermute | solution.py:585
  37.7 0.8 %collective-permute-done.8.qp_ref = bf16[128,384]{1,0:T(8,128)(2,1)S(1)} collective-permute-done((bf16[128,384]{1,0:T(8,128)(2,1)S(1)}, bf16[128,384]{1,0:T(8,128)(2,1)S(1)}, u32[]{:S(2)}, u32[]{:S(2)}) %collective-permute-start.8) | collective-permute-done | bytes 98336 | tf_op jit(solution)/shard_map/ppermute | solution.py:574
  38.5 2.2 %attend.2 = (f32[256,384]{1,0:T(8,128)S(1)}, f32[256,128]{1,0:T(8,128)S(1)}) custom-call(s32[2]{0:T(128)S(1)} %pad_add_fusion.place_ref, bf16[128,384]{1,0:T(8,128)(2,1)S(1)} %get-tuple-element.56.qo_ref, bf16[128,384]{1,0:T(8,128)(2,1)S(1)} %collective-permute-done.8.qp_ref, bf16[2,128,768]{2,1,0:T(8,128)(2,1)S(1)} %get-tuple-element.57.fresh_ref, ...), custom_call_target="tpu_custom_call" | custom-call | flops 163840 | bytes 983040 | tf_op jit(solution)/shard_map/attend/pallas_call | solution.py:607
  41.4 0.9 %collective-permute-done.16.refs_6_ = bf16[2,128,384]{2,1,0:T(8,128)(2,1)S(1)} collective-permute-done((bf16[2,128,384]{2,1,0:T(8,128)(2,1)S(1)}, bf16[2,128,384]{2,1,0:T(8,128)(2,1)S(1)}, u32[]{:S(2)}, u32[]{:S(2)}) %collective-permute-start.16) | collective-permute-done | bytes 196640 | tf_op jit(solution)/shard_map/ppermute | solution.py:585
  42.3 2.3 %attend.3 = (f32[128,384]{1,0:T(8,128)S(1)}, f32[128,128]{1,0:T(8,128)S(1)}, f32[128,512]{1,0:T(8,128)S(1)}, bf16[2,128,768]{2,1,0:T(8,128)(2,1)}) custom-call(s32[2]{0:T(128)S(1)} %pad_add_fusion.place_ref, bf16[128,384]{1,0:T(8,128)(2,1)S(1)} %get-tuple-element.70.qo_ref, bf16[128,384]{1,0:T(8,128)(2,1)S(1)} %collective-permute-done.13.qp_ref, ...), custom_call_target="tpu_custom_call" | custom-call | flops 163840 | bytes 983040 | tf_op jit(solution)/shard_map/attend/pallas_call | solution.py:607
  44.9 1.8 %collective-permute-start.18 = (bf16[128,384]{1,0:T(8,128)(2,1)S(1)}, bf16[128,384]{1,0:T(8,128)(2,1)S(1)}, u32[]{:S(2)}, u32[]{:S(2)}) collective-permute-start(bf16[128,384]{1,0:T(8,128)(2,1)S(1)} %merge.2.first_ref), channel_id=1, source_target_pairs={{0,1},{1,0},{2,3},{3,2},{4,5},{5,4},{6,7},{7,6},{8,9},{9,8},{10,11... | collective-permute-start | bytes 294920 | tf_op jit(solution)/shard_map/ppermute | solution.py:639
  46.9 1.4 %collective-permute-start.19 = (bf16[128,384]{1,0:T(8,128)(2,1)S(1)}, bf16[128,384]{1,0:T(8,128)(2,1)S(1)}, u32[]{:S(2)}, u32[]{:S(2)}) collective-permute-start(bf16[128,384]{1,0:T(8,128)(2,1)S(1)} %merge.3.second_ref), channel_id=1, source_target_pairs={{0,1},{1,0},{2,3},{3,2},{4,5},{5,4},{6,7},{7,6},{8,9},{9,8},{10,11... | collective-permute-start | bytes 294920 | tf_op jit(solution)/shard_map/ppermute | solution.py:639
  48.3 2.9 %part_out.1 = (f32[128,1536]{1,0:T(8,128)S(1)}, bf16[768,1536]{1,0:T(8,128)(2,1)S(1)}) custom-call(s32[2]{0:T(128)S(1)} %pad_add_fusion.place_ref, bf16[1536,1536]{1,0:T(8,128)(2,1)} %weight_ref.1, bf16[128,384]{1,0:T(8,128)(2,1)S(1)} %merge.2.first_ref, bf16[128,384]{1,0:T(8,128)(2,1)S(1)} %merge.3.second_ref), custom_call_target="tpu_custom_call" | custom-call | flops 603979776 | bytes 2359296 | tf_op jit(solution)/shard_map/part_out/pallas_call | solution.py:642
  51.6 0.7 %collective-permute-done.19.att_ref = bf16[128,384]{1,0:T(8,128)(2,1)S(1)} collective-permute-done((bf16[128,384]{1,0:T(8,128)(2,1)S(1)}, bf16[128,384]{1,0:T(8,128)(2,1)S(1)}, u32[]{:S(2)}, u32[]{:S(2)}) %collective-permute-start.19) | collective-permute-done | bytes 98336 | tf_op jit(solution)/shard_map/ppermute | solution.py:639
  52.3 1.1 %final_out.1 = bf16[128,1536]{1,0:T(8,128)(2,1)} custom-call(f32[128,1536]{1,0:T(8,128)S(1)} %more_out.1.part_ref, bf16[128,384]{1,0:T(8,128)(2,1)S(1)} %collective-permute-done.19.att_ref, bf16[768,1536]{1,0:T(8,128)(2,1)S(1)} %get-tuple-element.78.w_ref, bf16[128,1536]{1,0:T(8,128)(2,1)S(1)} %get-tuple-element.79.hidden_ref, ...), custom_call_target="tpu_custom_call" | custom-call | flops 603979776 | bytes 2359296 | tf_op jit(solution)/shard_map/final_out/pallas_call | solution.py:434
  (31 shorter events, 3.5 us)
Async XLA Ops:
  0.6 13.3 %collective-permute-start.2 = (bf16[2,128,768]{2,1,0:T(8,128)(2,1)}, bf16[2,128,768]{2,1,0:T(8,128)(2,1)S(1)}, u32[]{:S(2)}, u32[]{:S(2)}) collective-permute-start(bf16[2,128,768]{2,1,0:T(8,128)(2,1)} %refs_5_.1), channel_id=1, source_target_pairs={{0,8},{2,6},{4,0},{6,14},{8,16},{10,2},{12,4},{14,22},{16,24},{18,... | collective-permute-start | bytes 1179656 | tf_op jit(solution)/shard_map/ppermute | solution.py:479
  3.7 10.3 %collective-permute-start.3 = (bf16[2,128,768]{2,1,0:T(8,128)(2,1)}, bf16[2,128,768]{2,1,0:T(8,128)(2,1)S(1)}, u32[]{:S(2)}, u32[]{:S(2)}) collective-permute-start(bf16[2,128,768]{2,1,0:T(8,128)(2,1)} %refs_5_.1), channel_id=1, source_target_pairs={{0,4},{2,10},{4,12},{6,2},{8,0},{10,18},{12,20},{14,6},{16,8},{18,... | collective-permute-start | bytes 1179656 | tf_op jit(solution)/shard_map/ppermute | solution.py:479
  7.2 6.8 %collective-permute-start = (bf16[688,128]{1,0:T(8,128)(2,1)S(1)}, bf16[688,128]{1,0:T(8,128)(2,1)S(1)}, u32[]{:S(2)}, u32[]{:S(2)}) collective-permute-start(bf16[688,128]{1,0:T(8,128)(2,1)S(1)} %get-tuple-element.44), channel_id=1, source_target_pairs={{0,1},{1,0},{2,3},{3,2},{4,5},{5,4},{6,7},{7,6},{8,9},{9,8},{10,11... | collective-permute-start | bytes 528392 | tf_op jit(solution)/shard_map/ppermute | solution.py:516
  13.8 21.2 %collective-permute-start.1 = (bf16[3280,128]{1,0:T(8,128)(2,1)S(1)}, bf16[3280,128]{1,0:T(8,128)(2,1)S(1)}, u32[]{:S(2)}, u32[]{:S(2)}) collective-permute-start(bf16[3280,128]{1,0:T(8,128)(2,1)S(1)} %project_send_more.1), channel_id=1, source_target_pairs={{0,1},{1,0},{2,3},{3,2},{4,5},{5,4},{6,7},{7,6},{8,9},{9,8},{10,11... | collective-permute-start | bytes 2519048 | tf_op jit(solution)/shard_map/ppermute | solution.py:532
  14.1 12.9 %collective-permute-start.6 = (bf16[2,128,384]{2,1,0:T(8,128)(2,1)S(1)}, bf16[2,128,384]{2,1,0:T(8,128)(2,1)S(1)}, u32[]{:S(2)}, u32[]{:S(2)}) collective-permute-start(bf16[2,128,384]{2,1,0:T(8,128)(2,1)S(1)} %get-tuple-element.50), channel_id=1, source_target_pairs={{0,8},{2,6},{4,0},{6,14},{8,16},{10,2},{12,4},{14,22},{16,24},{18,... | collective-permute-start | bytes 589832 | tf_op jit(solution)/shard_map/ppermute | solution.py:479
  16.1 10.8 %collective-permute-start.7 = (bf16[2,128,384]{2,1,0:T(8,128)(2,1)S(1)}, bf16[2,128,384]{2,1,0:T(8,128)(2,1)S(1)}, u32[]{:S(2)}, u32[]{:S(2)}) collective-permute-start(bf16[2,128,384]{2,1,0:T(8,128)(2,1)S(1)} %get-tuple-element.51), channel_id=1, source_target_pairs={{0,4},{2,10},{4,12},{6,2},{8,0},{10,18},{12,20},{14,6},{16,8},{18,... | collective-permute-start | bytes 589832 | tf_op jit(solution)/shard_map/ppermute | solution.py:479
  16.1 9.5 %collective-permute-start.4 = (bf16[2,128,384]{2,1,0:T(8,128)(2,1)S(1)}, bf16[2,128,384]{2,1,0:T(8,128)(2,1)S(1)}, u32[]{:S(2)}, u32[]{:S(2)}) collective-permute-start(bf16[2,128,384]{2,1,0:T(8,128)(2,1)S(1)} %get-tuple-element.48), channel_id=1, source_target_pairs={{0,8},{2,6},{4,0},{6,14},{8,16},{10,2},{12,4},{14,22},{16,24},{18,... | collective-permute-start | bytes 589832 | tf_op jit(solution)/shard_map/ppermute | solution.py:479
  18.1 7.4 %collective-permute-start.5 = (bf16[2,128,384]{2,1,0:T(8,128)(2,1)S(1)}, bf16[2,128,384]{2,1,0:T(8,128)(2,1)S(1)}, u32[]{:S(2)}, u32[]{:S(2)}) collective-permute-start(bf16[2,128,384]{2,1,0:T(8,128)(2,1)S(1)} %get-tuple-element.49), channel_id=1, source_target_pairs={{0,4},{2,10},{4,12},{6,2},{8,0},{10,18},{12,20},{14,6},{16,8},{18,... | collective-permute-start | bytes 589832 | tf_op jit(solution)/shard_map/ppermute | solution.py:479
  25.6 5.9 %collective-permute-start.9 = (bf16[2,128,384]{2,1,0:T(8,128)(2,1)S(1)}, bf16[2,128,384]{2,1,0:T(8,128)(2,1)S(1)}, u32[]{:S(2)}, u32[]{:S(2)}) collective-permute-start(bf16[2,128,384]{2,1,0:T(8,128)(2,1)S(1)} %collective-permute-done.4.refs_2_), channel_id=1, source_target_pairs={{0,8},{2,6},{4,0},{6,14},{8,16},{10,2},{12,4},{14,22},{16,24},{18,... | collective-permute-start | bytes 589832 | tf_op jit(solution)/shard_map/ppermute | solution.py:479
  27.0 9.3 %collective-permute-start.14 = (bf16[2,128,384]{2,1,0:T(8,128)(2,1)S(1)}, bf16[2,128,384]{2,1,0:T(8,128)(2,1)S(1)}, u32[]{:S(2)}, u32[]{:S(2)}) collective-permute-start(bf16[2,128,384]{2,1,0:T(8,128)(2,1)S(1)} %collective-permute-done.6.refs_2_), channel_id=1, source_target_pairs={{0,8},{2,6},{4,0},{6,14},{8,16},{10,2},{12,4},{14,22},{16,24},{18,... | collective-permute-start | bytes 589832 | tf_op jit(solution)/shard_map/ppermute | solution.py:479
  27.6 9.5 %collective-permute-start.10 = (bf16[2,128,384]{2,1,0:T(8,128)(2,1)S(1)}, bf16[2,128,384]{2,1,0:T(8,128)(2,1)S(1)}, u32[]{:S(2)}, u32[]{:S(2)}) collective-permute-start(bf16[2,128,384]{2,1,0:T(8,128)(2,1)S(1)} %collective-permute-done.5.refs_3_), channel_id=1, source_target_pairs={{0,4},{2,10},{4,12},{6,2},{8,0},{10,18},{12,20},{14,6},{16,8},{18,... | collective-permute-start | bytes 589832 | tf_op jit(solution)/shard_map/ppermute | solution.py:479
  31.5 9.2 %collective-permute-start.11 = (bf16[2,128,384]{2,1,0:T(8,128)(2,1)S(1)}, bf16[2,128,384]{2,1,0:T(8,128)(2,1)S(1)}, u32[]{:S(2)}, u32[]{:S(2)}) collective-permute-start(bf16[2,128,384]{2,1,0:T(8,128)(2,1)S(1)} %collective-permute-done.9.refs_4_), channel_id=1, source_target_pairs={{0,8},{2,6},{4,0},{6,14},{8,16},{10,2},{12,4},{14,22},{16,24},{18,... | collective-permute-start | bytes 589832 | tf_op jit(solution)/shard_map/ppermute | solution.py:564
  32.9 8.5 %collective-permute-start.15 = (bf16[2,128,384]{2,1,0:T(8,128)(2,1)S(1)}, bf16[2,128,384]{2,1,0:T(8,128)(2,1)S(1)}, u32[]{:S(2)}, u32[]{:S(2)}) collective-permute-start(bf16[2,128,384]{2,1,0:T(8,128)(2,1)S(1)} %collective-permute-done.7.refs_3_), channel_id=1, source_target_pairs={{0,4},{2,10},{4,12},{6,2},{8,0},{10,18},{12,20},{14,6},{16,8},{18,... | collective-permute-start | bytes 589832 | tf_op jit(solution)/shard_map/ppermute | solution.py:479
  36.3 6.1 %collective-permute-start.16 = (bf16[2,128,384]{2,1,0:T(8,128)(2,1)S(1)}, bf16[2,128,384]{2,1,0:T(8,128)(2,1)S(1)}, u32[]{:S(2)}, u32[]{:S(2)}) collective-permute-start(bf16[2,128,384]{2,1,0:T(8,128)(2,1)S(1)} %collective-permute-done.14.refs_4_), channel_id=1, source_target_pairs={{0,8},{2,6},{4,0},{6,14},{8,16},{10,2},{12,4},{14,22},{16,24},{18,... | collective-permute-start | bytes 589832 | tf_op jit(solution)/shard_map/ppermute | solution.py:585
  37.1 1.3 %collective-permute-start.8 = (bf16[128,384]{1,0:T(8,128)(2,1)S(1)}, bf16[128,384]{1,0:T(8,128)(2,1)S(1)}, u32[]{:S(2)}, u32[]{:S(2)}) collective-permute-start(bf16[128,384]{1,0:T(8,128)(2,1)S(1)} %get-tuple-element.56.qo_ref), channel_id=1, source_target_pairs={{0,2},{2,0},{4,6},{6,4},{8,10},{10,8},{12,14},{14,12},{16,18},{18,... | collective-permute-start | bytes 294920 | tf_op jit(solution)/shard_map/ppermute | solution.py:574
  37.2 4.3 %collective-permute-start.13 = (bf16[128,384]{1,0:T(8,128)(2,1)S(1)}, bf16[128,384]{1,0:T(8,128)(2,1)S(1)}, u32[]{:S(2)}, u32[]{:S(2)}) collective-permute-start(bf16[128,384]{1,0:T(8,128)(2,1)S(1)} %get-tuple-element.70.qo_ref), channel_id=1, source_target_pairs={{0,2},{2,0},{4,6},{6,4},{8,10},{10,8},{12,14},{14,12},{16,18},{18,... | collective-permute-start | bytes 294920 | tf_op jit(solution)/shard_map/ppermute | solution.py:574
  41.2 3.6 %collective-permute-start.12 = (f32[128,512]{1,0:T(8,128)S(1)}, f32[128,512]{1,0:T(8,128)S(1)}, u32[]{:S(2)}, u32[]{:S(2)}) collective-permute-start(f32[128,512]{1,0:T(8,128)S(1)} %get-tuple-element.68), channel_id=1, source_target_pairs={{0,2},{2,0},{4,6},{6,4},{8,10},{10,8},{12,14},{14,12},{16,18},{18,... | collective-permute-start | bytes 786440 | tf_op jit(solution)/shard_map/ppermute | solution.py:631
  44.7 2.1 %collective-permute-start.17 = (f32[128,512]{1,0:T(8,128)S(1)}, f32[128,512]{1,0:T(8,128)S(1)}, u32[]{:S(2)}, u32[]{:S(2)}) collective-permute-start(f32[128,512]{1,0:T(8,128)S(1)} %get-tuple-element.76), channel_id=1, source_target_pairs={{0,2},{2,0},{4,6},{6,4},{8,10},{10,8},{12,14},{14,12},{16,18},{18,... | collective-permute-start | bytes 786440 | tf_op jit(solution)/shard_map/ppermute | solution.py:631
  44.9 6.3 %collective-permute-start.18 = (bf16[128,384]{1,0:T(8,128)(2,1)S(1)}, bf16[128,384]{1,0:T(8,128)(2,1)S(1)}, u32[]{:S(2)}, u32[]{:S(2)}) collective-permute-start(bf16[128,384]{1,0:T(8,128)(2,1)S(1)} %merge.2.first_ref), channel_id=1, source_target_pairs={{0,1},{1,0},{2,3},{3,2},{4,5},{5,4},{6,7},{7,6},{8,9},{9,8},{10,11... | collective-permute-start | bytes 294920 | tf_op jit(solution)/shard_map/ppermute | solution.py:639
  46.9 5.4 %collective-permute-start.19 = (bf16[128,384]{1,0:T(8,128)(2,1)S(1)}, bf16[128,384]{1,0:T(8,128)(2,1)S(1)}, u32[]{:S(2)}, u32[]{:S(2)}) collective-permute-start(bf16[128,384]{1,0:T(8,128)(2,1)S(1)} %merge.3.second_ref), channel_id=1, source_target_pairs={{0,1},{1,0},{2,3},{3,2},{4,5},{5,4},{6,7},{7,6},{8,9},{9,8},{10,11... | collective-permute-start | bytes 294920 | tf_op jit(solution)/shard_map/ppermute | solution.py:639

commit v15 on v13

--- a/solution.py
+++ b/solution.py
@@ -412,11 +412,25 @@
     )
 
 
-def final_kernel(part_ref, att_ref, w_ref, hidden_ref, gate_ref, out_ref):
+def final_kernel(part_ref, att_ref, w_ref, hidden_ref, gate_ref, out_ref, buffer_ref, sems):
     half = att_ref.shape[1]
-    total = part_ref[...] + jnp.dot(att_ref[...], w_ref[half:, :], preferred_element_type=F32)
-    gate = gate_ref[...].reshape(1, total.shape[1])
-    out_ref[...] = (hidden_ref[...].astype(F32) + gate * total).astype(BF16)
+    gate = gate_ref[...].reshape(1, part_ref.shape[1])
+    count = sems.shape[0]
+    step = part_ref.shape[1] // count
+    copies = []
+    for index in range(count):
+        cells = slice(index * step, (index + 1) * step)
+        total = part_ref[:, cells] + jnp.dot(
+            att_ref[...], w_ref[half:, cells], preferred_element_type=F32
+        )
+        mixed = hidden_ref[:, cells].astype(F32) + gate[:, cells] * total
+        buffer_ref[:, cells] = mixed.astype(BF16)
+        copies.append(
+            pltpu.make_async_copy(buffer_ref.at[:, cells], out_ref.at[:, cells], sems.at[index])
+        )
+        copies[-1].start()
+    for copy in copies:
+        copy.wait()
 
 
 def params(megabytes):
@@ -577,7 +591,7 @@
         cost(1000 * top * group_columns, 8 * top * group_columns),
         own, received, received_more, stats, query_gain, key_gain,
     )
-    other_queries = [lax.ppermute(half, "section", swap_core) for half in queries]
+    other_queries = [lax.ppermute(queries[0], "section", swap_core)]
     (text_kv,) = plain_call(
         functools.partial(text_kernel, features * 2),
         [((2, text, width), BF16)],
@@ -625,6 +639,8 @@
         if finish:
             *outs, new_cache = outs
         else:
+            later = lax.optimization_barrier((queries[1], outs[0]))[0]
+            other_queries.append(lax.ppermute(later, "section", swap_core))
             outs = plain_call(
                 functools.partial(last_kernel, first),
                 [(out.shape, out.dtype) for out in finished],
@@ -664,10 +680,19 @@
         more_kernel, [((video, out_features), F32)], "more_out", out_cost,
         part, other_attended[0], w_other,
     )
-    (mixed,) = plain_call(
-        final_kernel, [((video, out_features), BF16)], "final_out", out_cost,
-        part, other_attended[1], w_other, hidden, branch_gate,
-    )
+    mixed = pl.pallas_call(
+        final_kernel,
+        in_specs=[vmem] * 5,
+        out_specs=hbm,
+        out_shape=jax.ShapeDtypeStruct((video, out_features), BF16),
+        scratch_shapes=[
+            pltpu.VMEM((video, out_features), BF16),
+            pltpu.SemaphoreType.DMA((out_features // 512,)),
+        ],
+        compiler_params=params(24),
+        cost_estimate=out_cost,
+        name="final_out",
+    )(part, other_attended[1], w_other, hidden, branch_gate)
     return (mixed, new_cache)
 
 

time: 51.3 us -> 52.7 us (1.027)
  waiting for transfers between devices: 5.42 us -> 8.3 us
  starting transfers between devices: 21.4 us -> 20 us
    ppermute x2, starting transfers between devices: 2.67 us -> 1.38 us  [per_device(): other_attended.append(lax.ppermute(attended[-1], 'head', swap_head))]
    ppermute x1, waiting for transfers between devices: 0.01 us -> 1.26 us  [per_device(): far.append(lax.ppermute(last, 'section', ways[0]))]
    ppermute x10, starting transfers between devices: 12.1 us -> 13.4 us  [ring_step(): lax.ppermute(block, 'section', way)]
    pallas_call x8 -> x7, Pallas kernels: 3.57 us -> 2.45 us  [plain_call(): pl.pallas_call(kernel, in_specs=[pl.BlockSpec(memory_space=pltpu.VMEM)] *...]
    pallas_call x0 -> x1, Pallas kernels: none -> 1.08 us  [per_device(): pl.pallas_call(final_kernel, in_specs=[vmem] * 5, out_specs=hbm, out_shap...]
    ppermute x1, starting transfers between devices: 1.63 us -> 0.56 us  [per_device(): far.append(lax.ppermute(last, 'section', ways[0]))]
    ppermute x2, waiting for transfers between devices: 0.87 us -> 1.66 us  [per_device(): other_attended.append(lax.ppermute(attended[-1], 'head', swap_head))]
    ppermute x2, waiting for transfers between devices: 0.79 us -> 0.01 us  [the longest x1 0.01 us: per_device(): other_queries = [lax.ppermute(queries[0], 'section', swap_core)]]
  transfers between devices with their start and end apart: 20 -> 20, of which waited for: 5 -> 8; matrix products, arithmetic and copies ran while one was open for 0% -> 0% of each run, Pallas kernels for 44% -> 42%
where the time goes in v15:
time: 52.7 us; the launch traced here: 52.5 us
  Pallas kernels  23.3 us (44%)
  starting transfers between devices  20 us (38%)
  waiting for transfers between devices  8.3 us (16%)
  between operations  0.79 us (1%)
    ppermute x10, starting transfers between devices, ring_step(): lax.ppermute(block, 'section', way)  13.4 us
    pallas_call x1, Pallas kernels, per_device(): pl.pallas_call(own_kernel, in_specs=[smem, vmem, vmem, hbm] + [hbm] * len...  4.9 us
    pallas_call x2, Pallas kernels, per_device(): pl.pallas_call(functools.partial(attend_kernel, first, len(whole)), in_sp...  4.56 us
    pallas_call x1, Pallas kernels, per_device(): pl.pallas_call(functools.partial(send_more_kernel, video), in_specs=[smem...  4.01 us
    pallas_call x1, Pallas kernels, per_device(): pl.pallas_call(send_kernel, in_specs=[smem] + [hbm] * 5, out_specs=[vmem]...  3.4 us
    pallas_call x1, Pallas kernels, per_device(): pl.pallas_call(part_kernel, in_specs=[smem, hbm, vmem, vmem], out_specs=[...  2.94 us
    ppermute x1, waiting for transfers between devices, per_device(): received_more = lax.ppermute(message_more, 'head', swap_head)  2.6 us
    pallas_call x7, Pallas kernels, plain_call(): pl.pallas_call(kernel, in_specs=[pl.BlockSpec(memory_space=pltpu.VMEM)] *...  2.45 us
  transfers between devices with their start and end apart: 20, of which 8 were waited for; matrix products, arithmetic and copies ran while one was open for 0% of the time, Pallas kernels for 42%

profile of v15, /device:TPU:0, one launch (start us, length us, event | category | flops | bytes accessed | tf_op | source)
XLA Modules:
  0.0 52.5 jit_solution(11993788779978486534)
XLA Ops:
  0.6 3.1 %collective-permute-start.2 = (bf16[2,128,768]{2,1,0:T(8,128)(2,1)}, bf16[2,128,768]{2,1,0:T(8,128)(2,1)S(1)}, u32[]{:S(2)}, u32[]{:S(2)}) collective-permute-start(bf16[2,128,768]{2,1,0:T(8,128)(2,1)} %refs_5_.1), channel_id=1, source_target_pairs={{0,8},{2,6},{4,0},{6,14},{8,16},{10,2},{12,4},{14,22},{16,24},{18,... | collective-permute-start | bytes 1179656 | tf_op jit(solution)/shard_map/ppermute | solution.py:496
  3.8 3.4 %project_send.1 = (bf16[272,1536]{1,0:T(8,128)(2,1)S(1)}, bf16[688,128]{1,0:T(8,128)(2,1)S(1)}, f32[272,128]{1,0:T(8,128)S(1)}, bf16[1536,768]{1,0:T(8,128)(2,1)S(1)}) custom-call(s32[2]{0:T(128)S(1)} %pad_add_fusion.place_ref, bf16[128,1536]{1,0:T(8,128)(2,1)} %refs_4_.1, bf16[256,1536]{1,0:T(8,128)(2,1)} %t_ref.1, f32[1536]{0:T(1024)} %scale_ref.1, ...), custom_call_target="tpu_custom_call" | custom-call | flops 3080296960 | bytes 2831155 | tf_op jit(solution)/shard_map/project_send/pallas_call | solution.py:511
  7.2 2.0 %collective-permute-start = (bf16[688,128]{1,0:T(8,128)(2,1)S(1)}, bf16[688,128]{1,0:T(8,128)(2,1)S(1)}, u32[]{:S(2)}, u32[]{:S(2)}) collective-permute-start(bf16[688,128]{1,0:T(8,128)(2,1)S(1)} %get-tuple-element.48), channel_id=1, source_target_pairs={{0,1},{1,0},{2,3},{3,2},{4,5},{5,4},{6,7},{7,6},{8,9},{9,8},{10,11... | collective-permute-start | bytes 528392 | tf_op jit(solution)/shard_map/ppermute | solution.py:533
  9.2 4.0 %project_send_more.1 = (bf16[3280,128]{1,0:T(8,128)(2,1)S(1)}, bf16[1536,768]{1,0:T(8,128)(2,1)S(1)}) custom-call(s32[2]{0:T(128)S(1)} %pad_add_fusion.place_ref, bf16[272,1536]{1,0:T(8,128)(2,1)S(1)} %get-tuple-element.44.a_ref, bf16[1536,768]{1,0:T(8,128)(2,1)S(1)} %get-tuple-element.45.ahead_ref, bf16[1536,4608]{1,0:T(8,128)(2,1)} %w_ref.5), custom_call_target="tpu_custom_call" | custom-call | flops 4620445184 | bytes 4246732 | tf_op jit(solution)/shard_map/project_send_more/pallas_call | solution.py:535
  13.5 2.1 %collective-permute-start.4 = (bf16[2,128,384]{2,1,0:T(8,128)(2,1)S(1)}, bf16[2,128,384]{2,1,0:T(8,128)(2,1)S(1)}, u32[]{:S(2)}, u32[]{:S(2)}) collective-permute-start(bf16[2,128,384]{2,1,0:T(8,128)(2,1)S(1)} %get-tuple-element.52), channel_id=1, source_target_pairs={{0,8},{2,6},{4,0},{6,14},{8,16},{10,2},{12,4},{14,22},{16,24},{18,... | collective-permute-start | bytes 589832 | tf_op jit(solution)/shard_map/ppermute | solution.py:496
  15.9 1.7 %collective-permute-start.6 = (bf16[2,128,384]{2,1,0:T(8,128)(2,1)S(1)}, bf16[2,128,384]{2,1,0:T(8,128)(2,1)S(1)}, u32[]{:S(2)}, u32[]{:S(2)}) collective-permute-start(bf16[2,128,384]{2,1,0:T(8,128)(2,1)S(1)} %get-tuple-element.54), channel_id=1, source_target_pairs={{0,8},{2,6},{4,0},{6,14},{8,16},{10,2},{12,4},{14,22},{16,24},{18,... | collective-permute-start | bytes 589832 | tf_op jit(solution)/shard_map/ppermute | solution.py:496
  17.9 4.9 %project_own.1 = (f32[144,2304]{1,0:T(8,128)S(1)}, f32[128,1536]{1,0:T(8,128)S(1)}, f32[128]{0:T(128)S(1)}, f32[128]{0:T(128)S(1)}, s32[256]{0:T(256)S(1)}, /*in...) custom-call(s32[2]{0:T(128)S(1)} %pad_add_fusion.place_ref, ...), custom_call_target="tpu_custom_call" | custom-call | flops 7700742144 | bytes 7077888 | tf_op jit(solution)/shard_map/project_own/pallas_call | solution.py:561
  22.8 1.7 %collective-permute-start.9 = (bf16[2,128,384]{2,1,0:T(8,128)(2,1)S(1)}, bf16[2,128,384]{2,1,0:T(8,128)(2,1)S(1)}, u32[]{:S(2)}, u32[]{:S(2)}) collective-permute-start(bf16[2,128,384]{2,1,0:T(8,128)(2,1)S(1)} %collective-permute-done.4.refs_2_), channel_id=1, source_target_pairs={{0,8},{2,6},{4,0},{6,14},{8,16},{10,2},{12,4},{14,22},{16,24},{18,... | collective-permute-start | bytes 589832 | tf_op jit(solution)/shard_map/ppermute | solution.py:496
  24.9 2.0 %collective-permute-start.14 = (bf16[2,128,384]{2,1,0:T(8,128)(2,1)S(1)}, bf16[2,128,384]{2,1,0:T(8,128)(2,1)S(1)}, u32[]{:S(2)}, u32[]{:S(2)}) collective-permute-start(bf16[2,128,384]{2,1,0:T(8,128)(2,1)S(1)} %collective-permute-done.6.refs_2_), channel_id=1, source_target_pairs={{0,8},{2,6},{4,0},{6,14},{8,16},{10,2},{12,4},{14,22},{16,24},{18,... | collective-permute-start | bytes 589832 | tf_op jit(solution)/shard_map/ppermute | solution.py:496
  27.5 1.1 %collective-permute-done.9.refs_4_ = bf16[2,128,384]{2,1,0:T(8,128)(2,1)S(1)} collective-permute-done((bf16[2,128,384]{2,1,0:T(8,128)(2,1)S(1)}, bf16[2,128,384]{2,1,0:T(8,128)(2,1)S(1)}, u32[]{:S(2)}, u32[]{:S(2)}) %collective-permute-start.9) | collective-permute-done | bytes 196640 | tf_op jit(solution)/shard_map/ppermute | solution.py:496
  28.6 1.7 %collective-permute-start.11 = (bf16[2,128,384]{2,1,0:T(8,128)(2,1)S(1)}, bf16[2,128,384]{2,1,0:T(8,128)(2,1)S(1)}, u32[]{:S(2)}, u32[]{:S(2)}) collective-permute-start(bf16[2,128,384]{2,1,0:T(8,128)(2,1)S(1)} %collective-permute-done.9.refs_4_), channel_id=1, source_target_pairs={{0,8},{2,6},{4,0},{6,14},{8,16},{10,2},{12,4},{14,22},{16,24},{18,... | collective-permute-start | bytes 589832 | tf_op jit(solution)/shard_map/ppermute | solution.py:584
  30.3 2.6 %collective-permute-done.1.more_ref = bf16[3280,128]{1,0:T(8,128)(2,1)S(1)} collective-permute-done((bf16[3280,128]{1,0:T(8,128)(2,1)S(1)}, bf16[3280,128]{1,0:T(8,128)(2,1)S(1)}, u32[]{:S(2)}, u32[]{:S(2)}) %collective-permute-start.1) | collective-permute-done | bytes 839712 | tf_op jit(solution)/shard_map/ppermute | solution.py:552
  32.9 0.7 %norm_video.1 = (bf16[128,384]{1,0:T(8,128)(2,1)S(1)}, bf16[128,384]{1,0:T(8,128)(2,1)S(1)}, bf16[2,128,768]{2,1,0:T(8,128)(2,1)S(1)}) custom-call(f32[144,2304]{1,0:T(8,128)S(1)} %get-tuple-element.47.own_ref.top_ref, bf16[688,128]{1,0:T(8,128)(2,1)S(1)} %collective-permute-done.first_ref, bf16[3280,128]{1,0:T(8,128)(2,1)S(1)} %collective-permute-done.1.more_ref, ...), custom_call_target="tpu_custom_call" | custom-call | flops 331776000 | bytes 2654208 | tf_op jit(solution)/shard_map/norm_video/pallas_call | solution.py:451
  33.6 1.6 %collective-permute-start.15 = (bf16[2,128,384]{2,1,0:T(8,128)(2,1)S(1)}, bf16[2,128,384]{2,1,0:T(8,128)(2,1)S(1)}, u32[]{:S(2)}, u32[]{:S(2)}) collective-permute-start(bf16[2,128,384]{2,1,0:T(8,128)(2,1)S(1)} %collective-permute-done.7.refs_3_), channel_id=1, source_target_pairs={{0,4},{2,10},{4,12},{6,2},{8,0},{10,18},{12,20},{14,6},{16,8},{18,... | collective-permute-start | bytes 589832 | tf_op jit(solution)/shard_map/ppermute | solution.py:496
  35.8 0.6 %collective-permute-start.16 = (bf16[2,128,384]{2,1,0:T(8,128)(2,1)S(1)}, bf16[2,128,384]{2,1,0:T(8,128)(2,1)S(1)}, u32[]{:S(2)}, u32[]{:S(2)}) collective-permute-start(bf16[2,128,384]{2,1,0:T(8,128)(2,1)S(1)} %collective-permute-done.14.refs_4_), channel_id=1, source_target_pairs={{0,8},{2,6},{4,0},{6,14},{8,16},{10,2},{12,4},{14,22},{16,24},{18,... | collective-permute-start | bytes 589832 | tf_op jit(solution)/shard_map/ppermute | solution.py:604
  36.3 2.2 %attend.2 = (f32[256,384]{1,0:T(8,128)S(1)}, f32[256,128]{1,0:T(8,128)S(1)}) custom-call(s32[2]{0:T(128)S(1)} %pad_add_fusion.place_ref, bf16[128,384]{1,0:T(8,128)(2,1)S(1)} %get-tuple-element.60.qo_ref, bf16[128,384]{1,0:T(8,128)(2,1)S(1)} %collective-permute-done.8.qp_ref, bf16[2,128,768]{2,1,0:T(8,128)(2,1)S(1)} %get-tuple-element.61.fresh_ref, ...), custom_call_target="tpu_custom_call" | custom-call | flops 163840 | bytes 983040 | tf_op jit(solution)/shard_map/attend/pallas_call | solution.py:626
  39.1 0.6 %collective-permute-start.12 = (f32[128,512]{1,0:T(8,128)S(1)}, f32[128,512]{1,0:T(8,128)S(1)}, u32[]{:S(2)}, u32[]{:S(2)}) collective-permute-start(f32[128,512]{1,0:T(8,128)S(1)} %get-tuple-element.71), channel_id=1, source_target_pairs={{0,2},{2,0},{4,6},{6,4},{8,10},{10,8},{12,14},{14,12},{16,18},{18,... | collective-permute-start | bytes 786440 | tf_op jit(solution)/shard_map/ppermute | solution.py:652
  40.2 1.3 %collective-permute-done.16.refs_6_ = bf16[2,128,384]{2,1,0:T(8,128)(2,1)S(1)} collective-permute-done((bf16[2,128,384]{2,1,0:T(8,128)(2,1)S(1)}, bf16[2,128,384]{2,1,0:T(8,128)(2,1)S(1)}, u32[]{:S(2)}, u32[]{:S(2)}) %collective-permute-start.16) | collective-permute-done | bytes 196640 | tf_op jit(solution)/shard_map/ppermute | solution.py:604
  41.5 2.3 %attend.3 = (f32[128,384]{1,0:T(8,128)S(1)}, f32[128,128]{1,0:T(8,128)S(1)}, f32[128,512]{1,0:T(8,128)S(1)}, bf16[2,128,768]{2,1,0:T(8,128)(2,1)}) custom-call(s32[2]{0:T(128)S(1)} %pad_add_fusion.place_ref, bf16[128,384]{1,0:T(8,128)(2,1)S(1)} %get-tuple-element.74.qo_ref, bf16[128,384]{1,0:T(8,128)(2,1)S(1)} %collective-permute-done.13.qp_ref, ...), custom_call_target="tpu_custom_call" | custom-call | flops 163840 | bytes 983040 | tf_op jit(solution)/shard_map/attend/pallas_call | solution.py:626
  44.7 0.8 %collective-permute-done.17.msg_ref = f32[128,512]{1,0:T(8,128)S(1)} collective-permute-done((f32[128,512]{1,0:T(8,128)S(1)}, f32[128,512]{1,0:T(8,128)S(1)}, u32[]{:S(2)}, u32[]{:S(2)}) %collective-permute-start.17) | collective-permute-done | bytes 262176 | tf_op jit(solution)/shard_map/ppermute | solution.py:652
  45.6 0.9 %collective-permute-start.19 = (bf16[128,384]{1,0:T(8,128)(2,1)S(1)}, bf16[128,384]{1,0:T(8,128)(2,1)S(1)}, u32[]{:S(2)}, u32[]{:S(2)}) collective-permute-start(bf16[128,384]{1,0:T(8,128)(2,1)S(1)} %merge.3.second_ref), channel_id=1, source_target_pairs={{0,1},{1,0},{2,3},{3,2},{4,5},{5,4},{6,7},{7,6},{8,9},{9,8},{10,11... | collective-permute-start | bytes 294920 | tf_op jit(solution)/shard_map/ppermute | solution.py:660
  46.4 2.9 %part_out.1 = (f32[128,1536]{1,0:T(8,128)S(1)}, bf16[768,1536]{1,0:T(8,128)(2,1)S(1)}) custom-call(s32[2]{0:T(128)S(1)} %pad_add_fusion.place_ref, bf16[1536,1536]{1,0:T(8,128)(2,1)} %weight_ref.1, bf16[128,384]{1,0:T(8,128)(2,1)S(1)} %merge.2.first_ref, bf16[128,384]{1,0:T(8,128)(2,1)S(1)} %merge.3.second_ref), custom_call_target="tpu_custom_call" | custom-call | flops 603979776 | bytes 2359296 | tf_op jit(solution)/shard_map/part_out/pallas_call | solution.py:663
  50.2 1.2 %collective-permute-done.19.att_ref = bf16[128,384]{1,0:T(8,128)(2,1)S(1)} collective-permute-done((bf16[128,384]{1,0:T(8,128)(2,1)S(1)}, bf16[128,384]{1,0:T(8,128)(2,1)S(1)}, u32[]{:S(2)}, u32[]{:S(2)}) %collective-permute-start.19) | collective-permute-done | bytes 98336 | tf_op jit(solution)/shard_map/ppermute | solution.py:660
  51.4 1.1 %final_out.1 = bf16[128,1536]{1,0:T(8,128)(2,1)} custom-call(f32[128,1536]{1,0:T(8,128)S(1)} %more_out.1.part_ref, bf16[128,384]{1,0:T(8,128)(2,1)S(1)} %collective-permute-done.19.att_ref, bf16[768,1536]{1,0:T(8,128)(2,1)S(1)} %get-tuple-element.82.w_ref, bf16[128,1536]{1,0:T(8,128)(2,1)S(1)} %get-tuple-element.83.hidden_ref, ...), custom_call_target="tpu_custom_call" | custom-call | flops 603979776 | bytes 2359296 | tf_op jit(solution)/shard_map/final_out/pallas_call | solution.py:683
  (31 shorter events, 5.3 us)
Async XLA Ops:
  0.6 12.8 %collective-permute-start.2 = (bf16[2,128,768]{2,1,0:T(8,128)(2,1)}, bf16[2,128,768]{2,1,0:T(8,128)(2,1)S(1)}, u32[]{:S(2)}, u32[]{:S(2)}) collective-permute-start(bf16[2,128,768]{2,1,0:T(8,128)(2,1)} %refs_5_.1), channel_id=1, source_target_pairs={{0,8},{2,6},{4,0},{6,14},{8,16},{10,2},{12,4},{14,22},{16,24},{18,... | collective-permute-start | bytes 1179656 | tf_op jit(solution)/shard_map/ppermute | solution.py:496
  3.7 9.7 %collective-permute-start.3 = (bf16[2,128,768]{2,1,0:T(8,128)(2,1)}, bf16[2,128,768]{2,1,0:T(8,128)(2,1)S(1)}, u32[]{:S(2)}, u32[]{:S(2)}) collective-permute-start(bf16[2,128,768]{2,1,0:T(8,128)(2,1)} %refs_5_.1), channel_id=1, source_target_pairs={{0,4},{2,10},{4,12},{6,2},{8,0},{10,18},{12,20},{14,6},{16,8},{18,... | collective-permute-start | bytes 1179656 | tf_op jit(solution)/shard_map/ppermute | solution.py:496
  7.2 6.2 %collective-permute-start = (bf16[688,128]{1,0:T(8,128)(2,1)S(1)}, bf16[688,128]{1,0:T(8,128)(2,1)S(1)}, u32[]{:S(2)}, u32[]{:S(2)}) collective-permute-start(bf16[688,128]{1,0:T(8,128)(2,1)S(1)} %get-tuple-element.48), channel_id=1, source_target_pairs={{0,1},{1,0},{2,3},{3,2},{4,5},{5,4},{6,7},{7,6},{8,9},{9,8},{10,11... | collective-permute-start | bytes 528392 | tf_op jit(solution)/shard_map/ppermute | solution.py:533
  13.2 19.6 %collective-permute-start.1 = (bf16[3280,128]{1,0:T(8,128)(2,1)S(1)}, bf16[3280,128]{1,0:T(8,128)(2,1)S(1)}, u32[]{:S(2)}, u32[]{:S(2)}) collective-permute-start(bf16[3280,128]{1,0:T(8,128)(2,1)S(1)} %get-tuple-element.49), channel_id=1, source_target_pairs={{0,1},{1,0},{2,3},{3,2},{4,5},{5,4},{6,7},{7,6},{8,9},{9,8},{10,11... | collective-permute-start | bytes 2519048 | tf_op jit(solution)/shard_map/ppermute | solution.py:552
  13.5 9.4 %collective-permute-start.4 = (bf16[2,128,384]{2,1,0:T(8,128)(2,1)S(1)}, bf16[2,128,384]{2,1,0:T(8,128)(2,1)S(1)}, u32[]{:S(2)}, u32[]{:S(2)}) collective-permute-start(bf16[2,128,384]{2,1,0:T(8,128)(2,1)S(1)} %get-tuple-element.52), channel_id=1, source_target_pairs={{0,8},{2,6},{4,0},{6,14},{8,16},{10,2},{12,4},{14,22},{16,24},{18,... | collective-permute-start | bytes 589832 | tf_op jit(solution)/shard_map/ppermute | solution.py:496
  15.5 7.3 %collective-permute-start.5 = (bf16[2,128,384]{2,1,0:T(8,128)(2,1)S(1)}, bf16[2,128,384]{2,1,0:T(8,128)(2,1)S(1)}, u32[]{:S(2)}, u32[]{:S(2)}) collective-permute-start(bf16[2,128,384]{2,1,0:T(8,128)(2,1)S(1)} %get-tuple-element.53), channel_id=1, source_target_pairs={{0,4},{2,10},{4,12},{6,2},{8,0},{10,18},{12,20},{14,6},{16,8},{18,... | collective-permute-start | bytes 589832 | tf_op jit(solution)/shard_map/ppermute | solution.py:496
  15.9 9.0 %collective-permute-start.6 = (bf16[2,128,384]{2,1,0:T(8,128)(2,1)S(1)}, bf16[2,128,384]{2,1,0:T(8,128)(2,1)S(1)}, u32[]{:S(2)}, u32[]{:S(2)}) collective-permute-start(bf16[2,128,384]{2,1,0:T(8,128)(2,1)S(1)} %get-tuple-element.54), channel_id=1, source_target_pairs={{0,8},{2,6},{4,0},{6,14},{8,16},{10,2},{12,4},{14,22},{16,24},{18,... | collective-permute-start | bytes 589832 | tf_op jit(solution)/shard_map/ppermute | solution.py:496
  17.6 7.4 %collective-permute-start.7 = (bf16[2,128,384]{2,1,0:T(8,128)(2,1)S(1)}, bf16[2,128,384]{2,1,0:T(8,128)(2,1)S(1)}, u32[]{:S(2)}, u32[]{:S(2)}) collective-permute-start(bf16[2,128,384]{2,1,0:T(8,128)(2,1)S(1)} %get-tuple-element.55), channel_id=1, source_target_pairs={{0,4},{2,10},{4,12},{6,2},{8,0},{10,18},{12,20},{14,6},{16,8},{18,... | collective-permute-start | bytes 589832 | tf_op jit(solution)/shard_map/ppermute | solution.py:496
  22.8 5.7 %collective-permute-start.9 = (bf16[2,128,384]{2,1,0:T(8,128)(2,1)S(1)}, bf16[2,128,384]{2,1,0:T(8,128)(2,1)S(1)}, u32[]{:S(2)}, u32[]{:S(2)}) collective-permute-start(bf16[2,128,384]{2,1,0:T(8,128)(2,1)S(1)} %collective-permute-done.4.refs_2_), channel_id=1, source_target_pairs={{0,8},{2,6},{4,0},{6,14},{8,16},{10,2},{12,4},{14,22},{16,24},{18,... | collective-permute-start | bytes 589832 | tf_op jit(solution)/shard_map/ppermute | solution.py:496
  24.9 10.8 %collective-permute-start.14 = (bf16[2,128,384]{2,1,0:T(8,128)(2,1)S(1)}, bf16[2,128,384]{2,1,0:T(8,128)(2,1)S(1)}, u32[]{:S(2)}, u32[]{:S(2)}) collective-permute-start(bf16[2,128,384]{2,1,0:T(8,128)(2,1)S(1)} %collective-permute-done.6.refs_2_), channel_id=1, source_target_pairs={{0,8},{2,6},{4,0},{6,14},{8,16},{10,2},{12,4},{14,22},{16,24},{18,... | collective-permute-start | bytes 589832 | tf_op jit(solution)/shard_map/ppermute | solution.py:496
  27.0 9.4 %collective-permute-start.10 = (bf16[2,128,384]{2,1,0:T(8,128)(2,1)S(1)}, bf16[2,128,384]{2,1,0:T(8,128)(2,1)S(1)}, u32[]{:S(2)}, u32[]{:S(2)}) collective-permute-start(bf16[2,128,384]{2,1,0:T(8,128)(2,1)S(1)} %collective-permute-done.5.refs_3_), channel_id=1, source_target_pairs={{0,4},{2,10},{4,12},{6,2},{8,0},{10,18},{12,20},{14,6},{16,8},{18,... | collective-permute-start | bytes 589832 | tf_op jit(solution)/shard_map/ppermute | solution.py:496
  28.6 10.1 %collective-permute-start.11 = (bf16[2,128,384]{2,1,0:T(8,128)(2,1)S(1)}, bf16[2,128,384]{2,1,0:T(8,128)(2,1)S(1)}, u32[]{:S(2)}, u32[]{:S(2)}) collective-permute-start(bf16[2,128,384]{2,1,0:T(8,128)(2,1)S(1)} %collective-permute-done.9.refs_4_), channel_id=1, source_target_pairs={{0,8},{2,6},{4,0},{6,14},{8,16},{10,2},{12,4},{14,22},{16,24},{18,... | collective-permute-start | bytes 589832 | tf_op jit(solution)/shard_map/ppermute | solution.py:584
  33.6 2.8 %collective-permute-start.8 = (bf16[128,384]{1,0:T(8,128)(2,1)S(1)}, bf16[128,384]{1,0:T(8,128)(2,1)S(1)}, u32[]{:S(2)}, u32[]{:S(2)}) collective-permute-start(bf16[128,384]{1,0:T(8,128)(2,1)S(1)} %get-tuple-element.60.qo_ref), channel_id=1, source_target_pairs={{0,2},{2,0},{4,6},{6,4},{8,10},{10,8},{12,14},{14,12},{16,18},{18,... | collective-permute-start | bytes 294920 | tf_op jit(solution)/shard_map/ppermute | solution.py:594
  33.6 6.6 %collective-permute-start.15 = (bf16[2,128,384]{2,1,0:T(8,128)(2,1)S(1)}, bf16[2,128,384]{2,1,0:T(8,128)(2,1)S(1)}, u32[]{:S(2)}, u32[]{:S(2)}) collective-permute-start(bf16[2,128,384]{2,1,0:T(8,128)(2,1)S(1)} %collective-permute-done.7.refs_3_), channel_id=1, source_target_pairs={{0,4},{2,10},{4,12},{6,2},{8,0},{10,18},{12,20},{14,6},{16,8},{18,... | collective-permute-start | bytes 589832 | tf_op jit(solution)/shard_map/ppermute | solution.py:496
  35.8 5.7 %collective-permute-start.16 = (bf16[2,128,384]{2,1,0:T(8,128)(2,1)S(1)}, bf16[2,128,384]{2,1,0:T(8,128)(2,1)S(1)}, u32[]{:S(2)}, u32[]{:S(2)}) collective-permute-start(bf16[2,128,384]{2,1,0:T(8,128)(2,1)S(1)} %collective-permute-done.14.refs_4_), channel_id=1, source_target_pairs={{0,8},{2,6},{4,0},{6,14},{8,16},{10,2},{12,4},{14,22},{16,24},{18,... | collective-permute-start | bytes 589832 | tf_op jit(solution)/shard_map/ppermute | solution.py:604
  38.6 2.9 %collective-permute-start.13 = (bf16[128,384]{1,0:T(8,128)(2,1)S(1)}, bf16[128,384]{1,0:T(8,128)(2,1)S(1)}, u32[]{:S(2)}, u32[]{:S(2)}) collective-permute-start(bf16[128,384]{1,0:T(8,128)(2,1)S(1)} %get-tuple-element.74.qo_ref), channel_id=1, source_target_pairs={{0,2},{2,0},{4,6},{6,4},{8,10},{10,8},{12,14},{14,12},{16,18},{18,... | collective-permute-start | bytes 294920 | tf_op jit(solution)/shard_map/ppermute | solution.py:643
  39.1 4.9 %collective-permute-start.12 = (f32[128,512]{1,0:T(8,128)S(1)}, f32[128,512]{1,0:T(8,128)S(1)}, u32[]{:S(2)}, u32[]{:S(2)}) collective-permute-start(f32[128,512]{1,0:T(8,128)S(1)} %get-tuple-element.71), channel_id=1, source_target_pairs={{0,2},{2,0},{4,6},{6,4},{8,10},{10,8},{12,14},{14,12},{16,18},{18,... | collective-permute-start | bytes 786440 | tf_op jit(solution)/shard_map/ppermute | solution.py:652
  43.8 1.6 %collective-permute-start.17 = (f32[128,512]{1,0:T(8,128)S(1)}, f32[128,512]{1,0:T(8,128)S(1)}, u32[]{:S(2)}, u32[]{:S(2)}) collective-permute-start(f32[128,512]{1,0:T(8,128)S(1)} %get-tuple-element.80), channel_id=1, source_target_pairs={{0,2},{2,0},{4,6},{6,4},{8,10},{10,8},{12,14},{14,12},{16,18},{18,... | collective-permute-start | bytes 786440 | tf_op jit(solution)/shard_map/ppermute | solution.py:652
  44.1 5.7 %collective-permute-start.18 = (bf16[128,384]{1,0:T(8,128)(2,1)S(1)}, bf16[128,384]{1,0:T(8,128)(2,1)S(1)}, u32[]{:S(2)}, u32[]{:S(2)}) collective-permute-start(bf16[128,384]{1,0:T(8,128)(2,1)S(1)} %merge.2.first_ref), channel_id=1, source_target_pairs={{0,1},{1,0},{2,3},{3,2},{4,5},{5,4},{6,7},{7,6},{8,9},{9,8},{10,11... | collective-permute-start | bytes 294920 | tf_op jit(solution)/shard_map/ppermute | solution.py:660
  45.6 5.9 %collective-permute-start.19 = (bf16[128,384]{1,0:T(8,128)(2,1)S(1)}, bf16[128,384]{1,0:T(8,128)(2,1)S(1)}, u32[]{:S(2)}, u32[]{:S(2)}) collective-permute-start(bf16[128,384]{1,0:T(8,128)(2,1)S(1)} %merge.3.second_ref), channel_id=1, source_target_pairs={{0,1},{1,0},{2,3},{3,2},{4,5},{5,4},{6,7},{7,6},{8,9},{9,8},{10,11... | collective-permute-start | bytes 294920 | tf_op jit(solution)/shard_map/ppermute | solution.py:660

commit v16 on v15

--- a/solution.py
+++ b/solution.py
@@ -325,34 +325,49 @@
         == (lax.broadcasted_iota(jnp.int32, (2 * video, 2 * video), 1) < video)
     ).astype(F32)
     packed = jnp.zeros((2 * video, HEAD_DIM), F32)
+
+    def scores_of(head, group):
+        cells = slice(head * HEAD_DIM, (head + 1) * HEAD_DIM)
+        queries = jnp.concatenate([qo_ref[:, cells], qp_ref[:, cells]], axis=0)
+        return lax.dot_general(
+            queries, both(group, 0), (((1,), (1,)), ((), ())), preferred_element_type=F32
+        )
+
+    work = []
     for head in range(width // HEAD_DIM):
         cells = slice(head * HEAD_DIM, (head + 1) * HEAD_DIM)
         columns = slice((first + head) * HEAD_DIM, (first + head + 1) * HEAD_DIM)
-        queries = jnp.concatenate([qo_ref[:, cells], qp_ref[:, cells]], axis=0)
-        pair = [(fresh_ref, columns), (stale_ref, columns)]
-        weights = weigh(queries, both(pair, 0)) * same_patch
-        num = times(weights, both(pair, 1))
-        den = lanes(weights)
         blocks = [(ref, columns) for ref in refs[:count]] + [(ref, cells) for ref in refs[count:]]
         blocks.append((text_ref, columns))
+        work.append((head, [(fresh_ref, columns), (stale_ref, columns)], same_patch))
         odd = len(blocks) % 2
+        if odd:
+            work.append((head, blocks[:1], None))
         for start in range(odd, len(blocks), 2):
-            pair = blocks[start : start + 2]
-            weights = weigh(queries, both(pair, 0))
-            if start + 2 == len(blocks):
-                weights = weights * keep
-            num = num + times(weights, both(pair, 1))
-            den = den + lanes(weights)
-        if odd:
-            weights = weigh(queries, both(blocks[:1], 0))
-            num = num + times(weights, both(blocks[:1], 1))
-            den = den + weights
-        if finish:
-            own_ref[:, cells] = num[:video]
-            msg_ref[:, cells] = num[video:]
-        else:
-            num_ref[:, cells] = num
-        packed = jnp.where(lane == first + head, jnp.sum(den, axis=1, keepdims=True), packed)
+            last = start + 2 == len(blocks)
+            work.append((head, blocks[start : start + 2], keep if last else None))
+
+    upcoming = scores_of(*work[0][:2])
+    num = den = None
+    for index, (head, group, kept) in enumerate(work):
+        scores = upcoming
+        if index + 1 < len(work):
+            upcoming = scores_of(*work[index + 1][:2])
+        weights = jnp.exp2(scores * FACTOR)
+        if kept is not None:
+            weights = weights * kept
+        part, total = times(weights, both(group, 1)), lanes(weights)
+        num = part if num is None else num + part
+        den = total if den is None else den + total
+        if index + 1 == len(work) or work[index + 1][0] != head:
+            cells = slice(head * HEAD_DIM, (head + 1) * HEAD_DIM)
+            if finish:
+                own_ref[:, cells] = num[:video]
+                msg_ref[:, cells] = num[video:]
+            else:
+                num_ref[:, cells] = num
+            packed = jnp.where(lane == first + head, jnp.sum(den, axis=1, keepdims=True), packed)
+            num = den = None
     if finish:
         own_den_ref[...] = packed[:video]
         msg_ref[:, width:] = packed[video:]
@@ -591,7 +606,7 @@
         cost(1000 * top * group_columns, 8 * top * group_columns),
         own, received, received_more, stats, query_gain, key_gain,
     )
-    other_queries = [lax.ppermute(queries[0], "section", swap_core)]
+    other_queries = [lax.ppermute(half, "section", swap_core) for half in queries]
     (text_kv,) = plain_call(
         functools.partial(text_kernel, features * 2),
         [((2, text, width), BF16)],
@@ -639,8 +654,6 @@
         if finish:
             *outs, new_cache = outs
         else:
-            later = lax.optimization_barrier((queries[1], outs[0]))[0]
-            other_queries.append(lax.ppermute(later, "section", swap_core))
             outs = plain_call(
                 functools.partial(last_kernel, first),
                 [(out.shape, out.dtype) for out in finished],

time: 52.7 us -> 50.7 us (0.962)
  waiting for transfers between devices: 8.3 us -> 5.57 us
  starting transfers between devices: 20 us -> 21.6 us
  Pallas kernels: 23.3 us -> 22.5 us
    ppermute x2, starting transfers between devices: 1.38 us -> 3.18 us  [per_device(): other_attended.append(lax.ppermute(attended[-1], 'head', swap_head))]
    ppermute x10, starting transfers between devices: 13.4 us -> 12.1 us  [ring_step(): lax.ppermute(block, 'section', way)]
    ppermute x1, starting transfers between devices: 0.56 us -> 1.63 us  [per_device(): far.append(lax.ppermute(last, 'section', ways[0]))]
    ppermute x2, waiting for transfers between devices: 1.66 us -> 0.71 us  [per_device(): other_attended.append(lax.ppermute(attended[-1], 'head', swap_head))]
    ppermute x1, waiting for transfers between devices: 1.26 us -> 0.32 us  [per_device(): far.append(lax.ppermute(last, 'section', ways[0]))]
    pallas_call x2, Pallas kernels: 4.56 us -> 3.71 us  [per_device(): pl.pallas_call(functools.partial(attend_kernel, first, len(whole)), in_sp...]
    ppermute x2, waiting for transfers between devices: 0.01 us -> 0.79 us  [per_device(): lax.ppermute(half, 'section', swap_core)]
    ppermute x2, waiting for transfers between devices: 0.78 us -> 0.01 us  [per_device(): num_received = lax.ppermute(num_message, 'section', swap_core)]
  transfers between devices with their start and end apart: 20 -> 20, of which waited for: 8 -> 6; matrix products, arithmetic and copies ran while one was open for 0% -> 0% of each run, Pallas kernels for 42% -> 42%
where the time goes in v16:
time: 50.7 us; the launch traced here: 50.5 us
  Pallas kernels  22.5 us (44%)
  starting transfers between devices  21.6 us (43%)
  waiting for transfers between devices  5.57 us (11%)
  between operations  0.78 us (2%)
    ppermute x10, starting transfers between devices, ring_step(): lax.ppermute(block, 'section', way)  12.1 us
    pallas_call x1, Pallas kernels, per_device(): pl.pallas_call(own_kernel, in_specs=[smem, vmem, vmem, hbm] + [hbm] * len...  4.9 us
    pallas_call x1, Pallas kernels, per_device(): pl.pallas_call(functools.partial(send_more_kernel, video), in_specs=[smem...  4.01 us
    pallas_call x2, Pallas kernels, per_device(): pl.pallas_call(functools.partial(attend_kernel, first, len(whole)), in_sp...  3.71 us
    pallas_call x1, Pallas kernels, per_device(): pl.pallas_call(send_kernel, in_specs=[smem] + [hbm] * 5, out_specs=[vmem]...  3.4 us
    ppermute x2, starting transfers between devices, per_device(): other_attended.append(lax.ppermute(attended[-1], 'head', swap_head))  3.18 us
    pallas_call x1, Pallas kernels, per_device(): pl.pallas_call(part_kernel, in_specs=[smem, hbm, vmem, vmem], out_specs=[...  2.94 us
    pallas_call x7, Pallas kernels, plain_call(): pl.pallas_call(kernel, in_specs=[pl.BlockSpec(memory_space=pltpu.VMEM)] *...  2.43 us
  transfers between devices with their start and end apart: 20, of which 6 were waited for; matrix products, arithmetic and copies ran while one was open for 0% of the time, Pallas kernels for 42%

profile of v16, /device:TPU:0, one launch (start us, length us, event | category | flops | bytes accessed | tf_op | source)
XLA Modules:
  0.0 50.5 jit_solution(11764476895141118381)
XLA Ops:
  0.6 3.1 %collective-permute-start.2 = (bf16[2,128,768]{2,1,0:T(8,128)(2,1)}, bf16[2,128,768]{2,1,0:T(8,128)(2,1)S(1)}, u32[]{:S(2)}, u32[]{:S(2)}) collective-permute-start(bf16[2,128,768]{2,1,0:T(8,128)(2,1)} %refs_5_.1), channel_id=1, source_target_pairs={{0,8},{2,6},{4,0},{6,14},{8,16},{10,2},{12,4},{14,22},{16,24},{18,... | collective-permute-start | bytes 1179656 | tf_op jit(solution)/shard_map/ppermute | solution.py:511
  3.8 3.4 %project_send.1 = (bf16[272,1536]{1,0:T(8,128)(2,1)S(1)}, bf16[688,128]{1,0:T(8,128)(2,1)S(1)}, f32[272,128]{1,0:T(8,128)S(1)}, bf16[1536,768]{1,0:T(8,128)(2,1)S(1)}) custom-call(s32[2]{0:T(128)S(1)} %pad_add_fusion.place_ref, bf16[128,1536]{1,0:T(8,128)(2,1)} %refs_4_.1, bf16[256,1536]{1,0:T(8,128)(2,1)} %t_ref.1, f32[1536]{0:T(1024)} %scale_ref.1, ...), custom_call_target="tpu_custom_call" | custom-call | flops 3080296960 | bytes 2831155 | tf_op jit(solution)/shard_map/project_send/pallas_call | solution.py:526
  7.2 2.0 %collective-permute-start = (bf16[688,128]{1,0:T(8,128)(2,1)S(1)}, bf16[688,128]{1,0:T(8,128)(2,1)S(1)}, u32[]{:S(2)}, u32[]{:S(2)}) collective-permute-start(bf16[688,128]{1,0:T(8,128)(2,1)S(1)} %get-tuple-element.47), channel_id=1, source_target_pairs={{0,1},{1,0},{2,3},{3,2},{4,5},{5,4},{6,7},{7,6},{8,9},{9,8},{10,11... | collective-permute-start | bytes 528392 | tf_op jit(solution)/shard_map/ppermute | solution.py:548
  9.2 4.0 %project_send_more.1 = (bf16[3280,128]{1,0:T(8,128)(2,1)S(1)}, bf16[1536,768]{1,0:T(8,128)(2,1)S(1)}) custom-call(s32[2]{0:T(128)S(1)} %pad_add_fusion.place_ref, bf16[272,1536]{1,0:T(8,128)(2,1)S(1)} %get-tuple-element.43.a_ref, bf16[1536,768]{1,0:T(8,128)(2,1)S(1)} %get-tuple-element.44.ahead_ref, bf16[1536,4608]{1,0:T(8,128)(2,1)} %w_ref.5), custom_call_target="tpu_custom_call" | custom-call | flops 4620445184 | bytes 4246732 | tf_op jit(solution)/shard_map/project_send_more/pallas_call | solution.py:550
  13.5 2.1 %collective-permute-start.4 = (bf16[2,128,384]{2,1,0:T(8,128)(2,1)S(1)}, bf16[2,128,384]{2,1,0:T(8,128)(2,1)S(1)}, u32[]{:S(2)}, u32[]{:S(2)}) collective-permute-start(bf16[2,128,384]{2,1,0:T(8,128)(2,1)S(1)} %get-tuple-element.51), channel_id=1, source_target_pairs={{0,8},{2,6},{4,0},{6,14},{8,16},{10,2},{12,4},{14,22},{16,24},{18,... | collective-permute-start | bytes 589832 | tf_op jit(solution)/shard_map/ppermute | solution.py:511
  15.9 1.7 %collective-permute-start.6 = (bf16[2,128,384]{2,1,0:T(8,128)(2,1)S(1)}, bf16[2,128,384]{2,1,0:T(8,128)(2,1)S(1)}, u32[]{:S(2)}, u32[]{:S(2)}) collective-permute-start(bf16[2,128,384]{2,1,0:T(8,128)(2,1)S(1)} %get-tuple-element.53), channel_id=1, source_target_pairs={{0,8},{2,6},{4,0},{6,14},{8,16},{10,2},{12,4},{14,22},{16,24},{18,... | collective-permute-start | bytes 589832 | tf_op jit(solution)/shard_map/ppermute | solution.py:511
  17.9 4.9 %project_own.1 = (f32[144,2304]{1,0:T(8,128)S(1)}, f32[128,1536]{1,0:T(8,128)S(1)}, f32[128]{0:T(128)S(1)}, f32[128]{0:T(128)S(1)}, s32[256]{0:T(256)S(1)}, /*in...) custom-call(s32[2]{0:T(128)S(1)} %pad_add_fusion.place_ref, ...), custom_call_target="tpu_custom_call" | custom-call | flops 7700742144 | bytes 7077888 | tf_op jit(solution)/shard_map/project_own/pallas_call | solution.py:576
  22.8 1.7 %collective-permute-start.9 = (bf16[2,128,384]{2,1,0:T(8,128)(2,1)S(1)}, bf16[2,128,384]{2,1,0:T(8,128)(2,1)S(1)}, u32[]{:S(2)}, u32[]{:S(2)}) collective-permute-start(bf16[2,128,384]{2,1,0:T(8,128)(2,1)S(1)} %collective-permute-done.4.refs_2_), channel_id=1, source_target_pairs={{0,8},{2,6},{4,0},{6,14},{8,16},{10,2},{12,4},{14,22},{16,24},{18,... | collective-permute-start | bytes 589832 | tf_op jit(solution)/shard_map/ppermute | solution.py:511
  24.9 2.0 %collective-permute-start.14 = (bf16[2,128,384]{2,1,0:T(8,128)(2,1)S(1)}, bf16[2,128,384]{2,1,0:T(8,128)(2,1)S(1)}, u32[]{:S(2)}, u32[]{:S(2)}) collective-permute-start(bf16[2,128,384]{2,1,0:T(8,128)(2,1)S(1)} %collective-permute-done.6.refs_2_), channel_id=1, source_target_pairs={{0,8},{2,6},{4,0},{6,14},{8,16},{10,2},{12,4},{14,22},{16,24},{18,... | collective-permute-start | bytes 589832 | tf_op jit(solution)/shard_map/ppermute | solution.py:511
  27.5 1.1 %collective-permute-done.9.refs_4_ = bf16[2,128,384]{2,1,0:T(8,128)(2,1)S(1)} collective-permute-done((bf16[2,128,384]{2,1,0:T(8,128)(2,1)S(1)}, bf16[2,128,384]{2,1,0:T(8,128)(2,1)S(1)}, u32[]{:S(2)}, u32[]{:S(2)}) %collective-permute-start.9) | collective-permute-done | bytes 196640 | tf_op jit(solution)/shard_map/ppermute | solution.py:511
  28.6 1.7 %collective-permute-start.11 = (bf16[2,128,384]{2,1,0:T(8,128)(2,1)S(1)}, bf16[2,128,384]{2,1,0:T(8,128)(2,1)S(1)}, u32[]{:S(2)}, u32[]{:S(2)}) collective-permute-start(bf16[2,128,384]{2,1,0:T(8,128)(2,1)S(1)} %collective-permute-done.9.refs_4_), channel_id=1, source_target_pairs={{0,8},{2,6},{4,0},{6,14},{8,16},{10,2},{12,4},{14,22},{16,24},{18,... | collective-permute-start | bytes 589832 | tf_op jit(solution)/shard_map/ppermute | solution.py:599
  30.6 2.3 %collective-permute-done.1.more_ref = bf16[3280,128]{1,0:T(8,128)(2,1)S(1)} collective-permute-done((bf16[3280,128]{1,0:T(8,128)(2,1)S(1)}, bf16[3280,128]{1,0:T(8,128)(2,1)S(1)}, u32[]{:S(2)}, u32[]{:S(2)}) %collective-permute-start.1) | collective-permute-done | bytes 839712 | tf_op jit(solution)/shard_map/ppermute | solution.py:567
  32.9 0.5 %norm_text.1.text_ref = bf16[2,128,768]{2,1,0:T(8,128)(2,1)S(1)} custom-call(f32[128,1536]{1,0:T(8,128)S(1)} %get-tuple-element.62.own_ref, bf16[688,128]{1,0:T(8,128)(2,1)S(1)} %collective-permute-done.first_ref, bf16[3280,128]{1,0:T(8,128)(2,1)S(1)} %collective-permute-done.1.more_ref, f32[272,128]{1,0:T(8,128)S(1)} %get-tuple-element.56.stat_ref, ...), custom_call_target="tpu_custom_call" | custom-call | flops 294912 | bytes 294912 | tf_op jit(solution)/shard_map/norm_text/pallas_call | solution.py:466
  33.4 0.7 %norm_video.1 = (bf16[128,384]{1,0:T(8,128)(2,1)S(1)}, bf16[128,384]{1,0:T(8,128)(2,1)S(1)}, bf16[2,128,768]{2,1,0:T(8,128)(2,1)S(1)}) custom-call(f32[144,2304]{1,0:T(8,128)S(1)} %get-tuple-element.46.own_ref.top_ref, bf16[688,128]{1,0:T(8,128)(2,1)S(1)} %collective-permute-done.first_ref, bf16[3280,128]{1,0:T(8,128)(2,1)S(1)} %collective-permute-done.1.more_ref, ...), custom_call_target="tpu_custom_call" | custom-call | flops 331776000 | bytes 2654208 | tf_op jit(solution)/shard_map/norm_video/pallas_call | solution.py:466
  34.1 1.6 %collective-permute-start.16 = (bf16[2,128,384]{2,1,0:T(8,128)(2,1)S(1)}, bf16[2,128,384]{2,1,0:T(8,128)(2,1)S(1)}, u32[]{:S(2)}, u32[]{:S(2)}) collective-permute-start(bf16[2,128,384]{2,1,0:T(8,128)(2,1)S(1)} %collective-permute-done.14.refs_4_), channel_id=1, source_target_pairs={{0,8},{2,6},{4,0},{6,14},{8,16},{10,2},{12,4},{14,22},{16,24},{18,... | collective-permute-start | bytes 589832 | tf_op jit(solution)/shard_map/ppermute | solution.py:619
  35.7 0.5 %collective-permute-start.13 = (bf16[128,384]{1,0:T(8,128)(2,1)S(1)}, bf16[128,384]{1,0:T(8,128)(2,1)S(1)}, u32[]{:S(2)}, u32[]{:S(2)}) collective-permute-start(bf16[128,384]{1,0:T(8,128)(2,1)S(1)} %get-tuple-element.72.qo_ref), channel_id=1, source_target_pairs={{0,2},{2,0},{4,6},{6,4},{8,10},{10,8},{12,14},{14,12},{16,18},{18,... | collective-permute-start | bytes 294920 | tf_op jit(solution)/shard_map/ppermute | solution.py:609
  36.3 0.8 %collective-permute-done.8.qp_ref = bf16[128,384]{1,0:T(8,128)(2,1)S(1)} collective-permute-done((bf16[128,384]{1,0:T(8,128)(2,1)S(1)}, bf16[128,384]{1,0:T(8,128)(2,1)S(1)}, u32[]{:S(2)}, u32[]{:S(2)}) %collective-permute-start.8) | collective-permute-done | bytes 98336 | tf_op jit(solution)/shard_map/ppermute | solution.py:609
  37.0 1.7 %attend.2 = (f32[256,384]{1,0:T(8,128)S(1)}, f32[256,128]{1,0:T(8,128)S(1)}) custom-call(s32[2]{0:T(128)S(1)} %pad_add_fusion.place_ref, bf16[128,384]{1,0:T(8,128)(2,1)S(1)} %get-tuple-element.59.qo_ref, bf16[128,384]{1,0:T(8,128)(2,1)S(1)} %collective-permute-done.8.qp_ref, bf16[2,128,768]{2,1,0:T(8,128)(2,1)S(1)} %get-tuple-element.60.fresh_ref, ...), custom_call_target="tpu_custom_call" | custom-call | flops 163840 | bytes 983040 | tf_op jit(solution)/shard_map/attend/pallas_call | solution.py:641
  39.8 2.0 %attend.3 = (f32[128,384]{1,0:T(8,128)S(1)}, f32[128,128]{1,0:T(8,128)S(1)}, f32[128,512]{1,0:T(8,128)S(1)}, bf16[2,128,768]{2,1,0:T(8,128)(2,1)}) custom-call(s32[2]{0:T(128)S(1)} %pad_add_fusion.place_ref, bf16[128,384]{1,0:T(8,128)(2,1)S(1)} %get-tuple-element.72.qo_ref, bf16[128,384]{1,0:T(8,128)(2,1)S(1)} %collective-permute-done.13.qp_ref, ...), custom_call_target="tpu_custom_call" | custom-call | flops 163840 | bytes 983040 | tf_op jit(solution)/shard_map/attend/pallas_call | solution.py:641
  42.1 1.8 %collective-permute-start.18 = (bf16[128,384]{1,0:T(8,128)(2,1)S(1)}, bf16[128,384]{1,0:T(8,128)(2,1)S(1)}, u32[]{:S(2)}, u32[]{:S(2)}) collective-permute-start(bf16[128,384]{1,0:T(8,128)(2,1)S(1)} %merge.2.first_ref), channel_id=1, source_target_pairs={{0,1},{1,0},{2,3},{3,2},{4,5},{5,4},{6,7},{7,6},{8,9},{9,8},{10,11... | collective-permute-start | bytes 294920 | tf_op jit(solution)/shard_map/ppermute | solution.py:673
  44.0 1.4 %collective-permute-start.19 = (bf16[128,384]{1,0:T(8,128)(2,1)S(1)}, bf16[128,384]{1,0:T(8,128)(2,1)S(1)}, u32[]{:S(2)}, u32[]{:S(2)}) collective-permute-start(bf16[128,384]{1,0:T(8,128)(2,1)S(1)} %merge.3.second_ref), channel_id=1, source_target_pairs={{0,1},{1,0},{2,3},{3,2},{4,5},{5,4},{6,7},{7,6},{8,9},{9,8},{10,11... | collective-permute-start | bytes 294920 | tf_op jit(solution)/shard_map/ppermute | solution.py:673
  45.4 2.9 %part_out.1 = (f32[128,1536]{1,0:T(8,128)S(1)}, bf16[768,1536]{1,0:T(8,128)(2,1)S(1)}) custom-call(s32[2]{0:T(128)S(1)} %pad_add_fusion.place_ref, bf16[1536,1536]{1,0:T(8,128)(2,1)} %weight_ref.1, bf16[128,384]{1,0:T(8,128)(2,1)S(1)} %merge.2.first_ref, bf16[128,384]{1,0:T(8,128)(2,1)S(1)} %merge.3.second_ref), custom_call_target="tpu_custom_call" | custom-call | flops 603979776 | bytes 2359296 | tf_op jit(solution)/shard_map/part_out/pallas_call | solution.py:676
  48.7 0.7 %collective-permute-done.19.att_ref = bf16[128,384]{1,0:T(8,128)(2,1)S(1)} collective-permute-done((bf16[128,384]{1,0:T(8,128)(2,1)S(1)}, bf16[128,384]{1,0:T(8,128)(2,1)S(1)}, u32[]{:S(2)}, u32[]{:S(2)}) %collective-permute-start.19) | collective-permute-done | bytes 98336 | tf_op jit(solution)/shard_map/ppermute | solution.py:673
  49.5 1.1 %final_out.1 = bf16[128,1536]{1,0:T(8,128)(2,1)} custom-call(f32[128,1536]{1,0:T(8,128)S(1)} %more_out.1.part_ref, bf16[128,384]{1,0:T(8,128)(2,1)S(1)} %collective-permute-done.19.att_ref, bf16[768,1536]{1,0:T(8,128)(2,1)S(1)} %get-tuple-element.80.w_ref, bf16[128,1536]{1,0:T(8,128)(2,1)S(1)} %get-tuple-element.81.hidden_ref, ...), custom_call_target="tpu_custom_call" | custom-call | flops 603979776 | bytes 2359296 | tf_op jit(solution)/shard_map/final_out/pallas_call | solution.py:696
  (31 shorter events, 4.0 us)
Async XLA Ops:
  0.6 12.8 %collective-permute-start.2 = (bf16[2,128,768]{2,1,0:T(8,128)(2,1)}, bf16[2,128,768]{2,1,0:T(8,128)(2,1)S(1)}, u32[]{:S(2)}, u32[]{:S(2)}) collective-permute-start(bf16[2,128,768]{2,1,0:T(8,128)(2,1)} %refs_5_.1), channel_id=1, source_target_pairs={{0,8},{2,6},{4,0},{6,14},{8,16},{10,2},{12,4},{14,22},{16,24},{18,... | collective-permute-start | bytes 1179656 | tf_op jit(solution)/shard_map/ppermute | solution.py:511
  3.7 9.7 %collective-permute-start.3 = (bf16[2,128,768]{2,1,0:T(8,128)(2,1)}, bf16[2,128,768]{2,1,0:T(8,128)(2,1)S(1)}, u32[]{:S(2)}, u32[]{:S(2)}) collective-permute-start(bf16[2,128,768]{2,1,0:T(8,128)(2,1)} %refs_5_.1), channel_id=1, source_target_pairs={{0,4},{2,10},{4,12},{6,2},{8,0},{10,18},{12,20},{14,6},{16,8},{18,... | collective-permute-start | bytes 1179656 | tf_op jit(solution)/shard_map/ppermute | solution.py:511
  7.2 6.2 %collective-permute-start = (bf16[688,128]{1,0:T(8,128)(2,1)S(1)}, bf16[688,128]{1,0:T(8,128)(2,1)S(1)}, u32[]{:S(2)}, u32[]{:S(2)}) collective-permute-start(bf16[688,128]{1,0:T(8,128)(2,1)S(1)} %get-tuple-element.47), channel_id=1, source_target_pairs={{0,1},{1,0},{2,3},{3,2},{4,5},{5,4},{6,7},{7,6},{8,9},{9,8},{10,11... | collective-permute-start | bytes 528392 | tf_op jit(solution)/shard_map/ppermute | solution.py:548
  13.2 19.6 %collective-permute-start.1 = (bf16[3280,128]{1,0:T(8,128)(2,1)S(1)}, bf16[3280,128]{1,0:T(8,128)(2,1)S(1)}, u32[]{:S(2)}, u32[]{:S(2)}) collective-permute-start(bf16[3280,128]{1,0:T(8,128)(2,1)S(1)} %get-tuple-element.48), channel_id=1, source_target_pairs={{0,1},{1,0},{2,3},{3,2},{4,5},{5,4},{6,7},{7,6},{8,9},{9,8},{10,11... | collective-permute-start | bytes 2519048 | tf_op jit(solution)/shard_map/ppermute | solution.py:567
  13.5 9.4 %collective-permute-start.4 = (bf16[2,128,384]{2,1,0:T(8,128)(2,1)S(1)}, bf16[2,128,384]{2,1,0:T(8,128)(2,1)S(1)}, u32[]{:S(2)}, u32[]{:S(2)}) collective-permute-start(bf16[2,128,384]{2,1,0:T(8,128)(2,1)S(1)} %get-tuple-element.51), channel_id=1, source_target_pairs={{0,8},{2,6},{4,0},{6,14},{8,16},{10,2},{12,4},{14,22},{16,24},{18,... | collective-permute-start | bytes 589832 | tf_op jit(solution)/shard_map/ppermute | solution.py:511
  15.5 7.3 %collective-permute-start.5 = (bf16[2,128,384]{2,1,0:T(8,128)(2,1)S(1)}, bf16[2,128,384]{2,1,0:T(8,128)(2,1)S(1)}, u32[]{:S(2)}, u32[]{:S(2)}) collective-permute-start(bf16[2,128,384]{2,1,0:T(8,128)(2,1)S(1)} %get-tuple-element.52), channel_id=1, source_target_pairs={{0,4},{2,10},{4,12},{6,2},{8,0},{10,18},{12,20},{14,6},{16,8},{18,... | collective-permute-start | bytes 589832 | tf_op jit(solution)/shard_map/ppermute | solution.py:511
  15.9 9.0 %collective-permute-start.6 = (bf16[2,128,384]{2,1,0:T(8,128)(2,1)S(1)}, bf16[2,128,384]{2,1,0:T(8,128)(2,1)S(1)}, u32[]{:S(2)}, u32[]{:S(2)}) collective-permute-start(bf16[2,128,384]{2,1,0:T(8,128)(2,1)S(1)} %get-tuple-element.53), channel_id=1, source_target_pairs={{0,8},{2,6},{4,0},{6,14},{8,16},{10,2},{12,4},{14,22},{16,24},{18,... | collective-permute-start | bytes 589832 | tf_op jit(solution)/shard_map/ppermute | solution.py:511
  17.6 7.4 %collective-permute-start.7 = (bf16[2,128,384]{2,1,0:T(8,128)(2,1)S(1)}, bf16[2,128,384]{2,1,0:T(8,128)(2,1)S(1)}, u32[]{:S(2)}, u32[]{:S(2)}) collective-permute-start(bf16[2,128,384]{2,1,0:T(8,128)(2,1)S(1)} %get-tuple-element.54), channel_id=1, source_target_pairs={{0,4},{2,10},{4,12},{6,2},{8,0},{10,18},{12,20},{14,6},{16,8},{18,... | collective-permute-start | bytes 589832 | tf_op jit(solution)/shard_map/ppermute | solution.py:511
  22.8 5.7 %collective-permute-start.9 = (bf16[2,128,384]{2,1,0:T(8,128)(2,1)S(1)}, bf16[2,128,384]{2,1,0:T(8,128)(2,1)S(1)}, u32[]{:S(2)}, u32[]{:S(2)}) collective-permute-start(bf16[2,128,384]{2,1,0:T(8,128)(2,1)S(1)} %collective-permute-done.4.refs_2_), channel_id=1, source_target_pairs={{0,8},{2,6},{4,0},{6,14},{8,16},{10,2},{12,4},{14,22},{16,24},{18,... | collective-permute-start | bytes 589832 | tf_op jit(solution)/shard_map/ppermute | solution.py:511
  24.9 9.2 %collective-permute-start.14 = (bf16[2,128,384]{2,1,0:T(8,128)(2,1)S(1)}, bf16[2,128,384]{2,1,0:T(8,128)(2,1)S(1)}, u32[]{:S(2)}, u32[]{:S(2)}) collective-permute-start(bf16[2,128,384]{2,1,0:T(8,128)(2,1)S(1)} %collective-permute-done.6.refs_2_), channel_id=1, source_target_pairs={{0,8},{2,6},{4,0},{6,14},{8,16},{10,2},{12,4},{14,22},{16,24},{18,... | collective-permute-start | bytes 589832 | tf_op jit(solution)/shard_map/ppermute | solution.py:511
  27.0 8.8 %collective-permute-start.10 = (bf16[2,128,384]{2,1,0:T(8,128)(2,1)S(1)}, bf16[2,128,384]{2,1,0:T(8,128)(2,1)S(1)}, u32[]{:S(2)}, u32[]{:S(2)}) collective-permute-start(bf16[2,128,384]{2,1,0:T(8,128)(2,1)S(1)} %collective-permute-done.5.refs_3_), channel_id=1, source_target_pairs={{0,4},{2,10},{4,12},{6,2},{8,0},{10,18},{12,20},{14,6},{16,8},{18,... | collective-permute-start | bytes 589832 | tf_op jit(solution)/shard_map/ppermute | solution.py:511
  28.6 10.2 %collective-permute-start.11 = (bf16[2,128,384]{2,1,0:T(8,128)(2,1)S(1)}, bf16[2,128,384]{2,1,0:T(8,128)(2,1)S(1)}, u32[]{:S(2)}, u32[]{:S(2)}) collective-permute-start(bf16[2,128,384]{2,1,0:T(8,128)(2,1)S(1)} %collective-permute-done.9.refs_4_), channel_id=1, source_target_pairs={{0,8},{2,6},{4,0},{6,14},{8,16},{10,2},{12,4},{14,22},{16,24},{18,... | collective-permute-start | bytes 589832 | tf_op jit(solution)/shard_map/ppermute | solution.py:599
  30.3 9.2 %collective-permute-start.15 = (bf16[2,128,384]{2,1,0:T(8,128)(2,1)S(1)}, bf16[2,128,384]{2,1,0:T(8,128)(2,1)S(1)}, u32[]{:S(2)}, u32[]{:S(2)}) collective-permute-start(bf16[2,128,384]{2,1,0:T(8,128)(2,1)S(1)} %collective-permute-done.7.refs_3_), channel_id=1, source_target_pairs={{0,4},{2,10},{4,12},{6,2},{8,0},{10,18},{12,20},{14,6},{16,8},{18,... | collective-permute-start | bytes 589832 | tf_op jit(solution)/shard_map/ppermute | solution.py:511
  34.1 5.7 %collective-permute-start.16 = (bf16[2,128,384]{2,1,0:T(8,128)(2,1)S(1)}, bf16[2,128,384]{2,1,0:T(8,128)(2,1)S(1)}, u32[]{:S(2)}, u32[]{:S(2)}) collective-permute-start(bf16[2,128,384]{2,1,0:T(8,128)(2,1)S(1)} %collective-permute-done.14.refs_4_), channel_id=1, source_target_pairs={{0,8},{2,6},{4,0},{6,14},{8,16},{10,2},{12,4},{14,22},{16,24},{18,... | collective-permute-start | bytes 589832 | tf_op jit(solution)/shard_map/ppermute | solution.py:619
  35.7 1.3 %collective-permute-start.8 = (bf16[128,384]{1,0:T(8,128)(2,1)S(1)}, bf16[128,384]{1,0:T(8,128)(2,1)S(1)}, u32[]{:S(2)}, u32[]{:S(2)}) collective-permute-start(bf16[128,384]{1,0:T(8,128)(2,1)S(1)} %get-tuple-element.59.qo_ref), channel_id=1, source_target_pairs={{0,2},{2,0},{4,6},{6,4},{8,10},{10,8},{12,14},{14,12},{16,18},{18,... | collective-permute-start | bytes 294920 | tf_op jit(solution)/shard_map/ppermute | solution.py:609
  35.7 3.8 %collective-permute-start.13 = (bf16[128,384]{1,0:T(8,128)(2,1)S(1)}, bf16[128,384]{1,0:T(8,128)(2,1)S(1)}, u32[]{:S(2)}, u32[]{:S(2)}) collective-permute-start(bf16[128,384]{1,0:T(8,128)(2,1)S(1)} %get-tuple-element.72.qo_ref), channel_id=1, source_target_pairs={{0,2},{2,0},{4,6},{6,4},{8,10},{10,8},{12,14},{14,12},{16,18},{18,... | collective-permute-start | bytes 294920 | tf_op jit(solution)/shard_map/ppermute | solution.py:609
  39.3 2.7 %collective-permute-start.12 = (f32[128,512]{1,0:T(8,128)S(1)}, f32[128,512]{1,0:T(8,128)S(1)}, u32[]{:S(2)}, u32[]{:S(2)}) collective-permute-start(f32[128,512]{1,0:T(8,128)S(1)} %get-tuple-element.70), channel_id=1, source_target_pairs={{0,2},{2,0},{4,6},{6,4},{8,10},{10,8},{12,14},{14,12},{16,18},{18,... | collective-permute-start | bytes 786440 | tf_op jit(solution)/shard_map/ppermute | solution.py:665
  41.8 2.1 %collective-permute-start.17 = (f32[128,512]{1,0:T(8,128)S(1)}, f32[128,512]{1,0:T(8,128)S(1)}, u32[]{:S(2)}, u32[]{:S(2)}) collective-permute-start(f32[128,512]{1,0:T(8,128)S(1)} %get-tuple-element.78), channel_id=1, source_target_pairs={{0,2},{2,0},{4,6},{6,4},{8,10},{10,8},{12,14},{14,12},{16,18},{18,... | collective-permute-start | bytes 786440 | tf_op jit(solution)/shard_map/ppermute | solution.py:665
  42.1 6.3 %collective-permute-start.18 = (bf16[128,384]{1,0:T(8,128)(2,1)S(1)}, bf16[128,384]{1,0:T(8,128)(2,1)S(1)}, u32[]{:S(2)}, u32[]{:S(2)}) collective-permute-start(bf16[128,384]{1,0:T(8,128)(2,1)S(1)} %merge.2.first_ref), channel_id=1, source_target_pairs={{0,1},{1,0},{2,3},{3,2},{4,5},{5,4},{6,7},{7,6},{8,9},{9,8},{10,11... | collective-permute-start | bytes 294920 | tf_op jit(solution)/shard_map/ppermute | solution.py:673
  44.0 5.4 %collective-permute-start.19 = (bf16[128,384]{1,0:T(8,128)(2,1)S(1)}, bf16[128,384]{1,0:T(8,128)(2,1)S(1)}, u32[]{:S(2)}, u32[]{:S(2)}) collective-permute-start(bf16[128,384]{1,0:T(8,128)(2,1)S(1)} %merge.3.second_ref), channel_id=1, source_target_pairs={{0,1},{1,0},{2,3},{3,2},{4,5},{5,4},{6,7},{7,6},{8,9},{9,8},{10,11... | collective-permute-start | bytes 294920 | tf_op jit(solution)/shard_map/ppermute | solution.py:673

commit v17 on v16

--- a/solution.py
+++ b/solution.py
@@ -307,13 +307,12 @@
 def attend_kernel(
     first, count, place_ref, qo_ref, qp_ref, fresh_ref, stale_ref, text_ref, mask_ref, *refs,
 ):
-    finish = len(refs[-1].shape) == 0
-    if finish:
-        *refs, own_ref, own_den_ref, msg_ref, cache_ref, sem = refs
+    copy_out = len(refs[-1].shape) == 0
+    if copy_out:
+        *refs, cache_ref, sem = refs
         cache_copy = pltpu.make_async_copy(fresh_ref, cache_ref, sem)
         cache_copy.start()
-    else:
-        *refs, num_ref, den_ref = refs
+    *refs, own_ref, own_den_ref, msg_ref = refs
     video, width = qo_ref.shape
     text = text_ref.shape[1]
     lane = lax.broadcasted_iota(jnp.int32, (2 * video, HEAD_DIM), 1)
@@ -361,36 +360,14 @@
         den = total if den is None else den + total
         if index + 1 == len(work) or work[index + 1][0] != head:
             cells = slice(head * HEAD_DIM, (head + 1) * HEAD_DIM)
-            if finish:
-                own_ref[:, cells] = num[:video]
-                msg_ref[:, cells] = num[video:]
-            else:
-                num_ref[:, cells] = num
+            own_ref[:, cells] = num[:video]
+            msg_ref[:, cells] = num[video:]
             packed = jnp.where(lane == first + head, jnp.sum(den, axis=1, keepdims=True), packed)
             num = den = None
-    if finish:
-        own_den_ref[...] = packed[:video]
-        msg_ref[:, width:] = packed[video:]
-        cache_copy.wait()
-    else:
-        den_ref[...] = packed
-
-
-def last_kernel(first, qo_ref, qp_ref, num_ref, den_ref, far_ref, own_ref, own_den_ref, msg_ref):
-    video, width = qo_ref.shape
-    lane = lax.broadcasted_iota(jnp.int32, (2 * video, HEAD_DIM), 1)
-    packed = den_ref[...]
-    for head in range(width // HEAD_DIM):
-        cells = slice(head * HEAD_DIM, (head + 1) * HEAD_DIM)
-        queries = jnp.concatenate([qo_ref[:, cells], qp_ref[:, cells]], axis=0)
-        weights = weigh(queries, far_ref[0, :, cells])
-        num = num_ref[:, cells] + times(weights, far_ref[1, :, cells])
-        own_ref[:, cells] = num[:video]
-        msg_ref[:, cells] = num[video:]
-        total = jnp.sum(lanes(weights), axis=1, keepdims=True)
-        packed = packed + jnp.where(lane == first + head, total, 0.0)
     own_den_ref[...] = packed[:video]
     msg_ref[:, width:] = packed[video:]
+    if copy_out:
+        cache_copy.wait()
 
 
 def merge_kernel(first, own_ref, den_ref, msg_ref, att_ref):
@@ -596,7 +573,7 @@
     for _ in range(half_way - 3):
         for chain in chains:
             chain.append(ring_step(lax.optimization_barrier((*chain[-1], own))[:2]))
-    far = [lax.ppermute(chains[0][-1][0], "section", ways[0])]
+    far = [lax.ppermute(chain[-1][0], "section", ways[0]) for chain in chains]
 
     received_more = lax.optimization_barrier((received_more, *chains[0][0], *chains[1][0]))[0]
     *queries, fresh = plain_call(
@@ -615,35 +592,26 @@
         own_text, received, received_more, stats, own, key_gain,
     )
 
-    last = lax.optimization_barrier((chains[1][-1][0], text_kv, queries[0]))[0]
-    far.append(lax.ppermute(last, "section", ways[0]))
     context = chips * video + video + text
-    finished = [
-        jax.ShapeDtypeStruct((video, width // 2), F32),
-        jax.ShapeDtypeStruct((video, HEAD_DIM), F32),
-        jax.ShapeDtypeStruct((video, width // 2 + HEAD_DIM), F32),
-    ]
     attended, other_attended = [], []
     for index, chain in enumerate(chains):
         first = index * heads // 2
-        halves = [block for step in chain for block in step]
-        finish = index == 1
+        halves = [block for step in chain for block in step] + [far[index]]
+        copy_out = index == 1
         own_queries = queries[index]
-        if finish:
-            halves.append(far[index])
+        if copy_out:
             own_queries = lax.optimization_barrier((own_queries, num_own))[0]
-            outs = finished + [jax.ShapeDtypeStruct(fresh.shape, BF16)]
-        else:
-            outs = [
-                jax.ShapeDtypeStruct((2 * video, width // 2), F32),
-                jax.ShapeDtypeStruct((2 * video, HEAD_DIM), F32),
-            ]
-        outs = pl.pallas_call(
+        num_own, den_own, num_message, *copied = pl.pallas_call(
             functools.partial(attend_kernel, first, len(whole)),
             in_specs=[smem] + [vmem] * (6 + len(whole) + len(halves)),
-            out_specs=[vmem] * (len(outs) - finish) + [hbm] * finish,
-            out_shape=outs,
-            scratch_shapes=[pltpu.SemaphoreType.DMA] * finish,
+            out_specs=[vmem] * 3 + [hbm] * copy_out,
+            out_shape=[
+                jax.ShapeDtypeStruct((video, width // 2), F32),
+                jax.ShapeDtypeStruct((video, HEAD_DIM), F32),
+                jax.ShapeDtypeStruct((video, width // 2 + HEAD_DIM), F32),
+            ]
+            + [jax.ShapeDtypeStruct(fresh.shape, BF16)] * copy_out,
+            scratch_shapes=[pltpu.SemaphoreType.DMA] * copy_out,
             compiler_params=params(24),
             cost_estimate=cost(video * context, context * width, video * heads),
             name="attend",
@@ -651,17 +619,6 @@
             place, own_queries, other_queries[index], fresh, stale, text_kv, text_mask,
             *whole, *halves,
         )
-        if finish:
-            *outs, new_cache = outs
-        else:
-            outs = plain_call(
-                functools.partial(last_kernel, first),
-                [(out.shape, out.dtype) for out in finished],
-                "attend_last",
-                cost(video * video, video * width),
-                own_queries, other_queries[index], *outs, far[index],
-            )
-        num_own, den_own, num_message = outs
         num_received = lax.ppermute(num_message, "section", swap_core)
         attended += plain_call(
             functools.partial(merge_kernel, first),
@@ -706,7 +663,7 @@
         cost_estimate=out_cost,
         name="final_out",
     )(part, other_attended[1], w_other, hidden, branch_gate)
-    return (mixed, new_cache)
+    return (mixed, copied[0])
 
 
 def solution(mesh):

time: 50.7 us -> 50.7 us (level)
  starting transfers between devices: 21.6 us -> 22.8 us
  waiting for transfers between devices: 5.57 us -> 4.6 us
    ppermute x1, waiting for transfers between devices: 2.27 us -> 0.01 us  [per_device(): received_more = lax.ppermute(message_more, 'head', swap_head)]
    ppermute x10, waiting for transfers between devices: 1.47 us -> 3.12 us  [ring_step(): lax.ppermute(block, 'section', way)]
    ppermute x2, starting transfers between devices: 3.33 us -> 4.18 us  [per_device(): far = [lax.ppermute(chain[-1][0], 'section', ways[0]) for chain in chains]]
    ppermute x2, waiting for transfers between devices: 0.79 us -> 0.26 us  [per_device(): lax.ppermute(half, 'section', swap_core)]
    pallas_call x7 -> x6, Pallas kernels: 2.43 us -> 1.94 us  [plain_call(): pl.pallas_call(kernel, in_specs=[pl.BlockSpec(memory_space=pltpu.VMEM)] *...]
where the time goes in v17:
time: 50.7 us; the launch traced here: 50.5 us
  starting transfers between devices  22.8 us (45%)
  Pallas kernels  22.2 us (44%)
  waiting for transfers between devices  4.6 us (9%)
  between operations  0.79 us (2%)
    ppermute x10, starting transfers between devices, ring_step(): lax.ppermute(block, 'section', way)  12.1 us
    pallas_call x1, Pallas kernels, per_device(): pl.pallas_call(own_kernel, in_specs=[smem, vmem, vmem, hbm] + [hbm] * len...  4.9 us
    ppermute x2, starting transfers between devices, per_device(): far = [lax.ppermute(chain[-1][0], 'section', ways[0]) for chain in chains]  4.18 us
    pallas_call x1, Pallas kernels, per_device(): pl.pallas_call(functools.partial(send_more_kernel, video), in_specs=[smem...  4.01 us
    pallas_call x2, Pallas kernels, per_device(): pl.pallas_call(functools.partial(attend_kernel, first, len(whole)), in_sp...  3.97 us
    ppermute x2, starting transfers between devices, per_device(): other_attended.append(lax.ppermute(attended[-1], 'head', swap_head))  3.51 us
    pallas_call x1, Pallas kernels, per_device(): pl.pallas_call(send_kernel, in_specs=[smem] + [hbm] * 5, out_specs=[vmem]...  3.4 us
    ppermute x10, waiting for transfers between devices, ring_step(): lax.ppermute(block, 'section', way)  3.12 us
  transfers between devices with their start and end apart: 20, of which 6 were waited for; matrix products, arithmetic and copies ran while one was open for 0% of the time, Pallas kernels for 42%

profile of v17, /device:TPU:0, one launch (start us, length us, event | category | flops | bytes accessed | tf_op | source)
XLA Modules:
  0.0 50.5 jit_solution(6386528796034350593)
XLA Ops:
  0.6 3.1 %collective-permute-start.2 = (bf16[2,128,768]{2,1,0:T(8,128)(2,1)}, bf16[2,128,768]{2,1,0:T(8,128)(2,1)S(1)}, u32[]{:S(2)}, u32[]{:S(2)}) collective-permute-start(bf16[2,128,768]{2,1,0:T(8,128)(2,1)} %refs_5_.1), channel_id=1, source_target_pairs={{0,8},{2,6},{4,0},{6,14},{8,16},{10,2},{12,4},{14,22},{16,24},{18,... | collective-permute-start | bytes 1179656 | tf_op jit(solution)/shard_map/ppermute | solution.py:488
  3.8 3.4 %project_send.1 = (bf16[272,1536]{1,0:T(8,128)(2,1)S(1)}, bf16[688,128]{1,0:T(8,128)(2,1)S(1)}, f32[272,128]{1,0:T(8,128)S(1)}, bf16[1536,768]{1,0:T(8,128)(2,1)S(1)}) custom-call(s32[2]{0:T(128)S(1)} %pad_add_fusion.place_ref, bf16[128,1536]{1,0:T(8,128)(2,1)} %refs_4_.1, bf16[256,1536]{1,0:T(8,128)(2,1)} %t_ref.1, f32[1536]{0:T(1024)} %scale_ref.1, ...), custom_call_target="tpu_custom_call" | custom-call | flops 3080296960 | bytes 2831155 | tf_op jit(solution)/shard_map/project_send/pallas_call | solution.py:503
  7.2 2.0 %collective-permute-start = (bf16[688,128]{1,0:T(8,128)(2,1)S(1)}, bf16[688,128]{1,0:T(8,128)(2,1)S(1)}, u32[]{:S(2)}, u32[]{:S(2)}) collective-permute-start(bf16[688,128]{1,0:T(8,128)(2,1)S(1)} %get-tuple-element.44), channel_id=1, source_target_pairs={{0,1},{1,0},{2,3},{3,2},{4,5},{5,4},{6,7},{7,6},{8,9},{9,8},{10,11... | collective-permute-start | bytes 528392 | tf_op jit(solution)/shard_map/ppermute | solution.py:525
  9.2 4.0 %project_send_more.1 = (bf16[3280,128]{1,0:T(8,128)(2,1)S(1)}, bf16[1536,768]{1,0:T(8,128)(2,1)S(1)}) custom-call(s32[2]{0:T(128)S(1)} %pad_add_fusion.place_ref, bf16[272,1536]{1,0:T(8,128)(2,1)S(1)} %get-tuple-element.40.a_ref, bf16[1536,768]{1,0:T(8,128)(2,1)S(1)} %get-tuple-element.41.ahead_ref, bf16[1536,4608]{1,0:T(8,128)(2,1)} %w_ref.5), custom_call_target="tpu_custom_call" | custom-call | flops 4620445184 | bytes 4246732 | tf_op jit(solution)/shard_map/project_send_more/pallas_call | solution.py:527
  13.5 2.1 %collective-permute-start.4 = (bf16[2,128,384]{2,1,0:T(8,128)(2,1)S(1)}, bf16[2,128,384]{2,1,0:T(8,128)(2,1)S(1)}, u32[]{:S(2)}, u32[]{:S(2)}) collective-permute-start(bf16[2,128,384]{2,1,0:T(8,128)(2,1)S(1)} %get-tuple-element.48), channel_id=1, source_target_pairs={{0,8},{2,6},{4,0},{6,14},{8,16},{10,2},{12,4},{14,22},{16,24},{18,... | collective-permute-start | bytes 589832 | tf_op jit(solution)/shard_map/ppermute | solution.py:488
  15.9 1.7 %collective-permute-start.6 = (bf16[2,128,384]{2,1,0:T(8,128)(2,1)S(1)}, bf16[2,128,384]{2,1,0:T(8,128)(2,1)S(1)}, u32[]{:S(2)}, u32[]{:S(2)}) collective-permute-start(bf16[2,128,384]{2,1,0:T(8,128)(2,1)S(1)} %get-tuple-element.50), channel_id=1, source_target_pairs={{0,8},{2,6},{4,0},{6,14},{8,16},{10,2},{12,4},{14,22},{16,24},{18,... | collective-permute-start | bytes 589832 | tf_op jit(solution)/shard_map/ppermute | solution.py:488
  17.9 4.9 %project_own.1 = (f32[144,2304]{1,0:T(8,128)S(1)}, f32[128,1536]{1,0:T(8,128)S(1)}, f32[128]{0:T(128)S(1)}, f32[128]{0:T(128)S(1)}, s32[256]{0:T(256)S(1)}, /*in...) custom-call(s32[2]{0:T(128)S(1)} %pad_add_fusion.place_ref, ...), custom_call_target="tpu_custom_call" | custom-call | flops 7700742144 | bytes 7077888 | tf_op jit(solution)/shard_map/project_own/pallas_call | solution.py:553
  22.8 1.7 %collective-permute-start.9 = (bf16[2,128,384]{2,1,0:T(8,128)(2,1)S(1)}, bf16[2,128,384]{2,1,0:T(8,128)(2,1)S(1)}, u32[]{:S(2)}, u32[]{:S(2)}) collective-permute-start(bf16[2,128,384]{2,1,0:T(8,128)(2,1)S(1)} %collective-permute-done.4.refs_2_), channel_id=1, source_target_pairs={{0,8},{2,6},{4,0},{6,14},{8,16},{10,2},{12,4},{14,22},{16,24},{18,... | collective-permute-start | bytes 589832 | tf_op jit(solution)/shard_map/ppermute | solution.py:488
  24.9 2.0 %collective-permute-start.14 = (bf16[2,128,384]{2,1,0:T(8,128)(2,1)S(1)}, bf16[2,128,384]{2,1,0:T(8,128)(2,1)S(1)}, u32[]{:S(2)}, u32[]{:S(2)}) collective-permute-start(bf16[2,128,384]{2,1,0:T(8,128)(2,1)S(1)} %collective-permute-done.6.refs_2_), channel_id=1, source_target_pairs={{0,8},{2,6},{4,0},{6,14},{8,16},{10,2},{12,4},{14,22},{16,24},{18,... | collective-permute-start | bytes 589832 | tf_op jit(solution)/shard_map/ppermute | solution.py:488
  27.0 0.5 collective-permute-start.10
  27.5 1.1 %collective-permute-done.9.refs_4_ = bf16[2,128,384]{2,1,0:T(8,128)(2,1)S(1)} collective-permute-done((bf16[2,128,384]{2,1,0:T(8,128)(2,1)S(1)}, bf16[2,128,384]{2,1,0:T(8,128)(2,1)S(1)}, u32[]{:S(2)}, u32[]{:S(2)}) %collective-permute-start.9) | collective-permute-done | bytes 196640 | tf_op jit(solution)/shard_map/ppermute | solution.py:488
  28.6 1.7 %collective-permute-start.11 = (bf16[2,128,384]{2,1,0:T(8,128)(2,1)S(1)}, bf16[2,128,384]{2,1,0:T(8,128)(2,1)S(1)}, u32[]{:S(2)}, u32[]{:S(2)}) collective-permute-start(bf16[2,128,384]{2,1,0:T(8,128)(2,1)S(1)} %collective-permute-done.9.refs_4_), channel_id=1, source_target_pairs={{0,8},{2,6},{4,0},{6,14},{8,16},{10,2},{12,4},{14,22},{16,24},{18,... | collective-permute-start | bytes 589832 | tf_op jit(solution)/shard_map/ppermute | solution.py:576
  30.6 1.7 %collective-permute-done.14.refs_4_ = bf16[2,128,384]{2,1,0:T(8,128)(2,1)S(1)} collective-permute-done((bf16[2,128,384]{2,1,0:T(8,128)(2,1)S(1)}, bf16[2,128,384]{2,1,0:T(8,128)(2,1)S(1)}, u32[]{:S(2)}, u32[]{:S(2)}) %collective-permute-start.14) | collective-permute-done | bytes 196640 | tf_op jit(solution)/shard_map/ppermute | solution.py:488
  32.2 2.5 %collective-permute-start.16 = (bf16[2,128,384]{2,1,0:T(8,128)(2,1)S(1)}, bf16[2,128,384]{2,1,0:T(8,128)(2,1)S(1)}, u32[]{:S(2)}, u32[]{:S(2)}) collective-permute-start(bf16[2,128,384]{2,1,0:T(8,128)(2,1)S(1)} %collective-permute-done.14.refs_4_), channel_id=1, source_target_pairs={{0,8},{2,6},{4,0},{6,14},{8,16},{10,2},{12,4},{14,22},{16,24},{18,... | collective-permute-start | bytes 589832 | tf_op jit(solution)/shard_map/ppermute | solution.py:576
  34.7 0.7 %norm_video.1 = (bf16[128,384]{1,0:T(8,128)(2,1)S(1)}, bf16[128,384]{1,0:T(8,128)(2,1)S(1)}, bf16[2,128,768]{2,1,0:T(8,128)(2,1)S(1)}) custom-call(f32[144,2304]{1,0:T(8,128)S(1)} %get-tuple-element.43.own_ref.top_ref, bf16[688,128]{1,0:T(8,128)(2,1)S(1)} %collective-permute-done.first_ref, bf16[3280,128]{1,0:T(8,128)(2,1)S(1)} %collective-permute-done.1.more_ref, ...), custom_call_target="tpu_custom_call" | custom-call | flops 331776000 | bytes 2654208 | tf_op jit(solution)/shard_map/norm_video/pallas_call | solution.py:443
  36.0 0.5 %norm_text.1.text_ref = bf16[2,128,768]{2,1,0:T(8,128)(2,1)S(1)} custom-call(f32[128,1536]{1,0:T(8,128)S(1)} %get-tuple-element.59.own_ref, bf16[688,128]{1,0:T(8,128)(2,1)S(1)} %collective-permute-done.first_ref, bf16[3280,128]{1,0:T(8,128)(2,1)S(1)} %collective-permute-done.1.more_ref, f32[272,128]{1,0:T(8,128)S(1)} %get-tuple-element.53.stat_ref, ...), custom_call_target="tpu_custom_call" | custom-call | flops 294912 | bytes 294912 | tf_op jit(solution)/shard_map/norm_text/pallas_call | solution.py:443
  36.8 2.0 %attend.2 = (f32[128,384]{1,0:T(8,128)S(1)}, f32[128,128]{1,0:T(8,128)S(1)}, f32[128,512]{1,0:T(8,128)S(1)}) custom-call(s32[2]{0:T(128)S(1)} %pad_add_fusion.place_ref, bf16[128,384]{1,0:T(8,128)(2,1)S(1)} %get-tuple-element.56.qo_ref, bf16[128,384]{1,0:T(8,128)(2,1)S(1)} %collective-permute-done.8.qp_ref, ...), custom_call_target="tpu_custom_call" | custom-call | flops 163840 | bytes 983040 | tf_op jit(solution)/shard_map/attend/pallas_call | solution.py:604
  39.0 0.5 %collective-permute-done.16.refs_6_ = bf16[2,128,384]{2,1,0:T(8,128)(2,1)S(1)} collective-permute-done((bf16[2,128,384]{2,1,0:T(8,128)(2,1)S(1)}, bf16[2,128,384]{2,1,0:T(8,128)(2,1)S(1)}, u32[]{:S(2)}, u32[]{:S(2)}) %collective-permute-start.16) | collective-permute-done | bytes 196640 | tf_op jit(solution)/shard_map/ppermute | solution.py:576
  39.5 2.0 %attend.3 = (f32[128,384]{1,0:T(8,128)S(1)}, f32[128,128]{1,0:T(8,128)S(1)}, f32[128,512]{1,0:T(8,128)S(1)}, bf16[2,128,768]{2,1,0:T(8,128)(2,1)}) custom-call(s32[2]{0:T(128)S(1)} %pad_add_fusion.place_ref, bf16[128,384]{1,0:T(8,128)(2,1)S(1)} %get-tuple-element.67.qo_ref, bf16[128,384]{1,0:T(8,128)(2,1)S(1)} %collective-permute-done.13.qp_ref, ...), custom_call_target="tpu_custom_call" | custom-call | flops 163840 | bytes 983040 | tf_op jit(solution)/shard_map/attend/pallas_call | solution.py:604
  41.7 2.1 %collective-permute-start.18 = (bf16[128,384]{1,0:T(8,128)(2,1)S(1)}, bf16[128,384]{1,0:T(8,128)(2,1)S(1)}, u32[]{:S(2)}, u32[]{:S(2)}) collective-permute-start(bf16[128,384]{1,0:T(8,128)(2,1)S(1)} %merge.2.first_ref), channel_id=1, source_target_pairs={{0,1},{1,0},{2,3},{3,2},{4,5},{5,4},{6,7},{7,6},{8,9},{9,8},{10,11... | collective-permute-start | bytes 294920 | tf_op jit(solution)/shard_map/ppermute | solution.py:630
  44.0 1.4 %collective-permute-start.19 = (bf16[128,384]{1,0:T(8,128)(2,1)S(1)}, bf16[128,384]{1,0:T(8,128)(2,1)S(1)}, u32[]{:S(2)}, u32[]{:S(2)}) collective-permute-start(bf16[128,384]{1,0:T(8,128)(2,1)S(1)} %merge.3.second_ref), channel_id=1, source_target_pairs={{0,1},{1,0},{2,3},{3,2},{4,5},{5,4},{6,7},{7,6},{8,9},{9,8},{10,11... | collective-permute-start | bytes 294920 | tf_op jit(solution)/shard_map/ppermute | solution.py:630
  45.4 2.9 %part_out.1 = (f32[128,1536]{1,0:T(8,128)S(1)}, bf16[768,1536]{1,0:T(8,128)(2,1)S(1)}) custom-call(s32[2]{0:T(128)S(1)} %pad_add_fusion.place_ref, bf16[1536,1536]{1,0:T(8,128)(2,1)} %weight_ref.1, bf16[128,384]{1,0:T(8,128)(2,1)S(1)} %merge.2.first_ref, bf16[128,384]{1,0:T(8,128)(2,1)S(1)} %merge.3.second_ref), custom_call_target="tpu_custom_call" | custom-call | flops 603979776 | bytes 2359296 | tf_op jit(solution)/shard_map/part_out/pallas_call | solution.py:633
  48.8 0.7 %collective-permute-done.19.att_ref = bf16[128,384]{1,0:T(8,128)(2,1)S(1)} collective-permute-done((bf16[128,384]{1,0:T(8,128)(2,1)S(1)}, bf16[128,384]{1,0:T(8,128)(2,1)S(1)}, u32[]{:S(2)}, u32[]{:S(2)}) %collective-permute-start.19) | collective-permute-done | bytes 98336 | tf_op jit(solution)/shard_map/ppermute | solution.py:630
  49.4 1.1 %final_out.1 = bf16[128,1536]{1,0:T(8,128)(2,1)} custom-call(f32[128,1536]{1,0:T(8,128)S(1)} %more_out.1.part_ref, bf16[128,384]{1,0:T(8,128)(2,1)S(1)} %collective-permute-done.19.att_ref, bf16[768,1536]{1,0:T(8,128)(2,1)S(1)} %get-tuple-element.74.w_ref, bf16[128,1536]{1,0:T(8,128)(2,1)S(1)} %get-tuple-element.75.hidden_ref, ...), custom_call_target="tpu_custom_call" | custom-call | flops 603979776 | bytes 2359296 | tf_op jit(solution)/shard_map/final_out/pallas_call | solution.py:653
  (30 shorter events, 3.5 us)
Async XLA Ops:
  0.6 12.8 %collective-permute-start.2 = (bf16[2,128,768]{2,1,0:T(8,128)(2,1)}, bf16[2,128,768]{2,1,0:T(8,128)(2,1)S(1)}, u32[]{:S(2)}, u32[]{:S(2)}) collective-permute-start(bf16[2,128,768]{2,1,0:T(8,128)(2,1)} %refs_5_.1), channel_id=1, source_target_pairs={{0,8},{2,6},{4,0},{6,14},{8,16},{10,2},{12,4},{14,22},{16,24},{18,... | collective-permute-start | bytes 1179656 | tf_op jit(solution)/shard_map/ppermute | solution.py:488
  3.7 9.7 %collective-permute-start.3 = (bf16[2,128,768]{2,1,0:T(8,128)(2,1)}, bf16[2,128,768]{2,1,0:T(8,128)(2,1)S(1)}, u32[]{:S(2)}, u32[]{:S(2)}) collective-permute-start(bf16[2,128,768]{2,1,0:T(8,128)(2,1)} %refs_5_.1), channel_id=1, source_target_pairs={{0,4},{2,10},{4,12},{6,2},{8,0},{10,18},{12,20},{14,6},{16,8},{18,... | collective-permute-start | bytes 1179656 | tf_op jit(solution)/shard_map/ppermute | solution.py:488
  7.2 6.2 %collective-permute-start = (bf16[688,128]{1,0:T(8,128)(2,1)S(1)}, bf16[688,128]{1,0:T(8,128)(2,1)S(1)}, u32[]{:S(2)}, u32[]{:S(2)}) collective-permute-start(bf16[688,128]{1,0:T(8,128)(2,1)S(1)} %get-tuple-element.44), channel_id=1, source_target_pairs={{0,1},{1,0},{2,3},{3,2},{4,5},{5,4},{6,7},{7,6},{8,9},{9,8},{10,11... | collective-permute-start | bytes 528392 | tf_op jit(solution)/shard_map/ppermute | solution.py:525
  13.2 21.5 %collective-permute-start.1 = (bf16[3280,128]{1,0:T(8,128)(2,1)S(1)}, bf16[3280,128]{1,0:T(8,128)(2,1)S(1)}, u32[]{:S(2)}, u32[]{:S(2)}) collective-permute-start(bf16[3280,128]{1,0:T(8,128)(2,1)S(1)} %get-tuple-element.45), channel_id=1, source_target_pairs={{0,1},{1,0},{2,3},{3,2},{4,5},{5,4},{6,7},{7,6},{8,9},{9,8},{10,11... | collective-permute-start | bytes 2519048 | tf_op jit(solution)/shard_map/ppermute | solution.py:544
  13.5 9.4 %collective-permute-start.4 = (bf16[2,128,384]{2,1,0:T(8,128)(2,1)S(1)}, bf16[2,128,384]{2,1,0:T(8,128)(2,1)S(1)}, u32[]{:S(2)}, u32[]{:S(2)}) collective-permute-start(bf16[2,128,384]{2,1,0:T(8,128)(2,1)S(1)} %get-tuple-element.48), channel_id=1, source_target_pairs={{0,8},{2,6},{4,0},{6,14},{8,16},{10,2},{12,4},{14,22},{16,24},{18,... | collective-permute-start | bytes 589832 | tf_op jit(solution)/shard_map/ppermute | solution.py:488
  15.5 7.3 %collective-permute-start.5 = (bf16[2,128,384]{2,1,0:T(8,128)(2,1)S(1)}, bf16[2,128,384]{2,1,0:T(8,128)(2,1)S(1)}, u32[]{:S(2)}, u32[]{:S(2)}) collective-permute-start(bf16[2,128,384]{2,1,0:T(8,128)(2,1)S(1)} %get-tuple-element.49), channel_id=1, source_target_pairs={{0,4},{2,10},{4,12},{6,2},{8,0},{10,18},{12,20},{14,6},{16,8},{18,... | collective-permute-start | bytes 589832 | tf_op jit(solution)/shard_map/ppermute | solution.py:488
  15.9 9.0 %collective-permute-start.6 = (bf16[2,128,384]{2,1,0:T(8,128)(2,1)S(1)}, bf16[2,128,384]{2,1,0:T(8,128)(2,1)S(1)}, u32[]{:S(2)}, u32[]{:S(2)}) collective-permute-start(bf16[2,128,384]{2,1,0:T(8,128)(2,1)S(1)} %get-tuple-element.50), channel_id=1, source_target_pairs={{0,8},{2,6},{4,0},{6,14},{8,16},{10,2},{12,4},{14,22},{16,24},{18,... | collective-permute-start | bytes 589832 | tf_op jit(solution)/shard_map/ppermute | solution.py:488
  17.6 7.4 %collective-permute-start.7 = (bf16[2,128,384]{2,1,0:T(8,128)(2,1)S(1)}, bf16[2,128,384]{2,1,0:T(8,128)(2,1)S(1)}, u32[]{:S(2)}, u32[]{:S(2)}) collective-permute-start(bf16[2,128,384]{2,1,0:T(8,128)(2,1)S(1)} %get-tuple-element.51), channel_id=1, source_target_pairs={{0,4},{2,10},{4,12},{6,2},{8,0},{10,18},{12,20},{14,6},{16,8},{18,... | collective-permute-start | bytes 589832 | tf_op jit(solution)/shard_map/ppermute | solution.py:488
  22.8 5.7 %collective-permute-start.9 = (bf16[2,128,384]{2,1,0:T(8,128)(2,1)S(1)}, bf16[2,128,384]{2,1,0:T(8,128)(2,1)S(1)}, u32[]{:S(2)}, u32[]{:S(2)}) collective-permute-start(bf16[2,128,384]{2,1,0:T(8,128)(2,1)S(1)} %collective-permute-done.4.refs_2_), channel_id=1, source_target_pairs={{0,8},{2,6},{4,0},{6,14},{8,16},{10,2},{12,4},{14,22},{16,24},{18,... | collective-permute-start | bytes 589832 | tf_op jit(solution)/shard_map/ppermute | solution.py:488
  24.9 7.3 %collective-permute-start.14 = (bf16[2,128,384]{2,1,0:T(8,128)(2,1)S(1)}, bf16[2,128,384]{2,1,0:T(8,128)(2,1)S(1)}, u32[]{:S(2)}, u32[]{:S(2)}) collective-permute-start(bf16[2,128,384]{2,1,0:T(8,128)(2,1)S(1)} %collective-permute-done.6.refs_2_), channel_id=1, source_target_pairs={{0,8},{2,6},{4,0},{6,14},{8,16},{10,2},{12,4},{14,22},{16,24},{18,... | collective-permute-start | bytes 589832 | tf_op jit(solution)/shard_map/ppermute | solution.py:488
  27.0 8.6 %collective-permute-start.10 = (bf16[2,128,384]{2,1,0:T(8,128)(2,1)S(1)}, bf16[2,128,384]{2,1,0:T(8,128)(2,1)S(1)}, u32[]{:S(2)}, u32[]{:S(2)}) collective-permute-start(bf16[2,128,384]{2,1,0:T(8,128)(2,1)S(1)} %collective-permute-done.5.refs_3_), channel_id=1, source_target_pairs={{0,4},{2,10},{4,12},{6,2},{8,0},{10,18},{12,20},{14,6},{16,8},{18,... | collective-permute-start | bytes 589832 | tf_op jit(solution)/shard_map/ppermute | solution.py:488
  28.6 8.2 %collective-permute-start.11 = (bf16[2,128,384]{2,1,0:T(8,128)(2,1)S(1)}, bf16[2,128,384]{2,1,0:T(8,128)(2,1)S(1)}, u32[]{:S(2)}, u32[]{:S(2)}) collective-permute-start(bf16[2,128,384]{2,1,0:T(8,128)(2,1)S(1)} %collective-permute-done.9.refs_4_), channel_id=1, source_target_pairs={{0,8},{2,6},{4,0},{6,14},{8,16},{10,2},{12,4},{14,22},{16,24},{18,... | collective-permute-start | bytes 589832 | tf_op jit(solution)/shard_map/ppermute | solution.py:576
  30.3 8.7 %collective-permute-start.15 = (bf16[2,128,384]{2,1,0:T(8,128)(2,1)S(1)}, bf16[2,128,384]{2,1,0:T(8,128)(2,1)S(1)}, u32[]{:S(2)}, u32[]{:S(2)}) collective-permute-start(bf16[2,128,384]{2,1,0:T(8,128)(2,1)S(1)} %collective-permute-done.7.refs_3_), channel_id=1, source_target_pairs={{0,4},{2,10},{4,12},{6,2},{8,0},{10,18},{12,20},{14,6},{16,8},{18,... | collective-permute-start | bytes 589832 | tf_op jit(solution)/shard_map/ppermute | solution.py:488
  32.2 7.3 %collective-permute-start.16 = (bf16[2,128,384]{2,1,0:T(8,128)(2,1)S(1)}, bf16[2,128,384]{2,1,0:T(8,128)(2,1)S(1)}, u32[]{:S(2)}, u32[]{:S(2)}) collective-permute-start(bf16[2,128,384]{2,1,0:T(8,128)(2,1)S(1)} %collective-permute-done.14.refs_4_), channel_id=1, source_target_pairs={{0,8},{2,6},{4,0},{6,14},{8,16},{10,2},{12,4},{14,22},{16,24},{18,... | collective-permute-start | bytes 589832 | tf_op jit(solution)/shard_map/ppermute | solution.py:576
  35.4 1.4 %collective-permute-start.8 = (bf16[128,384]{1,0:T(8,128)(2,1)S(1)}, bf16[128,384]{1,0:T(8,128)(2,1)S(1)}, u32[]{:S(2)}, u32[]{:S(2)}) collective-permute-start(bf16[128,384]{1,0:T(8,128)(2,1)S(1)} %get-tuple-element.56.qo_ref), channel_id=1, source_target_pairs={{0,2},{2,0},{4,6},{6,4},{8,10},{10,8},{12,14},{14,12},{16,18},{18,... | collective-permute-start | bytes 294920 | tf_op jit(solution)/shard_map/ppermute | solution.py:586
  35.5 3.5 %collective-permute-start.13 = (bf16[128,384]{1,0:T(8,128)(2,1)S(1)}, bf16[128,384]{1,0:T(8,128)(2,1)S(1)}, u32[]{:S(2)}, u32[]{:S(2)}) collective-permute-start(bf16[128,384]{1,0:T(8,128)(2,1)S(1)} %get-tuple-element.67.qo_ref), channel_id=1, source_target_pairs={{0,2},{2,0},{4,6},{6,4},{8,10},{10,8},{12,14},{14,12},{16,18},{18,... | collective-permute-start | bytes 294920 | tf_op jit(solution)/shard_map/ppermute | solution.py:586
  38.8 2.8 %collective-permute-start.12 = (f32[128,512]{1,0:T(8,128)S(1)}, f32[128,512]{1,0:T(8,128)S(1)}, u32[]{:S(2)}, u32[]{:S(2)}) collective-permute-start(f32[128,512]{1,0:T(8,128)S(1)} %get-tuple-element.65), channel_id=1, source_target_pairs={{0,2},{2,0},{4,6},{6,4},{8,10},{10,8},{12,14},{14,12},{16,18},{18,... | collective-permute-start | bytes 786440 | tf_op jit(solution)/shard_map/ppermute | solution.py:622
  41.5 2.4 %collective-permute-start.17 = (f32[128,512]{1,0:T(8,128)S(1)}, f32[128,512]{1,0:T(8,128)S(1)}, u32[]{:S(2)}, u32[]{:S(2)}) collective-permute-start(f32[128,512]{1,0:T(8,128)S(1)} %get-tuple-element.72), channel_id=1, source_target_pairs={{0,2},{2,0},{4,6},{6,4},{8,10},{10,8},{12,14},{14,12},{16,18},{18,... | collective-permute-start | bytes 786440 | tf_op jit(solution)/shard_map/ppermute | solution.py:622
  41.7 6.6 %collective-permute-start.18 = (bf16[128,384]{1,0:T(8,128)(2,1)S(1)}, bf16[128,384]{1,0:T(8,128)(2,1)S(1)}, u32[]{:S(2)}, u32[]{:S(2)}) collective-permute-start(bf16[128,384]{1,0:T(8,128)(2,1)S(1)} %merge.2.first_ref), channel_id=1, source_target_pairs={{0,1},{1,0},{2,3},{3,2},{4,5},{5,4},{6,7},{7,6},{8,9},{9,8},{10,11... | collective-permute-start | bytes 294920 | tf_op jit(solution)/shard_map/ppermute | solution.py:630
  44.0 5.4 %collective-permute-start.19 = (bf16[128,384]{1,0:T(8,128)(2,1)S(1)}, bf16[128,384]{1,0:T(8,128)(2,1)S(1)}, u32[]{:S(2)}, u32[]{:S(2)}) collective-permute-start(bf16[128,384]{1,0:T(8,128)(2,1)S(1)} %merge.3.second_ref), channel_id=1, source_target_pairs={{0,1},{1,0},{2,3},{3,2},{4,5},{5,4},{6,7},{7,6},{8,9},{9,8},{10,11... | collective-permute-start | bytes 294920 | tf_op jit(solution)/shard_map/ppermute | solution.py:630

commit v18 on v17

--- a/solution.py
+++ b/solution.py
@@ -12,6 +12,7 @@
 TRIPLE = 3 * HEAD_DIM
 EXTRA = 16
 PIECE = 2 * HEAD_DIM
+LOOK_AHEAD = 2
 EPS = 1e-06
 F32 = jnp.float32
 BF16 = jnp.bfloat16
@@ -159,12 +160,14 @@
     ]
     for source, target in zip(refs[:small], refs[small + 2 : -2]):
         copies.append(pltpu.make_async_copy(source, target, sems.at[len(copies)]))
-    for copy in copies:
-        copy.start()
+    copies[0].start()
 
     for block in range(later + 1):
         if block:
             copies[block - 1].wait()
+        if block == 1:
+            for copy in copies[later:]:
+                copy.start()
         for start in range(0, columns, PIECE):
             cells = slice(start, start + PIECE)
             part = w_buffer[block - 1, :, cells] if block else ahead_ref[:, cells]
@@ -178,6 +181,9 @@
                     text_ref[:, target : target + HEAD_DIM] = product[
                         top:, local : local + HEAD_DIM
                     ]
+            if block == 0 and start == 0:
+                for copy in copies[1:later]:
+                    copy.start()
     for copy in copies[later:]:
         copy.wait()
 
@@ -346,12 +352,12 @@
             last = start + 2 == len(blocks)
             work.append((head, blocks[start : start + 2], keep if last else None))
 
-    upcoming = scores_of(*work[0][:2])
+    upcoming = [scores_of(*item[:2]) for item in work[:LOOK_AHEAD]]
     num = den = None
     for index, (head, group, kept) in enumerate(work):
-        scores = upcoming
-        if index + 1 < len(work):
-            upcoming = scores_of(*work[index + 1][:2])
+        scores = upcoming.pop(0)
+        if index + LOOK_AHEAD < len(work):
+            upcoming.append(scores_of(*work[index + LOOK_AHEAD][:2]))
         weights = jnp.exp2(scores * FACTOR)
         if kept is not None:
             weights = weights * kept
@@ -380,7 +386,10 @@
         att_ref[:, columns] = (num / den).astype(BF16)
 
 
-def part_kernel(place_ref, weight_ref, first_ref, second_ref, out_ref, w_other_ref, w_ref, sems):
+def part_kernel(
+    place_ref, weight_ref, hidden_ref, first_ref, second_ref, out_ref, w_other_ref, hidden_copy_ref,
+    w_ref, sems,
+):
     depth = w_ref.shape[0]
     half = first_ref.shape[1]
     copies = []
@@ -389,12 +398,15 @@
     ):
         rows = pl.ds(pl.multiple_of(group * depth, depth), depth)
         copies.append(pltpu.make_async_copy(weight_ref.at[rows], target, sems.at[index]))
-        copies[-1].start()
+    copies.append(pltpu.make_async_copy(hidden_ref, hidden_copy_ref, sems.at[2]))
+    for copy in copies:
+        copy.start()
     copies[0].wait()
     out_ref[...] = jnp.dot(
         first_ref[...], w_ref[:half, :], preferred_element_type=F32
     ) + jnp.dot(second_ref[...], w_ref[half:, :], preferred_element_type=F32)
-    copies[1].wait()
+    for copy in copies[1:]:
+        copy.wait()
 
 
 def more_kernel(part_ref, att_ref, w_ref, out_ref):
@@ -549,7 +561,7 @@
     )
     chains = [[ring_step((split[0], split[2]))], [ring_step((split[1], split[3]))]]
 
-    small = (query_gain, key_gain, text_mask, branch_gate, hidden, stale_cache)
+    small = (query_gain, key_gain, text_mask, branch_gate, stale_cache)
     outs = pl.pallas_call(
         own_kernel,
         in_specs=[smem, vmem, vmem, hbm] + [hbm] * len(small),
@@ -568,7 +580,7 @@
         name="project_own",
     )(place, a_rows, own_ahead, *map(in_hbm, (qkv_weight,) + small))
     own, own_text = outs[:2]
-    query_gain, key_gain, text_mask, branch_gate, hidden, stale = outs[2:]
+    query_gain, key_gain, text_mask, branch_gate, stale = outs[2:]
 
     for _ in range(half_way - 3):
         for chain in chains:
@@ -630,22 +642,23 @@
         other_attended.append(lax.ppermute(attended[-1], "head", swap_head))
 
     out_cost = cost(4 * video * width * out_features, 2 * width * out_features)
-    part, w_other = pl.pallas_call(
+    part, w_other, hidden = pl.pallas_call(
         part_kernel,
-        in_specs=[smem, hbm, vmem, vmem],
-        out_specs=[vmem] * 2,
+        in_specs=[smem, hbm, hbm, vmem, vmem],
+        out_specs=[vmem] * 3,
         out_shape=[
             jax.ShapeDtypeStruct((video, out_features), F32),
             jax.ShapeDtypeStruct((width, out_features), BF16),
+            jax.ShapeDtypeStruct(hidden.shape, BF16),
         ],
         scratch_shapes=[
             pltpu.VMEM((width, out_features), BF16),
-            pltpu.SemaphoreType.DMA((2,)),
+            pltpu.SemaphoreType.DMA((3,)),
         ],
         compiler_params=params(24),
         cost_estimate=out_cost,
         name="part_out",
-    )(place, in_hbm(out_weight), *attended)
+    )(place, in_hbm(out_weight), in_hbm(hidden), *attended)
     (part,) = plain_call(
         more_kernel, [((video, out_features), F32)], "more_out", out_cost,
         part, other_attended[0], w_other,

time: 50.7 us -> 51 us (level)
  waiting for transfers between devices: 4.6 us -> 5.72 us
    ppermute x10, waiting for transfers between devices: 3.12 us -> 4.25 us  [ring_step(): lax.ppermute(block, 'section', way)]
    pallas_call x1, Pallas kernels: 4.9 us -> 4.35 us  [per_device(): pl.pallas_call(own_kernel, in_specs=[smem, vmem, vmem, hbm] + [hbm] * len...]
  transfers between devices with their start and end apart: 20 -> 20, of which waited for: 6 -> 8; matrix products, arithmetic and copies ran while one was open for 0% -> 0% of each run, Pallas kernels for 42% -> 41%
where the time goes in v18:
time: 51 us; the launch traced here: 50.8 us
  starting transfers between devices  22.4 us (44%)
  Pallas kernels  21.8 us (43%)
  waiting for transfers between devices  5.72 us (11%)
  between operations  0.78 us (2%)
    ppermute x10, starting transfers between devices, ring_step(): lax.ppermute(block, 'section', way)  12.1 us
    pallas_call x1, Pallas kernels, per_device(): pl.pallas_call(own_kernel, in_specs=[smem, vmem, vmem, hbm] + [hbm] * len...  4.35 us
    ppermute x10, waiting for transfers between devices, ring_step(): lax.ppermute(block, 'section', way)  4.25 us
    pallas_call x2, Pallas kernels, per_device(): pl.pallas_call(functools.partial(attend_kernel, first, len(whole)), in_sp...  4.07 us
    pallas_call x1, Pallas kernels, per_device(): pl.pallas_call(functools.partial(send_more_kernel, video), in_specs=[smem...  4.01 us
    ppermute x2, starting transfers between devices, per_device(): far = [lax.ppermute(chain[-1][0], 'section', ways[0]) for chain in chains]  3.81 us
    ppermute x2, starting transfers between devices, per_device(): other_attended.append(lax.ppermute(attended[-1], 'head', swap_head))  3.51 us
    pallas_call x1, Pallas kernels, per_device(): pl.pallas_call(send_kernel, in_specs=[smem] + [hbm] * 5, out_specs=[vmem]...  3.4 us
  transfers between devices with their start and end apart: 20, of which 8 were waited for; matrix products, arithmetic and copies ran while one was open for 0% of the time, Pallas kernels for 41%

profile of v18, /device:TPU:0, one launch (start us, length us, event | category | flops | bytes accessed | tf_op | source)
XLA Modules:
  0.0 50.8 jit_solution(4108301210683572707)
XLA Ops:
  0.6 3.1 %collective-permute-start.2 = (bf16[2,128,768]{2,1,0:T(8,128)(2,1)}, bf16[2,128,768]{2,1,0:T(8,128)(2,1)S(1)}, u32[]{:S(2)}, u32[]{:S(2)}) collective-permute-start(bf16[2,128,768]{2,1,0:T(8,128)(2,1)} %refs_4_.1), channel_id=1, source_target_pairs={{0,8},{2,6},{4,0},{6,14},{8,16},{10,2},{12,4},{14,22},{16,24},{18,... | collective-permute-start | bytes 1179656 | tf_op jit(solution)/shard_map/ppermute | solution.py:500
  3.8 3.4 %project_send.1 = (bf16[272,1536]{1,0:T(8,128)(2,1)S(1)}, bf16[688,128]{1,0:T(8,128)(2,1)S(1)}, f32[272,128]{1,0:T(8,128)S(1)}, bf16[1536,768]{1,0:T(8,128)(2,1)S(1)}) custom-call(s32[2]{0:T(128)S(1)} %pad_add_fusion.place_ref, bf16[128,1536]{1,0:T(8,128)(2,1)} %hidden_ref.1, bf16[256,1536]{1,0:T(8,128)(2,1)} %t_ref.1, f32[1536]{0:T(1024)} %scale_ref.1, ...), custom_call_target="tpu_custom_call" | custom-call | flops 3080296960 | bytes 2831155 | tf_op jit(solution)/shard_map/project_send/pallas_call | solution.py:515
  7.2 2.0 %collective-permute-start = (bf16[688,128]{1,0:T(8,128)(2,1)S(1)}, bf16[688,128]{1,0:T(8,128)(2,1)S(1)}, u32[]{:S(2)}, u32[]{:S(2)}) collective-permute-start(bf16[688,128]{1,0:T(8,128)(2,1)S(1)} %get-tuple-element.44), channel_id=1, source_target_pairs={{0,1},{1,0},{2,3},{3,2},{4,5},{5,4},{6,7},{7,6},{8,9},{9,8},{10,11... | collective-permute-start | bytes 528392 | tf_op jit(solution)/shard_map/ppermute | solution.py:537
  9.2 4.0 %project_send_more.1 = (bf16[3280,128]{1,0:T(8,128)(2,1)S(1)}, bf16[1536,768]{1,0:T(8,128)(2,1)S(1)}) custom-call(s32[2]{0:T(128)S(1)} %pad_add_fusion.place_ref, bf16[272,1536]{1,0:T(8,128)(2,1)S(1)} %get-tuple-element.40.a_ref, bf16[1536,768]{1,0:T(8,128)(2,1)S(1)} %get-tuple-element.41.ahead_ref, bf16[1536,4608]{1,0:T(8,128)(2,1)} %w_ref.5), custom_call_target="tpu_custom_call" | custom-call | flops 4620445184 | bytes 4246732 | tf_op jit(solution)/shard_map/project_send_more/pallas_call | solution.py:539
  13.5 2.1 %collective-permute-start.4 = (bf16[2,128,384]{2,1,0:T(8,128)(2,1)S(1)}, bf16[2,128,384]{2,1,0:T(8,128)(2,1)S(1)}, u32[]{:S(2)}, u32[]{:S(2)}) collective-permute-start(bf16[2,128,384]{2,1,0:T(8,128)(2,1)S(1)} %get-tuple-element.48), channel_id=1, source_target_pairs={{0,8},{2,6},{4,0},{6,14},{8,16},{10,2},{12,4},{14,22},{16,24},{18,... | collective-permute-start | bytes 589832 | tf_op jit(solution)/shard_map/ppermute | solution.py:500
  15.9 1.7 %collective-permute-start.6 = (bf16[2,128,384]{2,1,0:T(8,128)(2,1)S(1)}, bf16[2,128,384]{2,1,0:T(8,128)(2,1)S(1)}, u32[]{:S(2)}, u32[]{:S(2)}) collective-permute-start(bf16[2,128,384]{2,1,0:T(8,128)(2,1)S(1)} %get-tuple-element.50), channel_id=1, source_target_pairs={{0,8},{2,6},{4,0},{6,14},{8,16},{10,2},{12,4},{14,22},{16,24},{18,... | collective-permute-start | bytes 589832 | tf_op jit(solution)/shard_map/ppermute | solution.py:500
  17.9 4.4 %project_own.1 = (f32[144,2304]{1,0:T(8,128)S(1)}, f32[128,1536]{1,0:T(8,128)S(1)}, f32[128]{0:T(128)S(1)}, f32[128]{0:T(128)S(1)}, s32[256]{0:T(256)S(1)}, /*in...) custom-call(s32[2]{0:T(128)S(1)} %pad_add_fusion.place_ref, bf16[272,1536]{1,0:T(8,128)(2,1)S(1)} %get-tuple-element.40.a_ref, ...), custom_call_target="tpu_custom_call" | custom-call | flops 7700742144 | bytes 7077888 | tf_op jit(solution)/shard_map/project_own/pallas_call | solution.py:565
  22.7 1.3 %collective-permute-start.9 = (bf16[2,128,384]{2,1,0:T(8,128)(2,1)S(1)}, bf16[2,128,384]{2,1,0:T(8,128)(2,1)S(1)}, u32[]{:S(2)}, u32[]{:S(2)}) collective-permute-start(bf16[2,128,384]{2,1,0:T(8,128)(2,1)S(1)} %collective-permute-done.4.refs_2_), channel_id=1, source_target_pairs={{0,8},{2,6},{4,0},{6,14},{8,16},{10,2},{12,4},{14,22},{16,24},{18,... | collective-permute-start | bytes 589832 | tf_op jit(solution)/shard_map/ppermute | solution.py:500
  24.0 0.9 %collective-permute-done.6.refs_2_ = bf16[2,128,384]{2,1,0:T(8,128)(2,1)S(1)} collective-permute-done((bf16[2,128,384]{2,1,0:T(8,128)(2,1)S(1)}, bf16[2,128,384]{2,1,0:T(8,128)(2,1)S(1)}, u32[]{:S(2)}, u32[]{:S(2)}) %collective-permute-start.6) | collective-permute-done | bytes 196640 | tf_op jit(solution)/shard_map/ppermute | solution.py:500
  24.9 2.0 %collective-permute-start.14 = (bf16[2,128,384]{2,1,0:T(8,128)(2,1)S(1)}, bf16[2,128,384]{2,1,0:T(8,128)(2,1)S(1)}, u32[]{:S(2)}, u32[]{:S(2)}) collective-permute-start(bf16[2,128,384]{2,1,0:T(8,128)(2,1)S(1)} %collective-permute-done.6.refs_2_), channel_id=1, source_target_pairs={{0,8},{2,6},{4,0},{6,14},{8,16},{10,2},{12,4},{14,22},{16,24},{18,... | collective-permute-start | bytes 589832 | tf_op jit(solution)/shard_map/ppermute | solution.py:500
  27.5 0.9 %collective-permute-done.9.refs_4_ = bf16[2,128,384]{2,1,0:T(8,128)(2,1)S(1)} collective-permute-done((bf16[2,128,384]{2,1,0:T(8,128)(2,1)S(1)}, bf16[2,128,384]{2,1,0:T(8,128)(2,1)S(1)}, u32[]{:S(2)}, u32[]{:S(2)}) %collective-permute-start.9) | collective-permute-done | bytes 196640 | tf_op jit(solution)/shard_map/ppermute | solution.py:500
  28.4 1.3 %collective-permute-start.11 = (bf16[2,128,384]{2,1,0:T(8,128)(2,1)S(1)}, bf16[2,128,384]{2,1,0:T(8,128)(2,1)S(1)}, u32[]{:S(2)}, u32[]{:S(2)}) collective-permute-start(bf16[2,128,384]{2,1,0:T(8,128)(2,1)S(1)} %collective-permute-done.9.refs_4_), channel_id=1, source_target_pairs={{0,8},{2,6},{4,0},{6,14},{8,16},{10,2},{12,4},{14,22},{16,24},{18,... | collective-permute-start | bytes 589832 | tf_op jit(solution)/shard_map/ppermute | solution.py:588
  29.7 0.7 %collective-permute-start.15 = (bf16[2,128,384]{2,1,0:T(8,128)(2,1)S(1)}, bf16[2,128,384]{2,1,0:T(8,128)(2,1)S(1)}, u32[]{:S(2)}, u32[]{:S(2)}) collective-permute-start(bf16[2,128,384]{2,1,0:T(8,128)(2,1)S(1)} %collective-permute-done.7.refs_3_), channel_id=1, source_target_pairs={{0,4},{2,10},{4,12},{6,2},{8,0},{10,18},{12,20},{14,6},{16,8},{18,... | collective-permute-start | bytes 589832 | tf_op jit(solution)/shard_map/ppermute | solution.py:500
  30.4 1.9 %collective-permute-done.14.refs_4_ = bf16[2,128,384]{2,1,0:T(8,128)(2,1)S(1)} collective-permute-done((bf16[2,128,384]{2,1,0:T(8,128)(2,1)S(1)}, bf16[2,128,384]{2,1,0:T(8,128)(2,1)S(1)}, u32[]{:S(2)}, u32[]{:S(2)}) %collective-permute-start.14) | collective-permute-done | bytes 196640 | tf_op jit(solution)/shard_map/ppermute | solution.py:500
  32.2 2.5 %collective-permute-start.16 = (bf16[2,128,384]{2,1,0:T(8,128)(2,1)S(1)}, bf16[2,128,384]{2,1,0:T(8,128)(2,1)S(1)}, u32[]{:S(2)}, u32[]{:S(2)}) collective-permute-start(bf16[2,128,384]{2,1,0:T(8,128)(2,1)S(1)} %collective-permute-done.14.refs_4_), channel_id=1, source_target_pairs={{0,8},{2,6},{4,0},{6,14},{8,16},{10,2},{12,4},{14,22},{16,24},{18,... | collective-permute-start | bytes 589832 | tf_op jit(solution)/shard_map/ppermute | solution.py:588
  34.7 0.7 %norm_video.1 = (bf16[128,384]{1,0:T(8,128)(2,1)S(1)}, bf16[128,384]{1,0:T(8,128)(2,1)S(1)}, bf16[2,128,768]{2,1,0:T(8,128)(2,1)S(1)}) custom-call(f32[144,2304]{1,0:T(8,128)S(1)} %get-tuple-element.43.own_ref.top_ref, bf16[688,128]{1,0:T(8,128)(2,1)S(1)} %collective-permute-done.first_ref, bf16[3280,128]{1,0:T(8,128)(2,1)S(1)} %collective-permute-done.1.more_ref, ...), custom_call_target="tpu_custom_call" | custom-call | flops 331776000 | bytes 2654208 | tf_op jit(solution)/shard_map/norm_video/pallas_call | solution.py:455
  36.0 0.5 %norm_text.1.text_ref = bf16[2,128,768]{2,1,0:T(8,128)(2,1)S(1)} custom-call(f32[128,1536]{1,0:T(8,128)S(1)} %get-tuple-element.59.own_ref, bf16[688,128]{1,0:T(8,128)(2,1)S(1)} %collective-permute-done.first_ref, bf16[3280,128]{1,0:T(8,128)(2,1)S(1)} %collective-permute-done.1.more_ref, f32[272,128]{1,0:T(8,128)S(1)} %get-tuple-element.53.stat_ref, ...), custom_call_target="tpu_custom_call" | custom-call | flops 294912 | bytes 294912 | tf_op jit(solution)/shard_map/norm_text/pallas_call | solution.py:455
  36.8 1.8 %attend.2 = (f32[128,384]{1,0:T(8,128)S(1)}, f32[128,128]{1,0:T(8,128)S(1)}, f32[128,512]{1,0:T(8,128)S(1)}) custom-call(s32[2]{0:T(128)S(1)} %pad_add_fusion.place_ref, bf16[128,384]{1,0:T(8,128)(2,1)S(1)} %get-tuple-element.56.qo_ref, bf16[128,384]{1,0:T(8,128)(2,1)S(1)} %collective-permute-done.8.qp_ref, ...), custom_call_target="tpu_custom_call" | custom-call | flops 163840 | bytes 983040 | tf_op jit(solution)/shard_map/attend/pallas_call | solution.py:616
  39.5 2.3 %attend.3 = (f32[128,384]{1,0:T(8,128)S(1)}, f32[128,128]{1,0:T(8,128)S(1)}, f32[128,512]{1,0:T(8,128)S(1)}, bf16[2,128,768]{2,1,0:T(8,128)(2,1)}) custom-call(s32[2]{0:T(128)S(1)} %pad_add_fusion.place_ref, bf16[128,384]{1,0:T(8,128)(2,1)S(1)} %get-tuple-element.67.qo_ref, bf16[128,384]{1,0:T(8,128)(2,1)S(1)} %collective-permute-done.13.qp_ref, ...), custom_call_target="tpu_custom_call" | custom-call | flops 163840 | bytes 983040 | tf_op jit(solution)/shard_map/attend/pallas_call | solution.py:616
  42.0 2.1 %collective-permute-start.18 = (bf16[128,384]{1,0:T(8,128)(2,1)S(1)}, bf16[128,384]{1,0:T(8,128)(2,1)S(1)}, u32[]{:S(2)}, u32[]{:S(2)}) collective-permute-start(bf16[128,384]{1,0:T(8,128)(2,1)S(1)} %merge.2.first_ref), channel_id=1, source_target_pairs={{0,1},{1,0},{2,3},{3,2},{4,5},{5,4},{6,7},{7,6},{8,9},{9,8},{10,11... | collective-permute-start | bytes 294920 | tf_op jit(solution)/shard_map/ppermute | solution.py:642
  44.3 1.4 %collective-permute-start.19 = (bf16[128,384]{1,0:T(8,128)(2,1)S(1)}, bf16[128,384]{1,0:T(8,128)(2,1)S(1)}, u32[]{:S(2)}, u32[]{:S(2)}) collective-permute-start(bf16[128,384]{1,0:T(8,128)(2,1)S(1)} %merge.3.second_ref), channel_id=1, source_target_pairs={{0,1},{1,0},{2,3},{3,2},{4,5},{5,4},{6,7},{7,6},{8,9},{9,8},{10,11... | collective-permute-start | bytes 294920 | tf_op jit(solution)/shard_map/ppermute | solution.py:642
  45.7 3.0 %part_out.1 = (f32[128,1536]{1,0:T(8,128)S(1)}, bf16[768,1536]{1,0:T(8,128)(2,1)S(1)}, bf16[128,1536]{1,0:T(8,128)(2,1)S(1)}) custom-call(s32[2]{0:T(128)S(1)} %pad_add_fusion.place_ref, bf16[1536,1536]{1,0:T(8,128)(2,1)} %weight_ref.1, bf16[128,1536]{1,0:T(8,128)(2,1)} %hidden_ref.1, bf16[128,384]{1,0:T(8,128)(2,1)S(1)} %merge.2.first_ref, ...), custom_call_target="tpu_custom_call" | custom-call | flops 603979776 | bytes 2359296 | tf_op jit(solution)/shard_map/part_out/pallas_call | solution.py:645
  49.1 0.7 %collective-permute-done.19.att_ref = bf16[128,384]{1,0:T(8,128)(2,1)S(1)} collective-permute-done((bf16[128,384]{1,0:T(8,128)(2,1)S(1)}, bf16[128,384]{1,0:T(8,128)(2,1)S(1)}, u32[]{:S(2)}, u32[]{:S(2)}) %collective-permute-start.19) | collective-permute-done | bytes 98336 | tf_op jit(solution)/shard_map/ppermute | solution.py:642
  49.7 1.1 %final_out.1 = bf16[128,1536]{1,0:T(8,128)(2,1)} custom-call(f32[128,1536]{1,0:T(8,128)S(1)} %more_out.1.part_ref, bf16[128,384]{1,0:T(8,128)(2,1)S(1)} %collective-permute-done.19.att_ref, bf16[768,1536]{1,0:T(8,128)(2,1)S(1)} %get-tuple-element.74.w_ref, bf16[128,1536]{1,0:T(8,128)(2,1)S(1)} %get-tuple-element.75.hidden_ref, ...), custom_call_target="tpu_custom_call" | custom-call | flops 603979776 | bytes 2359296 | tf_op jit(solution)/shard_map/final_out/pallas_call | solution.py:666
  (30 shorter events, 4.4 us)
Async XLA Ops:
  0.6 12.8 %collective-permute-start.2 = (bf16[2,128,768]{2,1,0:T(8,128)(2,1)}, bf16[2,128,768]{2,1,0:T(8,128)(2,1)S(1)}, u32[]{:S(2)}, u32[]{:S(2)}) collective-permute-start(bf16[2,128,768]{2,1,0:T(8,128)(2,1)} %refs_4_.1), channel_id=1, source_target_pairs={{0,8},{2,6},{4,0},{6,14},{8,16},{10,2},{12,4},{14,22},{16,24},{18,... | collective-permute-start | bytes 1179656 | tf_op jit(solution)/shard_map/ppermute | solution.py:500
  3.7 9.7 %collective-permute-start.3 = (bf16[2,128,768]{2,1,0:T(8,128)(2,1)}, bf16[2,128,768]{2,1,0:T(8,128)(2,1)S(1)}, u32[]{:S(2)}, u32[]{:S(2)}) collective-permute-start(bf16[2,128,768]{2,1,0:T(8,128)(2,1)} %refs_4_.1), channel_id=1, source_target_pairs={{0,4},{2,10},{4,12},{6,2},{8,0},{10,18},{12,20},{14,6},{16,8},{18,... | collective-permute-start | bytes 1179656 | tf_op jit(solution)/shard_map/ppermute | solution.py:500
  7.2 6.2 %collective-permute-start = (bf16[688,128]{1,0:T(8,128)(2,1)S(1)}, bf16[688,128]{1,0:T(8,128)(2,1)S(1)}, u32[]{:S(2)}, u32[]{:S(2)}) collective-permute-start(bf16[688,128]{1,0:T(8,128)(2,1)S(1)} %get-tuple-element.44), channel_id=1, source_target_pairs={{0,1},{1,0},{2,3},{3,2},{4,5},{5,4},{6,7},{7,6},{8,9},{9,8},{10,11... | collective-permute-start | bytes 528392 | tf_op jit(solution)/shard_map/ppermute | solution.py:537
  13.2 21.5 %collective-permute-start.1 = (bf16[3280,128]{1,0:T(8,128)(2,1)S(1)}, bf16[3280,128]{1,0:T(8,128)(2,1)S(1)}, u32[]{:S(2)}, u32[]{:S(2)}) collective-permute-start(bf16[3280,128]{1,0:T(8,128)(2,1)S(1)} %get-tuple-element.45), channel_id=1, source_target_pairs={{0,1},{1,0},{2,3},{3,2},{4,5},{5,4},{6,7},{7,6},{8,9},{9,8},{10,11... | collective-permute-start | bytes 2519048 | tf_op jit(solution)/shard_map/ppermute | solution.py:556
  13.5 8.8 %collective-permute-start.4 = (bf16[2,128,384]{2,1,0:T(8,128)(2,1)S(1)}, bf16[2,128,384]{2,1,0:T(8,128)(2,1)S(1)}, u32[]{:S(2)}, u32[]{:S(2)}) collective-permute-start(bf16[2,128,384]{2,1,0:T(8,128)(2,1)S(1)} %get-tuple-element.48), channel_id=1, source_target_pairs={{0,8},{2,6},{4,0},{6,14},{8,16},{10,2},{12,4},{14,22},{16,24},{18,... | collective-permute-start | bytes 589832 | tf_op jit(solution)/shard_map/ppermute | solution.py:500
  15.5 7.2 %collective-permute-start.5 = (bf16[2,128,384]{2,1,0:T(8,128)(2,1)S(1)}, bf16[2,128,384]{2,1,0:T(8,128)(2,1)S(1)}, u32[]{:S(2)}, u32[]{:S(2)}) collective-permute-start(bf16[2,128,384]{2,1,0:T(8,128)(2,1)S(1)} %get-tuple-element.49), channel_id=1, source_target_pairs={{0,4},{2,10},{4,12},{6,2},{8,0},{10,18},{12,20},{14,6},{16,8},{18,... | collective-permute-start | bytes 589832 | tf_op jit(solution)/shard_map/ppermute | solution.py:500
  15.9 9.0 %collective-permute-start.6 = (bf16[2,128,384]{2,1,0:T(8,128)(2,1)S(1)}, bf16[2,128,384]{2,1,0:T(8,128)(2,1)S(1)}, u32[]{:S(2)}, u32[]{:S(2)}) collective-permute-start(bf16[2,128,384]{2,1,0:T(8,128)(2,1)S(1)} %get-tuple-element.50), channel_id=1, source_target_pairs={{0,8},{2,6},{4,0},{6,14},{8,16},{10,2},{12,4},{14,22},{16,24},{18,... | collective-permute-start | bytes 589832 | tf_op jit(solution)/shard_map/ppermute | solution.py:500
  17.6 7.4 %collective-permute-start.7 = (bf16[2,128,384]{2,1,0:T(8,128)(2,1)S(1)}, bf16[2,128,384]{2,1,0:T(8,128)(2,1)S(1)}, u32[]{:S(2)}, u32[]{:S(2)}) collective-permute-start(bf16[2,128,384]{2,1,0:T(8,128)(2,1)S(1)} %get-tuple-element.51), channel_id=1, source_target_pairs={{0,4},{2,10},{4,12},{6,2},{8,0},{10,18},{12,20},{14,6},{16,8},{18,... | collective-permute-start | bytes 589832 | tf_op jit(solution)/shard_map/ppermute | solution.py:500
  22.7 5.7 %collective-permute-start.9 = (bf16[2,128,384]{2,1,0:T(8,128)(2,1)S(1)}, bf16[2,128,384]{2,1,0:T(8,128)(2,1)S(1)}, u32[]{:S(2)}, u32[]{:S(2)}) collective-permute-start(bf16[2,128,384]{2,1,0:T(8,128)(2,1)S(1)} %collective-permute-done.4.refs_2_), channel_id=1, source_target_pairs={{0,8},{2,6},{4,0},{6,14},{8,16},{10,2},{12,4},{14,22},{16,24},{18,... | collective-permute-start | bytes 589832 | tf_op jit(solution)/shard_map/ppermute | solution.py:500
  24.9 7.3 %collective-permute-start.14 = (bf16[2,128,384]{2,1,0:T(8,128)(2,1)S(1)}, bf16[2,128,384]{2,1,0:T(8,128)(2,1)S(1)}, u32[]{:S(2)}, u32[]{:S(2)}) collective-permute-start(bf16[2,128,384]{2,1,0:T(8,128)(2,1)S(1)} %collective-permute-done.6.refs_2_), channel_id=1, source_target_pairs={{0,8},{2,6},{4,0},{6,14},{8,16},{10,2},{12,4},{14,22},{16,24},{18,... | collective-permute-start | bytes 589832 | tf_op jit(solution)/shard_map/ppermute | solution.py:500
  27.0 8.6 %collective-permute-start.10 = (bf16[2,128,384]{2,1,0:T(8,128)(2,1)S(1)}, bf16[2,128,384]{2,1,0:T(8,128)(2,1)S(1)}, u32[]{:S(2)}, u32[]{:S(2)}) collective-permute-start(bf16[2,128,384]{2,1,0:T(8,128)(2,1)S(1)} %collective-permute-done.5.refs_3_), channel_id=1, source_target_pairs={{0,4},{2,10},{4,12},{6,2},{8,0},{10,18},{12,20},{14,6},{16,8},{18,... | collective-permute-start | bytes 589832 | tf_op jit(solution)/shard_map/ppermute | solution.py:500
  28.4 8.4 %collective-permute-start.11 = (bf16[2,128,384]{2,1,0:T(8,128)(2,1)S(1)}, bf16[2,128,384]{2,1,0:T(8,128)(2,1)S(1)}, u32[]{:S(2)}, u32[]{:S(2)}) collective-permute-start(bf16[2,128,384]{2,1,0:T(8,128)(2,1)S(1)} %collective-permute-done.9.refs_4_), channel_id=1, source_target_pairs={{0,8},{2,6},{4,0},{6,14},{8,16},{10,2},{12,4},{14,22},{16,24},{18,... | collective-permute-start | bytes 589832 | tf_op jit(solution)/shard_map/ppermute | solution.py:588
  29.7 9.3 %collective-permute-start.15 = (bf16[2,128,384]{2,1,0:T(8,128)(2,1)S(1)}, bf16[2,128,384]{2,1,0:T(8,128)(2,1)S(1)}, u32[]{:S(2)}, u32[]{:S(2)}) collective-permute-start(bf16[2,128,384]{2,1,0:T(8,128)(2,1)S(1)} %collective-permute-done.7.refs_3_), channel_id=1, source_target_pairs={{0,4},{2,10},{4,12},{6,2},{8,0},{10,18},{12,20},{14,6},{16,8},{18,... | collective-permute-start | bytes 589832 | tf_op jit(solution)/shard_map/ppermute | solution.py:500
  32.2 7.3 %collective-permute-start.16 = (bf16[2,128,384]{2,1,0:T(8,128)(2,1)S(1)}, bf16[2,128,384]{2,1,0:T(8,128)(2,1)S(1)}, u32[]{:S(2)}, u32[]{:S(2)}) collective-permute-start(bf16[2,128,384]{2,1,0:T(8,128)(2,1)S(1)} %collective-permute-done.14.refs_4_), channel_id=1, source_target_pairs={{0,8},{2,6},{4,0},{6,14},{8,16},{10,2},{12,4},{14,22},{16,24},{18,... | collective-permute-start | bytes 589832 | tf_op jit(solution)/shard_map/ppermute | solution.py:588
  35.4 1.4 %collective-permute-start.8 = (bf16[128,384]{1,0:T(8,128)(2,1)S(1)}, bf16[128,384]{1,0:T(8,128)(2,1)S(1)}, u32[]{:S(2)}, u32[]{:S(2)}) collective-permute-start(bf16[128,384]{1,0:T(8,128)(2,1)S(1)} %get-tuple-element.56.qo_ref), channel_id=1, source_target_pairs={{0,2},{2,0},{4,6},{6,4},{8,10},{10,8},{12,14},{14,12},{16,18},{18,... | collective-permute-start | bytes 294920 | tf_op jit(solution)/shard_map/ppermute | solution.py:598
  35.5 3.5 %collective-permute-start.13 = (bf16[128,384]{1,0:T(8,128)(2,1)S(1)}, bf16[128,384]{1,0:T(8,128)(2,1)S(1)}, u32[]{:S(2)}, u32[]{:S(2)}) collective-permute-start(bf16[128,384]{1,0:T(8,128)(2,1)S(1)} %get-tuple-element.67.qo_ref), channel_id=1, source_target_pairs={{0,2},{2,0},{4,6},{6,4},{8,10},{10,8},{12,14},{14,12},{16,18},{18,... | collective-permute-start | bytes 294920 | tf_op jit(solution)/shard_map/ppermute | solution.py:598
  38.6 3.3 %collective-permute-start.12 = (f32[128,512]{1,0:T(8,128)S(1)}, f32[128,512]{1,0:T(8,128)S(1)}, u32[]{:S(2)}, u32[]{:S(2)}) collective-permute-start(f32[128,512]{1,0:T(8,128)S(1)} %get-tuple-element.65), channel_id=1, source_target_pairs={{0,2},{2,0},{4,6},{6,4},{8,10},{10,8},{12,14},{14,12},{16,18},{18,... | collective-permute-start | bytes 786440 | tf_op jit(solution)/shard_map/ppermute | solution.py:634
  41.8 2.4 %collective-permute-start.17 = (f32[128,512]{1,0:T(8,128)S(1)}, f32[128,512]{1,0:T(8,128)S(1)}, u32[]{:S(2)}, u32[]{:S(2)}) collective-permute-start(f32[128,512]{1,0:T(8,128)S(1)} %get-tuple-element.72), channel_id=1, source_target_pairs={{0,2},{2,0},{4,6},{6,4},{8,10},{10,8},{12,14},{14,12},{16,18},{18,... | collective-permute-start | bytes 786440 | tf_op jit(solution)/shard_map/ppermute | solution.py:634
  42.0 6.6 %collective-permute-start.18 = (bf16[128,384]{1,0:T(8,128)(2,1)S(1)}, bf16[128,384]{1,0:T(8,128)(2,1)S(1)}, u32[]{:S(2)}, u32[]{:S(2)}) collective-permute-start(bf16[128,384]{1,0:T(8,128)(2,1)S(1)} %merge.2.first_ref), channel_id=1, source_target_pairs={{0,1},{1,0},{2,3},{3,2},{4,5},{5,4},{6,7},{7,6},{8,9},{9,8},{10,11... | collective-permute-start | bytes 294920 | tf_op jit(solution)/shard_map/ppermute | solution.py:642
  44.3 5.4 %collective-permute-start.19 = (bf16[128,384]{1,0:T(8,128)(2,1)S(1)}, bf16[128,384]{1,0:T(8,128)(2,1)S(1)}, u32[]{:S(2)}, u32[]{:S(2)}) collective-permute-start(bf16[128,384]{1,0:T(8,128)(2,1)S(1)} %merge.3.second_ref), channel_id=1, source_target_pairs={{0,1},{1,0},{2,3},{3,2},{4,5},{5,4},{6,7},{7,6},{8,9},{9,8},{10,11... | collective-permute-start | bytes 294920 | tf_op jit(solution)/shard_map/ppermute | solution.py:642

commit v19 on v16

--- a/solution.py
+++ b/solution.py
@@ -12,6 +12,7 @@
 TRIPLE = 3 * HEAD_DIM
 EXTRA = 16
 PIECE = 2 * HEAD_DIM
+LOOK_AHEAD = 2
 EPS = 1e-06
 F32 = jnp.float32
 BF16 = jnp.bfloat16
@@ -159,12 +160,14 @@
     ]
     for source, target in zip(refs[:small], refs[small + 2 : -2]):
         copies.append(pltpu.make_async_copy(source, target, sems.at[len(copies)]))
-    for copy in copies:
-        copy.start()
+    copies[0].start()
 
     for block in range(later + 1):
         if block:
             copies[block - 1].wait()
+        if block == 1:
+            for copy in copies[later:]:
+                copy.start()
         for start in range(0, columns, PIECE):
             cells = slice(start, start + PIECE)
             part = w_buffer[block - 1, :, cells] if block else ahead_ref[:, cells]
@@ -178,6 +181,9 @@
                     text_ref[:, target : target + HEAD_DIM] = product[
                         top:, local : local + HEAD_DIM
                     ]
+            if block == 0 and start == 0:
+                for copy in copies[1:later]:
+                    copy.start()
     for copy in copies[later:]:
         copy.wait()
 
@@ -305,15 +311,12 @@
 
 
 def attend_kernel(
-    first, count, place_ref, qo_ref, qp_ref, fresh_ref, stale_ref, text_ref, mask_ref, *refs,
+    first, count, finish, place_ref, qo_ref, qp_ref, fresh_ref, stale_ref, text_ref, mask_ref, *refs,
 ):
-    finish = len(refs[-1].shape) == 0
+    *refs, num_ref, den_ref = refs
     if finish:
-        *refs, own_ref, own_den_ref, msg_ref, cache_ref, sem = refs
-        cache_copy = pltpu.make_async_copy(fresh_ref, cache_ref, sem)
-        cache_copy.start()
-    else:
-        *refs, num_ref, den_ref = refs
+        *refs, own_ref = refs
+        own_den_ref, msg_ref = num_ref, den_ref
     video, width = qo_ref.shape
     text = text_ref.shape[1]
     lane = lax.broadcasted_iota(jnp.int32, (2 * video, HEAD_DIM), 1)
@@ -347,12 +350,12 @@
             last = start + 2 == len(blocks)
             work.append((head, blocks[start : start + 2], keep if last else None))
 
-    upcoming = scores_of(*work[0][:2])
+    upcoming = [scores_of(*item[:2]) for item in work[:LOOK_AHEAD]]
     num = den = None
     for index, (head, group, kept) in enumerate(work):
-        scores = upcoming
-        if index + 1 < len(work):
-            upcoming = scores_of(*work[index + 1][:2])
+        scores = upcoming.pop(0)
+        if index + LOOK_AHEAD < len(work):
+            upcoming.append(scores_of(*work[index + LOOK_AHEAD][:2]))
         weights = jnp.exp2(scores * FACTOR)
         if kept is not None:
             weights = weights * kept
@@ -371,7 +374,6 @@
     if finish:
         own_den_ref[...] = packed[:video]
         msg_ref[:, width:] = packed[video:]
-        cache_copy.wait()
     else:
         den_ref[...] = packed
 
@@ -403,7 +405,10 @@
         att_ref[:, columns] = (num / den).astype(BF16)
 
 
-def part_kernel(place_ref, weight_ref, first_ref, second_ref, out_ref, w_other_ref, w_ref, sems):
+def part_kernel(
+    place_ref, weight_ref, hidden_ref, fresh_ref, first_ref, second_ref,
+    out_ref, w_other_ref, hidden_copy_ref, cache_ref, w_ref, sems,
+):
     depth = w_ref.shape[0]
     half = first_ref.shape[1]
     copies = []
@@ -412,12 +417,16 @@
     ):
         rows = pl.ds(pl.multiple_of(group * depth, depth), depth)
         copies.append(pltpu.make_async_copy(weight_ref.at[rows], target, sems.at[index]))
-        copies[-1].start()
+    copies.append(pltpu.make_async_copy(hidden_ref, hidden_copy_ref, sems.at[2]))
+    copies.append(pltpu.make_async_copy(fresh_ref, cache_ref, sems.at[3]))
+    for copy in copies:
+        copy.start()
     copies[0].wait()
     out_ref[...] = jnp.dot(
         first_ref[...], w_ref[:half, :], preferred_element_type=F32
     ) + jnp.dot(second_ref[...], w_ref[half:, :], preferred_element_type=F32)
-    copies[1].wait()
+    for copy in copies[1:]:
+        copy.wait()
 
 
 def more_kernel(part_ref, att_ref, w_ref, out_ref):
@@ -572,7 +581,7 @@
     )
     chains = [[ring_step((split[0], split[2]))], [ring_step((split[1], split[3]))]]
 
-    small = (query_gain, key_gain, text_mask, branch_gate, hidden, stale_cache)
+    small = (query_gain, key_gain, text_mask, branch_gate, stale_cache)
     outs = pl.pallas_call(
         own_kernel,
         in_specs=[smem, vmem, vmem, hbm] + [hbm] * len(small),
@@ -591,12 +600,12 @@
         name="project_own",
     )(place, a_rows, own_ahead, *map(in_hbm, (qkv_weight,) + small))
     own, own_text = outs[:2]
-    query_gain, key_gain, text_mask, branch_gate, hidden, stale = outs[2:]
+    query_gain, key_gain, text_mask, branch_gate, stale = outs[2:]
 
     for _ in range(half_way - 3):
         for chain in chains:
             chain.append(ring_step(lax.optimization_barrier((*chain[-1], own))[:2]))
-    far = [lax.ppermute(chains[0][-1][0], "section", ways[0])]
+    far = [lax.ppermute(chain[-1][0], "section", ways[0]) for chain in chains]
 
     received_more = lax.optimization_barrier((received_more, *chains[0][0], *chains[1][0]))[0]
     *queries, fresh = plain_call(
@@ -615,8 +624,6 @@
         own_text, received, received_more, stats, own, key_gain,
     )
 
-    last = lax.optimization_barrier((chains[1][-1][0], text_kv, queries[0]))[0]
-    far.append(lax.ppermute(last, "section", ways[0]))
     context = chips * video + video + text
     finished = [
         jax.ShapeDtypeStruct((video, width // 2), F32),
@@ -627,23 +634,22 @@
     for index, chain in enumerate(chains):
         first = index * heads // 2
         halves = [block for step in chain for block in step]
-        finish = index == 1
+        finish = index == 0
         own_queries = queries[index]
         if finish:
             halves.append(far[index])
+            outs = finished
+        else:
             own_queries = lax.optimization_barrier((own_queries, num_own))[0]
-            outs = finished + [jax.ShapeDtypeStruct(fresh.shape, BF16)]
-        else:
             outs = [
                 jax.ShapeDtypeStruct((2 * video, width // 2), F32),
                 jax.ShapeDtypeStruct((2 * video, HEAD_DIM), F32),
             ]
         outs = pl.pallas_call(
-            functools.partial(attend_kernel, first, len(whole)),
+            functools.partial(attend_kernel, first, len(whole), finish),
             in_specs=[smem] + [vmem] * (6 + len(whole) + len(halves)),
-            out_specs=[vmem] * (len(outs) - finish) + [hbm] * finish,
+            out_specs=[vmem] * len(outs),
             out_shape=outs,
-            scratch_shapes=[pltpu.SemaphoreType.DMA] * finish,
             compiler_params=params(24),
             cost_estimate=cost(video * context, context * width, video * heads),
             name="attend",
@@ -651,9 +657,7 @@
             place, own_queries, other_queries[index], fresh, stale, text_kv, text_mask,
             *whole, *halves,
         )
-        if finish:
-            *outs, new_cache = outs
-        else:
+        if not finish:
             outs = plain_call(
                 functools.partial(last_kernel, first),
                 [(out.shape, out.dtype) for out in finished],
@@ -673,22 +677,24 @@
         other_attended.append(lax.ppermute(attended[-1], "head", swap_head))
 
     out_cost = cost(4 * video * width * out_features, 2 * width * out_features)
-    part, w_other = pl.pallas_call(
+    part, w_other, hidden, new_cache = pl.pallas_call(
         part_kernel,
-        in_specs=[smem, hbm, vmem, vmem],
-        out_specs=[vmem] * 2,
+        in_specs=[smem, hbm, hbm] + [vmem] * 3,
+        out_specs=[vmem] * 3 + [hbm],
         out_shape=[
             jax.ShapeDtypeStruct((video, out_features), F32),
             jax.ShapeDtypeStruct((width, out_features), BF16),
+            jax.ShapeDtypeStruct(hidden.shape, BF16),
+            jax.ShapeDtypeStruct(fresh.shape, BF16),
         ],
         scratch_shapes=[
             pltpu.VMEM((width, out_features), BF16),
-            pltpu.SemaphoreType.DMA((2,)),
+            pltpu.SemaphoreType.DMA((4,)),
         ],
         compiler_params=params(24),
         cost_estimate=out_cost,
         name="part_out",
-    )(place, in_hbm(out_weight), *attended)
+    )(place, in_hbm(out_weight), in_hbm(hidden), fresh, *attended)
     (part,) = plain_call(
         more_kernel, [((video, out_features), F32)], "more_out", out_cost,
         part, other_attended[0], w_other,

time: 50.7 us -> 50.2 us (level)
  starting transfers between devices: 21.6 us -> 22.3 us
  waiting for transfers between devices: 5.57 us -> 4.92 us
    ppermute x10, waiting for transfers between devices: 1.47 us -> 4.25 us  [ring_step(): lax.ppermute(block, 'section', way)]
    ppermute x1, waiting for transfers between devices: 2.27 us -> 0.01 us  [per_device(): received_more = lax.ppermute(message_more, 'head', swap_head)]
    pallas_call x1, Pallas kernels: 4.9 us -> 4.35 us  [per_device(): pl.pallas_call(own_kernel, in_specs=[smem, vmem, vmem, hbm] + [hbm] * len...]
    ppermute x2, waiting for transfers between devices: 0.79 us -> 0.26 us  [per_device(): lax.ppermute(half, 'section', swap_core)]
  transfers between devices with their start and end apart: 20 -> 20, of which waited for: 6 -> 7; matrix products, arithmetic and copies ran while one was open for 0% -> 0% of each run, Pallas kernels for 42% -> 42%
where the time goes in v19:
time: 50.2 us; the launch traced here: 50 us
  starting transfers between devices  22.3 us (44%)
  Pallas kernels  22 us (44%)
  waiting for transfers between devices  4.92 us (10%)
  between operations  0.78 us (2%)
    ppermute x10, starting transfers between devices, ring_step(): lax.ppermute(block, 'section', way)  12.1 us
    pallas_call x1, Pallas kernels, per_device(): pl.pallas_call(own_kernel, in_specs=[smem, vmem, vmem, hbm] + [hbm] * len...  4.35 us
    ppermute x10, waiting for transfers between devices, ring_step(): lax.ppermute(block, 'section', way)  4.25 us
    pallas_call x1, Pallas kernels, per_device(): pl.pallas_call(functools.partial(send_more_kernel, video), in_specs=[smem...  4.01 us
    ppermute x2, starting transfers between devices, per_device(): far = [lax.ppermute(chain[-1][0], 'section', ways[0]) for chain in chains]  3.81 us
    pallas_call x2, Pallas kernels, per_device(): pl.pallas_call(functools.partial(attend_kernel, first, len(whole), finish...  3.55 us
    pallas_call x1, Pallas kernels, per_device(): pl.pallas_call(send_kernel, in_specs=[smem] + [hbm] * 5, out_specs=[vmem]...  3.4 us
    ppermute x2, starting transfers between devices, per_device(): other_attended.append(lax.ppermute(attended[-1], 'head', swap_head))  3.19 us
  transfers between devices with their start and end apart: 20, of which 7 were waited for; matrix products, arithmetic and copies ran while one was open for 0% of the time, Pallas kernels for 42%

profile of v19, /device:TPU:0, one launch (start us, length us, event | category | flops | bytes accessed | tf_op | source)
XLA Modules:
  0.0 50.0 jit_solution(3283187841742408779)
XLA Ops:
  0.6 3.1 %collective-permute-start.2 = (bf16[2,128,768]{2,1,0:T(8,128)(2,1)}, bf16[2,128,768]{2,1,0:T(8,128)(2,1)S(1)}, u32[]{:S(2)}, u32[]{:S(2)}) collective-permute-start(bf16[2,128,768]{2,1,0:T(8,128)(2,1)} %refs_4_.1), channel_id=1, source_target_pairs={{0,8},{2,6},{4,0},{6,14},{8,16},{10,2},{12,4},{14,22},{16,24},{18,... | collective-permute-start | bytes 1179656 | tf_op jit(solution)/shard_map/ppermute | solution.py:520
  3.8 3.4 %project_send.1 = (bf16[272,1536]{1,0:T(8,128)(2,1)S(1)}, bf16[688,128]{1,0:T(8,128)(2,1)S(1)}, f32[272,128]{1,0:T(8,128)S(1)}, bf16[1536,768]{1,0:T(8,128)(2,1)S(1)}) custom-call(s32[2]{0:T(128)S(1)} %pad_add_fusion.place_ref, bf16[128,1536]{1,0:T(8,128)(2,1)} %hidden_ref.1, bf16[256,1536]{1,0:T(8,128)(2,1)} %t_ref.1, f32[1536]{0:T(1024)} %scale_ref.1, ...), custom_call_target="tpu_custom_call" | custom-call | flops 3080296960 | bytes 2831155 | tf_op jit(solution)/shard_map/project_send/pallas_call | solution.py:535
  7.2 2.0 %collective-permute-start = (bf16[688,128]{1,0:T(8,128)(2,1)S(1)}, bf16[688,128]{1,0:T(8,128)(2,1)S(1)}, u32[]{:S(2)}, u32[]{:S(2)}) collective-permute-start(bf16[688,128]{1,0:T(8,128)(2,1)S(1)} %get-tuple-element.46), channel_id=1, source_target_pairs={{0,1},{1,0},{2,3},{3,2},{4,5},{5,4},{6,7},{7,6},{8,9},{9,8},{10,11... | collective-permute-start | bytes 528392 | tf_op jit(solution)/shard_map/ppermute | solution.py:557
  9.2 4.0 %project_send_more.1 = (bf16[3280,128]{1,0:T(8,128)(2,1)S(1)}, bf16[1536,768]{1,0:T(8,128)(2,1)S(1)}) custom-call(s32[2]{0:T(128)S(1)} %pad_add_fusion.place_ref, bf16[272,1536]{1,0:T(8,128)(2,1)S(1)} %get-tuple-element.42.a_ref, bf16[1536,768]{1,0:T(8,128)(2,1)S(1)} %get-tuple-element.43.ahead_ref, bf16[1536,4608]{1,0:T(8,128)(2,1)} %w_ref.5), custom_call_target="tpu_custom_call" | custom-call | flops 4620445184 | bytes 4246732 | tf_op jit(solution)/shard_map/project_send_more/pallas_call | solution.py:559
  13.5 2.1 %collective-permute-start.4 = (bf16[2,128,384]{2,1,0:T(8,128)(2,1)S(1)}, bf16[2,128,384]{2,1,0:T(8,128)(2,1)S(1)}, u32[]{:S(2)}, u32[]{:S(2)}) collective-permute-start(bf16[2,128,384]{2,1,0:T(8,128)(2,1)S(1)} %get-tuple-element.50), channel_id=1, source_target_pairs={{0,8},{2,6},{4,0},{6,14},{8,16},{10,2},{12,4},{14,22},{16,24},{18,... | collective-permute-start | bytes 589832 | tf_op jit(solution)/shard_map/ppermute | solution.py:520
  15.9 1.7 %collective-permute-start.6 = (bf16[2,128,384]{2,1,0:T(8,128)(2,1)S(1)}, bf16[2,128,384]{2,1,0:T(8,128)(2,1)S(1)}, u32[]{:S(2)}, u32[]{:S(2)}) collective-permute-start(bf16[2,128,384]{2,1,0:T(8,128)(2,1)S(1)} %get-tuple-element.52), channel_id=1, source_target_pairs={{0,8},{2,6},{4,0},{6,14},{8,16},{10,2},{12,4},{14,22},{16,24},{18,... | collective-permute-start | bytes 589832 | tf_op jit(solution)/shard_map/ppermute | solution.py:520
  17.9 4.4 %project_own.1 = (f32[144,2304]{1,0:T(8,128)S(1)}, f32[128,1536]{1,0:T(8,128)S(1)}, f32[128]{0:T(128)S(1)}, f32[128]{0:T(128)S(1)}, s32[256]{0:T(256)S(1)}, /*in...) custom-call(s32[2]{0:T(128)S(1)} %pad_add_fusion.place_ref, bf16[272,1536]{1,0:T(8,128)(2,1)S(1)} %get-tuple-element.42.a_ref, ...), custom_call_target="tpu_custom_call" | custom-call | flops 7700742144 | bytes 7077888 | tf_op jit(solution)/shard_map/project_own/pallas_call | solution.py:585
  22.7 1.3 %collective-permute-start.9 = (bf16[2,128,384]{2,1,0:T(8,128)(2,1)S(1)}, bf16[2,128,384]{2,1,0:T(8,128)(2,1)S(1)}, u32[]{:S(2)}, u32[]{:S(2)}) collective-permute-start(bf16[2,128,384]{2,1,0:T(8,128)(2,1)S(1)} %collective-permute-done.4.refs_2_), channel_id=1, source_target_pairs={{0,8},{2,6},{4,0},{6,14},{8,16},{10,2},{12,4},{14,22},{16,24},{18,... | collective-permute-start | bytes 589832 | tf_op jit(solution)/shard_map/ppermute | solution.py:520
  24.0 0.9 %collective-permute-done.6.refs_2_ = bf16[2,128,384]{2,1,0:T(8,128)(2,1)S(1)} collective-permute-done((bf16[2,128,384]{2,1,0:T(8,128)(2,1)S(1)}, bf16[2,128,384]{2,1,0:T(8,128)(2,1)S(1)}, u32[]{:S(2)}, u32[]{:S(2)}) %collective-permute-start.6) | collective-permute-done | bytes 196640 | tf_op jit(solution)/shard_map/ppermute | solution.py:520
  24.9 2.0 %collective-permute-start.14 = (bf16[2,128,384]{2,1,0:T(8,128)(2,1)S(1)}, bf16[2,128,384]{2,1,0:T(8,128)(2,1)S(1)}, u32[]{:S(2)}, u32[]{:S(2)}) collective-permute-start(bf16[2,128,384]{2,1,0:T(8,128)(2,1)S(1)} %collective-permute-done.6.refs_2_), channel_id=1, source_target_pairs={{0,8},{2,6},{4,0},{6,14},{8,16},{10,2},{12,4},{14,22},{16,24},{18,... | collective-permute-start | bytes 589832 | tf_op jit(solution)/shard_map/ppermute | solution.py:520
  27.5 0.9 %collective-permute-done.9.refs_4_ = bf16[2,128,384]{2,1,0:T(8,128)(2,1)S(1)} collective-permute-done((bf16[2,128,384]{2,1,0:T(8,128)(2,1)S(1)}, bf16[2,128,384]{2,1,0:T(8,128)(2,1)S(1)}, u32[]{:S(2)}, u32[]{:S(2)}) %collective-permute-start.9) | collective-permute-done | bytes 196640 | tf_op jit(solution)/shard_map/ppermute | solution.py:520
  28.4 1.3 %collective-permute-start.11 = (bf16[2,128,384]{2,1,0:T(8,128)(2,1)S(1)}, bf16[2,128,384]{2,1,0:T(8,128)(2,1)S(1)}, u32[]{:S(2)}, u32[]{:S(2)}) collective-permute-start(bf16[2,128,384]{2,1,0:T(8,128)(2,1)S(1)} %collective-permute-done.9.refs_4_), channel_id=1, source_target_pairs={{0,8},{2,6},{4,0},{6,14},{8,16},{10,2},{12,4},{14,22},{16,24},{18,... | collective-permute-start | bytes 589832 | tf_op jit(solution)/shard_map/ppermute | solution.py:608
  29.7 0.7 %collective-permute-start.15 = (bf16[2,128,384]{2,1,0:T(8,128)(2,1)S(1)}, bf16[2,128,384]{2,1,0:T(8,128)(2,1)S(1)}, u32[]{:S(2)}, u32[]{:S(2)}) collective-permute-start(bf16[2,128,384]{2,1,0:T(8,128)(2,1)S(1)} %collective-permute-done.7.refs_3_), channel_id=1, source_target_pairs={{0,4},{2,10},{4,12},{6,2},{8,0},{10,18},{12,20},{14,6},{16,8},{18,... | collective-permute-start | bytes 589832 | tf_op jit(solution)/shard_map/ppermute | solution.py:520
  30.4 1.9 %collective-permute-done.14.refs_4_ = bf16[2,128,384]{2,1,0:T(8,128)(2,1)S(1)} collective-permute-done((bf16[2,128,384]{2,1,0:T(8,128)(2,1)S(1)}, bf16[2,128,384]{2,1,0:T(8,128)(2,1)S(1)}, u32[]{:S(2)}, u32[]{:S(2)}) %collective-permute-start.14) | collective-permute-done | bytes 196640 | tf_op jit(solution)/shard_map/ppermute | solution.py:520
  32.2 2.5 %collective-permute-start.16 = (bf16[2,128,384]{2,1,0:T(8,128)(2,1)S(1)}, bf16[2,128,384]{2,1,0:T(8,128)(2,1)S(1)}, u32[]{:S(2)}, u32[]{:S(2)}) collective-permute-start(bf16[2,128,384]{2,1,0:T(8,128)(2,1)S(1)} %collective-permute-done.14.refs_4_), channel_id=1, source_target_pairs={{0,8},{2,6},{4,0},{6,14},{8,16},{10,2},{12,4},{14,22},{16,24},{18,... | collective-permute-start | bytes 589832 | tf_op jit(solution)/shard_map/ppermute | solution.py:608
  34.7 0.7 %norm_video.1 = (bf16[128,384]{1,0:T(8,128)(2,1)S(1)}, bf16[128,384]{1,0:T(8,128)(2,1)S(1)}, bf16[2,128,768]{2,1,0:T(8,128)(2,1)S(1)}) custom-call(f32[144,2304]{1,0:T(8,128)S(1)} %get-tuple-element.45.own_ref.top_ref, bf16[688,128]{1,0:T(8,128)(2,1)S(1)} %collective-permute-done.first_ref, bf16[3280,128]{1,0:T(8,128)(2,1)S(1)} %collective-permute-done.1.more_ref, ...), custom_call_target="tpu_custom_call" | custom-call | flops 331776000 | bytes 2654208 | tf_op jit(solution)/shard_map/norm_video/pallas_call | solution.py:475
  36.0 0.5 %norm_text.1.text_ref = bf16[2,128,768]{2,1,0:T(8,128)(2,1)S(1)} custom-call(f32[128,1536]{1,0:T(8,128)S(1)} %get-tuple-element.61.own_ref, bf16[688,128]{1,0:T(8,128)(2,1)S(1)} %collective-permute-done.first_ref, bf16[3280,128]{1,0:T(8,128)(2,1)S(1)} %collective-permute-done.1.more_ref, f32[272,128]{1,0:T(8,128)S(1)} %get-tuple-element.55.stat_ref, ...), custom_call_target="tpu_custom_call" | custom-call | flops 294912 | bytes 294912 | tf_op jit(solution)/shard_map/norm_text/pallas_call | solution.py:475
  36.8 1.8 %attend.2 = (f32[128,384]{1,0:T(8,128)S(1)}, f32[128,128]{1,0:T(8,128)S(1)}, f32[128,512]{1,0:T(8,128)S(1)}) custom-call(s32[2]{0:T(128)S(1)} %pad_add_fusion.place_ref, bf16[128,384]{1,0:T(8,128)(2,1)S(1)} %get-tuple-element.59.qo_ref, bf16[128,384]{1,0:T(8,128)(2,1)S(1)} %collective-permute-done.8.qp_ref, ...), custom_call_target="tpu_custom_call" | custom-call | flops 163840 | bytes 983040 | tf_op jit(solution)/shard_map/attend/pallas_call | solution.py:648
  39.0 1.7 %attend.3 = (f32[256,384]{1,0:T(8,128)S(1)}, f32[256,128]{1,0:T(8,128)S(1)}) custom-call(s32[2]{0:T(128)S(1)} %pad_add_fusion.place_ref, bf16[128,384]{1,0:T(8,128)(2,1)S(1)} %get-tuple-element.69.qo_ref, bf16[128,384]{1,0:T(8,128)(2,1)S(1)} %collective-permute-done.13.qp_ref, bf16[2,128,768]{2,1,0:T(8,128)(2,1)S(1)} %get-tuple-element.58.fresh_ref, ...), custom_call_target="tpu_custom_call" | custom-call | flops 163840 | bytes 983040 | tf_op jit(solution)/shard_map/attend/pallas_call | solution.py:648
  40.8 0.5 %attend_last.1 = (f32[128,384]{1,0:T(8,128)S(1)}, f32[128,128]{1,0:T(8,128)S(1)}, f32[128,512]{1,0:T(8,128)S(1)}) custom-call(bf16[128,384]{1,0:T(8,128)(2,1)S(1)} %get-tuple-element.69.qo_ref, bf16[128,384]{1,0:T(8,128)(2,1)S(1)} %collective-permute-done.13.qp_ref, f32[256,384]{1,0:T(8,128)S(1)} %get-tuple-element.72.num_ref, ...), custom_call_target="tpu_custom_call" | custom-call | flops 16384 | bytes 98304 | tf_op jit(solution)/shard_map/attend_last/pallas_call | solution.py:475
  41.7 2.2 %collective-permute-start.18 = (bf16[128,384]{1,0:T(8,128)(2,1)S(1)}, bf16[128,384]{1,0:T(8,128)(2,1)S(1)}, u32[]{:S(2)}, u32[]{:S(2)}) collective-permute-start(bf16[128,384]{1,0:T(8,128)(2,1)S(1)} %merge.2.first_ref), channel_id=1, source_target_pairs={{0,1},{1,0},{2,3},{3,2},{4,5},{5,4},{6,7},{7,6},{8,9},{9,8},{10,11... | collective-permute-start | bytes 294920 | tf_op jit(solution)/shard_map/ppermute | solution.py:677
  44.0 1.0 %collective-permute-start.19 = (bf16[128,384]{1,0:T(8,128)(2,1)S(1)}, bf16[128,384]{1,0:T(8,128)(2,1)S(1)}, u32[]{:S(2)}, u32[]{:S(2)}) collective-permute-start(bf16[128,384]{1,0:T(8,128)(2,1)S(1)} %merge.3.second_ref), channel_id=1, source_target_pairs={{0,1},{1,0},{2,3},{3,2},{4,5},{5,4},{6,7},{7,6},{8,9},{9,8},{10,11... | collective-permute-start | bytes 294920 | tf_op jit(solution)/shard_map/ppermute | solution.py:677
  45.0 3.1 %part_out.1 = (f32[128,1536]{1,0:T(8,128)S(1)}, bf16[768,1536]{1,0:T(8,128)(2,1)S(1)}, bf16[128,1536]{1,0:T(8,128)(2,1)S(1)}, bf16[2,128,768]{2,1,0:T(8,128)(2,1)}) custom-call(s32[2]{0:T(128)S(1)} %pad_add_fusion.place_ref, bf16[1536,1536]{1,0:T(8,128)(2,1)} %weight_ref.1, bf16[128,1536]{1,0:T(8,128)(2,1)} %hidden_ref.1, ...), custom_call_target="tpu_custom_call" | custom-call | flops 603979776 | bytes 2359296 | tf_op jit(solution)/shard_map/part_out/pallas_call | solution.py:680
  48.9 1.1 %final_out.1 = bf16[128,1536]{1,0:T(8,128)(2,1)} custom-call(f32[128,1536]{1,0:T(8,128)S(1)} %more_out.1.part_ref, bf16[128,384]{1,0:T(8,128)(2,1)S(1)} %collective-permute-done.19.att_ref, bf16[768,1536]{1,0:T(8,128)(2,1)S(1)} %get-tuple-element.78.w_ref, bf16[128,1536]{1,0:T(8,128)(2,1)S(1)} %get-tuple-element.79.hidden_ref, ...), custom_call_target="tpu_custom_call" | custom-call | flops 603979776 | bytes 2359296 | tf_op jit(solution)/shard_map/final_out/pallas_call | solution.py:702
  (31 shorter events, 4.4 us)
Async XLA Ops:
  0.6 12.8 %collective-permute-start.2 = (bf16[2,128,768]{2,1,0:T(8,128)(2,1)}, bf16[2,128,768]{2,1,0:T(8,128)(2,1)S(1)}, u32[]{:S(2)}, u32[]{:S(2)}) collective-permute-start(bf16[2,128,768]{2,1,0:T(8,128)(2,1)} %refs_4_.1), channel_id=1, source_target_pairs={{0,8},{2,6},{4,0},{6,14},{8,16},{10,2},{12,4},{14,22},{16,24},{18,... | collective-permute-start | bytes 1179656 | tf_op jit(solution)/shard_map/ppermute | solution.py:520
  3.7 9.7 %collective-permute-start.3 = (bf16[2,128,768]{2,1,0:T(8,128)(2,1)}, bf16[2,128,768]{2,1,0:T(8,128)(2,1)S(1)}, u32[]{:S(2)}, u32[]{:S(2)}) collective-permute-start(bf16[2,128,768]{2,1,0:T(8,128)(2,1)} %refs_4_.1), channel_id=1, source_target_pairs={{0,4},{2,10},{4,12},{6,2},{8,0},{10,18},{12,20},{14,6},{16,8},{18,... | collective-permute-start | bytes 1179656 | tf_op jit(solution)/shard_map/ppermute | solution.py:520
  7.2 6.2 %collective-permute-start = (bf16[688,128]{1,0:T(8,128)(2,1)S(1)}, bf16[688,128]{1,0:T(8,128)(2,1)S(1)}, u32[]{:S(2)}, u32[]{:S(2)}) collective-permute-start(bf16[688,128]{1,0:T(8,128)(2,1)S(1)} %get-tuple-element.46), channel_id=1, source_target_pairs={{0,1},{1,0},{2,3},{3,2},{4,5},{5,4},{6,7},{7,6},{8,9},{9,8},{10,11... | collective-permute-start | bytes 528392 | tf_op jit(solution)/shard_map/ppermute | solution.py:557
  13.2 21.5 %collective-permute-start.1 = (bf16[3280,128]{1,0:T(8,128)(2,1)S(1)}, bf16[3280,128]{1,0:T(8,128)(2,1)S(1)}, u32[]{:S(2)}, u32[]{:S(2)}) collective-permute-start(bf16[3280,128]{1,0:T(8,128)(2,1)S(1)} %get-tuple-element.47), channel_id=1, source_target_pairs={{0,1},{1,0},{2,3},{3,2},{4,5},{5,4},{6,7},{7,6},{8,9},{9,8},{10,11... | collective-permute-start | bytes 2519048 | tf_op jit(solution)/shard_map/ppermute | solution.py:576
  13.5 8.8 %collective-permute-start.4 = (bf16[2,128,384]{2,1,0:T(8,128)(2,1)S(1)}, bf16[2,128,384]{2,1,0:T(8,128)(2,1)S(1)}, u32[]{:S(2)}, u32[]{:S(2)}) collective-permute-start(bf16[2,128,384]{2,1,0:T(8,128)(2,1)S(1)} %get-tuple-element.50), channel_id=1, source_target_pairs={{0,8},{2,6},{4,0},{6,14},{8,16},{10,2},{12,4},{14,22},{16,24},{18,... | collective-permute-start | bytes 589832 | tf_op jit(solution)/shard_map/ppermute | solution.py:520
  15.5 7.2 %collective-permute-start.5 = (bf16[2,128,384]{2,1,0:T(8,128)(2,1)S(1)}, bf16[2,128,384]{2,1,0:T(8,128)(2,1)S(1)}, u32[]{:S(2)}, u32[]{:S(2)}) collective-permute-start(bf16[2,128,384]{2,1,0:T(8,128)(2,1)S(1)} %get-tuple-element.51), channel_id=1, source_target_pairs={{0,4},{2,10},{4,12},{6,2},{8,0},{10,18},{12,20},{14,6},{16,8},{18,... | collective-permute-start | bytes 589832 | tf_op jit(solution)/shard_map/ppermute | solution.py:520
  15.9 9.0 %collective-permute-start.6 = (bf16[2,128,384]{2,1,0:T(8,128)(2,1)S(1)}, bf16[2,128,384]{2,1,0:T(8,128)(2,1)S(1)}, u32[]{:S(2)}, u32[]{:S(2)}) collective-permute-start(bf16[2,128,384]{2,1,0:T(8,128)(2,1)S(1)} %get-tuple-element.52), channel_id=1, source_target_pairs={{0,8},{2,6},{4,0},{6,14},{8,16},{10,2},{12,4},{14,22},{16,24},{18,... | collective-permute-start | bytes 589832 | tf_op jit(solution)/shard_map/ppermute | solution.py:520
  17.6 7.4 %collective-permute-start.7 = (bf16[2,128,384]{2,1,0:T(8,128)(2,1)S(1)}, bf16[2,128,384]{2,1,0:T(8,128)(2,1)S(1)}, u32[]{:S(2)}, u32[]{:S(2)}) collective-permute-start(bf16[2,128,384]{2,1,0:T(8,128)(2,1)S(1)} %get-tuple-element.53), channel_id=1, source_target_pairs={{0,4},{2,10},{4,12},{6,2},{8,0},{10,18},{12,20},{14,6},{16,8},{18,... | collective-permute-start | bytes 589832 | tf_op jit(solution)/shard_map/ppermute | solution.py:520
  22.7 5.7 %collective-permute-start.9 = (bf16[2,128,384]{2,1,0:T(8,128)(2,1)S(1)}, bf16[2,128,384]{2,1,0:T(8,128)(2,1)S(1)}, u32[]{:S(2)}, u32[]{:S(2)}) collective-permute-start(bf16[2,128,384]{2,1,0:T(8,128)(2,1)S(1)} %collective-permute-done.4.refs_2_), channel_id=1, source_target_pairs={{0,8},{2,6},{4,0},{6,14},{8,16},{10,2},{12,4},{14,22},{16,24},{18,... | collective-permute-start | bytes 589832 | tf_op jit(solution)/shard_map/ppermute | solution.py:520
  24.9 7.3 %collective-permute-start.14 = (bf16[2,128,384]{2,1,0:T(8,128)(2,1)S(1)}, bf16[2,128,384]{2,1,0:T(8,128)(2,1)S(1)}, u32[]{:S(2)}, u32[]{:S(2)}) collective-permute-start(bf16[2,128,384]{2,1,0:T(8,128)(2,1)S(1)} %collective-permute-done.6.refs_2_), channel_id=1, source_target_pairs={{0,8},{2,6},{4,0},{6,14},{8,16},{10,2},{12,4},{14,22},{16,24},{18,... | collective-permute-start | bytes 589832 | tf_op jit(solution)/shard_map/ppermute | solution.py:520
  27.0 8.6 %collective-permute-start.10 = (bf16[2,128,384]{2,1,0:T(8,128)(2,1)S(1)}, bf16[2,128,384]{2,1,0:T(8,128)(2,1)S(1)}, u32[]{:S(2)}, u32[]{:S(2)}) collective-permute-start(bf16[2,128,384]{2,1,0:T(8,128)(2,1)S(1)} %collective-permute-done.5.refs_3_), channel_id=1, source_target_pairs={{0,4},{2,10},{4,12},{6,2},{8,0},{10,18},{12,20},{14,6},{16,8},{18,... | collective-permute-start | bytes 589832 | tf_op jit(solution)/shard_map/ppermute | solution.py:520
  28.4 8.4 %collective-permute-start.11 = (bf16[2,128,384]{2,1,0:T(8,128)(2,1)S(1)}, bf16[2,128,384]{2,1,0:T(8,128)(2,1)S(1)}, u32[]{:S(2)}, u32[]{:S(2)}) collective-permute-start(bf16[2,128,384]{2,1,0:T(8,128)(2,1)S(1)} %collective-permute-done.9.refs_4_), channel_id=1, source_target_pairs={{0,8},{2,6},{4,0},{6,14},{8,16},{10,2},{12,4},{14,22},{16,24},{18,... | collective-permute-start | bytes 589832 | tf_op jit(solution)/shard_map/ppermute | solution.py:608
  29.7 9.3 %collective-permute-start.15 = (bf16[2,128,384]{2,1,0:T(8,128)(2,1)S(1)}, bf16[2,128,384]{2,1,0:T(8,128)(2,1)S(1)}, u32[]{:S(2)}, u32[]{:S(2)}) collective-permute-start(bf16[2,128,384]{2,1,0:T(8,128)(2,1)S(1)} %collective-permute-done.7.refs_3_), channel_id=1, source_target_pairs={{0,4},{2,10},{4,12},{6,2},{8,0},{10,18},{12,20},{14,6},{16,8},{18,... | collective-permute-start | bytes 589832 | tf_op jit(solution)/shard_map/ppermute | solution.py:520
  32.2 8.5 %collective-permute-start.16 = (bf16[2,128,384]{2,1,0:T(8,128)(2,1)S(1)}, bf16[2,128,384]{2,1,0:T(8,128)(2,1)S(1)}, u32[]{:S(2)}, u32[]{:S(2)}) collective-permute-start(bf16[2,128,384]{2,1,0:T(8,128)(2,1)S(1)} %collective-permute-done.14.refs_4_), channel_id=1, source_target_pairs={{0,8},{2,6},{4,0},{6,14},{8,16},{10,2},{12,4},{14,22},{16,24},{18,... | collective-permute-start | bytes 589832 | tf_op jit(solution)/shard_map/ppermute | solution.py:608
  35.4 1.4 %collective-permute-start.8 = (bf16[128,384]{1,0:T(8,128)(2,1)S(1)}, bf16[128,384]{1,0:T(8,128)(2,1)S(1)}, u32[]{:S(2)}, u32[]{:S(2)}) collective-permute-start(bf16[128,384]{1,0:T(8,128)(2,1)S(1)} %get-tuple-element.59.qo_ref), channel_id=1, source_target_pairs={{0,2},{2,0},{4,6},{6,4},{8,10},{10,8},{12,14},{14,12},{16,18},{18,... | collective-permute-start | bytes 294920 | tf_op jit(solution)/shard_map/ppermute | solution.py:618
  35.5 3.5 %collective-permute-start.13 = (bf16[128,384]{1,0:T(8,128)(2,1)S(1)}, bf16[128,384]{1,0:T(8,128)(2,1)S(1)}, u32[]{:S(2)}, u32[]{:S(2)}) collective-permute-start(bf16[128,384]{1,0:T(8,128)(2,1)S(1)} %get-tuple-element.69.qo_ref), channel_id=1, source_target_pairs={{0,2},{2,0},{4,6},{6,4},{8,10},{10,8},{12,14},{14,12},{16,18},{18,... | collective-permute-start | bytes 294920 | tf_op jit(solution)/shard_map/ppermute | solution.py:618
  38.6 2.9 %collective-permute-start.12 = (f32[128,512]{1,0:T(8,128)S(1)}, f32[128,512]{1,0:T(8,128)S(1)}, u32[]{:S(2)}, u32[]{:S(2)}) collective-permute-start(f32[128,512]{1,0:T(8,128)S(1)} %get-tuple-element.67), channel_id=1, source_target_pairs={{0,2},{2,0},{4,6},{6,4},{8,10},{10,8},{12,14},{14,12},{16,18},{18,... | collective-permute-start | bytes 786440 | tf_op jit(solution)/shard_map/ppermute | solution.py:669
  41.3 2.6 %collective-permute-start.17 = (f32[128,512]{1,0:T(8,128)S(1)}, f32[128,512]{1,0:T(8,128)S(1)}, u32[]{:S(2)}, u32[]{:S(2)}) collective-permute-start(f32[128,512]{1,0:T(8,128)S(1)} %get-tuple-element.76), channel_id=1, source_target_pairs={{0,2},{2,0},{4,6},{6,4},{8,10},{10,8},{12,14},{14,12},{16,18},{18,... | collective-permute-start | bytes 786440 | tf_op jit(solution)/shard_map/ppermute | solution.py:669
  41.7 6.5 %collective-permute-start.18 = (bf16[128,384]{1,0:T(8,128)(2,1)S(1)}, bf16[128,384]{1,0:T(8,128)(2,1)S(1)}, u32[]{:S(2)}, u32[]{:S(2)}) collective-permute-start(bf16[128,384]{1,0:T(8,128)(2,1)S(1)} %merge.2.first_ref), channel_id=1, source_target_pairs={{0,1},{1,0},{2,3},{3,2},{4,5},{5,4},{6,7},{7,6},{8,9},{9,8},{10,11... | collective-permute-start | bytes 294920 | tf_op jit(solution)/shard_map/ppermute | solution.py:677
  44.0 5.0 %collective-permute-start.19 = (bf16[128,384]{1,0:T(8,128)(2,1)S(1)}, bf16[128,384]{1,0:T(8,128)(2,1)S(1)}, u32[]{:S(2)}, u32[]{:S(2)}) collective-permute-start(bf16[128,384]{1,0:T(8,128)(2,1)S(1)} %merge.3.second_ref), channel_id=1, source_target_pairs={{0,1},{1,0},{2,3},{3,2},{4,5},{5,4},{6,7},{7,6},{8,9},{9,8},{10,11... | collective-permute-start | bytes 294920 | tf_op jit(solution)/shard_map/ppermute | solution.py:677

commit v20 on v19

--- a/solution.py
+++ b/solution.py
@@ -12,7 +12,7 @@
 TRIPLE = 3 * HEAD_DIM
 EXTRA = 16
 PIECE = 2 * HEAD_DIM
-LOOK_AHEAD = 2
+LOOK_AHEAD = 3
 EPS = 1e-06
 F32 = jnp.float32
 BF16 = jnp.bfloat16

time: 50.2 us -> 50.1 us (level)
  no operation moved by 1% of the time
where the time goes in v20:
time: 50.1 us; the launch traced here: 49.9 us
  starting transfers between devices  22.2 us (44%)
  Pallas kernels  21.9 us (44%)
  waiting for transfers between devices  4.95 us (10%)
  between operations  0.78 us (2%)
    ppermute x10, starting transfers between devices, ring_step(): lax.ppermute(block, 'section', way)  12.1 us
    pallas_call x1, Pallas kernels, per_device(): pl.pallas_call(own_kernel, in_specs=[smem, vmem, vmem, hbm] + [hbm] * len...  4.35 us
    ppermute x10, waiting for transfers between devices, ring_step(): lax.ppermute(block, 'section', way)  4.28 us
    pallas_call x1, Pallas kernels, per_device(): pl.pallas_call(functools.partial(send_more_kernel, video), in_specs=[smem...  4.01 us
    ppermute x2, starting transfers between devices, per_device(): far = [lax.ppermute(chain[-1][0], 'section', ways[0]) for chain in chains]  3.81 us
    pallas_call x2, Pallas kernels, per_device(): pl.pallas_call(functools.partial(attend_kernel, first, len(whole), finish...  3.46 us
    pallas_call x1, Pallas kernels, per_device(): pl.pallas_call(send_kernel, in_specs=[smem] + [hbm] * 5, out_specs=[vmem]...  3.4 us
    ppermute x2, starting transfers between devices, per_device(): other_attended.append(lax.ppermute(attended[-1], 'head', swap_head))  3.18 us
  transfers between devices with their start and end apart: 20, of which 7 were waited for; matrix products, arithmetic and copies ran while one was open for 0% of the time, Pallas kernels for 42%

profile of v20, /device:TPU:0, one launch (start us, length us, event | category | flops | bytes accessed | tf_op | source)
XLA Modules:
  0.0 49.9 jit_solution(15979530495189498121)
XLA Ops:
  0.6 3.1 %collective-permute-start.2 = (bf16[2,128,768]{2,1,0:T(8,128)(2,1)}, bf16[2,128,768]{2,1,0:T(8,128)(2,1)S(1)}, u32[]{:S(2)}, u32[]{:S(2)}) collective-permute-start(bf16[2,128,768]{2,1,0:T(8,128)(2,1)} %refs_4_.1), channel_id=1, source_target_pairs={{0,8},{2,6},{4,0},{6,14},{8,16},{10,2},{12,4},{14,22},{16,24},{18,... | collective-permute-start | bytes 1179656 | tf_op jit(solution)/shard_map/ppermute | solution.py:520
  3.8 3.4 %project_send.1 = (bf16[272,1536]{1,0:T(8,128)(2,1)S(1)}, bf16[688,128]{1,0:T(8,128)(2,1)S(1)}, f32[272,128]{1,0:T(8,128)S(1)}, bf16[1536,768]{1,0:T(8,128)(2,1)S(1)}) custom-call(s32[2]{0:T(128)S(1)} %pad_add_fusion.place_ref, bf16[128,1536]{1,0:T(8,128)(2,1)} %hidden_ref.1, bf16[256,1536]{1,0:T(8,128)(2,1)} %t_ref.1, f32[1536]{0:T(1024)} %scale_ref.1, ...), custom_call_target="tpu_custom_call" | custom-call | flops 3080296960 | bytes 2831155 | tf_op jit(solution)/shard_map/project_send/pallas_call | solution.py:535
  7.2 2.0 %collective-permute-start = (bf16[688,128]{1,0:T(8,128)(2,1)S(1)}, bf16[688,128]{1,0:T(8,128)(2,1)S(1)}, u32[]{:S(2)}, u32[]{:S(2)}) collective-permute-start(bf16[688,128]{1,0:T(8,128)(2,1)S(1)} %get-tuple-element.46), channel_id=1, source_target_pairs={{0,1},{1,0},{2,3},{3,2},{4,5},{5,4},{6,7},{7,6},{8,9},{9,8},{10,11... | collective-permute-start | bytes 528392 | tf_op jit(solution)/shard_map/ppermute | solution.py:557
  9.2 4.0 %project_send_more.1 = (bf16[3280,128]{1,0:T(8,128)(2,1)S(1)}, bf16[1536,768]{1,0:T(8,128)(2,1)S(1)}) custom-call(s32[2]{0:T(128)S(1)} %pad_add_fusion.place_ref, bf16[272,1536]{1,0:T(8,128)(2,1)S(1)} %get-tuple-element.42.a_ref, bf16[1536,768]{1,0:T(8,128)(2,1)S(1)} %get-tuple-element.43.ahead_ref, bf16[1536,4608]{1,0:T(8,128)(2,1)} %w_ref.5), custom_call_target="tpu_custom_call" | custom-call | flops 4620445184 | bytes 4246732 | tf_op jit(solution)/shard_map/project_send_more/pallas_call | solution.py:559
  13.5 2.1 %collective-permute-start.4 = (bf16[2,128,384]{2,1,0:T(8,128)(2,1)S(1)}, bf16[2,128,384]{2,1,0:T(8,128)(2,1)S(1)}, u32[]{:S(2)}, u32[]{:S(2)}) collective-permute-start(bf16[2,128,384]{2,1,0:T(8,128)(2,1)S(1)} %get-tuple-element.50), channel_id=1, source_target_pairs={{0,8},{2,6},{4,0},{6,14},{8,16},{10,2},{12,4},{14,22},{16,24},{18,... | collective-permute-start | bytes 589832 | tf_op jit(solution)/shard_map/ppermute | solution.py:520
  15.9 1.7 %collective-permute-start.6 = (bf16[2,128,384]{2,1,0:T(8,128)(2,1)S(1)}, bf16[2,128,384]{2,1,0:T(8,128)(2,1)S(1)}, u32[]{:S(2)}, u32[]{:S(2)}) collective-permute-start(bf16[2,128,384]{2,1,0:T(8,128)(2,1)S(1)} %get-tuple-element.52), channel_id=1, source_target_pairs={{0,8},{2,6},{4,0},{6,14},{8,16},{10,2},{12,4},{14,22},{16,24},{18,... | collective-permute-start | bytes 589832 | tf_op jit(solution)/shard_map/ppermute | solution.py:520
  17.9 4.4 %project_own.1 = (f32[144,2304]{1,0:T(8,128)S(1)}, f32[128,1536]{1,0:T(8,128)S(1)}, f32[128]{0:T(128)S(1)}, f32[128]{0:T(128)S(1)}, s32[256]{0:T(256)S(1)}, /*in...) custom-call(s32[2]{0:T(128)S(1)} %pad_add_fusion.place_ref, bf16[272,1536]{1,0:T(8,128)(2,1)S(1)} %get-tuple-element.42.a_ref, ...), custom_call_target="tpu_custom_call" | custom-call | flops 7700742144 | bytes 7077888 | tf_op jit(solution)/shard_map/project_own/pallas_call | solution.py:585
  22.7 1.3 %collective-permute-start.9 = (bf16[2,128,384]{2,1,0:T(8,128)(2,1)S(1)}, bf16[2,128,384]{2,1,0:T(8,128)(2,1)S(1)}, u32[]{:S(2)}, u32[]{:S(2)}) collective-permute-start(bf16[2,128,384]{2,1,0:T(8,128)(2,1)S(1)} %collective-permute-done.4.refs_2_), channel_id=1, source_target_pairs={{0,8},{2,6},{4,0},{6,14},{8,16},{10,2},{12,4},{14,22},{16,24},{18,... | collective-permute-start | bytes 589832 | tf_op jit(solution)/shard_map/ppermute | solution.py:520
  24.0 0.9 %collective-permute-done.6.refs_2_ = bf16[2,128,384]{2,1,0:T(8,128)(2,1)S(1)} collective-permute-done((bf16[2,128,384]{2,1,0:T(8,128)(2,1)S(1)}, bf16[2,128,384]{2,1,0:T(8,128)(2,1)S(1)}, u32[]{:S(2)}, u32[]{:S(2)}) %collective-permute-start.6) | collective-permute-done | bytes 196640 | tf_op jit(solution)/shard_map/ppermute | solution.py:520
  24.9 2.0 %collective-permute-start.14 = (bf16[2,128,384]{2,1,0:T(8,128)(2,1)S(1)}, bf16[2,128,384]{2,1,0:T(8,128)(2,1)S(1)}, u32[]{:S(2)}, u32[]{:S(2)}) collective-permute-start(bf16[2,128,384]{2,1,0:T(8,128)(2,1)S(1)} %collective-permute-done.6.refs_2_), channel_id=1, source_target_pairs={{0,8},{2,6},{4,0},{6,14},{8,16},{10,2},{12,4},{14,22},{16,24},{18,... | collective-permute-start | bytes 589832 | tf_op jit(solution)/shard_map/ppermute | solution.py:520
  27.5 0.9 %collective-permute-done.9.refs_4_ = bf16[2,128,384]{2,1,0:T(8,128)(2,1)S(1)} collective-permute-done((bf16[2,128,384]{2,1,0:T(8,128)(2,1)S(1)}, bf16[2,128,384]{2,1,0:T(8,128)(2,1)S(1)}, u32[]{:S(2)}, u32[]{:S(2)}) %collective-permute-start.9) | collective-permute-done | bytes 196640 | tf_op jit(solution)/shard_map/ppermute | solution.py:520
  28.4 1.3 %collective-permute-start.11 = (bf16[2,128,384]{2,1,0:T(8,128)(2,1)S(1)}, bf16[2,128,384]{2,1,0:T(8,128)(2,1)S(1)}, u32[]{:S(2)}, u32[]{:S(2)}) collective-permute-start(bf16[2,128,384]{2,1,0:T(8,128)(2,1)S(1)} %collective-permute-done.9.refs_4_), channel_id=1, source_target_pairs={{0,8},{2,6},{4,0},{6,14},{8,16},{10,2},{12,4},{14,22},{16,24},{18,... | collective-permute-start | bytes 589832 | tf_op jit(solution)/shard_map/ppermute | solution.py:608
  29.7 0.7 %collective-permute-start.15 = (bf16[2,128,384]{2,1,0:T(8,128)(2,1)S(1)}, bf16[2,128,384]{2,1,0:T(8,128)(2,1)S(1)}, u32[]{:S(2)}, u32[]{:S(2)}) collective-permute-start(bf16[2,128,384]{2,1,0:T(8,128)(2,1)S(1)} %collective-permute-done.7.refs_3_), channel_id=1, source_target_pairs={{0,4},{2,10},{4,12},{6,2},{8,0},{10,18},{12,20},{14,6},{16,8},{18,... | collective-permute-start | bytes 589832 | tf_op jit(solution)/shard_map/ppermute | solution.py:520
  30.4 1.9 %collective-permute-done.14.refs_4_ = bf16[2,128,384]{2,1,0:T(8,128)(2,1)S(1)} collective-permute-done((bf16[2,128,384]{2,1,0:T(8,128)(2,1)S(1)}, bf16[2,128,384]{2,1,0:T(8,128)(2,1)S(1)}, u32[]{:S(2)}, u32[]{:S(2)}) %collective-permute-start.14) | collective-permute-done | bytes 196640 | tf_op jit(solution)/shard_map/ppermute | solution.py:520
  32.2 2.5 %collective-permute-start.16 = (bf16[2,128,384]{2,1,0:T(8,128)(2,1)S(1)}, bf16[2,128,384]{2,1,0:T(8,128)(2,1)S(1)}, u32[]{:S(2)}, u32[]{:S(2)}) collective-permute-start(bf16[2,128,384]{2,1,0:T(8,128)(2,1)S(1)} %collective-permute-done.14.refs_4_), channel_id=1, source_target_pairs={{0,8},{2,6},{4,0},{6,14},{8,16},{10,2},{12,4},{14,22},{16,24},{18,... | collective-permute-start | bytes 589832 | tf_op jit(solution)/shard_map/ppermute | solution.py:608
  34.7 0.7 %norm_video.1 = (bf16[128,384]{1,0:T(8,128)(2,1)S(1)}, bf16[128,384]{1,0:T(8,128)(2,1)S(1)}, bf16[2,128,768]{2,1,0:T(8,128)(2,1)S(1)}) custom-call(f32[144,2304]{1,0:T(8,128)S(1)} %get-tuple-element.45.own_ref.top_ref, bf16[688,128]{1,0:T(8,128)(2,1)S(1)} %collective-permute-done.first_ref, bf16[3280,128]{1,0:T(8,128)(2,1)S(1)} %collective-permute-done.1.more_ref, ...), custom_call_target="tpu_custom_call" | custom-call | flops 331776000 | bytes 2654208 | tf_op jit(solution)/shard_map/norm_video/pallas_call | solution.py:475
  36.0 0.5 %norm_text.1.text_ref = bf16[2,128,768]{2,1,0:T(8,128)(2,1)S(1)} custom-call(f32[128,1536]{1,0:T(8,128)S(1)} %get-tuple-element.61.own_ref, bf16[688,128]{1,0:T(8,128)(2,1)S(1)} %collective-permute-done.first_ref, bf16[3280,128]{1,0:T(8,128)(2,1)S(1)} %collective-permute-done.1.more_ref, f32[272,128]{1,0:T(8,128)S(1)} %get-tuple-element.55.stat_ref, ...), custom_call_target="tpu_custom_call" | custom-call | flops 294912 | bytes 294912 | tf_op jit(solution)/shard_map/norm_text/pallas_call | solution.py:475
  36.8 1.8 %attend.2 = (f32[128,384]{1,0:T(8,128)S(1)}, f32[128,128]{1,0:T(8,128)S(1)}, f32[128,512]{1,0:T(8,128)S(1)}) custom-call(s32[2]{0:T(128)S(1)} %pad_add_fusion.place_ref, bf16[128,384]{1,0:T(8,128)(2,1)S(1)} %get-tuple-element.59.qo_ref, bf16[128,384]{1,0:T(8,128)(2,1)S(1)} %collective-permute-done.8.qp_ref, ...), custom_call_target="tpu_custom_call" | custom-call | flops 163840 | bytes 983040 | tf_op jit(solution)/shard_map/attend/pallas_call | solution.py:648
  39.0 1.7 %attend.3 = (f32[256,384]{1,0:T(8,128)S(1)}, f32[256,128]{1,0:T(8,128)S(1)}) custom-call(s32[2]{0:T(128)S(1)} %pad_add_fusion.place_ref, bf16[128,384]{1,0:T(8,128)(2,1)S(1)} %get-tuple-element.69.qo_ref, bf16[128,384]{1,0:T(8,128)(2,1)S(1)} %collective-permute-done.13.qp_ref, bf16[2,128,768]{2,1,0:T(8,128)(2,1)S(1)} %get-tuple-element.58.fresh_ref, ...), custom_call_target="tpu_custom_call" | custom-call | flops 163840 | bytes 983040 | tf_op jit(solution)/shard_map/attend/pallas_call | solution.py:648
  40.7 0.5 %attend_last.1 = (f32[128,384]{1,0:T(8,128)S(1)}, f32[128,128]{1,0:T(8,128)S(1)}, f32[128,512]{1,0:T(8,128)S(1)}) custom-call(bf16[128,384]{1,0:T(8,128)(2,1)S(1)} %get-tuple-element.69.qo_ref, bf16[128,384]{1,0:T(8,128)(2,1)S(1)} %collective-permute-done.13.qp_ref, f32[256,384]{1,0:T(8,128)S(1)} %get-tuple-element.72.num_ref, ...), custom_call_target="tpu_custom_call" | custom-call | flops 16384 | bytes 98304 | tf_op jit(solution)/shard_map/attend_last/pallas_call | solution.py:475
  41.6 2.2 %collective-permute-start.18 = (bf16[128,384]{1,0:T(8,128)(2,1)S(1)}, bf16[128,384]{1,0:T(8,128)(2,1)S(1)}, u32[]{:S(2)}, u32[]{:S(2)}) collective-permute-start(bf16[128,384]{1,0:T(8,128)(2,1)S(1)} %merge.2.first_ref), channel_id=1, source_target_pairs={{0,1},{1,0},{2,3},{3,2},{4,5},{5,4},{6,7},{7,6},{8,9},{9,8},{10,11... | collective-permute-start | bytes 294920 | tf_op jit(solution)/shard_map/ppermute | solution.py:677
  43.9 1.0 %collective-permute-start.19 = (bf16[128,384]{1,0:T(8,128)(2,1)S(1)}, bf16[128,384]{1,0:T(8,128)(2,1)S(1)}, u32[]{:S(2)}, u32[]{:S(2)}) collective-permute-start(bf16[128,384]{1,0:T(8,128)(2,1)S(1)} %merge.3.second_ref), channel_id=1, source_target_pairs={{0,1},{1,0},{2,3},{3,2},{4,5},{5,4},{6,7},{7,6},{8,9},{9,8},{10,11... | collective-permute-start | bytes 294920 | tf_op jit(solution)/shard_map/ppermute | solution.py:677
  44.9 3.1 %part_out.1 = (f32[128,1536]{1,0:T(8,128)S(1)}, bf16[768,1536]{1,0:T(8,128)(2,1)S(1)}, bf16[128,1536]{1,0:T(8,128)(2,1)S(1)}, bf16[2,128,768]{2,1,0:T(8,128)(2,1)}) custom-call(s32[2]{0:T(128)S(1)} %pad_add_fusion.place_ref, bf16[1536,1536]{1,0:T(8,128)(2,1)} %weight_ref.1, bf16[128,1536]{1,0:T(8,128)(2,1)} %hidden_ref.1, ...), custom_call_target="tpu_custom_call" | custom-call | flops 603979776 | bytes 2359296 | tf_op jit(solution)/shard_map/part_out/pallas_call | solution.py:680
  48.8 1.1 %final_out.1 = bf16[128,1536]{1,0:T(8,128)(2,1)} custom-call(f32[128,1536]{1,0:T(8,128)S(1)} %more_out.1.part_ref, bf16[128,384]{1,0:T(8,128)(2,1)S(1)} %collective-permute-done.19.att_ref, bf16[768,1536]{1,0:T(8,128)(2,1)S(1)} %get-tuple-element.78.w_ref, bf16[128,1536]{1,0:T(8,128)(2,1)S(1)} %get-tuple-element.79.hidden_ref, ...), custom_call_target="tpu_custom_call" | custom-call | flops 603979776 | bytes 2359296 | tf_op jit(solution)/shard_map/final_out/pallas_call | solution.py:702
  (31 shorter events, 4.4 us)
Async XLA Ops:
  0.6 12.8 %collective-permute-start.2 = (bf16[2,128,768]{2,1,0:T(8,128)(2,1)}, bf16[2,128,768]{2,1,0:T(8,128)(2,1)S(1)}, u32[]{:S(2)}, u32[]{:S(2)}) collective-permute-start(bf16[2,128,768]{2,1,0:T(8,128)(2,1)} %refs_4_.1), channel_id=1, source_target_pairs={{0,8},{2,6},{4,0},{6,14},{8,16},{10,2},{12,4},{14,22},{16,24},{18,... | collective-permute-start | bytes 1179656 | tf_op jit(solution)/shard_map/ppermute | solution.py:520
  3.7 9.7 %collective-permute-start.3 = (bf16[2,128,768]{2,1,0:T(8,128)(2,1)}, bf16[2,128,768]{2,1,0:T(8,128)(2,1)S(1)}, u32[]{:S(2)}, u32[]{:S(2)}) collective-permute-start(bf16[2,128,768]{2,1,0:T(8,128)(2,1)} %refs_4_.1), channel_id=1, source_target_pairs={{0,4},{2,10},{4,12},{6,2},{8,0},{10,18},{12,20},{14,6},{16,8},{18,... | collective-permute-start | bytes 1179656 | tf_op jit(solution)/shard_map/ppermute | solution.py:520
  7.2 6.2 %collective-permute-start = (bf16[688,128]{1,0:T(8,128)(2,1)S(1)}, bf16[688,128]{1,0:T(8,128)(2,1)S(1)}, u32[]{:S(2)}, u32[]{:S(2)}) collective-permute-start(bf16[688,128]{1,0:T(8,128)(2,1)S(1)} %get-tuple-element.46), channel_id=1, source_target_pairs={{0,1},{1,0},{2,3},{3,2},{4,5},{5,4},{6,7},{7,6},{8,9},{9,8},{10,11... | collective-permute-start | bytes 528392 | tf_op jit(solution)/shard_map/ppermute | solution.py:557
  13.2 21.5 %collective-permute-start.1 = (bf16[3280,128]{1,0:T(8,128)(2,1)S(1)}, bf16[3280,128]{1,0:T(8,128)(2,1)S(1)}, u32[]{:S(2)}, u32[]{:S(2)}) collective-permute-start(bf16[3280,128]{1,0:T(8,128)(2,1)S(1)} %get-tuple-element.47), channel_id=1, source_target_pairs={{0,1},{1,0},{2,3},{3,2},{4,5},{5,4},{6,7},{7,6},{8,9},{9,8},{10,11... | collective-permute-start | bytes 2519048 | tf_op jit(solution)/shard_map/ppermute | solution.py:576
  13.5 8.8 %collective-permute-start.4 = (bf16[2,128,384]{2,1,0:T(8,128)(2,1)S(1)}, bf16[2,128,384]{2,1,0:T(8,128)(2,1)S(1)}, u32[]{:S(2)}, u32[]{:S(2)}) collective-permute-start(bf16[2,128,384]{2,1,0:T(8,128)(2,1)S(1)} %get-tuple-element.50), channel_id=1, source_target_pairs={{0,8},{2,6},{4,0},{6,14},{8,16},{10,2},{12,4},{14,22},{16,24},{18,... | collective-permute-start | bytes 589832 | tf_op jit(solution)/shard_map/ppermute | solution.py:520
  15.5 7.2 %collective-permute-start.5 = (bf16[2,128,384]{2,1,0:T(8,128)(2,1)S(1)}, bf16[2,128,384]{2,1,0:T(8,128)(2,1)S(1)}, u32[]{:S(2)}, u32[]{:S(2)}) collective-permute-start(bf16[2,128,384]{2,1,0:T(8,128)(2,1)S(1)} %get-tuple-element.51), channel_id=1, source_target_pairs={{0,4},{2,10},{4,12},{6,2},{8,0},{10,18},{12,20},{14,6},{16,8},{18,... | collective-permute-start | bytes 589832 | tf_op jit(solution)/shard_map/ppermute | solution.py:520
  15.9 9.0 %collective-permute-start.6 = (bf16[2,128,384]{2,1,0:T(8,128)(2,1)S(1)}, bf16[2,128,384]{2,1,0:T(8,128)(2,1)S(1)}, u32[]{:S(2)}, u32[]{:S(2)}) collective-permute-start(bf16[2,128,384]{2,1,0:T(8,128)(2,1)S(1)} %get-tuple-element.52), channel_id=1, source_target_pairs={{0,8},{2,6},{4,0},{6,14},{8,16},{10,2},{12,4},{14,22},{16,24},{18,... | collective-permute-start | bytes 589832 | tf_op jit(solution)/shard_map/ppermute | solution.py:520
  17.6 7.4 %collective-permute-start.7 = (bf16[2,128,384]{2,1,0:T(8,128)(2,1)S(1)}, bf16[2,128,384]{2,1,0:T(8,128)(2,1)S(1)}, u32[]{:S(2)}, u32[]{:S(2)}) collective-permute-start(bf16[2,128,384]{2,1,0:T(8,128)(2,1)S(1)} %get-tuple-element.53), channel_id=1, source_target_pairs={{0,4},{2,10},{4,12},{6,2},{8,0},{10,18},{12,20},{14,6},{16,8},{18,... | collective-permute-start | bytes 589832 | tf_op jit(solution)/shard_map/ppermute | solution.py:520
  22.7 5.7 %collective-permute-start.9 = (bf16[2,128,384]{2,1,0:T(8,128)(2,1)S(1)}, bf16[2,128,384]{2,1,0:T(8,128)(2,1)S(1)}, u32[]{:S(2)}, u32[]{:S(2)}) collective-permute-start(bf16[2,128,384]{2,1,0:T(8,128)(2,1)S(1)} %collective-permute-done.4.refs_2_), channel_id=1, source_target_pairs={{0,8},{2,6},{4,0},{6,14},{8,16},{10,2},{12,4},{14,22},{16,24},{18,... | collective-permute-start | bytes 589832 | tf_op jit(solution)/shard_map/ppermute | solution.py:520
  24.9 7.3 %collective-permute-start.14 = (bf16[2,128,384]{2,1,0:T(8,128)(2,1)S(1)}, bf16[2,128,384]{2,1,0:T(8,128)(2,1)S(1)}, u32[]{:S(2)}, u32[]{:S(2)}) collective-permute-start(bf16[2,128,384]{2,1,0:T(8,128)(2,1)S(1)} %collective-permute-done.6.refs_2_), channel_id=1, source_target_pairs={{0,8},{2,6},{4,0},{6,14},{8,16},{10,2},{12,4},{14,22},{16,24},{18,... | collective-permute-start | bytes 589832 | tf_op jit(solution)/shard_map/ppermute | solution.py:520
  27.0 8.6 %collective-permute-start.10 = (bf16[2,128,384]{2,1,0:T(8,128)(2,1)S(1)}, bf16[2,128,384]{2,1,0:T(8,128)(2,1)S(1)}, u32[]{:S(2)}, u32[]{:S(2)}) collective-permute-start(bf16[2,128,384]{2,1,0:T(8,128)(2,1)S(1)} %collective-permute-done.5.refs_3_), channel_id=1, source_target_pairs={{0,4},{2,10},{4,12},{6,2},{8,0},{10,18},{12,20},{14,6},{16,8},{18,... | collective-permute-start | bytes 589832 | tf_op jit(solution)/shard_map/ppermute | solution.py:520
  28.4 8.4 %collective-permute-start.11 = (bf16[2,128,384]{2,1,0:T(8,128)(2,1)S(1)}, bf16[2,128,384]{2,1,0:T(8,128)(2,1)S(1)}, u32[]{:S(2)}, u32[]{:S(2)}) collective-permute-start(bf16[2,128,384]{2,1,0:T(8,128)(2,1)S(1)} %collective-permute-done.9.refs_4_), channel_id=1, source_target_pairs={{0,8},{2,6},{4,0},{6,14},{8,16},{10,2},{12,4},{14,22},{16,24},{18,... | collective-permute-start | bytes 589832 | tf_op jit(solution)/shard_map/ppermute | solution.py:608
  29.7 9.3 %collective-permute-start.15 = (bf16[2,128,384]{2,1,0:T(8,128)(2,1)S(1)}, bf16[2,128,384]{2,1,0:T(8,128)(2,1)S(1)}, u32[]{:S(2)}, u32[]{:S(2)}) collective-permute-start(bf16[2,128,384]{2,1,0:T(8,128)(2,1)S(1)} %collective-permute-done.7.refs_3_), channel_id=1, source_target_pairs={{0,4},{2,10},{4,12},{6,2},{8,0},{10,18},{12,20},{14,6},{16,8},{18,... | collective-permute-start | bytes 589832 | tf_op jit(solution)/shard_map/ppermute | solution.py:520
  32.2 8.5 %collective-permute-start.16 = (bf16[2,128,384]{2,1,0:T(8,128)(2,1)S(1)}, bf16[2,128,384]{2,1,0:T(8,128)(2,1)S(1)}, u32[]{:S(2)}, u32[]{:S(2)}) collective-permute-start(bf16[2,128,384]{2,1,0:T(8,128)(2,1)S(1)} %collective-permute-done.14.refs_4_), channel_id=1, source_target_pairs={{0,8},{2,6},{4,0},{6,14},{8,16},{10,2},{12,4},{14,22},{16,24},{18,... | collective-permute-start | bytes 589832 | tf_op jit(solution)/shard_map/ppermute | solution.py:608
  35.4 1.4 %collective-permute-start.8 = (bf16[128,384]{1,0:T(8,128)(2,1)S(1)}, bf16[128,384]{1,0:T(8,128)(2,1)S(1)}, u32[]{:S(2)}, u32[]{:S(2)}) collective-permute-start(bf16[128,384]{1,0:T(8,128)(2,1)S(1)} %get-tuple-element.59.qo_ref), channel_id=1, source_target_pairs={{0,2},{2,0},{4,6},{6,4},{8,10},{10,8},{12,14},{14,12},{16,18},{18,... | collective-permute-start | bytes 294920 | tf_op jit(solution)/shard_map/ppermute | solution.py:618
  35.5 3.5 %collective-permute-start.13 = (bf16[128,384]{1,0:T(8,128)(2,1)S(1)}, bf16[128,384]{1,0:T(8,128)(2,1)S(1)}, u32[]{:S(2)}, u32[]{:S(2)}) collective-permute-start(bf16[128,384]{1,0:T(8,128)(2,1)S(1)} %get-tuple-element.69.qo_ref), channel_id=1, source_target_pairs={{0,2},{2,0},{4,6},{6,4},{8,10},{10,8},{12,14},{14,12},{16,18},{18,... | collective-permute-start | bytes 294920 | tf_op jit(solution)/shard_map/ppermute | solution.py:618
  38.6 2.9 %collective-permute-start.12 = (f32[128,512]{1,0:T(8,128)S(1)}, f32[128,512]{1,0:T(8,128)S(1)}, u32[]{:S(2)}, u32[]{:S(2)}) collective-permute-start(f32[128,512]{1,0:T(8,128)S(1)} %get-tuple-element.67), channel_id=1, source_target_pairs={{0,2},{2,0},{4,6},{6,4},{8,10},{10,8},{12,14},{14,12},{16,18},{18,... | collective-permute-start | bytes 786440 | tf_op jit(solution)/shard_map/ppermute | solution.py:669
  41.2 2.5 %collective-permute-start.17 = (f32[128,512]{1,0:T(8,128)S(1)}, f32[128,512]{1,0:T(8,128)S(1)}, u32[]{:S(2)}, u32[]{:S(2)}) collective-permute-start(f32[128,512]{1,0:T(8,128)S(1)} %get-tuple-element.76), channel_id=1, source_target_pairs={{0,2},{2,0},{4,6},{6,4},{8,10},{10,8},{12,14},{14,12},{16,18},{18,... | collective-permute-start | bytes 786440 | tf_op jit(solution)/shard_map/ppermute | solution.py:669
  41.6 6.5 %collective-permute-start.18 = (bf16[128,384]{1,0:T(8,128)(2,1)S(1)}, bf16[128,384]{1,0:T(8,128)(2,1)S(1)}, u32[]{:S(2)}, u32[]{:S(2)}) collective-permute-start(bf16[128,384]{1,0:T(8,128)(2,1)S(1)} %merge.2.first_ref), channel_id=1, source_target_pairs={{0,1},{1,0},{2,3},{3,2},{4,5},{5,4},{6,7},{7,6},{8,9},{9,8},{10,11... | collective-permute-start | bytes 294920 | tf_op jit(solution)/shard_map/ppermute | solution.py:677
  43.9 5.0 %collective-permute-start.19 = (bf16[128,384]{1,0:T(8,128)(2,1)S(1)}, bf16[128,384]{1,0:T(8,128)(2,1)S(1)}, u32[]{:S(2)}, u32[]{:S(2)}) collective-permute-start(bf16[128,384]{1,0:T(8,128)(2,1)S(1)} %merge.3.second_ref), channel_id=1, source_target_pairs={{0,1},{1,0},{2,3},{3,2},{4,5},{5,4},{6,7},{7,6},{8,9},{9,8},{10,11... | collective-permute-start | bytes 294920 | tf_op jit(solution)/shard_map/ppermute | solution.py:677

commit v21 on v20

--- a/solution.py
+++ b/solution.py
@@ -39,7 +39,8 @@
 
 
 def partial_sums(a_ref, w_ref, video, text, msg_ref, first):
-    band = lax.broadcasted_iota(jnp.int32, (EXTRA, HEAD_DIM), 0) // 4
+    row = lax.broadcasted_iota(jnp.int32, (EXTRA, HEAD_DIM), 0)
+    band, member = row // 4, row % 4
     top = video + EXTRA
     terms = None
     for start in range(0, w_ref.shape[1], PIECE):
@@ -50,7 +51,12 @@
             head, kind = divmod((start + local) // HEAD_DIM, 3)
             base = (first + head) * head_rows(video, text)
             msg_ref[base + kind * video : base + (kind + 1) * video, :] = part[:video].astype(BF16)
-            terms = part[video:top] if kind == 0 else jnp.where(band == kind, part[video:top], terms)
+            extra = part[video:top]
+            pieces = split_bf16(extra[0:1] + extra[1:2], 2) + split_bf16(extra[2:3] + extra[3:4], 2)
+            split = pieces[3].astype(F32)
+            for index in range(3):
+                split = jnp.where(member == index, pieces[index].astype(F32), split)
+            terms = split if kind == 0 else jnp.where(band == kind, split, terms)
             base += 3 * video
             if kind:
                 rows = slice(base + (kind - 1) * text, base + kind * text)

time: 50.1 us -> 50.1 us (level)
  no operation moved by 1% of the time
where the time goes in v21:
time: 50.1 us; the launch traced here: 49.9 us
  starting transfers between devices  22.2 us (44%)
  Pallas kernels  21.9 us (44%)
  waiting for transfers between devices  4.95 us (10%)
  between operations  0.78 us (2%)
    ppermute x10, starting transfers between devices, ring_step(): lax.ppermute(block, 'section', way)  12.1 us
    pallas_call x1, Pallas kernels, per_device(): pl.pallas_call(own_kernel, in_specs=[smem, vmem, vmem, hbm] + [hbm] * len...  4.35 us
    ppermute x10, waiting for transfers between devices, ring_step(): lax.ppermute(block, 'section', way)  4.28 us
    pallas_call x1, Pallas kernels, per_device(): pl.pallas_call(functools.partial(send_more_kernel, video), in_specs=[smem...  4.01 us
    ppermute x2, starting transfers between devices, per_device(): far = [lax.ppermute(chain[-1][0], 'section', ways[0]) for chain in chains]  3.81 us
    pallas_call x2, Pallas kernels, per_device(): pl.pallas_call(functools.partial(attend_kernel, first, len(whole), finish...  3.46 us
    pallas_call x1, Pallas kernels, per_device(): pl.pallas_call(send_kernel, in_specs=[smem] + [hbm] * 5, out_specs=[vmem]...  3.4 us
    ppermute x2, starting transfers between devices, per_device(): other_attended.append(lax.ppermute(attended[-1], 'head', swap_head))  3.18 us
  transfers between devices with their start and end apart: 20, of which 7 were waited for; matrix products, arithmetic and copies ran while one was open for 0% of the time, Pallas kernels for 42%

profile of v21, /device:TPU:0, one launch (start us, length us, event | category | flops | bytes accessed | tf_op | source)
XLA Modules:
  0.0 49.9 jit_solution(18195081800609579804)
XLA Ops:
  0.6 3.1 %collective-permute-start.2 = (bf16[2,128,768]{2,1,0:T(8,128)(2,1)}, bf16[2,128,768]{2,1,0:T(8,128)(2,1)S(1)}, u32[]{:S(2)}, u32[]{:S(2)}) collective-permute-start(bf16[2,128,768]{2,1,0:T(8,128)(2,1)} %refs_4_.1), channel_id=1, source_target_pairs={{0,8},{2,6},{4,0},{6,14},{8,16},{10,2},{12,4},{14,22},{16,24},{18,... | collective-permute-start | bytes 1179656 | tf_op jit(solution)/shard_map/ppermute | solution.py:526
  3.8 3.4 %project_send.1 = (bf16[272,1536]{1,0:T(8,128)(2,1)S(1)}, bf16[688,128]{1,0:T(8,128)(2,1)S(1)}, f32[272,128]{1,0:T(8,128)S(1)}, bf16[1536,768]{1,0:T(8,128)(2,1)S(1)}) custom-call(s32[2]{0:T(128)S(1)} %pad_add_fusion.place_ref, bf16[128,1536]{1,0:T(8,128)(2,1)} %hidden_ref.1, bf16[256,1536]{1,0:T(8,128)(2,1)} %t_ref.1, f32[1536]{0:T(1024)} %scale_ref.1, ...), custom_call_target="tpu_custom_call" | custom-call | flops 3080296960 | bytes 2831155 | tf_op jit(solution)/shard_map/project_send/pallas_call | solution.py:541
  7.2 2.0 %collective-permute-start = (bf16[688,128]{1,0:T(8,128)(2,1)S(1)}, bf16[688,128]{1,0:T(8,128)(2,1)S(1)}, u32[]{:S(2)}, u32[]{:S(2)}) collective-permute-start(bf16[688,128]{1,0:T(8,128)(2,1)S(1)} %get-tuple-element.46), channel_id=1, source_target_pairs={{0,1},{1,0},{2,3},{3,2},{4,5},{5,4},{6,7},{7,6},{8,9},{9,8},{10,11... | collective-permute-start | bytes 528392 | tf_op jit(solution)/shard_map/ppermute | solution.py:563
  9.2 4.0 %project_send_more.1 = (bf16[3280,128]{1,0:T(8,128)(2,1)S(1)}, bf16[1536,768]{1,0:T(8,128)(2,1)S(1)}) custom-call(s32[2]{0:T(128)S(1)} %pad_add_fusion.place_ref, bf16[272,1536]{1,0:T(8,128)(2,1)S(1)} %get-tuple-element.42.a_ref, bf16[1536,768]{1,0:T(8,128)(2,1)S(1)} %get-tuple-element.43.ahead_ref, bf16[1536,4608]{1,0:T(8,128)(2,1)} %w_ref.5), custom_call_target="tpu_custom_call" | custom-call | flops 4620445184 | bytes 4246732 | tf_op jit(solution)/shard_map/project_send_more/pallas_call | solution.py:565
  13.5 2.1 %collective-permute-start.4 = (bf16[2,128,384]{2,1,0:T(8,128)(2,1)S(1)}, bf16[2,128,384]{2,1,0:T(8,128)(2,1)S(1)}, u32[]{:S(2)}, u32[]{:S(2)}) collective-permute-start(bf16[2,128,384]{2,1,0:T(8,128)(2,1)S(1)} %get-tuple-element.50), channel_id=1, source_target_pairs={{0,8},{2,6},{4,0},{6,14},{8,16},{10,2},{12,4},{14,22},{16,24},{18,... | collective-permute-start | bytes 589832 | tf_op jit(solution)/shard_map/ppermute | solution.py:526
  15.9 1.7 %collective-permute-start.6 = (bf16[2,128,384]{2,1,0:T(8,128)(2,1)S(1)}, bf16[2,128,384]{2,1,0:T(8,128)(2,1)S(1)}, u32[]{:S(2)}, u32[]{:S(2)}) collective-permute-start(bf16[2,128,384]{2,1,0:T(8,128)(2,1)S(1)} %get-tuple-element.52), channel_id=1, source_target_pairs={{0,8},{2,6},{4,0},{6,14},{8,16},{10,2},{12,4},{14,22},{16,24},{18,... | collective-permute-start | bytes 589832 | tf_op jit(solution)/shard_map/ppermute | solution.py:526
  17.9 4.4 %project_own.1 = (f32[144,2304]{1,0:T(8,128)S(1)}, f32[128,1536]{1,0:T(8,128)S(1)}, f32[128]{0:T(128)S(1)}, f32[128]{0:T(128)S(1)}, s32[256]{0:T(256)S(1)}, /*in...) custom-call(s32[2]{0:T(128)S(1)} %pad_add_fusion.place_ref, bf16[272,1536]{1,0:T(8,128)(2,1)S(1)} %get-tuple-element.42.a_ref, ...), custom_call_target="tpu_custom_call" | custom-call | flops 7700742144 | bytes 7077888 | tf_op jit(solution)/shard_map/project_own/pallas_call | solution.py:591
  22.7 1.3 %collective-permute-start.9 = (bf16[2,128,384]{2,1,0:T(8,128)(2,1)S(1)}, bf16[2,128,384]{2,1,0:T(8,128)(2,1)S(1)}, u32[]{:S(2)}, u32[]{:S(2)}) collective-permute-start(bf16[2,128,384]{2,1,0:T(8,128)(2,1)S(1)} %collective-permute-done.4.refs_2_), channel_id=1, source_target_pairs={{0,8},{2,6},{4,0},{6,14},{8,16},{10,2},{12,4},{14,22},{16,24},{18,... | collective-permute-start | bytes 589832 | tf_op jit(solution)/shard_map/ppermute | solution.py:526
  24.0 0.9 %collective-permute-done.6.refs_2_ = bf16[2,128,384]{2,1,0:T(8,128)(2,1)S(1)} collective-permute-done((bf16[2,128,384]{2,1,0:T(8,128)(2,1)S(1)}, bf16[2,128,384]{2,1,0:T(8,128)(2,1)S(1)}, u32[]{:S(2)}, u32[]{:S(2)}) %collective-permute-start.6) | collective-permute-done | bytes 196640 | tf_op jit(solution)/shard_map/ppermute | solution.py:526
  24.9 2.0 %collective-permute-start.14 = (bf16[2,128,384]{2,1,0:T(8,128)(2,1)S(1)}, bf16[2,128,384]{2,1,0:T(8,128)(2,1)S(1)}, u32[]{:S(2)}, u32[]{:S(2)}) collective-permute-start(bf16[2,128,384]{2,1,0:T(8,128)(2,1)S(1)} %collective-permute-done.6.refs_2_), channel_id=1, source_target_pairs={{0,8},{2,6},{4,0},{6,14},{8,16},{10,2},{12,4},{14,22},{16,24},{18,... | collective-permute-start | bytes 589832 | tf_op jit(solution)/shard_map/ppermute | solution.py:526
  27.5 0.9 %collective-permute-done.9.refs_4_ = bf16[2,128,384]{2,1,0:T(8,128)(2,1)S(1)} collective-permute-done((bf16[2,128,384]{2,1,0:T(8,128)(2,1)S(1)}, bf16[2,128,384]{2,1,0:T(8,128)(2,1)S(1)}, u32[]{:S(2)}, u32[]{:S(2)}) %collective-permute-start.9) | collective-permute-done | bytes 196640 | tf_op jit(solution)/shard_map/ppermute | solution.py:526
  28.4 1.3 %collective-permute-start.11 = (bf16[2,128,384]{2,1,0:T(8,128)(2,1)S(1)}, bf16[2,128,384]{2,1,0:T(8,128)(2,1)S(1)}, u32[]{:S(2)}, u32[]{:S(2)}) collective-permute-start(bf16[2,128,384]{2,1,0:T(8,128)(2,1)S(1)} %collective-permute-done.9.refs_4_), channel_id=1, source_target_pairs={{0,8},{2,6},{4,0},{6,14},{8,16},{10,2},{12,4},{14,22},{16,24},{18,... | collective-permute-start | bytes 589832 | tf_op jit(solution)/shard_map/ppermute | solution.py:614
  29.7 0.7 %collective-permute-start.15 = (bf16[2,128,384]{2,1,0:T(8,128)(2,1)S(1)}, bf16[2,128,384]{2,1,0:T(8,128)(2,1)S(1)}, u32[]{:S(2)}, u32[]{:S(2)}) collective-permute-start(bf16[2,128,384]{2,1,0:T(8,128)(2,1)S(1)} %collective-permute-done.7.refs_3_), channel_id=1, source_target_pairs={{0,4},{2,10},{4,12},{6,2},{8,0},{10,18},{12,20},{14,6},{16,8},{18,... | collective-permute-start | bytes 589832 | tf_op jit(solution)/shard_map/ppermute | solution.py:526
  30.4 1.9 %collective-permute-done.14.refs_4_ = bf16[2,128,384]{2,1,0:T(8,128)(2,1)S(1)} collective-permute-done((bf16[2,128,384]{2,1,0:T(8,128)(2,1)S(1)}, bf16[2,128,384]{2,1,0:T(8,128)(2,1)S(1)}, u32[]{:S(2)}, u32[]{:S(2)}) %collective-permute-start.14) | collective-permute-done | bytes 196640 | tf_op jit(solution)/shard_map/ppermute | solution.py:526
  32.2 2.5 %collective-permute-start.16 = (bf16[2,128,384]{2,1,0:T(8,128)(2,1)S(1)}, bf16[2,128,384]{2,1,0:T(8,128)(2,1)S(1)}, u32[]{:S(2)}, u32[]{:S(2)}) collective-permute-start(bf16[2,128,384]{2,1,0:T(8,128)(2,1)S(1)} %collective-permute-done.14.refs_4_), channel_id=1, source_target_pairs={{0,8},{2,6},{4,0},{6,14},{8,16},{10,2},{12,4},{14,22},{16,24},{18,... | collective-permute-start | bytes 589832 | tf_op jit(solution)/shard_map/ppermute | solution.py:614
  34.7 0.7 %norm_video.1 = (bf16[128,384]{1,0:T(8,128)(2,1)S(1)}, bf16[128,384]{1,0:T(8,128)(2,1)S(1)}, bf16[2,128,768]{2,1,0:T(8,128)(2,1)S(1)}) custom-call(f32[144,2304]{1,0:T(8,128)S(1)} %get-tuple-element.45.own_ref.top_ref, bf16[688,128]{1,0:T(8,128)(2,1)S(1)} %collective-permute-done.first_ref, bf16[3280,128]{1,0:T(8,128)(2,1)S(1)} %collective-permute-done.1.more_ref, ...), custom_call_target="tpu_custom_call" | custom-call | flops 331776000 | bytes 2654208 | tf_op jit(solution)/shard_map/norm_video/pallas_call | solution.py:481
  36.0 0.5 %norm_text.1.text_ref = bf16[2,128,768]{2,1,0:T(8,128)(2,1)S(1)} custom-call(f32[128,1536]{1,0:T(8,128)S(1)} %get-tuple-element.61.own_ref, bf16[688,128]{1,0:T(8,128)(2,1)S(1)} %collective-permute-done.first_ref, bf16[3280,128]{1,0:T(8,128)(2,1)S(1)} %collective-permute-done.1.more_ref, f32[272,128]{1,0:T(8,128)S(1)} %get-tuple-element.55.stat_ref, ...), custom_call_target="tpu_custom_call" | custom-call | flops 294912 | bytes 294912 | tf_op jit(solution)/shard_map/norm_text/pallas_call | solution.py:481
  36.8 1.8 %attend.2 = (f32[128,384]{1,0:T(8,128)S(1)}, f32[128,128]{1,0:T(8,128)S(1)}, f32[128,512]{1,0:T(8,128)S(1)}) custom-call(s32[2]{0:T(128)S(1)} %pad_add_fusion.place_ref, bf16[128,384]{1,0:T(8,128)(2,1)S(1)} %get-tuple-element.59.qo_ref, bf16[128,384]{1,0:T(8,128)(2,1)S(1)} %collective-permute-done.8.qp_ref, ...), custom_call_target="tpu_custom_call" | custom-call | flops 163840 | bytes 983040 | tf_op jit(solution)/shard_map/attend/pallas_call | solution.py:654
  39.0 1.7 %attend.3 = (f32[256,384]{1,0:T(8,128)S(1)}, f32[256,128]{1,0:T(8,128)S(1)}) custom-call(s32[2]{0:T(128)S(1)} %pad_add_fusion.place_ref, bf16[128,384]{1,0:T(8,128)(2,1)S(1)} %get-tuple-element.69.qo_ref, bf16[128,384]{1,0:T(8,128)(2,1)S(1)} %collective-permute-done.13.qp_ref, bf16[2,128,768]{2,1,0:T(8,128)(2,1)S(1)} %get-tuple-element.58.fresh_ref, ...), custom_call_target="tpu_custom_call" | custom-call | flops 163840 | bytes 983040 | tf_op jit(solution)/shard_map/attend/pallas_call | solution.py:654
  40.7 0.5 %attend_last.1 = (f32[128,384]{1,0:T(8,128)S(1)}, f32[128,128]{1,0:T(8,128)S(1)}, f32[128,512]{1,0:T(8,128)S(1)}) custom-call(bf16[128,384]{1,0:T(8,128)(2,1)S(1)} %get-tuple-element.69.qo_ref, bf16[128,384]{1,0:T(8,128)(2,1)S(1)} %collective-permute-done.13.qp_ref, f32[256,384]{1,0:T(8,128)S(1)} %get-tuple-element.72.num_ref, ...), custom_call_target="tpu_custom_call" | custom-call | flops 16384 | bytes 98304 | tf_op jit(solution)/shard_map/attend_last/pallas_call | solution.py:481
  41.6 2.2 %collective-permute-start.18 = (bf16[128,384]{1,0:T(8,128)(2,1)S(1)}, bf16[128,384]{1,0:T(8,128)(2,1)S(1)}, u32[]{:S(2)}, u32[]{:S(2)}) collective-permute-start(bf16[128,384]{1,0:T(8,128)(2,1)S(1)} %merge.2.first_ref), channel_id=1, source_target_pairs={{0,1},{1,0},{2,3},{3,2},{4,5},{5,4},{6,7},{7,6},{8,9},{9,8},{10,11... | collective-permute-start | bytes 294920 | tf_op jit(solution)/shard_map/ppermute | solution.py:683
  43.9 1.0 %collective-permute-start.19 = (bf16[128,384]{1,0:T(8,128)(2,1)S(1)}, bf16[128,384]{1,0:T(8,128)(2,1)S(1)}, u32[]{:S(2)}, u32[]{:S(2)}) collective-permute-start(bf16[128,384]{1,0:T(8,128)(2,1)S(1)} %merge.3.second_ref), channel_id=1, source_target_pairs={{0,1},{1,0},{2,3},{3,2},{4,5},{5,4},{6,7},{7,6},{8,9},{9,8},{10,11... | collective-permute-start | bytes 294920 | tf_op jit(solution)/shard_map/ppermute | solution.py:683
  44.9 3.1 %part_out.1 = (f32[128,1536]{1,0:T(8,128)S(1)}, bf16[768,1536]{1,0:T(8,128)(2,1)S(1)}, bf16[128,1536]{1,0:T(8,128)(2,1)S(1)}, bf16[2,128,768]{2,1,0:T(8,128)(2,1)}) custom-call(s32[2]{0:T(128)S(1)} %pad_add_fusion.place_ref, bf16[1536,1536]{1,0:T(8,128)(2,1)} %weight_ref.1, bf16[128,1536]{1,0:T(8,128)(2,1)} %hidden_ref.1, ...), custom_call_target="tpu_custom_call" | custom-call | flops 603979776 | bytes 2359296 | tf_op jit(solution)/shard_map/part_out/pallas_call | solution.py:686
  48.8 1.1 %final_out.1 = bf16[128,1536]{1,0:T(8,128)(2,1)} custom-call(f32[128,1536]{1,0:T(8,128)S(1)} %more_out.1.part_ref, bf16[128,384]{1,0:T(8,128)(2,1)S(1)} %collective-permute-done.19.att_ref, bf16[768,1536]{1,0:T(8,128)(2,1)S(1)} %get-tuple-element.78.w_ref, bf16[128,1536]{1,0:T(8,128)(2,1)S(1)} %get-tuple-element.79.hidden_ref, ...), custom_call_target="tpu_custom_call" | custom-call | flops 603979776 | bytes 2359296 | tf_op jit(solution)/shard_map/final_out/pallas_call | solution.py:708
  (31 shorter events, 4.4 us)
Async XLA Ops:
  0.6 12.8 %collective-permute-start.2 = (bf16[2,128,768]{2,1,0:T(8,128)(2,1)}, bf16[2,128,768]{2,1,0:T(8,128)(2,1)S(1)}, u32[]{:S(2)}, u32[]{:S(2)}) collective-permute-start(bf16[2,128,768]{2,1,0:T(8,128)(2,1)} %refs_4_.1), channel_id=1, source_target_pairs={{0,8},{2,6},{4,0},{6,14},{8,16},{10,2},{12,4},{14,22},{16,24},{18,... | collective-permute-start | bytes 1179656 | tf_op jit(solution)/shard_map/ppermute | solution.py:526
  3.7 9.7 %collective-permute-start.3 = (bf16[2,128,768]{2,1,0:T(8,128)(2,1)}, bf16[2,128,768]{2,1,0:T(8,128)(2,1)S(1)}, u32[]{:S(2)}, u32[]{:S(2)}) collective-permute-start(bf16[2,128,768]{2,1,0:T(8,128)(2,1)} %refs_4_.1), channel_id=1, source_target_pairs={{0,4},{2,10},{4,12},{6,2},{8,0},{10,18},{12,20},{14,6},{16,8},{18,... | collective-permute-start | bytes 1179656 | tf_op jit(solution)/shard_map/ppermute | solution.py:526
  7.2 6.2 %collective-permute-start = (bf16[688,128]{1,0:T(8,128)(2,1)S(1)}, bf16[688,128]{1,0:T(8,128)(2,1)S(1)}, u32[]{:S(2)}, u32[]{:S(2)}) collective-permute-start(bf16[688,128]{1,0:T(8,128)(2,1)S(1)} %get-tuple-element.46), channel_id=1, source_target_pairs={{0,1},{1,0},{2,3},{3,2},{4,5},{5,4},{6,7},{7,6},{8,9},{9,8},{10,11... | collective-permute-start | bytes 528392 | tf_op jit(solution)/shard_map/ppermute | solution.py:563
  13.2 21.5 %collective-permute-start.1 = (bf16[3280,128]{1,0:T(8,128)(2,1)S(1)}, bf16[3280,128]{1,0:T(8,128)(2,1)S(1)}, u32[]{:S(2)}, u32[]{:S(2)}) collective-permute-start(bf16[3280,128]{1,0:T(8,128)(2,1)S(1)} %get-tuple-element.47), channel_id=1, source_target_pairs={{0,1},{1,0},{2,3},{3,2},{4,5},{5,4},{6,7},{7,6},{8,9},{9,8},{10,11... | collective-permute-start | bytes 2519048 | tf_op jit(solution)/shard_map/ppermute | solution.py:582
  13.5 8.8 %collective-permute-start.4 = (bf16[2,128,384]{2,1,0:T(8,128)(2,1)S(1)}, bf16[2,128,384]{2,1,0:T(8,128)(2,1)S(1)}, u32[]{:S(2)}, u32[]{:S(2)}) collective-permute-start(bf16[2,128,384]{2,1,0:T(8,128)(2,1)S(1)} %get-tuple-element.50), channel_id=1, source_target_pairs={{0,8},{2,6},{4,0},{6,14},{8,16},{10,2},{12,4},{14,22},{16,24},{18,... | collective-permute-start | bytes 589832 | tf_op jit(solution)/shard_map/ppermute | solution.py:526
  15.5 7.2 %collective-permute-start.5 = (bf16[2,128,384]{2,1,0:T(8,128)(2,1)S(1)}, bf16[2,128,384]{2,1,0:T(8,128)(2,1)S(1)}, u32[]{:S(2)}, u32[]{:S(2)}) collective-permute-start(bf16[2,128,384]{2,1,0:T(8,128)(2,1)S(1)} %get-tuple-element.51), channel_id=1, source_target_pairs={{0,4},{2,10},{4,12},{6,2},{8,0},{10,18},{12,20},{14,6},{16,8},{18,... | collective-permute-start | bytes 589832 | tf_op jit(solution)/shard_map/ppermute | solution.py:526
  15.9 9.0 %collective-permute-start.6 = (bf16[2,128,384]{2,1,0:T(8,128)(2,1)S(1)}, bf16[2,128,384]{2,1,0:T(8,128)(2,1)S(1)}, u32[]{:S(2)}, u32[]{:S(2)}) collective-permute-start(bf16[2,128,384]{2,1,0:T(8,128)(2,1)S(1)} %get-tuple-element.52), channel_id=1, source_target_pairs={{0,8},{2,6},{4,0},{6,14},{8,16},{10,2},{12,4},{14,22},{16,24},{18,... | collective-permute-start | bytes 589832 | tf_op jit(solution)/shard_map/ppermute | solution.py:526
  17.6 7.4 %collective-permute-start.7 = (bf16[2,128,384]{2,1,0:T(8,128)(2,1)S(1)}, bf16[2,128,384]{2,1,0:T(8,128)(2,1)S(1)}, u32[]{:S(2)}, u32[]{:S(2)}) collective-permute-start(bf16[2,128,384]{2,1,0:T(8,128)(2,1)S(1)} %get-tuple-element.53), channel_id=1, source_target_pairs={{0,4},{2,10},{4,12},{6,2},{8,0},{10,18},{12,20},{14,6},{16,8},{18,... | collective-permute-start | bytes 589832 | tf_op jit(solution)/shard_map/ppermute | solution.py:526
  22.7 5.7 %collective-permute-start.9 = (bf16[2,128,384]{2,1,0:T(8,128)(2,1)S(1)}, bf16[2,128,384]{2,1,0:T(8,128)(2,1)S(1)}, u32[]{:S(2)}, u32[]{:S(2)}) collective-permute-start(bf16[2,128,384]{2,1,0:T(8,128)(2,1)S(1)} %collective-permute-done.4.refs_2_), channel_id=1, source_target_pairs={{0,8},{2,6},{4,0},{6,14},{8,16},{10,2},{12,4},{14,22},{16,24},{18,... | collective-permute-start | bytes 589832 | tf_op jit(solution)/shard_map/ppermute | solution.py:526
  24.9 7.3 %collective-permute-start.14 = (bf16[2,128,384]{2,1,0:T(8,128)(2,1)S(1)}, bf16[2,128,384]{2,1,0:T(8,128)(2,1)S(1)}, u32[]{:S(2)}, u32[]{:S(2)}) collective-permute-start(bf16[2,128,384]{2,1,0:T(8,128)(2,1)S(1)} %collective-permute-done.6.refs_2_), channel_id=1, source_target_pairs={{0,8},{2,6},{4,0},{6,14},{8,16},{10,2},{12,4},{14,22},{16,24},{18,... | collective-permute-start | bytes 589832 | tf_op jit(solution)/shard_map/ppermute | solution.py:526
  27.0 8.6 %collective-permute-start.10 = (bf16[2,128,384]{2,1,0:T(8,128)(2,1)S(1)}, bf16[2,128,384]{2,1,0:T(8,128)(2,1)S(1)}, u32[]{:S(2)}, u32[]{:S(2)}) collective-permute-start(bf16[2,128,384]{2,1,0:T(8,128)(2,1)S(1)} %collective-permute-done.5.refs_3_), channel_id=1, source_target_pairs={{0,4},{2,10},{4,12},{6,2},{8,0},{10,18},{12,20},{14,6},{16,8},{18,... | collective-permute-start | bytes 589832 | tf_op jit(solution)/shard_map/ppermute | solution.py:526
  28.4 8.4 %collective-permute-start.11 = (bf16[2,128,384]{2,1,0:T(8,128)(2,1)S(1)}, bf16[2,128,384]{2,1,0:T(8,128)(2,1)S(1)}, u32[]{:S(2)}, u32[]{:S(2)}) collective-permute-start(bf16[2,128,384]{2,1,0:T(8,128)(2,1)S(1)} %collective-permute-done.9.refs_4_), channel_id=1, source_target_pairs={{0,8},{2,6},{4,0},{6,14},{8,16},{10,2},{12,4},{14,22},{16,24},{18,... | collective-permute-start | bytes 589832 | tf_op jit(solution)/shard_map/ppermute | solution.py:614
  29.7 9.3 %collective-permute-start.15 = (bf16[2,128,384]{2,1,0:T(8,128)(2,1)S(1)}, bf16[2,128,384]{2,1,0:T(8,128)(2,1)S(1)}, u32[]{:S(2)}, u32[]{:S(2)}) collective-permute-start(bf16[2,128,384]{2,1,0:T(8,128)(2,1)S(1)} %collective-permute-done.7.refs_3_), channel_id=1, source_target_pairs={{0,4},{2,10},{4,12},{6,2},{8,0},{10,18},{12,20},{14,6},{16,8},{18,... | collective-permute-start | bytes 589832 | tf_op jit(solution)/shard_map/ppermute | solution.py:526
  32.2 8.5 %collective-permute-start.16 = (bf16[2,128,384]{2,1,0:T(8,128)(2,1)S(1)}, bf16[2,128,384]{2,1,0:T(8,128)(2,1)S(1)}, u32[]{:S(2)}, u32[]{:S(2)}) collective-permute-start(bf16[2,128,384]{2,1,0:T(8,128)(2,1)S(1)} %collective-permute-done.14.refs_4_), channel_id=1, source_target_pairs={{0,8},{2,6},{4,0},{6,14},{8,16},{10,2},{12,4},{14,22},{16,24},{18,... | collective-permute-start | bytes 589832 | tf_op jit(solution)/shard_map/ppermute | solution.py:614
  35.4 1.4 %collective-permute-start.8 = (bf16[128,384]{1,0:T(8,128)(2,1)S(1)}, bf16[128,384]{1,0:T(8,128)(2,1)S(1)}, u32[]{:S(2)}, u32[]{:S(2)}) collective-permute-start(bf16[128,384]{1,0:T(8,128)(2,1)S(1)} %get-tuple-element.59.qo_ref), channel_id=1, source_target_pairs={{0,2},{2,0},{4,6},{6,4},{8,10},{10,8},{12,14},{14,12},{16,18},{18,... | collective-permute-start | bytes 294920 | tf_op jit(solution)/shard_map/ppermute | solution.py:624
  35.5 3.5 %collective-permute-start.13 = (bf16[128,384]{1,0:T(8,128)(2,1)S(1)}, bf16[128,384]{1,0:T(8,128)(2,1)S(1)}, u32[]{:S(2)}, u32[]{:S(2)}) collective-permute-start(bf16[128,384]{1,0:T(8,128)(2,1)S(1)} %get-tuple-element.69.qo_ref), channel_id=1, source_target_pairs={{0,2},{2,0},{4,6},{6,4},{8,10},{10,8},{12,14},{14,12},{16,18},{18,... | collective-permute-start | bytes 294920 | tf_op jit(solution)/shard_map/ppermute | solution.py:624
  38.6 2.9 %collective-permute-start.12 = (f32[128,512]{1,0:T(8,128)S(1)}, f32[128,512]{1,0:T(8,128)S(1)}, u32[]{:S(2)}, u32[]{:S(2)}) collective-permute-start(f32[128,512]{1,0:T(8,128)S(1)} %get-tuple-element.67), channel_id=1, source_target_pairs={{0,2},{2,0},{4,6},{6,4},{8,10},{10,8},{12,14},{14,12},{16,18},{18,... | collective-permute-start | bytes 786440 | tf_op jit(solution)/shard_map/ppermute | solution.py:675
  41.2 2.5 %collective-permute-start.17 = (f32[128,512]{1,0:T(8,128)S(1)}, f32[128,512]{1,0:T(8,128)S(1)}, u32[]{:S(2)}, u32[]{:S(2)}) collective-permute-start(f32[128,512]{1,0:T(8,128)S(1)} %get-tuple-element.76), channel_id=1, source_target_pairs={{0,2},{2,0},{4,6},{6,4},{8,10},{10,8},{12,14},{14,12},{16,18},{18,... | collective-permute-start | bytes 786440 | tf_op jit(solution)/shard_map/ppermute | solution.py:675
  41.6 6.5 %collective-permute-start.18 = (bf16[128,384]{1,0:T(8,128)(2,1)S(1)}, bf16[128,384]{1,0:T(8,128)(2,1)S(1)}, u32[]{:S(2)}, u32[]{:S(2)}) collective-permute-start(bf16[128,384]{1,0:T(8,128)(2,1)S(1)} %merge.2.first_ref), channel_id=1, source_target_pairs={{0,1},{1,0},{2,3},{3,2},{4,5},{5,4},{6,7},{7,6},{8,9},{9,8},{10,11... | collective-permute-start | bytes 294920 | tf_op jit(solution)/shard_map/ppermute | solution.py:683
  43.9 5.0 %collective-permute-start.19 = (bf16[128,384]{1,0:T(8,128)(2,1)S(1)}, bf16[128,384]{1,0:T(8,128)(2,1)S(1)}, u32[]{:S(2)}, u32[]{:S(2)}) collective-permute-start(bf16[128,384]{1,0:T(8,128)(2,1)S(1)} %merge.3.second_ref), channel_id=1, source_target_pairs={{0,1},{1,0},{2,3},{3,2},{4,5},{5,4},{6,7},{7,6},{8,9},{9,8},{10,11... | collective-permute-start | bytes 294920 | tf_op jit(solution)/shard_map/ppermute | solution.py:683
